TPU v7x, 32 devices: a whole 2x2x4 slice. The times are simulated.
32 devices in a mesh: basin: 8 (over z, x), tm: 4 (over y, core).
Axes of the slice: x: 2, y: 2, z: 4, core: 2. Of those that a mesh axis runs over, the one named last changes fastest.
Arguments:
- incidence: int32 [256, 16, 128], P('basin'), may hold values 0 or 1
- row_gauge: int32 [4096], P('basin'), may hold values from 0 to 2047, as said below
- gauge_kernel: int32 [2048], P('basin'), may hold values from 0 to 31
- kernels: float32 [32, 128], replicated, may hold values from 0 to 0.0156
- observed: float32 [2048, 512], P('basin', 'tm'), may hold values from -8 to 8
- first_guess: float32 [32768, 512], P('basin', 'tm'), may hold values from -4 to 4
Outputs:
- inflows: float32 [32768, 512], P('basin', 'tm')
Inputs may be any that keep to these rules, and one draw needn't show every extreme that they name: `row_gauge`: the 512 slots of one index of basin name gauges of any one owner (gauges o * 256 to o * 256 + 255 belong to owner o) at most 128 times; in every draw one owner is named exactly 128 times by the slots of every index of basin.
All inputs are finite; a program needn't handle non-finite values. No bound on the sum of `incidence` on one device may be relied on, other than what follows from the above.
Results may differ from a plain program's by a relative error of at most 0.0001.
Values sent between devices are 32-bit elements; how exact they have to be, the bound alone decides.
No kernel may reach another device: no remote copies, remote signals or barrier semaphores. Data moves between devices by JAX's collectives and lax.ppermute only.
A program may use at most 128 MiB of HBM per device.

v0:
```python
import jax
import jax.numpy as jnp
from jax import lax
from jax.sharding import PartitionSpec as P

ITERS = 3


HIGH = lax.Precision.HIGHEST


def from_behind(x, axis, by):
    devices = lax.axis_size(axis)
    pairs = [(i, i + by) for i in range(devices) if 0 <= i + by < devices]
    return lax.ppermute(x, axis, pairs)


def lag_table(kernels, lag):
    taps = kernels.shape[1]
    valid = (lag >= 0) & (lag < taps)
    picked = jnp.take(kernels, jnp.clip(lag, 0, taps - 1), axis=1)
    picked = jnp.where(valid[None, :, :], picked, 0.0)
    return jnp.transpose(picked, (1, 0, 2)).reshape(lag.shape[0], -1)


def class_mix(extended, table, selector):
    gauges = extended.shape[0]
    classes = selector.shape[1]
    spread = jnp.dot(extended, table, precision=HIGH).reshape(gauges, classes, -1)
    return jnp.einsum("gch,gc->gh", spread, selector, precision=HIGH)


def squared(values):
    return jnp.sum(values * values)


def gauge_total(value):
    return lax.psum(value, ("basin", "tm"))


def reach_total(value):
    return lax.psum(value, ("basin", "tm"))


def shards(incidence, row_gauge, gauge_kernel, kernels, observed, first_guess):
    weights = incidence.astype(jnp.float32)
    blocks, slots, width = weights.shape
    gauges_here, hours = observed.shape
    owners = lax.axis_size("basin")
    classes = kernels.shape[0]
    partials = blocks * slots
    outer = jnp.arange(2 * hours)[:, None]
    inner = jnp.arange(hours)[None, :]
    table_fwd = lag_table(kernels, inner + hours - outer)
    table_bwd = lag_table(kernels, outer - inner)
    selector = (gauge_kernel[:, None] == jnp.arange(classes)[None, :]).astype(jnp.float32)

    def to_gauges(partial_value):
        table = (
            jnp.zeros((gauges_here * owners, hours), jnp.float32).at[row_gauge].add(partial_value)
        )
        return lax.psum_scatter(table, "basin", scatter_dimension=0, tiled=True)

    def from_gauges(upstream):
        everything = lax.all_gather(upstream, "basin", axis=0, tiled=True)
        return everything[row_gauge]

    def forward(field):
        partial_value = jnp.einsum(
            "bjr,brt->bjt", weights, field.reshape(blocks, width, hours), precision=HIGH
        )
        sums = to_gauges(partial_value.reshape(partials, hours))
        earlier = from_behind(sums, "tm", 1)
        return class_mix(jnp.concatenate([earlier, sums], axis=1), table_fwd, selector)

    def backward(series):
        later = from_behind(series, "tm", -1)
        upstream = class_mix(jnp.concatenate([series, later], axis=1), table_bwd, selector)
        rows = from_gauges(upstream)
        spread = jnp.einsum(
            "bjr,bjt->brt", weights, rows.reshape(blocks, slots, hours), precision=HIGH
        )
        return spread.reshape(blocks * width, hours)

    start = observed - forward(first_guess)
    beta = jnp.sqrt(gauge_total(squared(start)))
    u = start / beta
    pulled = backward(u)
    alpha = jnp.sqrt(reach_total(squared(pulled)))
    v = pulled / alpha
    w = v
    correction = jnp.zeros(first_guess.shape, jnp.float32)
    phibar = beta
    rhobar = alpha
    for step in range(ITERS):
        final = step == ITERS - 1
        p = forward(v) - alpha * u
        beta = jnp.sqrt(gauge_total(squared(p)))
        if not final:
            pulled = backward(p / beta) - beta * v
            alpha_next = jnp.sqrt(reach_total(squared(pulled)))
            v_next = pulled / alpha_next
        u = p / beta
        rho = jnp.sqrt(rhobar * rhobar + beta * beta)
        cosine = rhobar / rho
        sine = beta / rho
        phi = cosine * phibar
        phibar = sine * phibar
        correction = correction + phi / rho * w
        if not final:
            theta = sine * alpha_next
            rhobar = -cosine * alpha_next
            w = v_next - theta / rho * w
            v = v_next
            alpha = alpha_next
    return first_guess + correction


def solution(mesh):
    in_specs = (
        P("basin", None, None),
        P("basin"),
        P("basin"),
        P(),
        P("basin", "tm"),
        P("basin", "tm"),
    )
    out_specs = P("basin", "tm")
    return jax.shard_map(shards, mesh=mesh, in_specs=in_specs, out_specs=out_specs, check_vma=False)
```

profile of v0, /device:TPU:1, one launch (start us, length us, event | category | flops | bytes accessed | tf_op | source)
XLA Modules:
  0.0 1022.2 jit_solution(551064777691343393)
XLA Ops:
  14.3 108.2 %gather_fusion.3 = f32[32768,32]{1,0:T(8,128)} fusion(f32[32,128]{0,1:T(8,128)S(1)} %copy.21, s32[32768]{0:T(1024)S(1)} %bitcast_clamp_fusion.1), kind=kCustom, calls=%fused_computation.clone | custom fusion | bytes 8519680 | tf_op jit(solution)/shard_map/jit(_take)/gather | solution.py:21
  122.5 14.0 %copy.22 = f32[256,128,32]{0,1,2:T(8,128)} copy(f32[256,128,32]{2,1,0:T(8,128)} %bitcast.119) | data formatting | bytes 8388608 | tf_op jit(solution)/shard_map/jit(_take)/gather | solution.py:21
  143.7 5.6 fusion.12
  154.4 40.7 %psum.49 = f32[]{:T(128)} all-reduce(f32[]{:T(128)} %get-tuple-element.6), channel_id=1, replica_groups=mesh['basin'=8,'tm'=4] {'basin','tm'}, use_global_device_ids=true, to_apply=%region_3.5 | all-reduce | flops 1 | bytes 8 | tf_op jit(solution)/shard_map/psum | solution.py:38
  199.5 108.2 %gather_fusion.4 = f32[32768,32]{1,0:T(8,128)} fusion(f32[32,128]{0,1:T(8,128)S(1)} %copy.21, s32[32768]{0:T(1024)S(1)} %bitcast_clamp_fusion), kind=kCustom, calls=%fused_computation.1.clone | custom fusion | bytes 8519680 | tf_op jit(solution)/shard_map/jit(_take)/gather | solution.py:21
  307.7 14.0 %copy.26 = f32[256,128,32]{0,1,2:T(8,128)} copy(f32[256,128,32]{2,1,0:T(8,128)} %bitcast.118) | data formatting | bytes 8388608 | tf_op jit(solution)/shard_map/jit(_take)/gather | solution.py:21
  322.0 5.6 fusion.4
  327.6 5.1 fusion.24
  332.8 38.7 %all-gather.4.cloned.1.call-done = f32[2048,128]{1,0:T(8,128)} async-done(((f32[256,128]{1,0:T(8,128)}), f32[2048,128]{1,0:T(8,128)}) %all-gather.4.cloned.1.call-update) | async-done | bytes 1048592 | tf_op jit(solution)/shard_map/all_gather | solution.py:65
  377.8 39.0 %psum.50 = f32[]{:T(128)} all-reduce(f32[]{:T(128)} %get-tuple-element.10), channel_id=1, replica_groups=mesh['basin'=8,'tm'=4] {'basin','tm'}, use_global_device_ids=true, to_apply=%region_5.7 | all-reduce | flops 1 | bytes 8 | tf_op jit(solution)/shard_map/psum | solution.py:42
  422.8 63.8 %reduce-scatter.7.cloned.1.call-done = f32[256,128]{1,0:T(8,128)} async-done(((f32[2048,128]{1,0:T(8,128)}), f32[256,128]{1,0:T(8,128)}) %reduce-scatter.7.cloned.1.call-update) | async-done | bytes 131088 | tf_op jit(solution)/shard_map/reduce_scatter | solution.py:62
  486.6 5.2 collective-permute-start.2
  494.0 5.6 fusion.10
  504.6 40.2 %psum.51 = f32[]{:T(128)} all-reduce(f32[]{:T(128)} %multiply_reduce_fusion.5), channel_id=1, replica_groups=mesh['basin'=8,'tm'=4] {'basin','tm'}, use_global_device_ids=true, to_apply=%region_9.11 | all-reduce | flops 1 | bytes 8 | tf_op jit(solution)/shard_map/psum | solution.py:38
  553.5 5.6 fusion.2
  559.1 5.1 fusion.20
  564.2 36.1 %all-gather.6.cloned.1.call-done = f32[2048,128]{1,0:T(8,128)} async-done(((f32[256,128]{1,0:T(8,128)}), f32[2048,128]{1,0:T(8,128)}) %all-gather.6.cloned.1.call-update) | async-done | bytes 1048592 | tf_op jit(solution)/shard_map/all_gather | solution.py:65
  602.6 5.4 multiply_reduce_fusion.1
  608.0 39.2 %psum.52 = f32[]{:T(128)} all-reduce(f32[]{:T(128)} %get-tuple-element.12), channel_id=1, replica_groups=mesh['basin'=8,'tm'=4] {'basin','tm'}, use_global_device_ids=true, to_apply=%region_11.13 | all-reduce | flops 1 | bytes 8 | tf_op jit(solution)/shard_map/psum | solution.py:42
  654.7 63.8 %reduce-scatter.9.cloned.1.call-done = f32[256,128]{1,0:T(8,128)} async-done(((f32[2048,128]{1,0:T(8,128)}), f32[256,128]{1,0:T(8,128)}) %reduce-scatter.9.cloned.1.call-update) | async-done | bytes 131088 | tf_op jit(solution)/shard_map/reduce_scatter | solution.py:62
  718.5 5.2 collective-permute-start.4
  725.9 5.6 fusion.8
  736.6 40.3 %psum.53 = f32[]{:T(128)} all-reduce(f32[]{:T(128)} %multiply_reduce_fusion.4), channel_id=1, replica_groups=mesh['basin'=8,'tm'=4] {'basin','tm'}, use_global_device_ids=true, to_apply=%region_15.17 | all-reduce | flops 1 | bytes 8 | tf_op jit(solution)/shard_map/psum | solution.py:38
  785.6 5.6 fusion
  791.2 5.1 fusion.16
  796.4 36.1 %all-gather.8.cloned.1.call-done = f32[2048,128]{1,0:T(8,128)} async-done(((f32[256,128]{1,0:T(8,128)}), f32[2048,128]{1,0:T(8,128)}) %all-gather.8.cloned.1.call-update) | async-done | bytes 1048592 | tf_op jit(solution)/shard_map/all_gather | solution.py:65
  834.7 6.5 multiply_reduce_fusion
  841.3 39.0 %psum.54 = f32[]{:T(128)} all-reduce(f32[]{:T(128)} %get-tuple-element.14), channel_id=1, replica_groups=mesh['basin'=8,'tm'=4] {'basin','tm'}, use_global_device_ids=true, to_apply=%region_17.19 | all-reduce | flops 1 | bytes 8 | tf_op jit(solution)/shard_map/psum | solution.py:42
  887.7 63.5 %reduce-scatter.11.cloned.1.call-done = f32[256,128]{1,0:T(8,128)} async-done(((f32[2048,128]{1,0:T(8,128)}), f32[256,128]{1,0:T(8,128)}) %reduce-scatter.11.cloned.1.call-update) | async-done | bytes 131088 | tf_op jit(solution)/shard_map/reduce_scatter | solution.py:62
  951.3 5.2 collective-permute-start.6
  958.7 5.6 fusion.6
  969.4 40.2 %psum.55 = f32[]{:T(128)} all-reduce(f32[]{:T(128)} %multiply_reduce_fusion.3), channel_id=1, replica_groups=mesh['basin'=8,'tm'=4] {'basin','tm'}, use_global_device_ids=true, to_apply=%region_21.23 | all-reduce | flops 1 | bytes 8 | tf_op jit(solution)/shard_map/psum | solution.py:38
  (75 shorter events, 96.1 us)
Async XLA Ops:
  6.5 7.5 copy-start.3
  6.5 130.4 %reduce-scatter.5.cloned.1.call-start = ((), (), s32[]{:S(2)}) async-start(), calls=%async_computation.4 | async-start | bytes 1179648 | tf_op jit(solution)/shard_map/reduce_scatter | solution.py:62
  14.0 357.5 %all-gather.4.cloned.1.call-start = ((), (), s32[]{:S(2)}) async-start(), calls=%async_computation.5 | async-start | bytes 1179648 | tf_op jit(solution)/shard_map/all_gather | solution.py:65
  122.5 19.2 %copy-start.4 = (s32[256]{0:T(256)S(1)}, s32[256]{0:T(256)}, u32[]{:S(2)}) copy-start(s32[256]{0:T(256)} %param.10) | copy-start | bytes 3076
  136.9 6.8 collective-permute-start
  149.3 4.4 copy-start.2
  195.8 126.2 %collective-permute-start.1 = (f32[256,128]{1,0:T(8,128)S(1)}, f32[256,128]{1,0:T(8,128)S(1)}, u32[]{:S(2)}, u32[]{:S(2)}) collective-permute-start(f32[256,128]{1,0:T(8,128)S(1)} %broadcast_divide_fusion.6), channel_id=1, source_target_pairs={{1,0},{2,1},{3,2},{5,4},{6,5},{7,6},{9,8},{10,9},{11,10},{13,12},{... | collective-permute-start | bytes 393224 | tf_op jit(solution)/shard_map/ppermute | solution.py:15
  327.6 46.2 %copy-start.1 = (s32[32,16,128]{2,1,0:T(8,128)S(1)}, s32[32,16,128]{2,1,0:T(8,128)}, u32[]{:S(2)}) copy-start(s32[32,16,128]{2,1,0:T(8,128)} %param.8) | copy-start | bytes 786436
  332.7 153.8 %reduce-scatter.7.cloned.1.call-start = ((), (), s32[]{:S(2)}) async-start(), calls=%async_computation.6 | async-start | bytes 1179648 | tf_op jit(solution)/shard_map/reduce_scatter | solution.py:62
  422.7 177.6 %all-gather.6.cloned.1.call-start = ((), (), s32[]{:S(2)}) async-start(), calls=%async_computation.7 | async-start | bytes 1179648 | tf_op jit(solution)/shard_map/all_gather | solution.py:65
  486.6 7.4 collective-permute-start.2
  545.6 7.9 collective-permute-start.3
  564.2 154.3 %reduce-scatter.9.cloned.1.call-start = ((), (), s32[]{:S(2)}) async-start(), calls=%async_computation.8 | async-start | bytes 1179648 | tf_op jit(solution)/shard_map/reduce_scatter | solution.py:62
  654.7 177.8 %all-gather.8.cloned.1.call-start = ((), (), s32[]{:S(2)}) async-start(), calls=%async_computation.9 | async-start | bytes 1179648 | tf_op jit(solution)/shard_map/all_gather | solution.py:65
  718.5 7.4 collective-permute-start.4
  777.7 7.9 collective-permute-start.5
  796.3 154.9 %reduce-scatter.11.cloned.1.call-start = ((), (), s32[]{:S(2)}) async-start(), calls=%async_computation.10 | async-start | bytes 1179648 | tf_op jit(solution)/shard_map/reduce_scatter | solution.py:62
  951.3 7.4 collective-permute-start.6
  1010.4 3.2 copy-start
Sparse Core Ops, SparseCore 0:
  14.1 64.3 reduce-scatter.4
  332.8 38.6 all-gather.3
  422.9 63.6 reduce-scatter.6
  564.3 35.9 all-gather.5
  654.8 63.6 reduce-scatter.8
  796.4 35.9 all-gather.7
  887.9 63.3 reduce-scatter.10
where the time goes:
time: 1030 us; the launch traced here: 1020 us
  waiting for transfers between devices  319 us (31%)
  blocking collectives  279 us (27%)
  local copies, waits for them, and re-layouts  252 us (24%)
  matrix products  101 us (10%)
  starting transfers between devices  30.8 us (3%)
  other arithmetic  21.5 us (2%)
  between operations  19.4 us (2%)
    gather x4, local copies, waits for them, and re-layouts, lag_table(): picked = jnp.take(kernels, jnp.clip(lag, 0, taps - 1), axis=1)  244 us
    reduce_scatter x4, waiting for transfers between devices, to_gauges(): return lax.psum_scatter(table, 'basin', scatter_dimension=0, tiled=True)  191 us
    psum x4, blocking collectives, gauge_total(): return lax.psum(value, ('basin', 'tm'))  161 us
    psum x3, blocking collectives, reach_total(): return lax.psum(value, ('basin', 'tm'))  117 us
    all_gather x3, waiting for transfers between devices, from_gauges(): everything = lax.all_gather(upstream, 'basin', axis=0, tiled=True)  111 us
    dot_general x7, matrix products, class_mix(): jnp.dot(extended, table, precision=HIGH).reshape(gauges, classes, -1)  39.2 us
    dot_general x7, matrix products, class_mix(): return jnp.einsum('gch,gc->gh', spread, selector, precision=HIGH)  32.9 us
    ppermute x7, starting transfers between devices, from_behind(): return lax.ppermute(x, axis, pairs)  30.5 us
  transfers between devices with their start and end apart: 14, of which 12 were waited for; matrix products, arithmetic and copies ran while one was open for 24% of the time, Pallas kernels for 0%

commit v1 on v0

v1 whole, which is shorter than its diff:
```python
import functools

import jax
import jax.numpy as jnp
import numpy as np
from jax import lax
from jax.experimental import pallas as pl
from jax.experimental.pallas import tpu as pltpu
from jax.sharding import PartitionSpec as P

F32 = jnp.float32
BF16 = jnp.bfloat16
HIGH = lax.Precision.HIGHEST
SPAN = 256
VMEM_BYTES = 56 * 1024 * 1024


def params():
    return pltpu.CompilerParams(vmem_limit_bytes=VMEM_BYTES)


def transforms():
    half = SPAN // 2
    freq = 2.0 * np.pi * (np.arange(half) + 0.5) / SPAN
    phase = np.arange(SPAN)[:, None] * freq[None, :]
    forward = np.concatenate([np.cos(phase), -np.sin(phase)], axis=1)
    inverse = forward.T * (2.0 / SPAN)
    return (
        jnp.asarray(forward, F32),
        jnp.asarray(inverse[:, :half], F32),
        jnp.asarray(inverse[:, half:], F32),
    )


def dot(a, b):
    return jnp.dot(a, b, preferred_element_type=F32)


def exact(a, b):
    return jnp.dot(a, b, precision=HIGH, preferred_element_type=F32)


def pieces(value, count):
    out = []
    for _ in range(count):
        piece = value.astype(BF16)
        out.append(piece)
        value = value - piece.astype(F32)
    return out


def pick(hot, value):
    return sum(dot(hot, piece) for piece in pieces(value, 3))


def prepare_kernel(inc_ref, field_ref, partial_ref, gram_ref):
    blocks, slots, width = inc_ref.shape
    rows = blocks * slots
    weights = inc_ref[...].astype(F32).astype(BF16)
    for b in range(blocks):
        value = field_ref[pl.ds(b * width, width), :]
        partial_ref[pl.ds(b * slots, slots), :] = pick(weights[b], value)
    flat = weights.reshape(rows, width)
    full = lax.dot_general(flat, flat, (((1,), (1,)), ((), ())), preferred_element_type=F32)
    row = lax.broadcasted_iota(jnp.int32, (rows, rows), 0)
    col = lax.broadcasted_iota(jnp.int32, (rows, rows), 1)
    own = jnp.where(row // slots == col // slots, full, 0.0)
    gram_ref[...] = jnp.sum(own.reshape(blocks, slots, rows), axis=0)


def prepare(incidence, field):
    blocks, slots, width = incidence.shape
    hours = field.shape[1]
    step = 8
    return pl.pallas_call(
        prepare_kernel,
        grid=(blocks // step,),
        in_specs=[
            pl.BlockSpec((step, slots, width), lambda i: (i, 0, 0)),
            pl.BlockSpec((step * width, hours), lambda i: (i, 0)),
        ],
        out_specs=[
            pl.BlockSpec((step * slots, hours), lambda i: (i, 0)),
            pl.BlockSpec((slots, step * slots), lambda i: (0, i)),
        ],
        out_shape=[
            jax.ShapeDtypeStruct((blocks * slots, hours), F32),
            jax.ShapeDtypeStruct((slots, blocks * slots), F32),
        ],
        compiler_params=params(),
        name="prepare",
    )(incidence, field)


def table_kernel(gauge_ref, partial_ref, out_ref):
    slots = partial_ref.shape[0]
    rows = out_ref.shape[0]
    first = pl.program_id(0) * rows
    gauge = lax.broadcasted_iota(jnp.int32, (rows, slots), 0) + first
    hot = jnp.where(gauge_ref[...] == gauge, 1.0, 0.0).astype(BF16)
    out_ref[...] = pick(hot, partial_ref[...])


def table(row_gauge, partial, gauges):
    slots, hours = partial.shape
    step = 256
    return pl.pallas_call(
        table_kernel,
        grid=(gauges // step,),
        in_specs=[
            pl.BlockSpec((1, slots), lambda i: (0, 0)),
            pl.BlockSpec((slots, hours), lambda i: (0, 0)),
        ],
        out_specs=pl.BlockSpec((step, hours), lambda i: (i, 0)),
        out_shape=jax.ShapeDtypeStruct((gauges, hours), F32),
        compiler_params=params(),
        name="table",
    )(row_gauge.reshape(1, slots), partial)


def couple_kernel(first_ref, lane_ref, sub_ref, gram_ref, high_ref, low_ref, near_ref):
    slots = gram_ref.shape[0]
    count = lane_ref.shape[1]
    rows, cols = high_ref.shape
    tile = 256
    first = first_ref[0]

    @pl.when(pl.program_id(0) == 0)
    def _():
        row = lax.broadcasted_iota(jnp.int32, (tile, tile), 0)
        col = lax.broadcasted_iota(jnp.int32, (tile, tile), 1)
        same = row // slots == col // slots
        mine = lax.broadcasted_iota(jnp.int32, (rows, tile), 0) + first

        def body(i, carry):
            here = pl.ds(pl.multiple_of(i * tile, tile), tile)
            block = jnp.concatenate([gram_ref[:, here]] * (tile // slots), axis=0)
            block = jnp.where(same, block, 0.0).astype(BF16)
            hot = jnp.where(lane_ref[:, here] == mine, 1.0, 0.0).astype(BF16)
            near_ref[:, here] = dot(hot, block)
            return carry

        lax.fori_loop(0, count // tile, body, 0)

    def chunk(i, total):
        here = pl.ds(pl.multiple_of(i * 1024, 1024), 1024)
        gauge = lax.broadcasted_iota(jnp.int32, (1024, cols), 1) + pl.program_id(0) * cols
        hot = jnp.where(sub_ref[here, :] == gauge, 1.0, 0.0).astype(BF16)
        near = near_ref[:, here]
        high = near.astype(BF16)
        low = (near - high.astype(F32)).astype(BF16)
        return total + dot(high, hot) + dot(low, hot)

    total = lax.fori_loop(0, count // 1024, chunk, jnp.zeros((rows, cols), F32))
    high, low = pieces(total, 2)
    high_ref[...] = high
    low_ref[...] = low


def couple(first, row_gauge, gram, rows, gauges):
    count = row_gauge.shape[0]
    step = 256
    return pl.pallas_call(
        couple_kernel,
        grid=(gauges // step,),
        in_specs=[
            pl.BlockSpec(memory_space=pltpu.SMEM),
            pl.BlockSpec((1, count), lambda i: (0, 0)),
            pl.BlockSpec((count, 1), lambda i: (0, 0)),
            pl.BlockSpec(gram.shape, lambda i: (0, 0)),
        ],
        out_specs=[pl.BlockSpec((rows, step), lambda i: (0, i))] * 2,
        out_shape=[jax.ShapeDtypeStruct((rows, gauges), BF16)] * 2,
        scratch_shapes=[pltpu.VMEM((rows, count), F32)],
        compiler_params=params(),
        name="couple",
    )(first, row_gauge.reshape(1, count), row_gauge.reshape(count, 1), gram)


def mix_kernel(high_ref, low_ref, value_ref, out_ref):
    high = high_ref[...]
    low = low_ref[...]
    one, two, three = pieces(value_ref[...], 3)
    out_ref[...] = (dot(high, three) + dot(low, two)) + (dot(high, two) + dot(low, one)) + dot(high, one)


def mix(high, low, value):
    return pl.pallas_call(
        mix_kernel,
        out_shape=jax.ShapeDtypeStruct((high.shape[0], value.shape[1]), F32),
        compiler_params=params(),
        name="mix",
    )(high, low, value)


def spectrum_kernel(class_ref, kernels_ref, forward_ref, out_ref):
    rows = class_ref.shape[0]
    classes, taps = kernels_ref.shape
    kind = lax.broadcasted_iota(jnp.int32, (rows, classes), 1)
    hot = jnp.where(class_ref[...] == kind, 1.0, 0.0)
    out_ref[...] = exact(exact(hot, kernels_ref[...]), forward_ref[pl.ds(0, taps), :])


def spectrum(gauge_kernel, kernels, forward):
    rows = gauge_kernel.shape[0]
    return pl.pallas_call(
        spectrum_kernel,
        out_shape=jax.ShapeDtypeStruct((rows, SPAN), F32),
        compiler_params=params(),
        name="spectrum",
    )(gauge_kernel.reshape(rows, 1), kernels, forward)


def delayed(before, here, after, spec, forward, inverse_last):
    rows, half = here.shape
    stacked = jnp.concatenate(
        [jnp.concatenate([before, here], axis=1), jnp.concatenate([here, after], axis=1)], axis=0
    )
    waves = exact(stacked, forward)
    real, imag = waves[:, :half], waves[:, half:]
    kr = jnp.concatenate([spec[:, :half]] * 2, axis=0)
    ki = jnp.concatenate([spec[:, half:]] * 2, axis=0)
    turned = jnp.concatenate([real * kr - imag * ki, real * ki + imag * kr], axis=1)
    out = exact(turned, inverse_last)
    return out[:rows], out[rows:]


def advanced(here, after, spec, forward, inverse_first):
    half = here.shape[1]
    waves = exact(jnp.concatenate([here, after], axis=1), forward)
    real, imag = waves[:, :half], waves[:, half:]
    kr, ki = spec[:, :half], spec[:, half:]
    turned = jnp.concatenate([real * kr + imag * ki, imag * kr - real * ki], axis=1)
    return exact(turned, inverse_first)


def lanes(a, b):
    return jnp.sum(a * b, axis=0, keepdims=True)


def total(ref, row):
    return jnp.sum(ref[row : row + 1, :], axis=1, keepdims=True)


def ratios(ref):
    square = total(ref, 0)
    alpha = jnp.sqrt(square)
    beta = jnp.sqrt(jnp.maximum(total(ref, 1) / square - 2.0 * total(ref, 2) + square, 0.0))
    return alpha, beta


def first_kernel(
    more_ref, sums_ref, observed_ref, spec_ref, forward_ref, first_ref, last_ref, out_ref, note_ref
):
    rows, half = observed_ref.shape[0] // 2, observed_ref.shape[1]
    spec, forward = spec_ref[...], forward_ref[...]
    before, here, after = (sums_ref[pl.ds(i * rows, rows), :] for i in range(3))
    now, later = delayed(before, here, after, spec, forward, last_ref[...])
    start = observed_ref[pl.ds(0, rows), :] - now
    start_later = (observed_ref[pl.ds(rows, rows), :] - later) * more_ref[0]
    out_ref[...] = advanced(start, start_later, spec, forward, first_ref[...])
    note_ref[...] = jnp.concatenate([lanes(start, start), jnp.zeros((7, half), F32)], axis=0)


def first_step(more, sums, observed, spec, mats):
    rows, half = spec.shape[0], observed.shape[1]
    return pl.pallas_call(
        first_kernel,
        in_specs=[pl.BlockSpec(memory_space=pltpu.SMEM)] + [pl.BlockSpec(memory_space=pltpu.VMEM)] * 6,
        out_shape=[jax.ShapeDtypeStruct((rows, half), F32), jax.ShapeDtypeStruct((8, half), F32)],
        compiler_params=params(),
        name="first_step",
    )(more, sums, observed, spec, *mats)


def step_kernel(
    opening,
    final,
    more_ref,
    note_ref,
    sums_ref,
    spec_ref,
    forward_ref,
    first_ref,
    last_ref,
    pulled_ref,
    *refs,
):
    if opening:
        state_ref = None
    else:
        state_ref, *refs = refs
    if final:
        (out_note_ref,) = refs
    else:
        new_ref, out_ref, out_note_ref = refs
    rows, half = pulled_ref.shape
    spec, forward = spec_ref[...], forward_ref[...]
    if opening:
        scale = 1.0 / jnp.sqrt(total(note_ref, 0))
        along = sums_ref[...] * scale
        new_s, new_su = along, along
        new_zu = pulled_ref[...] * scale
        new_z = new_zu
    else:
        alpha, beta = ratios(note_ref)
        a, b, g = 1.0 / (alpha * beta), alpha / beta, beta / alpha
        wide = pl.ds(0, 3 * rows), pl.ds(3 * rows, 3 * rows)
        new_su = sums_ref[...] * a - state_ref[wide[1], :] * b
        new_s = new_su - state_ref[wide[0], :] * g
        new_zu = pulled_ref[...] * a - state_ref[pl.ds(7 * rows, rows), :] * b
        new_z = new_zu - state_ref[pl.ds(6 * rows, rows), :] * g
    before, here, after = (new_s[i * rows : (i + 1) * rows] for i in range(3))
    now, later = delayed(before, here, after, spec, forward, last_ref[...])
    out_note_ref[...] = jnp.concatenate(
        [lanes(new_z, here), lanes(now, now), lanes(new_zu, here), jnp.zeros((5, half), F32)], axis=0
    )
    if not final:
        new_ref[pl.ds(0, 3 * rows), :] = new_s
        new_ref[pl.ds(3 * rows, 3 * rows), :] = new_su
        new_ref[pl.ds(6 * rows, rows), :] = new_z
        new_ref[pl.ds(7 * rows, rows), :] = new_zu
        out_ref[...] = advanced(now, later * more_ref[0], spec, forward, first_ref[...])


def next_step(more, note, sums, spec, mats, pulled, state, final):
    rows, half = pulled.shape
    opening = state is None
    shapes = [
        jax.ShapeDtypeStruct((8 * rows, half), F32),
        jax.ShapeDtypeStruct((rows, half), F32),
        jax.ShapeDtypeStruct((8, half), F32),
    ]
    args = [more, note, sums, spec, *mats, pulled] + ([] if opening else [state])
    return pl.pallas_call(
        functools.partial(step_kernel, opening, final),
        in_specs=[pl.BlockSpec(memory_space=pltpu.SMEM)]
        + [pl.BlockSpec(memory_space=pltpu.VMEM)] * (len(args) - 1),
        out_shape=shapes[2:] if final else shapes,
        compiler_params=params(),
        name="next_step",
    )(*args)


def weights_of(notes):
    start = jnp.sqrt(total(notes[0], 0))
    zero = jnp.zeros_like(start)
    units = [1.0 / start, zero, zero]
    z, zu = list(units), list(units)
    phibar = start
    alpha, beta = ratios(notes[1])
    rhobar = alpha
    w = [value / alpha for value in z]
    result = [zero] * 3
    steps = len(notes) - 1
    for k in range(steps):
        rho = jnp.sqrt(rhobar * rhobar + beta * beta)
        cosine, sine = rhobar / rho, beta / rho
        phi, phibar = cosine * phibar, sine * phibar
        result = [r + phi / rho * value for r, value in zip(result, w)]
        if k < steps - 1:
            a, b, g = 1.0 / (alpha * beta), alpha / beta, beta / alpha
            zu = [(a if i == k + 1 else 0.0) - b * value for i, value in enumerate(zu)]
            z = [value - g * old for value, old in zip(zu, z)]
            alpha, beta = ratios(notes[k + 2])
            theta = sine * alpha
            rhobar = -cosine * alpha
            w = [value / alpha - theta / rho * old for value, old in zip(z, w)]
    return result


def finish_kernel(n0, n1, n2, n3, gauge_ref, q0, q1, q2, inc_ref, field_ref, out_ref, rows_ref):
    blocks, slots, width = inc_ref.shape
    count = rows_ref.shape[0]
    gauges = q0.shape[0]
    step = pl.program_id(0)

    @pl.when(step == 0)
    def _():
        e0, e1, e2 = weights_of([n0, n1, n2, n3])
        width_ = 512

        def body(i, value):
            here = pl.ds(pl.multiple_of(i * width_, width_), width_)
            mixed = q0[here, :] * e0 + q1[here, :] * e1 + q2[here, :] * e2
            gauge = lax.broadcasted_iota(jnp.int32, (count, width_), 1) + i * width_
            hot = jnp.where(gauge_ref[...] == gauge, 1.0, 0.0).astype(BF16)
            return value + pick(hot, mixed)

        rows_ref[...] = lax.fori_loop(0, gauges // width_, body, jnp.zeros(rows_ref.shape, F32))

    weights = inc_ref[...].astype(F32).astype(BF16)
    for b in range(blocks):
        here = pl.ds(b * width, width)
        rows = rows_ref[pl.ds(pl.multiple_of((step * blocks + b) * slots, slots), slots), :]
        added = sum(
            lax.dot_general(weights[b], piece, (((0,), (0,)), ((), ())), preferred_element_type=F32)
            for piece in pieces(rows, 3)
        )
        out_ref[here, :] = field_ref[here, :] + added


def finish(notes, row_gauge, gathered, incidence, field):
    blocks, slots, width = incidence.shape
    hours = field.shape[1]
    count = row_gauge.shape[0]
    step = 8
    whole = lambda shape: pl.BlockSpec(shape, lambda i: (0, 0))
    return pl.pallas_call(
        finish_kernel,
        grid=(blocks // step,),
        in_specs=[whole(n.shape) for n in notes]
        + [whole((count, 1))]
        + [whole(q.shape) for q in gathered]
        + [
            pl.BlockSpec((step, slots, width), lambda i: (i, 0, 0)),
            pl.BlockSpec((step * width, hours), lambda i: (i, 0)),
        ],
        out_specs=pl.BlockSpec((step * width, hours), lambda i: (i, 0)),
        out_shape=jax.ShapeDtypeStruct(field.shape, F32),
        scratch_shapes=[pltpu.VMEM((count, hours), F32)],
        compiler_params=params(),
        name="finish",
    )(*notes, row_gauge.reshape(count, 1), *gathered, incidence, field)


def shifted(value, axis, by):
    devices = lax.axis_size(axis)
    pairs = [(i, i + by) for i in range(devices) if 0 <= i + by < devices]
    return lax.ppermute(value, axis, pairs)


def window(value):
    return jnp.concatenate([shifted(value, "tm", 1), value, shifted(value, "tm", -1)], axis=0)


def gathered_rows(value):
    owners = lax.axis_size("basin")
    copies = jnp.broadcast_to(value[None], (owners,) + value.shape)
    return lax.all_to_all(copies, "basin", 0, 0, tiled=False)


def over_hours(note):
    blocks = lax.axis_size("tm")
    result = note
    for by in range(1, blocks):
        result = result + lax.ppermute(note, "tm", [(i, (i + by) % blocks) for i in range(blocks)])
    return result


def shards(incidence, row_gauge, gauge_kernel, kernels, observed, first_guess):
    owners = lax.axis_size("basin")
    rows, hours = observed.shape
    gauges = rows * owners
    mats = transforms()
    spec = spectrum(gauge_kernel, kernels, mats[0])
    more = (lax.axis_index("tm") < lax.axis_size("tm") - 1).astype(F32).reshape(1)
    partial, gram = prepare(incidence, first_guess)
    all_gram = lax.all_gather(gram, "basin", axis=1, tiled=True)
    all_rows = lax.all_gather(row_gauge, "basin", axis=0, tiled=True)
    dense = table(row_gauge, partial, gauges).reshape(owners, rows, hours)
    sums = jnp.sum(lax.all_to_all(dense, "basin", 0, 0, tiled=False), axis=0)
    both = jnp.concatenate([observed, shifted(observed, "tm", -1)], axis=0)
    first = (lax.axis_index("basin") * rows).astype(jnp.int32).reshape(1)
    high, low = couple(first, all_rows, all_gram, rows, gauges)

    pulled, note = first_step(more, window(sums), both, spec, mats)
    notes, kept, state = [], [], None
    for k in range(3):
        everyone = gathered_rows(jnp.concatenate([pulled, note], axis=0))
        value = everyone[:, :rows].reshape(gauges, hours)
        notes.append(over_hours(jnp.sum(everyone[:, rows:], axis=0)))
        kept.append(value)
        around = window(mix(high, low, value))
        final = k == 2
        result = next_step(more, notes[-1], around, spec, mats, pulled, state, final)
        if final:
            (note,) = result
        else:
            state, pulled, note = result
    notes.append(over_hours(jnp.sum(gathered_rows(note), axis=0)))
    return finish(notes, row_gauge, kept, incidence, first_guess)


def solution(mesh):
    in_specs = (
        P("basin", None, None),
        P("basin"),
        P("basin"),
        P(),
        P("basin", "tm"),
        P("basin", "tm"),
    )
    return jax.shard_map(
        shards, mesh=mesh, in_specs=in_specs, out_specs=P("basin", "tm"), check_vma=False
    )
```

time: 1030 us -> 310 us (0.30)
  waiting for transfers between devices: 319 us -> 26.7 us
  local copies, waits for them, and re-layouts: 252 us -> 8.68 us
  blocking collectives: 279 us -> 131 us
  matrix products: 101 us -> 0 us
  Pallas kernels: 0 us -> 74.3 us
  starting transfers between devices: 30.8 us -> 54.4 us
  between operations: 19.4 us -> 0.26 us
    psum x7 -> x0, blocking collectives: 279 us -> none  [the longest x4 161 us: gauge_total(): return lax.psum(value, ('basin', 'tm'))]
    gather x7 -> x0, local copies, waits for them, and re-layouts: 251 us -> none  [the longest x4 244 us: lag_table(): picked = jnp.take(kernels, jnp.clip(lag, 0, taps - 1), axis=1)]
    reduce_scatter x4 -> x0, waiting for transfers between devices: 191 us -> none  [to_gauges(): return lax.psum_scatter(table, 'basin', scatter_dimension=0, tiled=True)]
    all_gather x3 -> x0, waiting for transfers between devices: 111 us -> none  [from_gauges(): everything = lax.all_gather(upstream, 'basin', axis=0, tiled=True)]
    dot_general x21 -> x0, matrix products: 101 us -> none  [the longest x7 39.2 us: class_mix(): jnp.dot(extended, table, precision=HIGH).reshape(gauges, classes, -1)]
    pallas_call x0 -> x12, Pallas kernels: none -> 74.3 us  [the longest x1 22.9 us: couple(): pl.pallas_call(couple_kernel, grid=(gauges // step,), in_specs=[pl.BlockS...]
    all_gather x0 -> x2, blocking collectives: none -> 66 us  [the longest x1 44.6 us: shards(): all_gram = lax.all_gather(gram, 'basin', axis=1, tiled=True)]
    all_to_all x0 -> x3, blocking collectives: none -> 65 us  [gathered_rows(): return lax.all_to_all(copies, 'basin', 0, 0, tiled=False)]
  transfers between devices with their start and end apart: 14 -> 23, of which waited for: 12 -> 8; matrix products, arithmetic and copies ran while one was open for 24% -> 3% of each run, Pallas kernels for 0% -> 12%
where the time goes in v1:
time: 310 us; the launch traced here: 307 us
  blocking collectives  131 us (42%)
  Pallas kernels  74.3 us (24%)
  starting transfers between devices  54.4 us (18%)
  waiting for transfers between devices  26.7 us (9%)
  other arithmetic  11.8 us (4%)
  local copies, waits for them, and re-layouts  8.68 us (3%)
    all_to_all x3, blocking collectives, gathered_rows(): return lax.all_to_all(copies, 'basin', 0, 0, tiled=False)  65 us
    all_gather x1, blocking collectives, shards(): all_gram = lax.all_gather(gram, 'basin', axis=1, tiled=True)  44.6 us
    ppermute x9, starting transfers between devices, shifted(): return lax.ppermute(value, axis, pairs)  29.8 us
    pallas_call x1, Pallas kernels, couple(): pl.pallas_call(couple_kernel, grid=(gauges // step,), in_specs=[pl.BlockS...  22.9 us
    all_to_all x1, waiting for transfers between devices, shards(): sums = jnp.sum(lax.all_to_all(dense, 'basin', 0, 0, tiled=False), axis=0)  21.7 us
    all_gather x1, blocking collectives, shards(): all_rows = lax.all_gather(row_gauge, 'basin', axis=0, tiled=True)  21.4 us
    ppermute x12, starting transfers between devices, over_hours(): lax.ppermute(note, 'tm', [(i, (i + by) % blocks) for i in range(blocks)])  14.4 us
    pallas_call x3, Pallas kernels, next_step(): pl.pallas_call(functools.partial(step_kernel, opening, final), in_specs=[...  13.9 us
  transfers between devices with their start and end apart: 23, of which 8 were waited for; matrix products, arithmetic and copies ran while one was open for 3% of the time, Pallas kernels for 12%

profile of v1, /device:TPU:1, one launch (start us, length us, event | category | flops | bytes accessed | tf_op | source)
XLA Modules:
  0.0 307.1 jit_solution(2563699020721428012)
XLA Ops:
  0.0 4.1 %prepare.1 = (f32[512,128]{1,0:T(8,128)}, f32[16,512]{1,0:T(8,128)}) custom-call(s32[32,16,128]{2,1,0:T(8,128)} %inc_ref.3, f32[4096,128]{1,0:T(8,128)} %field_ref.3), custom_call_target="tpu_custom_call" | custom-call | tf_op jit(solution)/shard_map/prepare/pallas_call | solution.py:75
  4.1 5.5 %table.1 = f32[2048,128]{1,0:T(8,128)} custom-call(s32[1,512]{1,0:T(1,128)} %bitcast.21, f32[512,128]{1,0:T(8,128)} %get-tuple-element.17.partial_ref), custom_call_target="tpu_custom_call" | custom-call | tf_op jit(solution)/shard_map/table/pallas_call | solution.py:107
  9.6 6.5 %all-to-all-start = ((f32[8,256,128]{2,1,0:T(8,128)}), f32[8,256,128]{2,1,0:T(8,128)S(1)}, u32[]{:S(2)}, u32[]{:S(2)}) async-start(f32[8,256,128]{2,1,0:T(8,128)} %bitcast.18), calls=%async_computation | async-start | bytes 2097152 | tf_op jit(solution)/shard_map/all_to_all | solution.py:462
  16.1 2.9 collective-permute-start.2
  19.0 21.7 %all-to-all-done = f32[8,256,128]{2,1,0:T(8,128)S(1)} async-done(((f32[8,256,128]{2,1,0:T(8,128)}), f32[8,256,128]{2,1,0:T(8,128)S(1)}, u32[]{:S(2)}, u32[]{:S(2)}) %all-to-all-start) | async-done | bytes 1048608 | tf_op jit(solution)/shard_map/all_to_all | solution.py:462
  40.8 4.0 %collective-permute-start.1 = (f32[256,128]{1,0:T(8,128)S(1)}, f32[256,128]{1,0:T(8,128)S(1)}, u32[]{:S(2)}, u32[]{:S(2)}) collective-permute-start(f32[256,128]{1,0:T(8,128)S(1)} %reduce_sum.45), channel_id=1, source_target_pairs={{1,0},{2,1},{3,2},{5,4},{6,5},{7,6},{9,8},{10,9},{11,10},{13,12},{... | collective-permute-start | bytes 393224 | tf_op jit(solution)/shard_map/ppermute | solution.py:430
  44.8 3.0 collective-permute-start
  48.7 2.6 spectrum.1.spec_ref
  52.7 4.6 %first_step.1 = (f32[256,128]{1,0:T(8,128)}, f32[8,128]{1,0:T(8,128)}) custom-call(f32[1]{0:T(128)} %bitcast.more_ref, f32[768,128]{1,0:T(8,128)} %pad_maximum_fusion.sums_ref, f32[512,128]{1,0:T(8,128)} %pad_maximum_fusion.4.observed_ref, f32[256,256]{1,0:T(8,128)} %spectrum.1.spec_ref, f32[256,256]{1,0:T(8,128)} %constant.21.clone.forward_ref, ...), custom_call_target="tpu_custom_call" | custom-call | tf_op jit(solution)/shard_map/first_step/pallas_call | solution.py:267
  59.4 3.7 %all-to-all-start.1 = ((f32[8,264,128]{2,1,0:T(8,128)}), f32[8,264,128]{2,1,0:T(8,128)S(1)}, u32[]{:S(2)}, u32[]{:S(2)}) async-start(f32[8,264,128]{2,1,0:T(8,128)} %broadcast_in_dim.8), calls=%async_computation.1 | async-start | bytes 2162688 | tf_op jit(solution)/shard_map/all_to_all | solution.py:440
  63.1 44.6 %all_gather.7.gram_ref = f32[16,4096]{1,0:T(8,128)} all-gather(f32[16,512]{1,0:T(8,128)S(1)} %copy-done.2), channel_id=1, replica_groups=mesh['basin'=8,'tm'=4] {'basin'}, dimensions={1}, use_global_device_ids=true | all-gather | bytes 294912 | tf_op jit(solution)/shard_map/all_gather | solution.py:459
  107.7 5.2 %collective-permute-start.5 = (f32[8,128]{1,0:T(8,128)S(1)}, f32[8,128]{1,0:T(8,128)S(1)}, u32[]{:S(2)}, u32[]{:S(2)}) collective-permute-start(f32[8,128]{1,0:T(8,128)S(1)} %slice_reduce_fusion.2), channel_id=1, source_target_pairs={{0,3},{1,0},{2,1},{3,2},{4,7},{5,4},{6,5},{7,6},{8,11},{9,8},{10,9... | collective-permute-start | bytes 12296 | tf_op jit(solution)/shard_map/ppermute | solution.py:447
  114.6 21.4 %all-gather = s32[8,1,512]{2,1,0:T(1,128)S(1)} all-gather(s32[1,1,512]{2,1,0:T(1,128)S(1)} %bitcast.22), channel_id=1, replica_groups=mesh['basin'=8,'tm'=4] {'basin'}, dimensions={0}, use_global_device_ids=true | all-gather | bytes 18432 | tf_op jit(solution)/shard_map/all_gather | solution.py:460
  136.0 2.0 copy.17.sub_ref
  138.0 22.9 %couple.1 = (bf16[256,2048]{1,0:T(8,128)(2,1)}, bf16[256,2048]{1,0:T(8,128)(2,1)}) custom-call(s32[1]{0:T(128)} %bitcast.4.first_ref, s32[1,4096]{1,0:T(1,128)} %bitcast.20, s32[4096,1]{1,0:T(8,128)} %copy.17.sub_ref, f32[16,4096]{1,0:T(8,128)} %all_gather.7.gram_ref), custom_call_target="tpu_custom_call" | custom-call | tf_op jit(solution)/shard_map/couple/pallas_call | solution.py:163
  162.0 4.1 %mix.3 = f32[256,128]{1,0:T(8,128)} custom-call(bf16[256,2048]{1,0:T(8,128)(2,1)} %get-tuple-element.21.high_ref, bf16[256,2048]{1,0:T(8,128)(2,1)} %get-tuple-element.22.low_ref, f32[2048,128]{1,0:T(8,128)} %bitcast.12), custom_call_target="tpu_custom_call" | custom-call | tf_op jit(solution)/shard_map/mix/pallas_call | solution.py:188
  166.0 5.3 %collective-permute-start.7 = (f32[256,128]{1,0:T(8,128)}, f32[256,128]{1,0:T(8,128)S(1)}, u32[]{:S(2)}, u32[]{:S(2)}) collective-permute-start(f32[256,128]{1,0:T(8,128)} %mix.3), channel_id=1, source_target_pairs={{1,0},{2,1},{3,2},{5,4},{6,5},{7,6},{9,8},{10,9},{11,10},{13,12},{... | collective-permute-start | bytes 393224 | tf_op jit(solution)/shard_map/ppermute | solution.py:430
  171.4 3.3 %collective-permute-start.6 = (f32[256,128]{1,0:T(8,128)}, f32[256,128]{1,0:T(8,128)S(1)}, u32[]{:S(2)}, u32[]{:S(2)}) collective-permute-start(f32[256,128]{1,0:T(8,128)} %mix.3), channel_id=1, source_target_pairs={{0,1},{1,2},{2,3},{4,5},{5,6},{6,7},{8,9},{9,10},{10,11},{12,13},{... | collective-permute-start | bytes 393224 | tf_op jit(solution)/shard_map/ppermute | solution.py:430
  178.6 4.7 %next_step.3 = (f32[2048,128]{1,0:T(8,128)}, f32[256,128]{1,0:T(8,128)}, f32[8,128]{1,0:T(8,128)}) custom-call(f32[1]{0:T(128)} %bitcast.more_ref, f32[8,128]{1,0:T(8,128)} %add_add_fusion.3.note_ref.n0, f32[768,128]{1,0:T(8,128)} %pad_maximum_fusion.1.sums_ref, f32[256,256]{1,0:T(8,128)} %spectrum.1.spec_ref, f32[256,256]{1,0:T(8,128)} %constant.21.clone.forward_ref, ...), custom_call_target="tpu_custom_call" | custom-call | tf_op jit(solution)/shard_map/next_step/pallas_call | solution.py:335
  184.3 28.4 %all_to_all.25 = f32[8,264,128]{2,1,0:T(8,128)S(1)} all-to-all(f32[8,264,128]{2,1,0:T(8,128)S(1)} %broadcast_in_dim.9), channel_id=1, replica_groups=mesh['basin'=8,'tm'=4] {'basin'}, dimensions={0} | all-to-all | bytes 2162688 | tf_op jit(solution)/shard_map/all_to_all | solution.py:440
  215.6 4.1 %mix.4 = f32[256,128]{1,0:T(8,128)} custom-call(bf16[256,2048]{1,0:T(8,128)(2,1)} %get-tuple-element.21.high_ref, bf16[256,2048]{1,0:T(8,128)(2,1)} %get-tuple-element.22.low_ref, f32[2048,128]{1,0:T(8,128)} %bitcast.14), custom_call_target="tpu_custom_call" | custom-call | tf_op jit(solution)/shard_map/mix/pallas_call | solution.py:188
  219.6 2.3 collective-permute-start.12
  221.9 3.5 %collective-permute-start.11 = (f32[256,128]{1,0:T(8,128)}, f32[256,128]{1,0:T(8,128)S(1)}, u32[]{:S(2)}, u32[]{:S(2)}) collective-permute-start(f32[256,128]{1,0:T(8,128)} %mix.4), channel_id=1, source_target_pairs={{0,1},{1,2},{2,3},{4,5},{5,6},{6,7},{8,9},{9,10},{10,11},{12,13},{... | collective-permute-start | bytes 393224 | tf_op jit(solution)/shard_map/ppermute | solution.py:430
  229.1 5.1 %next_step.4 = (f32[2048,128]{1,0:T(8,128)}, f32[256,128]{1,0:T(8,128)}, f32[8,128]{1,0:T(8,128)}) custom-call(f32[1]{0:T(128)} %bitcast.more_ref, f32[8,128]{1,0:T(8,128)} %add_add_fusion.2.note_ref.n1, f32[768,128]{1,0:T(8,128)} %pad_maximum_fusion.2.sums_ref, f32[256,256]{1,0:T(8,128)} %spectrum.1.spec_ref, f32[256,256]{1,0:T(8,128)} %constant.21.clone.forward_ref, ...), custom_call_target="tpu_custom_call" | custom-call | tf_op jit(solution)/shard_map/next_step/pallas_call | solution.py:335
  235.2 28.6 %all_to_all.26 = f32[8,264,128]{2,1,0:T(8,128)S(1)} all-to-all(f32[8,264,128]{2,1,0:T(8,128)S(1)} %broadcast_in_dim.10), channel_id=1, replica_groups=mesh['basin'=8,'tm'=4] {'basin'}, dimensions={0} | all-to-all | bytes 2162688 | tf_op jit(solution)/shard_map/all_to_all | solution.py:440
  266.7 4.1 %mix.5 = f32[256,128]{1,0:T(8,128)} custom-call(bf16[256,2048]{1,0:T(8,128)(2,1)} %get-tuple-element.21.high_ref, bf16[256,2048]{1,0:T(8,128)(2,1)} %get-tuple-element.22.low_ref, f32[2048,128]{1,0:T(8,128)} %bitcast.16), custom_call_target="tpu_custom_call" | custom-call | tf_op jit(solution)/shard_map/mix/pallas_call | solution.py:188
  270.8 2.2 collective-permute-start.17
  273.0 3.3 %collective-permute-start.16 = (f32[256,128]{1,0:T(8,128)}, f32[256,128]{1,0:T(8,128)S(1)}, u32[]{:S(2)}, u32[]{:S(2)}) collective-permute-start(f32[256,128]{1,0:T(8,128)} %mix.5), channel_id=1, source_target_pairs={{0,1},{1,2},{2,3},{4,5},{5,6},{6,7},{8,9},{9,10},{10,11},{12,13},{... | collective-permute-start | bytes 393224 | tf_op jit(solution)/shard_map/ppermute | solution.py:430
  280.2 4.1 %next_step.5 = f32[8,128]{1,0:T(8,128)} custom-call(f32[1]{0:T(128)} %bitcast.more_ref, f32[8,128]{1,0:T(8,128)} %add_add_fusion.1.note_ref.n2, f32[768,128]{1,0:T(8,128)} %pad_maximum_fusion.3.sums_ref, f32[256,256]{1,0:T(8,128)} %spectrum.1.spec_ref, f32[256,256]{1,0:T(8,128)} %constant.21.clone.forward_ref, f32[256,128]{1,0:T(8,128)} %constant.22.clone.first_ref, ...), custom_call_target="tpu_custom_call" | custom-call | tf_op jit(solution)/shard_map/next_step/pallas_call | solution.py:335
  285.0 8.0 %all_to_all.27 = f32[8,8,128]{2,1,0:T(8,128)S(1)} all-to-all(f32[8,8,128]{2,1,0:T(8,128)S(1)} %broadcast_in_dim.11), channel_id=1, replica_groups=mesh['basin'=8,'tm'=4] {'basin'}, dimensions={0} | all-to-all | bytes 65536 | tf_op jit(solution)/shard_map/all_to_all | solution.py:440
  293.0 3.9 %collective-permute-start.19 = (f32[8,128]{1,0:T(8,128)S(1)}, f32[8,128]{1,0:T(8,128)S(1)}, u32[]{:S(2)}, u32[]{:S(2)}) collective-permute-start(f32[8,128]{1,0:T(8,128)S(1)} %reduce_sum.49), channel_id=1, source_target_pairs={{0,2},{1,3},{2,0},{3,1},{4,6},{5,7},{6,4},{7,5},{8,10},{9,11},{10,... | collective-permute-start | bytes 12296 | tf_op jit(solution)/shard_map/ppermute | solution.py:447
  298.6 8.5 %finish.1 = f32[4096,128]{1,0:T(8,128)} custom-call(f32[8,128]{1,0:T(8,128)} %add_add_fusion.3.note_ref.n0, f32[8,128]{1,0:T(8,128)} %add_add_fusion.2.note_ref.n1, f32[8,128]{1,0:T(8,128)} %add_add_fusion.1.note_ref.n2, f32[8,128]{1,0:T(8,128)} %add_add_fusion.n3, s32[512,1]{1,0:T(8,128)} %copy.18.gauge_ref, f32[2048,128]{1,0:T(8,128)} %bitcast.13, ...), custom_call_target="tpu_custom_call" | custom-call | tf_op jit(solution)/shard_map/finish/pallas_call | solution.py:409
  (68 shorter events, 28.8 us)
Async XLA Ops:
  9.6 6.5 %copy-start.1 = (f32[256,128]{1,0:T(8,128)S(1)}, f32[256,128]{1,0:T(8,128)}, u32[]{:S(2)}) copy-start(f32[256,128]{1,0:T(8,128)} %param.13) | copy-start | bytes 393220
  9.6 31.1 %all-to-all-start = ((f32[8,256,128]{2,1,0:T(8,128)}), f32[8,256,128]{2,1,0:T(8,128)S(1)}, u32[]{:S(2)}, u32[]{:S(2)}) async-start(f32[8,256,128]{2,1,0:T(8,128)} %bitcast.18), calls=%async_computation | async-start | bytes 2097152 | tf_op jit(solution)/shard_map/all_to_all | solution.py:462
  16.1 31.8 %copy-start.4 = (s32[256]{0:T(256)S(1)}, s32[256]{0:T(256)}, u32[]{:S(2)}) copy-start(s32[256]{0:T(256)} %param.11) | copy-start | bytes 3076
  16.1 35.1 %collective-permute-start.2 = (f32[256,128]{1,0:T(8,128)S(1)}, f32[256,128]{1,0:T(8,128)S(1)}, u32[]{:S(2)}, u32[]{:S(2)}) collective-permute-start(f32[256,128]{1,0:T(8,128)S(1)} %copy-done.1), channel_id=1, source_target_pairs={{1,0},{2,1},{3,2},{5,4},{6,5},{7,6},{9,8},{10,9},{11,10},{13,12},{... | collective-permute-start | bytes 393224 | tf_op jit(solution)/shard_map/ppermute | solution.py:430
  40.8 11.2 %collective-permute-start.1 = (f32[256,128]{1,0:T(8,128)S(1)}, f32[256,128]{1,0:T(8,128)S(1)}, u32[]{:S(2)}, u32[]{:S(2)}) collective-permute-start(f32[256,128]{1,0:T(8,128)S(1)} %reduce_sum.45), channel_id=1, source_target_pairs={{1,0},{2,1},{3,2},{5,4},{6,5},{7,6},{9,8},{10,9},{11,10},{13,12},{... | collective-permute-start | bytes 393224 | tf_op jit(solution)/shard_map/ppermute | solution.py:430
  44.8 7.2 %collective-permute-start = (f32[256,128]{1,0:T(8,128)S(1)}, f32[256,128]{1,0:T(8,128)S(1)}, u32[]{:S(2)}, u32[]{:S(2)}) collective-permute-start(f32[256,128]{1,0:T(8,128)S(1)} %reduce_sum.45), channel_id=1, source_target_pairs={{0,1},{1,2},{2,3},{4,5},{5,6},{6,7},{8,9},{9,10},{10,11},{12,13},{... | collective-permute-start | bytes 393224 | tf_op jit(solution)/shard_map/ppermute | solution.py:430
  59.4 3.7 %copy-start.2 = (f32[16,512]{1,0:T(8,128)S(1)}, f32[16,512]{1,0:T(8,128)}, u32[]{:S(2)}) copy-start(f32[16,512]{1,0:T(8,128)} %get-tuple-element.20) | copy-start | bytes 98308
  59.4 55.3 %copy-start.3 = (s32[512]{0:T(512)S(1)}, s32[512]{0:T(512)}, u32[]{:S(2)}) copy-start(s32[512]{0:T(512)} %param.10) | copy-start | bytes 6148
  59.4 48.3 %all-to-all-start.1 = ((f32[8,264,128]{2,1,0:T(8,128)}), f32[8,264,128]{2,1,0:T(8,128)S(1)}, u32[]{:S(2)}, u32[]{:S(2)}) async-start(f32[8,264,128]{2,1,0:T(8,128)} %broadcast_in_dim.8), calls=%async_computation.1 | async-start | bytes 2162688 | tf_op jit(solution)/shard_map/all_to_all | solution.py:440
  107.7 67.0 %collective-permute-start.5 = (f32[8,128]{1,0:T(8,128)S(1)}, f32[8,128]{1,0:T(8,128)S(1)}, u32[]{:S(2)}, u32[]{:S(2)}) collective-permute-start(f32[8,128]{1,0:T(8,128)S(1)} %slice_reduce_fusion.2), channel_id=1, source_target_pairs={{0,3},{1,0},{2,1},{3,2},{4,7},{5,4},{6,5},{7,6},{8,11},{9,8},{10,9... | collective-permute-start | bytes 12296 | tf_op jit(solution)/shard_map/ppermute | solution.py:447
  112.9 61.7 %collective-permute-start.4 = (f32[8,128]{1,0:T(8,128)S(1)}, f32[8,128]{1,0:T(8,128)S(1)}, u32[]{:S(2)}, u32[]{:S(2)}) collective-permute-start(f32[8,128]{1,0:T(8,128)S(1)} %slice_reduce_fusion.2), channel_id=1, source_target_pairs={{0,2},{1,3},{2,0},{3,1},{4,6},{5,7},{6,4},{7,5},{8,10},{9,11},{10,... | collective-permute-start | bytes 12296 | tf_op jit(solution)/shard_map/ppermute | solution.py:447
  112.9 61.8 %collective-permute-start.3 = (f32[8,128]{1,0:T(8,128)S(1)}, f32[8,128]{1,0:T(8,128)S(1)}, u32[]{:S(2)}, u32[]{:S(2)}) collective-permute-start(f32[8,128]{1,0:T(8,128)S(1)} %slice_reduce_fusion.2), channel_id=1, source_target_pairs={{0,1},{1,2},{2,3},{3,0},{4,5},{5,6},{6,7},{7,4},{8,9},{9,10},{10,1... | collective-permute-start | bytes 12296 | tf_op jit(solution)/shard_map/ppermute | solution.py:447
  136.0 2.0 copy-start
  166.0 9.5 %collective-permute-start.7 = (f32[256,128]{1,0:T(8,128)}, f32[256,128]{1,0:T(8,128)S(1)}, u32[]{:S(2)}, u32[]{:S(2)}) collective-permute-start(f32[256,128]{1,0:T(8,128)} %mix.3), channel_id=1, source_target_pairs={{1,0},{2,1},{3,2},{5,4},{6,5},{7,6},{9,8},{10,9},{11,10},{13,12},{... | collective-permute-start | bytes 393224 | tf_op jit(solution)/shard_map/ppermute | solution.py:430
  171.4 5.5 %collective-permute-start.6 = (f32[256,128]{1,0:T(8,128)}, f32[256,128]{1,0:T(8,128)S(1)}, u32[]{:S(2)}, u32[]{:S(2)}) collective-permute-start(f32[256,128]{1,0:T(8,128)} %mix.3), channel_id=1, source_target_pairs={{0,1},{1,2},{2,3},{4,5},{5,6},{6,7},{8,9},{9,10},{10,11},{12,13},{... | collective-permute-start | bytes 393224 | tf_op jit(solution)/shard_map/ppermute | solution.py:430
  212.7 12.7 %collective-permute-start.10 = (f32[8,128]{1,0:T(8,128)S(1)}, f32[8,128]{1,0:T(8,128)S(1)}, u32[]{:S(2)}, u32[]{:S(2)}) collective-permute-start(f32[8,128]{1,0:T(8,128)S(1)} %slice_reduce_fusion.1), channel_id=1, source_target_pairs={{0,3},{1,0},{2,1},{3,2},{4,7},{5,4},{6,5},{7,6},{8,11},{9,8},{10,9... | collective-permute-start | bytes 12296 | tf_op jit(solution)/shard_map/ppermute | solution.py:447
  212.7 12.7 %collective-permute-start.9 = (f32[8,128]{1,0:T(8,128)S(1)}, f32[8,128]{1,0:T(8,128)S(1)}, u32[]{:S(2)}, u32[]{:S(2)}) collective-permute-start(f32[8,128]{1,0:T(8,128)S(1)} %slice_reduce_fusion.1), channel_id=1, source_target_pairs={{0,2},{1,3},{2,0},{3,1},{4,6},{5,7},{6,4},{7,5},{8,10},{9,11},{10,... | collective-permute-start | bytes 12296 | tf_op jit(solution)/shard_map/ppermute | solution.py:447
  214.3 11.1 %collective-permute-start.8 = (f32[8,128]{1,0:T(8,128)S(1)}, f32[8,128]{1,0:T(8,128)S(1)}, u32[]{:S(2)}, u32[]{:S(2)}) collective-permute-start(f32[8,128]{1,0:T(8,128)S(1)} %slice_reduce_fusion.1), channel_id=1, source_target_pairs={{0,1},{1,2},{2,3},{3,0},{4,5},{5,6},{6,7},{7,4},{8,9},{9,10},{10,1... | collective-permute-start | bytes 12296 | tf_op jit(solution)/shard_map/ppermute | solution.py:447
  219.6 6.5 %collective-permute-start.12 = (f32[256,128]{1,0:T(8,128)}, f32[256,128]{1,0:T(8,128)S(1)}, u32[]{:S(2)}, u32[]{:S(2)}) collective-permute-start(f32[256,128]{1,0:T(8,128)} %mix.4), channel_id=1, source_target_pairs={{1,0},{2,1},{3,2},{5,4},{6,5},{7,6},{9,8},{10,9},{11,10},{13,12},{... | collective-permute-start | bytes 393224 | tf_op jit(solution)/shard_map/ppermute | solution.py:430
  221.9 5.5 %collective-permute-start.11 = (f32[256,128]{1,0:T(8,128)}, f32[256,128]{1,0:T(8,128)S(1)}, u32[]{:S(2)}, u32[]{:S(2)}) collective-permute-start(f32[256,128]{1,0:T(8,128)} %mix.4), channel_id=1, source_target_pairs={{0,1},{1,2},{2,3},{4,5},{5,6},{6,7},{8,9},{9,10},{10,11},{12,13},{... | collective-permute-start | bytes 393224 | tf_op jit(solution)/shard_map/ppermute | solution.py:430
  263.9 12.5 %collective-permute-start.15 = (f32[8,128]{1,0:T(8,128)S(1)}, f32[8,128]{1,0:T(8,128)S(1)}, u32[]{:S(2)}, u32[]{:S(2)}) collective-permute-start(f32[8,128]{1,0:T(8,128)S(1)} %slice_reduce_fusion), channel_id=1, source_target_pairs={{0,3},{1,0},{2,1},{3,2},{4,7},{5,4},{6,5},{7,6},{8,11},{9,8},{10,9... | collective-permute-start | bytes 12296 | tf_op jit(solution)/shard_map/ppermute | solution.py:447
  263.9 12.5 %collective-permute-start.14 = (f32[8,128]{1,0:T(8,128)S(1)}, f32[8,128]{1,0:T(8,128)S(1)}, u32[]{:S(2)}, u32[]{:S(2)}) collective-permute-start(f32[8,128]{1,0:T(8,128)S(1)} %slice_reduce_fusion), channel_id=1, source_target_pairs={{0,2},{1,3},{2,0},{3,1},{4,6},{5,7},{6,4},{7,5},{8,10},{9,11},{10,... | collective-permute-start | bytes 12296 | tf_op jit(solution)/shard_map/ppermute | solution.py:447
  265.0 11.4 %collective-permute-start.13 = (f32[8,128]{1,0:T(8,128)S(1)}, f32[8,128]{1,0:T(8,128)S(1)}, u32[]{:S(2)}, u32[]{:S(2)}) collective-permute-start(f32[8,128]{1,0:T(8,128)S(1)} %slice_reduce_fusion), channel_id=1, source_target_pairs={{0,1},{1,2},{2,3},{3,0},{4,5},{5,6},{6,7},{7,4},{8,9},{9,10},{10,1... | collective-permute-start | bytes 12296 | tf_op jit(solution)/shard_map/ppermute | solution.py:447
  270.8 6.5 %collective-permute-start.17 = (f32[256,128]{1,0:T(8,128)}, f32[256,128]{1,0:T(8,128)S(1)}, u32[]{:S(2)}, u32[]{:S(2)}) collective-permute-start(f32[256,128]{1,0:T(8,128)} %mix.5), channel_id=1, source_target_pairs={{1,0},{2,1},{3,2},{5,4},{6,5},{7,6},{9,8},{10,9},{11,10},{13,12},{... | collective-permute-start | bytes 393224 | tf_op jit(solution)/shard_map/ppermute | solution.py:430
  273.0 5.6 %collective-permute-start.16 = (f32[256,128]{1,0:T(8,128)}, f32[256,128]{1,0:T(8,128)S(1)}, u32[]{:S(2)}, u32[]{:S(2)}) collective-permute-start(f32[256,128]{1,0:T(8,128)} %mix.5), channel_id=1, source_target_pairs={{0,1},{1,2},{2,3},{4,5},{5,6},{6,7},{8,9},{9,10},{10,11},{12,13},{... | collective-permute-start | bytes 393224 | tf_op jit(solution)/shard_map/ppermute | solution.py:430
  293.0 5.1 %collective-permute-start.20 = (f32[8,128]{1,0:T(8,128)S(1)}, f32[8,128]{1,0:T(8,128)S(1)}, u32[]{:S(2)}, u32[]{:S(2)}) collective-permute-start(f32[8,128]{1,0:T(8,128)S(1)} %reduce_sum.49), channel_id=1, source_target_pairs={{0,3},{1,0},{2,1},{3,2},{4,7},{5,4},{6,5},{7,6},{8,11},{9,8},{10,9... | collective-permute-start | bytes 12296 | tf_op jit(solution)/shard_map/ppermute | solution.py:447
  293.0 5.1 %collective-permute-start.19 = (f32[8,128]{1,0:T(8,128)S(1)}, f32[8,128]{1,0:T(8,128)S(1)}, u32[]{:S(2)}, u32[]{:S(2)}) collective-permute-start(f32[8,128]{1,0:T(8,128)S(1)} %reduce_sum.49), channel_id=1, source_target_pairs={{0,2},{1,3},{2,0},{3,1},{4,6},{5,7},{6,4},{7,5},{8,10},{9,11},{10,... | collective-permute-start | bytes 12296 | tf_op jit(solution)/shard_map/ppermute | solution.py:447
  296.9 1.2 collective-permute-start.18

commit v2 on v1

--- a/solution.py
+++ b/solution.py
@@ -482,7 +482,517 @@
     return finish(notes, row_gauge, kept, incidence, first_guess)
 
 
+Z_, X_, Y_, C_ = 4, 2, 2, 2
+NOTE = 8
+
+
+def device(z, x, y, c):
+    return (z * X_ + x) * (Y_ * C_) + y * C_ + c
+
+
+def moved(value, where):
+    pairs = []
+    for z, x, y, c in np.ndindex(Z_, X_, Y_, C_):
+        target = where(z, x, y, c)
+        if target is not None:
+            pairs.append((device(z, x, y, c), device(*target)))
+    return lax.ppermute(value, ("basin", "tm"), pairs)
+
+
+def to_plane(z, x, y, c):
+    return 2 * y + c, x, z & 1, z >> 1
+
+
+def to_plane_before(z, x, y, c):
+    t = 2 * y + c
+    return (t - 1, x, z & 1, z >> 1) if t else None
+
+
+def from_plane(z, x, y, c):
+    return 2 * c + y, x, z >> 1, z & 1
+
+
+def over_x(z, x, y, c):
+    return z, 1 - x, y, c
+
+
+def over_y(z, x, y, c):
+    return z, x, 1 - y, c
+
+
+def over_xy(z, x, y, c):
+    return z, 1 - x, 1 - y, c
+
+
+def over_core(z, x, y, c):
+    return z, x, y, 1 - c
+
+
+def z_pair(z, x, y, c):
+    return z ^ 1, x, y, c
+
+
+def z_middle(z, x, y, c):
+    return (3 - z, x, y, c) if z in (1, 2) else None
+
+
+def z_two(z, x, y, c):
+    return z ^ 2, x, y, c
+
+
+def z_mirror(z, x, y, c):
+    return 3 - z, x, y, c
+
+
+SQUARE = (over_x, over_y, over_xy)
+
+
+def split_constant(value):
+    out = []
+    for _ in range(3):
+        piece = value.astype(jnp.bfloat16)
+        out.append(jnp.asarray(piece))
+        value = value - piece.astype(np.float64)
+    return out
+
+
+def turned_transforms():
+    half = SPAN // 2
+    freq = 2.0 * np.pi * (np.arange(half) + 0.5) / SPAN
+    phase = freq[:, None] * np.arange(SPAN)[None, :]
+    forward = np.concatenate([np.cos(phase), -np.sin(phase)], axis=0)
+    inverse = forward.T * (2.0 / SPAN)
+    return split_constant(forward), split_constant(inverse[:half]), split_constant(inverse[half:])
+
+
+def product(mats, value, order):
+    parts = pieces(value, order)
+    result = None
+    for level in reversed(range(order)):
+        for i in range(level + 1):
+            term = dot(mats[i][...], parts[level - i])
+            result = term if result is None else result + term
+    return result
+
+
+def turn(waves, spec, sign):
+    half = waves.shape[0] // 2
+    real, imag = waves[:half], waves[half:]
+    kr, ki = spec[:half], spec[half:] * sign
+    return jnp.concatenate([real * kr - imag * ki, real * ki + imag * kr], axis=0)
+
+
+def plane_delayed(before, here, after, spec, forward, last, order):
+    out = []
+    for pair in ((before, here), (here, after)):
+        waves = product(forward, jnp.concatenate(pair, axis=0), order)
+        out.append(product(last, turn(waves, spec, 1.0), order))
+    return out
+
+
+def plane_advanced(here, after, spec, forward, first, order):
+    waves = product(forward, jnp.concatenate([here, after], axis=0), order)
+    return product(first, turn(waves, spec, -1.0), order)
+
+
+def send_kernel(inc_ref, field_ref, gauge_ref, out_ref):
+    blocks, slots, width = inc_ref.shape
+    rows = blocks * slots
+    hours = field_ref.shape[1]
+    weights = inc_ref[...].astype(F32).astype(BF16)
+    parts = []
+    for b in range(blocks):
+        parts.append(pick(weights[b], field_ref[pl.ds(b * width, width), :]))
+    out_ref[pl.ds(0, hours), :] = jnp.transpose(jnp.concatenate(parts, axis=0))
+    flat = weights.reshape(rows, width)
+    full = lax.dot_general(flat, flat, (((1,), (1,)), ((), ())), preferred_element_type=F32)
+    row = lax.broadcasted_iota(jnp.int32, (rows, rows), 0)
+    col = lax.broadcasted_iota(jnp.int32, (rows, rows), 1)
+    own = jnp.where(row // slots == col // slots, full, 0.0)
+    out_ref[pl.ds(hours, slots), :] = jnp.sum(own.reshape(blocks, slots, rows), axis=0)
+    out_ref[pl.ds(hours + slots, 8), :] = jnp.broadcast_to(gauge_ref[...].astype(F32), (8, rows))
+
+
+def send(incidence, field, row_gauge):
+    blocks, slots, width = incidence.shape
+    hours = field.shape[1]
+    step = 8
+    height = hours + slots + 8
+    return pl.pallas_call(
+        send_kernel,
+        grid=(blocks // step,),
+        in_specs=[
+            pl.BlockSpec((step, slots, width), lambda i: (i, 0, 0)),
+            pl.BlockSpec((step * width, hours), lambda i: (i, 0)),
+            pl.BlockSpec((1, step * slots), lambda i: (0, i)),
+        ],
+        out_specs=pl.BlockSpec((height, step * slots), lambda i: (0, i)),
+        out_shape=jax.ShapeDtypeStruct((height, blocks * slots), F32),
+        compiler_params=params(),
+        name="send",
+    )(incidence, field, row_gauge.reshape(1, blocks * slots))
+
+
+def hot_rows(gauge, first, rows):
+    mine = (lax.broadcasted_iota(jnp.int32, (rows, gauge.shape[1]), 0) + first).astype(F32)
+    return jnp.where(gauge == mine, 1.0, 0.0).astype(BF16)
+
+
+def spread_kernel(first_ref, mine_ref, other_ref, *out_refs):
+    hours, rows = out_refs[0].shape
+    slots = mine_ref.shape[0] - hours - 8
+    where = hours + slots
+    for m, out_ref in enumerate(out_refs):
+        result = None
+        for ref in (mine_ref, other_ref):
+            hot = hot_rows(ref[where : where + 1, :], first_ref[m], rows)
+            for piece in reversed(pieces(ref[pl.ds(0, hours), :], 3)):
+                term = lax.dot_general(
+                    piece, hot, (((1,), (1,)), ((), ())), preferred_element_type=F32
+                )
+                result = term if result is None else result + term
+        out_ref[...] = result
+
+
+def spread(first, mine, other, hours, rows):
+    return pl.pallas_call(
+        spread_kernel,
+        in_specs=[pl.BlockSpec(memory_space=pltpu.SMEM)] + [pl.BlockSpec(memory_space=pltpu.VMEM)] * 2,
+        out_shape=[jax.ShapeDtypeStruct((hours, rows), F32)] * 4,
+        compiler_params=params(),
+        name="spread",
+    )(first, mine, other)
+
+
+def plane_couple_kernel(first_ref, a_ref, b_ref, c_ref, d_ref, high_ref, low_ref, total_ref, meta_ref):
+    height, double = a_ref.shape
+    slots = height - 8
+    count = double // 2
+    cols, rows = high_ref.shape
+    part = cols // 4
+    tile = 256
+    for i, ref in enumerate((a_ref, b_ref, c_ref, d_ref)):
+        for j in range(2):
+            meta_ref[2 * i + j] = ref[:, j * count : (j + 1) * count]
+    row = lax.broadcasted_iota(jnp.int32, (tile, tile), 0)
+    col = lax.broadcasted_iota(jnp.int32, (tile, tile), 1)
+    same = row // slots == col // slots
+    total_ref[...] = jnp.zeros_like(total_ref)
+
+    def body(i, carry):
+        gauge = meta_ref[i, slots : slots + 1, :]
+        near = []
+        for j in range(count // tile):
+            here = slice(j * tile, (j + 1) * tile)
+            block = jnp.concatenate([meta_ref[i, :slots, here]] * (tile // slots), axis=0)
+            block = jnp.where(same, block, 0.0).astype(BF16)
+            mine = jnp.concatenate(
+                [hot_rows(gauge[:, here], first_ref[4 + h], rows // 2) for h in range(2)], axis=0
+            )
+            near.append(
+                lax.dot_general(block, mine, (((1,), (1,)), ((), ())), preferred_element_type=F32)
+            )
+        near = jnp.concatenate(near, axis=0)
+        high = near.astype(BF16)
+        rest = near - high.astype(F32)
+        hot = jnp.concatenate([hot_rows(gauge, first_ref[m], part) for m in range(4)], axis=0)
+        total_ref[...] += dot(hot, high)
+
+        @pl.when(jnp.max(jnp.abs(rest)) > 0.0)
+        def _():
+            total_ref[...] += dot(hot, rest.astype(BF16))
+
+        return carry
+
+    lax.fori_loop(0, 8, body, 0)
+    high, low = pieces(total_ref[...], 2)
+    high_ref[...] = high
+    low_ref[...] = low
+
+
+def plane_couple(first, metas, rows):
+    height, double = metas[0].shape
+    return pl.pallas_call(
+        plane_couple_kernel,
+        in_specs=[pl.BlockSpec(memory_space=pltpu.SMEM)] + [pl.BlockSpec(memory_space=pltpu.VMEM)] * 4,
+        out_shape=[jax.ShapeDtypeStruct((4 * rows, 2 * rows), BF16)] * 2,
+        scratch_shapes=[
+            pltpu.VMEM((4 * rows, 2 * rows), F32),
+            pltpu.VMEM((8, height, double // 2), F32),
+        ],
+        compiler_params=params(),
+        name="plane_couple",
+        cost_estimate=pl.CostEstimate(flops=14_000_000_000, bytes_accessed=4_000_000, transcendentals=0),
+    )(first, *metas)
+
+
+def plane_mix_kernel(high_ref, low_ref, a_ref, b_ref, c_ref, d_ref, mine_ref, other_ref):
+    refs = (a_ref, b_ref, c_ref, d_ref)
+    height, rows = a_ref.shape
+    hours = height - NOTE
+    value = jnp.concatenate([ref[pl.ds(0, hours), :] for ref in refs], axis=1)
+    one, two = pieces(value, 2)
+    high, low = high_ref[...], low_ref[...]
+    result = (dot(two, high) + dot(one, low)) + dot(one, high)
+    note = sum(ref[pl.ds(hours, NOTE), :] for ref in refs)
+    mine_ref[pl.ds(0, hours), :] = result[:, :rows]
+    other_ref[pl.ds(0, hours), :] = result[:, rows:]
+    mine_ref[pl.ds(hours, NOTE), :] = note
+    other_ref[pl.ds(hours, NOTE), :] = note
+
+
+def plane_mix(high, low, values):
+    return pl.pallas_call(
+        plane_mix_kernel,
+        out_shape=[jax.ShapeDtypeStruct(values[0].shape, F32)] * 2,
+        compiler_params=params(),
+        name="plane_mix",
+    )(high, low, *values)
+
+
+def plane_rows_kernel(first_ref, mine_ref, other_ref, a_ref, b_ref, c_ref, d_ref, out_mine_ref, out_other_ref):
+    height, rows = a_ref.shape
+    hours = height - NOTE
+    where = mine_ref.shape[0] - 8
+    for ref, out_ref in ((mine_ref, out_mine_ref), (other_ref, out_other_ref)):
+        gauge = ref[where : where + 1, :]
+        result = None
+        for m, value_ref in enumerate((a_ref, b_ref, c_ref, d_ref)):
+            hot = hot_rows(gauge, first_ref[m], rows)
+            for piece in reversed(pieces(value_ref[pl.ds(0, hours), :], 2)):
+                term = dot(piece, hot)
+                result = term if result is None else result + term
+        out_ref[...] = result
+
+
+def plane_rows(first, mine, other, values):
+    hours = values[0].shape[0] - NOTE
+    slots = mine.shape[1]
+    return pl.pallas_call(
+        plane_rows_kernel,
+        in_specs=[pl.BlockSpec(memory_space=pltpu.SMEM)] + [pl.BlockSpec(memory_space=pltpu.VMEM)] * 6,
+        out_shape=[jax.ShapeDtypeStruct((hours, slots), F32)] * 2,
+        compiler_params=params(),
+        name="plane_rows",
+        cost_estimate=pl.CostEstimate(flops=1_000_000_000, bytes_accessed=2_000_000, transcendentals=0),
+    )(first, mine, other, *values)
+
+
+def plane_spectrum_kernel(class_ref, kernels_ref, f0_ref, f1_ref, f2_ref, out_ref):
+    classes, taps = kernels_ref.shape
+    kind = jnp.concatenate([class_ref[0:1, :], class_ref[1:2, :]], axis=1)
+    hot = jnp.where(
+        lax.broadcasted_iota(jnp.int32, (classes, kind.shape[1]), 0).astype(F32) == kind, 1.0, 0.0
+    ).astype(BF16)
+    chosen = None
+    for piece in reversed(pieces(jnp.transpose(kernels_ref[...]), 3)):
+        term = dot(piece, hot)
+        chosen = term if chosen is None else chosen + term
+    mats = [ref[:, :taps] for ref in (f0_ref, f1_ref, f2_ref)]
+    out_ref[...] = product(mats, chosen, 3)
+
+
+def plane_spectrum(kinds, kernels, forward):
+    return pl.pallas_call(
+        plane_spectrum_kernel,
+        out_shape=jax.ShapeDtypeStruct((SPAN, 2 * kinds.shape[1]), F32),
+        compiler_params=params(),
+        name="plane_spectrum",
+    )(kinds, kernels, *forward)
+
+
+def sides(even, pair, middle):
+    return jnp.where(even, middle, pair), jnp.where(even, pair, middle)
+
+
+def plane_first_kernel(
+    flag_ref, here_ref, pair_ref, middle_ref, seen_ref, seen_later_ref, spec_ref, *refs
+):
+    *mats, out_ref = refs
+    forward, first, last = mats[0:3], mats[3:6], mats[6:9]
+    hours, rows = here_ref.shape
+    spec = spec_ref[...]
+    before, after = sides(flag_ref[0] > 0.5, pair_ref[...], middle_ref[...])
+    now, later = plane_delayed(before, here_ref[...], after, spec, forward, last, 3)
+    start = jnp.transpose(seen_ref[pl.ds(0, rows), :]) - now
+    start_later = (jnp.transpose(seen_later_ref[...]) - later) * flag_ref[1]
+    out_ref[pl.ds(0, hours), :] = plane_advanced(start, start_later, spec, forward, first, 3)
+    out_ref[pl.ds(hours, NOTE), :] = jnp.concatenate(
+        [lanes(start, start), jnp.zeros((NOTE - 1, rows), F32)], axis=0
+    )
+
+
+def plane_first(flags, sums, seen, seen_later, spec, mats):
+    hours, rows = sums[0].shape
+    args = [flags, *sums, seen, seen_later, spec, *mats]
+    return pl.pallas_call(
+        plane_first_kernel,
+        in_specs=[pl.BlockSpec(memory_space=pltpu.SMEM)]
+        + [pl.BlockSpec(memory_space=pltpu.VMEM)] * (len(args) - 1),
+        out_shape=jax.ShapeDtypeStruct((hours + NOTE, rows), F32),
+        compiler_params=params(),
+        name="plane_first",
+    )(*args)
+
+
+def plane_step_kernel(opening, final, flag_ref, here_ref, pair_ref, middle_ref, two_ref, mirror_ref, pulled_ref, spec_ref, *refs):
+    mats, refs = refs[:9], refs[9:]
+    forward, first, last = mats[0:3], mats[3:6], mats[6:9]
+    if not opening:
+        state_ref, *refs = refs
+    if final:
+        total_ref, out_ref = refs
+    else:
+        total_ref, out_ref, new_ref = refs
+    height, rows = pulled_ref.shape
+    hours = height - NOTE
+    tail, body = pl.ds(hours, NOTE), pl.ds(0, hours)
+    total_ref[...] = (here_ref[tail, :] + pair_ref[tail, :]) + (two_ref[...] + mirror_ref[...])
+    spec = spec_ref[...]
+    pulled = pulled_ref[body, :]
+    sums = [ref[body, :] for ref in (here_ref, pair_ref, middle_ref)]
+    if opening:
+        scale = 1.0 / jnp.sqrt(total(total_ref, 0))
+        new_su = [value * scale for value in sums]
+        new_s = new_su
+        new_zu = pulled * scale
+        new_z = new_zu
+    else:
+        alpha, beta = ratios(total_ref)
+        a, b, g = 1.0 / (alpha * beta), alpha / beta, beta / alpha
+        old = lambda i: state_ref[pl.ds(i * hours, hours), :]
+        new_su = [value * a - old(3 + i) * b for i, value in enumerate(sums)]
+        new_s = [value - old(i) * g for i, value in enumerate(new_su)]
+        new_zu = pulled * a - old(7) * b
+        new_z = new_zu - old(6) * g
+    here = new_s[0]
+    before, after = sides(flag_ref[0] > 0.5, new_s[1], new_s[2])
+    now, later = plane_delayed(before, here, after, spec, forward, last, 2)
+    note = jnp.concatenate(
+        [lanes(new_z, here), lanes(now, now), lanes(new_zu, here), jnp.zeros((NOTE - 3, rows), F32)],
+        axis=0,
+    )
+    if final:
+        out_ref[...] = note[:, : rows // 2] + note[:, rows // 2 :]
+    else:
+        for i, value in enumerate(new_s + new_su + [new_z, new_zu]):
+            new_ref[pl.ds(i * hours, hours), :] = value
+        out_ref[body, :] = plane_advanced(now, later * flag_ref[1], spec, forward, first, 2)
+        out_ref[tail, :] = note
+
+
+def plane_step(flags, sums, two, mirror, pulled, spec, mats, state, final):
+    height, rows = pulled.shape
+    hours = height - NOTE
+    opening = state is None
+    args = [flags, *sums, two, mirror, pulled, spec, *mats] + ([] if opening else [state])
+    out = [jax.ShapeDtypeStruct((NOTE, rows), F32)]
+    if final:
+        out += [jax.ShapeDtypeStruct((NOTE, rows // 2), F32)]
+    else:
+        out += [jax.ShapeDtypeStruct((height, rows), F32), jax.ShapeDtypeStruct((8 * hours, rows), F32)]
+    return pl.pallas_call(
+        functools.partial(plane_step_kernel, opening, final),
+        in_specs=[pl.BlockSpec(memory_space=pltpu.SMEM)]
+        + [pl.BlockSpec(memory_space=pltpu.VMEM)] * (len(args) - 1),
+        out_shape=out,
+        compiler_params=params(),
+        name="plane_step",
+    )(*args)
+
+
+def plane_finish_kernel(n0, n1, n2, n3, q0, q1, q2, inc_ref, field_ref, out_ref, rows_ref):
+    blocks, slots, width = inc_ref.shape
+    step = pl.program_id(0)
+
+    @pl.when(step == 0)
+    def _():
+        e0, e1, e2 = weights_of([n0, n1, n2, n3])
+        rows_ref[...] = jnp.transpose(q0[...] * e0 + q1[...] * e1 + q2[...] * e2)
+
+    weights = inc_ref[...].astype(F32).astype(BF16)
+    for b in range(blocks):
+        here = pl.ds(b * width, width)
+        rows = rows_ref[pl.ds(pl.multiple_of((step * blocks + b) * slots, slots), slots), :]
+        added = sum(
+            lax.dot_general(weights[b], piece, (((0,), (0,)), ((), ())), preferred_element_type=F32)
+            for piece in pieces(rows, 2)
+        )
+        out_ref[here, :] = field_ref[here, :] + added
+
+
+def plane_finish(notes, rows, incidence, field):
+    blocks, slots, width = incidence.shape
+    hours = field.shape[1]
+    step = 8
+    whole = lambda shape: pl.BlockSpec(shape, lambda i: (0, 0))
+    return pl.pallas_call(
+        plane_finish_kernel,
+        grid=(blocks // step,),
+        in_specs=[whole(n.shape) for n in notes]
+        + [whole(q.shape) for q in rows]
+        + [
+            pl.BlockSpec((step, slots, width), lambda i: (i, 0, 0)),
+            pl.BlockSpec((step * width, hours), lambda i: (i, 0)),
+        ],
+        out_specs=pl.BlockSpec((step * width, hours), lambda i: (i, 0)),
+        out_shape=jax.ShapeDtypeStruct(field.shape, F32),
+        scratch_shapes=[pltpu.VMEM((blocks * slots, hours), F32)],
+        compiler_params=params(),
+        name="plane_finish",
+    )(*notes, *rows, incidence, field)
+
+
+def plane_shards(incidence, row_gauge, gauge_kernel, kernels, observed, first_guess):
+    rows, hours = observed.shape
+    slots = incidence.shape[1]
+    basin, tm = lax.axis_index("basin"), lax.axis_index("tm")
+    z, x, y, c = basin // X_, basin % X_, tm // C_, tm % C_
+    place = 2 * y + x
+    first = jnp.stack([4 * c + (place ^ m) for m in range(4)] + [4 * c + place, 4 * (1 - c) + place])
+    first = (first * rows).astype(jnp.int32)
+    flags = jnp.stack([1 - z % 2, (z < Z_ - 1).astype(z.dtype)]).astype(F32)
+    forward, inverse_first, inverse_last = turned_transforms()
+    mats = [*forward, *inverse_first, *inverse_last]
+
+    kinds = gauge_kernel.astype(F32).reshape(rows // hours, hours)
+    parcel = moved(send(incidence, first_guess, row_gauge), to_plane)
+    seen, kinds, parcel = lax.optimization_barrier((observed, kinds, parcel))
+    seen_later = moved(seen, to_plane_before)
+    seen = moved(jnp.concatenate([seen, kinds, jnp.zeros((8 - kinds.shape[0], hours), F32)]), to_plane)
+    spec = plane_spectrum(seen[rows : rows + kinds.shape[0]], kernels, forward)
+
+    beside = moved(parcel, over_core)
+    meta = jnp.concatenate([parcel[hours:], beside[hours:]], axis=1)
+    metas = [meta] + [moved(meta, where) for where in SQUARE]
+    dense = spread(first, parcel, beside, hours, rows)
+    sums = dense[0] + sum(moved(value, where) for value, where in zip(dense[1:], SQUARE))
+    sums = [sums, moved(sums, z_pair), moved(sums, z_middle)]
+    high, low = plane_couple(first, metas, rows)
+    pulled = plane_first(flags, sums, seen, seen_later, spec, mats)
+    notes, kept, state = [], [], None
+    for k in range(3):
+        values = [pulled] + [moved(pulled, where) for where in SQUARE]
+        mine, other = plane_mix(high, low, values)
+        mixed = mine + moved(other, over_core)
+        note = mixed[hours:]
+        sums = [mixed, moved(mixed, z_pair), moved(mixed, z_middle)]
+        two, mirror = moved(note, z_two), moved(note, z_mirror)
+        rows_mine, rows_other = plane_rows(first, parcel, beside, values)
+        kept.append(moved(rows_mine + moved(rows_other, over_core), from_plane))
+        result = plane_step(flags, sums, two, mirror, pulled, spec, mats, state, k == 2)
+        if k == 2:
+            total_note, last = result
+        else:
+            total_note, pulled, state = result
+        notes.append(total_note)
+    copies = jnp.broadcast_to(last[None], (Z_ * X_ * Y_ * C_,) + last.shape)
+    notes.append(jnp.sum(lax.all_to_all(copies, ("basin", "tm"), 0, 0, tiled=False), axis=0))
+    return plane_finish(notes, kept, incidence, first_guess)
+
+
 def solution(mesh):
+    planes = dict(mesh.shape) == {"basin": Z_ * X_, "tm": Y_ * C_}
     in_specs = (
         P("basin", None, None),
         P("basin"),
@@ -492,5 +1002,5 @@
         P("basin", "tm"),
     )
     return jax.shard_map(
-        shards, mesh=mesh, in_specs=in_specs, out_specs=P("basin", "tm"), check_vma=False
+        plane_shards if planes else shards, mesh=mesh, in_specs=in_specs, out_specs=P("basin", "tm"), check_vma=False
     )

time: 310 us -> 191 us (0.62)
  blocking collectives: 131 us -> 17 us
  Pallas kernels: 74.3 us -> 59.8 us
  starting transfers between devices: 54.4 us -> 62.5 us
  other arithmetic: 11.8 us -> 4.81 us
  waiting for transfers between devices: 26.7 us -> 32.7 us
  local copies, waits for them, and re-layouts: 8.68 us -> 12.4 us
    all_gather x2 -> x0, blocking collectives: 66 us -> none  [the longest x1 44.6 us: shards(): all_gram = lax.all_gather(gram, 'basin', axis=1, tiled=True)]
    all_to_all x3 -> x1, blocking collectives: 65 us -> 17 us  [plane_shards(): lax.all_to_all(copies, ('basin', 'tm'), 0, 0, tiled=False)]
    ppermute x21 -> x42, waiting for transfers between devices: 4.98 us -> 32.7 us  [moved(): return lax.ppermute(value, ('basin', 'tm'), pairs)]
    all_to_all x2 -> x0, waiting for transfers between devices: 21.7 us -> none  [the longest x1 21.7 us: shards(): sums = jnp.sum(lax.all_to_all(dense, 'basin', 0, 0, tiled=False), axis=0)]
    ppermute x21 -> x42, starting transfers between devices: 44.2 us -> 62.5 us  [moved(): return lax.ppermute(value, ('basin', 'tm'), pairs)]
    pallas_call x12 -> x15, Pallas kernels: 74.3 us -> 59.8 us  [the longest x3 12 us: plane_step(): pl.pallas_call(functools.partial(plane_step_kernel, opening, final), in_s...]
    all_to_all x2 -> x0, starting transfers between devices: 10.2 us -> none  [the longest x1 6.48 us: shards(): sums = jnp.sum(lax.all_to_all(dense, 'basin', 0, 0, tiled=False), axis=0)]
    unnamed x10 -> x88, local copies, waits for them, and re-layouts: 0.02 us -> 10.2 us
  transfers between devices with their start and end apart: 23 -> 42, of which waited for: 8 -> 10; matrix products, arithmetic and copies ran while one was open for 3% -> 3% of each run, Pallas kernels for 12% -> 19%
where the time goes in v2:
time: 191 us; the launch traced here: 190 us
  starting transfers between devices  62.5 us (33%)
  Pallas kernels  59.8 us (31%)
  waiting for transfers between devices  32.7 us (17%)
  blocking collectives  17 us (9%)
  local copies, waits for them, and re-layouts  12.4 us (6%)
  other arithmetic  4.81 us (3%)
    ppermute x42, starting transfers between devices, moved(): return lax.ppermute(value, ('basin', 'tm'), pairs)  62.5 us
    ppermute x42, waiting for transfers between devices, moved(): return lax.ppermute(value, ('basin', 'tm'), pairs)  32.7 us
    all_to_all x1, blocking collectives, plane_shards(): lax.all_to_all(copies, ('basin', 'tm'), 0, 0, tiled=False)  17 us
    pallas_call x3, Pallas kernels, plane_step(): pl.pallas_call(functools.partial(plane_step_kernel, opening, final), in_s...  12 us
    pallas_call x1, Pallas kernels, plane_couple(): pl.pallas_call(plane_couple_kernel, in_specs=[pl.BlockSpec(memory_space=p...  10.5 us
    unnamed x88, local copies, waits for them, and re-layouts  10.2 us
    pallas_call x3, Pallas kernels, plane_mix(): pl.pallas_call(plane_mix_kernel, out_shape=[jax.ShapeDtypeStruct(values[0...  8.85 us
    pallas_call x3, Pallas kernels, plane_rows(): pl.pallas_call(plane_rows_kernel, in_specs=[pl.BlockSpec(memory_space=plt...  8.29 us
  transfers between devices with their start and end apart: 42, of which 10 were waited for; matrix products, arithmetic and copies ran while one was open for 3% of the time, Pallas kernels for 19%

profile of v2, /device:TPU:1, one launch (start us, length us, event | category | flops | bytes accessed | tf_op | source)
XLA Modules:
  0.0 189.8 jit_solution(6363561979164376360)
XLA Ops:
  0.0 4.3 %send.1 = f32[152,512]{1,0:T(8,128)} custom-call(s32[32,16,128]{2,1,0:T(8,128)} %inc_ref.3, f32[4096,128]{1,0:T(8,128)} %field_ref.3, s32[1,512]{1,0:T(1,128)} %bitcast.10), custom_call_target="tpu_custom_call" | custom-call | tf_op jit(solution)/shard_map/send/pallas_call | solution.py:621
  4.3 4.6 %collective-permute-start = (f32[152,512]{1,0:T(8,128)}, f32[152,512]{1,0:T(8,128)S(1)}, u32[]{:S(2)}, u32[]{:S(2)}) collective-permute-start(f32[152,512]{1,0:T(8,128)} %send.1), channel_id=1, source_target_pairs={{0,0},{1,8},{2,16},{3,24},{4,4},{5,12},{6,20},{7,28},{8,2},{9,10},... | collective-permute-start | bytes 933896 | tf_op jit(solution)/shard_map/ppermute | solution.py:499
  8.9 15.1 %collective-permute-done.mine_ref = f32[152,512]{1,0:T(8,128)S(1)} collective-permute-done((f32[152,512]{1,0:T(8,128)}, f32[152,512]{1,0:T(8,128)S(1)}, u32[]{:S(2)}, u32[]{:S(2)}) %collective-permute-start) | collective-permute-done | bytes 311328 | tf_op jit(solution)/shard_map/ppermute | solution.py:499
  24.7 2.4 %collective-permute-start.11 = (f32[256,128]{1,0:T(8,128)S(1)}, f32[256,128]{1,0:T(8,128)S(1)}, u32[]{:S(2)}, u32[]{:S(2)}) collective-permute-start(f32[256,128]{1,0:T(8,128)S(1)} %copy-done.32), channel_id=1, source_target_pairs={{1,0},{2,8},{3,16},{5,4},{6,12},{7,20},{9,2},{10,10},{11,18},{13,6... | collective-permute-start | bytes 393224 | tf_op jit(solution)/shard_map/ppermute | solution.py:499
  27.8 3.9 %spread.1 = (f32[128,256]{1,0:T(8,128)}, f32[128,256]{1,0:T(8,128)}, f32[128,256]{1,0:T(8,128)}, f32[128,256]{1,0:T(8,128)}) custom-call(s32[6]{0:T(128)} %broadcast_multiply_fusion.first_ref, f32[152,512]{1,0:T(8,128)} %copy-done.4, f32[152,512]{1,0:T(8,128)} %copy-done.5), custom_call_target="tpu_custom_call" | custom-call | tf_op jit(solution)/shard_map/spread/pallas_call | solution.py:658
  37.3 4.0 %collective-permute-done.6 = f32[128,256]{1,0:T(8,128)S(1)} collective-permute-done((f32[128,256]{1,0:T(8,128)}, f32[128,256]{1,0:T(8,128)S(1)}, u32[]{:S(2)}, u32[]{:S(2)}) %collective-permute-start.6) | collective-permute-done | bytes 131104 | tf_op jit(solution)/shard_map/ppermute | solution.py:499
  43.0 3.1 %collective-permute-start.8 = (f32[128,256]{1,0:T(8,128)S(1)}, f32[128,256]{1,0:T(8,128)S(1)}, u32[]{:S(2)}, u32[]{:S(2)}) collective-permute-start(f32[128,256]{1,0:T(8,128)S(1)} %add_add_fusion.here_ref), channel_id=1, source_target_pairs={{0,8},{1,9},{2,10},{3,11},{4,12},{5,13},{6,14},{7,15},{8,0},{9,1},... | collective-permute-start | bytes 393224 | tf_op jit(solution)/shard_map/ppermute | solution.py:499
  50.1 2.4 %plane_spectrum.1.spec_ref = f32[256,256]{1,0:T(8,128)} custom-call(f32[2,128]{1,0:T(2,128)} %slice.25.class_ref, f32[32,128]{1,0:T(8,128)} %kernels_ref.1, bf16[256,256]{1,0:T(8,128)(2,1)} %constant.76.clone.f0_ref.refs_0_, bf16[256,256]{1,0:T(8,128)(2,1)} %constant.77.clone.f1_ref.refs_1_, bf16[256,256]{1,0:T(8,128)(2,1)} %constant.78.clone.f2_ref.refs_2_), custom_call_target="tpu_custom_call" | custom-call | tf_op jit(solution)/shard_map/plane_spectrum/pallas_call | solution.py:796
  53.9 4.5 %plane_first.1.a_ref.pulled_ref = f32[136,256]{1,0:T(8,128)} custom-call(f32[2]{0:T(128)} %add_convert_fusion.flag_ref, f32[128,256]{1,0:T(8,128)} %copy-done.3, f32[128,256]{1,0:T(8,128)} %copy-done.31, f32[128,256]{1,0:T(8,128)} %copy-done.30, f32[264,128]{1,0:T(8,128)} %copy-done.28, f32[256,128]{1,0:T(8,128)} %copy-done.29, ...), custom_call_target="tpu_custom_call" | custom-call | tf_op jit(solution)/shard_map/plane_first/pallas_call | solution.py:828
  62.3 10.5 %plane_couple.1 = (bf16[1024,512]{1,0:T(8,128)(2,1)}, bf16[1024,512]{1,0:T(8,128)(2,1)}) custom-call(s32[6]{0:T(128)} %broadcast_multiply_fusion.first_ref, f32[24,1024]{1,0:T(8,128)} %copy-done.33, f32[24,1024]{1,0:T(8,128)} %copy-done.43, f32[24,1024]{1,0:T(8,128)} %copy-done.42, f32[24,1024]{1,0:T(8,128)} %copy-done.41), custom_call_target="tpu_custom_call" | custom-call | flops 14000000000 | bytes 4000000 | tf_op jit(solution)/shard_map/plane_couple/pallas_call | solution.py:715
  73.6 3.0 %plane_mix.3 = (f32[136,256]{1,0:T(8,128)}, f32[136,256]{1,0:T(8,128)}) custom-call(bf16[1024,512]{1,0:T(8,128)(2,1)} %get-tuple-element.35.high_ref, bf16[1024,512]{1,0:T(8,128)(2,1)} %get-tuple-element.36.low_ref, f32[136,256]{1,0:T(8,128)} %plane_first.1.a_ref.pulled_ref, f32[136,256]{1,0:T(8,128)} %copy-done.21, f32[136,256]{1,0:T(8,128)} %copy-done.20, ...), custom_call_target="tpu_custom_call" | custom-call | tf_op jit(solution)/shard_map/plane_mix/pallas_call | solution.py:745
  76.6 3.3 %collective-permute-start.15 = (f32[136,256]{1,0:T(8,128)}, f32[136,256]{1,0:T(8,128)S(1)}, u32[]{:S(2)}, u32[]{:S(2)}) collective-permute-start(f32[136,256]{1,0:T(8,128)} %get-tuple-element.44), channel_id=1, source_target_pairs={{0,1},{1,0},{2,3},{3,2},{4,5},{5,4},{6,7},{7,6},{8,9},{9,8},{10,11... | collective-permute-start | bytes 417800 | tf_op jit(solution)/shard_map/ppermute | solution.py:499
  82.7 2.5 %collective-permute-start.16 = (f32[136,256]{1,0:T(8,128)S(1)}, f32[136,256]{1,0:T(8,128)S(1)}, u32[]{:S(2)}, u32[]{:S(2)}) collective-permute-start(f32[136,256]{1,0:T(8,128)S(1)} %add.70.here_ref), channel_id=1, source_target_pairs={{0,8},{1,9},{2,10},{3,11},{4,12},{5,13},{6,14},{7,15},{8,0},{9,1},... | collective-permute-start | bytes 417800 | tf_op jit(solution)/shard_map/ppermute | solution.py:499
  86.5 3.1 %collective-permute-done.19.mirror_ref = f32[8,256]{1,0:T(8,128)S(1)} collective-permute-done((f32[8,256]{1,0:T(8,128)S(1)}, f32[8,256]{1,0:T(8,128)S(1)}, u32[]{:S(2)}, u32[]{:S(2)}) %collective-permute-start.19) | collective-permute-done | bytes 8224 | tf_op jit(solution)/shard_map/ppermute | solution.py:499
  90.9 4.2 %plane_step.3 = (f32[8,256]{1,0:T(8,128)}, f32[136,256]{1,0:T(8,128)}, f32[1024,256]{1,0:T(8,128)}) custom-call(f32[2]{0:T(128)} %add_convert_fusion.flag_ref, f32[136,256]{1,0:T(8,128)} %copy-done.2, f32[136,256]{1,0:T(8,128)} %copy-done.17, f32[136,256]{1,0:T(8,128)} %copy-done.15, f32[8,256]{1,0:T(8,128)} %copy-done.39, f32[8,256]{1,0:T(8,128)} %copy-done.37, ...), custom_call_target="tpu_custom_call" | custom-call | tf_op jit(solution)/shard_map/plane_step/pallas_call | solution.py:894
  97.8 2.5 %collective-permute-done.22.d_ref = f32[136,256]{1,0:T(8,128)S(1)} collective-permute-done((f32[136,256]{1,0:T(8,128)}, f32[136,256]{1,0:T(8,128)S(1)}, u32[]{:S(2)}, u32[]{:S(2)}) %collective-permute-start.22) | collective-permute-done | bytes 139296 | tf_op jit(solution)/shard_map/ppermute | solution.py:499
  103.5 2.9 %plane_mix.4 = (f32[136,256]{1,0:T(8,128)}, f32[136,256]{1,0:T(8,128)}) custom-call(bf16[1024,512]{1,0:T(8,128)(2,1)} %get-tuple-element.35.high_ref, bf16[1024,512]{1,0:T(8,128)(2,1)} %get-tuple-element.36.low_ref, f32[136,256]{1,0:T(8,128)} %get-tuple-element.46.a_ref.pulled_ref, f32[136,256]{1,0:T(8,128)} %copy-done.24, f32[136,256]{1,0:T(8,128)} %copy-done.23, ...), custom_call_target="tpu_custom_call" | custom-call | tf_op jit(solution)/shard_map/plane_mix/pallas_call | solution.py:745
  106.4 3.2 %collective-permute-start.23 = (f32[136,256]{1,0:T(8,128)}, f32[136,256]{1,0:T(8,128)S(1)}, u32[]{:S(2)}, u32[]{:S(2)}) collective-permute-start(f32[136,256]{1,0:T(8,128)} %get-tuple-element.48), channel_id=1, source_target_pairs={{0,1},{1,0},{2,3},{3,2},{4,5},{5,4},{6,7},{7,6},{8,9},{9,8},{10,11... | collective-permute-start | bytes 417800 | tf_op jit(solution)/shard_map/ppermute | solution.py:499
  112.7 2.5 %collective-permute-start.24 = (f32[136,256]{1,0:T(8,128)S(1)}, f32[136,256]{1,0:T(8,128)S(1)}, u32[]{:S(2)}, u32[]{:S(2)}) collective-permute-start(f32[136,256]{1,0:T(8,128)S(1)} %add.71.here_ref), channel_id=1, source_target_pairs={{0,8},{1,9},{2,10},{3,11},{4,12},{5,13},{6,14},{7,15},{8,0},{9,1},... | collective-permute-start | bytes 417800 | tf_op jit(solution)/shard_map/ppermute | solution.py:499
  116.7 3.0 %collective-permute-done.27.mirror_ref = f32[8,256]{1,0:T(8,128)S(1)} collective-permute-done((f32[8,256]{1,0:T(8,128)S(1)}, f32[8,256]{1,0:T(8,128)S(1)}, u32[]{:S(2)}, u32[]{:S(2)}) %collective-permute-start.27) | collective-permute-done | bytes 8224 | tf_op jit(solution)/shard_map/ppermute | solution.py:499
  120.8 4.6 %plane_step.4 = (f32[8,256]{1,0:T(8,128)}, f32[136,256]{1,0:T(8,128)}, f32[1024,256]{1,0:T(8,128)}) custom-call(f32[2]{0:T(128)} %add_convert_fusion.flag_ref, f32[136,256]{1,0:T(8,128)} %copy-done.1, f32[136,256]{1,0:T(8,128)} %copy-done.16, f32[136,256]{1,0:T(8,128)} %copy-done.14, f32[8,256]{1,0:T(8,128)} %copy-done.38, f32[8,256]{1,0:T(8,128)} %copy-done.36, ...), custom_call_target="tpu_custom_call" | custom-call | tf_op jit(solution)/shard_map/plane_step/pallas_call | solution.py:894
  128.1 2.8 %plane_rows.3 = (f32[128,512]{1,0:T(8,128)}, f32[128,512]{1,0:T(8,128)}) custom-call(s32[6]{0:T(128)} %broadcast_multiply_fusion.first_ref, f32[152,512]{1,0:T(8,128)} %copy-done.4, f32[152,512]{1,0:T(8,128)} %copy-done.5, f32[136,256]{1,0:T(8,128)} %plane_first.1.a_ref.pulled_ref, f32[136,256]{1,0:T(8,128)} %copy-done.21, f32[136,256]{1,0:T(8,128)} %copy-done.20, ...), custom_call_target="tpu_custom_call" | custom-call | flops 1000000000 | bytes 2000000 | tf_op jit(solution)/shard_map/plane_rows/pallas_call | solution.py:771
  130.9 3.2 %collective-permute-start.36 = (f32[128,512]{1,0:T(8,128)}, f32[128,512]{1,0:T(8,128)S(1)}, u32[]{:S(2)}, u32[]{:S(2)}) collective-permute-start(f32[128,512]{1,0:T(8,128)} %get-tuple-element.58), channel_id=1, source_target_pairs={{0,1},{1,0},{2,3},{3,2},{4,5},{5,4},{6,7},{7,6},{8,9},{9,8},{10,11... | collective-permute-start | bytes 786440 | tf_op jit(solution)/shard_map/ppermute | solution.py:499
  134.1 2.8 %plane_rows.4 = (f32[128,512]{1,0:T(8,128)}, f32[128,512]{1,0:T(8,128)}) custom-call(s32[6]{0:T(128)} %broadcast_multiply_fusion.first_ref, f32[152,512]{1,0:T(8,128)} %copy-done.4, f32[152,512]{1,0:T(8,128)} %copy-done.5, f32[136,256]{1,0:T(8,128)} %get-tuple-element.46.a_ref.pulled_ref, f32[136,256]{1,0:T(8,128)} %copy-done.24, f32[136,256]{1,0:T(8,128)} %copy-done.23, ...), custom_call_target="tpu_custom_call" | custom-call | flops 1000000000 | bytes 2000000 | tf_op jit(solution)/shard_map/plane_rows/pallas_call | solution.py:771
  138.2 2.9 %plane_mix.5 = (f32[136,256]{1,0:T(8,128)}, f32[136,256]{1,0:T(8,128)}) custom-call(bf16[1024,512]{1,0:T(8,128)(2,1)} %get-tuple-element.35.high_ref, bf16[1024,512]{1,0:T(8,128)(2,1)} %get-tuple-element.36.low_ref, f32[136,256]{1,0:T(8,128)} %get-tuple-element.51.a_ref.pulled_ref, f32[136,256]{1,0:T(8,128)} %copy-done.27, f32[136,256]{1,0:T(8,128)} %copy-done.26, ...), custom_call_target="tpu_custom_call" | custom-call | tf_op jit(solution)/shard_map/plane_mix/pallas_call | solution.py:745
  141.7 2.8 %plane_rows.5 = (f32[128,512]{1,0:T(8,128)}, f32[128,512]{1,0:T(8,128)}) custom-call(s32[6]{0:T(128)} %broadcast_multiply_fusion.first_ref, f32[152,512]{1,0:T(8,128)} %copy-done.4, f32[152,512]{1,0:T(8,128)} %copy-done.5, f32[136,256]{1,0:T(8,128)} %get-tuple-element.51.a_ref.pulled_ref, f32[136,256]{1,0:T(8,128)} %copy-done.27, f32[136,256]{1,0:T(8,128)} %copy-done.26, ...), custom_call_target="tpu_custom_call" | custom-call | flops 1000000000 | bytes 2000000 | tf_op jit(solution)/shard_map/plane_rows/pallas_call | solution.py:771
  148.6 5.7 %collective-permute-start.37 = (f32[128,512]{1,0:T(8,128)S(1)}, f32[128,512]{1,0:T(8,128)S(1)}, u32[]{:S(2)}, u32[]{:S(2)}) collective-permute-start(f32[128,512]{1,0:T(8,128)S(1)} %add.73), channel_id=1, source_target_pairs={{0,0},{1,16},{2,8},{3,24},{4,4},{5,20},{6,12},{7,28},{8,1},{9,17},... | collective-permute-start | bytes 786440 | tf_op jit(solution)/shard_map/ppermute | solution.py:499
  154.4 2.5 %collective-permute-start.39 = (f32[128,512]{1,0:T(8,128)S(1)}, f32[128,512]{1,0:T(8,128)S(1)}, u32[]{:S(2)}, u32[]{:S(2)}) collective-permute-start(f32[128,512]{1,0:T(8,128)S(1)} %add.74), channel_id=1, source_target_pairs={{0,0},{1,16},{2,8},{3,24},{4,4},{5,20},{6,12},{7,28},{8,1},{9,17},... | collective-permute-start | bytes 786440 | tf_op jit(solution)/shard_map/ppermute | solution.py:499
  156.9 4.7 %collective-permute-start.41 = (f32[128,512]{1,0:T(8,128)S(1)}, f32[128,512]{1,0:T(8,128)S(1)}, u32[]{:S(2)}, u32[]{:S(2)}) collective-permute-start(f32[128,512]{1,0:T(8,128)S(1)} %add.75), channel_id=1, source_target_pairs={{0,0},{1,16},{2,8},{3,24},{4,4},{5,20},{6,12},{7,28},{8,1},{9,17},... | collective-permute-start | bytes 786440 | tf_op jit(solution)/shard_map/ppermute | solution.py:499
  162.4 3.2 %plane_step.5 = (f32[8,256]{1,0:T(8,128)}, f32[8,128]{1,0:T(8,128)}) custom-call(f32[2]{0:T(128)} %add_convert_fusion.flag_ref, f32[136,256]{1,0:T(8,128)} %copy-done, f32[136,256]{1,0:T(8,128)} %copy-done.13, f32[136,256]{1,0:T(8,128)} %copy-done.12, f32[8,256]{1,0:T(8,128)} %copy-done.35, f32[8,256]{1,0:T(8,128)} %copy-done.34, ...), custom_call_target="tpu_custom_call" | custom-call | tf_op jit(solution)/shard_map/plane_step/pallas_call | solution.py:894
  166.3 17.0 %all_to_all.5 = f32[32,8,128]{2,1,0:T(8,128)S(1)} all-to-all(f32[32,8,128]{2,1,0:T(8,128)S(1)} %broadcast_in_dim.10), channel_id=1, replica_groups=mesh['basin'=8,'tm'=4] {'basin','tm'}, dimensions={0} | all-to-all | bytes 262144 | tf_op jit(solution)/shard_map/all_to_all | solution.py:990
  184.8 5.0 %plane_finish.1 = f32[4096,128]{1,0:T(8,128)} custom-call(f32[8,256]{1,0:T(8,128)} %get-tuple-element.45.n0, f32[8,256]{1,0:T(8,128)} %get-tuple-element.50.n1, f32[8,256]{1,0:T(8,128)} %get-tuple-element.55.n2, f32[8,128]{1,0:T(8,128)} %reduce_sum.9.n3, f32[128,512]{1,0:T(8,128)} %copy-done.8, f32[128,512]{1,0:T(8,128)} %copy-done.10, ...), custom_call_target="tpu_custom_call" | custom-call | tf_op jit(solution)/shard_map/plane_finish/pallas_call | solution.py:929
  (179 shorter events, 47.1 us)
Async XLA Ops:
  4.3 19.7 %collective-permute-start = (f32[152,512]{1,0:T(8,128)}, f32[152,512]{1,0:T(8,128)S(1)}, u32[]{:S(2)}, u32[]{:S(2)}) collective-permute-start(f32[152,512]{1,0:T(8,128)} %send.1), channel_id=1, source_target_pairs={{0,0},{1,8},{2,16},{3,24},{4,4},{5,12},{6,20},{7,28},{8,2},{9,10},... | collective-permute-start | bytes 933896 | tf_op jit(solution)/shard_map/ppermute | solution.py:499
  24.7 22.9 %collective-permute-start.11 = (f32[256,128]{1,0:T(8,128)S(1)}, f32[256,128]{1,0:T(8,128)S(1)}, u32[]{:S(2)}, u32[]{:S(2)}) collective-permute-start(f32[256,128]{1,0:T(8,128)S(1)} %copy-done.32), channel_id=1, source_target_pairs={{1,0},{2,8},{3,16},{5,4},{6,12},{7,20},{9,2},{10,10},{11,18},{13,6... | collective-permute-start | bytes 393224 | tf_op jit(solution)/shard_map/ppermute | solution.py:499
  31.8 5.6 %collective-permute-start.5 = (f32[128,256]{1,0:T(8,128)}, f32[128,256]{1,0:T(8,128)S(1)}, u32[]{:S(2)}, u32[]{:S(2)}) collective-permute-start(f32[128,256]{1,0:T(8,128)} %get-tuple-element.38), channel_id=1, source_target_pairs={{0,4},{1,5},{2,6},{3,7},{4,0},{5,1},{6,2},{7,3},{8,12},{9,13},{10,... | collective-permute-start | bytes 393224 | tf_op jit(solution)/shard_map/ppermute | solution.py:499
  33.0 8.4 %collective-permute-start.6 = (f32[128,256]{1,0:T(8,128)}, f32[128,256]{1,0:T(8,128)S(1)}, u32[]{:S(2)}, u32[]{:S(2)}) collective-permute-start(f32[128,256]{1,0:T(8,128)} %get-tuple-element.39), channel_id=1, source_target_pairs={{0,2},{1,3},{2,0},{3,1},{4,6},{5,7},{6,4},{7,5},{8,10},{9,11},{10,... | collective-permute-start | bytes 393224 | tf_op jit(solution)/shard_map/ppermute | solution.py:499
  33.6 7.8 %collective-permute-start.7 = (f32[128,256]{1,0:T(8,128)}, f32[128,256]{1,0:T(8,128)S(1)}, u32[]{:S(2)}, u32[]{:S(2)}) collective-permute-start(f32[128,256]{1,0:T(8,128)} %get-tuple-element.40), channel_id=1, source_target_pairs={{0,6},{1,7},{2,4},{3,5},{4,2},{5,3},{6,0},{7,1},{8,14},{9,15},{10,... | collective-permute-start | bytes 393224 | tf_op jit(solution)/shard_map/ppermute | solution.py:499
  34.5 14.4 %collective-permute-start.10 = (f32[264,128]{1,0:T(8,128)S(1)}, f32[264,128]{1,0:T(8,128)S(1)}, u32[]{:S(2)}, u32[]{:S(2)}) collective-permute-start(f32[264,128]{1,0:T(8,128)S(1)} %maximum_maximum_fusion), channel_id=1, source_target_pairs={{0,0},{1,8},{2,16},{3,24},{4,4},{5,12},{6,20},{7,28},{8,2},{9,10},... | collective-permute-start | bytes 405512 | tf_op jit(solution)/shard_map/ppermute | solution.py:499
  42.3 10.2 %collective-permute-start.9 = (f32[128,256]{1,0:T(8,128)S(1)}, f32[128,256]{1,0:T(8,128)S(1)}, u32[]{:S(2)}, u32[]{:S(2)}) collective-permute-start(f32[128,256]{1,0:T(8,128)S(1)} %add_add_fusion.here_ref), channel_id=1, source_target_pairs={{8,16},{9,17},{10,18},{11,19},{12,20},{13,21},{14,22},{15,23},{16,... | collective-permute-start | bytes 393224 | tf_op jit(solution)/shard_map/ppermute | solution.py:499
  43.0 9.5 %collective-permute-start.8 = (f32[128,256]{1,0:T(8,128)S(1)}, f32[128,256]{1,0:T(8,128)S(1)}, u32[]{:S(2)}, u32[]{:S(2)}) collective-permute-start(f32[128,256]{1,0:T(8,128)S(1)} %add_add_fusion.here_ref), channel_id=1, source_target_pairs={{0,8},{1,9},{2,10},{3,11},{4,12},{5,13},{6,14},{7,15},{8,0},{9,1},... | collective-permute-start | bytes 393224 | tf_op jit(solution)/shard_map/ppermute | solution.py:499
  46.1 14.9 %collective-permute-start.4 = (f32[24,1024]{1,0:T(8,128)S(1)}, f32[24,1024]{1,0:T(8,128)S(1)}, u32[]{:S(2)}, u32[]{:S(2)}) collective-permute-start(f32[24,1024]{1,0:T(8,128)S(1)} %pad_maximum_fusion.a_ref), channel_id=1, source_target_pairs={{0,6},{1,7},{2,4},{3,5},{4,2},{5,3},{6,0},{7,1},{8,14},{9,15},{10,... | collective-permute-start | bytes 294920 | tf_op jit(solution)/shard_map/ppermute | solution.py:499
  47.6 13.4 %collective-permute-start.3 = (f32[24,1024]{1,0:T(8,128)S(1)}, f32[24,1024]{1,0:T(8,128)S(1)}, u32[]{:S(2)}, u32[]{:S(2)}) collective-permute-start(f32[24,1024]{1,0:T(8,128)S(1)} %pad_maximum_fusion.a_ref), channel_id=1, source_target_pairs={{0,2},{1,3},{2,0},{3,1},{4,6},{5,7},{6,4},{7,5},{8,10},{9,11},{10,... | collective-permute-start | bytes 294920 | tf_op jit(solution)/shard_map/ppermute | solution.py:499
  48.9 12.2 %collective-permute-start.2 = (f32[24,1024]{1,0:T(8,128)S(1)}, f32[24,1024]{1,0:T(8,128)S(1)}, u32[]{:S(2)}, u32[]{:S(2)}) collective-permute-start(f32[24,1024]{1,0:T(8,128)S(1)} %pad_maximum_fusion.a_ref), channel_id=1, source_target_pairs={{0,4},{1,5},{2,6},{3,7},{4,0},{5,1},{6,2},{7,3},{8,12},{9,13},{10,... | collective-permute-start | bytes 294920 | tf_op jit(solution)/shard_map/ppermute | solution.py:499
  58.4 14.5 %collective-permute-start.14 = (f32[136,256]{1,0:T(8,128)}, f32[136,256]{1,0:T(8,128)S(1)}, u32[]{:S(2)}, u32[]{:S(2)}) collective-permute-start(f32[136,256]{1,0:T(8,128)} %plane_first.1.a_ref.pulled_ref), channel_id=1, source_target_pairs={{0,6},{1,7},{2,4},{3,5},{4,2},{5,3},{6,0},{7,1},{8,14},{9,15},{10,... | collective-permute-start | bytes 417800 | tf_op jit(solution)/shard_map/ppermute | solution.py:499
  59.7 13.1 %collective-permute-start.13 = (f32[136,256]{1,0:T(8,128)}, f32[136,256]{1,0:T(8,128)S(1)}, u32[]{:S(2)}, u32[]{:S(2)}) collective-permute-start(f32[136,256]{1,0:T(8,128)} %plane_first.1.a_ref.pulled_ref), channel_id=1, source_target_pairs={{0,2},{1,3},{2,0},{3,1},{4,6},{5,7},{6,4},{7,5},{8,10},{9,11},{10,... | collective-permute-start | bytes 417800 | tf_op jit(solution)/shard_map/ppermute | solution.py:499
  61.0 11.9 %collective-permute-start.12 = (f32[136,256]{1,0:T(8,128)}, f32[136,256]{1,0:T(8,128)S(1)}, u32[]{:S(2)}, u32[]{:S(2)}) collective-permute-start(f32[136,256]{1,0:T(8,128)} %plane_first.1.a_ref.pulled_ref), channel_id=1, source_target_pairs={{0,4},{1,5},{2,6},{3,7},{4,0},{5,1},{6,2},{7,3},{8,12},{9,13},{10,... | collective-permute-start | bytes 417800 | tf_op jit(solution)/shard_map/ppermute | solution.py:499
  82.0 7.6 %collective-permute-start.17 = (f32[136,256]{1,0:T(8,128)S(1)}, f32[136,256]{1,0:T(8,128)S(1)}, u32[]{:S(2)}, u32[]{:S(2)}) collective-permute-start(f32[136,256]{1,0:T(8,128)S(1)} %add.70.here_ref), channel_id=1, source_target_pairs={{8,16},{9,17},{10,18},{11,19},{12,20},{13,21},{14,22},{15,23},{16,... | collective-permute-start | bytes 417800 | tf_op jit(solution)/shard_map/ppermute | solution.py:499
  82.7 6.9 %collective-permute-start.16 = (f32[136,256]{1,0:T(8,128)S(1)}, f32[136,256]{1,0:T(8,128)S(1)}, u32[]{:S(2)}, u32[]{:S(2)}) collective-permute-start(f32[136,256]{1,0:T(8,128)S(1)} %add.70.here_ref), channel_id=1, source_target_pairs={{0,8},{1,9},{2,10},{3,11},{4,12},{5,13},{6,14},{7,15},{8,0},{9,1},... | collective-permute-start | bytes 417800 | tf_op jit(solution)/shard_map/ppermute | solution.py:499
  95.1 5.1 %collective-permute-start.22 = (f32[136,256]{1,0:T(8,128)}, f32[136,256]{1,0:T(8,128)S(1)}, u32[]{:S(2)}, u32[]{:S(2)}) collective-permute-start(f32[136,256]{1,0:T(8,128)} %get-tuple-element.46.a_ref.pulled_ref), channel_id=1, source_target_pairs={{0,6},{1,7},{2,4},{3,5},{4,2},{5,3},{6,0},{7,1},{8,14},{9,15},{10,... | collective-permute-start | bytes 417800 | tf_op jit(solution)/shard_map/ppermute | solution.py:499
  96.4 5.7 %collective-permute-start.21 = (f32[136,256]{1,0:T(8,128)}, f32[136,256]{1,0:T(8,128)S(1)}, u32[]{:S(2)}, u32[]{:S(2)}) collective-permute-start(f32[136,256]{1,0:T(8,128)} %get-tuple-element.46.a_ref.pulled_ref), channel_id=1, source_target_pairs={{0,2},{1,3},{2,0},{3,1},{4,6},{5,7},{6,4},{7,5},{8,10},{9,11},{10,... | collective-permute-start | bytes 417800 | tf_op jit(solution)/shard_map/ppermute | solution.py:499
  111.8 8.3 %collective-permute-start.25 = (f32[136,256]{1,0:T(8,128)S(1)}, f32[136,256]{1,0:T(8,128)S(1)}, u32[]{:S(2)}, u32[]{:S(2)}) collective-permute-start(f32[136,256]{1,0:T(8,128)S(1)} %add.71.here_ref), channel_id=1, source_target_pairs={{8,16},{9,17},{10,18},{11,19},{12,20},{13,21},{14,22},{15,23},{16,... | collective-permute-start | bytes 417800 | tf_op jit(solution)/shard_map/ppermute | solution.py:499
  112.7 7.4 %collective-permute-start.24 = (f32[136,256]{1,0:T(8,128)S(1)}, f32[136,256]{1,0:T(8,128)S(1)}, u32[]{:S(2)}, u32[]{:S(2)}) collective-permute-start(f32[136,256]{1,0:T(8,128)S(1)} %add.71.here_ref), channel_id=1, source_target_pairs={{0,8},{1,9},{2,10},{3,11},{4,12},{5,13},{6,14},{7,15},{8,0},{9,1},... | collective-permute-start | bytes 417800 | tf_op jit(solution)/shard_map/ppermute | solution.py:499
  125.4 11.4 %collective-permute-start.30 = (f32[136,256]{1,0:T(8,128)}, f32[136,256]{1,0:T(8,128)S(1)}, u32[]{:S(2)}, u32[]{:S(2)}) collective-permute-start(f32[136,256]{1,0:T(8,128)} %get-tuple-element.51.a_ref.pulled_ref), channel_id=1, source_target_pairs={{0,6},{1,7},{2,4},{3,5},{4,2},{5,3},{6,0},{7,1},{8,14},{9,15},{10,... | collective-permute-start | bytes 417800 | tf_op jit(solution)/shard_map/ppermute | solution.py:499
  126.3 10.5 %collective-permute-start.29 = (f32[136,256]{1,0:T(8,128)}, f32[136,256]{1,0:T(8,128)S(1)}, u32[]{:S(2)}, u32[]{:S(2)}) collective-permute-start(f32[136,256]{1,0:T(8,128)} %get-tuple-element.51.a_ref.pulled_ref), channel_id=1, source_target_pairs={{0,2},{1,3},{2,0},{3,1},{4,6},{5,7},{6,4},{7,5},{8,10},{9,11},{10,... | collective-permute-start | bytes 417800 | tf_op jit(solution)/shard_map/ppermute | solution.py:499
  127.6 9.3 %collective-permute-start.28 = (f32[136,256]{1,0:T(8,128)}, f32[136,256]{1,0:T(8,128)S(1)}, u32[]{:S(2)}, u32[]{:S(2)}) collective-permute-start(f32[136,256]{1,0:T(8,128)} %get-tuple-element.51.a_ref.pulled_ref), channel_id=1, source_target_pairs={{0,4},{1,5},{2,6},{3,7},{4,0},{5,1},{6,2},{7,3},{8,12},{9,13},{10,... | collective-permute-start | bytes 417800 | tf_op jit(solution)/shard_map/ppermute | solution.py:499
  130.9 16.0 %collective-permute-start.36 = (f32[128,512]{1,0:T(8,128)}, f32[128,512]{1,0:T(8,128)S(1)}, u32[]{:S(2)}, u32[]{:S(2)}) collective-permute-start(f32[128,512]{1,0:T(8,128)} %get-tuple-element.58), channel_id=1, source_target_pairs={{0,1},{1,0},{2,3},{3,2},{4,5},{5,4},{6,7},{7,6},{8,9},{9,8},{10,11... | collective-permute-start | bytes 786440 | tf_op jit(solution)/shard_map/ppermute | solution.py:499
  136.8 11.7 %collective-permute-start.38 = (f32[128,512]{1,0:T(8,128)}, f32[128,512]{1,0:T(8,128)S(1)}, u32[]{:S(2)}, u32[]{:S(2)}) collective-permute-start(f32[128,512]{1,0:T(8,128)} %get-tuple-element.60), channel_id=1, source_target_pairs={{0,1},{1,0},{2,3},{3,2},{4,5},{5,4},{6,7},{7,6},{8,9},{9,8},{10,11... | collective-permute-start | bytes 786440 | tf_op jit(solution)/shard_map/ppermute | solution.py:499
  144.6 17.0 %collective-permute-start.33 = (f32[136,256]{1,0:T(8,128)S(1)}, f32[136,256]{1,0:T(8,128)S(1)}, u32[]{:S(2)}, u32[]{:S(2)}) collective-permute-start(f32[136,256]{1,0:T(8,128)S(1)} %add.72.here_ref), channel_id=1, source_target_pairs={{8,16},{9,17},{10,18},{11,19},{12,20},{13,21},{14,22},{15,23},{16,... | collective-permute-start | bytes 417800 | tf_op jit(solution)/shard_map/ppermute | solution.py:499
  145.3 16.4 %collective-permute-start.32 = (f32[136,256]{1,0:T(8,128)S(1)}, f32[136,256]{1,0:T(8,128)S(1)}, u32[]{:S(2)}, u32[]{:S(2)}) collective-permute-start(f32[136,256]{1,0:T(8,128)S(1)} %add.72.here_ref), channel_id=1, source_target_pairs={{0,8},{1,9},{2,10},{3,11},{4,12},{5,13},{6,14},{7,15},{8,0},{9,1},... | collective-permute-start | bytes 417800 | tf_op jit(solution)/shard_map/ppermute | solution.py:499
  146.9 7.5 %collective-permute-start.35 = (f32[8,256]{1,0:T(8,128)S(1)}, f32[8,256]{1,0:T(8,128)S(1)}, u32[]{:S(2)}, u32[]{:S(2)}) collective-permute-start(f32[8,256]{1,0:T(8,128)S(1)} %slice.28), channel_id=1, source_target_pairs={{0,24},{1,25},{2,26},{3,27},{4,28},{5,29},{6,30},{7,31},{8,16},{9,... | collective-permute-start | bytes 24584 | tf_op jit(solution)/shard_map/ppermute | solution.py:499
  148.5 8.4 %collective-permute-start.34 = (f32[8,256]{1,0:T(8,128)S(1)}, f32[8,256]{1,0:T(8,128)S(1)}, u32[]{:S(2)}, u32[]{:S(2)}) collective-permute-start(f32[8,256]{1,0:T(8,128)S(1)} %slice.28), channel_id=1, source_target_pairs={{0,16},{1,17},{2,18},{3,19},{4,20},{5,21},{6,22},{7,23},{8,24},{9,... | collective-permute-start | bytes 24584 | tf_op jit(solution)/shard_map/ppermute | solution.py:499
  148.6 35.3 %collective-permute-start.37 = (f32[128,512]{1,0:T(8,128)S(1)}, f32[128,512]{1,0:T(8,128)S(1)}, u32[]{:S(2)}, u32[]{:S(2)}) collective-permute-start(f32[128,512]{1,0:T(8,128)S(1)} %add.73), channel_id=1, source_target_pairs={{0,0},{1,16},{2,8},{3,24},{4,4},{5,20},{6,12},{7,28},{8,1},{9,17},... | collective-permute-start | bytes 786440 | tf_op jit(solution)/shard_map/ppermute | solution.py:499
  154.4 29.6 %collective-permute-start.39 = (f32[128,512]{1,0:T(8,128)S(1)}, f32[128,512]{1,0:T(8,128)S(1)}, u32[]{:S(2)}, u32[]{:S(2)}) collective-permute-start(f32[128,512]{1,0:T(8,128)S(1)} %add.74), channel_id=1, source_target_pairs={{0,0},{1,16},{2,8},{3,24},{4,4},{5,20},{6,12},{7,28},{8,1},{9,17},... | collective-permute-start | bytes 786440 | tf_op jit(solution)/shard_map/ppermute | solution.py:499
  156.9 27.0 %collective-permute-start.41 = (f32[128,512]{1,0:T(8,128)S(1)}, f32[128,512]{1,0:T(8,128)S(1)}, u32[]{:S(2)}, u32[]{:S(2)}) collective-permute-start(f32[128,512]{1,0:T(8,128)S(1)} %add.75), channel_id=1, source_target_pairs={{0,0},{1,16},{2,8},{3,24},{4,4},{5,20},{6,12},{7,28},{8,1},{9,17},... | collective-permute-start | bytes 786440 | tf_op jit(solution)/shard_map/ppermute | solution.py:499
  (54 other events, 203.8 us)

commit v3 on v2

--- a/solution.py
+++ b/solution.py
@@ -12,11 +12,11 @@
 BF16 = jnp.bfloat16
 HIGH = lax.Precision.HIGHEST
 SPAN = 256
-VMEM_BYTES = 56 * 1024 * 1024
-
-
-def params():
-    return pltpu.CompilerParams(vmem_limit_bytes=VMEM_BYTES)
+MIB = 1024 * 1024
+
+
+def params(mib=16):
+    return pltpu.CompilerParams(vmem_limit_bytes=mib * MIB)
 
 
 def transforms():
@@ -87,7 +87,7 @@
             jax.ShapeDtypeStruct((blocks * slots, hours), F32),
             jax.ShapeDtypeStruct((slots, blocks * slots), F32),
         ],
-        compiler_params=params(),
+        compiler_params=params(56),
         name="prepare",
     )(incidence, field)
 
@@ -113,7 +113,7 @@
         ],
         out_specs=pl.BlockSpec((step, hours), lambda i: (i, 0)),
         out_shape=jax.ShapeDtypeStruct((gauges, hours), F32),
-        compiler_params=params(),
+        compiler_params=params(56),
         name="table",
     )(row_gauge.reshape(1, slots), partial)
 
@@ -172,7 +172,7 @@
         out_specs=[pl.BlockSpec((rows, step), lambda i: (0, i))] * 2,
         out_shape=[jax.ShapeDtypeStruct((rows, gauges), BF16)] * 2,
         scratch_shapes=[pltpu.VMEM((rows, count), F32)],
-        compiler_params=params(),
+        compiler_params=params(56),
         name="couple",
     )(first, row_gauge.reshape(1, count), row_gauge.reshape(count, 1), gram)
 
@@ -188,7 +188,7 @@
     return pl.pallas_call(
         mix_kernel,
         out_shape=jax.ShapeDtypeStruct((high.shape[0], value.shape[1]), F32),
-        compiler_params=params(),
+        compiler_params=params(56),
         name="mix",
     )(high, low, value)
 
@@ -206,7 +206,7 @@
     return pl.pallas_call(
         spectrum_kernel,
         out_shape=jax.ShapeDtypeStruct((rows, SPAN), F32),
-        compiler_params=params(),
+        compiler_params=params(56),
         name="spectrum",
     )(gauge_kernel.reshape(rows, 1), kernels, forward)
 
@@ -268,7 +268,7 @@
         first_kernel,
         in_specs=[pl.BlockSpec(memory_space=pltpu.SMEM)] + [pl.BlockSpec(memory_space=pltpu.VMEM)] * 6,
         out_shape=[jax.ShapeDtypeStruct((rows, half), F32), jax.ShapeDtypeStruct((8, half), F32)],
-        compiler_params=params(),
+        compiler_params=params(56),
         name="first_step",
     )(more, sums, observed, spec, *mats)
 
@@ -337,7 +337,7 @@
         in_specs=[pl.BlockSpec(memory_space=pltpu.SMEM)]
         + [pl.BlockSpec(memory_space=pltpu.VMEM)] * (len(args) - 1),
         out_shape=shapes[2:] if final else shapes,
-        compiler_params=params(),
+        compiler_params=params(56),
         name="next_step",
     )(*args)
 
@@ -419,7 +419,7 @@
         out_specs=pl.BlockSpec((step * width, hours), lambda i: (i, 0)),
         out_shape=jax.ShapeDtypeStruct(field.shape, F32),
         scratch_shapes=[pltpu.VMEM((count, hours), F32)],
-        compiler_params=params(),
+        compiler_params=params(56),
         name="finish",
     )(*notes, row_gauge.reshape(count, 1), *gathered, incidence, field)
 

time: 191 us -> 157 us (0.82)
  Pallas kernels: 59.8 us -> 32.6 us
  local copies, waits for them, and re-layouts: 12.4 us -> 3.49 us
  blocking collectives: 17 us -> 20.1 us
  other arithmetic: 4.81 us -> 2.55 us
  starting transfers between devices: 62.5 us -> 64.5 us
    pallas_call x3, Pallas kernels: 8.85 us -> 1.74 us  [plane_mix(): pl.pallas_call(plane_mix_kernel, out_shape=[jax.ShapeDtypeStruct(values[0...]
    unnamed x88 -> x34, local copies, waits for them, and re-layouts: 10.2 us -> 3.31 us
    pallas_call x3, Pallas kernels: 12 us -> 5.91 us  [plane_step(): pl.pallas_call(functools.partial(plane_step_kernel, opening, final), in_s...]
    pallas_call x3, Pallas kernels: 8.29 us -> 3.95 us  [plane_rows(): pl.pallas_call(plane_rows_kernel, in_specs=[pl.BlockSpec(memory_space=plt...]
    all_to_all x1, blocking collectives: 17 us -> 20.1 us  [plane_shards(): lax.all_to_all(copies, ('basin', 'tm'), 0, 0, tiled=False)]
    pallas_call x1, Pallas kernels: 4.25 us -> 1.73 us  [send(): pl.pallas_call(send_kernel, grid=(blocks // step,), in_specs=[pl.BlockSpe...]
    add x3, other arithmetic: 0.12 us -> 2.23 us  [plane_shards(): kept.append(moved(rows_mine + moved(rows_other, over_core), from_plane))]
    ppermute x42, starting transfers between devices: 62.5 us -> 64.5 us  [moved(): return lax.ppermute(value, ('basin', 'tm'), pairs)]
  transfers between devices with their start and end apart: 42 -> 42, of which waited for: 10 -> 12; matrix products, arithmetic and copies ran while one was open for 3% -> 2% of each run, Pallas kernels for 19% -> 14%
where the time goes in v3:
time: 157 us; the launch traced here: 156 us
  starting transfers between devices  64.5 us (41%)
  Pallas kernels  32.6 us (21%)
  waiting for transfers between devices  32.5 us (21%)
  blocking collectives  20.1 us (13%)
  local copies, waits for them, and re-layouts  3.49 us (2%)
  other arithmetic  2.55 us (2%)
    ppermute x42, starting transfers between devices, moved(): return lax.ppermute(value, ('basin', 'tm'), pairs)  64.5 us
    ppermute x42, waiting for transfers between devices, moved(): return lax.ppermute(value, ('basin', 'tm'), pairs)  32.5 us
    all_to_all x1, blocking collectives, plane_shards(): lax.all_to_all(copies, ('basin', 'tm'), 0, 0, tiled=False)  20.1 us
    pallas_call x1, Pallas kernels, plane_couple(): pl.pallas_call(plane_couple_kernel, in_specs=[pl.BlockSpec(memory_space=p...  8.88 us
    pallas_call x3, Pallas kernels, plane_step(): pl.pallas_call(functools.partial(plane_step_kernel, opening, final), in_s...  5.91 us
    pallas_call x1, Pallas kernels, plane_finish(): pl.pallas_call(plane_finish_kernel, grid=(blocks // step,), in_specs=[who...  3.96 us
    pallas_call x3, Pallas kernels, plane_rows(): pl.pallas_call(plane_rows_kernel, in_specs=[pl.BlockSpec(memory_space=plt...  3.95 us
    unnamed x34, local copies, waits for them, and re-layouts  3.31 us
  transfers between devices with their start and end apart: 42, of which 12 were waited for; matrix products, arithmetic and copies ran while one was open for 2% of the time, Pallas kernels for 14%

profile of v3, /device:TPU:1, one launch (start us, length us, event | category | flops | bytes accessed | tf_op | source)
XLA Modules:
  0.0 156.3 jit_solution(15207105214644952729)
XLA Ops:
  0.0 1.6 %copy-done = f32[4096,128]{1,0:T(8,128)S(1)} copy-done((f32[4096,128]{1,0:T(8,128)S(1)}, f32[4096,128]{1,0:T(8,128)}, u32[]{:S(2)}) %copy-start) | copy-done | bytes 2097176
  3.3 1.7 %send.1 = f32[152,512]{1,0:T(8,128)S(1)} custom-call(s32[32,16,128]{2,1,0:T(8,128)S(1)} %copy-done.5, f32[4096,128]{1,0:T(8,128)S(1)} %copy-done, s32[1,512]{1,0:T(1,128)S(1)} %bitcast.10), custom_call_target="tpu_custom_call" | custom-call | tf_op jit(solution)/shard_map/send/pallas_call | solution.py:621
  5.1 4.6 %collective-permute-start = (f32[152,512]{1,0:T(8,128)S(1)}, f32[152,512]{1,0:T(8,128)S(1)}, u32[]{:S(2)}, u32[]{:S(2)}) collective-permute-start(f32[152,512]{1,0:T(8,128)S(1)} %send.1), channel_id=1, source_target_pairs={{0,0},{1,8},{2,16},{3,24},{4,4},{5,12},{6,20},{7,28},{8,2},{9,10},... | collective-permute-start | bytes 933896 | tf_op jit(solution)/shard_map/ppermute | solution.py:499
  9.7 14.9 %collective-permute-done.mine_ref = f32[152,512]{1,0:T(8,128)S(1)} collective-permute-done((f32[152,512]{1,0:T(8,128)S(1)}, f32[152,512]{1,0:T(8,128)S(1)}, u32[]{:S(2)}, u32[]{:S(2)}) %collective-permute-start) | collective-permute-done | bytes 311328 | tf_op jit(solution)/shard_map/ppermute | solution.py:499
  24.7 2.4 %collective-permute-start.11 = (f32[256,128]{1,0:T(8,128)S(1)}, f32[256,128]{1,0:T(8,128)S(1)}, u32[]{:S(2)}, u32[]{:S(2)}) collective-permute-start(f32[256,128]{1,0:T(8,128)S(1)} %copy-done.15), channel_id=1, source_target_pairs={{1,0},{2,8},{3,16},{5,4},{6,12},{7,20},{9,2},{10,10},{11,18},{13,6... | collective-permute-start | bytes 393224 | tf_op jit(solution)/shard_map/ppermute | solution.py:499
  27.2 2.7 %spread.1 = (f32[128,256]{1,0:T(8,128)S(1)}, f32[128,256]{1,0:T(8,128)S(1)}, f32[128,256]{1,0:T(8,128)S(1)}, f32[128,256]{1,0:T(8,128)S(1)}) custom-call(s32[6]{0:T(128)S(1)} %broadcast_multiply_fusion.first_ref, f32[152,512]{1,0:T(8,128)S(1)} %collective-permute-done.mine_ref, f32[152,512]{1,0:T(8,128)S(1)} %collective-permute-done.1.other_ref), custom_call_target="tpu_custom_call" | custom-call | tf_op jit(solution)/shard_map/spread/pallas_call | solution.py:658
  32.7 2.1 %collective-permute-start.10 = (f32[264,128]{1,0:T(8,128)S(1)}, f32[264,128]{1,0:T(8,128)S(1)}, u32[]{:S(2)}, u32[]{:S(2)}) collective-permute-start(f32[264,128]{1,0:T(8,128)S(1)} %maximum_maximum_fusion), channel_id=1, source_target_pairs={{0,0},{1,8},{2,16},{3,24},{4,4},{5,12},{6,20},{7,28},{8,2},{9,10},... | collective-permute-start | bytes 405512 | tf_op jit(solution)/shard_map/ppermute | solution.py:499
  35.3 4.0 %collective-permute-done.6 = f32[128,256]{1,0:T(8,128)S(1)} collective-permute-done((f32[128,256]{1,0:T(8,128)S(1)}, f32[128,256]{1,0:T(8,128)S(1)}, u32[]{:S(2)}, u32[]{:S(2)}) %collective-permute-start.6) | collective-permute-done | bytes 131104 | tf_op jit(solution)/shard_map/ppermute | solution.py:499
  40.1 3.1 %collective-permute-start.8 = (f32[128,256]{1,0:T(8,128)S(1)}, f32[128,256]{1,0:T(8,128)S(1)}, u32[]{:S(2)}, u32[]{:S(2)}) collective-permute-start(f32[128,256]{1,0:T(8,128)S(1)} %add_add_fusion.here_ref), channel_id=1, source_target_pairs={{0,8},{1,9},{2,10},{3,11},{4,12},{5,13},{6,14},{7,15},{8,0},{9,1},... | collective-permute-start | bytes 393224 | tf_op jit(solution)/shard_map/ppermute | solution.py:499
  46.8 3.0 %plane_first.1.a_ref.pulled_ref = f32[136,256]{1,0:T(8,128)S(1)} custom-call(f32[2]{0:T(128)S(1)} %add_convert_fusion.flag_ref, f32[128,256]{1,0:T(8,128)S(1)} %add_add_fusion.here_ref, f32[128,256]{1,0:T(8,128)S(1)} %collective-permute-done.8.pair_ref, f32[128,256]{1,0:T(8,128)S(1)} %collective-permute-done.9.middle_ref, ...), custom_call_target="tpu_custom_call" | custom-call | tf_op jit(solution)/shard_map/plane_first/pallas_call | solution.py:828
  52.6 8.9 %plane_couple.1 = (bf16[1024,512]{1,0:T(8,128)(2,1)S(1)}, bf16[1024,512]{1,0:T(8,128)(2,1)S(1)}) custom-call(s32[6]{0:T(128)S(1)} %broadcast_multiply_fusion.first_ref, f32[24,1024]{1,0:T(8,128)S(1)} %pad_maximum_fusion.a_ref, f32[24,1024]{1,0:T(8,128)S(1)} %collective-permute-done.2.b_ref, f32[24,1024]{1,0:T(8,128)S(1)} %collective-permute-done.3.c_ref, ...), custom_call_target="tpu_custom_call" | custom-call | flops 14000000000 | bytes 4000000 | tf_op jit(solution)/shard_map/plane_couple/pallas_call | solution.py:715
  62.1 3.4 %collective-permute-start.15 = (f32[136,256]{1,0:T(8,128)S(1)}, f32[136,256]{1,0:T(8,128)S(1)}, u32[]{:S(2)}, u32[]{:S(2)}) collective-permute-start(f32[136,256]{1,0:T(8,128)S(1)} %get-tuple-element.44), channel_id=1, source_target_pairs={{0,1},{1,0},{2,3},{3,2},{4,5},{5,4},{6,7},{7,6},{8,9},{9,8},{10,11... | collective-permute-start | bytes 417800 | tf_op jit(solution)/shard_map/ppermute | solution.py:499
  67.2 2.4 %collective-permute-start.16 = (f32[136,256]{1,0:T(8,128)S(1)}, f32[136,256]{1,0:T(8,128)S(1)}, u32[]{:S(2)}, u32[]{:S(2)}) collective-permute-start(f32[136,256]{1,0:T(8,128)S(1)} %add.70.here_ref), channel_id=1, source_target_pairs={{0,8},{1,9},{2,10},{3,11},{4,12},{5,13},{6,14},{7,15},{8,0},{9,1},... | collective-permute-start | bytes 417800 | tf_op jit(solution)/shard_map/ppermute | solution.py:499
  69.6 1.6 %collective-permute-start.19 = (f32[8,256]{1,0:T(8,128)S(1)}, f32[8,256]{1,0:T(8,128)S(1)}, u32[]{:S(2)}, u32[]{:S(2)}) collective-permute-start(f32[8,256]{1,0:T(8,128)S(1)} %slice.26), channel_id=1, source_target_pairs={{0,24},{1,25},{2,26},{3,27},{4,28},{5,29},{6,30},{7,31},{8,16},{9,... | collective-permute-start | bytes 24584 | tf_op jit(solution)/shard_map/ppermute | solution.py:499
  71.1 3.0 %collective-permute-done.19.mirror_ref = f32[8,256]{1,0:T(8,128)S(1)} collective-permute-done((f32[8,256]{1,0:T(8,128)S(1)}, f32[8,256]{1,0:T(8,128)S(1)}, u32[]{:S(2)}, u32[]{:S(2)}) %collective-permute-start.19) | collective-permute-done | bytes 8224 | tf_op jit(solution)/shard_map/ppermute | solution.py:499
  74.5 2.3 %plane_step.3 = (f32[8,256]{1,0:T(8,128)S(1)}, f32[136,256]{1,0:T(8,128)S(1)}, f32[1024,256]{1,0:T(8,128)S(1)}) custom-call(f32[2]{0:T(128)S(1)} %add_convert_fusion.flag_ref, f32[136,256]{1,0:T(8,128)S(1)} %add.70.here_ref, f32[136,256]{1,0:T(8,128)S(1)} %collective-permute-done.16.pair_ref, f32[136,256]{1,0:T(8,128)S(1)} %collective-permute-done.17.middle_ref, ...), custom_call_target="tpu_custom_call" | custom-call | tf_op jit(solution)/shard_map/plane_step/pallas_call | solution.py:894
  79.5 2.3 %collective-permute-done.22.d_ref = f32[136,256]{1,0:T(8,128)S(1)} collective-permute-done((f32[136,256]{1,0:T(8,128)S(1)}, f32[136,256]{1,0:T(8,128)S(1)}, u32[]{:S(2)}, u32[]{:S(2)}) %collective-permute-start.22) | collective-permute-done | bytes 139296 | tf_op jit(solution)/shard_map/ppermute | solution.py:499
  81.8 1.8 %collective-permute-done.21.c_ref = f32[136,256]{1,0:T(8,128)S(1)} collective-permute-done((f32[136,256]{1,0:T(8,128)S(1)}, f32[136,256]{1,0:T(8,128)S(1)}, u32[]{:S(2)}, u32[]{:S(2)}) %collective-permute-start.21) | collective-permute-done | bytes 139296 | tf_op jit(solution)/shard_map/ppermute | solution.py:499
  84.4 3.5 %collective-permute-start.23 = (f32[136,256]{1,0:T(8,128)S(1)}, f32[136,256]{1,0:T(8,128)S(1)}, u32[]{:S(2)}, u32[]{:S(2)}) collective-permute-start(f32[136,256]{1,0:T(8,128)S(1)} %get-tuple-element.48), channel_id=1, source_target_pairs={{0,1},{1,0},{2,3},{3,2},{4,5},{5,4},{6,7},{7,6},{8,9},{9,8},{10,11... | collective-permute-start | bytes 417800 | tf_op jit(solution)/shard_map/ppermute | solution.py:499
  89.8 1.7 %collective-permute-start.24 = (f32[136,256]{1,0:T(8,128)S(1)}, f32[136,256]{1,0:T(8,128)S(1)}, u32[]{:S(2)}, u32[]{:S(2)}) collective-permute-start(f32[136,256]{1,0:T(8,128)S(1)} %add.71.here_ref), channel_id=1, source_target_pairs={{0,8},{1,9},{2,10},{3,11},{4,12},{5,13},{6,14},{7,15},{8,0},{9,1},... | collective-permute-start | bytes 417800 | tf_op jit(solution)/shard_map/ppermute | solution.py:499
  91.5 1.8 %collective-permute-start.27 = (f32[8,256]{1,0:T(8,128)S(1)}, f32[8,256]{1,0:T(8,128)S(1)}, u32[]{:S(2)}, u32[]{:S(2)}) collective-permute-start(f32[8,256]{1,0:T(8,128)S(1)} %slice.27), channel_id=1, source_target_pairs={{0,24},{1,25},{2,26},{3,27},{4,28},{5,29},{6,30},{7,31},{8,16},{9,... | collective-permute-start | bytes 24584 | tf_op jit(solution)/shard_map/ppermute | solution.py:499
  93.3 3.0 %collective-permute-done.27.mirror_ref = f32[8,256]{1,0:T(8,128)S(1)} collective-permute-done((f32[8,256]{1,0:T(8,128)S(1)}, f32[8,256]{1,0:T(8,128)S(1)}, u32[]{:S(2)}, u32[]{:S(2)}) %collective-permute-start.27) | collective-permute-done | bytes 8224 | tf_op jit(solution)/shard_map/ppermute | solution.py:499
  96.7 2.3 %plane_step.4 = (f32[8,256]{1,0:T(8,128)S(1)}, f32[136,256]{1,0:T(8,128)S(1)}, f32[1024,256]{1,0:T(8,128)S(1)}) custom-call(f32[2]{0:T(128)S(1)} %add_convert_fusion.flag_ref, f32[136,256]{1,0:T(8,128)S(1)} %add.71.here_ref, f32[136,256]{1,0:T(8,128)S(1)} %collective-permute-done.24.pair_ref, f32[136,256]{1,0:T(8,128)S(1)} %collective-permute-done.25.middle_ref, ...), custom_call_target="tpu_custom_call" | custom-call | tf_op jit(solution)/shard_map/plane_step/pallas_call | solution.py:894
  103.1 3.3 %collective-permute-start.36 = (f32[128,512]{1,0:T(8,128)S(1)}, f32[128,512]{1,0:T(8,128)S(1)}, u32[]{:S(2)}, u32[]{:S(2)}) collective-permute-start(f32[128,512]{1,0:T(8,128)S(1)} %get-tuple-element.58), channel_id=1, source_target_pairs={{0,1},{1,0},{2,3},{3,2},{4,5},{5,4},{6,7},{7,6},{8,9},{9,8},{10,11... | collective-permute-start | bytes 786440 | tf_op jit(solution)/shard_map/ppermute | solution.py:499
  108.4 1.6 %collective-permute-start.31 = (f32[136,256]{1,0:T(8,128)S(1)}, f32[136,256]{1,0:T(8,128)S(1)}, u32[]{:S(2)}, u32[]{:S(2)}) collective-permute-start(f32[136,256]{1,0:T(8,128)S(1)} %get-tuple-element.53), channel_id=1, source_target_pairs={{0,1},{1,0},{2,3},{3,2},{4,5},{5,4},{6,7},{7,6},{8,9},{9,8},{10,11... | collective-permute-start | bytes 417800 | tf_op jit(solution)/shard_map/ppermute | solution.py:499
  112.1 1.7 %collective-permute-start.32 = (f32[136,256]{1,0:T(8,128)S(1)}, f32[136,256]{1,0:T(8,128)S(1)}, u32[]{:S(2)}, u32[]{:S(2)}) collective-permute-start(f32[136,256]{1,0:T(8,128)S(1)} %add.72.here_ref), channel_id=1, source_target_pairs={{0,8},{1,9},{2,10},{3,11},{4,12},{5,13},{6,14},{7,15},{8,0},{9,1},... | collective-permute-start | bytes 417800 | tf_op jit(solution)/shard_map/ppermute | solution.py:499
  113.8 1.8 %collective-permute-start.35 = (f32[8,256]{1,0:T(8,128)S(1)}, f32[8,256]{1,0:T(8,128)S(1)}, u32[]{:S(2)}, u32[]{:S(2)}) collective-permute-start(f32[8,256]{1,0:T(8,128)S(1)} %slice.28), channel_id=1, source_target_pairs={{0,24},{1,25},{2,26},{3,27},{4,28},{5,29},{6,30},{7,31},{8,16},{9,... | collective-permute-start | bytes 24584 | tf_op jit(solution)/shard_map/ppermute | solution.py:499
  117.1 5.9 %collective-permute-start.37 = (f32[128,512]{1,0:T(8,128)}, f32[128,512]{1,0:T(8,128)S(1)}, u32[]{:S(2)}, u32[]{:S(2)}) collective-permute-start(f32[128,512]{1,0:T(8,128)} %add.73), channel_id=1, source_target_pairs={{0,0},{1,16},{2,8},{3,24},{4,4},{5,20},{6,12},{7,28},{8,1},{9,17},... | collective-permute-start | bytes 786440 | tf_op jit(solution)/shard_map/ppermute | solution.py:499
  123.7 2.8 %collective-permute-start.39 = (f32[128,512]{1,0:T(8,128)}, f32[128,512]{1,0:T(8,128)}, u32[]{:S(2)}, u32[]{:S(2)}) collective-permute-start(f32[128,512]{1,0:T(8,128)} %add.74), channel_id=1, source_target_pairs={{0,0},{1,16},{2,8},{3,24},{4,4},{5,20},{6,12},{7,28},{8,1},{9,17},... | collective-permute-start | bytes 786440 | tf_op jit(solution)/shard_map/ppermute | solution.py:499
  126.5 4.2 %collective-permute-start.41 = (f32[128,512]{1,0:T(8,128)}, f32[128,512]{1,0:T(8,128)}, u32[]{:S(2)}, u32[]{:S(2)}) collective-permute-start(f32[128,512]{1,0:T(8,128)} %add.75), channel_id=1, source_target_pairs={{0,0},{1,16},{2,8},{3,24},{4,4},{5,20},{6,12},{7,28},{8,1},{9,17},... | collective-permute-start | bytes 786440 | tf_op jit(solution)/shard_map/ppermute | solution.py:499
  132.1 20.1 %all_to_all.5 = f32[32,8,128]{2,1,0:T(8,128)S(1)} all-to-all(f32[32,8,128]{2,1,0:T(8,128)S(1)} %broadcast_in_dim.10), channel_id=1, replica_groups=mesh['basin'=8,'tm'=4] {'basin','tm'}, dimensions={0} | all-to-all | bytes 262144 | tf_op jit(solution)/shard_map/all_to_all | solution.py:990
  152.4 4.0 %plane_finish.1 = f32[4096,128]{1,0:T(8,128)} custom-call(f32[8,256]{1,0:T(8,128)S(1)} %get-tuple-element.45.n0, f32[8,256]{1,0:T(8,128)S(1)} %get-tuple-element.50.n1, f32[8,256]{1,0:T(8,128)S(1)} %get-tuple-element.55.n2, f32[8,128]{1,0:T(8,128)S(1)} %reduce_sum.9.n3, f32[128,512]{1,0:T(8,128)S(1)} %collective-permute-done.37.q0, ...), custom_call_target="tpu_custom_call" | custom-call | tf_op jit(solution)/shard_map/plane_finish/pallas_call | solution.py:929
  (125 shorter events, 32.4 us)
Async XLA Ops:
  5.1 19.5 %collective-permute-start = (f32[152,512]{1,0:T(8,128)S(1)}, f32[152,512]{1,0:T(8,128)S(1)}, u32[]{:S(2)}, u32[]{:S(2)}) collective-permute-start(f32[152,512]{1,0:T(8,128)S(1)} %send.1), channel_id=1, source_target_pairs={{0,0},{1,8},{2,16},{3,24},{4,4},{5,12},{6,20},{7,28},{8,2},{9,10},... | collective-permute-start | bytes 933896 | tf_op jit(solution)/shard_map/ppermute | solution.py:499
  24.7 19.9 %collective-permute-start.11 = (f32[256,128]{1,0:T(8,128)S(1)}, f32[256,128]{1,0:T(8,128)S(1)}, u32[]{:S(2)}, u32[]{:S(2)}) collective-permute-start(f32[256,128]{1,0:T(8,128)S(1)} %copy-done.15), channel_id=1, source_target_pairs={{1,0},{2,8},{3,16},{5,4},{6,12},{7,20},{9,2},{10,10},{11,18},{13,6... | collective-permute-start | bytes 393224 | tf_op jit(solution)/shard_map/ppermute | solution.py:499
  29.9 5.4 %collective-permute-start.5 = (f32[128,256]{1,0:T(8,128)S(1)}, f32[128,256]{1,0:T(8,128)S(1)}, u32[]{:S(2)}, u32[]{:S(2)}) collective-permute-start(f32[128,256]{1,0:T(8,128)S(1)} %get-tuple-element.38), channel_id=1, source_target_pairs={{0,4},{1,5},{2,6},{3,7},{4,0},{5,1},{6,2},{7,3},{8,12},{9,13},{10,... | collective-permute-start | bytes 393224 | tf_op jit(solution)/shard_map/ppermute | solution.py:499
  31.2 8.2 %collective-permute-start.6 = (f32[128,256]{1,0:T(8,128)S(1)}, f32[128,256]{1,0:T(8,128)S(1)}, u32[]{:S(2)}, u32[]{:S(2)}) collective-permute-start(f32[128,256]{1,0:T(8,128)S(1)} %get-tuple-element.39), channel_id=1, source_target_pairs={{0,2},{1,3},{2,0},{3,1},{4,6},{5,7},{6,4},{7,5},{8,10},{9,11},{10,... | collective-permute-start | bytes 393224 | tf_op jit(solution)/shard_map/ppermute | solution.py:499
  31.7 7.7 %collective-permute-start.7 = (f32[128,256]{1,0:T(8,128)S(1)}, f32[128,256]{1,0:T(8,128)S(1)}, u32[]{:S(2)}, u32[]{:S(2)}) collective-permute-start(f32[128,256]{1,0:T(8,128)S(1)} %get-tuple-element.40), channel_id=1, source_target_pairs={{0,6},{1,7},{2,4},{3,5},{4,2},{5,3},{6,0},{7,1},{8,14},{9,15},{10,... | collective-permute-start | bytes 393224 | tf_op jit(solution)/shard_map/ppermute | solution.py:499
  32.7 13.2 %collective-permute-start.10 = (f32[264,128]{1,0:T(8,128)S(1)}, f32[264,128]{1,0:T(8,128)S(1)}, u32[]{:S(2)}, u32[]{:S(2)}) collective-permute-start(f32[264,128]{1,0:T(8,128)S(1)} %maximum_maximum_fusion), channel_id=1, source_target_pairs={{0,0},{1,8},{2,16},{3,24},{4,4},{5,12},{6,20},{7,28},{8,2},{9,10},... | collective-permute-start | bytes 405512 | tf_op jit(solution)/shard_map/ppermute | solution.py:499
  39.4 7.3 %collective-permute-start.9 = (f32[128,256]{1,0:T(8,128)S(1)}, f32[128,256]{1,0:T(8,128)S(1)}, u32[]{:S(2)}, u32[]{:S(2)}) collective-permute-start(f32[128,256]{1,0:T(8,128)S(1)} %add_add_fusion.here_ref), channel_id=1, source_target_pairs={{8,16},{9,17},{10,18},{11,19},{12,20},{13,21},{14,22},{15,23},{16,... | collective-permute-start | bytes 393224 | tf_op jit(solution)/shard_map/ppermute | solution.py:499
  40.1 6.6 %collective-permute-start.8 = (f32[128,256]{1,0:T(8,128)S(1)}, f32[128,256]{1,0:T(8,128)S(1)}, u32[]{:S(2)}, u32[]{:S(2)}) collective-permute-start(f32[128,256]{1,0:T(8,128)S(1)} %add_add_fusion.here_ref), channel_id=1, source_target_pairs={{0,8},{1,9},{2,10},{3,11},{4,12},{5,13},{6,14},{7,15},{8,0},{9,1},... | collective-permute-start | bytes 393224 | tf_op jit(solution)/shard_map/ppermute | solution.py:499
  43.2 9.4 %collective-permute-start.4 = (f32[24,1024]{1,0:T(8,128)S(1)}, f32[24,1024]{1,0:T(8,128)S(1)}, u32[]{:S(2)}, u32[]{:S(2)}) collective-permute-start(f32[24,1024]{1,0:T(8,128)S(1)} %pad_maximum_fusion.a_ref), channel_id=1, source_target_pairs={{0,6},{1,7},{2,4},{3,5},{4,2},{5,3},{6,0},{7,1},{8,14},{9,15},{10,... | collective-permute-start | bytes 294920 | tf_op jit(solution)/shard_map/ppermute | solution.py:499
  44.7 7.9 %collective-permute-start.3 = (f32[24,1024]{1,0:T(8,128)S(1)}, f32[24,1024]{1,0:T(8,128)S(1)}, u32[]{:S(2)}, u32[]{:S(2)}) collective-permute-start(f32[24,1024]{1,0:T(8,128)S(1)} %pad_maximum_fusion.a_ref), channel_id=1, source_target_pairs={{0,2},{1,3},{2,0},{3,1},{4,6},{5,7},{6,4},{7,5},{8,10},{9,11},{10,... | collective-permute-start | bytes 294920 | tf_op jit(solution)/shard_map/ppermute | solution.py:499
  45.9 6.7 %collective-permute-start.2 = (f32[24,1024]{1,0:T(8,128)S(1)}, f32[24,1024]{1,0:T(8,128)S(1)}, u32[]{:S(2)}, u32[]{:S(2)}) collective-permute-start(f32[24,1024]{1,0:T(8,128)S(1)} %pad_maximum_fusion.a_ref), channel_id=1, source_target_pairs={{0,4},{1,5},{2,6},{3,7},{4,0},{5,1},{6,2},{7,3},{8,12},{9,13},{10,... | collective-permute-start | bytes 294920 | tf_op jit(solution)/shard_map/ppermute | solution.py:499
  49.8 11.6 %collective-permute-start.14 = (f32[136,256]{1,0:T(8,128)S(1)}, f32[136,256]{1,0:T(8,128)S(1)}, u32[]{:S(2)}, u32[]{:S(2)}) collective-permute-start(f32[136,256]{1,0:T(8,128)S(1)} %plane_first.1.a_ref.pulled_ref), channel_id=1, source_target_pairs={{0,6},{1,7},{2,4},{3,5},{4,2},{5,3},{6,0},{7,1},{8,14},{9,15},{10,... | collective-permute-start | bytes 417800 | tf_op jit(solution)/shard_map/ppermute | solution.py:499
  51.3 10.2 %collective-permute-start.13 = (f32[136,256]{1,0:T(8,128)S(1)}, f32[136,256]{1,0:T(8,128)S(1)}, u32[]{:S(2)}, u32[]{:S(2)}) collective-permute-start(f32[136,256]{1,0:T(8,128)S(1)} %plane_first.1.a_ref.pulled_ref), channel_id=1, source_target_pairs={{0,2},{1,3},{2,0},{3,1},{4,6},{5,7},{6,4},{7,5},{8,10},{9,11},{10,... | collective-permute-start | bytes 417800 | tf_op jit(solution)/shard_map/ppermute | solution.py:499
  52.5 9.0 %collective-permute-start.12 = (f32[136,256]{1,0:T(8,128)S(1)}, f32[136,256]{1,0:T(8,128)S(1)}, u32[]{:S(2)}, u32[]{:S(2)}) collective-permute-start(f32[136,256]{1,0:T(8,128)S(1)} %plane_first.1.a_ref.pulled_ref), channel_id=1, source_target_pairs={{0,4},{1,5},{2,6},{3,7},{4,0},{5,1},{6,2},{7,3},{8,12},{9,13},{10,... | collective-permute-start | bytes 417800 | tf_op jit(solution)/shard_map/ppermute | solution.py:499
  66.5 8.1 %collective-permute-start.17 = (f32[136,256]{1,0:T(8,128)S(1)}, f32[136,256]{1,0:T(8,128)S(1)}, u32[]{:S(2)}, u32[]{:S(2)}) collective-permute-start(f32[136,256]{1,0:T(8,128)S(1)} %add.70.here_ref), channel_id=1, source_target_pairs={{8,16},{9,17},{10,18},{11,19},{12,20},{13,21},{14,22},{15,23},{16,... | collective-permute-start | bytes 417800 | tf_op jit(solution)/shard_map/ppermute | solution.py:499
  67.2 7.4 %collective-permute-start.16 = (f32[136,256]{1,0:T(8,128)S(1)}, f32[136,256]{1,0:T(8,128)S(1)}, u32[]{:S(2)}, u32[]{:S(2)}) collective-permute-start(f32[136,256]{1,0:T(8,128)S(1)} %add.70.here_ref), channel_id=1, source_target_pairs={{0,8},{1,9},{2,10},{3,11},{4,12},{5,13},{6,14},{7,15},{8,0},{9,1},... | collective-permute-start | bytes 417800 | tf_op jit(solution)/shard_map/ppermute | solution.py:499
  78.3 5.3 %collective-permute-start.21 = (f32[136,256]{1,0:T(8,128)S(1)}, f32[136,256]{1,0:T(8,128)S(1)}, u32[]{:S(2)}, u32[]{:S(2)}) collective-permute-start(f32[136,256]{1,0:T(8,128)S(1)} %get-tuple-element.46.a_ref.pulled_ref), channel_id=1, source_target_pairs={{0,2},{1,3},{2,0},{3,1},{4,6},{5,7},{6,4},{7,5},{8,10},{9,11},{10,... | collective-permute-start | bytes 417800 | tf_op jit(solution)/shard_map/ppermute | solution.py:499
  88.9 7.8 %collective-permute-start.25 = (f32[136,256]{1,0:T(8,128)S(1)}, f32[136,256]{1,0:T(8,128)S(1)}, u32[]{:S(2)}, u32[]{:S(2)}) collective-permute-start(f32[136,256]{1,0:T(8,128)S(1)} %add.71.here_ref), channel_id=1, source_target_pairs={{8,16},{9,17},{10,18},{11,19},{12,20},{13,21},{14,22},{15,23},{16,... | collective-permute-start | bytes 417800 | tf_op jit(solution)/shard_map/ppermute | solution.py:499
  89.8 6.9 %collective-permute-start.24 = (f32[136,256]{1,0:T(8,128)S(1)}, f32[136,256]{1,0:T(8,128)S(1)}, u32[]{:S(2)}, u32[]{:S(2)}) collective-permute-start(f32[136,256]{1,0:T(8,128)S(1)} %add.71.here_ref), channel_id=1, source_target_pairs={{0,8},{1,9},{2,10},{3,11},{4,12},{5,13},{6,14},{7,15},{8,0},{9,1},... | collective-permute-start | bytes 417800 | tf_op jit(solution)/shard_map/ppermute | solution.py:499
  99.0 8.7 %collective-permute-start.30 = (f32[136,256]{1,0:T(8,128)S(1)}, f32[136,256]{1,0:T(8,128)S(1)}, u32[]{:S(2)}, u32[]{:S(2)}) collective-permute-start(f32[136,256]{1,0:T(8,128)S(1)} %get-tuple-element.51.a_ref.pulled_ref), channel_id=1, source_target_pairs={{0,6},{1,7},{2,4},{3,5},{4,2},{5,3},{6,0},{7,1},{8,14},{9,15},{10,... | collective-permute-start | bytes 417800 | tf_op jit(solution)/shard_map/ppermute | solution.py:499
  100.4 7.4 %collective-permute-start.29 = (f32[136,256]{1,0:T(8,128)S(1)}, f32[136,256]{1,0:T(8,128)S(1)}, u32[]{:S(2)}, u32[]{:S(2)}) collective-permute-start(f32[136,256]{1,0:T(8,128)S(1)} %get-tuple-element.51.a_ref.pulled_ref), channel_id=1, source_target_pairs={{0,2},{1,3},{2,0},{3,1},{4,6},{5,7},{6,4},{7,5},{8,10},{9,11},{10,... | collective-permute-start | bytes 417800 | tf_op jit(solution)/shard_map/ppermute | solution.py:499
  101.3 6.5 %collective-permute-start.28 = (f32[136,256]{1,0:T(8,128)S(1)}, f32[136,256]{1,0:T(8,128)S(1)}, u32[]{:S(2)}, u32[]{:S(2)}) collective-permute-start(f32[136,256]{1,0:T(8,128)S(1)} %get-tuple-element.51.a_ref.pulled_ref), channel_id=1, source_target_pairs={{0,4},{1,5},{2,6},{3,7},{4,0},{5,1},{6,2},{7,3},{8,12},{9,13},{10,... | collective-permute-start | bytes 417800 | tf_op jit(solution)/shard_map/ppermute | solution.py:499
  103.1 10.7 %collective-permute-start.36 = (f32[128,512]{1,0:T(8,128)S(1)}, f32[128,512]{1,0:T(8,128)S(1)}, u32[]{:S(2)}, u32[]{:S(2)}) collective-permute-start(f32[128,512]{1,0:T(8,128)S(1)} %get-tuple-element.58), channel_id=1, source_target_pairs={{0,1},{1,0},{2,3},{3,2},{4,5},{5,4},{6,7},{7,6},{8,9},{9,8},{10,11... | collective-permute-start | bytes 786440 | tf_op jit(solution)/shard_map/ppermute | solution.py:499
  107.7 7.9 %collective-permute-start.38 = (f32[128,512]{1,0:T(8,128)S(1)}, f32[128,512]{1,0:T(8,128)S(1)}, u32[]{:S(2)}, u32[]{:S(2)}) collective-permute-start(f32[128,512]{1,0:T(8,128)S(1)} %get-tuple-element.60), channel_id=1, source_target_pairs={{0,1},{1,0},{2,3},{3,2},{4,5},{5,4},{6,7},{7,6},{8,9},{9,8},{10,11... | collective-permute-start | bytes 786440 | tf_op jit(solution)/shard_map/ppermute | solution.py:499
  111.3 5.8 %collective-permute-start.40 = (f32[128,512]{1,0:T(8,128)S(1)}, f32[128,512]{1,0:T(8,128)S(1)}, u32[]{:S(2)}, u32[]{:S(2)}) collective-permute-start(f32[128,512]{1,0:T(8,128)S(1)} %get-tuple-element.62), channel_id=1, source_target_pairs={{0,1},{1,0},{2,3},{3,2},{4,5},{5,4},{6,7},{7,6},{8,9},{9,8},{10,11... | collective-permute-start | bytes 786440 | tf_op jit(solution)/shard_map/ppermute | solution.py:499
  111.4 19.4 %collective-permute-start.33 = (f32[136,256]{1,0:T(8,128)S(1)}, f32[136,256]{1,0:T(8,128)S(1)}, u32[]{:S(2)}, u32[]{:S(2)}) collective-permute-start(f32[136,256]{1,0:T(8,128)S(1)} %add.72.here_ref), channel_id=1, source_target_pairs={{8,16},{9,17},{10,18},{11,19},{12,20},{13,21},{14,22},{15,23},{16,... | collective-permute-start | bytes 417800 | tf_op jit(solution)/shard_map/ppermute | solution.py:499
  112.1 18.7 %collective-permute-start.32 = (f32[136,256]{1,0:T(8,128)S(1)}, f32[136,256]{1,0:T(8,128)S(1)}, u32[]{:S(2)}, u32[]{:S(2)}) collective-permute-start(f32[136,256]{1,0:T(8,128)S(1)} %add.72.here_ref), channel_id=1, source_target_pairs={{0,8},{1,9},{2,10},{3,11},{4,12},{5,13},{6,14},{7,15},{8,0},{9,1},... | collective-permute-start | bytes 417800 | tf_op jit(solution)/shard_map/ppermute | solution.py:499
  113.8 9.9 %collective-permute-start.35 = (f32[8,256]{1,0:T(8,128)S(1)}, f32[8,256]{1,0:T(8,128)S(1)}, u32[]{:S(2)}, u32[]{:S(2)}) collective-permute-start(f32[8,256]{1,0:T(8,128)S(1)} %slice.28), channel_id=1, source_target_pairs={{0,24},{1,25},{2,26},{3,27},{4,28},{5,29},{6,30},{7,31},{8,16},{9,... | collective-permute-start | bytes 24584 | tf_op jit(solution)/shard_map/ppermute | solution.py:499
  115.6 10.9 %collective-permute-start.34 = (f32[8,256]{1,0:T(8,128)S(1)}, f32[8,256]{1,0:T(8,128)S(1)}, u32[]{:S(2)}, u32[]{:S(2)}) collective-permute-start(f32[8,256]{1,0:T(8,128)S(1)} %slice.28), channel_id=1, source_target_pairs={{0,16},{1,17},{2,18},{3,19},{4,20},{5,21},{6,22},{7,23},{8,24},{9,... | collective-permute-start | bytes 24584 | tf_op jit(solution)/shard_map/ppermute | solution.py:499
  117.1 35.2 %collective-permute-start.37 = (f32[128,512]{1,0:T(8,128)}, f32[128,512]{1,0:T(8,128)S(1)}, u32[]{:S(2)}, u32[]{:S(2)}) collective-permute-start(f32[128,512]{1,0:T(8,128)} %add.73), channel_id=1, source_target_pairs={{0,0},{1,16},{2,8},{3,24},{4,4},{5,20},{6,12},{7,28},{8,1},{9,17},... | collective-permute-start | bytes 786440 | tf_op jit(solution)/shard_map/ppermute | solution.py:499
  123.7 28.6 %collective-permute-start.39 = (f32[128,512]{1,0:T(8,128)}, f32[128,512]{1,0:T(8,128)}, u32[]{:S(2)}, u32[]{:S(2)}) collective-permute-start(f32[128,512]{1,0:T(8,128)} %add.74), channel_id=1, source_target_pairs={{0,0},{1,16},{2,8},{3,24},{4,4},{5,20},{6,12},{7,28},{8,1},{9,17},... | collective-permute-start | bytes 786440 | tf_op jit(solution)/shard_map/ppermute | solution.py:499
  126.5 25.8 %collective-permute-start.41 = (f32[128,512]{1,0:T(8,128)}, f32[128,512]{1,0:T(8,128)}, u32[]{:S(2)}, u32[]{:S(2)}) collective-permute-start(f32[128,512]{1,0:T(8,128)} %add.75), channel_id=1, source_target_pairs={{0,0},{1,16},{2,8},{3,24},{4,4},{5,20},{6,12},{7,28},{8,1},{9,17},... | collective-permute-start | bytes 786440 | tf_op jit(solution)/shard_map/ppermute | solution.py:499
  (27 other events, 577.0 us)

commit v4 on v3

--- a/solution.py
+++ b/solution.py
@@ -595,42 +595,68 @@
     return product(first, turn(waves, spec, -1.0), order)
 
 
-def send_kernel(inc_ref, field_ref, gauge_ref, out_ref):
+def describe_kernel(inc_ref, gauge_ref, kind_ref, out_ref):
     blocks, slots, width = inc_ref.shape
-    rows = blocks * slots
-    hours = field_ref.shape[1]
+    tile = 8
+    rows = tile * slots
+    weights = inc_ref[...].astype(F32).astype(BF16)
+    row = lax.broadcasted_iota(jnp.int32, (rows, rows), 0)
+    col = lax.broadcasted_iota(jnp.int32, (rows, rows), 1)
+    same = row // slots == col // slots
+    for i in range(blocks // tile):
+        flat = weights[i * tile : (i + 1) * tile].reshape(rows, width)
+        full = lax.dot_general(flat, flat, (((1,), (1,)), ((), ())), preferred_element_type=F32)
+        own = jnp.where(same, full, 0.0)
+        out_ref[pl.ds(0, slots), pl.ds(i * rows, rows)] = jnp.sum(own.reshape(tile, slots, rows), axis=0)
+    kinds = kind_ref.shape[1]
+    out_ref[pl.ds(slots, 8), :] = jnp.concatenate(
+        [
+            gauge_ref[...].astype(F32),
+            jnp.concatenate(
+                [kind_ref[...].astype(F32), jnp.zeros((1, blocks * slots - kinds), F32)], axis=1
+            ),
+            jnp.zeros((6, blocks * slots), F32),
+        ],
+        axis=0,
+    )
+
+
+def describe(incidence, row_gauge, gauge_kernel):
+    blocks, slots, _ = incidence.shape
+    count = blocks * slots
+    return pl.pallas_call(
+        describe_kernel,
+        out_shape=jax.ShapeDtypeStruct((slots + 8, count), F32),
+        compiler_params=params(),
+        name="describe",
+    )(incidence, row_gauge.reshape(1, count), gauge_kernel.reshape(1, gauge_kernel.shape[0]))
+
+
+def send_kernel(inc_ref, field_ref, out_ref):
+    blocks, slots, width = inc_ref.shape
     weights = inc_ref[...].astype(F32).astype(BF16)
     parts = []
     for b in range(blocks):
         parts.append(pick(weights[b], field_ref[pl.ds(b * width, width), :]))
-    out_ref[pl.ds(0, hours), :] = jnp.transpose(jnp.concatenate(parts, axis=0))
-    flat = weights.reshape(rows, width)
-    full = lax.dot_general(flat, flat, (((1,), (1,)), ((), ())), preferred_element_type=F32)
-    row = lax.broadcasted_iota(jnp.int32, (rows, rows), 0)
-    col = lax.broadcasted_iota(jnp.int32, (rows, rows), 1)
-    own = jnp.where(row // slots == col // slots, full, 0.0)
-    out_ref[pl.ds(hours, slots), :] = jnp.sum(own.reshape(blocks, slots, rows), axis=0)
-    out_ref[pl.ds(hours + slots, 8), :] = jnp.broadcast_to(gauge_ref[...].astype(F32), (8, rows))
-
-
-def send(incidence, field, row_gauge):
+    out_ref[...] = jnp.transpose(jnp.concatenate(parts, axis=0))
+
+
+def send(incidence, field):
     blocks, slots, width = incidence.shape
     hours = field.shape[1]
     step = 8
-    height = hours + slots + 8
     return pl.pallas_call(
         send_kernel,
         grid=(blocks // step,),
         in_specs=[
             pl.BlockSpec((step, slots, width), lambda i: (i, 0, 0)),
             pl.BlockSpec((step * width, hours), lambda i: (i, 0)),
-            pl.BlockSpec((1, step * slots), lambda i: (0, i)),
         ],
-        out_specs=pl.BlockSpec((height, step * slots), lambda i: (0, i)),
-        out_shape=jax.ShapeDtypeStruct((height, blocks * slots), F32),
+        out_specs=pl.BlockSpec((hours, step * slots), lambda i: (0, i)),
+        out_shape=jax.ShapeDtypeStruct((hours, blocks * slots), F32),
         compiler_params=params(),
         name="send",
-    )(incidence, field, row_gauge.reshape(1, blocks * slots))
+    )(incidence, field)
 
 
 def hot_rows(gauge, first, rows):
@@ -638,15 +664,14 @@
     return jnp.where(gauge == mine, 1.0, 0.0).astype(BF16)
 
 
-def spread_kernel(first_ref, mine_ref, other_ref, *out_refs):
-    hours, rows = out_refs[0].shape
-    slots = mine_ref.shape[0] - hours - 8
-    where = hours + slots
+def spread_kernel(first_ref, mine_ref, other_ref, meta_ref, meta_other_ref, *out_refs):
+    rows = out_refs[0].shape[1]
+    where = meta_ref.shape[0] - 8
     for m, out_ref in enumerate(out_refs):
         result = None
-        for ref in (mine_ref, other_ref):
-            hot = hot_rows(ref[where : where + 1, :], first_ref[m], rows)
-            for piece in reversed(pieces(ref[pl.ds(0, hours), :], 3)):
+        for ref, meta in ((mine_ref, meta_ref), (other_ref, meta_other_ref)):
+            hot = hot_rows(meta[where : where + 1, :], first_ref[m], rows)
+            for piece in reversed(pieces(ref[...], 3)):
                 term = lax.dot_general(
                     piece, hot, (((1,), (1,)), ((), ())), preferred_element_type=F32
                 )
@@ -654,22 +679,25 @@
         out_ref[...] = result
 
 
-def spread(first, mine, other, hours, rows):
+def spread(first, parcels, metas, rows):
+    hours = parcels[0].shape[0]
     return pl.pallas_call(
         spread_kernel,
-        in_specs=[pl.BlockSpec(memory_space=pltpu.SMEM)] + [pl.BlockSpec(memory_space=pltpu.VMEM)] * 2,
+        in_specs=[pl.BlockSpec(memory_space=pltpu.SMEM)] + [pl.BlockSpec(memory_space=pltpu.VMEM)] * 4,
         out_shape=[jax.ShapeDtypeStruct((hours, rows), F32)] * 4,
         compiler_params=params(),
         name="spread",
-    )(first, mine, other)
-
-
-def plane_couple_kernel(first_ref, a_ref, b_ref, c_ref, d_ref, high_ref, low_ref, total_ref, meta_ref):
+    )(first, *parcels, *metas)
+
+
+def plane_couple_kernel(
+    owners, first_ref, a_ref, b_ref, c_ref, d_ref, high_ref, low_ref, total_ref, meta_ref
+):
     height, double = a_ref.shape
     slots = height - 8
     count = double // 2
     cols, rows = high_ref.shape
-    part = cols // 4
+    part = cols // len(owners)
     tile = 256
     for i, ref in enumerate((a_ref, b_ref, c_ref, d_ref)):
         for j in range(2):
@@ -695,7 +723,7 @@
         near = jnp.concatenate(near, axis=0)
         high = near.astype(BF16)
         rest = near - high.astype(F32)
-        hot = jnp.concatenate([hot_rows(gauge, first_ref[m], part) for m in range(4)], axis=0)
+        hot = jnp.concatenate([hot_rows(gauge, first_ref[m], part) for m in owners], axis=0)
         total_ref[...] += dot(hot, high)
 
         @pl.when(jnp.max(jnp.abs(rest)) > 0.0)
@@ -710,30 +738,36 @@
     low_ref[...] = low
 
 
-def plane_couple(first, metas, rows):
+def plane_couple(first, metas, rows, owners):
     height, double = metas[0].shape
-    return pl.pallas_call(
-        plane_couple_kernel,
+    cols = len(owners) * rows
+    return pl.pallas_call(
+        functools.partial(plane_couple_kernel, owners),
         in_specs=[pl.BlockSpec(memory_space=pltpu.SMEM)] + [pl.BlockSpec(memory_space=pltpu.VMEM)] * 4,
-        out_shape=[jax.ShapeDtypeStruct((4 * rows, 2 * rows), BF16)] * 2,
+        out_shape=[jax.ShapeDtypeStruct((cols, 2 * rows), BF16)] * 2,
         scratch_shapes=[
-            pltpu.VMEM((4 * rows, 2 * rows), F32),
+            pltpu.VMEM((cols, 2 * rows), F32),
             pltpu.VMEM((8, height, double // 2), F32),
         ],
         compiler_params=params(),
         name="plane_couple",
-        cost_estimate=pl.CostEstimate(flops=14_000_000_000, bytes_accessed=4_000_000, transcendentals=0),
+        cost_estimate=pl.CostEstimate(
+            flops=2 * 8 * double * cols * rows, bytes_accessed=2_000_000, transcendentals=0
+        ),
     )(first, *metas)
 
 
-def plane_mix_kernel(high_ref, low_ref, a_ref, b_ref, c_ref, d_ref, mine_ref, other_ref):
+def plane_mix_kernel(high0_ref, low0_ref, high1_ref, low1_ref, a_ref, b_ref, c_ref, d_ref, mine_ref, other_ref):
     refs = (a_ref, b_ref, c_ref, d_ref)
     height, rows = a_ref.shape
     hours = height - NOTE
-    value = jnp.concatenate([ref[pl.ds(0, hours), :] for ref in refs], axis=1)
-    one, two = pieces(value, 2)
-    high, low = high_ref[...], low_ref[...]
-    result = (dot(two, high) + dot(one, low)) + dot(one, high)
+    result = None
+    for pair, high_ref, low_ref in ((refs[:2], high0_ref, low0_ref), (refs[2:], high1_ref, low1_ref)):
+        value = jnp.concatenate([ref[pl.ds(0, hours), :] for ref in pair], axis=1)
+        one, two = pieces(value, 2)
+        high, low = high_ref[...], low_ref[...]
+        term = (dot(two, high) + dot(one, low)) + dot(one, high)
+        result = term if result is None else result + term
     note = sum(ref[pl.ds(hours, NOTE), :] for ref in refs)
     mine_ref[pl.ds(0, hours), :] = result[:, :rows]
     other_ref[pl.ds(0, hours), :] = result[:, rows:]
@@ -741,13 +775,13 @@
     other_ref[pl.ds(hours, NOTE), :] = note
 
 
-def plane_mix(high, low, values):
+def plane_mix(coupling, values):
     return pl.pallas_call(
         plane_mix_kernel,
         out_shape=[jax.ShapeDtypeStruct(values[0].shape, F32)] * 2,
         compiler_params=params(),
         name="plane_mix",
-    )(high, low, *values)
+    )(*coupling, *values)
 
 
 def plane_rows_kernel(first_ref, mine_ref, other_ref, a_ref, b_ref, c_ref, d_ref, out_mine_ref, out_other_ref):
@@ -780,7 +814,7 @@
 
 def plane_spectrum_kernel(class_ref, kernels_ref, f0_ref, f1_ref, f2_ref, out_ref):
     classes, taps = kernels_ref.shape
-    kind = jnp.concatenate([class_ref[0:1, :], class_ref[1:2, :]], axis=1)
+    kind = class_ref[class_ref.shape[0] - 7 : class_ref.shape[0] - 6, : out_ref.shape[1]]
     hot = jnp.where(
         lax.broadcasted_iota(jnp.int32, (classes, kind.shape[1]), 0).astype(F32) == kind, 1.0, 0.0
     ).astype(BF16)
@@ -792,13 +826,13 @@
     out_ref[...] = product(mats, chosen, 3)
 
 
-def plane_spectrum(kinds, kernels, forward):
+def plane_spectrum(meta, kernels, forward, rows):
     return pl.pallas_call(
         plane_spectrum_kernel,
-        out_shape=jax.ShapeDtypeStruct((SPAN, 2 * kinds.shape[1]), F32),
+        out_shape=jax.ShapeDtypeStruct((SPAN, rows), F32),
         compiler_params=params(),
         name="plane_spectrum",
-    )(kinds, kernels, *forward)
+    )(meta, kernels, *forward)
 
 
 def sides(even, pair, middle):
@@ -814,7 +848,7 @@
     spec = spec_ref[...]
     before, after = sides(flag_ref[0] > 0.5, pair_ref[...], middle_ref[...])
     now, later = plane_delayed(before, here_ref[...], after, spec, forward, last, 3)
-    start = jnp.transpose(seen_ref[pl.ds(0, rows), :]) - now
+    start = jnp.transpose(seen_ref[...]) - now
     start_later = (jnp.transpose(seen_later_ref[...]) - later) * flag_ref[1]
     out_ref[pl.ds(0, hours), :] = plane_advanced(start, start_later, spec, forward, first, 3)
     out_ref[pl.ds(hours, NOTE), :] = jnp.concatenate(
@@ -945,7 +979,6 @@
 
 def plane_shards(incidence, row_gauge, gauge_kernel, kernels, observed, first_guess):
     rows, hours = observed.shape
-    slots = incidence.shape[1]
     basin, tm = lax.axis_index("basin"), lax.axis_index("tm")
     z, x, y, c = basin // X_, basin % X_, tm // C_, tm % C_
     place = 2 * y + x
@@ -955,36 +988,51 @@
     forward, inverse_first, inverse_last = turned_transforms()
     mats = [*forward, *inverse_first, *inverse_last]
 
-    kinds = gauge_kernel.astype(F32).reshape(rows // hours, hours)
-    parcel = moved(send(incidence, first_guess, row_gauge), to_plane)
-    seen, kinds, parcel = lax.optimization_barrier((observed, kinds, parcel))
+    meta = describe(incidence, row_gauge, gauge_kernel)
+    meta, field = lax.optimization_barrier((meta, first_guess))
+    meta = moved(meta, to_plane)
+    parcel = moved(send(incidence, field), to_plane)
+    metas = [meta, moved(meta, over_core)]
+    both = jnp.concatenate(metas, axis=1)
+    around = [both] + [moved(both, where) for where in SQUARE]
+    spec = plane_spectrum(meta, kernels, forward, rows)
+    seen, parcel, around, spec = lax.optimization_barrier((observed, parcel, around, spec))
     seen_later = moved(seen, to_plane_before)
-    seen = moved(jnp.concatenate([seen, kinds, jnp.zeros((8 - kinds.shape[0], hours), F32)]), to_plane)
-    spec = plane_spectrum(seen[rows : rows + kinds.shape[0]], kernels, forward)
-
-    beside = moved(parcel, over_core)
-    meta = jnp.concatenate([parcel[hours:], beside[hours:]], axis=1)
-    metas = [meta] + [moved(meta, where) for where in SQUARE]
-    dense = spread(first, parcel, beside, hours, rows)
+    seen = moved(seen, to_plane)
+
+    dense = spread(first, [parcel, moved(parcel, over_core)], metas, rows)
     sums = dense[0] + sum(moved(value, where) for value, where in zip(dense[1:], SQUARE))
     sums = [sums, moved(sums, z_pair), moved(sums, z_middle)]
-    high, low = plane_couple(first, metas, rows)
+    coupling = plane_couple(first, around, rows, (0, 1))
+    coupling, sums = lax.optimization_barrier((coupling, sums))
+    coupling = [*coupling, *plane_couple(first, around, rows, (2, 3))]
     pulled = plane_first(flags, sums, seen, seen_later, spec, mats)
-    notes, kept, state = [], [], None
+    notes, kept, state, values = [], [], None, None
+
+    def ship(values):
+        mine, other = plane_rows(first, *metas, values)
+        return moved(mine + moved(other, over_core), from_plane)
+
     for k in range(3):
+        if k:
+            pulled, values = lax.optimization_barrier((pulled, values))
+            kept.append(ship(values))
         values = [pulled] + [moved(pulled, where) for where in SQUARE]
-        mine, other = plane_mix(high, low, values)
+        mine, other = plane_mix(coupling, values)
         mixed = mine + moved(other, over_core)
         note = mixed[hours:]
         sums = [mixed, moved(mixed, z_pair), moved(mixed, z_middle)]
         two, mirror = moved(note, z_two), moved(note, z_mirror)
-        rows_mine, rows_other = plane_rows(first, parcel, beside, values)
-        kept.append(moved(rows_mine + moved(rows_other, over_core), from_plane))
         result = plane_step(flags, sums, two, mirror, pulled, spec, mats, state, k == 2)
         if k == 2:
+            mixed, values = lax.optimization_barrier((mixed, values))
+            kept.append(ship(values))
             total_note, last = result
+            last, kept[1] = lax.optimization_barrier((last, kept[1]))
         else:
             total_note, pulled, state = result
+        if k == 1:
+            pulled, kept[0] = lax.optimization_barrier((pulled, kept[0]))
         notes.append(total_note)
     copies = jnp.broadcast_to(last[None], (Z_ * X_ * Y_ * C_,) + last.shape)
     notes.append(jnp.sum(lax.all_to_all(copies, ("basin", "tm"), 0, 0, tiled=False), axis=0))

time: 157 us -> 160 us (1.019)
  blocking collectives: 20.1 us -> 11.9 us
  Pallas kernels: 32.6 us -> 36.7 us
  waiting for transfers between devices: 32.5 us -> 36 us
  starting transfers between devices: 64.5 us -> 67.6 us
  local copies, waits for them, and re-layouts: 3.49 us -> 5.36 us
    all_to_all x1, blocking collectives: 20.1 us -> 11.9 us  [plane_shards(): lax.all_to_all(copies, ('basin', 'tm'), 0, 0, tiled=False)]
    pallas_call x1 -> x3, Pallas kernels: 8.88 us -> 13.2 us  [the longest x2 13 us: plane_couple(): pl.pallas_call(functools.partial(plane_couple_kernel, owners), in_specs=[...]
    ppermute x42 -> x44, waiting for transfers between devices: 32.5 us -> 36 us  [moved(): return lax.ppermute(value, ('basin', 'tm'), pairs)]
    ppermute x42 -> x44, starting transfers between devices: 64.5 us -> 67.6 us  [moved(): return lax.ppermute(value, ('basin', 'tm'), pairs)]
    unnamed x34 -> x39, local copies, waits for them, and re-layouts: 3.31 us -> 5.26 us
  transfers between devices with their start and end apart: 42 -> 44, of which waited for: 12 -> 19; matrix products, arithmetic and copies ran while one was open for 2% -> 1% of each run, Pallas kernels for 14% -> 13%
where the time goes in v4:
time: 160 us; the launch traced here: 159 us
  starting transfers between devices  67.6 us (42%)
  Pallas kernels  36.7 us (23%)
  waiting for transfers between devices  36 us (22%)
  blocking collectives  11.9 us (7%)
  local copies, waits for them, and re-layouts  5.36 us (3%)
    ppermute x44, starting transfers between devices, moved(): return lax.ppermute(value, ('basin', 'tm'), pairs)  67.6 us
    ppermute x44, waiting for transfers between devices, moved(): return lax.ppermute(value, ('basin', 'tm'), pairs)  36 us
    pallas_call x2, Pallas kernels, plane_couple(): pl.pallas_call(functools.partial(plane_couple_kernel, owners), in_specs=[...  13 us
    all_to_all x1, blocking collectives, plane_shards(): lax.all_to_all(copies, ('basin', 'tm'), 0, 0, tiled=False)  11.9 us
    pallas_call x3, Pallas kernels, plane_step(): pl.pallas_call(functools.partial(plane_step_kernel, opening, final), in_s...  5.9 us
    unnamed x39, local copies, waits for them, and re-layouts  5.26 us
    pallas_call x3, Pallas kernels, plane_rows(): pl.pallas_call(plane_rows_kernel, in_specs=[pl.BlockSpec(memory_space=plt...  3.95 us
    pallas_call x1, Pallas kernels, plane_finish(): pl.pallas_call(plane_finish_kernel, grid=(blocks // step,), in_specs=[who...  3.85 us
  transfers between devices with their start and end apart: 44, of which 19 were waited for; matrix products, arithmetic and copies ran while one was open for 1% of the time, Pallas kernels for 13%

profile of v4, /device:TPU:1, one launch (start us, length us, event | category | flops | bytes accessed | tf_op | source)
XLA Modules:
  0.0 159.2 jit_solution(2013229750651683496)
XLA Ops:
  2.6 4.6 %collective-permute-start.1 = (f32[24,512]{1,0:T(8,128)S(1)}, f32[24,512]{1,0:T(8,128)S(1)}, u32[]{:S(2)}, u32[]{:S(2)}) collective-permute-start(f32[24,512]{1,0:T(8,128)S(1)} %describe.1), channel_id=1, source_target_pairs={{0,0},{1,8},{2,16},{3,24},{4,4},{5,12},{6,20},{7,28},{8,2},{9,10},... | collective-permute-start | bytes 147464 | tf_op jit(solution)/shard_map/ppermute | solution.py:499
  10.5 3.3 %collective-permute-start = (f32[128,512]{1,0:T(8,128)S(1)}, f32[128,512]{1,0:T(8,128)S(1)}, u32[]{:S(2)}, u32[]{:S(2)}) collective-permute-start(f32[128,512]{1,0:T(8,128)S(1)} %send.1), channel_id=1, source_target_pairs={{0,0},{1,8},{2,16},{3,24},{4,4},{5,12},{6,20},{7,28},{8,2},{9,10},... | collective-permute-start | bytes 786440 | tf_op jit(solution)/shard_map/ppermute | solution.py:499
  15.1 3.3 %collective-permute-start.5 = (f32[24,1024]{1,0:T(8,128)S(1)}, f32[24,1024]{1,0:T(8,128)S(1)}, u32[]{:S(2)}, u32[]{:S(2)}) collective-permute-start(f32[24,1024]{1,0:T(8,128)S(1)} %constant_dynamic-update-slice_fusion.a_ref), channel_id=1, source_target_pairs={{0,6},{1,7},{2,4},{3,5},{4,2},{5,3},{6,0},{7,1},{8,14},{9,15},{10,... | collective-permute-start | bytes 294920 | tf_op jit(solution)/shard_map/ppermute | solution.py:499
  19.5 2.0 %collective-permute-done.5.d_ref = f32[24,1024]{1,0:T(8,128)S(1)} collective-permute-done((f32[24,1024]{1,0:T(8,128)S(1)}, f32[24,1024]{1,0:T(8,128)S(1)}, u32[]{:S(2)}, u32[]{:S(2)}) %collective-permute-start.5) | collective-permute-done | bytes 98336 | tf_op jit(solution)/shard_map/ppermute | solution.py:499
  21.4 5.7 %collective-permute-done.4.c_ref = f32[24,1024]{1,0:T(8,128)S(1)} collective-permute-done((f32[24,1024]{1,0:T(8,128)S(1)}, f32[24,1024]{1,0:T(8,128)S(1)}, u32[]{:S(2)}, u32[]{:S(2)}) %collective-permute-start.4) | collective-permute-done | bytes 98336 | tf_op jit(solution)/shard_map/ppermute | solution.py:499
  29.1 2.7 %spread.1 = (f32[128,256]{1,0:T(8,128)S(1)}, f32[128,256]{1,0:T(8,128)S(1)}, f32[128,256]{1,0:T(8,128)S(1)}, f32[128,256]{1,0:T(8,128)S(1)}) custom-call(s32[6]{0:T(128)S(1)} %broadcast_multiply_fusion.first_ref, f32[128,512]{1,0:T(8,128)S(1)} %collective-permute-done.mine_ref, f32[128,512]{1,0:T(8,128)S(1)} %collective-permute-done.6.other_ref, ...), custom_call_target="tpu_custom_call" | custom-call | tf_op jit(solution)/shard_map/spread/pallas_call | solution.py:684
  33.0 1.9 %collective-permute-start.8 = (f32[128,256]{1,0:T(8,128)S(1)}, f32[128,256]{1,0:T(8,128)S(1)}, u32[]{:S(2)}, u32[]{:S(2)}) collective-permute-start(f32[128,256]{1,0:T(8,128)S(1)} %get-tuple-element.76), channel_id=1, source_target_pairs={{0,2},{1,3},{2,0},{3,1},{4,6},{5,7},{6,4},{7,5},{8,10},{9,11},{10,... | collective-permute-start | bytes 393224 | tf_op jit(solution)/shard_map/ppermute | solution.py:499
  35.1 2.9 %collective-permute-start.13 = (f32[256,128]{1,0:T(8,128)S(1)}, f32[256,128]{1,0:T(8,128)S(1)}, u32[]{:S(2)}, u32[]{:S(2)}) collective-permute-start(f32[256,128]{1,0:T(8,128)S(1)} %copy-done.18), channel_id=1, source_target_pairs={{1,0},{2,8},{3,16},{5,4},{6,12},{7,20},{9,2},{10,10},{11,18},{13,6... | collective-permute-start | bytes 393224 | tf_op jit(solution)/shard_map/ppermute | solution.py:499
  37.9 1.9 %collective-permute-start.12 = (f32[256,128]{1,0:T(8,128)S(1)}, f32[256,128]{1,0:T(8,128)S(1)}, u32[]{:S(2)}, u32[]{:S(2)}) collective-permute-start(f32[256,128]{1,0:T(8,128)S(1)} %copy-done.18), channel_id=1, source_target_pairs={{0,0},{1,8},{2,16},{3,24},{4,4},{5,12},{6,20},{7,28},{8,2},{9,10},... | collective-permute-start | bytes 393224 | tf_op jit(solution)/shard_map/ppermute | solution.py:499
  41.7 4.6 %collective-permute-start.10 = (f32[128,256]{1,0:T(8,128)S(1)}, f32[128,256]{1,0:T(8,128)S(1)}, u32[]{:S(2)}, u32[]{:S(2)}) collective-permute-start(f32[128,256]{1,0:T(8,128)S(1)} %add_add_fusion.here_ref), channel_id=1, source_target_pairs={{0,8},{1,9},{2,10},{3,11},{4,12},{5,13},{6,14},{7,15},{8,0},{9,1},... | collective-permute-start | bytes 393224 | tf_op jit(solution)/shard_map/ppermute | solution.py:499
  46.4 6.5 %plane_couple.2 = (bf16[512,512]{1,0:T(8,128)(2,1)S(1)}, bf16[512,512]{1,0:T(8,128)(2,1)S(1)}) custom-call(s32[6]{0:T(128)S(1)} %broadcast_multiply_fusion.first_ref, f32[24,1024]{1,0:T(8,128)S(1)} %constant_dynamic-update-slice_fusion.a_ref, f32[24,1024]{1,0:T(8,128)S(1)} %collective-permute-done.3.b_ref, f32[24,1024]{1,0:T(8,128)S(1)} %collective-permute-done.4.c_ref, ...), custom_call_target="tpu_custom_call" | custom-call | flops 2147483648 | bytes 2000000 | tf_op jit(solution)/shard_map/plane_couple/pallas_call | solution.py:744
  53.0 3.0 %plane_first.1.a_ref.pulled_ref = f32[136,256]{1,0:T(8,128)S(1)} custom-call(f32[2]{0:T(128)S(1)} %add_convert_fusion.flag_ref, f32[128,256]{1,0:T(8,128)S(1)} %add_add_fusion.here_ref, f32[128,256]{1,0:T(8,128)S(1)} %collective-permute-done.10.pair_ref, f32[128,256]{1,0:T(8,128)S(1)} %collective-permute-done.11.middle_ref, ...), custom_call_target="tpu_custom_call" | custom-call | tf_op jit(solution)/shard_map/plane_first/pallas_call | solution.py:862
  58.7 6.5 %plane_couple.3 = (bf16[512,512]{1,0:T(8,128)(2,1)S(1)}, bf16[512,512]{1,0:T(8,128)(2,1)S(1)}) custom-call(s32[6]{0:T(128)S(1)} %broadcast_multiply_fusion.first_ref, f32[24,1024]{1,0:T(8,128)S(1)} %constant_dynamic-update-slice_fusion.a_ref, f32[24,1024]{1,0:T(8,128)S(1)} %collective-permute-done.3.b_ref, f32[24,1024]{1,0:T(8,128)S(1)} %collective-permute-done.4.c_ref, ...), custom_call_target="tpu_custom_call" | custom-call | flops 2147483648 | bytes 2000000 | tf_op jit(solution)/shard_map/plane_couple/pallas_call | solution.py:744
  68.2 2.2 %collective-permute-start.18 = (f32[136,256]{1,0:T(8,128)S(1)}, f32[136,256]{1,0:T(8,128)S(1)}, u32[]{:S(2)}, u32[]{:S(2)}) collective-permute-start(f32[136,256]{1,0:T(8,128)S(1)} %add.70.here_ref), channel_id=1, source_target_pairs={{0,8},{1,9},{2,10},{3,11},{4,12},{5,13},{6,14},{7,15},{8,0},{9,1},... | collective-permute-start | bytes 417800 | tf_op jit(solution)/shard_map/ppermute | solution.py:499
  70.4 2.2 %collective-permute-start.21 = (f32[8,256]{1,0:T(8,128)S(1)}, f32[8,256]{1,0:T(8,128)S(1)}, u32[]{:S(2)}, u32[]{:S(2)}) collective-permute-start(f32[8,256]{1,0:T(8,128)S(1)} %slice.12), channel_id=1, source_target_pairs={{0,24},{1,25},{2,26},{3,27},{4,28},{5,29},{6,30},{7,31},{8,16},{9,... | collective-permute-start | bytes 24584 | tf_op jit(solution)/shard_map/ppermute | solution.py:499
  72.6 3.0 %collective-permute-done.21.mirror_ref = f32[8,256]{1,0:T(8,128)S(1)} collective-permute-done((f32[8,256]{1,0:T(8,128)S(1)}, f32[8,256]{1,0:T(8,128)S(1)}, u32[]{:S(2)}, u32[]{:S(2)}) %collective-permute-start.21) | collective-permute-done | bytes 8224 | tf_op jit(solution)/shard_map/ppermute | solution.py:499
  76.0 2.3 %plane_step.3 = (f32[8,256]{1,0:T(8,128)S(1)}, f32[136,256]{1,0:T(8,128)S(1)}, f32[1024,256]{1,0:T(8,128)S(1)}) custom-call(f32[2]{0:T(128)S(1)} %add_convert_fusion.flag_ref, f32[136,256]{1,0:T(8,128)S(1)} %add.70.here_ref, f32[136,256]{1,0:T(8,128)S(1)} %collective-permute-done.18.pair_ref, f32[136,256]{1,0:T(8,128)S(1)} %collective-permute-done.19.middle_ref, ...), custom_call_target="tpu_custom_call" | custom-call | tf_op jit(solution)/shard_map/plane_step/pallas_call | solution.py:928
  79.6 2.4 %collective-permute-start.30 = (f32[128,512]{1,0:T(8,128)S(1)}, f32[128,512]{1,0:T(8,128)S(1)}, u32[]{:S(2)}, u32[]{:S(2)}) collective-permute-start(f32[128,512]{1,0:T(8,128)S(1)} %get-tuple-element.102), channel_id=1, source_target_pairs={{0,1},{1,0},{2,3},{3,2},{4,5},{5,4},{6,7},{7,6},{8,9},{9,8},{10,11... | collective-permute-start | bytes 786440 | tf_op jit(solution)/shard_map/ppermute | solution.py:499
  85.0 3.3 %collective-permute-done.24.d_ref = f32[136,256]{1,0:T(8,128)S(1)} collective-permute-done((f32[136,256]{1,0:T(8,128)S(1)}, f32[136,256]{1,0:T(8,128)S(1)}, u32[]{:S(2)}, u32[]{:S(2)}) %collective-permute-start.24) | collective-permute-done | bytes 139296 | tf_op jit(solution)/shard_map/ppermute | solution.py:499
  88.2 3.3 %collective-permute-done.23.c_ref = f32[136,256]{1,0:T(8,128)S(1)} collective-permute-done((f32[136,256]{1,0:T(8,128)S(1)}, f32[136,256]{1,0:T(8,128)S(1)}, u32[]{:S(2)}, u32[]{:S(2)}) %collective-permute-start.23) | collective-permute-done | bytes 139296 | tf_op jit(solution)/shard_map/ppermute | solution.py:499
  98.0 1.9 %collective-permute-start.29 = (f32[8,256]{1,0:T(8,128)S(1)}, f32[8,256]{1,0:T(8,128)S(1)}, u32[]{:S(2)}, u32[]{:S(2)}) collective-permute-start(f32[8,256]{1,0:T(8,128)S(1)} %slice.13), channel_id=1, source_target_pairs={{0,24},{1,25},{2,26},{3,27},{4,28},{5,29},{6,30},{7,31},{8,16},{9,... | collective-permute-start | bytes 24584 | tf_op jit(solution)/shard_map/ppermute | solution.py:499
  99.9 4.1 %collective-permute-done.29.mirror_ref = f32[8,256]{1,0:T(8,128)S(1)} collective-permute-done((f32[8,256]{1,0:T(8,128)S(1)}, f32[8,256]{1,0:T(8,128)S(1)}, u32[]{:S(2)}, u32[]{:S(2)}) %collective-permute-start.29) | collective-permute-done | bytes 8224 | tf_op jit(solution)/shard_map/ppermute | solution.py:499
  105.7 2.0 %collective-permute-done.26.pair_ref = f32[136,256]{1,0:T(8,128)S(1)} collective-permute-done((f32[136,256]{1,0:T(8,128)S(1)}, f32[136,256]{1,0:T(8,128)S(1)}, u32[]{:S(2)}, u32[]{:S(2)}) %collective-permute-start.26) | collective-permute-done | bytes 139296 | tf_op jit(solution)/shard_map/ppermute | solution.py:499
  107.7 2.3 %plane_step.4 = (f32[8,256]{1,0:T(8,128)S(1)}, f32[136,256]{1,0:T(8,128)S(1)}, f32[1024,256]{1,0:T(8,128)S(1)}) custom-call(f32[2]{0:T(128)S(1)} %add_convert_fusion.flag_ref, f32[136,256]{1,0:T(8,128)S(1)} %add.71.here_ref, f32[136,256]{1,0:T(8,128)S(1)} %collective-permute-done.26.pair_ref, f32[136,256]{1,0:T(8,128)S(1)} %collective-permute-done.27.middle_ref, ...), custom_call_target="tpu_custom_call" | custom-call | tf_op jit(solution)/shard_map/plane_step/pallas_call | solution.py:928
  114.1 3.8 %collective-permute-start.40 = (f32[128,512]{1,0:T(8,128)S(1)}, f32[128,512]{1,0:T(8,128)S(1)}, u32[]{:S(2)}, u32[]{:S(2)}) collective-permute-start(f32[128,512]{1,0:T(8,128)S(1)} %get-tuple-element.115), channel_id=1, source_target_pairs={{0,1},{1,0},{2,3},{3,2},{4,5},{5,4},{6,7},{7,6},{8,9},{9,8},{10,11... | collective-permute-start | bytes 786440 | tf_op jit(solution)/shard_map/ppermute | solution.py:499
  118.5 2.0 %collective-permute-start.35 = (f32[136,256]{1,0:T(8,128)S(1)}, f32[136,256]{1,0:T(8,128)S(1)}, u32[]{:S(2)}, u32[]{:S(2)}) collective-permute-start(f32[136,256]{1,0:T(8,128)S(1)} %get-tuple-element.106), channel_id=1, source_target_pairs={{0,1},{1,0},{2,3},{3,2},{4,5},{5,4},{6,7},{7,6},{8,9},{9,8},{10,11... | collective-permute-start | bytes 417800 | tf_op jit(solution)/shard_map/ppermute | solution.py:499
  123.4 2.2 %collective-permute-start.41 = (f32[128,512]{1,0:T(8,128)S(1)}, f32[128,512]{1,0:T(8,128)S(1)}, u32[]{:S(2)}, u32[]{:S(2)}) collective-permute-start(f32[128,512]{1,0:T(8,128)S(1)} %add.74), channel_id=1, source_target_pairs={{0,0},{1,16},{2,8},{3,24},{4,4},{5,20},{6,12},{7,28},{8,1},{9,17},... | collective-permute-start | bytes 786440 | tf_op jit(solution)/shard_map/ppermute | solution.py:499
  126.3 2.7 %collective-permute-start.36 = (f32[136,256]{1,0:T(8,128)S(1)}, f32[136,256]{1,0:T(8,128)S(1)}, u32[]{:S(2)}, u32[]{:S(2)}) collective-permute-start(f32[136,256]{1,0:T(8,128)S(1)} %add.73.here_ref), channel_id=1, source_target_pairs={{0,8},{1,9},{2,10},{3,11},{4,12},{5,13},{6,14},{7,15},{8,0},{9,1},... | collective-permute-start | bytes 417800 | tf_op jit(solution)/shard_map/ppermute | solution.py:499
  131.0 4.1 %collective-permute-done.39.mirror_ref = f32[8,256]{1,0:T(8,128)S(1)} collective-permute-done((f32[8,256]{1,0:T(8,128)S(1)}, f32[8,256]{1,0:T(8,128)S(1)}, u32[]{:S(2)}, u32[]{:S(2)}) %collective-permute-start.39) | collective-permute-done | bytes 8224 | tf_op jit(solution)/shard_map/ppermute | solution.py:499
  135.2 5.5 %collective-permute-start.43 = (f32[128,512]{1,0:T(8,128)}, f32[128,512]{1,0:T(8,128)}, u32[]{:S(2)}, u32[]{:S(2)}) collective-permute-start(f32[128,512]{1,0:T(8,128)} %add.75), channel_id=1, source_target_pairs={{0,0},{1,16},{2,8},{3,24},{4,4},{5,20},{6,12},{7,28},{8,1},{9,17},... | collective-permute-start | bytes 786440 | tf_op jit(solution)/shard_map/ppermute | solution.py:499
  142.7 11.9 %all_to_all.5 = f32[32,8,128]{2,1,0:T(8,128)S(1)} all-to-all(f32[32,8,128]{2,1,0:T(8,128)S(1)} %broadcast_in_dim.2), channel_id=1, replica_groups=mesh['basin'=8,'tm'=4] {'basin','tm'}, dimensions={0} | all-to-all | bytes 262144 | tf_op jit(solution)/shard_map/all_to_all | solution.py:1038
  155.3 3.9 %plane_finish.1 = f32[4096,128]{1,0:T(8,128)} custom-call(f32[8,256]{1,0:T(8,128)S(1)} %get-tuple-element.89.n0, f32[8,256]{1,0:T(8,128)S(1)} %get-tuple-element.95.n1, f32[8,256]{1,0:T(8,128)S(1)} %copy-done.15, f32[8,128]{1,0:T(8,128)S(1)} %reduce_sum.9.n3, f32[128,512]{1,0:T(8,128)S(1)} %collective-permute-done.31.q0, ...), custom_call_target="tpu_custom_call" | custom-call | tf_op jit(solution)/shard_map/plane_finish/pallas_call | solution.py:963
  (129 shorter events, 44.3 us)
Async XLA Ops:
  2.6 11.2 %collective-permute-start.1 = (f32[24,512]{1,0:T(8,128)S(1)}, f32[24,512]{1,0:T(8,128)S(1)}, u32[]{:S(2)}, u32[]{:S(2)}) collective-permute-start(f32[24,512]{1,0:T(8,128)S(1)} %describe.1), channel_id=1, source_target_pairs={{0,0},{1,8},{2,16},{3,24},{4,4},{5,12},{6,20},{7,28},{8,2},{9,10},... | collective-permute-start | bytes 147464 | tf_op jit(solution)/shard_map/ppermute | solution.py:499
  10.5 17.1 %collective-permute-start = (f32[128,512]{1,0:T(8,128)S(1)}, f32[128,512]{1,0:T(8,128)S(1)}, u32[]{:S(2)}, u32[]{:S(2)}) collective-permute-start(f32[128,512]{1,0:T(8,128)S(1)} %send.1), channel_id=1, source_target_pairs={{0,0},{1,8},{2,16},{3,24},{4,4},{5,12},{6,20},{7,28},{8,2},{9,10},... | collective-permute-start | bytes 786440 | tf_op jit(solution)/shard_map/ppermute | solution.py:499
  15.1 6.4 %collective-permute-start.5 = (f32[24,1024]{1,0:T(8,128)S(1)}, f32[24,1024]{1,0:T(8,128)S(1)}, u32[]{:S(2)}, u32[]{:S(2)}) collective-permute-start(f32[24,1024]{1,0:T(8,128)S(1)} %constant_dynamic-update-slice_fusion.a_ref), channel_id=1, source_target_pairs={{0,6},{1,7},{2,4},{3,5},{4,2},{5,3},{6,0},{7,1},{8,14},{9,15},{10,... | collective-permute-start | bytes 294920 | tf_op jit(solution)/shard_map/ppermute | solution.py:499
  18.4 8.7 %collective-permute-start.4 = (f32[24,1024]{1,0:T(8,128)S(1)}, f32[24,1024]{1,0:T(8,128)S(1)}, u32[]{:S(2)}, u32[]{:S(2)}) collective-permute-start(f32[24,1024]{1,0:T(8,128)S(1)} %constant_dynamic-update-slice_fusion.a_ref), channel_id=1, source_target_pairs={{0,2},{1,3},{2,0},{3,1},{4,6},{5,7},{6,4},{7,5},{8,10},{9,11},{10,... | collective-permute-start | bytes 294920 | tf_op jit(solution)/shard_map/ppermute | solution.py:499
  18.4 8.7 %collective-permute-start.3 = (f32[24,1024]{1,0:T(8,128)S(1)}, f32[24,1024]{1,0:T(8,128)S(1)}, u32[]{:S(2)}, u32[]{:S(2)}) collective-permute-start(f32[24,1024]{1,0:T(8,128)S(1)} %constant_dynamic-update-slice_fusion.a_ref), channel_id=1, source_target_pairs={{0,4},{1,5},{2,6},{3,7},{4,0},{5,1},{6,2},{7,3},{8,12},{9,13},{10,... | collective-permute-start | bytes 294920 | tf_op jit(solution)/shard_map/ppermute | solution.py:499
  31.8 8.0 %collective-permute-start.7 = (f32[128,256]{1,0:T(8,128)S(1)}, f32[128,256]{1,0:T(8,128)S(1)}, u32[]{:S(2)}, u32[]{:S(2)}) collective-permute-start(f32[128,256]{1,0:T(8,128)S(1)} %get-tuple-element.75), channel_id=1, source_target_pairs={{0,4},{1,5},{2,6},{3,7},{4,0},{5,1},{6,2},{7,3},{8,12},{9,13},{10,... | collective-permute-start | bytes 393224 | tf_op jit(solution)/shard_map/ppermute | solution.py:499
  33.0 6.9 %collective-permute-start.8 = (f32[128,256]{1,0:T(8,128)S(1)}, f32[128,256]{1,0:T(8,128)S(1)}, u32[]{:S(2)}, u32[]{:S(2)}) collective-permute-start(f32[128,256]{1,0:T(8,128)S(1)} %get-tuple-element.76), channel_id=1, source_target_pairs={{0,2},{1,3},{2,0},{3,1},{4,6},{5,7},{6,4},{7,5},{8,10},{9,11},{10,... | collective-permute-start | bytes 393224 | tf_op jit(solution)/shard_map/ppermute | solution.py:499
  35.1 17.8 %collective-permute-start.13 = (f32[256,128]{1,0:T(8,128)S(1)}, f32[256,128]{1,0:T(8,128)S(1)}, u32[]{:S(2)}, u32[]{:S(2)}) collective-permute-start(f32[256,128]{1,0:T(8,128)S(1)} %copy-done.18), channel_id=1, source_target_pairs={{1,0},{2,8},{3,16},{5,4},{6,12},{7,20},{9,2},{10,10},{11,18},{13,6... | collective-permute-start | bytes 393224 | tf_op jit(solution)/shard_map/ppermute | solution.py:499
  37.9 15.0 %collective-permute-start.12 = (f32[256,128]{1,0:T(8,128)S(1)}, f32[256,128]{1,0:T(8,128)S(1)}, u32[]{:S(2)}, u32[]{:S(2)}) collective-permute-start(f32[256,128]{1,0:T(8,128)S(1)} %copy-done.18), channel_id=1, source_target_pairs={{0,0},{1,8},{2,16},{3,24},{4,4},{5,12},{6,20},{7,28},{8,2},{9,10},... | collective-permute-start | bytes 393224 | tf_op jit(solution)/shard_map/ppermute | solution.py:499
  40.9 12.0 %collective-permute-start.11 = (f32[128,256]{1,0:T(8,128)S(1)}, f32[128,256]{1,0:T(8,128)S(1)}, u32[]{:S(2)}, u32[]{:S(2)}) collective-permute-start(f32[128,256]{1,0:T(8,128)S(1)} %add_add_fusion.here_ref), channel_id=1, source_target_pairs={{8,16},{9,17},{10,18},{11,19},{12,20},{13,21},{14,22},{15,23},{16,... | collective-permute-start | bytes 393224 | tf_op jit(solution)/shard_map/ppermute | solution.py:499
  41.7 11.2 %collective-permute-start.10 = (f32[128,256]{1,0:T(8,128)S(1)}, f32[128,256]{1,0:T(8,128)S(1)}, u32[]{:S(2)}, u32[]{:S(2)}) collective-permute-start(f32[128,256]{1,0:T(8,128)S(1)} %add_add_fusion.here_ref), channel_id=1, source_target_pairs={{0,8},{1,9},{2,10},{3,11},{4,12},{5,13},{6,14},{7,15},{8,0},{9,1},... | collective-permute-start | bytes 393224 | tf_op jit(solution)/shard_map/ppermute | solution.py:499
  56.0 9.2 %collective-permute-start.16 = (f32[136,256]{1,0:T(8,128)S(1)}, f32[136,256]{1,0:T(8,128)S(1)}, u32[]{:S(2)}, u32[]{:S(2)}) collective-permute-start(f32[136,256]{1,0:T(8,128)S(1)} %plane_first.1.a_ref.pulled_ref), channel_id=1, source_target_pairs={{0,6},{1,7},{2,4},{3,5},{4,2},{5,3},{6,0},{7,1},{8,14},{9,15},{10,... | collective-permute-start | bytes 417800 | tf_op jit(solution)/shard_map/ppermute | solution.py:499
  57.9 7.6 %collective-permute-start.15 = (f32[136,256]{1,0:T(8,128)S(1)}, f32[136,256]{1,0:T(8,128)S(1)}, u32[]{:S(2)}, u32[]{:S(2)}) collective-permute-start(f32[136,256]{1,0:T(8,128)S(1)} %plane_first.1.a_ref.pulled_ref), channel_id=1, source_target_pairs={{0,2},{1,3},{2,0},{3,1},{4,6},{5,7},{6,4},{7,5},{8,10},{9,11},{10,... | collective-permute-start | bytes 417800 | tf_op jit(solution)/shard_map/ppermute | solution.py:499
  58.5 7.0 %collective-permute-start.14 = (f32[136,256]{1,0:T(8,128)S(1)}, f32[136,256]{1,0:T(8,128)S(1)}, u32[]{:S(2)}, u32[]{:S(2)}) collective-permute-start(f32[136,256]{1,0:T(8,128)S(1)} %plane_first.1.a_ref.pulled_ref), channel_id=1, source_target_pairs={{0,4},{1,5},{2,6},{3,7},{4,0},{5,1},{6,2},{7,3},{8,12},{9,13},{10,... | collective-permute-start | bytes 417800 | tf_op jit(solution)/shard_map/ppermute | solution.py:499
  67.5 8.5 %collective-permute-start.19 = (f32[136,256]{1,0:T(8,128)S(1)}, f32[136,256]{1,0:T(8,128)S(1)}, u32[]{:S(2)}, u32[]{:S(2)}) collective-permute-start(f32[136,256]{1,0:T(8,128)S(1)} %add.70.here_ref), channel_id=1, source_target_pairs={{8,16},{9,17},{10,18},{11,19},{12,20},{13,21},{14,22},{15,23},{16,... | collective-permute-start | bytes 417800 | tf_op jit(solution)/shard_map/ppermute | solution.py:499
  68.2 7.8 %collective-permute-start.18 = (f32[136,256]{1,0:T(8,128)S(1)}, f32[136,256]{1,0:T(8,128)S(1)}, u32[]{:S(2)}, u32[]{:S(2)}) collective-permute-start(f32[136,256]{1,0:T(8,128)S(1)} %add.70.here_ref), channel_id=1, source_target_pairs={{0,8},{1,9},{2,10},{3,11},{4,12},{5,13},{6,14},{7,15},{8,0},{9,1},... | collective-permute-start | bytes 417800 | tf_op jit(solution)/shard_map/ppermute | solution.py:499
  79.6 13.6 %collective-permute-start.30 = (f32[128,512]{1,0:T(8,128)S(1)}, f32[128,512]{1,0:T(8,128)S(1)}, u32[]{:S(2)}, u32[]{:S(2)}) collective-permute-start(f32[128,512]{1,0:T(8,128)S(1)} %get-tuple-element.102), channel_id=1, source_target_pairs={{0,1},{1,0},{2,3},{3,2},{4,5},{5,4},{6,7},{7,6},{8,9},{9,8},{10,11... | collective-permute-start | bytes 786440 | tf_op jit(solution)/shard_map/ppermute | solution.py:499
  82.0 6.2 %collective-permute-start.24 = (f32[136,256]{1,0:T(8,128)S(1)}, f32[136,256]{1,0:T(8,128)S(1)}, u32[]{:S(2)}, u32[]{:S(2)}) collective-permute-start(f32[136,256]{1,0:T(8,128)S(1)} %get-tuple-element.110.a_ref.pulled_ref), channel_id=1, source_target_pairs={{0,6},{1,7},{2,4},{3,5},{4,2},{5,3},{6,0},{7,1},{8,14},{9,15},{10,... | collective-permute-start | bytes 417800 | tf_op jit(solution)/shard_map/ppermute | solution.py:499
  83.2 8.3 %collective-permute-start.23 = (f32[136,256]{1,0:T(8,128)S(1)}, f32[136,256]{1,0:T(8,128)S(1)}, u32[]{:S(2)}, u32[]{:S(2)}) collective-permute-start(f32[136,256]{1,0:T(8,128)S(1)} %get-tuple-element.110.a_ref.pulled_ref), channel_id=1, source_target_pairs={{0,2},{1,3},{2,0},{3,1},{4,6},{5,7},{6,4},{7,5},{8,10},{9,11},{10,... | collective-permute-start | bytes 417800 | tf_op jit(solution)/shard_map/ppermute | solution.py:499
  83.9 7.9 %collective-permute-start.22 = (f32[136,256]{1,0:T(8,128)S(1)}, f32[136,256]{1,0:T(8,128)S(1)}, u32[]{:S(2)}, u32[]{:S(2)}) collective-permute-start(f32[136,256]{1,0:T(8,128)S(1)} %get-tuple-element.110.a_ref.pulled_ref), channel_id=1, source_target_pairs={{0,4},{1,5},{2,6},{3,7},{4,0},{5,1},{6,2},{7,3},{8,12},{9,13},{10,... | collective-permute-start | bytes 417800 | tf_op jit(solution)/shard_map/ppermute | solution.py:499
  93.3 16.7 %collective-permute-start.31 = (f32[128,512]{1,0:T(8,128)S(1)}, f32[128,512]{1,0:T(8,128)S(1)}, u32[]{:S(2)}, u32[]{:S(2)}) collective-permute-start(f32[128,512]{1,0:T(8,128)S(1)} %add.72), channel_id=1, source_target_pairs={{0,0},{1,16},{2,8},{3,24},{4,4},{5,20},{6,12},{7,28},{8,1},{9,17},... | collective-permute-start | bytes 786440 | tf_op jit(solution)/shard_map/ppermute | solution.py:499
  95.3 10.5 %collective-permute-start.27 = (f32[136,256]{1,0:T(8,128)S(1)}, f32[136,256]{1,0:T(8,128)S(1)}, u32[]{:S(2)}, u32[]{:S(2)}) collective-permute-start(f32[136,256]{1,0:T(8,128)S(1)} %add.71.here_ref), channel_id=1, source_target_pairs={{8,16},{9,17},{10,18},{11,19},{12,20},{13,21},{14,22},{15,23},{16,... | collective-permute-start | bytes 417800 | tf_op jit(solution)/shard_map/ppermute | solution.py:499
  96.1 11.6 %collective-permute-start.26 = (f32[136,256]{1,0:T(8,128)S(1)}, f32[136,256]{1,0:T(8,128)S(1)}, u32[]{:S(2)}, u32[]{:S(2)}) collective-permute-start(f32[136,256]{1,0:T(8,128)S(1)} %add.71.here_ref), channel_id=1, source_target_pairs={{0,8},{1,9},{2,10},{3,11},{4,12},{5,13},{6,14},{7,15},{8,0},{9,1},... | collective-permute-start | bytes 417800 | tf_op jit(solution)/shard_map/ppermute | solution.py:499
  110.1 7.9 %collective-permute-start.34 = (f32[136,256]{1,0:T(8,128)S(1)}, f32[136,256]{1,0:T(8,128)S(1)}, u32[]{:S(2)}, u32[]{:S(2)}) collective-permute-start(f32[136,256]{1,0:T(8,128)S(1)} %get-tuple-element.119.a_ref.pulled_ref), channel_id=1, source_target_pairs={{0,6},{1,7},{2,4},{3,5},{4,2},{5,3},{6,0},{7,1},{8,14},{9,15},{10,... | collective-permute-start | bytes 417800 | tf_op jit(solution)/shard_map/ppermute | solution.py:499
  110.1 7.8 %collective-permute-start.33 = (f32[136,256]{1,0:T(8,128)S(1)}, f32[136,256]{1,0:T(8,128)S(1)}, u32[]{:S(2)}, u32[]{:S(2)}) collective-permute-start(f32[136,256]{1,0:T(8,128)S(1)} %get-tuple-element.119.a_ref.pulled_ref), channel_id=1, source_target_pairs={{0,2},{1,3},{2,0},{3,1},{4,6},{5,7},{6,4},{7,5},{8,10},{9,11},{10,... | collective-permute-start | bytes 417800 | tf_op jit(solution)/shard_map/ppermute | solution.py:499
  114.1 9.3 %collective-permute-start.40 = (f32[128,512]{1,0:T(8,128)S(1)}, f32[128,512]{1,0:T(8,128)S(1)}, u32[]{:S(2)}, u32[]{:S(2)}) collective-permute-start(f32[128,512]{1,0:T(8,128)S(1)} %get-tuple-element.115), channel_id=1, source_target_pairs={{0,1},{1,0},{2,3},{3,2},{4,5},{5,4},{6,7},{7,6},{8,9},{9,8},{10,11... | collective-permute-start | bytes 786440 | tf_op jit(solution)/shard_map/ppermute | solution.py:499
  122.9 7.2 %collective-permute-start.42 = (f32[128,512]{1,0:T(8,128)S(1)}, f32[128,512]{1,0:T(8,128)S(1)}, u32[]{:S(2)}, u32[]{:S(2)}) collective-permute-start(f32[128,512]{1,0:T(8,128)S(1)} %get-tuple-element.124), channel_id=1, source_target_pairs={{0,1},{1,0},{2,3},{3,2},{4,5},{5,4},{6,7},{7,6},{8,9},{9,8},{10,11... | collective-permute-start | bytes 786440 | tf_op jit(solution)/shard_map/ppermute | solution.py:499
  123.4 18.7 %collective-permute-start.41 = (f32[128,512]{1,0:T(8,128)S(1)}, f32[128,512]{1,0:T(8,128)S(1)}, u32[]{:S(2)}, u32[]{:S(2)}) collective-permute-start(f32[128,512]{1,0:T(8,128)S(1)} %add.74), channel_id=1, source_target_pairs={{0,0},{1,16},{2,8},{3,24},{4,4},{5,20},{6,12},{7,28},{8,1},{9,17},... | collective-permute-start | bytes 786440 | tf_op jit(solution)/shard_map/ppermute | solution.py:499
  125.6 15.1 %collective-permute-start.37 = (f32[136,256]{1,0:T(8,128)S(1)}, f32[136,256]{1,0:T(8,128)S(1)}, u32[]{:S(2)}, u32[]{:S(2)}) collective-permute-start(f32[136,256]{1,0:T(8,128)S(1)} %add.73.here_ref), channel_id=1, source_target_pairs={{8,16},{9,17},{10,18},{11,19},{12,20},{13,21},{14,22},{15,23},{16,... | collective-permute-start | bytes 417800 | tf_op jit(solution)/shard_map/ppermute | solution.py:499
  126.3 14.5 %collective-permute-start.36 = (f32[136,256]{1,0:T(8,128)S(1)}, f32[136,256]{1,0:T(8,128)S(1)}, u32[]{:S(2)}, u32[]{:S(2)}) collective-permute-start(f32[136,256]{1,0:T(8,128)S(1)} %add.73.here_ref), channel_id=1, source_target_pairs={{0,8},{1,9},{2,10},{3,11},{4,12},{5,13},{6,14},{7,15},{8,0},{9,1},... | collective-permute-start | bytes 417800 | tf_op jit(solution)/shard_map/ppermute | solution.py:499
  130.1 10.6 %collective-permute-start.38 = (f32[8,256]{1,0:T(8,128)S(1)}, f32[8,256]{1,0:T(8,128)S(1)}, u32[]{:S(2)}, u32[]{:S(2)}) collective-permute-start(f32[8,256]{1,0:T(8,128)S(1)} %slice.14), channel_id=1, source_target_pairs={{0,16},{1,17},{2,18},{3,19},{4,20},{5,21},{6,22},{7,23},{8,24},{9,... | collective-permute-start | bytes 24584 | tf_op jit(solution)/shard_map/ppermute | solution.py:499
  135.2 19.4 %collective-permute-start.43 = (f32[128,512]{1,0:T(8,128)}, f32[128,512]{1,0:T(8,128)}, u32[]{:S(2)}, u32[]{:S(2)}) collective-permute-start(f32[128,512]{1,0:T(8,128)} %add.75), channel_id=1, source_target_pairs={{0,0},{1,16},{2,8},{3,24},{4,4},{5,20},{6,12},{7,28},{8,1},{9,17},... | collective-permute-start | bytes 786440 | tf_op jit(solution)/shard_map/ppermute | solution.py:499
  (31 other events, 279.3 us)

commit v5 on v3

--- a/solution.py
+++ b/solution.py
@@ -595,7 +595,7 @@
     return product(first, turn(waves, spec, -1.0), order)
 
 
-def send_kernel(inc_ref, field_ref, gauge_ref, out_ref):
+def send_kernel(inc_ref, field_ref, gauge_ref, kind_ref, out_ref):
     blocks, slots, width = inc_ref.shape
     rows = blocks * slots
     hours = field_ref.shape[1]
@@ -610,14 +610,18 @@
     col = lax.broadcasted_iota(jnp.int32, (rows, rows), 1)
     own = jnp.where(row // slots == col // slots, full, 0.0)
     out_ref[pl.ds(hours, slots), :] = jnp.sum(own.reshape(blocks, slots, rows), axis=0)
-    out_ref[pl.ds(hours + slots, 8), :] = jnp.broadcast_to(gauge_ref[...].astype(F32), (8, rows))
-
-
-def send(incidence, field, row_gauge):
+    out_ref[pl.ds(hours + slots, 8), :] = jnp.concatenate(
+        [gauge_ref[...].astype(F32), kind_ref[...].astype(F32), jnp.zeros((6, rows), F32)], axis=0
+    )
+
+
+def send(incidence, field, row_gauge, gauge_kernel):
     blocks, slots, width = incidence.shape
+    count = blocks * slots
     hours = field.shape[1]
     step = 8
     height = hours + slots + 8
+    kinds = jnp.pad(gauge_kernel, (0, count - gauge_kernel.shape[0]))
     return pl.pallas_call(
         send_kernel,
         grid=(blocks // step,),
@@ -625,12 +629,13 @@
             pl.BlockSpec((step, slots, width), lambda i: (i, 0, 0)),
             pl.BlockSpec((step * width, hours), lambda i: (i, 0)),
             pl.BlockSpec((1, step * slots), lambda i: (0, i)),
+            pl.BlockSpec((1, step * slots), lambda i: (0, i)),
         ],
         out_specs=pl.BlockSpec((height, step * slots), lambda i: (0, i)),
-        out_shape=jax.ShapeDtypeStruct((height, blocks * slots), F32),
+        out_shape=jax.ShapeDtypeStruct((height, count), F32),
         compiler_params=params(),
         name="send",
-    )(incidence, field, row_gauge.reshape(1, blocks * slots))
+    )(incidence, field, row_gauge.reshape(1, count), kinds.reshape(1, count))
 
 
 def hot_rows(gauge, first, rows):
@@ -640,8 +645,7 @@
 
 def spread_kernel(first_ref, mine_ref, other_ref, *out_refs):
     hours, rows = out_refs[0].shape
-    slots = mine_ref.shape[0] - hours - 8
-    where = hours + slots
+    where = mine_ref.shape[0] - 8
     for m, out_ref in enumerate(out_refs):
         result = None
         for ref in (mine_ref, other_ref):
@@ -654,30 +658,34 @@
         out_ref[...] = result
 
 
-def spread(first, mine, other, hours, rows):
+def spread(first, parcels, hours, rows):
     return pl.pallas_call(
         spread_kernel,
         in_specs=[pl.BlockSpec(memory_space=pltpu.SMEM)] + [pl.BlockSpec(memory_space=pltpu.VMEM)] * 2,
         out_shape=[jax.ShapeDtypeStruct((hours, rows), F32)] * 4,
         compiler_params=params(),
         name="spread",
-    )(first, mine, other)
-
-
-def plane_couple_kernel(first_ref, a_ref, b_ref, c_ref, d_ref, high_ref, low_ref, total_ref, meta_ref):
+    )(first, *parcels)
+
+
+def plane_couple_kernel(last, first_ref, *refs):
+    if last:
+        a_ref, b_ref, before_ref, high_ref, low_ref, total_ref, meta_ref = refs
+        total_ref[...] = before_ref[...]
+    else:
+        a_ref, b_ref, total_ref, meta_ref = refs
+        total_ref[...] = jnp.zeros_like(total_ref)
     height, double = a_ref.shape
     slots = height - 8
     count = double // 2
-    cols, rows = high_ref.shape
-    part = cols // 4
+    cols, rows = total_ref.shape
     tile = 256
-    for i, ref in enumerate((a_ref, b_ref, c_ref, d_ref)):
+    for i, ref in enumerate((a_ref, b_ref)):
         for j in range(2):
             meta_ref[2 * i + j] = ref[:, j * count : (j + 1) * count]
     row = lax.broadcasted_iota(jnp.int32, (tile, tile), 0)
     col = lax.broadcasted_iota(jnp.int32, (tile, tile), 1)
     same = row // slots == col // slots
-    total_ref[...] = jnp.zeros_like(total_ref)
 
     def body(i, carry):
         gauge = meta_ref[i, slots : slots + 1, :]
@@ -695,7 +703,7 @@
         near = jnp.concatenate(near, axis=0)
         high = near.astype(BF16)
         rest = near - high.astype(F32)
-        hot = jnp.concatenate([hot_rows(gauge, first_ref[m], part) for m in range(4)], axis=0)
+        hot = jnp.concatenate([hot_rows(gauge, first_ref[m], cols // 4) for m in range(4)], axis=0)
         total_ref[...] += dot(hot, high)
 
         @pl.when(jnp.max(jnp.abs(rest)) > 0.0)
@@ -704,83 +712,81 @@
 
         return carry
 
-    lax.fori_loop(0, 8, body, 0)
-    high, low = pieces(total_ref[...], 2)
-    high_ref[...] = high
-    low_ref[...] = low
-
-
-def plane_couple(first, metas, rows):
+    lax.fori_loop(0, 4, body, 0)
+    if last:
+        high, low = pieces(total_ref[...], 2)
+        high_ref[...] = high
+        low_ref[...] = low
+
+
+def plane_couple(first, metas, rows, before=None):
     height, double = metas[0].shape
-    return pl.pallas_call(
-        plane_couple_kernel,
-        in_specs=[pl.BlockSpec(memory_space=pltpu.SMEM)] + [pl.BlockSpec(memory_space=pltpu.VMEM)] * 4,
-        out_shape=[jax.ShapeDtypeStruct((4 * rows, 2 * rows), BF16)] * 2,
-        scratch_shapes=[
-            pltpu.VMEM((4 * rows, 2 * rows), F32),
-            pltpu.VMEM((8, height, double // 2), F32),
-        ],
+    shape = (4 * rows, 2 * rows)
+    last = before is not None
+    args = [first, *metas] + ([before] if last else [])
+    scratch = [pltpu.VMEM((4, height, double // 2), F32)]
+    return pl.pallas_call(
+        functools.partial(plane_couple_kernel, last),
+        in_specs=[pl.BlockSpec(memory_space=pltpu.SMEM)]
+        + [pl.BlockSpec(memory_space=pltpu.VMEM)] * (len(args) - 1),
+        out_shape=[jax.ShapeDtypeStruct(shape, BF16)] * 2 if last else jax.ShapeDtypeStruct(shape, F32),
+        scratch_shapes=([pltpu.VMEM(shape, F32)] if last else []) + scratch,
         compiler_params=params(),
         name="plane_couple",
-        cost_estimate=pl.CostEstimate(flops=14_000_000_000, bytes_accessed=4_000_000, transcendentals=0),
-    )(first, *metas)
-
-
-def plane_mix_kernel(high_ref, low_ref, a_ref, b_ref, c_ref, d_ref, mine_ref, other_ref):
+        cost_estimate=pl.CostEstimate(
+            flops=2 * 2 * double * 8 * rows * rows, bytes_accessed=2_000_000, transcendentals=0
+        ),
+    )(*args)
+
+
+def plane_mix_kernel(
+    first_ref, high_ref, low_ref, meta_ref, meta_other_ref, a_ref, b_ref, c_ref, d_ref, mine_ref, other_ref, rows_ref
+):
     refs = (a_ref, b_ref, c_ref, d_ref)
     height, rows = a_ref.shape
     hours = height - NOTE
-    value = jnp.concatenate([ref[pl.ds(0, hours), :] for ref in refs], axis=1)
+    body, tail = pl.ds(0, hours), pl.ds(hours, NOTE)
+    value = jnp.concatenate([ref[body, :] for ref in refs], axis=1)
     one, two = pieces(value, 2)
     high, low = high_ref[...], low_ref[...]
     result = (dot(two, high) + dot(one, low)) + dot(one, high)
-    note = sum(ref[pl.ds(hours, NOTE), :] for ref in refs)
-    mine_ref[pl.ds(0, hours), :] = result[:, :rows]
-    other_ref[pl.ds(0, hours), :] = result[:, rows:]
-    mine_ref[pl.ds(hours, NOTE), :] = note
-    other_ref[pl.ds(hours, NOTE), :] = note
-
-
-def plane_mix(high, low, values):
+    note = sum(ref[tail, :] for ref in refs)
+    mine_ref[body, :] = result[:, :rows]
+    other_ref[body, :] = result[:, rows:]
+    mine_ref[tail, :] = note
+    other_ref[tail, :] = note
+    where = meta_ref.shape[0] - 8
+    for ref in (meta_ref, meta_other_ref):
+        gauge = ref[where : where + 1, :]
+        hot = jnp.concatenate([hot_rows(gauge, first_ref[m], rows) for m in range(4)], axis=0)
+        picked = dot(two, hot) + dot(one, hot)
+        if ref is meta_ref:
+            rows_ref[...] = picked
+        else:
+            for i in range(gauge.shape[1] // rows):
+                other_ref[pl.ds(height + i * hours, hours), :] = picked[:, i * rows : (i + 1) * rows]
+
+
+def plane_mix(first, coupling, metas, values):
+    height, rows = values[0].shape
+    hours = height - NOTE
+    slots = metas[0].shape[1]
     return pl.pallas_call(
         plane_mix_kernel,
-        out_shape=[jax.ShapeDtypeStruct(values[0].shape, F32)] * 2,
+        in_specs=[pl.BlockSpec(memory_space=pltpu.SMEM)] + [pl.BlockSpec(memory_space=pltpu.VMEM)] * 8,
+        out_shape=[
+            jax.ShapeDtypeStruct((height, rows), F32),
+            jax.ShapeDtypeStruct((height + slots // rows * hours, rows), F32),
+            jax.ShapeDtypeStruct((hours, slots), F32),
+        ],
         compiler_params=params(),
         name="plane_mix",
-    )(high, low, *values)
-
-
-def plane_rows_kernel(first_ref, mine_ref, other_ref, a_ref, b_ref, c_ref, d_ref, out_mine_ref, out_other_ref):
-    height, rows = a_ref.shape
-    hours = height - NOTE
-    where = mine_ref.shape[0] - 8
-    for ref, out_ref in ((mine_ref, out_mine_ref), (other_ref, out_other_ref)):
-        gauge = ref[where : where + 1, :]
-        result = None
-        for m, value_ref in enumerate((a_ref, b_ref, c_ref, d_ref)):
-            hot = hot_rows(gauge, first_ref[m], rows)
-            for piece in reversed(pieces(value_ref[pl.ds(0, hours), :], 2)):
-                term = dot(piece, hot)
-                result = term if result is None else result + term
-        out_ref[...] = result
-
-
-def plane_rows(first, mine, other, values):
-    hours = values[0].shape[0] - NOTE
-    slots = mine.shape[1]
-    return pl.pallas_call(
-        plane_rows_kernel,
-        in_specs=[pl.BlockSpec(memory_space=pltpu.SMEM)] + [pl.BlockSpec(memory_space=pltpu.VMEM)] * 6,
-        out_shape=[jax.ShapeDtypeStruct((hours, slots), F32)] * 2,
-        compiler_params=params(),
-        name="plane_rows",
-        cost_estimate=pl.CostEstimate(flops=1_000_000_000, bytes_accessed=2_000_000, transcendentals=0),
-    )(first, mine, other, *values)
+    )(first, *coupling, *metas, *values)
 
 
 def plane_spectrum_kernel(class_ref, kernels_ref, f0_ref, f1_ref, f2_ref, out_ref):
     classes, taps = kernels_ref.shape
-    kind = jnp.concatenate([class_ref[0:1, :], class_ref[1:2, :]], axis=1)
+    kind = class_ref[class_ref.shape[0] - 7 : class_ref.shape[0] - 6, : out_ref.shape[1]]
     hot = jnp.where(
         lax.broadcasted_iota(jnp.int32, (classes, kind.shape[1]), 0).astype(F32) == kind, 1.0, 0.0
     ).astype(BF16)
@@ -792,122 +798,223 @@
     out_ref[...] = product(mats, chosen, 3)
 
 
-def plane_spectrum(kinds, kernels, forward):
+def plane_spectrum(meta, kernels, forward, rows):
     return pl.pallas_call(
         plane_spectrum_kernel,
-        out_shape=jax.ShapeDtypeStruct((SPAN, 2 * kinds.shape[1]), F32),
+        out_shape=jax.ShapeDtypeStruct((SPAN, rows), F32),
         compiler_params=params(),
         name="plane_spectrum",
-    )(kinds, kernels, *forward)
+    )(meta, kernels, *forward)
 
 
 def sides(even, pair, middle):
     return jnp.where(even, middle, pair), jnp.where(even, pair, middle)
 
 
-def plane_first_kernel(
-    flag_ref, here_ref, pair_ref, middle_ref, seen_ref, seen_later_ref, spec_ref, *refs
-):
+def plane_first_kernel(flag_ref, here_ref, pair_ref, middle_ref, spec_ref, *refs):
     *mats, out_ref = refs
     forward, first, last = mats[0:3], mats[3:6], mats[6:9]
-    hours, rows = here_ref.shape
+    rows = here_ref.shape[1]
+    hours = here_ref.shape[0] // 2
     spec = spec_ref[...]
     before, after = sides(flag_ref[0] > 0.5, pair_ref[...], middle_ref[...])
-    now, later = plane_delayed(before, here_ref[...], after, spec, forward, last, 3)
-    start = jnp.transpose(seen_ref[pl.ds(0, rows), :]) - now
-    start_later = (jnp.transpose(seen_later_ref[...]) - later) * flag_ref[1]
+    now, later = plane_delayed(
+        before[:hours], here_ref[pl.ds(0, hours), :], after[:hours], spec, forward, last, 3
+    )
+    start = here_ref[pl.ds(hours, hours), :] - now
+    start_later = (after[hours:] - later) * flag_ref[1]
     out_ref[pl.ds(0, hours), :] = plane_advanced(start, start_later, spec, forward, first, 3)
     out_ref[pl.ds(hours, NOTE), :] = jnp.concatenate(
         [lanes(start, start), jnp.zeros((NOTE - 1, rows), F32)], axis=0
     )
 
 
-def plane_first(flags, sums, seen, seen_later, spec, mats):
-    hours, rows = sums[0].shape
-    args = [flags, *sums, seen, seen_later, spec, *mats]
+def plane_first(flags, sums, spec, mats):
+    double, rows = sums[0].shape
+    args = [flags, *sums, spec, *mats]
     return pl.pallas_call(
         plane_first_kernel,
         in_specs=[pl.BlockSpec(memory_space=pltpu.SMEM)]
         + [pl.BlockSpec(memory_space=pltpu.VMEM)] * (len(args) - 1),
-        out_shape=jax.ShapeDtypeStruct((hours + NOTE, rows), F32),
+        out_shape=jax.ShapeDtypeStruct((double // 2 + NOTE, rows), F32),
         compiler_params=params(),
         name="plane_first",
     )(*args)
 
 
-def plane_step_kernel(opening, final, flag_ref, here_ref, pair_ref, middle_ref, two_ref, mirror_ref, pulled_ref, spec_ref, *refs):
-    mats, refs = refs[:9], refs[9:]
+def plane_open_kernel(flag_ref, here_ref, pair_ref, middle_ref, pulled_ref, spec_ref, *refs):
+    mats, (out_ref, now_ref) = refs[:9], refs[9:]
     forward, first, last = mats[0:3], mats[3:6], mats[6:9]
-    if not opening:
-        state_ref, *refs = refs
-    if final:
-        total_ref, out_ref = refs
-    else:
-        total_ref, out_ref, new_ref = refs
+    height, rows = pulled_ref.shape
+    hours = height - NOTE
+    tail, body = pl.ds(hours, NOTE), pl.ds(0, hours)
+    spec = spec_ref[...]
+    here = here_ref[body, :]
+    before, after = sides(flag_ref[0] > 0.5, pair_ref[body, :], middle_ref[body, :])
+    now, later = plane_delayed(before, here, after, spec, forward, last, 2)
+    out_ref[body, :] = plane_advanced(now, later * flag_ref[1], spec, forward, first, 2)
+    out_ref[tail, :] = jnp.concatenate(
+        [
+            lanes(pulled_ref[body, :], here),
+            lanes(now, now),
+            pulled_ref[hours : hours + 1, :],
+            jnp.zeros((NOTE - 3, rows), F32),
+        ],
+        axis=0,
+    )
+    now_ref[...] = now
+
+
+def plane_open(flags, sums, pulled, spec, mats):
+    height, rows = pulled.shape
+    args = [flags, *sums, pulled, spec, *mats]
+    return pl.pallas_call(
+        plane_open_kernel,
+        in_specs=[pl.BlockSpec(memory_space=pltpu.SMEM)]
+        + [pl.BlockSpec(memory_space=pltpu.VMEM)] * (len(args) - 1),
+        out_shape=[
+            jax.ShapeDtypeStruct((height, rows), F32),
+            jax.ShapeDtypeStruct((height - NOTE, rows), F32),
+        ],
+        compiler_params=params(),
+        name="plane_open",
+    )(*args)
+
+
+def opening(ref):
+    start = total(ref, 2)
+    square = total(ref, 0) / start
+    alpha = jnp.sqrt(square)
+    beta = jnp.sqrt(jnp.maximum(total(ref, 1) / total(ref, 0) - square, 0.0))
+    return 1.0 / jnp.sqrt(start), alpha, beta
+
+
+def plane_step_kernel(flag_ref, here_ref, pair_ref, middle_ref, two_ref, mirror_ref, *refs):
+    old_refs, (pulled_ref, old_z_ref, old_now_ref, spec_ref), refs = refs[:3], refs[3:7], refs[7:]
+    mats, (total_ref, out_ref, kept_ref) = refs[:9], refs[9:]
+    forward, first, last = mats[0:3], mats[3:6], mats[6:9]
     height, rows = pulled_ref.shape
     hours = height - NOTE
     tail, body = pl.ds(hours, NOTE), pl.ds(0, hours)
     total_ref[...] = (here_ref[tail, :] + pair_ref[tail, :]) + (two_ref[...] + mirror_ref[...])
+    scale, alpha, beta = opening(total_ref)
+    a, b, g = scale / (alpha * beta), scale * alpha / beta, scale * beta / alpha
     spec = spec_ref[...]
-    pulled = pulled_ref[body, :]
-    sums = [ref[body, :] for ref in (here_ref, pair_ref, middle_ref)]
-    if opening:
-        scale = 1.0 / jnp.sqrt(total(total_ref, 0))
-        new_su = [value * scale for value in sums]
-        new_s = new_su
-        new_zu = pulled * scale
-        new_z = new_zu
-    else:
-        alpha, beta = ratios(total_ref)
-        a, b, g = 1.0 / (alpha * beta), alpha / beta, beta / alpha
-        old = lambda i: state_ref[pl.ds(i * hours, hours), :]
-        new_su = [value * a - old(3 + i) * b for i, value in enumerate(sums)]
-        new_s = [value - old(i) * g for i, value in enumerate(new_su)]
-        new_zu = pulled * a - old(7) * b
-        new_z = new_zu - old(6) * g
-    here = new_s[0]
-    before, after = sides(flag_ref[0] > 0.5, new_s[1], new_s[2])
-    now, later = plane_delayed(before, here, after, spec, forward, last, 2)
-    note = jnp.concatenate(
-        [lanes(new_z, here), lanes(now, now), lanes(new_zu, here), jnp.zeros((NOTE - 3, rows), F32)],
-        axis=0,
+    s, su = [], []
+    for ref, old_ref in zip((here_ref, pair_ref, middle_ref), old_refs):
+        old = old_ref[body, :]
+        su.append(ref[body, :] * a - old * b)
+        s.append(su[-1] - old * g)
+    zu = pulled_ref[body, :] * a - old_z_ref[body, :] * b
+    z = zu - old_z_ref[body, :] * g
+    before, after = sides(flag_ref[0] > 0.5, s[1], s[2])
+    now, later = plane_delayed(before, s[0], after, spec, forward, last, 2)
+    out_ref[body, :] = plane_advanced(now, later * flag_ref[1], spec, forward, first, 2)
+    out_ref[tail, :] = jnp.concatenate(
+        [lanes(z, s[0]), lanes(now, now), lanes(zu, s[0]), jnp.zeros((NOTE - 3, rows), F32)], axis=0
     )
-    if final:
-        out_ref[...] = note[:, : rows // 2] + note[:, rows // 2 :]
-    else:
-        for i, value in enumerate(new_s + new_su + [new_z, new_zu]):
-            new_ref[pl.ds(i * hours, hours), :] = value
-        out_ref[body, :] = plane_advanced(now, later * flag_ref[1], spec, forward, first, 2)
-        out_ref[tail, :] = note
-
-
-def plane_step(flags, sums, two, mirror, pulled, spec, mats, state, final):
+    for i, value in enumerate((s[0], su[0], z, zu, now, now + old_now_ref[...] * g)):
+        kept_ref[pl.ds(i * hours, hours), :] = value
+
+
+def plane_step(flags, sums, two, mirror, old, pulled, old_z, old_now, spec, mats):
     height, rows = pulled.shape
-    hours = height - NOTE
-    opening = state is None
-    args = [flags, *sums, two, mirror, pulled, spec, *mats] + ([] if opening else [state])
-    out = [jax.ShapeDtypeStruct((NOTE, rows), F32)]
-    if final:
-        out += [jax.ShapeDtypeStruct((NOTE, rows // 2), F32)]
-    else:
-        out += [jax.ShapeDtypeStruct((height, rows), F32), jax.ShapeDtypeStruct((8 * hours, rows), F32)]
-    return pl.pallas_call(
-        functools.partial(plane_step_kernel, opening, final),
+    args = [flags, *sums, two, mirror, *old, pulled, old_z, old_now, spec, *mats]
+    return pl.pallas_call(
+        plane_step_kernel,
         in_specs=[pl.BlockSpec(memory_space=pltpu.SMEM)]
         + [pl.BlockSpec(memory_space=pltpu.VMEM)] * (len(args) - 1),
-        out_shape=out,
+        out_shape=[
+            jax.ShapeDtypeStruct((NOTE, rows), F32),
+            jax.ShapeDtypeStruct((height, rows), F32),
+            jax.ShapeDtypeStruct((6 * (height - NOTE), rows), F32),
+        ],
         compiler_params=params(),
         name="plane_step",
     )(*args)
 
 
-def plane_finish_kernel(n0, n1, n2, n3, q0, q1, q2, inc_ref, field_ref, out_ref, rows_ref):
+def plane_close_kernel(flag_ref, here_ref, pair_ref, middle_ref, pulled_ref, kept_ref, spec_ref, *refs):
+    mats, (out_ref,) = refs[:9], refs[9:]
+    forward, last = mats[0:3], mats[6:9]
+    height, rows = pulled_ref.shape
+    hours = height - NOTE
+    body = pl.ds(0, hours)
+    before, after = sides(flag_ref[0] > 0.5, pair_ref[body, :], middle_ref[body, :])
+    here = here_ref[body, :]
+    waves = product(forward, jnp.concatenate([before, here], axis=0), 2)
+    now = product(last, turn(waves, spec_ref[...], 1.0), 2)
+    s, su, z, zu, old_now, old_now_u = (kept_ref[pl.ds(i * hours, hours), :] for i in range(6))
+    raw = pulled_ref[body, :]
+    note = [pulled_ref[hours + i : hours + i + 1, :] for i in range(3)]
+    for left in (raw, zu, z):
+        note += [lanes(left, right) for right in (here, su, s)]
+    parts = (now, old_now_u, old_now)
+    for i in range(3):
+        note += [lanes(parts[i], parts[j]) for j in range(i, 3)]
+    note.append(jnp.zeros((24 - len(note), rows), F32))
+    note = jnp.concatenate(note, axis=0)
+    out_ref[...] = note[:, : rows // 2] + note[:, rows // 2 :]
+
+
+def plane_close(flags, sums, pulled, kept, spec, mats):
+    rows = pulled.shape[1]
+    args = [flags, *sums, pulled, kept, spec, *mats]
+    return pl.pallas_call(
+        plane_close_kernel,
+        in_specs=[pl.BlockSpec(memory_space=pltpu.SMEM)]
+        + [pl.BlockSpec(memory_space=pltpu.VMEM)] * (len(args) - 1),
+        out_shape=jax.ShapeDtypeStruct((24, rows // 2), F32),
+        compiler_params=params(),
+        name="plane_close",
+    )(*args)
+
+
+def plane_weights(open_ref, close_ref):
+    scale, alpha, beta = opening(open_ref)
+    start = 1.0 / scale
+    phibar, rhobar = start, alpha
+    zero = jnp.zeros_like(start)
+    z = zu = [scale, zero, zero]
+    w = [value / alpha for value in z]
+    result = [zero] * 3
+    for k in range(3):
+        rho = jnp.sqrt(rhobar * rhobar + beta * beta)
+        cosine, sine = rhobar / rho, beta / rho
+        phi, phibar = cosine * phibar, sine * phibar
+        result = [r + phi / rho * value for r, value in zip(result, w)]
+        if k == 2:
+            return result
+        a, b, g = 1.0 / (alpha * beta), alpha / beta, beta / alpha
+        zu = [-b * value for value in zu]
+        zu[k + 1] = zu[k + 1] + (a * scale if k == 0 else a)
+        z = [value - g * old for value, old in zip(zu, z)]
+        if k == 0:
+            square, norm, along = (total(close_ref, i) for i in range(3))
+        else:
+            plain = (a, -b, -g)
+            cross = [[total(close_ref, 3 + 3 * i + j) for j in range(3)] for i in range(3)]
+            along = sum(plain[i] * plain[j] * cross[i][j] for i in range(2) for j in range(3))
+            square = along + sum(plain[2] * plain[j] * cross[2][j] for j in range(3))
+            pairs = [(i, j) for i in range(3) for j in range(i, 3)]
+            norm = sum(
+                plain[i] * plain[j] * total(close_ref, 12 + n) * (1.0 if i == j else 2.0)
+                for n, (i, j) in enumerate(pairs)
+            )
+        alpha = jnp.sqrt(square)
+        beta = jnp.sqrt(jnp.maximum(norm / square - 2.0 * along + square, 0.0))
+        theta = sine * alpha
+        rhobar = -cosine * alpha
+        w = [value / alpha - theta / rho * old for value, old in zip(z, w)]
+
+
+def plane_finish_kernel(open_ref, close_ref, q0, q1, q2, inc_ref, field_ref, out_ref, rows_ref):
     blocks, slots, width = inc_ref.shape
     step = pl.program_id(0)
 
     @pl.when(step == 0)
     def _():
-        e0, e1, e2 = weights_of([n0, n1, n2, n3])
+        e0, e1, e2 = plane_weights(open_ref, close_ref)
         rows_ref[...] = jnp.transpose(q0[...] * e0 + q1[...] * e1 + q2[...] * e2)
 
     weights = inc_ref[...].astype(F32).astype(BF16)
@@ -945,7 +1052,6 @@
 
 def plane_shards(incidence, row_gauge, gauge_kernel, kernels, observed, first_guess):
     rows, hours = observed.shape
-    slots = incidence.shape[1]
     basin, tm = lax.axis_index("basin"), lax.axis_index("tm")
     z, x, y, c = basin // X_, basin % X_, tm // C_, tm % C_
     place = 2 * y + x
@@ -955,40 +1061,57 @@
     forward, inverse_first, inverse_last = turned_transforms()
     mats = [*forward, *inverse_first, *inverse_last]
 
-    kinds = gauge_kernel.astype(F32).reshape(rows // hours, hours)
-    parcel = moved(send(incidence, first_guess, row_gauge), to_plane)
-    seen, kinds, parcel = lax.optimization_barrier((observed, kinds, parcel))
-    seen_later = moved(seen, to_plane_before)
-    seen = moved(jnp.concatenate([seen, kinds, jnp.zeros((8 - kinds.shape[0], hours), F32)]), to_plane)
-    spec = plane_spectrum(seen[rows : rows + kinds.shape[0]], kernels, forward)
-
-    beside = moved(parcel, over_core)
-    meta = jnp.concatenate([parcel[hours:], beside[hours:]], axis=1)
-    metas = [meta] + [moved(meta, where) for where in SQUARE]
-    dense = spread(first, parcel, beside, hours, rows)
+    parcel = moved(send(incidence, first_guess, row_gauge, gauge_kernel), to_plane)
+    seen, parcel = lax.optimization_barrier((jnp.transpose(observed), parcel))
+    parcels = [parcel, moved(parcel, over_core)]
+    seen = moved(seen, to_plane)
+    metas = [value[hours:] for value in parcels]
+    both = jnp.concatenate(metas, axis=1)
+    around = [both] + [moved(both, where) for where in SQUARE]
+    spec = plane_spectrum(metas[0], kernels, forward, rows)
+
+    dense = spread(first, parcels, hours, rows)
     sums = dense[0] + sum(moved(value, where) for value, where in zip(dense[1:], SQUARE))
+    sums = jnp.concatenate([sums, seen], axis=0)
     sums = [sums, moved(sums, z_pair), moved(sums, z_middle)]
-    high, low = plane_couple(first, metas, rows)
-    pulled = plane_first(flags, sums, seen, seen_later, spec, mats)
-    notes, kept, state = [], [], None
+    coupled = plane_couple(first, around[:2], rows)
+    coupled, sums = lax.optimization_barrier((coupled, sums))
+    coupling = plane_couple(first, around[2:], rows, coupled)
+    pulled = [plane_first(flags, sums, spec, mats)]
+    kept, shipped, mixes = [], [], []
     for k in range(3):
-        values = [pulled] + [moved(pulled, where) for where in SQUARE]
-        mine, other = plane_mix(high, low, values)
-        mixed = mine + moved(other, over_core)
-        note = mixed[hours:]
+        if k:
+            pulled[k], kept[k - 1] = lax.optimization_barrier((pulled[k], kept[k - 1]))
+            shipped.append(moved(kept[k - 1], from_plane))
+        values = [pulled[k]] + [moved(pulled[k], where) for where in SQUARE]
+        mine, other, slot_rows = plane_mix(first, coupling, metas, values)
+        beside = moved(other, over_core)
+        mixed = mine + beside[: hours + NOTE]
+        kept.append(
+            slot_rows
+            + jnp.concatenate(
+                [beside[hours + NOTE + i * hours :][:hours] for i in range(slot_rows.shape[1] // rows)], axis=1
+            )
+        )
         sums = [mixed, moved(mixed, z_pair), moved(mixed, z_middle)]
-        two, mirror = moved(note, z_two), moved(note, z_mirror)
-        rows_mine, rows_other = plane_rows(first, parcel, beside, values)
-        kept.append(moved(rows_mine + moved(rows_other, over_core), from_plane))
-        result = plane_step(flags, sums, two, mirror, pulled, spec, mats, state, k == 2)
-        if k == 2:
-            total_note, last = result
+        mixes.append(sums)
+        if k == 0:
+            following, now = plane_open(flags, sums, pulled[0], spec, mats)
+        elif k == 1:
+            note = mixed[hours:]
+            two, mirror = moved(note, z_two), moved(note, z_mirror)
+            open_note, following, state = plane_step(
+                flags, sums, two, mirror, mixes[0], pulled[1], pulled[0], now, spec, mats
+            )
+            following, shipped[0] = lax.optimization_barrier((following, shipped[0]))
         else:
-            total_note, pulled, state = result
-        notes.append(total_note)
-    copies = jnp.broadcast_to(last[None], (Z_ * X_ * Y_ * C_,) + last.shape)
-    notes.append(jnp.sum(lax.all_to_all(copies, ("basin", "tm"), 0, 0, tiled=False), axis=0))
-    return plane_finish(notes, kept, incidence, first_guess)
+            shipped.append(moved(kept[2], from_plane))
+            note = plane_close(flags, sums, pulled[2], state, spec, mats)
+        pulled.append(following)
+    note, shipped[1] = lax.optimization_barrier((note, shipped[1]))
+    copies = jnp.broadcast_to(note[None], (Z_ * X_ * Y_ * C_,) + note.shape)
+    close_note = jnp.sum(lax.all_to_all(copies, ("basin", "tm"), 0, 0, tiled=False), axis=0)
+    return plane_finish([open_note, close_note], shipped, incidence, first_guess)
 
 
 def solution(mesh):

time: 157 us -> 165 us (1.051)
  waiting for transfers between devices: 32.5 us -> 62.5 us
  blocking collectives: 20.1 us -> 0 us
  local copies, waits for them, and re-layouts: 3.49 us -> 5.99 us
  starting transfers between devices: 64.5 us -> 62.3 us
    ppermute x42 -> x34, waiting for transfers between devices: 32.5 us -> 54.2 us  [moved(): return lax.ppermute(value, ('basin', 'tm'), pairs)]
    all_to_all x1 -> x0, blocking collectives: 20.1 us -> none  [plane_shards(): lax.all_to_all(copies, ('basin', 'tm'), 0, 0, tiled=False)]
    ppermute x42 -> x34, starting transfers between devices: 64.5 us -> 56 us  [moved(): return lax.ppermute(value, ('basin', 'tm'), pairs)]
    all_to_all x0 -> x1, waiting for transfers between devices: none -> 8.28 us  [plane_shards(): lax.all_to_all(copies, ('basin', 'tm'), 0, 0, tiled=False)]
    all_to_all x0 -> x1, starting transfers between devices: none -> 6.23 us  [plane_shards(): lax.all_to_all(copies, ('basin', 'tm'), 0, 0, tiled=False)]
    unnamed x34 -> x35, local copies, waits for them, and re-layouts: 3.31 us -> 3.39 us
    pallas_call x10 -> x8, Pallas kernels: 20.5 us -> 20.5 us  [the longest x2 9.56 us: plane_couple(): pl.pallas_call(functools.partial(plane_couple_kernel, last), in_specs=[pl...]
  transfers between devices with their start and end apart: 42 -> 35, of which waited for: 12 -> 18; matrix products, arithmetic and copies ran while one was open for 2% -> 2% of each run, Pallas kernels for 14% -> 10%
where the time goes in v5:
time: 165 us
  waiting for transfers between devices  62.5 us (38%)
  starting transfers between devices  62.3 us (38%)
  Pallas kernels  31.5 us (19%)
  local copies, waits for them, and re-layouts  5.99 us (4%)
  other arithmetic  2.05 us (1%)
    ppermute x34, starting transfers between devices, moved(): return lax.ppermute(value, ('basin', 'tm'), pairs)  56 us
    ppermute x34, waiting for transfers between devices, moved(): return lax.ppermute(value, ('basin', 'tm'), pairs)  54.2 us
    pallas_call x2, Pallas kernels, plane_couple(): pl.pallas_call(functools.partial(plane_couple_kernel, last), in_specs=[pl...  9.56 us
    all_to_all x1, waiting for transfers between devices, plane_shards(): lax.all_to_all(copies, ('basin', 'tm'), 0, 0, tiled=False)  8.28 us
    all_to_all x1, starting transfers between devices, plane_shards(): lax.all_to_all(copies, ('basin', 'tm'), 0, 0, tiled=False)  6.23 us
    pallas_call x3, Pallas kernels, plane_mix(): pl.pallas_call(plane_mix_kernel, in_specs=[pl.BlockSpec(memory_space=pltp...  5.3 us
    unnamed x35, local copies, waits for them, and re-layouts  3.39 us
  transfers between devices with their start and end apart: 35, of which 18 were waited for; matrix products, arithmetic and copies ran while one was open for 2% of the time, Pallas kernels for 10%

profile of v5, /device:TPU:1, one launch (start us, length us, event | category | flops | bytes accessed | tf_op | source)
XLA Modules:
  0.0 164.8 jit_solution(7834546994343064249)
XLA Ops:
  5.7 4.6 %collective-permute-start = (f32[152,512]{1,0:T(8,128)S(1)}, f32[152,512]{1,0:T(8,128)S(1)}, u32[]{:S(2)}, u32[]{:S(2)}) collective-permute-start(f32[152,512]{1,0:T(8,128)S(1)} %send.1), channel_id=1, source_target_pairs={{0,0},{1,8},{2,16},{3,24},{4,4},{5,12},{6,20},{7,28},{8,2},{9,10},... | collective-permute-start | bytes 933896 | tf_op jit(solution)/shard_map/ppermute | solution.py:499
  10.4 14.8 %collective-permute-done.mine_ref = f32[152,512]{1,0:T(8,128)S(1)} collective-permute-done((f32[152,512]{1,0:T(8,128)S(1)}, f32[152,512]{1,0:T(8,128)S(1)}, u32[]{:S(2)}, u32[]{:S(2)}) %collective-permute-start) | collective-permute-done | bytes 311328 | tf_op jit(solution)/shard_map/ppermute | solution.py:499
  26.8 2.7 %spread.1 = (f32[128,256]{1,0:T(8,128)S(1)}, f32[128,256]{1,0:T(8,128)S(1)}, f32[128,256]{1,0:T(8,128)S(1)}, f32[128,256]{1,0:T(8,128)S(1)}) custom-call(s32[6]{0:T(128)S(1)} %broadcast_multiply_fusion.first_ref, f32[152,512]{1,0:T(8,128)S(1)} %collective-permute-done.mine_ref, f32[152,512]{1,0:T(8,128)S(1)} %collective-permute-done.1.other_ref), custom_call_target="tpu_custom_call" | custom-call | tf_op jit(solution)/shard_map/spread/pallas_call | solution.py:662
  32.2 3.1 %collective-permute-start.8 = (f32[128,256]{1,0:T(8,128)S(1)}, f32[128,256]{1,0:T(8,128)S(1)}, u32[]{:S(2)}, u32[]{:S(2)}) collective-permute-start(f32[128,256]{1,0:T(8,128)S(1)} %bitcast.12), channel_id=1, source_target_pairs={{0,0},{1,8},{2,16},{3,24},{4,4},{5,12},{6,20},{7,28},{8,2},{9,10},... | collective-permute-start | bytes 393224 | tf_op jit(solution)/shard_map/ppermute | solution.py:499
  38.3 4.6 %collective-permute-done.8 = f32[128,256]{1,0:T(8,128)S(1)} collective-permute-done((f32[128,256]{1,0:T(8,128)S(1)}, f32[128,256]{1,0:T(8,128)S(1)}, u32[]{:S(2)}, u32[]{:S(2)}) %collective-permute-start.8) | collective-permute-done | bytes 131104 | tf_op jit(solution)/shard_map/ppermute | solution.py:499
  43.6 2.4 %collective-permute-start.9 = (f32[256,256]{1,0:T(8,128)S(1)}, f32[256,256]{1,0:T(8,128)S(1)}, u32[]{:S(2)}, u32[]{:S(2)}) collective-permute-start(f32[256,256]{1,0:T(8,128)S(1)} %pad_maximum_fusion.here_ref), channel_id=1, source_target_pairs={{0,8},{1,9},{2,10},{3,11},{4,12},{5,13},{6,14},{7,15},{8,0},{9,1},... | collective-permute-start | bytes 786440 | tf_op jit(solution)/shard_map/ppermute | solution.py:499
  46.8 1.9 %collective-permute-start.2 = (f32[24,1024]{1,0:T(8,128)S(1)}, f32[24,1024]{1,0:T(8,128)S(1)}, u32[]{:S(2)}, u32[]{:S(2)}) collective-permute-start(f32[24,1024]{1,0:T(8,128)S(1)} %pad_maximum_fusion.1.refs_0_), channel_id=1, source_target_pairs={{0,2},{1,3},{2,0},{3,1},{4,6},{5,7},{6,4},{7,5},{8,10},{9,11},{10,... | collective-permute-start | bytes 294920 | tf_op jit(solution)/shard_map/ppermute | solution.py:499
  49.7 4.6 %plane_couple.2.refs_2_ = f32[1024,512]{1,0:T(8,128)S(1)} custom-call(s32[6]{0:T(128)S(1)} %broadcast_multiply_fusion.first_ref, f32[24,1024]{1,0:T(8,128)S(1)} %pad_maximum_fusion.1.refs_0_, f32[24,1024]{1,0:T(8,128)S(1)} %collective-permute-done.4.refs_1_), custom_call_target="tpu_custom_call" | custom-call | flops 2147483648 | bytes 2000000 | tf_op jit(solution)/shard_map/plane_couple/pallas_call | solution.py:728
  54.5 3.0 %plane_first.1.a_ref.pulled_ref.refs_4_ = f32[136,256]{1,0:T(8,128)S(1)} custom-call(f32[2]{0:T(128)S(1)} %add_convert_fusion.flag_ref, f32[256,256]{1,0:T(8,128)S(1)} %pad_maximum_fusion.here_ref, f32[256,256]{1,0:T(8,128)S(1)} %collective-permute-done.9.pair_ref, f32[256,256]{1,0:T(8,128)S(1)} %collective-permute-done.10.middle_ref, ...), custom_call_target="tpu_custom_call" | custom-call | tf_op jit(solution)/shard_map/plane_first/pallas_call | solution.py:835
  60.2 4.9 %plane_couple.3 = (bf16[1024,512]{1,0:T(8,128)(2,1)S(1)}, bf16[1024,512]{1,0:T(8,128)(2,1)S(1)}) custom-call(s32[6]{0:T(128)S(1)} %broadcast_multiply_fusion.first_ref, f32[24,1024]{1,0:T(8,128)S(1)} %collective-permute-done.2.refs_0_, f32[24,1024]{1,0:T(8,128)S(1)} %collective-permute-done.3.refs_1_, f32[1024,512]{1,0:T(8,128)S(1)} %plane_couple.2.refs_2_), custom_call_target="tpu_custom_call" | custom-call | flops 2147483648 | bytes 2000000 | tf_op jit(solution)/shard_map/plane_couple/pallas_call | solution.py:728
  65.2 1.8 %plane_mix.3 = (f32[136,256]{1,0:T(8,128)S(1)}, f32[392,256]{1,0:T(8,128)S(1)}, f32[128,512]{1,0:T(8,128)S(1)}) custom-call(s32[6]{0:T(128)S(1)} %broadcast_multiply_fusion.first_ref, bf16[1024,512]{1,0:T(8,128)(2,1)S(1)} %get-tuple-element.46.high_ref, bf16[1024,512]{1,0:T(8,128)(2,1)S(1)} %get-tuple-element.47.low_ref, ...), custom_call_target="tpu_custom_call" | custom-call | tf_op jit(solution)/shard_map/plane_mix/pallas_call | solution.py:774
  66.9 3.9 %collective-permute-start.14 = (f32[392,256]{1,0:T(8,128)S(1)}, f32[392,256]{1,0:T(8,128)S(1)}, u32[]{:S(2)}, u32[]{:S(2)}) collective-permute-start(f32[392,256]{1,0:T(8,128)S(1)} %get-tuple-element.52), channel_id=1, source_target_pairs={{0,1},{1,0},{2,3},{3,2},{4,5},{5,4},{6,7},{7,6},{8,9},{9,8},{10,11... | collective-permute-start | bytes 1204232 | tf_op jit(solution)/shard_map/ppermute | solution.py:499
  73.1 4.1 %collective-permute-done.15.pair_ref.refs_1_ = f32[136,256]{1,0:T(8,128)S(1)} collective-permute-done((f32[136,256]{1,0:T(8,128)S(1)}, f32[136,256]{1,0:T(8,128)S(1)}, u32[]{:S(2)}, u32[]{:S(2)}) %collective-permute-start.15) | collective-permute-done | bytes 139296 | tf_op jit(solution)/shard_map/ppermute | solution.py:499
  77.2 2.1 %plane_open.1 = (f32[136,256]{1,0:T(8,128)S(1)}, f32[128,256]{1,0:T(8,128)S(1)}) custom-call(f32[2]{0:T(128)S(1)} %add_convert_fusion.flag_ref, f32[136,256]{1,0:T(8,128)S(1)} %slice_add_fusion.2.here_ref.refs_0_, f32[136,256]{1,0:T(8,128)S(1)} %collective-permute-done.15.pair_ref.refs_1_, f32[136,256]{1,0:T(8,128)S(1)} %collective-permute-done.16.middle_ref.refs_2_, ...), custom_call_target="tpu_custom_call" | custom-call | tf_op jit(solution)/shard_map/plane_open/pallas_call | solution.py:871
  84.8 2.6 %collective-permute-done.19.d_ref = f32[136,256]{1,0:T(8,128)S(1)} collective-permute-done((f32[136,256]{1,0:T(8,128)S(1)}, f32[136,256]{1,0:T(8,128)S(1)}, u32[]{:S(2)}, u32[]{:S(2)}) %collective-permute-start.19) | collective-permute-done | bytes 139296 | tf_op jit(solution)/shard_map/ppermute | solution.py:499
  87.5 1.8 %plane_mix.4 = (f32[136,256]{1,0:T(8,128)S(1)}, f32[392,256]{1,0:T(8,128)S(1)}, f32[128,512]{1,0:T(8,128)S(1)}) custom-call(s32[6]{0:T(128)S(1)} %broadcast_multiply_fusion.first_ref, bf16[1024,512]{1,0:T(8,128)(2,1)S(1)} %get-tuple-element.46.high_ref, bf16[1024,512]{1,0:T(8,128)(2,1)S(1)} %get-tuple-element.47.low_ref, ...), custom_call_target="tpu_custom_call" | custom-call | tf_op jit(solution)/shard_map/plane_mix/pallas_call | solution.py:774
  89.3 2.5 %collective-permute-start.20 = (f32[392,256]{1,0:T(8,128)S(1)}, f32[392,256]{1,0:T(8,128)S(1)}, u32[]{:S(2)}, u32[]{:S(2)}) collective-permute-start(f32[392,256]{1,0:T(8,128)S(1)} %get-tuple-element.57), channel_id=1, source_target_pairs={{0,1},{1,0},{2,3},{3,2},{4,5},{5,4},{6,7},{7,6},{8,9},{9,8},{10,11... | collective-permute-start | bytes 1204232 | tf_op jit(solution)/shard_map/ppermute | solution.py:499
  91.8 5.0 %collective-permute-start.25 = (f32[128,512]{1,0:T(8,128)S(1)}, f32[128,512]{1,0:T(8,128)S(1)}, u32[]{:S(2)}, u32[]{:S(2)}) collective-permute-start(f32[128,512]{1,0:T(8,128)S(1)} %maximum_add_fusion), channel_id=1, source_target_pairs={{0,0},{1,16},{2,8},{3,24},{4,4},{5,20},{6,12},{7,28},{8,1},{9,17},... | collective-permute-start | bytes 786440 | tf_op jit(solution)/shard_map/ppermute | solution.py:499
  98.0 3.6 %collective-permute-start.23 = (f32[8,256]{1,0:T(8,128)S(1)}, f32[8,256]{1,0:T(8,128)S(1)}, u32[]{:S(2)}, u32[]{:S(2)}) collective-permute-start(f32[8,256]{1,0:T(8,128)S(1)} %slice.59), channel_id=1, source_target_pairs={{0,16},{1,17},{2,18},{3,19},{4,20},{5,21},{6,22},{7,23},{8,24},{9,... | collective-permute-start | bytes 24584 | tf_op jit(solution)/shard_map/ppermute | solution.py:499
  103.3 3.3 %collective-permute-done.23.two_ref = f32[8,256]{1,0:T(8,128)S(1)} collective-permute-done((f32[8,256]{1,0:T(8,128)S(1)}, f32[8,256]{1,0:T(8,128)S(1)}, u32[]{:S(2)}, u32[]{:S(2)}) %collective-permute-start.23) | collective-permute-done | bytes 8224 | tf_op jit(solution)/shard_map/ppermute | solution.py:499
  108.2 2.3 %plane_step.1 = (f32[8,256]{1,0:T(8,128)S(1)}, f32[136,256]{1,0:T(8,128)S(1)}, f32[768,256]{1,0:T(8,128)S(1)}) custom-call(f32[2]{0:T(128)S(1)} %add_convert_fusion.flag_ref, f32[136,256]{1,0:T(8,128)S(1)} %slice_add_fusion.1.here_ref, f32[136,256]{1,0:T(8,128)S(1)} %collective-permute-done.21.pair_ref, f32[136,256]{1,0:T(8,128)S(1)} %collective-permute-done.22.middle_ref, ...), custom_call_target="tpu_custom_call" | custom-call | tf_op jit(solution)/shard_map/plane_step/pallas_call | solution.py:923
  111.4 1.8 %collective-permute-start.28 = (f32[136,256]{1,0:T(8,128)S(1)}, f32[136,256]{1,0:T(8,128)S(1)}, u32[]{:S(2)}, u32[]{:S(2)}) collective-permute-start(f32[136,256]{1,0:T(8,128)S(1)} %get-tuple-element.64.a_ref.pulled_ref), channel_id=1, source_target_pairs={{0,6},{1,7},{2,4},{3,5},{4,2},{5,3},{6,0},{7,1},{8,14},{9,15},{10,... | collective-permute-start | bytes 417800 | tf_op jit(solution)/shard_map/ppermute | solution.py:499
  114.5 2.2 %collective-permute-done.27.c_ref = f32[136,256]{1,0:T(8,128)S(1)} collective-permute-done((f32[136,256]{1,0:T(8,128)S(1)}, f32[136,256]{1,0:T(8,128)S(1)}, u32[]{:S(2)}, u32[]{:S(2)}) %collective-permute-start.27) | collective-permute-done | bytes 139296 | tf_op jit(solution)/shard_map/ppermute | solution.py:499
  117.2 1.8 %plane_mix.5 = (f32[136,256]{1,0:T(8,128)S(1)}, f32[392,256]{1,0:T(8,128)S(1)}, f32[128,512]{1,0:T(8,128)S(1)}) custom-call(s32[6]{0:T(128)S(1)} %broadcast_multiply_fusion.first_ref, bf16[1024,512]{1,0:T(8,128)(2,1)S(1)} %get-tuple-element.46.high_ref, bf16[1024,512]{1,0:T(8,128)(2,1)S(1)} %get-tuple-element.47.low_ref, ...), custom_call_target="tpu_custom_call" | custom-call | tf_op jit(solution)/shard_map/plane_mix/pallas_call | solution.py:774
  119.0 3.6 %collective-permute-start.29 = (f32[392,256]{1,0:T(8,128)S(1)}, f32[392,256]{1,0:T(8,128)S(1)}, u32[]{:S(2)}, u32[]{:S(2)}) collective-permute-start(f32[392,256]{1,0:T(8,128)S(1)} %get-tuple-element.66), channel_id=1, source_target_pairs={{0,1},{1,0},{2,3},{3,2},{4,5},{5,4},{6,7},{7,6},{8,9},{9,8},{10,11... | collective-permute-start | bytes 1204232 | tf_op jit(solution)/shard_map/ppermute | solution.py:499
  122.6 2.2 %collective-permute-start.32 = (f32[128,512]{1,0:T(8,128)S(1)}, f32[128,512]{1,0:T(8,128)S(1)}, u32[]{:S(2)}, u32[]{:S(2)}) collective-permute-start(f32[128,512]{1,0:T(8,128)S(1)} %maximum_add_fusion.1), channel_id=1, source_target_pairs={{0,0},{1,16},{2,8},{3,24},{4,4},{5,20},{6,12},{7,28},{8,1},{9,17},... | collective-permute-start | bytes 786440 | tf_op jit(solution)/shard_map/ppermute | solution.py:499
  125.9 9.4 %collective-permute-done.30.pair_ref = f32[136,256]{1,0:T(8,128)S(1)} collective-permute-done((f32[136,256]{1,0:T(8,128)S(1)}, f32[136,256]{1,0:T(8,128)S(1)}, u32[]{:S(2)}, u32[]{:S(2)}) %collective-permute-start.30) | collective-permute-done | bytes 139296 | tf_op jit(solution)/shard_map/ppermute | solution.py:499
  138.0 6.2 %all-to-all-start = ((f32[32,24,128]{2,1,0:T(8,128)}), f32[32,24,128]{2,1,0:T(8,128)}, u32[]{:S(2)}, u32[]{:S(2)}) async-start(f32[32,24,128]{2,1,0:T(8,128)} %broadcast_in_dim.2), calls=%async_computation | async-start | bytes 786432 | tf_op jit(solution)/shard_map/all_to_all | solution.py:1113
  146.0 4.6 %collective-permute-start.33 = (f32[128,512]{1,0:T(8,128)}, f32[128,512]{1,0:T(8,128)S(1)}, u32[]{:S(2)}, u32[]{:S(2)}) collective-permute-start(f32[128,512]{1,0:T(8,128)} %maximum_add_fusion.2), channel_id=1, source_target_pairs={{0,0},{1,16},{2,8},{3,24},{4,4},{5,20},{6,12},{7,28},{8,1},{9,17},... | collective-permute-start | bytes 786440 | tf_op jit(solution)/shard_map/ppermute | solution.py:499
  150.5 8.3 %all-to-all-done = f32[32,24,128]{2,1,0:T(8,128)} async-done(((f32[32,24,128]{2,1,0:T(8,128)}), f32[32,24,128]{2,1,0:T(8,128)}, u32[]{:S(2)}, u32[]{:S(2)}) %all-to-all-start) | async-done | bytes 393248 | tf_op jit(solution)/shard_map/all_to_all | solution.py:1113
  159.9 2.1 %collective-permute-done.33.q2 = f32[128,512]{1,0:T(8,128)S(1)} collective-permute-done((f32[128,512]{1,0:T(8,128)}, f32[128,512]{1,0:T(8,128)S(1)}, u32[]{:S(2)}, u32[]{:S(2)}) %collective-permute-start.33) | collective-permute-done | bytes 262176 | tf_op jit(solution)/shard_map/ppermute | solution.py:499
  161.9 2.9 %plane_finish.1 = f32[4096,128]{1,0:T(8,128)} custom-call(f32[8,256]{1,0:T(8,128)S(1)} %get-tuple-element.59.open_ref, f32[24,128]{1,0:T(8,128)S(1)} %reduce_sum.9.close_ref, f32[128,512]{1,0:T(8,128)S(1)} %collective-permute-done.25.q0, f32[128,512]{1,0:T(8,128)S(1)} %collective-permute-done.32.q1, f32[128,512]{1,0:T(8,128)S(1)} %collective-permute-done.33.q2, ...), custom_call_target="tpu_custom_call" | custom-call | tf_op jit(solution)/shard_map/plane_finish/pallas_call | solution.py:1036
  (107 shorter events, 39.5 us)
Async XLA Ops:
  5.7 19.5 %collective-permute-start = (f32[152,512]{1,0:T(8,128)S(1)}, f32[152,512]{1,0:T(8,128)S(1)}, u32[]{:S(2)}, u32[]{:S(2)}) collective-permute-start(f32[152,512]{1,0:T(8,128)S(1)} %send.1), channel_id=1, source_target_pairs={{0,0},{1,8},{2,16},{3,24},{4,4},{5,12},{6,20},{7,28},{8,2},{9,10},... | collective-permute-start | bytes 933896 | tf_op jit(solution)/shard_map/ppermute | solution.py:499
  29.5 7.1 %collective-permute-start.5 = (f32[128,256]{1,0:T(8,128)S(1)}, f32[128,256]{1,0:T(8,128)S(1)}, u32[]{:S(2)}, u32[]{:S(2)}) collective-permute-start(f32[128,256]{1,0:T(8,128)S(1)} %get-tuple-element.41), channel_id=1, source_target_pairs={{0,4},{1,5},{2,6},{3,7},{4,0},{5,1},{6,2},{7,3},{8,12},{9,13},{10,... | collective-permute-start | bytes 393224 | tf_op jit(solution)/shard_map/ppermute | solution.py:499
  30.8 7.5 %collective-permute-start.6 = (f32[128,256]{1,0:T(8,128)S(1)}, f32[128,256]{1,0:T(8,128)S(1)}, u32[]{:S(2)}, u32[]{:S(2)}) collective-permute-start(f32[128,256]{1,0:T(8,128)S(1)} %get-tuple-element.42), channel_id=1, source_target_pairs={{0,2},{1,3},{2,0},{3,1},{4,6},{5,7},{6,4},{7,5},{8,10},{9,11},{10,... | collective-permute-start | bytes 393224 | tf_op jit(solution)/shard_map/ppermute | solution.py:499
  30.8 7.5 %collective-permute-start.7 = (f32[128,256]{1,0:T(8,128)S(1)}, f32[128,256]{1,0:T(8,128)S(1)}, u32[]{:S(2)}, u32[]{:S(2)}) collective-permute-start(f32[128,256]{1,0:T(8,128)S(1)} %get-tuple-element.43), channel_id=1, source_target_pairs={{0,6},{1,7},{2,4},{3,5},{4,2},{5,3},{6,0},{7,1},{8,14},{9,15},{10,... | collective-permute-start | bytes 393224 | tf_op jit(solution)/shard_map/ppermute | solution.py:499
  32.2 10.7 %collective-permute-start.8 = (f32[128,256]{1,0:T(8,128)S(1)}, f32[128,256]{1,0:T(8,128)S(1)}, u32[]{:S(2)}, u32[]{:S(2)}) collective-permute-start(f32[128,256]{1,0:T(8,128)S(1)} %bitcast.12), channel_id=1, source_target_pairs={{0,0},{1,8},{2,16},{3,24},{4,4},{5,12},{6,20},{7,28},{8,2},{9,10},... | collective-permute-start | bytes 393224 | tf_op jit(solution)/shard_map/ppermute | solution.py:499
  35.4 14.4 %collective-permute-start.4 = (f32[24,1024]{1,0:T(8,128)S(1)}, f32[24,1024]{1,0:T(8,128)S(1)}, u32[]{:S(2)}, u32[]{:S(2)}) collective-permute-start(f32[24,1024]{1,0:T(8,128)S(1)} %pad_maximum_fusion.1.refs_0_), channel_id=1, source_target_pairs={{0,4},{1,5},{2,6},{3,7},{4,0},{5,1},{6,2},{7,3},{8,12},{9,13},{10,... | collective-permute-start | bytes 294920 | tf_op jit(solution)/shard_map/ppermute | solution.py:499
  42.9 11.5 %collective-permute-start.10 = (f32[256,256]{1,0:T(8,128)S(1)}, f32[256,256]{1,0:T(8,128)S(1)}, u32[]{:S(2)}, u32[]{:S(2)}) collective-permute-start(f32[256,256]{1,0:T(8,128)S(1)} %pad_maximum_fusion.here_ref), channel_id=1, source_target_pairs={{8,16},{9,17},{10,18},{11,19},{12,20},{13,21},{14,22},{15,23},{16,... | collective-permute-start | bytes 786440 | tf_op jit(solution)/shard_map/ppermute | solution.py:499
  43.6 10.8 %collective-permute-start.9 = (f32[256,256]{1,0:T(8,128)S(1)}, f32[256,256]{1,0:T(8,128)S(1)}, u32[]{:S(2)}, u32[]{:S(2)}) collective-permute-start(f32[256,256]{1,0:T(8,128)S(1)} %pad_maximum_fusion.here_ref), channel_id=1, source_target_pairs={{0,8},{1,9},{2,10},{3,11},{4,12},{5,13},{6,14},{7,15},{8,0},{9,1},... | collective-permute-start | bytes 786440 | tf_op jit(solution)/shard_map/ppermute | solution.py:499
  46.8 13.4 %collective-permute-start.2 = (f32[24,1024]{1,0:T(8,128)S(1)}, f32[24,1024]{1,0:T(8,128)S(1)}, u32[]{:S(2)}, u32[]{:S(2)}) collective-permute-start(f32[24,1024]{1,0:T(8,128)S(1)} %pad_maximum_fusion.1.refs_0_), channel_id=1, source_target_pairs={{0,2},{1,3},{2,0},{3,1},{4,6},{5,7},{6,4},{7,5},{8,10},{9,11},{10,... | collective-permute-start | bytes 294920 | tf_op jit(solution)/shard_map/ppermute | solution.py:499
  48.7 11.5 %collective-permute-start.3 = (f32[24,1024]{1,0:T(8,128)S(1)}, f32[24,1024]{1,0:T(8,128)S(1)}, u32[]{:S(2)}, u32[]{:S(2)}) collective-permute-start(f32[24,1024]{1,0:T(8,128)S(1)} %pad_maximum_fusion.1.refs_0_), channel_id=1, source_target_pairs={{0,6},{1,7},{2,4},{3,5},{4,2},{5,3},{6,0},{7,1},{8,14},{9,15},{10,... | collective-permute-start | bytes 294920 | tf_op jit(solution)/shard_map/ppermute | solution.py:499
  57.5 7.7 %collective-permute-start.11 = (f32[136,256]{1,0:T(8,128)S(1)}, f32[136,256]{1,0:T(8,128)S(1)}, u32[]{:S(2)}, u32[]{:S(2)}) collective-permute-start(f32[136,256]{1,0:T(8,128)S(1)} %plane_first.1.a_ref.pulled_ref.refs_4_), channel_id=1, source_target_pairs={{0,4},{1,5},{2,6},{3,7},{4,0},{5,1},{6,2},{7,3},{8,12},{9,13},{10,... | collective-permute-start | bytes 417800 | tf_op jit(solution)/shard_map/ppermute | solution.py:499
  57.8 7.3 %collective-permute-start.12 = (f32[136,256]{1,0:T(8,128)S(1)}, f32[136,256]{1,0:T(8,128)S(1)}, u32[]{:S(2)}, u32[]{:S(2)}) collective-permute-start(f32[136,256]{1,0:T(8,128)S(1)} %plane_first.1.a_ref.pulled_ref.refs_4_), channel_id=1, source_target_pairs={{0,2},{1,3},{2,0},{3,1},{4,6},{5,7},{6,4},{7,5},{8,10},{9,11},{10,... | collective-permute-start | bytes 417800 | tf_op jit(solution)/shard_map/ppermute | solution.py:499
  59.2 6.0 %collective-permute-start.13 = (f32[136,256]{1,0:T(8,128)S(1)}, f32[136,256]{1,0:T(8,128)S(1)}, u32[]{:S(2)}, u32[]{:S(2)}) collective-permute-start(f32[136,256]{1,0:T(8,128)S(1)} %plane_first.1.a_ref.pulled_ref.refs_4_), channel_id=1, source_target_pairs={{0,6},{1,7},{2,4},{3,5},{4,2},{5,3},{6,0},{7,1},{8,14},{9,15},{10,... | collective-permute-start | bytes 417800 | tf_op jit(solution)/shard_map/ppermute | solution.py:499
  66.9 5.3 %collective-permute-start.14 = (f32[392,256]{1,0:T(8,128)S(1)}, f32[392,256]{1,0:T(8,128)S(1)}, u32[]{:S(2)}, u32[]{:S(2)}) collective-permute-start(f32[392,256]{1,0:T(8,128)S(1)} %get-tuple-element.52), channel_id=1, source_target_pairs={{0,1},{1,0},{2,3},{3,2},{4,5},{5,4},{6,7},{7,6},{8,9},{9,8},{10,11... | collective-permute-start | bytes 1204232 | tf_op jit(solution)/shard_map/ppermute | solution.py:499
  72.3 4.9 %collective-permute-start.15 = (f32[136,256]{1,0:T(8,128)S(1)}, f32[136,256]{1,0:T(8,128)S(1)}, u32[]{:S(2)}, u32[]{:S(2)}) collective-permute-start(f32[136,256]{1,0:T(8,128)S(1)} %slice_add_fusion.2.here_ref.refs_0_), channel_id=1, source_target_pairs={{0,8},{1,9},{2,10},{3,11},{4,12},{5,13},{6,14},{7,15},{8,0},{9,1},... | collective-permute-start | bytes 417800 | tf_op jit(solution)/shard_map/ppermute | solution.py:499
  72.3 4.9 %collective-permute-start.16 = (f32[136,256]{1,0:T(8,128)S(1)}, f32[136,256]{1,0:T(8,128)S(1)}, u32[]{:S(2)}, u32[]{:S(2)}) collective-permute-start(f32[136,256]{1,0:T(8,128)S(1)} %slice_add_fusion.2.here_ref.refs_0_), channel_id=1, source_target_pairs={{8,16},{9,17},{10,18},{11,19},{12,20},{13,21},{14,22},{15,23},{16,... | collective-permute-start | bytes 417800 | tf_op jit(solution)/shard_map/ppermute | solution.py:499
  80.6 4.2 %collective-permute-start.18 = (f32[136,256]{1,0:T(8,128)S(1)}, f32[136,256]{1,0:T(8,128)S(1)}, u32[]{:S(2)}, u32[]{:S(2)}) collective-permute-start(f32[136,256]{1,0:T(8,128)S(1)} %get-tuple-element.55.a_ref.refs_3_), channel_id=1, source_target_pairs={{0,2},{1,3},{2,0},{3,1},{4,6},{5,7},{6,4},{7,5},{8,10},{9,11},{10,... | collective-permute-start | bytes 417800 | tf_op jit(solution)/shard_map/ppermute | solution.py:499
  81.3 6.2 %collective-permute-start.19 = (f32[136,256]{1,0:T(8,128)S(1)}, f32[136,256]{1,0:T(8,128)S(1)}, u32[]{:S(2)}, u32[]{:S(2)}) collective-permute-start(f32[136,256]{1,0:T(8,128)S(1)} %get-tuple-element.55.a_ref.refs_3_), channel_id=1, source_target_pairs={{0,6},{1,7},{2,4},{3,5},{4,2},{5,3},{6,0},{7,1},{8,14},{9,15},{10,... | collective-permute-start | bytes 417800 | tf_op jit(solution)/shard_map/ppermute | solution.py:499
  89.3 7.5 %collective-permute-start.20 = (f32[392,256]{1,0:T(8,128)S(1)}, f32[392,256]{1,0:T(8,128)S(1)}, u32[]{:S(2)}, u32[]{:S(2)}) collective-permute-start(f32[392,256]{1,0:T(8,128)S(1)} %get-tuple-element.57), channel_id=1, source_target_pairs={{0,1},{1,0},{2,3},{3,2},{4,5},{5,4},{6,7},{7,6},{8,9},{9,8},{10,11... | collective-permute-start | bytes 1204232 | tf_op jit(solution)/shard_map/ppermute | solution.py:499
  91.8 18.8 %collective-permute-start.25 = (f32[128,512]{1,0:T(8,128)S(1)}, f32[128,512]{1,0:T(8,128)S(1)}, u32[]{:S(2)}, u32[]{:S(2)}) collective-permute-start(f32[128,512]{1,0:T(8,128)S(1)} %maximum_add_fusion), channel_id=1, source_target_pairs={{0,0},{1,16},{2,8},{3,24},{4,4},{5,20},{6,12},{7,28},{8,1},{9,17},... | collective-permute-start | bytes 786440 | tf_op jit(solution)/shard_map/ppermute | solution.py:499
  96.8 11.3 %collective-permute-start.21 = (f32[136,256]{1,0:T(8,128)S(1)}, f32[136,256]{1,0:T(8,128)S(1)}, u32[]{:S(2)}, u32[]{:S(2)}) collective-permute-start(f32[136,256]{1,0:T(8,128)S(1)} %slice_add_fusion.1.here_ref), channel_id=1, source_target_pairs={{0,8},{1,9},{2,10},{3,11},{4,12},{5,13},{6,14},{7,15},{8,0},{9,1},... | collective-permute-start | bytes 417800 | tf_op jit(solution)/shard_map/ppermute | solution.py:499
  97.3 10.9 %collective-permute-start.22 = (f32[136,256]{1,0:T(8,128)S(1)}, f32[136,256]{1,0:T(8,128)S(1)}, u32[]{:S(2)}, u32[]{:S(2)}) collective-permute-start(f32[136,256]{1,0:T(8,128)S(1)} %slice_add_fusion.1.here_ref), channel_id=1, source_target_pairs={{8,16},{9,17},{10,18},{11,19},{12,20},{13,21},{14,22},{15,23},{16,... | collective-permute-start | bytes 417800 | tf_op jit(solution)/shard_map/ppermute | solution.py:499
  98.0 8.7 %collective-permute-start.23 = (f32[8,256]{1,0:T(8,128)S(1)}, f32[8,256]{1,0:T(8,128)S(1)}, u32[]{:S(2)}, u32[]{:S(2)}) collective-permute-start(f32[8,256]{1,0:T(8,128)S(1)} %slice.59), channel_id=1, source_target_pairs={{0,16},{1,17},{2,18},{3,19},{4,20},{5,21},{6,22},{7,23},{8,24},{9,... | collective-permute-start | bytes 24584 | tf_op jit(solution)/shard_map/ppermute | solution.py:499
  101.5 6.6 %collective-permute-start.24 = (f32[8,256]{1,0:T(8,128)S(1)}, f32[8,256]{1,0:T(8,128)S(1)}, u32[]{:S(2)}, u32[]{:S(2)}) collective-permute-start(f32[8,256]{1,0:T(8,128)S(1)} %slice.59), channel_id=1, source_target_pairs={{0,24},{1,25},{2,26},{3,27},{4,28},{5,29},{6,30},{7,31},{8,16},{9,... | collective-permute-start | bytes 24584 | tf_op jit(solution)/shard_map/ppermute | solution.py:499
  111.4 5.3 %collective-permute-start.27 = (f32[136,256]{1,0:T(8,128)S(1)}, f32[136,256]{1,0:T(8,128)S(1)}, u32[]{:S(2)}, u32[]{:S(2)}) collective-permute-start(f32[136,256]{1,0:T(8,128)S(1)} %get-tuple-element.64.a_ref.pulled_ref), channel_id=1, source_target_pairs={{0,2},{1,3},{2,0},{3,1},{4,6},{5,7},{6,4},{7,5},{8,10},{9,11},{10,... | collective-permute-start | bytes 417800 | tf_op jit(solution)/shard_map/ppermute | solution.py:499
  111.4 5.8 %collective-permute-start.28 = (f32[136,256]{1,0:T(8,128)S(1)}, f32[136,256]{1,0:T(8,128)S(1)}, u32[]{:S(2)}, u32[]{:S(2)}) collective-permute-start(f32[136,256]{1,0:T(8,128)S(1)} %get-tuple-element.64.a_ref.pulled_ref), channel_id=1, source_target_pairs={{0,6},{1,7},{2,4},{3,5},{4,2},{5,3},{6,0},{7,1},{8,14},{9,15},{10,... | collective-permute-start | bytes 417800 | tf_op jit(solution)/shard_map/ppermute | solution.py:499
  119.0 5.8 %collective-permute-start.29 = (f32[392,256]{1,0:T(8,128)S(1)}, f32[392,256]{1,0:T(8,128)S(1)}, u32[]{:S(2)}, u32[]{:S(2)}) collective-permute-start(f32[392,256]{1,0:T(8,128)S(1)} %get-tuple-element.66), channel_id=1, source_target_pairs={{0,1},{1,0},{2,3},{3,2},{4,5},{5,4},{6,7},{7,6},{8,9},{9,8},{10,11... | collective-permute-start | bytes 1204232 | tf_op jit(solution)/shard_map/ppermute | solution.py:499
  122.6 14.7 %collective-permute-start.32 = (f32[128,512]{1,0:T(8,128)S(1)}, f32[128,512]{1,0:T(8,128)S(1)}, u32[]{:S(2)}, u32[]{:S(2)}) collective-permute-start(f32[128,512]{1,0:T(8,128)S(1)} %maximum_add_fusion.1), channel_id=1, source_target_pairs={{0,0},{1,16},{2,8},{3,24},{4,4},{5,20},{6,12},{7,28},{8,1},{9,17},... | collective-permute-start | bytes 786440 | tf_op jit(solution)/shard_map/ppermute | solution.py:499
  124.8 10.5 %collective-permute-start.30 = (f32[136,256]{1,0:T(8,128)S(1)}, f32[136,256]{1,0:T(8,128)S(1)}, u32[]{:S(2)}, u32[]{:S(2)}) collective-permute-start(f32[136,256]{1,0:T(8,128)S(1)} %slice_add_fusion.here_ref), channel_id=1, source_target_pairs={{0,8},{1,9},{2,10},{3,11},{4,12},{5,13},{6,14},{7,15},{8,0},{9,1},... | collective-permute-start | bytes 417800 | tf_op jit(solution)/shard_map/ppermute | solution.py:499
  125.3 10.1 %collective-permute-start.31 = (f32[136,256]{1,0:T(8,128)S(1)}, f32[136,256]{1,0:T(8,128)S(1)}, u32[]{:S(2)}, u32[]{:S(2)}) collective-permute-start(f32[136,256]{1,0:T(8,128)S(1)} %slice_add_fusion.here_ref), channel_id=1, source_target_pairs={{8,16},{9,17},{10,18},{11,19},{12,20},{13,21},{14,22},{15,23},{16,... | collective-permute-start | bytes 417800 | tf_op jit(solution)/shard_map/ppermute | solution.py:499
  138.0 20.8 %all-to-all-start = ((f32[32,24,128]{2,1,0:T(8,128)}), f32[32,24,128]{2,1,0:T(8,128)}, u32[]{:S(2)}, u32[]{:S(2)}) async-start(f32[32,24,128]{2,1,0:T(8,128)} %broadcast_in_dim.2), calls=%async_computation | async-start | bytes 786432 | tf_op jit(solution)/shard_map/all_to_all | solution.py:1113
  146.0 16.0 %collective-permute-start.33 = (f32[128,512]{1,0:T(8,128)}, f32[128,512]{1,0:T(8,128)S(1)}, u32[]{:S(2)}, u32[]{:S(2)}) collective-permute-start(f32[128,512]{1,0:T(8,128)} %maximum_add_fusion.2), channel_id=1, source_target_pairs={{0,0},{1,16},{2,8},{3,24},{4,4},{5,20},{6,12},{7,28},{8,1},{9,17},... | collective-permute-start | bytes 786440 | tf_op jit(solution)/shard_map/ppermute | solution.py:499
  (20 other events, 299.3 us)

commit v6 on v5

--- a/solution.py
+++ b/solution.py
@@ -13,6 +13,9 @@
 HIGH = lax.Precision.HIGHEST
 SPAN = 256
 MIB = 1024 * 1024
+
+
+SMALL = pl.CostEstimate(flops=1, bytes_accessed=1, transcendentals=0)
 
 
 def params(mib=16):
@@ -595,47 +598,70 @@
     return product(first, turn(waves, spec, -1.0), order)
 
 
-def send_kernel(inc_ref, field_ref, gauge_ref, kind_ref, out_ref):
+def describe_kernel(inc_ref, gauge_ref, kind_ref, seen_ref, out_ref):
     blocks, slots, width = inc_ref.shape
-    rows = blocks * slots
-    hours = field_ref.shape[1]
+    rows, hours = seen_ref.shape
+    count = blocks * slots
+    tile = 8
+    side = tile * slots
+    weights = inc_ref[...].astype(F32).astype(BF16)
+    row = lax.broadcasted_iota(jnp.int32, (side, side), 0)
+    col = lax.broadcasted_iota(jnp.int32, (side, side), 1)
+    same = row // slots == col // slots
+    for i in range(blocks // tile):
+        flat = weights[i * tile : (i + 1) * tile].reshape(side, width)
+        full = lax.dot_general(flat, flat, (((1,), (1,)), ((), ())), preferred_element_type=F32)
+        own = jnp.where(same, full, 0.0)
+        out_ref[pl.ds(0, slots), pl.ds(i * side, side)] = jnp.sum(own.reshape(tile, slots, side), axis=0)
+    kinds = jnp.concatenate([kind_ref[...].astype(F32), jnp.zeros((1, count - rows), F32)], axis=1)
+    out_ref[pl.ds(slots, 8), :] = jnp.concatenate(
+        [gauge_ref[...].astype(F32), kinds, jnp.zeros((6, count), F32)], axis=0
+    )
+    turned = jnp.transpose(seen_ref[...])
+    step = hours * rows // count
+    for i in range(count // rows):
+        out_ref[pl.ds(slots + 8, step), pl.ds(i * rows, rows)] = turned[i * step : (i + 1) * step]
+
+
+def describe(incidence, row_gauge, gauge_kernel, observed):
+    blocks, slots, _ = incidence.shape
+    rows, hours = observed.shape
+    count = blocks * slots
+    return pl.pallas_call(
+        describe_kernel,
+        out_shape=jax.ShapeDtypeStruct((slots + 8 + hours * rows // count, count), F32),
+        compiler_params=params(),
+        name="describe",
+        cost_estimate=SMALL,
+    )(incidence, row_gauge.reshape(1, count), gauge_kernel.reshape(1, rows), observed)
+
+
+def send_kernel(inc_ref, field_ref, out_ref):
+    blocks, slots, width = inc_ref.shape
     weights = inc_ref[...].astype(F32).astype(BF16)
     parts = []
     for b in range(blocks):
         parts.append(pick(weights[b], field_ref[pl.ds(b * width, width), :]))
-    out_ref[pl.ds(0, hours), :] = jnp.transpose(jnp.concatenate(parts, axis=0))
-    flat = weights.reshape(rows, width)
-    full = lax.dot_general(flat, flat, (((1,), (1,)), ((), ())), preferred_element_type=F32)
-    row = lax.broadcasted_iota(jnp.int32, (rows, rows), 0)
-    col = lax.broadcasted_iota(jnp.int32, (rows, rows), 1)
-    own = jnp.where(row // slots == col // slots, full, 0.0)
-    out_ref[pl.ds(hours, slots), :] = jnp.sum(own.reshape(blocks, slots, rows), axis=0)
-    out_ref[pl.ds(hours + slots, 8), :] = jnp.concatenate(
-        [gauge_ref[...].astype(F32), kind_ref[...].astype(F32), jnp.zeros((6, rows), F32)], axis=0
-    )
-
-
-def send(incidence, field, row_gauge, gauge_kernel):
+    out_ref[...] = jnp.transpose(jnp.concatenate(parts, axis=0))
+
+
+def send(incidence, field):
     blocks, slots, width = incidence.shape
-    count = blocks * slots
     hours = field.shape[1]
     step = 8
-    height = hours + slots + 8
-    kinds = jnp.pad(gauge_kernel, (0, count - gauge_kernel.shape[0]))
     return pl.pallas_call(
         send_kernel,
         grid=(blocks // step,),
         in_specs=[
             pl.BlockSpec((step, slots, width), lambda i: (i, 0, 0)),
             pl.BlockSpec((step * width, hours), lambda i: (i, 0)),
-            pl.BlockSpec((1, step * slots), lambda i: (0, i)),
-            pl.BlockSpec((1, step * slots), lambda i: (0, i)),
         ],
-        out_specs=pl.BlockSpec((height, step * slots), lambda i: (0, i)),
-        out_shape=jax.ShapeDtypeStruct((height, count), F32),
+        out_specs=pl.BlockSpec((hours, step * slots), lambda i: (0, i)),
+        out_shape=jax.ShapeDtypeStruct((hours, blocks * slots), F32),
         compiler_params=params(),
         name="send",
-    )(incidence, field, row_gauge.reshape(1, count), kinds.reshape(1, count))
+        cost_estimate=SMALL,
+    )(incidence, field)
 
 
 def hot_rows(gauge, first, rows):
@@ -643,14 +669,14 @@
     return jnp.where(gauge == mine, 1.0, 0.0).astype(BF16)
 
 
-def spread_kernel(first_ref, mine_ref, other_ref, *out_refs):
-    hours, rows = out_refs[0].shape
-    where = mine_ref.shape[0] - 8
+def spread_kernel(first_ref, mine_ref, other_ref, meta_ref, meta_other_ref, *out_refs):
+    rows = out_refs[0].shape[1]
+    where = meta_ref.shape[0] - 8
     for m, out_ref in enumerate(out_refs):
         result = None
-        for ref in (mine_ref, other_ref):
-            hot = hot_rows(ref[where : where + 1, :], first_ref[m], rows)
-            for piece in reversed(pieces(ref[pl.ds(0, hours), :], 3)):
+        for ref, meta in ((mine_ref, meta_ref), (other_ref, meta_other_ref)):
+            hot = hot_rows(meta[where : where + 1, :], first_ref[m], rows)
+            for piece in reversed(pieces(ref[...], 3)):
                 term = lax.dot_general(
                     piece, hot, (((1,), (1,)), ((), ())), preferred_element_type=F32
                 )
@@ -658,14 +684,16 @@
         out_ref[...] = result
 
 
-def spread(first, parcels, hours, rows):
+def spread(first, parcels, metas, rows):
+    hours = parcels[0].shape[0]
     return pl.pallas_call(
         spread_kernel,
-        in_specs=[pl.BlockSpec(memory_space=pltpu.SMEM)] + [pl.BlockSpec(memory_space=pltpu.VMEM)] * 2,
+        in_specs=[pl.BlockSpec(memory_space=pltpu.SMEM)] + [pl.BlockSpec(memory_space=pltpu.VMEM)] * 4,
         out_shape=[jax.ShapeDtypeStruct((hours, rows), F32)] * 4,
         compiler_params=params(),
         name="spread",
-    )(first, *parcels)
+        cost_estimate=SMALL,
+    )(first, *parcels, *metas)
 
 
 def plane_couple_kernel(last, first_ref, *refs):
@@ -781,6 +809,7 @@
         ],
         compiler_params=params(),
         name="plane_mix",
+        cost_estimate=SMALL,
     )(first, *coupling, *metas, *values)
 
 
@@ -804,6 +833,7 @@
         out_shape=jax.ShapeDtypeStruct((SPAN, rows), F32),
         compiler_params=params(),
         name="plane_spectrum",
+        cost_estimate=SMALL,
     )(meta, kernels, *forward)
 
 
@@ -811,34 +841,33 @@
     return jnp.where(even, middle, pair), jnp.where(even, pair, middle)
 
 
-def plane_first_kernel(flag_ref, here_ref, pair_ref, middle_ref, spec_ref, *refs):
-    *mats, out_ref = refs
+def plane_first_kernel(flag_ref, *refs):
+    sums, seen, (spec_ref, *mats, out_ref) = refs[:3], refs[3:6], refs[6:]
     forward, first, last = mats[0:3], mats[3:6], mats[6:9]
-    rows = here_ref.shape[1]
-    hours = here_ref.shape[0] // 2
+    hours, rows = sums[0].shape
     spec = spec_ref[...]
-    before, after = sides(flag_ref[0] > 0.5, pair_ref[...], middle_ref[...])
-    now, later = plane_delayed(
-        before[:hours], here_ref[pl.ds(0, hours), :], after[:hours], spec, forward, last, 3
-    )
-    start = here_ref[pl.ds(hours, hours), :] - now
-    start_later = (after[hours:] - later) * flag_ref[1]
+    even = flag_ref[0] > 0.5
+    before, after = sides(even, sums[1][...], sums[2][...])
+    now, later = plane_delayed(before, sums[0][...], after, spec, forward, last, 3)
+    start = seen[0][...] - now
+    start_later = (sides(even, seen[1][...], seen[2][...])[1] - later) * flag_ref[1]
     out_ref[pl.ds(0, hours), :] = plane_advanced(start, start_later, spec, forward, first, 3)
     out_ref[pl.ds(hours, NOTE), :] = jnp.concatenate(
         [lanes(start, start), jnp.zeros((NOTE - 1, rows), F32)], axis=0
     )
 
 
-def plane_first(flags, sums, spec, mats):
-    double, rows = sums[0].shape
-    args = [flags, *sums, spec, *mats]
+def plane_first(flags, sums, seen, spec, mats):
+    hours, rows = sums[0].shape
+    args = [flags, *sums, *seen, spec, *mats]
     return pl.pallas_call(
         plane_first_kernel,
         in_specs=[pl.BlockSpec(memory_space=pltpu.SMEM)]
         + [pl.BlockSpec(memory_space=pltpu.VMEM)] * (len(args) - 1),
-        out_shape=jax.ShapeDtypeStruct((double // 2 + NOTE, rows), F32),
+        out_shape=jax.ShapeDtypeStruct((hours + NOTE, rows), F32),
         compiler_params=params(),
         name="plane_first",
+        cost_estimate=SMALL,
     )(*args)
 
 
@@ -878,6 +907,7 @@
         ],
         compiler_params=params(),
         name="plane_open",
+        cost_estimate=SMALL,
     )(*args)
 
 
@@ -931,6 +961,7 @@
         ],
         compiler_params=params(),
         name="plane_step",
+        cost_estimate=SMALL,
     )(*args)
 
 
@@ -967,6 +998,7 @@
         out_shape=jax.ShapeDtypeStruct((24, rows // 2), F32),
         compiler_params=params(),
         name="plane_close",
+        cost_estimate=SMALL,
     )(*args)
 
 
@@ -1061,23 +1093,27 @@
     forward, inverse_first, inverse_last = turned_transforms()
     mats = [*forward, *inverse_first, *inverse_last]
 
-    parcel = moved(send(incidence, first_guess, row_gauge, gauge_kernel), to_plane)
-    seen, parcel = lax.optimization_barrier((jnp.transpose(observed), parcel))
-    parcels = [parcel, moved(parcel, over_core)]
-    seen = moved(seen, to_plane)
-    metas = [value[hours:] for value in parcels]
+    slots = incidence.shape[1]
+    ahead = describe(incidence, row_gauge, gauge_kernel, observed)
+    ahead, field = lax.optimization_barrier((ahead, first_guess))
+    ahead = moved(ahead, to_plane)
+    parcel = moved(send(incidence, field), to_plane)
+    meta, seen = ahead[: slots + 8], ahead[slots + 8 :]
+    seen = jnp.concatenate([seen[:, i : i + rows] for i in range(0, seen.shape[1], rows)], axis=0)
+    seen = [seen, moved(seen, z_pair), moved(seen, z_middle)]
+    metas = [meta, moved(meta, over_core)]
     both = jnp.concatenate(metas, axis=1)
     around = [both] + [moved(both, where) for where in SQUARE]
-    spec = plane_spectrum(metas[0], kernels, forward, rows)
-
-    dense = spread(first, parcels, hours, rows)
+    spec = plane_spectrum(meta, kernels, forward, rows)
+    parcel, seen, around, spec = lax.optimization_barrier((parcel, seen, around, spec))
+
+    dense = spread(first, [parcel, moved(parcel, over_core)], metas, rows)
     sums = dense[0] + sum(moved(value, where) for value, where in zip(dense[1:], SQUARE))
-    sums = jnp.concatenate([sums, seen], axis=0)
     sums = [sums, moved(sums, z_pair), moved(sums, z_middle)]
     coupled = plane_couple(first, around[:2], rows)
     coupled, sums = lax.optimization_barrier((coupled, sums))
     coupling = plane_couple(first, around[2:], rows, coupled)
-    pulled = [plane_first(flags, sums, spec, mats)]
+    pulled = [plane_first(flags, sums, seen, spec, mats)]
     kept, shipped, mixes = [], [], []
     for k in range(3):
         if k:
@@ -1095,6 +1131,8 @@
         )
         sums = [mixed, moved(mixed, z_pair), moved(mixed, z_middle)]
         mixes.append(sums)
+        if k:
+            sums, shipped[k - 1] = lax.optimization_barrier((sums, shipped[k - 1]))
         if k == 0:
             following, now = plane_open(flags, sums, pulled[0], spec, mats)
         elif k == 1:
@@ -1103,12 +1141,10 @@
             open_note, following, state = plane_step(
                 flags, sums, two, mirror, mixes[0], pulled[1], pulled[0], now, spec, mats
             )
-            following, shipped[0] = lax.optimization_barrier((following, shipped[0]))
         else:
             shipped.append(moved(kept[2], from_plane))
             note = plane_close(flags, sums, pulled[2], state, spec, mats)
         pulled.append(following)
-    note, shipped[1] = lax.optimization_barrier((note, shipped[1]))
     copies = jnp.broadcast_to(note[None], (Z_ * X_ * Y_ * C_,) + note.shape)
     close_note = jnp.sum(lax.all_to_all(copies, ("basin", "tm"), 0, 0, tiled=False), axis=0)
     return plane_finish([open_note, close_note], shipped, incidence, first_guess)

time: 165 us -> 166 us (level)
  waiting for transfers between devices: 62.5 us -> 56.4 us
  starting transfers between devices: 62.3 us -> 66.8 us
    ppermute x34 -> x37, waiting for transfers between devices: 54.2 us -> 48.4 us  [moved(): return lax.ppermute(value, ('basin', 'tm'), pairs)]
    ppermute x34 -> x37, starting transfers between devices: 56 us -> 61.8 us  [moved(): return lax.ppermute(value, ('basin', 'tm'), pairs)]
    unnamed x35 -> x36, local copies, waits for them, and re-layouts: 3.39 us -> 4.92 us
  transfers between devices with their start and end apart: 35 -> 38, of which waited for: 18 -> 19; matrix products, arithmetic and copies ran while one was open for 2% -> 3% of each run, Pallas kernels for 10% -> 6%
where the time goes in v6:
time: 166 us; the launch traced here: 165 us
  starting transfers between devices  66.8 us (40%)
  waiting for transfers between devices  56.4 us (34%)
  Pallas kernels  31.6 us (19%)
  local copies, waits for them, and re-layouts  6.81 us (4%)
  other arithmetic  3.18 us (2%)
    ppermute x37, starting transfers between devices, moved(): return lax.ppermute(value, ('basin', 'tm'), pairs)  61.8 us
    ppermute x37, waiting for transfers between devices, moved(): return lax.ppermute(value, ('basin', 'tm'), pairs)  48.4 us
    pallas_call x2, Pallas kernels, plane_couple(): pl.pallas_call(functools.partial(plane_couple_kernel, last), in_specs=[pl...  9.56 us
    all_to_all x1, waiting for transfers between devices, plane_shards(): lax.all_to_all(copies, ('basin', 'tm'), 0, 0, tiled=False)  8.02 us
    pallas_call x3, Pallas kernels, plane_mix(): pl.pallas_call(plane_mix_kernel, in_specs=[pl.BlockSpec(memory_space=pltp...  5.29 us
    all_to_all x1, starting transfers between devices, plane_shards(): lax.all_to_all(copies, ('basin', 'tm'), 0, 0, tiled=False)  4.98 us
    unnamed x36, local copies, waits for them, and re-layouts  4.92 us
  transfers between devices with their start and end apart: 38, of which 19 were waited for; matrix products, arithmetic and copies ran while one was open for 3% of the time, Pallas kernels for 6%

profile of v6, /device:TPU:1, one launch (start us, length us, event | category | flops | bytes accessed | tf_op | source)
XLA Modules:
  0.0 165.4 jit_solution(3446863599175289863)
XLA Ops:
  3.5 4.6 %collective-permute-start.1 = (f32[88,512]{1,0:T(8,128)S(1)}, f32[88,512]{1,0:T(8,128)S(1)}, u32[]{:S(2)}, u32[]{:S(2)}) collective-permute-start(f32[88,512]{1,0:T(8,128)S(1)} %describe.1), channel_id=1, source_target_pairs={{0,0},{1,8},{2,16},{3,24},{4,4},{5,12},{6,20},{7,28},{8,2},{9,10},... | collective-permute-start | bytes 540680 | tf_op jit(solution)/shard_map/ppermute | solution.py:502
  11.4 3.3 %collective-permute-start = (f32[128,512]{1,0:T(8,128)S(1)}, f32[128,512]{1,0:T(8,128)S(1)}, u32[]{:S(2)}, u32[]{:S(2)}) collective-permute-start(f32[128,512]{1,0:T(8,128)S(1)} %send.1), channel_id=1, source_target_pairs={{0,0},{1,8},{2,16},{3,24},{4,4},{5,12},{6,20},{7,28},{8,2},{9,10},... | collective-permute-start | bytes 786440 | tf_op jit(solution)/shard_map/ppermute | solution.py:502
  14.7 3.3 %collective-permute-done.1 = f32[88,512]{1,0:T(8,128)S(1)} collective-permute-done((f32[88,512]{1,0:T(8,128)S(1)}, f32[88,512]{1,0:T(8,128)S(1)}, u32[]{:S(2)}, u32[]{:S(2)}) %collective-permute-start.1) | collective-permute-done | bytes 180256 | tf_op jit(solution)/shard_map/ppermute | solution.py:502
  20.5 9.8 %collective-permute-start.7 = (f32[24,1024]{1,0:T(8,128)S(1)}, f32[24,1024]{1,0:T(8,128)S(1)}, u32[]{:S(2)}, u32[]{:S(2)}) collective-permute-start(f32[24,1024]{1,0:T(8,128)S(1)} %pad_maximum_fusion.1.refs_0_), channel_id=1, source_target_pairs={{0,6},{1,7},{2,4},{3,5},{4,2},{5,3},{6,0},{7,1},{8,14},{9,15},{10,... | collective-permute-start | bytes 294920 | tf_op jit(solution)/shard_map/ppermute | solution.py:502
  32.9 2.1 %collective-permute-done.6.refs_0_ = f32[24,1024]{1,0:T(8,128)S(1)} collective-permute-done((f32[24,1024]{1,0:T(8,128)S(1)}, f32[24,1024]{1,0:T(8,128)S(1)}, u32[]{:S(2)}, u32[]{:S(2)}) %collective-permute-start.6) | collective-permute-done | bytes 98336 | tf_op jit(solution)/shard_map/ppermute | solution.py:502
  37.6 2.7 %spread.1 = (f32[128,256]{1,0:T(8,128)S(1)}, f32[128,256]{1,0:T(8,128)S(1)}, f32[128,256]{1,0:T(8,128)S(1)}, f32[128,256]{1,0:T(8,128)S(1)}) custom-call(s32[6]{0:T(128)S(1)} %broadcast_multiply_fusion.first_ref, f32[128,512]{1,0:T(8,128)S(1)} %collective-permute-done.mine_ref, f32[128,512]{1,0:T(8,128)S(1)} %collective-permute-done.8.other_ref, ...), custom_call_target="tpu_custom_call" | custom-call | flops 1 | bytes 1 | tf_op jit(solution)/shard_map/spread/pallas_call | solution.py:689
  43.1 2.0 %collective-permute-done.9 = f32[128,256]{1,0:T(8,128)S(1)} collective-permute-done((f32[128,256]{1,0:T(8,128)S(1)}, f32[128,256]{1,0:T(8,128)S(1)}, u32[]{:S(2)}, u32[]{:S(2)}) %collective-permute-start.9) | collective-permute-done | bytes 131104 | tf_op jit(solution)/shard_map/ppermute | solution.py:502
  46.1 2.7 %collective-permute-done.11 = f32[128,256]{1,0:T(8,128)S(1)} collective-permute-done((f32[128,256]{1,0:T(8,128)S(1)}, f32[128,256]{1,0:T(8,128)S(1)}, u32[]{:S(2)}, u32[]{:S(2)}) %collective-permute-start.11) | collective-permute-done | bytes 131104 | tf_op jit(solution)/shard_map/ppermute | solution.py:502
  49.7 2.0 %collective-permute-start.12 = (f32[128,256]{1,0:T(8,128)S(1)}, f32[128,256]{1,0:T(8,128)S(1)}, u32[]{:S(2)}, u32[]{:S(2)}) collective-permute-start(f32[128,256]{1,0:T(8,128)S(1)} %add_add_fusion.refs_0_), channel_id=1, source_target_pairs={{0,8},{1,9},{2,10},{3,11},{4,12},{5,13},{6,14},{7,15},{8,0},{9,1},... | collective-permute-start | bytes 393224 | tf_op jit(solution)/shard_map/ppermute | solution.py:502
  51.7 4.6 %plane_couple.2.refs_2_ = f32[1024,512]{1,0:T(8,128)S(1)} custom-call(s32[6]{0:T(128)S(1)} %broadcast_multiply_fusion.first_ref, f32[24,1024]{1,0:T(8,128)S(1)} %pad_maximum_fusion.1.refs_0_, f32[24,1024]{1,0:T(8,128)S(1)} %collective-permute-done.5.refs_1_), custom_call_target="tpu_custom_call" | custom-call | flops 2147483648 | bytes 2000000 | tf_op jit(solution)/shard_map/plane_couple/pallas_call | solution.py:756
  56.4 3.0 %plane_first.1.a_ref.pulled_ref.refs_4_ = f32[136,256]{1,0:T(8,128)S(1)} custom-call(f32[2]{0:T(128)S(1)} %add_convert_fusion.flag_ref, f32[128,256]{1,0:T(8,128)S(1)} %add_add_fusion.refs_0_, f32[128,256]{1,0:T(8,128)S(1)} %collective-permute-done.12.refs_1_, f32[128,256]{1,0:T(8,128)S(1)} %collective-permute-done.13.refs_2_, ...), custom_call_target="tpu_custom_call" | custom-call | flops 1 | bytes 1 | tf_op jit(solution)/shard_map/plane_first/pallas_call | solution.py:863
  62.2 4.9 %plane_couple.3 = (bf16[1024,512]{1,0:T(8,128)(2,1)S(1)}, bf16[1024,512]{1,0:T(8,128)(2,1)S(1)}) custom-call(s32[6]{0:T(128)S(1)} %broadcast_multiply_fusion.first_ref, f32[24,1024]{1,0:T(8,128)S(1)} %collective-permute-done.6.refs_0_, f32[24,1024]{1,0:T(8,128)S(1)} %collective-permute-done.7.refs_1_, f32[1024,512]{1,0:T(8,128)S(1)} %plane_couple.2.refs_2_), custom_call_target="tpu_custom_call" | custom-call | flops 2147483648 | bytes 2000000 | tf_op jit(solution)/shard_map/plane_couple/pallas_call | solution.py:756
  69.5 2.4 %collective-permute-start.17 = (f32[392,256]{1,0:T(8,128)S(1)}, f32[392,256]{1,0:T(8,128)S(1)}, u32[]{:S(2)}, u32[]{:S(2)}) collective-permute-start(f32[392,256]{1,0:T(8,128)S(1)} %get-tuple-element.74), channel_id=1, source_target_pairs={{0,1},{1,0},{2,3},{3,2},{4,5},{5,4},{6,7},{7,6},{8,9},{9,8},{10,11... | collective-permute-start | bytes 1204232 | tf_op jit(solution)/shard_map/ppermute | solution.py:502
  74.1 2.1 %collective-permute-start.18 = (f32[136,256]{1,0:T(8,128)S(1)}, f32[136,256]{1,0:T(8,128)S(1)}, u32[]{:S(2)}, u32[]{:S(2)}) collective-permute-start(f32[136,256]{1,0:T(8,128)S(1)} %slice_add_fusion.2.here_ref.refs_0_), channel_id=1, source_target_pairs={{0,8},{1,9},{2,10},{3,11},{4,12},{5,13},{6,14},{7,15},{8,0},{9,1},... | collective-permute-start | bytes 417800 | tf_op jit(solution)/shard_map/ppermute | solution.py:502
  76.3 3.4 %collective-permute-done.18.pair_ref.refs_1_ = f32[136,256]{1,0:T(8,128)S(1)} collective-permute-done((f32[136,256]{1,0:T(8,128)S(1)}, f32[136,256]{1,0:T(8,128)S(1)}, u32[]{:S(2)}, u32[]{:S(2)}) %collective-permute-start.18) | collective-permute-done | bytes 139296 | tf_op jit(solution)/shard_map/ppermute | solution.py:502
  79.7 2.1 %plane_open.1 = (f32[136,256]{1,0:T(8,128)S(1)}, f32[128,256]{1,0:T(8,128)S(1)}) custom-call(f32[2]{0:T(128)S(1)} %add_convert_fusion.flag_ref, f32[136,256]{1,0:T(8,128)S(1)} %slice_add_fusion.2.here_ref.refs_0_, f32[136,256]{1,0:T(8,128)S(1)} %collective-permute-done.18.pair_ref.refs_1_, f32[136,256]{1,0:T(8,128)S(1)} %collective-permute-done.19.middle_ref.refs_2_, ...), custom_call_target="tpu_custom_call" | custom-call | flops 1 | bytes 1 | tf_op jit(solution)/shard_map/plane_open/pallas_call | solution.py:900
  84.6 2.3 %collective-permute-done.22.d_ref = f32[136,256]{1,0:T(8,128)S(1)} collective-permute-done((f32[136,256]{1,0:T(8,128)S(1)}, f32[136,256]{1,0:T(8,128)S(1)}, u32[]{:S(2)}, u32[]{:S(2)}) %collective-permute-start.22) | collective-permute-done | bytes 139296 | tf_op jit(solution)/shard_map/ppermute | solution.py:502
  86.8 4.1 %collective-permute-done.21.c_ref = f32[136,256]{1,0:T(8,128)S(1)} collective-permute-done((f32[136,256]{1,0:T(8,128)S(1)}, f32[136,256]{1,0:T(8,128)S(1)}, u32[]{:S(2)}, u32[]{:S(2)}) %collective-permute-start.21) | collective-permute-done | bytes 139296 | tf_op jit(solution)/shard_map/ppermute | solution.py:502
  93.7 3.3 %collective-permute-start.26 = (f32[128,512]{1,0:T(8,128)S(1)}, f32[128,512]{1,0:T(8,128)S(1)}, u32[]{:S(2)}, u32[]{:S(2)}) collective-permute-start(f32[128,512]{1,0:T(8,128)S(1)} %maximum_add_fusion), channel_id=1, source_target_pairs={{0,0},{1,16},{2,8},{3,24},{4,4},{5,20},{6,12},{7,28},{8,1},{9,17},... | collective-permute-start | bytes 786440 | tf_op jit(solution)/shard_map/ppermute | solution.py:502
  99.4 3.8 %collective-permute-start.24 = (f32[136,256]{1,0:T(8,128)S(1)}, f32[136,256]{1,0:T(8,128)S(1)}, u32[]{:S(2)}, u32[]{:S(2)}) collective-permute-start(f32[136,256]{1,0:T(8,128)S(1)} %slice_add_fusion.1.here_ref), channel_id=1, source_target_pairs={{0,8},{1,9},{2,10},{3,11},{4,12},{5,13},{6,14},{7,15},{8,0},{9,1},... | collective-permute-start | bytes 417800 | tf_op jit(solution)/shard_map/ppermute | solution.py:502
  103.2 5.6 %collective-permute-done.26.q0 = f32[128,512]{1,0:T(8,128)S(1)} collective-permute-done((f32[128,512]{1,0:T(8,128)S(1)}, f32[128,512]{1,0:T(8,128)S(1)}, u32[]{:S(2)}, u32[]{:S(2)}) %collective-permute-start.26) | collective-permute-done | bytes 262176 | tf_op jit(solution)/shard_map/ppermute | solution.py:502
  108.9 2.3 %plane_step.1 = (f32[8,256]{1,0:T(8,128)S(1)}, f32[136,256]{1,0:T(8,128)S(1)}, f32[768,256]{1,0:T(8,128)S(1)}) custom-call(f32[2]{0:T(128)S(1)} %add_convert_fusion.flag_ref, f32[136,256]{1,0:T(8,128)S(1)} %slice_add_fusion.1.here_ref, f32[136,256]{1,0:T(8,128)S(1)} %collective-permute-done.24.pair_ref, f32[136,256]{1,0:T(8,128)S(1)} %collective-permute-done.25.middle_ref, ...), custom_call_target="tpu_custom_call" | custom-call | flops 1 | bytes 1 | tf_op jit(solution)/shard_map/plane_step/pallas_call | solution.py:953
  111.3 2.2 %collective-permute-start.30 = (f32[136,256]{1,0:T(8,128)S(1)}, f32[136,256]{1,0:T(8,128)S(1)}, u32[]{:S(2)}, u32[]{:S(2)}) collective-permute-start(f32[136,256]{1,0:T(8,128)S(1)} %get-tuple-element.88.a_ref.pulled_ref), channel_id=1, source_target_pairs={{0,2},{1,3},{2,0},{3,1},{4,6},{5,7},{6,4},{7,5},{8,10},{9,11},{10,... | collective-permute-start | bytes 417800 | tf_op jit(solution)/shard_map/ppermute | solution.py:502
  113.9 2.3 %collective-permute-done.31.d_ref = f32[136,256]{1,0:T(8,128)S(1)} collective-permute-done((f32[136,256]{1,0:T(8,128)S(1)}, f32[136,256]{1,0:T(8,128)S(1)}, u32[]{:S(2)}, u32[]{:S(2)}) %collective-permute-start.31) | collective-permute-done | bytes 139296 | tf_op jit(solution)/shard_map/ppermute | solution.py:502
  116.2 4.0 %collective-permute-done.30.c_ref = f32[136,256]{1,0:T(8,128)S(1)} collective-permute-done((f32[136,256]{1,0:T(8,128)S(1)}, f32[136,256]{1,0:T(8,128)S(1)}, u32[]{:S(2)}, u32[]{:S(2)}) %collective-permute-start.30) | collective-permute-done | bytes 139296 | tf_op jit(solution)/shard_map/ppermute | solution.py:502
  126.5 2.5 %collective-permute-start.33 = (f32[136,256]{1,0:T(8,128)S(1)}, f32[136,256]{1,0:T(8,128)S(1)}, u32[]{:S(2)}, u32[]{:S(2)}) collective-permute-start(f32[136,256]{1,0:T(8,128)S(1)} %slice_add_fusion.here_ref), channel_id=1, source_target_pairs={{0,8},{1,9},{2,10},{3,11},{4,12},{5,13},{6,14},{7,15},{8,0},{9,1},... | collective-permute-start | bytes 417800 | tf_op jit(solution)/shard_map/ppermute | solution.py:502
  129.1 8.7 %collective-permute-done.35.q1 = f32[128,512]{1,0:T(8,128)S(1)} collective-permute-done((f32[128,512]{1,0:T(8,128)S(1)}, f32[128,512]{1,0:T(8,128)S(1)}, u32[]{:S(2)}, u32[]{:S(2)}) %collective-permute-start.35) | collective-permute-done | bytes 262176 | tf_op jit(solution)/shard_map/ppermute | solution.py:502
  139.8 5.0 %all-to-all-start = ((f32[32,24,128]{2,1,0:T(8,128)}), f32[32,24,128]{2,1,0:T(8,128)}, u32[]{:S(2)}, u32[]{:S(2)}) async-start(f32[32,24,128]{2,1,0:T(8,128)} %broadcast_in_dim.2), calls=%async_computation | async-start | bytes 786432 | tf_op jit(solution)/shard_map/all_to_all | solution.py:1149
  146.7 4.6 %collective-permute-start.36 = (f32[128,512]{1,0:T(8,128)S(1)}, f32[128,512]{1,0:T(8,128)S(1)}, u32[]{:S(2)}, u32[]{:S(2)}) collective-permute-start(f32[128,512]{1,0:T(8,128)S(1)} %maximum_add_fusion.2), channel_id=1, source_target_pairs={{0,0},{1,16},{2,8},{3,24},{4,4},{5,20},{6,12},{7,28},{8,1},{9,17},... | collective-permute-start | bytes 786440 | tf_op jit(solution)/shard_map/ppermute | solution.py:502
  151.3 8.0 %all-to-all-done = f32[32,24,128]{2,1,0:T(8,128)} async-done(((f32[32,24,128]{2,1,0:T(8,128)}), f32[32,24,128]{2,1,0:T(8,128)}, u32[]{:S(2)}, u32[]{:S(2)}) %all-to-all-start) | async-done | bytes 393248 | tf_op jit(solution)/shard_map/all_to_all | solution.py:1149
  160.4 2.1 %collective-permute-done.36.q2 = f32[128,512]{1,0:T(8,128)S(1)} collective-permute-done((f32[128,512]{1,0:T(8,128)S(1)}, f32[128,512]{1,0:T(8,128)S(1)}, u32[]{:S(2)}, u32[]{:S(2)}) %collective-permute-start.36) | collective-permute-done | bytes 262176 | tf_op jit(solution)/shard_map/ppermute | solution.py:502
  162.5 2.9 %plane_finish.1 = f32[4096,128]{1,0:T(8,128)} custom-call(f32[8,256]{1,0:T(8,128)S(1)} %get-tuple-element.85.open_ref, f32[24,128]{1,0:T(8,128)S(1)} %reduce_sum.9.close_ref, f32[128,512]{1,0:T(8,128)S(1)} %collective-permute-done.26.q0, f32[128,512]{1,0:T(8,128)S(1)} %collective-permute-done.35.q1, f32[128,512]{1,0:T(8,128)S(1)} %collective-permute-done.36.q2, ...), custom_call_target="tpu_custom_call" | custom-call | tf_op jit(solution)/shard_map/plane_finish/pallas_call | solution.py:1068
  (114 shorter events, 46.0 us)
Async XLA Ops:
  3.5 14.5 %collective-permute-start.1 = (f32[88,512]{1,0:T(8,128)S(1)}, f32[88,512]{1,0:T(8,128)S(1)}, u32[]{:S(2)}, u32[]{:S(2)}) collective-permute-start(f32[88,512]{1,0:T(8,128)S(1)} %describe.1), channel_id=1, source_target_pairs={{0,0},{1,8},{2,16},{3,24},{4,4},{5,12},{6,20},{7,28},{8,2},{9,10},... | collective-permute-start | bytes 540680 | tf_op jit(solution)/shard_map/ppermute | solution.py:502
  11.4 18.9 %collective-permute-start = (f32[128,512]{1,0:T(8,128)S(1)}, f32[128,512]{1,0:T(8,128)S(1)}, u32[]{:S(2)}, u32[]{:S(2)}) collective-permute-start(f32[128,512]{1,0:T(8,128)S(1)} %send.1), channel_id=1, source_target_pairs={{0,0},{1,8},{2,16},{3,24},{4,4},{5,12},{6,20},{7,28},{8,2},{9,10},... | collective-permute-start | bytes 786440 | tf_op jit(solution)/shard_map/ppermute | solution.py:502
  18.1 13.3 %collective-permute-start.3 = (f32[128,256]{1,0:T(8,128)S(1)}, f32[128,256]{1,0:T(8,128)S(1)}, u32[]{:S(2)}, u32[]{:S(2)}) collective-permute-start(f32[128,256]{1,0:T(8,128)S(1)} %pad_maximum_fusion.refs_3_), channel_id=1, source_target_pairs={{8,16},{9,17},{10,18},{11,19},{12,20},{13,21},{14,22},{15,23},{16,... | collective-permute-start | bytes 393224 | tf_op jit(solution)/shard_map/ppermute | solution.py:502
  18.8 12.6 %collective-permute-start.2 = (f32[128,256]{1,0:T(8,128)S(1)}, f32[128,256]{1,0:T(8,128)S(1)}, u32[]{:S(2)}, u32[]{:S(2)}) collective-permute-start(f32[128,256]{1,0:T(8,128)S(1)} %pad_maximum_fusion.refs_3_), channel_id=1, source_target_pairs={{0,8},{1,9},{2,10},{3,11},{4,12},{5,13},{6,14},{7,15},{8,0},{9,1},... | collective-permute-start | bytes 393224 | tf_op jit(solution)/shard_map/ppermute | solution.py:502
  20.5 12.5 %collective-permute-start.7 = (f32[24,1024]{1,0:T(8,128)S(1)}, f32[24,1024]{1,0:T(8,128)S(1)}, u32[]{:S(2)}, u32[]{:S(2)}) collective-permute-start(f32[24,1024]{1,0:T(8,128)S(1)} %pad_maximum_fusion.1.refs_0_), channel_id=1, source_target_pairs={{0,6},{1,7},{2,4},{3,5},{4,2},{5,3},{6,0},{7,1},{8,14},{9,15},{10,... | collective-permute-start | bytes 294920 | tf_op jit(solution)/shard_map/ppermute | solution.py:502
  30.3 4.7 %collective-permute-start.6 = (f32[24,1024]{1,0:T(8,128)S(1)}, f32[24,1024]{1,0:T(8,128)S(1)}, u32[]{:S(2)}, u32[]{:S(2)}) collective-permute-start(f32[24,1024]{1,0:T(8,128)S(1)} %pad_maximum_fusion.1.refs_0_), channel_id=1, source_target_pairs={{0,2},{1,3},{2,0},{3,1},{4,6},{5,7},{6,4},{7,5},{8,10},{9,11},{10,... | collective-permute-start | bytes 294920 | tf_op jit(solution)/shard_map/ppermute | solution.py:502
  30.3 4.8 %collective-permute-start.5 = (f32[24,1024]{1,0:T(8,128)S(1)}, f32[24,1024]{1,0:T(8,128)S(1)}, u32[]{:S(2)}, u32[]{:S(2)}) collective-permute-start(f32[24,1024]{1,0:T(8,128)S(1)} %pad_maximum_fusion.1.refs_0_), channel_id=1, source_target_pairs={{0,4},{1,5},{2,6},{3,7},{4,0},{5,1},{6,2},{7,3},{8,12},{9,13},{10,... | collective-permute-start | bytes 294920 | tf_op jit(solution)/shard_map/ppermute | solution.py:502
  40.3 4.8 %collective-permute-start.9 = (f32[128,256]{1,0:T(8,128)S(1)}, f32[128,256]{1,0:T(8,128)S(1)}, u32[]{:S(2)}, u32[]{:S(2)}) collective-permute-start(f32[128,256]{1,0:T(8,128)S(1)} %get-tuple-element.60), channel_id=1, source_target_pairs={{0,4},{1,5},{2,6},{3,7},{4,0},{5,1},{6,2},{7,3},{8,12},{9,13},{10,... | collective-permute-start | bytes 393224 | tf_op jit(solution)/shard_map/ppermute | solution.py:502
  41.6 4.5 %collective-permute-start.10 = (f32[128,256]{1,0:T(8,128)S(1)}, f32[128,256]{1,0:T(8,128)S(1)}, u32[]{:S(2)}, u32[]{:S(2)}) collective-permute-start(f32[128,256]{1,0:T(8,128)S(1)} %get-tuple-element.61), channel_id=1, source_target_pairs={{0,2},{1,3},{2,0},{3,1},{4,6},{5,7},{6,4},{7,5},{8,10},{9,11},{10,... | collective-permute-start | bytes 393224 | tf_op jit(solution)/shard_map/ppermute | solution.py:502
  41.9 6.8 %collective-permute-start.11 = (f32[128,256]{1,0:T(8,128)S(1)}, f32[128,256]{1,0:T(8,128)S(1)}, u32[]{:S(2)}, u32[]{:S(2)}) collective-permute-start(f32[128,256]{1,0:T(8,128)S(1)} %get-tuple-element.62), channel_id=1, source_target_pairs={{0,6},{1,7},{2,4},{3,5},{4,2},{5,3},{6,0},{7,1},{8,14},{9,15},{10,... | collective-permute-start | bytes 393224 | tf_op jit(solution)/shard_map/ppermute | solution.py:502
  48.9 7.5 %collective-permute-start.13 = (f32[128,256]{1,0:T(8,128)S(1)}, f32[128,256]{1,0:T(8,128)S(1)}, u32[]{:S(2)}, u32[]{:S(2)}) collective-permute-start(f32[128,256]{1,0:T(8,128)S(1)} %add_add_fusion.refs_0_), channel_id=1, source_target_pairs={{8,16},{9,17},{10,18},{11,19},{12,20},{13,21},{14,22},{15,23},{16,... | collective-permute-start | bytes 393224 | tf_op jit(solution)/shard_map/ppermute | solution.py:502
  49.7 6.7 %collective-permute-start.12 = (f32[128,256]{1,0:T(8,128)S(1)}, f32[128,256]{1,0:T(8,128)S(1)}, u32[]{:S(2)}, u32[]{:S(2)}) collective-permute-start(f32[128,256]{1,0:T(8,128)S(1)} %add_add_fusion.refs_0_), channel_id=1, source_target_pairs={{0,8},{1,9},{2,10},{3,11},{4,12},{5,13},{6,14},{7,15},{8,0},{9,1},... | collective-permute-start | bytes 393224 | tf_op jit(solution)/shard_map/ppermute | solution.py:502
  59.5 7.6 %collective-permute-start.16 = (f32[136,256]{1,0:T(8,128)S(1)}, f32[136,256]{1,0:T(8,128)S(1)}, u32[]{:S(2)}, u32[]{:S(2)}) collective-permute-start(f32[136,256]{1,0:T(8,128)S(1)} %plane_first.1.a_ref.pulled_ref.refs_4_), channel_id=1, source_target_pairs={{0,6},{1,7},{2,4},{3,5},{4,2},{5,3},{6,0},{7,1},{8,14},{9,15},{10,... | collective-permute-start | bytes 417800 | tf_op jit(solution)/shard_map/ppermute | solution.py:502
  60.8 7.0 %collective-permute-start.15 = (f32[136,256]{1,0:T(8,128)S(1)}, f32[136,256]{1,0:T(8,128)S(1)}, u32[]{:S(2)}, u32[]{:S(2)}) collective-permute-start(f32[136,256]{1,0:T(8,128)S(1)} %plane_first.1.a_ref.pulled_ref.refs_4_), channel_id=1, source_target_pairs={{0,2},{1,3},{2,0},{3,1},{4,6},{5,7},{6,4},{7,5},{8,10},{9,11},{10,... | collective-permute-start | bytes 417800 | tf_op jit(solution)/shard_map/ppermute | solution.py:502
  61.2 6.6 %collective-permute-start.14 = (f32[136,256]{1,0:T(8,128)S(1)}, f32[136,256]{1,0:T(8,128)S(1)}, u32[]{:S(2)}, u32[]{:S(2)}) collective-permute-start(f32[136,256]{1,0:T(8,128)S(1)} %plane_first.1.a_ref.pulled_ref.refs_4_), channel_id=1, source_target_pairs={{0,4},{1,5},{2,6},{3,7},{4,0},{5,1},{6,2},{7,3},{8,12},{9,13},{10,... | collective-permute-start | bytes 417800 | tf_op jit(solution)/shard_map/ppermute | solution.py:502
  74.1 5.6 %collective-permute-start.18 = (f32[136,256]{1,0:T(8,128)S(1)}, f32[136,256]{1,0:T(8,128)S(1)}, u32[]{:S(2)}, u32[]{:S(2)}) collective-permute-start(f32[136,256]{1,0:T(8,128)S(1)} %slice_add_fusion.2.here_ref.refs_0_), channel_id=1, source_target_pairs={{0,8},{1,9},{2,10},{3,11},{4,12},{5,13},{6,14},{7,15},{8,0},{9,1},... | collective-permute-start | bytes 417800 | tf_op jit(solution)/shard_map/ppermute | solution.py:502
  81.8 5.0 %collective-permute-start.22 = (f32[136,256]{1,0:T(8,128)S(1)}, f32[136,256]{1,0:T(8,128)S(1)}, u32[]{:S(2)}, u32[]{:S(2)}) collective-permute-start(f32[136,256]{1,0:T(8,128)S(1)} %get-tuple-element.77.a_ref.refs_3_), channel_id=1, source_target_pairs={{0,6},{1,7},{2,4},{3,5},{4,2},{5,3},{6,0},{7,1},{8,14},{9,15},{10,... | collective-permute-start | bytes 417800 | tf_op jit(solution)/shard_map/ppermute | solution.py:502
  83.0 7.9 %collective-permute-start.21 = (f32[136,256]{1,0:T(8,128)S(1)}, f32[136,256]{1,0:T(8,128)S(1)}, u32[]{:S(2)}, u32[]{:S(2)}) collective-permute-start(f32[136,256]{1,0:T(8,128)S(1)} %get-tuple-element.77.a_ref.refs_3_), channel_id=1, source_target_pairs={{0,2},{1,3},{2,0},{3,1},{4,6},{5,7},{6,4},{7,5},{8,10},{9,11},{10,... | collective-permute-start | bytes 417800 | tf_op jit(solution)/shard_map/ppermute | solution.py:502
  83.3 7.7 %collective-permute-start.20 = (f32[136,256]{1,0:T(8,128)S(1)}, f32[136,256]{1,0:T(8,128)S(1)}, u32[]{:S(2)}, u32[]{:S(2)}) collective-permute-start(f32[136,256]{1,0:T(8,128)S(1)} %get-tuple-element.77.a_ref.refs_3_), channel_id=1, source_target_pairs={{0,4},{1,5},{2,6},{3,7},{4,0},{5,1},{6,2},{7,3},{8,12},{9,13},{10,... | collective-permute-start | bytes 417800 | tf_op jit(solution)/shard_map/ppermute | solution.py:502
  93.7 15.1 %collective-permute-start.26 = (f32[128,512]{1,0:T(8,128)S(1)}, f32[128,512]{1,0:T(8,128)S(1)}, u32[]{:S(2)}, u32[]{:S(2)}) collective-permute-start(f32[128,512]{1,0:T(8,128)S(1)} %maximum_add_fusion), channel_id=1, source_target_pairs={{0,0},{1,16},{2,8},{3,24},{4,4},{5,20},{6,12},{7,28},{8,1},{9,17},... | collective-permute-start | bytes 786440 | tf_op jit(solution)/shard_map/ppermute | solution.py:502
  97.1 11.8 %collective-permute-start.28 = (f32[8,256]{1,0:T(8,128)S(1)}, f32[8,256]{1,0:T(8,128)S(1)}, u32[]{:S(2)}, u32[]{:S(2)}) collective-permute-start(f32[8,256]{1,0:T(8,128)S(1)} %slice.68), channel_id=1, source_target_pairs={{0,24},{1,25},{2,26},{3,27},{4,28},{5,29},{6,30},{7,31},{8,16},{9,... | collective-permute-start | bytes 24584 | tf_op jit(solution)/shard_map/ppermute | solution.py:502
  98.5 10.3 %collective-permute-start.27 = (f32[8,256]{1,0:T(8,128)S(1)}, f32[8,256]{1,0:T(8,128)S(1)}, u32[]{:S(2)}, u32[]{:S(2)}) collective-permute-start(f32[8,256]{1,0:T(8,128)S(1)} %slice.68), channel_id=1, source_target_pairs={{0,16},{1,17},{2,18},{3,19},{4,20},{5,21},{6,22},{7,23},{8,24},{9,... | collective-permute-start | bytes 24584 | tf_op jit(solution)/shard_map/ppermute | solution.py:502
  98.7 10.2 %collective-permute-start.25 = (f32[136,256]{1,0:T(8,128)S(1)}, f32[136,256]{1,0:T(8,128)S(1)}, u32[]{:S(2)}, u32[]{:S(2)}) collective-permute-start(f32[136,256]{1,0:T(8,128)S(1)} %slice_add_fusion.1.here_ref), channel_id=1, source_target_pairs={{8,16},{9,17},{10,18},{11,19},{12,20},{13,21},{14,22},{15,23},{16,... | collective-permute-start | bytes 417800 | tf_op jit(solution)/shard_map/ppermute | solution.py:502
  99.4 9.5 %collective-permute-start.24 = (f32[136,256]{1,0:T(8,128)S(1)}, f32[136,256]{1,0:T(8,128)S(1)}, u32[]{:S(2)}, u32[]{:S(2)}) collective-permute-start(f32[136,256]{1,0:T(8,128)S(1)} %slice_add_fusion.1.here_ref), channel_id=1, source_target_pairs={{0,8},{1,9},{2,10},{3,11},{4,12},{5,13},{6,14},{7,15},{8,0},{9,1},... | collective-permute-start | bytes 417800 | tf_op jit(solution)/shard_map/ppermute | solution.py:502
  111.2 5.0 %collective-permute-start.31 = (f32[136,256]{1,0:T(8,128)S(1)}, f32[136,256]{1,0:T(8,128)S(1)}, u32[]{:S(2)}, u32[]{:S(2)}) collective-permute-start(f32[136,256]{1,0:T(8,128)S(1)} %get-tuple-element.88.a_ref.pulled_ref), channel_id=1, source_target_pairs={{0,6},{1,7},{2,4},{3,5},{4,2},{5,3},{6,0},{7,1},{8,14},{9,15},{10,... | collective-permute-start | bytes 417800 | tf_op jit(solution)/shard_map/ppermute | solution.py:502
  111.3 8.9 %collective-permute-start.30 = (f32[136,256]{1,0:T(8,128)S(1)}, f32[136,256]{1,0:T(8,128)S(1)}, u32[]{:S(2)}, u32[]{:S(2)}) collective-permute-start(f32[136,256]{1,0:T(8,128)S(1)} %get-tuple-element.88.a_ref.pulled_ref), channel_id=1, source_target_pairs={{0,2},{1,3},{2,0},{3,1},{4,6},{5,7},{6,4},{7,5},{8,10},{9,11},{10,... | collective-permute-start | bytes 417800 | tf_op jit(solution)/shard_map/ppermute | solution.py:502
  113.5 6.7 %collective-permute-start.29 = (f32[136,256]{1,0:T(8,128)S(1)}, f32[136,256]{1,0:T(8,128)S(1)}, u32[]{:S(2)}, u32[]{:S(2)}) collective-permute-start(f32[136,256]{1,0:T(8,128)S(1)} %get-tuple-element.88.a_ref.pulled_ref), channel_id=1, source_target_pairs={{0,4},{1,5},{2,6},{3,7},{4,0},{5,1},{6,2},{7,3},{8,12},{9,13},{10,... | collective-permute-start | bytes 417800 | tf_op jit(solution)/shard_map/ppermute | solution.py:502
  123.0 14.8 %collective-permute-start.35 = (f32[128,512]{1,0:T(8,128)S(1)}, f32[128,512]{1,0:T(8,128)S(1)}, u32[]{:S(2)}, u32[]{:S(2)}) collective-permute-start(f32[128,512]{1,0:T(8,128)S(1)} %maximum_add_fusion.1), channel_id=1, source_target_pairs={{0,0},{1,16},{2,8},{3,24},{4,4},{5,20},{6,12},{7,28},{8,1},{9,17},... | collective-permute-start | bytes 786440 | tf_op jit(solution)/shard_map/ppermute | solution.py:502
  125.8 11.9 %collective-permute-start.34 = (f32[136,256]{1,0:T(8,128)S(1)}, f32[136,256]{1,0:T(8,128)S(1)}, u32[]{:S(2)}, u32[]{:S(2)}) collective-permute-start(f32[136,256]{1,0:T(8,128)S(1)} %slice_add_fusion.here_ref), channel_id=1, source_target_pairs={{8,16},{9,17},{10,18},{11,19},{12,20},{13,21},{14,22},{15,23},{16,... | collective-permute-start | bytes 417800 | tf_op jit(solution)/shard_map/ppermute | solution.py:502
  126.5 11.3 %collective-permute-start.33 = (f32[136,256]{1,0:T(8,128)S(1)}, f32[136,256]{1,0:T(8,128)S(1)}, u32[]{:S(2)}, u32[]{:S(2)}) collective-permute-start(f32[136,256]{1,0:T(8,128)S(1)} %slice_add_fusion.here_ref), channel_id=1, source_target_pairs={{0,8},{1,9},{2,10},{3,11},{4,12},{5,13},{6,14},{7,15},{8,0},{9,1},... | collective-permute-start | bytes 417800 | tf_op jit(solution)/shard_map/ppermute | solution.py:502
  139.8 19.6 %all-to-all-start = ((f32[32,24,128]{2,1,0:T(8,128)}), f32[32,24,128]{2,1,0:T(8,128)}, u32[]{:S(2)}, u32[]{:S(2)}) async-start(f32[32,24,128]{2,1,0:T(8,128)} %broadcast_in_dim.2), calls=%async_computation | async-start | bytes 786432 | tf_op jit(solution)/shard_map/all_to_all | solution.py:1149
  146.7 15.7 %collective-permute-start.36 = (f32[128,512]{1,0:T(8,128)S(1)}, f32[128,512]{1,0:T(8,128)S(1)}, u32[]{:S(2)}, u32[]{:S(2)}) collective-permute-start(f32[128,512]{1,0:T(8,128)S(1)} %maximum_add_fusion.2), channel_id=1, source_target_pairs={{0,0},{1,16},{2,8},{3,24},{4,4},{5,20},{6,12},{7,28},{8,1},{9,17},... | collective-permute-start | bytes 786440 | tf_op jit(solution)/shard_map/ppermute | solution.py:502
  (24 other events, 253.6 us)

commit v7 on v5

--- a/solution.py
+++ b/solution.py
@@ -13,6 +13,9 @@
 HIGH = lax.Precision.HIGHEST
 SPAN = 256
 MIB = 1024 * 1024
+
+
+SMALL = pl.CostEstimate(flops=1, bytes_accessed=1, transcendentals=0)
 
 
 def params(mib=16):
@@ -595,23 +598,50 @@
     return product(first, turn(waves, spec, -1.0), order)
 
 
+def describe_kernel(inc_ref, seen_ref, out_ref):
+    blocks, slots, width = inc_ref.shape
+    rows, hours = seen_ref.shape
+    count = blocks * slots
+    tile = 8
+    side = tile * slots
+    weights = inc_ref[...].astype(F32).astype(BF16)
+    row = lax.broadcasted_iota(jnp.int32, (side, side), 0)
+    col = lax.broadcasted_iota(jnp.int32, (side, side), 1)
+    same = row // slots == col // slots
+    for i in range(blocks // tile):
+        flat = weights[i * tile : (i + 1) * tile].reshape(side, width)
+        full = lax.dot_general(flat, flat, (((1,), (1,)), ((), ())), preferred_element_type=F32)
+        own = jnp.where(same, full, 0.0)
+        out_ref[pl.ds(0, slots), pl.ds(i * side, side)] = jnp.sum(own.reshape(tile, slots, side), axis=0)
+    turned = jnp.transpose(seen_ref[...])
+    step = hours * rows // count
+    for i in range(count // rows):
+        out_ref[pl.ds(slots, step), pl.ds(i * rows, rows)] = turned[i * step : (i + 1) * step]
+
+
+def describe(incidence, observed):
+    blocks, slots, _ = incidence.shape
+    rows, hours = observed.shape
+    count = blocks * slots
+    return pl.pallas_call(
+        describe_kernel,
+        out_shape=jax.ShapeDtypeStruct((slots + hours * rows // count, count), F32),
+        compiler_params=params(),
+        name="describe",
+        cost_estimate=SMALL,
+    )(incidence, observed)
+
+
 def send_kernel(inc_ref, field_ref, gauge_ref, kind_ref, out_ref):
     blocks, slots, width = inc_ref.shape
-    rows = blocks * slots
     hours = field_ref.shape[1]
     weights = inc_ref[...].astype(F32).astype(BF16)
     parts = []
     for b in range(blocks):
         parts.append(pick(weights[b], field_ref[pl.ds(b * width, width), :]))
     out_ref[pl.ds(0, hours), :] = jnp.transpose(jnp.concatenate(parts, axis=0))
-    flat = weights.reshape(rows, width)
-    full = lax.dot_general(flat, flat, (((1,), (1,)), ((), ())), preferred_element_type=F32)
-    row = lax.broadcasted_iota(jnp.int32, (rows, rows), 0)
-    col = lax.broadcasted_iota(jnp.int32, (rows, rows), 1)
-    own = jnp.where(row // slots == col // slots, full, 0.0)
-    out_ref[pl.ds(hours, slots), :] = jnp.sum(own.reshape(blocks, slots, rows), axis=0)
-    out_ref[pl.ds(hours + slots, 8), :] = jnp.concatenate(
-        [gauge_ref[...].astype(F32), kind_ref[...].astype(F32), jnp.zeros((6, rows), F32)], axis=0
+    out_ref[pl.ds(hours, 8), :] = jnp.concatenate(
+        [gauge_ref[...].astype(F32), kind_ref[...].astype(F32), jnp.zeros((6, blocks * slots), F32)], axis=0
     )
 
 
@@ -620,7 +650,6 @@
     count = blocks * slots
     hours = field.shape[1]
     step = 8
-    height = hours + slots + 8
     kinds = jnp.pad(gauge_kernel, (0, count - gauge_kernel.shape[0]))
     return pl.pallas_call(
         send_kernel,
@@ -631,10 +660,11 @@
             pl.BlockSpec((1, step * slots), lambda i: (0, i)),
             pl.BlockSpec((1, step * slots), lambda i: (0, i)),
         ],
-        out_specs=pl.BlockSpec((height, step * slots), lambda i: (0, i)),
-        out_shape=jax.ShapeDtypeStruct((height, count), F32),
+        out_specs=pl.BlockSpec((hours + 8, step * slots), lambda i: (0, i)),
+        out_shape=jax.ShapeDtypeStruct((hours + 8, count), F32),
         compiler_params=params(),
         name="send",
+        cost_estimate=SMALL,
     )(incidence, field, row_gauge.reshape(1, count), kinds.reshape(1, count))
 
 
@@ -645,11 +675,10 @@
 
 def spread_kernel(first_ref, mine_ref, other_ref, *out_refs):
     hours, rows = out_refs[0].shape
-    where = mine_ref.shape[0] - 8
     for m, out_ref in enumerate(out_refs):
         result = None
         for ref in (mine_ref, other_ref):
-            hot = hot_rows(ref[where : where + 1, :], first_ref[m], rows)
+            hot = hot_rows(ref[hours : hours + 1, :], first_ref[m], rows)
             for piece in reversed(pieces(ref[pl.ds(0, hours), :], 3)):
                 term = lax.dot_general(
                     piece, hot, (((1,), (1,)), ((), ())), preferred_element_type=F32
@@ -665,6 +694,7 @@
         out_shape=[jax.ShapeDtypeStruct((hours, rows), F32)] * 4,
         compiler_params=params(),
         name="spread",
+        cost_estimate=SMALL,
     )(first, *parcels)
 
 
@@ -755,9 +785,8 @@
     other_ref[body, :] = result[:, rows:]
     mine_ref[tail, :] = note
     other_ref[tail, :] = note
-    where = meta_ref.shape[0] - 8
     for ref in (meta_ref, meta_other_ref):
-        gauge = ref[where : where + 1, :]
+        gauge = ref[0:1, :]
         hot = jnp.concatenate([hot_rows(gauge, first_ref[m], rows) for m in range(4)], axis=0)
         picked = dot(two, hot) + dot(one, hot)
         if ref is meta_ref:
@@ -781,12 +810,13 @@
         ],
         compiler_params=params(),
         name="plane_mix",
+        cost_estimate=SMALL,
     )(first, *coupling, *metas, *values)
 
 
 def plane_spectrum_kernel(class_ref, kernels_ref, f0_ref, f1_ref, f2_ref, out_ref):
     classes, taps = kernels_ref.shape
-    kind = class_ref[class_ref.shape[0] - 7 : class_ref.shape[0] - 6, : out_ref.shape[1]]
+    kind = class_ref[1:2, : out_ref.shape[1]]
     hot = jnp.where(
         lax.broadcasted_iota(jnp.int32, (classes, kind.shape[1]), 0).astype(F32) == kind, 1.0, 0.0
     ).astype(BF16)
@@ -804,6 +834,7 @@
         out_shape=jax.ShapeDtypeStruct((SPAN, rows), F32),
         compiler_params=params(),
         name="plane_spectrum",
+        cost_estimate=SMALL,
     )(meta, kernels, *forward)
 
 
@@ -839,6 +870,7 @@
         out_shape=jax.ShapeDtypeStruct((double // 2 + NOTE, rows), F32),
         compiler_params=params(),
         name="plane_first",
+        cost_estimate=SMALL,
     )(*args)
 
 
@@ -878,6 +910,7 @@
         ],
         compiler_params=params(),
         name="plane_open",
+        cost_estimate=SMALL,
     )(*args)
 
 
@@ -931,6 +964,7 @@
         ],
         compiler_params=params(),
         name="plane_step",
+        cost_estimate=SMALL,
     )(*args)
 
 
@@ -953,8 +987,11 @@
     for i in range(3):
         note += [lanes(parts[i], parts[j]) for j in range(i, 3)]
     note.append(jnp.zeros((24 - len(note), rows), F32))
-    note = jnp.concatenate(note, axis=0)
-    out_ref[...] = note[:, : rows // 2] + note[:, rows // 2 :]
+    note = jnp.sum(jnp.concatenate(note, axis=0), axis=1, keepdims=True)
+    shape = (24, out_ref.shape[2])
+    row, col = (lax.broadcasted_iota(jnp.int32, shape, i) for i in range(2))
+    note = jnp.sum(jnp.where(row == col, jnp.broadcast_to(note, shape), 0.0), axis=0, keepdims=True)
+    out_ref[...] = jnp.broadcast_to(note[None], out_ref.shape)
 
 
 def plane_close(flags, sums, pulled, kept, spec, mats):
@@ -964,13 +1001,14 @@
         plane_close_kernel,
         in_specs=[pl.BlockSpec(memory_space=pltpu.SMEM)]
         + [pl.BlockSpec(memory_space=pltpu.VMEM)] * (len(args) - 1),
-        out_shape=jax.ShapeDtypeStruct((24, rows // 2), F32),
+        out_shape=jax.ShapeDtypeStruct((Z_ * X_ * Y_ * C_, 8, rows // 2), F32),
         compiler_params=params(),
         name="plane_close",
+        cost_estimate=SMALL,
     )(*args)
 
 
-def plane_weights(open_ref, close_ref):
+def plane_weights(open_ref, close):
     scale, alpha, beta = opening(open_ref)
     start = 1.0 / scale
     phibar, rhobar = start, alpha
@@ -990,15 +1028,15 @@
         zu[k + 1] = zu[k + 1] + (a * scale if k == 0 else a)
         z = [value - g * old for value, old in zip(zu, z)]
         if k == 0:
-            square, norm, along = (total(close_ref, i) for i in range(3))
+            square, norm, along = (close[:, i : i + 1] for i in range(3))
         else:
             plain = (a, -b, -g)
-            cross = [[total(close_ref, 3 + 3 * i + j) for j in range(3)] for i in range(3)]
+            cross = [[close[:, 3 + 3 * i + j : 4 + 3 * i + j] for j in range(3)] for i in range(3)]
             along = sum(plain[i] * plain[j] * cross[i][j] for i in range(2) for j in range(3))
             square = along + sum(plain[2] * plain[j] * cross[2][j] for j in range(3))
             pairs = [(i, j) for i in range(3) for j in range(i, 3)]
             norm = sum(
-                plain[i] * plain[j] * total(close_ref, 12 + n) * (1.0 if i == j else 2.0)
+                plain[i] * plain[j] * close[:, 12 + n : 13 + n] * (1.0 if i == j else 2.0)
                 for n, (i, j) in enumerate(pairs)
             )
         alpha = jnp.sqrt(square)
@@ -1008,46 +1046,59 @@
         w = [value / alpha - theta / rho * old for value, old in zip(z, w)]
 
 
-def plane_finish_kernel(open_ref, close_ref, q0, q1, q2, inc_ref, field_ref, out_ref, rows_ref):
+def plane_combine_kernel(open_ref, close_ref, *refs):
+    *parts, out_ref = refs
+    hours, rows = out_ref.shape[1], open_ref.shape[1]
+    close = jnp.sum(close_ref[...], axis=0)[0:1, :]
+    weights = plane_weights(open_ref, close)
+    mine = sum(ref[...] * e for ref, e in zip(parts[:3], weights))
+    skip = parts[3].shape[0] - mine.shape[1] // rows * hours
+    for i in range(mine.shape[1] // rows):
+        here = pl.ds(skip + i * hours, hours)
+        other = sum(ref[here, :] * e for ref, e in zip(parts[3:], weights))
+        out_ref[pl.ds(i * rows, rows), :] = jnp.transpose(mine[:, i * rows : (i + 1) * rows] + other)
+
+
+def plane_combine(open_note, close_note, mine, other):
+    hours, slots = mine[0].shape
+    return pl.pallas_call(
+        plane_combine_kernel,
+        out_shape=jax.ShapeDtypeStruct((slots, hours), F32),
+        compiler_params=params(),
+        name="plane_combine",
+        cost_estimate=SMALL,
+    )(open_note, close_note, *mine, *other)
+
+
+def plane_finish_kernel(rows_ref, inc_ref, field_ref, out_ref):
     blocks, slots, width = inc_ref.shape
-    step = pl.program_id(0)
-
-    @pl.when(step == 0)
-    def _():
-        e0, e1, e2 = plane_weights(open_ref, close_ref)
-        rows_ref[...] = jnp.transpose(q0[...] * e0 + q1[...] * e1 + q2[...] * e2)
-
     weights = inc_ref[...].astype(F32).astype(BF16)
     for b in range(blocks):
         here = pl.ds(b * width, width)
-        rows = rows_ref[pl.ds(pl.multiple_of((step * blocks + b) * slots, slots), slots), :]
         added = sum(
             lax.dot_general(weights[b], piece, (((0,), (0,)), ((), ())), preferred_element_type=F32)
-            for piece in pieces(rows, 2)
+            for piece in pieces(rows_ref[pl.ds(b * slots, slots), :], 2)
         )
         out_ref[here, :] = field_ref[here, :] + added
 
 
-def plane_finish(notes, rows, incidence, field):
+def plane_finish(rows, incidence, field):
     blocks, slots, width = incidence.shape
     hours = field.shape[1]
     step = 8
-    whole = lambda shape: pl.BlockSpec(shape, lambda i: (0, 0))
     return pl.pallas_call(
         plane_finish_kernel,
         grid=(blocks // step,),
-        in_specs=[whole(n.shape) for n in notes]
-        + [whole(q.shape) for q in rows]
-        + [
+        in_specs=[
+            pl.BlockSpec((step * slots, hours), lambda i: (i, 0)),
             pl.BlockSpec((step, slots, width), lambda i: (i, 0, 0)),
             pl.BlockSpec((step * width, hours), lambda i: (i, 0)),
         ],
         out_specs=pl.BlockSpec((step * width, hours), lambda i: (i, 0)),
         out_shape=jax.ShapeDtypeStruct(field.shape, F32),
-        scratch_shapes=[pltpu.VMEM((blocks * slots, hours), F32)],
         compiler_params=params(),
         name="plane_finish",
-    )(*notes, *rows, incidence, field)
+    )(rows, incidence, field)
 
 
 def plane_shards(incidence, row_gauge, gauge_kernel, kernels, observed, first_guess):
@@ -1061,38 +1112,38 @@
     forward, inverse_first, inverse_last = turned_transforms()
     mats = [*forward, *inverse_first, *inverse_last]
 
-    parcel = moved(send(incidence, first_guess, row_gauge, gauge_kernel), to_plane)
-    seen, parcel = lax.optimization_barrier((jnp.transpose(observed), parcel))
+    parcel = send(incidence, first_guess, row_gauge, gauge_kernel)
+    incidence_, seen, parcel = lax.optimization_barrier((incidence, observed, parcel))
+    parcel = moved(parcel, to_plane)
+    behind = moved(describe(incidence_, seen), to_plane)
+    parcel, behind = lax.optimization_barrier((parcel, behind))
     parcels = [parcel, moved(parcel, over_core)]
-    seen = moved(seen, to_plane)
     metas = [value[hours:] for value in parcels]
-    both = jnp.concatenate(metas, axis=1)
-    around = [both] + [moved(both, where) for where in SQUARE]
     spec = plane_spectrum(metas[0], kernels, forward, rows)
-
     dense = spread(first, parcels, hours, rows)
     sums = dense[0] + sum(moved(value, where) for value, where in zip(dense[1:], SQUARE))
-    sums = jnp.concatenate([sums, seen], axis=0)
+
+    slots = incidence.shape[1]
+    gram, seen = behind[:slots], behind[slots:]
+    seen = [seen[:, i : i + rows] for i in range(0, seen.shape[1], rows)]
+    sums = jnp.concatenate([sums, *seen], axis=0)
     sums = [sums, moved(sums, z_pair), moved(sums, z_middle)]
+    both = jnp.concatenate([gram, moved(gram, over_core)], axis=1)
+    both = jnp.concatenate([both, jnp.concatenate(metas, axis=1)], axis=0)
+    around = [both] + [moved(both, where) for where in SQUARE]
     coupled = plane_couple(first, around[:2], rows)
     coupled, sums = lax.optimization_barrier((coupled, sums))
     coupling = plane_couple(first, around[2:], rows, coupled)
     pulled = [plane_first(flags, sums, spec, mats)]
-    kept, shipped, mixes = [], [], []
+
+    slot_rows, slot_rows_other, mixes = [], [], []
     for k in range(3):
-        if k:
-            pulled[k], kept[k - 1] = lax.optimization_barrier((pulled[k], kept[k - 1]))
-            shipped.append(moved(kept[k - 1], from_plane))
         values = [pulled[k]] + [moved(pulled[k], where) for where in SQUARE]
-        mine, other, slot_rows = plane_mix(first, coupling, metas, values)
+        mine, other, picked = plane_mix(first, coupling, metas, values)
         beside = moved(other, over_core)
+        slot_rows.append(picked)
+        slot_rows_other.append(beside)
         mixed = mine + beside[: hours + NOTE]
-        kept.append(
-            slot_rows
-            + jnp.concatenate(
-                [beside[hours + NOTE + i * hours :][:hours] for i in range(slot_rows.shape[1] // rows)], axis=1
-            )
-        )
         sums = [mixed, moved(mixed, z_pair), moved(mixed, z_middle)]
         mixes.append(sums)
         if k == 0:
@@ -1103,15 +1154,12 @@
             open_note, following, state = plane_step(
                 flags, sums, two, mirror, mixes[0], pulled[1], pulled[0], now, spec, mats
             )
-            following, shipped[0] = lax.optimization_barrier((following, shipped[0]))
         else:
-            shipped.append(moved(kept[2], from_plane))
             note = plane_close(flags, sums, pulled[2], state, spec, mats)
         pulled.append(following)
-    note, shipped[1] = lax.optimization_barrier((note, shipped[1]))
-    copies = jnp.broadcast_to(note[None], (Z_ * X_ * Y_ * C_,) + note.shape)
-    close_note = jnp.sum(lax.all_to_all(copies, ("basin", "tm"), 0, 0, tiled=False), axis=0)
-    return plane_finish([open_note, close_note], shipped, incidence, first_guess)
+    close_note = lax.all_to_all(note, ("basin", "tm"), 0, 0, tiled=False)
+    answer = moved(plane_combine(open_note, close_note, slot_rows, slot_rows_other), from_plane)
+    return plane_finish(answer, incidence, first_guess)
 
 
 def solution(mesh):

time: 165 us -> 156 us (0.945)
  starting transfers between devices: 62.3 us -> 49.3 us
  blocking collectives: 0 us -> 11.9 us
  waiting for transfers between devices: 62.5 us -> 58 us
  local copies, waits for them, and re-layouts: 5.99 us -> 4.09 us
  other arithmetic: 2.05 us -> 0.21 us
    all_to_all x0 -> x1, blocking collectives: none -> 11.9 us  [plane_shards(): close_note = lax.all_to_all(note, ('basin', 'tm'), 0, 0, tiled=False)]
    all_to_all x1 -> x0, waiting for transfers between devices: 8.28 us -> none  [plane_shards(): lax.all_to_all(copies, ('basin', 'tm'), 0, 0, tiled=False)]
    ppermute x34 -> x33, starting transfers between devices: 56 us -> 49.3 us  [moved(): return lax.ppermute(value, ('basin', 'tm'), pairs)]
    all_to_all x1 -> x0, starting transfers between devices: 6.23 us -> none  [plane_shards(): lax.all_to_all(copies, ('basin', 'tm'), 0, 0, tiled=False)]
    ppermute x34 -> x33, waiting for transfers between devices: 54.2 us -> 58 us  [moved(): return lax.ppermute(value, ('basin', 'tm'), pairs)]
    pallas_call x1 -> x3, Pallas kernels: 2.9 us -> 3.4 us  [the longest x1 2.6 us: plane_finish(): pl.pallas_call(plane_finish_kernel, grid=(blocks // step,), in_specs=[pl....]
    unnamed x35 -> x32, local copies, waits for them, and re-layouts: 3.39 us -> 3.3 us
  transfers between devices with their start and end apart: 35 -> 33, of which waited for: 18 -> 16; matrix products, arithmetic and copies ran while one was open for 2% -> 0% of each run, Pallas kernels for 10% -> 10%
where the time goes in v7:
time: 156 us
  waiting for transfers between devices  58 us (37%)
  starting transfers between devices  49.3 us (32%)
  Pallas kernels  32 us (21%)
  blocking collectives  11.9 us (8%)
  local copies, waits for them, and re-layouts  4.09 us (3%)
    ppermute x33, waiting for transfers between devices, moved(): return lax.ppermute(value, ('basin', 'tm'), pairs)  58 us
    ppermute x33, starting transfers between devices, moved(): return lax.ppermute(value, ('basin', 'tm'), pairs)  49.3 us
    all_to_all x1, blocking collectives, plane_shards(): close_note = lax.all_to_all(note, ('basin', 'tm'), 0, 0, tiled=False)  11.9 us
    pallas_call x2, Pallas kernels, plane_couple(): pl.pallas_call(functools.partial(plane_couple_kernel, last), in_specs=[pl...  9.57 us
    pallas_call x3, Pallas kernels, plane_mix(): pl.pallas_call(plane_mix_kernel, in_specs=[pl.BlockSpec(memory_space=pltp...  5.29 us
    unnamed x32, local copies, waits for them, and re-layouts  3.3 us
  transfers between devices with their start and end apart: 33, of which 16 were waited for; matrix products, arithmetic and copies ran while one was open for 0% of the time, Pallas kernels for 10%

profile of v7, /device:TPU:1, one launch (start us, length us, event | category | flops | bytes accessed | tf_op | source)
XLA Modules:
  0.0 155.9 jit_solution(17080526920122612063)
XLA Ops:
  0.7 1.6 %copy-done = f32[4096,128]{1,0:T(8,128)S(1)} copy-done((f32[4096,128]{1,0:T(8,128)S(1)}, f32[4096,128]{1,0:T(8,128)}, u32[]{:S(2)}) %copy-start) | copy-done | bytes 2097176
  3.9 1.7 %send.1 = f32[136,512]{1,0:T(8,128)S(1)} custom-call(s32[32,16,128]{2,1,0:T(8,128)S(1)} %copy-done.5, f32[4096,128]{1,0:T(8,128)S(1)} %copy-done, s32[1,512]{1,0:T(1,128)S(1)} %bitcast.10, s32[1,512]{1,0:T(1,128)S(1)} %bitcast.9), custom_call_target="tpu_custom_call" | custom-call | flops 1 | bytes 1 | tf_op jit(solution)/shard_map/send/pallas_call | solution.py:654
  5.6 4.7 %collective-permute-start = (f32[136,512]{1,0:T(8,128)S(1)}, f32[136,512]{1,0:T(8,128)S(1)}, u32[]{:S(2)}, u32[]{:S(2)}) collective-permute-start(f32[136,512]{1,0:T(8,128)S(1)} %send.1), channel_id=1, source_target_pairs={{0,0},{1,8},{2,16},{3,24},{4,4},{5,12},{6,20},{7,28},{8,2},{9,10},... | collective-permute-start | bytes 835592 | tf_op jit(solution)/shard_map/ppermute | solution.py:502
  10.6 3.3 %collective-permute-start.1 = (f32[80,512]{1,0:T(8,128)S(1)}, f32[80,512]{1,0:T(8,128)S(1)}, u32[]{:S(2)}, u32[]{:S(2)}) collective-permute-start(f32[80,512]{1,0:T(8,128)S(1)} %describe.1), channel_id=1, source_target_pairs={{0,0},{1,8},{2,16},{3,24},{4,4},{5,12},{6,20},{7,28},{8,2},{9,10},... | collective-permute-start | bytes 491528 | tf_op jit(solution)/shard_map/ppermute | solution.py:502
  13.9 16.9 %collective-permute-done.1 = f32[80,512]{1,0:T(8,128)S(1)} collective-permute-done((f32[80,512]{1,0:T(8,128)S(1)}, f32[80,512]{1,0:T(8,128)S(1)}, u32[]{:S(2)}, u32[]{:S(2)}) %collective-permute-start.1) | collective-permute-done | bytes 163872 | tf_op jit(solution)/shard_map/ppermute | solution.py:502
  32.4 2.7 %spread.1 = (f32[128,256]{1,0:T(8,128)S(1)}, f32[128,256]{1,0:T(8,128)S(1)}, f32[128,256]{1,0:T(8,128)S(1)}, f32[128,256]{1,0:T(8,128)S(1)}) custom-call(s32[6]{0:T(128)S(1)} %broadcast_multiply_fusion.first_ref, f32[136,512]{1,0:T(8,128)S(1)} %collective-permute-done.mine_ref, f32[136,512]{1,0:T(8,128)S(1)} %collective-permute-done.3.other_ref), custom_call_target="tpu_custom_call" | custom-call | flops 1 | bytes 1 | tf_op jit(solution)/shard_map/spread/pallas_call | solution.py:691
  40.2 3.7 %collective-permute-done.8 = f32[128,256]{1,0:T(8,128)S(1)} collective-permute-done((f32[128,256]{1,0:T(8,128)S(1)}, f32[128,256]{1,0:T(8,128)S(1)}, u32[]{:S(2)}, u32[]{:S(2)}) %collective-permute-start.8) | collective-permute-done | bytes 131104 | tf_op jit(solution)/shard_map/ppermute | solution.py:502
  44.6 3.5 %collective-permute-start.10 = (f32[256,256]{1,0:T(8,128)S(1)}, f32[256,256]{1,0:T(8,128)S(1)}, u32[]{:S(2)}, u32[]{:S(2)}) collective-permute-start(f32[256,256]{1,0:T(8,128)S(1)} %pad_maximum_fusion.here_ref), channel_id=1, source_target_pairs={{0,8},{1,9},{2,10},{3,11},{4,12},{5,13},{6,14},{7,15},{8,0},{9,1},... | collective-permute-start | bytes 786440 | tf_op jit(solution)/shard_map/ppermute | solution.py:502
  50.2 1.5 collective-permute-start.4
  51.7 4.6 %plane_couple.2.refs_2_ = f32[1024,512]{1,0:T(8,128)S(1)} custom-call(s32[6]{0:T(128)S(1)} %broadcast_multiply_fusion.first_ref, f32[24,1024]{1,0:T(8,128)S(1)} %maximum_maximum_fusion.refs_0_, f32[24,1024]{1,0:T(8,128)S(1)} %collective-permute-done.6.refs_1_), custom_call_target="tpu_custom_call" | custom-call | flops 2147483648 | bytes 2000000 | tf_op jit(solution)/shard_map/plane_couple/pallas_call | solution.py:758
  56.5 3.0 %plane_first.1.a_ref.pulled_ref.refs_4_ = f32[136,256]{1,0:T(8,128)S(1)} custom-call(f32[2]{0:T(128)S(1)} %add_convert_fusion.flag_ref, f32[256,256]{1,0:T(8,128)S(1)} %pad_maximum_fusion.here_ref, f32[256,256]{1,0:T(8,128)S(1)} %collective-permute-done.10.pair_ref, f32[256,256]{1,0:T(8,128)S(1)} %collective-permute-done.11.middle_ref, ...), custom_call_target="tpu_custom_call" | custom-call | flops 1 | bytes 1 | tf_op jit(solution)/shard_map/plane_first/pallas_call | solution.py:866
  62.2 4.9 %plane_couple.3 = (bf16[1024,512]{1,0:T(8,128)(2,1)S(1)}, bf16[1024,512]{1,0:T(8,128)(2,1)S(1)}) custom-call(s32[6]{0:T(128)S(1)} %broadcast_multiply_fusion.first_ref, f32[24,1024]{1,0:T(8,128)S(1)} %collective-permute-done.4.refs_0_, f32[24,1024]{1,0:T(8,128)S(1)} %collective-permute-done.5.refs_1_, f32[1024,512]{1,0:T(8,128)S(1)} %plane_couple.2.refs_2_), custom_call_target="tpu_custom_call" | custom-call | flops 2147483648 | bytes 2000000 | tf_op jit(solution)/shard_map/plane_couple/pallas_call | solution.py:758
  67.2 1.8 %plane_mix.3 = (f32[136,256]{1,0:T(8,128)S(1)}, f32[392,256]{1,0:T(8,128)S(1)}, f32[128,512]{1,0:T(8,128)S(1)}) custom-call(s32[6]{0:T(128)S(1)} %broadcast_multiply_fusion.first_ref, bf16[1024,512]{1,0:T(8,128)(2,1)S(1)} %get-tuple-element.44.high_ref, bf16[1024,512]{1,0:T(8,128)(2,1)S(1)} %get-tuple-element.45.low_ref, ...), custom_call_target="tpu_custom_call" | custom-call | flops 1 | bytes 1 | tf_op jit(solution)/shard_map/plane_mix/pallas_call | solution.py:803
  69.0 4.0 %collective-permute-start.15 = (f32[392,256]{1,0:T(8,128)S(1)}, f32[392,256]{1,0:T(8,128)S(1)}, u32[]{:S(2)}, u32[]{:S(2)}) collective-permute-start(f32[392,256]{1,0:T(8,128)S(1)} %get-tuple-element.50), channel_id=1, source_target_pairs={{0,1},{1,0},{2,3},{3,2},{4,5},{5,4},{6,7},{7,6},{8,9},{9,8},{10,11... | collective-permute-start | bytes 1204232 | tf_op jit(solution)/shard_map/ppermute | solution.py:502
  76.5 3.6 %collective-permute-done.16.pair_ref.refs_1_ = f32[136,256]{1,0:T(8,128)S(1)} collective-permute-done((f32[136,256]{1,0:T(8,128)S(1)}, f32[136,256]{1,0:T(8,128)S(1)}, u32[]{:S(2)}, u32[]{:S(2)}) %collective-permute-start.16) | collective-permute-done | bytes 139296 | tf_op jit(solution)/shard_map/ppermute | solution.py:502
  80.2 2.1 %plane_open.1 = (f32[136,256]{1,0:T(8,128)S(1)}, f32[128,256]{1,0:T(8,128)S(1)}) custom-call(f32[2]{0:T(128)S(1)} %add_convert_fusion.flag_ref, f32[136,256]{1,0:T(8,128)S(1)} %slice_add_fusion.2.here_ref.refs_0_, f32[136,256]{1,0:T(8,128)S(1)} %collective-permute-done.16.pair_ref.refs_1_, f32[136,256]{1,0:T(8,128)S(1)} %collective-permute-done.17.middle_ref.refs_2_, ...), custom_call_target="tpu_custom_call" | custom-call | flops 1 | bytes 1 | tf_op jit(solution)/shard_map/plane_open/pallas_call | solution.py:903
  85.0 2.3 %collective-permute-done.20.d_ref = f32[136,256]{1,0:T(8,128)S(1)} collective-permute-done((f32[136,256]{1,0:T(8,128)S(1)}, f32[136,256]{1,0:T(8,128)S(1)}, u32[]{:S(2)}, u32[]{:S(2)}) %collective-permute-start.20) | collective-permute-done | bytes 139296 | tf_op jit(solution)/shard_map/ppermute | solution.py:502
  87.3 3.9 %collective-permute-done.19.c_ref = f32[136,256]{1,0:T(8,128)S(1)} collective-permute-done((f32[136,256]{1,0:T(8,128)S(1)}, f32[136,256]{1,0:T(8,128)S(1)}, u32[]{:S(2)}, u32[]{:S(2)}) %collective-permute-start.19) | collective-permute-done | bytes 139296 | tf_op jit(solution)/shard_map/ppermute | solution.py:502
  91.2 1.8 %plane_mix.4 = (f32[136,256]{1,0:T(8,128)S(1)}, f32[392,256]{1,0:T(8,128)S(1)}, f32[128,512]{1,0:T(8,128)S(1)}) custom-call(s32[6]{0:T(128)S(1)} %broadcast_multiply_fusion.first_ref, bf16[1024,512]{1,0:T(8,128)(2,1)S(1)} %get-tuple-element.44.high_ref, bf16[1024,512]{1,0:T(8,128)(2,1)S(1)} %get-tuple-element.45.low_ref, ...), custom_call_target="tpu_custom_call" | custom-call | flops 1 | bytes 1 | tf_op jit(solution)/shard_map/plane_mix/pallas_call | solution.py:803
  96.0 3.4 %collective-permute-start.22 = (f32[136,256]{1,0:T(8,128)S(1)}, f32[136,256]{1,0:T(8,128)S(1)}, u32[]{:S(2)}, u32[]{:S(2)}) collective-permute-start(f32[136,256]{1,0:T(8,128)S(1)} %slice_add_fusion.1.here_ref), channel_id=1, source_target_pairs={{0,8},{1,9},{2,10},{3,11},{4,12},{5,13},{6,14},{7,15},{8,0},{9,1},... | collective-permute-start | bytes 417800 | tf_op jit(solution)/shard_map/ppermute | solution.py:502
  100.7 3.1 %collective-permute-done.25.mirror_ref = f32[8,256]{1,0:T(8,128)S(1)} collective-permute-done((f32[8,256]{1,0:T(8,128)S(1)}, f32[8,256]{1,0:T(8,128)S(1)}, u32[]{:S(2)}, u32[]{:S(2)}) %collective-permute-start.25) | collective-permute-done | bytes 8224 | tf_op jit(solution)/shard_map/ppermute | solution.py:502
  104.1 2.3 %plane_step.1 = (f32[8,256]{1,0:T(8,128)S(1)}, f32[136,256]{1,0:T(8,128)S(1)}, f32[768,256]{1,0:T(8,128)S(1)}) custom-call(f32[2]{0:T(128)S(1)} %add_convert_fusion.flag_ref, f32[136,256]{1,0:T(8,128)S(1)} %slice_add_fusion.1.here_ref, f32[136,256]{1,0:T(8,128)S(1)} %collective-permute-done.22.pair_ref, f32[136,256]{1,0:T(8,128)S(1)} %collective-permute-done.23.middle_ref, ...), custom_call_target="tpu_custom_call" | custom-call | flops 1 | bytes 1 | tf_op jit(solution)/shard_map/plane_step/pallas_call | solution.py:956
  109.1 2.3 %collective-permute-done.28.d_ref = f32[136,256]{1,0:T(8,128)S(1)} collective-permute-done((f32[136,256]{1,0:T(8,128)S(1)}, f32[136,256]{1,0:T(8,128)S(1)}, u32[]{:S(2)}, u32[]{:S(2)}) %collective-permute-start.28) | collective-permute-done | bytes 139296 | tf_op jit(solution)/shard_map/ppermute | solution.py:502
  111.4 1.8 %collective-permute-done.27.c_ref = f32[136,256]{1,0:T(8,128)S(1)} collective-permute-done((f32[136,256]{1,0:T(8,128)S(1)}, f32[136,256]{1,0:T(8,128)S(1)}, u32[]{:S(2)}, u32[]{:S(2)}) %collective-permute-start.27) | collective-permute-done | bytes 139296 | tf_op jit(solution)/shard_map/ppermute | solution.py:502
  113.2 1.8 %plane_mix.5 = (f32[136,256]{1,0:T(8,128)S(1)}, f32[392,256]{1,0:T(8,128)S(1)}, f32[128,512]{1,0:T(8,128)S(1)}) custom-call(s32[6]{0:T(128)S(1)} %broadcast_multiply_fusion.first_ref, bf16[1024,512]{1,0:T(8,128)(2,1)S(1)} %get-tuple-element.44.high_ref, bf16[1024,512]{1,0:T(8,128)(2,1)S(1)} %get-tuple-element.45.low_ref, ...), custom_call_target="tpu_custom_call" | custom-call | flops 1 | bytes 1 | tf_op jit(solution)/shard_map/plane_mix/pallas_call | solution.py:803
  115.0 3.3 %collective-permute-start.29 = (f32[392,256]{1,0:T(8,128)S(1)}, f32[392,256]{1,0:T(8,128)S(1)}, u32[]{:S(2)}, u32[]{:S(2)}) collective-permute-start(f32[392,256]{1,0:T(8,128)S(1)} %get-tuple-element.58), channel_id=1, source_target_pairs={{0,1},{1,0},{2,3},{3,2},{4,5},{5,4},{6,7},{7,6},{8,9},{9,8},{10,11... | collective-permute-start | bytes 1204232 | tf_op jit(solution)/shard_map/ppermute | solution.py:502
  120.3 2.5 %collective-permute-start.30 = (f32[136,256]{1,0:T(8,128)S(1)}, f32[136,256]{1,0:T(8,128)S(1)}, u32[]{:S(2)}, u32[]{:S(2)}) collective-permute-start(f32[136,256]{1,0:T(8,128)S(1)} %slice_add_fusion.here_ref), channel_id=1, source_target_pairs={{0,8},{1,9},{2,10},{3,11},{4,12},{5,13},{6,14},{7,15},{8,0},{9,1},... | collective-permute-start | bytes 417800 | tf_op jit(solution)/shard_map/ppermute | solution.py:502
  122.8 3.4 %collective-permute-done.30.pair_ref = f32[136,256]{1,0:T(8,128)S(1)} collective-permute-done((f32[136,256]{1,0:T(8,128)S(1)}, f32[136,256]{1,0:T(8,128)S(1)}, u32[]{:S(2)}, u32[]{:S(2)}) %collective-permute-start.30) | collective-permute-done | bytes 139296 | tf_op jit(solution)/shard_map/ppermute | solution.py:502
  127.5 11.9 %all_to_all.5.close_ref = f32[32,8,128]{2,1,0:T(8,128)S(1)} all-to-all(f32[32,8,128]{2,1,0:T(8,128)S(1)} %plane_close.1), channel_id=1, replica_groups=mesh['basin'=8,'tm'=4] {'basin','tm'}, dimensions={0} | all-to-all | bytes 262144 | tf_op jit(solution)/shard_map/all_to_all | solution.py:1160
  140.0 2.6 %collective-permute-start.32 = (f32[512,128]{1,0:T(8,128)S(1)}, f32[512,128]{1,0:T(8,128)S(1)}, u32[]{:S(2)}, u32[]{:S(2)}) collective-permute-start(f32[512,128]{1,0:T(8,128)S(1)} %plane_combine.1), channel_id=1, source_target_pairs={{0,0},{1,16},{2,8},{3,24},{4,4},{5,20},{6,12},{7,28},{8,1},{9,17},... | collective-permute-start | bytes 786440 | tf_op jit(solution)/shard_map/ppermute | solution.py:502
  142.6 10.7 %collective-permute-done.32.rows_ref = f32[512,128]{1,0:T(8,128)S(1)} collective-permute-done((f32[512,128]{1,0:T(8,128)S(1)}, f32[512,128]{1,0:T(8,128)S(1)}, u32[]{:S(2)}, u32[]{:S(2)}) %collective-permute-start.32) | collective-permute-done | bytes 262176 | tf_op jit(solution)/shard_map/ppermute | solution.py:502
  153.3 2.6 %plane_finish.1 = f32[4096,128]{1,0:T(8,128)} custom-call(f32[512,128]{1,0:T(8,128)S(1)} %collective-permute-done.32.rows_ref, s32[32,16,128]{2,1,0:T(8,128)S(1)} %copy-done.6, f32[4096,128]{1,0:T(8,128)S(1)} %copy-done.1), custom_call_target="tpu_custom_call" | custom-call | tf_op jit(solution)/shard_map/plane_finish/pallas_call | solution.py:1089
  (97 shorter events, 32.0 us)
Async XLA Ops:
  5.6 25.2 %collective-permute-start = (f32[136,512]{1,0:T(8,128)S(1)}, f32[136,512]{1,0:T(8,128)S(1)}, u32[]{:S(2)}, u32[]{:S(2)}) collective-permute-start(f32[136,512]{1,0:T(8,128)S(1)} %send.1), channel_id=1, source_target_pairs={{0,0},{1,8},{2,16},{3,24},{4,4},{5,12},{6,20},{7,28},{8,2},{9,10},... | collective-permute-start | bytes 835592 | tf_op jit(solution)/shard_map/ppermute | solution.py:502
  10.6 20.3 %collective-permute-start.1 = (f32[80,512]{1,0:T(8,128)S(1)}, f32[80,512]{1,0:T(8,128)S(1)}, u32[]{:S(2)}, u32[]{:S(2)}) collective-permute-start(f32[80,512]{1,0:T(8,128)S(1)} %describe.1), channel_id=1, source_target_pairs={{0,0},{1,8},{2,16},{3,24},{4,4},{5,12},{6,20},{7,28},{8,2},{9,10},... | collective-permute-start | bytes 491528 | tf_op jit(solution)/shard_map/ppermute | solution.py:502
  31.0 6.9 %collective-permute-start.2 = (f32[16,512]{1,0:T(8,128)S(1)}, f32[16,512]{1,0:T(8,128)S(1)}, u32[]{:S(2)}, u32[]{:S(2)}) collective-permute-start(f32[16,512]{1,0:T(8,128)S(1)} %slice.30), channel_id=1, source_target_pairs={{0,1},{1,0},{2,3},{3,2},{4,5},{5,4},{6,7},{7,6},{8,9},{9,8},{10,11... | collective-permute-start | bytes 98312 | tf_op jit(solution)/shard_map/ppermute | solution.py:502
  35.1 5.0 %collective-permute-start.7 = (f32[128,256]{1,0:T(8,128)S(1)}, f32[128,256]{1,0:T(8,128)S(1)}, u32[]{:S(2)}, u32[]{:S(2)}) collective-permute-start(f32[128,256]{1,0:T(8,128)S(1)} %get-tuple-element.40), channel_id=1, source_target_pairs={{0,4},{1,5},{2,6},{3,7},{4,0},{5,1},{6,2},{7,3},{8,12},{9,13},{10,... | collective-permute-start | bytes 393224 | tf_op jit(solution)/shard_map/ppermute | solution.py:502
  36.4 7.4 %collective-permute-start.8 = (f32[128,256]{1,0:T(8,128)S(1)}, f32[128,256]{1,0:T(8,128)S(1)}, u32[]{:S(2)}, u32[]{:S(2)}) collective-permute-start(f32[128,256]{1,0:T(8,128)S(1)} %get-tuple-element.41), channel_id=1, source_target_pairs={{0,2},{1,3},{2,0},{3,1},{4,6},{5,7},{6,4},{7,5},{8,10},{9,11},{10,... | collective-permute-start | bytes 393224 | tf_op jit(solution)/shard_map/ppermute | solution.py:502
  36.4 7.4 %collective-permute-start.9 = (f32[128,256]{1,0:T(8,128)S(1)}, f32[128,256]{1,0:T(8,128)S(1)}, u32[]{:S(2)}, u32[]{:S(2)}) collective-permute-start(f32[128,256]{1,0:T(8,128)S(1)} %get-tuple-element.42), channel_id=1, source_target_pairs={{0,6},{1,7},{2,4},{3,5},{4,2},{5,3},{6,0},{7,1},{8,14},{9,15},{10,... | collective-permute-start | bytes 393224 | tf_op jit(solution)/shard_map/ppermute | solution.py:502
  37.9 13.8 %collective-permute-start.6 = (f32[24,1024]{1,0:T(8,128)S(1)}, f32[24,1024]{1,0:T(8,128)S(1)}, u32[]{:S(2)}, u32[]{:S(2)}) collective-permute-start(f32[24,1024]{1,0:T(8,128)S(1)} %maximum_maximum_fusion.refs_0_), channel_id=1, source_target_pairs={{0,4},{1,5},{2,6},{3,7},{4,0},{5,1},{6,2},{7,3},{8,12},{9,13},{10,... | collective-permute-start | bytes 294920 | tf_op jit(solution)/shard_map/ppermute | solution.py:502
  44.0 12.4 %collective-permute-start.11 = (f32[256,256]{1,0:T(8,128)S(1)}, f32[256,256]{1,0:T(8,128)S(1)}, u32[]{:S(2)}, u32[]{:S(2)}) collective-permute-start(f32[256,256]{1,0:T(8,128)S(1)} %pad_maximum_fusion.here_ref), channel_id=1, source_target_pairs={{8,16},{9,17},{10,18},{11,19},{12,20},{13,21},{14,22},{15,23},{16,... | collective-permute-start | bytes 786440 | tf_op jit(solution)/shard_map/ppermute | solution.py:502
  44.6 11.8 %collective-permute-start.10 = (f32[256,256]{1,0:T(8,128)S(1)}, f32[256,256]{1,0:T(8,128)S(1)}, u32[]{:S(2)}, u32[]{:S(2)}) collective-permute-start(f32[256,256]{1,0:T(8,128)S(1)} %pad_maximum_fusion.here_ref), channel_id=1, source_target_pairs={{0,8},{1,9},{2,10},{3,11},{4,12},{5,13},{6,14},{7,15},{8,0},{9,1},... | collective-permute-start | bytes 786440 | tf_op jit(solution)/shard_map/ppermute | solution.py:502
  49.0 13.2 %collective-permute-start.5 = (f32[24,1024]{1,0:T(8,128)S(1)}, f32[24,1024]{1,0:T(8,128)S(1)}, u32[]{:S(2)}, u32[]{:S(2)}) collective-permute-start(f32[24,1024]{1,0:T(8,128)S(1)} %maximum_maximum_fusion.refs_0_), channel_id=1, source_target_pairs={{0,6},{1,7},{2,4},{3,5},{4,2},{5,3},{6,0},{7,1},{8,14},{9,15},{10,... | collective-permute-start | bytes 294920 | tf_op jit(solution)/shard_map/ppermute | solution.py:502
  50.2 12.0 %collective-permute-start.4 = (f32[24,1024]{1,0:T(8,128)S(1)}, f32[24,1024]{1,0:T(8,128)S(1)}, u32[]{:S(2)}, u32[]{:S(2)}) collective-permute-start(f32[24,1024]{1,0:T(8,128)S(1)} %maximum_maximum_fusion.refs_0_), channel_id=1, source_target_pairs={{0,2},{1,3},{2,0},{3,1},{4,6},{5,7},{6,4},{7,5},{8,10},{9,11},{10,... | collective-permute-start | bytes 294920 | tf_op jit(solution)/shard_map/ppermute | solution.py:502
  59.5 7.7 %collective-permute-start.14 = (f32[136,256]{1,0:T(8,128)S(1)}, f32[136,256]{1,0:T(8,128)S(1)}, u32[]{:S(2)}, u32[]{:S(2)}) collective-permute-start(f32[136,256]{1,0:T(8,128)S(1)} %plane_first.1.a_ref.pulled_ref.refs_4_), channel_id=1, source_target_pairs={{0,6},{1,7},{2,4},{3,5},{4,2},{5,3},{6,0},{7,1},{8,14},{9,15},{10,... | collective-permute-start | bytes 417800 | tf_op jit(solution)/shard_map/ppermute | solution.py:502
  60.6 6.6 %collective-permute-start.13 = (f32[136,256]{1,0:T(8,128)S(1)}, f32[136,256]{1,0:T(8,128)S(1)}, u32[]{:S(2)}, u32[]{:S(2)}) collective-permute-start(f32[136,256]{1,0:T(8,128)S(1)} %plane_first.1.a_ref.pulled_ref.refs_4_), channel_id=1, source_target_pairs={{0,2},{1,3},{2,0},{3,1},{4,6},{5,7},{6,4},{7,5},{8,10},{9,11},{10,... | collective-permute-start | bytes 417800 | tf_op jit(solution)/shard_map/ppermute | solution.py:502
  60.8 6.4 %collective-permute-start.12 = (f32[136,256]{1,0:T(8,128)S(1)}, f32[136,256]{1,0:T(8,128)S(1)}, u32[]{:S(2)}, u32[]{:S(2)}) collective-permute-start(f32[136,256]{1,0:T(8,128)S(1)} %plane_first.1.a_ref.pulled_ref.refs_4_), channel_id=1, source_target_pairs={{0,4},{1,5},{2,6},{3,7},{4,0},{5,1},{6,2},{7,3},{8,12},{9,13},{10,... | collective-permute-start | bytes 417800 | tf_op jit(solution)/shard_map/ppermute | solution.py:502
  69.0 5.4 %collective-permute-start.15 = (f32[392,256]{1,0:T(8,128)S(1)}, f32[392,256]{1,0:T(8,128)S(1)}, u32[]{:S(2)}, u32[]{:S(2)}) collective-permute-start(f32[392,256]{1,0:T(8,128)S(1)} %get-tuple-element.50), channel_id=1, source_target_pairs={{0,1},{1,0},{2,3},{3,2},{4,5},{5,4},{6,7},{7,6},{8,9},{9,8},{10,11... | collective-permute-start | bytes 1204232 | tf_op jit(solution)/shard_map/ppermute | solution.py:502
  74.3 2.2 %collective-permute-start.17 = (f32[136,256]{1,0:T(8,128)S(1)}, f32[136,256]{1,0:T(8,128)S(1)}, u32[]{:S(2)}, u32[]{:S(2)}) collective-permute-start(f32[136,256]{1,0:T(8,128)S(1)} %slice_add_fusion.2.here_ref.refs_0_), channel_id=1, source_target_pairs={{8,16},{9,17},{10,18},{11,19},{12,20},{13,21},{14,22},{15,23},{16,... | collective-permute-start | bytes 417800 | tf_op jit(solution)/shard_map/ppermute | solution.py:502
  75.2 5.0 %collective-permute-start.16 = (f32[136,256]{1,0:T(8,128)S(1)}, f32[136,256]{1,0:T(8,128)S(1)}, u32[]{:S(2)}, u32[]{:S(2)}) collective-permute-start(f32[136,256]{1,0:T(8,128)S(1)} %slice_add_fusion.2.here_ref.refs_0_), channel_id=1, source_target_pairs={{0,8},{1,9},{2,10},{3,11},{4,12},{5,13},{6,14},{7,15},{8,0},{9,1},... | collective-permute-start | bytes 417800 | tf_op jit(solution)/shard_map/ppermute | solution.py:502
  82.3 5.0 %collective-permute-start.20 = (f32[136,256]{1,0:T(8,128)S(1)}, f32[136,256]{1,0:T(8,128)S(1)}, u32[]{:S(2)}, u32[]{:S(2)}) collective-permute-start(f32[136,256]{1,0:T(8,128)S(1)} %get-tuple-element.51.a_ref.refs_3_), channel_id=1, source_target_pairs={{0,6},{1,7},{2,4},{3,5},{4,2},{5,3},{6,0},{7,1},{8,14},{9,15},{10,... | collective-permute-start | bytes 417800 | tf_op jit(solution)/shard_map/ppermute | solution.py:502
  83.0 8.2 %collective-permute-start.19 = (f32[136,256]{1,0:T(8,128)S(1)}, f32[136,256]{1,0:T(8,128)S(1)}, u32[]{:S(2)}, u32[]{:S(2)}) collective-permute-start(f32[136,256]{1,0:T(8,128)S(1)} %get-tuple-element.51.a_ref.refs_3_), channel_id=1, source_target_pairs={{0,2},{1,3},{2,0},{3,1},{4,6},{5,7},{6,4},{7,5},{8,10},{9,11},{10,... | collective-permute-start | bytes 417800 | tf_op jit(solution)/shard_map/ppermute | solution.py:502
  84.0 7.2 %collective-permute-start.18 = (f32[136,256]{1,0:T(8,128)S(1)}, f32[136,256]{1,0:T(8,128)S(1)}, u32[]{:S(2)}, u32[]{:S(2)}) collective-permute-start(f32[136,256]{1,0:T(8,128)S(1)} %get-tuple-element.51.a_ref.refs_3_), channel_id=1, source_target_pairs={{0,4},{1,5},{2,6},{3,7},{4,0},{5,1},{6,2},{7,3},{8,12},{9,13},{10,... | collective-permute-start | bytes 417800 | tf_op jit(solution)/shard_map/ppermute | solution.py:502
  93.0 2.4 %collective-permute-start.21 = (f32[392,256]{1,0:T(8,128)S(1)}, f32[392,256]{1,0:T(8,128)S(1)}, u32[]{:S(2)}, u32[]{:S(2)}) collective-permute-start(f32[392,256]{1,0:T(8,128)S(1)} %get-tuple-element.53), channel_id=1, source_target_pairs={{0,1},{1,0},{2,3},{3,2},{4,5},{5,4},{6,7},{7,6},{8,9},{9,8},{10,11... | collective-permute-start | bytes 1204232 | tf_op jit(solution)/shard_map/ppermute | solution.py:502
  95.4 8.7 %collective-permute-start.23 = (f32[136,256]{1,0:T(8,128)S(1)}, f32[136,256]{1,0:T(8,128)S(1)}, u32[]{:S(2)}, u32[]{:S(2)}) collective-permute-start(f32[136,256]{1,0:T(8,128)S(1)} %slice_add_fusion.1.here_ref), channel_id=1, source_target_pairs={{8,16},{9,17},{10,18},{11,19},{12,20},{13,21},{14,22},{15,23},{16,... | collective-permute-start | bytes 417800 | tf_op jit(solution)/shard_map/ppermute | solution.py:502
  96.0 8.0 %collective-permute-start.22 = (f32[136,256]{1,0:T(8,128)S(1)}, f32[136,256]{1,0:T(8,128)S(1)}, u32[]{:S(2)}, u32[]{:S(2)}) collective-permute-start(f32[136,256]{1,0:T(8,128)S(1)} %slice_add_fusion.1.here_ref), channel_id=1, source_target_pairs={{0,8},{1,9},{2,10},{3,11},{4,12},{5,13},{6,14},{7,15},{8,0},{9,1},... | collective-permute-start | bytes 417800 | tf_op jit(solution)/shard_map/ppermute | solution.py:502
  99.5 4.4 %collective-permute-start.25 = (f32[8,256]{1,0:T(8,128)S(1)}, f32[8,256]{1,0:T(8,128)S(1)}, u32[]{:S(2)}, u32[]{:S(2)}) collective-permute-start(f32[8,256]{1,0:T(8,128)S(1)} %slice.42), channel_id=1, source_target_pairs={{0,24},{1,25},{2,26},{3,27},{4,28},{5,29},{6,30},{7,31},{8,16},{9,... | collective-permute-start | bytes 24584 | tf_op jit(solution)/shard_map/ppermute | solution.py:502
  100.6 3.4 %collective-permute-start.24 = (f32[8,256]{1,0:T(8,128)S(1)}, f32[8,256]{1,0:T(8,128)S(1)}, u32[]{:S(2)}, u32[]{:S(2)}) collective-permute-start(f32[8,256]{1,0:T(8,128)S(1)} %slice.42), channel_id=1, source_target_pairs={{0,16},{1,17},{2,18},{3,19},{4,20},{5,21},{6,22},{7,23},{8,24},{9,... | collective-permute-start | bytes 24584 | tf_op jit(solution)/shard_map/ppermute | solution.py:502
  106.4 5.0 %collective-permute-start.28 = (f32[136,256]{1,0:T(8,128)S(1)}, f32[136,256]{1,0:T(8,128)S(1)}, u32[]{:S(2)}, u32[]{:S(2)}) collective-permute-start(f32[136,256]{1,0:T(8,128)S(1)} %get-tuple-element.56.a_ref.pulled_ref), channel_id=1, source_target_pairs={{0,6},{1,7},{2,4},{3,5},{4,2},{5,3},{6,0},{7,1},{8,14},{9,15},{10,... | collective-permute-start | bytes 417800 | tf_op jit(solution)/shard_map/ppermute | solution.py:502
  107.4 5.8 %collective-permute-start.27 = (f32[136,256]{1,0:T(8,128)S(1)}, f32[136,256]{1,0:T(8,128)S(1)}, u32[]{:S(2)}, u32[]{:S(2)}) collective-permute-start(f32[136,256]{1,0:T(8,128)S(1)} %get-tuple-element.56.a_ref.pulled_ref), channel_id=1, source_target_pairs={{0,2},{1,3},{2,0},{3,1},{4,6},{5,7},{6,4},{7,5},{8,10},{9,11},{10,... | collective-permute-start | bytes 417800 | tf_op jit(solution)/shard_map/ppermute | solution.py:502
  108.2 5.0 %collective-permute-start.26 = (f32[136,256]{1,0:T(8,128)S(1)}, f32[136,256]{1,0:T(8,128)S(1)}, u32[]{:S(2)}, u32[]{:S(2)}) collective-permute-start(f32[136,256]{1,0:T(8,128)S(1)} %get-tuple-element.56.a_ref.pulled_ref), channel_id=1, source_target_pairs={{0,4},{1,5},{2,6},{3,7},{4,0},{5,1},{6,2},{7,3},{8,12},{9,13},{10,... | collective-permute-start | bytes 417800 | tf_op jit(solution)/shard_map/ppermute | solution.py:502
  115.0 4.7 %collective-permute-start.29 = (f32[392,256]{1,0:T(8,128)S(1)}, f32[392,256]{1,0:T(8,128)S(1)}, u32[]{:S(2)}, u32[]{:S(2)}) collective-permute-start(f32[392,256]{1,0:T(8,128)S(1)} %get-tuple-element.58), channel_id=1, source_target_pairs={{0,1},{1,0},{2,3},{3,2},{4,5},{5,4},{6,7},{7,6},{8,9},{9,8},{10,11... | collective-permute-start | bytes 1204232 | tf_op jit(solution)/shard_map/ppermute | solution.py:502
  119.7 3.2 %collective-permute-start.31 = (f32[136,256]{1,0:T(8,128)S(1)}, f32[136,256]{1,0:T(8,128)S(1)}, u32[]{:S(2)}, u32[]{:S(2)}) collective-permute-start(f32[136,256]{1,0:T(8,128)S(1)} %slice_add_fusion.here_ref), channel_id=1, source_target_pairs={{8,16},{9,17},{10,18},{11,19},{12,20},{13,21},{14,22},{15,23},{16,... | collective-permute-start | bytes 417800 | tf_op jit(solution)/shard_map/ppermute | solution.py:502
  120.3 5.9 %collective-permute-start.30 = (f32[136,256]{1,0:T(8,128)S(1)}, f32[136,256]{1,0:T(8,128)S(1)}, u32[]{:S(2)}, u32[]{:S(2)}) collective-permute-start(f32[136,256]{1,0:T(8,128)S(1)} %slice_add_fusion.here_ref), channel_id=1, source_target_pairs={{0,8},{1,9},{2,10},{3,11},{4,12},{5,13},{6,14},{7,15},{8,0},{9,1},... | collective-permute-start | bytes 417800 | tf_op jit(solution)/shard_map/ppermute | solution.py:502
  140.0 13.3 %collective-permute-start.32 = (f32[512,128]{1,0:T(8,128)S(1)}, f32[512,128]{1,0:T(8,128)S(1)}, u32[]{:S(2)}, u32[]{:S(2)}) collective-permute-start(f32[512,128]{1,0:T(8,128)S(1)} %plane_combine.1), channel_id=1, source_target_pairs={{0,0},{1,16},{2,8},{3,24},{4,4},{5,20},{6,12},{7,28},{8,1},{9,17},... | collective-permute-start | bytes 786440 | tf_op jit(solution)/shard_map/ppermute | solution.py:502
  (17 other events, 280.6 us)

commit v8 on v7

--- a/solution.py
+++ b/solution.py
@@ -598,74 +598,70 @@
     return product(first, turn(waves, spec, -1.0), order)
 
 
-def describe_kernel(inc_ref, seen_ref, out_ref):
+def describe_kernel(inc_ref, gauge_ref, kind_ref, out_ref):
     blocks, slots, width = inc_ref.shape
-    rows, hours = seen_ref.shape
-    count = blocks * slots
     tile = 8
-    side = tile * slots
+    rows = tile * slots
     weights = inc_ref[...].astype(F32).astype(BF16)
-    row = lax.broadcasted_iota(jnp.int32, (side, side), 0)
-    col = lax.broadcasted_iota(jnp.int32, (side, side), 1)
+    row = lax.broadcasted_iota(jnp.int32, (rows, rows), 0)
+    col = lax.broadcasted_iota(jnp.int32, (rows, rows), 1)
     same = row // slots == col // slots
     for i in range(blocks // tile):
-        flat = weights[i * tile : (i + 1) * tile].reshape(side, width)
+        flat = weights[i * tile : (i + 1) * tile].reshape(rows, width)
         full = lax.dot_general(flat, flat, (((1,), (1,)), ((), ())), preferred_element_type=F32)
         own = jnp.where(same, full, 0.0)
-        out_ref[pl.ds(0, slots), pl.ds(i * side, side)] = jnp.sum(own.reshape(tile, slots, side), axis=0)
-    turned = jnp.transpose(seen_ref[...])
-    step = hours * rows // count
-    for i in range(count // rows):
-        out_ref[pl.ds(slots, step), pl.ds(i * rows, rows)] = turned[i * step : (i + 1) * step]
-
-
-def describe(incidence, observed):
+        out_ref[pl.ds(0, slots), pl.ds(i * rows, rows)] = jnp.sum(own.reshape(tile, slots, rows), axis=0)
+    kinds = kind_ref.shape[1]
+    out_ref[pl.ds(slots, 8), :] = jnp.concatenate(
+        [
+            gauge_ref[...].astype(F32),
+            jnp.concatenate(
+                [kind_ref[...].astype(F32), jnp.zeros((1, blocks * slots - kinds), F32)], axis=1
+            ),
+            jnp.zeros((6, blocks * slots), F32),
+        ],
+        axis=0,
+    )
+
+
+def describe(incidence, row_gauge, gauge_kernel):
     blocks, slots, _ = incidence.shape
-    rows, hours = observed.shape
     count = blocks * slots
     return pl.pallas_call(
         describe_kernel,
-        out_shape=jax.ShapeDtypeStruct((slots + hours * rows // count, count), F32),
+        out_shape=jax.ShapeDtypeStruct((slots + 8, count), F32),
         compiler_params=params(),
         name="describe",
         cost_estimate=SMALL,
-    )(incidence, observed)
-
-
-def send_kernel(inc_ref, field_ref, gauge_ref, kind_ref, out_ref):
+    )(incidence, row_gauge.reshape(1, count), gauge_kernel.reshape(1, gauge_kernel.shape[0]))
+
+
+def send_kernel(inc_ref, field_ref, out_ref):
     blocks, slots, width = inc_ref.shape
-    hours = field_ref.shape[1]
     weights = inc_ref[...].astype(F32).astype(BF16)
     parts = []
     for b in range(blocks):
         parts.append(pick(weights[b], field_ref[pl.ds(b * width, width), :]))
-    out_ref[pl.ds(0, hours), :] = jnp.transpose(jnp.concatenate(parts, axis=0))
-    out_ref[pl.ds(hours, 8), :] = jnp.concatenate(
-        [gauge_ref[...].astype(F32), kind_ref[...].astype(F32), jnp.zeros((6, blocks * slots), F32)], axis=0
-    )
-
-
-def send(incidence, field, row_gauge, gauge_kernel):
+    out_ref[...] = jnp.transpose(jnp.concatenate(parts, axis=0))
+
+
+def send(incidence, field):
     blocks, slots, width = incidence.shape
-    count = blocks * slots
     hours = field.shape[1]
     step = 8
-    kinds = jnp.pad(gauge_kernel, (0, count - gauge_kernel.shape[0]))
     return pl.pallas_call(
         send_kernel,
         grid=(blocks // step,),
         in_specs=[
             pl.BlockSpec((step, slots, width), lambda i: (i, 0, 0)),
             pl.BlockSpec((step * width, hours), lambda i: (i, 0)),
-            pl.BlockSpec((1, step * slots), lambda i: (0, i)),
-            pl.BlockSpec((1, step * slots), lambda i: (0, i)),
-        ],
-        out_specs=pl.BlockSpec((hours + 8, step * slots), lambda i: (0, i)),
-        out_shape=jax.ShapeDtypeStruct((hours + 8, count), F32),
+        ],
+        out_specs=pl.BlockSpec((hours, step * slots), lambda i: (0, i)),
+        out_shape=jax.ShapeDtypeStruct((hours, blocks * slots), F32),
         compiler_params=params(),
         name="send",
         cost_estimate=SMALL,
-    )(incidence, field, row_gauge.reshape(1, count), kinds.reshape(1, count))
+    )(incidence, field)
 
 
 def hot_rows(gauge, first, rows):
@@ -673,13 +669,14 @@
     return jnp.where(gauge == mine, 1.0, 0.0).astype(BF16)
 
 
-def spread_kernel(first_ref, mine_ref, other_ref, *out_refs):
-    hours, rows = out_refs[0].shape
+def spread_kernel(first_ref, mine_ref, other_ref, meta_ref, meta_other_ref, *out_refs):
+    rows = out_refs[0].shape[1]
+    where = meta_ref.shape[0] - 8
     for m, out_ref in enumerate(out_refs):
         result = None
-        for ref in (mine_ref, other_ref):
-            hot = hot_rows(ref[hours : hours + 1, :], first_ref[m], rows)
-            for piece in reversed(pieces(ref[pl.ds(0, hours), :], 3)):
+        for ref, meta in ((mine_ref, meta_ref), (other_ref, meta_other_ref)):
+            hot = hot_rows(meta[where : where + 1, :], first_ref[m], rows)
+            for piece in reversed(pieces(ref[...], 3)):
                 term = lax.dot_general(
                     piece, hot, (((1,), (1,)), ((), ())), preferred_element_type=F32
                 )
@@ -687,15 +684,16 @@
         out_ref[...] = result
 
 
-def spread(first, parcels, hours, rows):
+def spread(first, parcels, metas, rows):
+    hours = parcels[0].shape[0]
     return pl.pallas_call(
         spread_kernel,
-        in_specs=[pl.BlockSpec(memory_space=pltpu.SMEM)] + [pl.BlockSpec(memory_space=pltpu.VMEM)] * 2,
+        in_specs=[pl.BlockSpec(memory_space=pltpu.SMEM)] + [pl.BlockSpec(memory_space=pltpu.VMEM)] * 4,
         out_shape=[jax.ShapeDtypeStruct((hours, rows), F32)] * 4,
         compiler_params=params(),
         name="spread",
         cost_estimate=SMALL,
-    )(first, *parcels)
+    )(first, *parcels, *metas)
 
 
 def plane_couple_kernel(last, first_ref, *refs):
@@ -785,8 +783,9 @@
     other_ref[body, :] = result[:, rows:]
     mine_ref[tail, :] = note
     other_ref[tail, :] = note
+    where = meta_ref.shape[0] - 8
     for ref in (meta_ref, meta_other_ref):
-        gauge = ref[0:1, :]
+        gauge = ref[where : where + 1, :]
         hot = jnp.concatenate([hot_rows(gauge, first_ref[m], rows) for m in range(4)], axis=0)
         picked = dot(two, hot) + dot(one, hot)
         if ref is meta_ref:
@@ -816,7 +815,7 @@
 
 def plane_spectrum_kernel(class_ref, kernels_ref, f0_ref, f1_ref, f2_ref, out_ref):
     classes, taps = kernels_ref.shape
-    kind = class_ref[1:2, : out_ref.shape[1]]
+    kind = class_ref[class_ref.shape[0] - 7 : class_ref.shape[0] - 6, : out_ref.shape[1]]
     hot = jnp.where(
         lax.broadcasted_iota(jnp.int32, (classes, kind.shape[1]), 0).astype(F32) == kind, 1.0, 0.0
     ).astype(BF16)
@@ -842,32 +841,29 @@
     return jnp.where(even, middle, pair), jnp.where(even, pair, middle)
 
 
-def plane_first_kernel(flag_ref, here_ref, pair_ref, middle_ref, spec_ref, *refs):
+def plane_first_kernel(flag_ref, here_ref, pair_ref, middle_ref, seen_ref, seen_later_ref, spec_ref, *refs):
     *mats, out_ref = refs
     forward, first, last = mats[0:3], mats[3:6], mats[6:9]
-    rows = here_ref.shape[1]
-    hours = here_ref.shape[0] // 2
+    hours, rows = here_ref.shape
     spec = spec_ref[...]
     before, after = sides(flag_ref[0] > 0.5, pair_ref[...], middle_ref[...])
-    now, later = plane_delayed(
-        before[:hours], here_ref[pl.ds(0, hours), :], after[:hours], spec, forward, last, 3
-    )
-    start = here_ref[pl.ds(hours, hours), :] - now
-    start_later = (after[hours:] - later) * flag_ref[1]
+    now, later = plane_delayed(before, here_ref[...], after, spec, forward, last, 3)
+    start = jnp.transpose(seen_ref[...]) - now
+    start_later = (jnp.transpose(seen_later_ref[...]) - later) * flag_ref[1]
     out_ref[pl.ds(0, hours), :] = plane_advanced(start, start_later, spec, forward, first, 3)
     out_ref[pl.ds(hours, NOTE), :] = jnp.concatenate(
         [lanes(start, start), jnp.zeros((NOTE - 1, rows), F32)], axis=0
     )
 
 
-def plane_first(flags, sums, spec, mats):
-    double, rows = sums[0].shape
-    args = [flags, *sums, spec, *mats]
+def plane_first(flags, sums, seen, seen_later, spec, mats):
+    hours, rows = sums[0].shape
+    args = [flags, *sums, seen, seen_later, spec, *mats]
     return pl.pallas_call(
         plane_first_kernel,
         in_specs=[pl.BlockSpec(memory_space=pltpu.SMEM)]
         + [pl.BlockSpec(memory_space=pltpu.VMEM)] * (len(args) - 1),
-        out_shape=jax.ShapeDtypeStruct((double // 2 + NOTE, rows), F32),
+        out_shape=jax.ShapeDtypeStruct((hours + NOTE, rows), F32),
         compiler_params=params(),
         name="plane_first",
         cost_estimate=SMALL,
@@ -1112,29 +1108,25 @@
     forward, inverse_first, inverse_last = turned_transforms()
     mats = [*forward, *inverse_first, *inverse_last]
 
-    parcel = send(incidence, first_guess, row_gauge, gauge_kernel)
-    incidence_, seen, parcel = lax.optimization_barrier((incidence, observed, parcel))
-    parcel = moved(parcel, to_plane)
-    behind = moved(describe(incidence_, seen), to_plane)
-    parcel, behind = lax.optimization_barrier((parcel, behind))
-    parcels = [parcel, moved(parcel, over_core)]
-    metas = [value[hours:] for value in parcels]
-    spec = plane_spectrum(metas[0], kernels, forward, rows)
-    dense = spread(first, parcels, hours, rows)
+    meta = describe(incidence, row_gauge, gauge_kernel)
+    meta, field = lax.optimization_barrier((meta, first_guess))
+    meta = moved(meta, to_plane)
+    parcel = moved(send(incidence, field), to_plane)
+    metas = [meta, moved(meta, over_core)]
+    both = jnp.concatenate(metas, axis=1)
+    around = [both] + [moved(both, where) for where in SQUARE]
+    spec = plane_spectrum(meta, kernels, forward, rows)
+    seen, parcel, around, spec = lax.optimization_barrier((observed, parcel, around, spec))
+    seen_later = moved(seen, to_plane_before)
+    seen = moved(seen, to_plane)
+
+    dense = spread(first, [parcel, moved(parcel, over_core)], metas, rows)
     sums = dense[0] + sum(moved(value, where) for value, where in zip(dense[1:], SQUARE))
-
-    slots = incidence.shape[1]
-    gram, seen = behind[:slots], behind[slots:]
-    seen = [seen[:, i : i + rows] for i in range(0, seen.shape[1], rows)]
-    sums = jnp.concatenate([sums, *seen], axis=0)
     sums = [sums, moved(sums, z_pair), moved(sums, z_middle)]
-    both = jnp.concatenate([gram, moved(gram, over_core)], axis=1)
-    both = jnp.concatenate([both, jnp.concatenate(metas, axis=1)], axis=0)
-    around = [both] + [moved(both, where) for where in SQUARE]
     coupled = plane_couple(first, around[:2], rows)
     coupled, sums = lax.optimization_barrier((coupled, sums))
     coupling = plane_couple(first, around[2:], rows, coupled)
-    pulled = [plane_first(flags, sums, spec, mats)]
+    pulled = [plane_first(flags, sums, seen, seen_later, spec, mats)]
 
     slot_rows, slot_rows_other, mixes = [], [], []
     for k in range(3):

time: 156 us -> 152 us (0.974)
  waiting for transfers between devices: 58 us -> 49.9 us
  starting transfers between devices: 49.3 us -> 52.4 us
    ppermute x33 -> x35, waiting for transfers between devices: 58 us -> 49.9 us  [moved(): return lax.ppermute(value, ('basin', 'tm'), pairs)]
    ppermute x33 -> x35, starting transfers between devices: 49.3 us -> 52.4 us  [moved(): return lax.ppermute(value, ('basin', 'tm'), pairs)]
    unnamed x32 -> x35, local copies, waits for them, and re-layouts: 3.3 us -> 4.01 us
  transfers between devices with their start and end apart: 33 -> 35, of which waited for: 16 -> 21; matrix products, arithmetic and copies ran while one was open for 0% -> 0% of each run, Pallas kernels for 10% -> 7%
where the time goes in v8:
time: 152 us; the launch traced here: 151 us
  starting transfers between devices  52.4 us (34%)
  waiting for transfers between devices  49.9 us (33%)
  Pallas kernels  32 us (21%)
  blocking collectives  12.2 us (8%)
  local copies, waits for them, and re-layouts  4.1 us (3%)
    ppermute x35, starting transfers between devices, moved(): return lax.ppermute(value, ('basin', 'tm'), pairs)  52.4 us
    ppermute x35, waiting for transfers between devices, moved(): return lax.ppermute(value, ('basin', 'tm'), pairs)  49.9 us
    all_to_all x1, blocking collectives, plane_shards(): close_note = lax.all_to_all(note, ('basin', 'tm'), 0, 0, tiled=False)  12.2 us
    pallas_call x2, Pallas kernels, plane_couple(): pl.pallas_call(functools.partial(plane_couple_kernel, last), in_specs=[pl...  9.56 us
    pallas_call x3, Pallas kernels, plane_mix(): pl.pallas_call(plane_mix_kernel, in_specs=[pl.BlockSpec(memory_space=pltp...  5.3 us
    unnamed x35, local copies, waits for them, and re-layouts  4.01 us
  transfers between devices with their start and end apart: 35, of which 21 were waited for; matrix products, arithmetic and copies ran while one was open for 0% of the time, Pallas kernels for 7%

profile of v8, /device:TPU:1, one launch (start us, length us, event | category | flops | bytes accessed | tf_op | source)
XLA Modules:
  0.0 151.2 jit_solution(12784780446146224957)
XLA Ops:
  2.6 4.6 %collective-permute-start.1 = (f32[24,512]{1,0:T(8,128)S(1)}, f32[24,512]{1,0:T(8,128)S(1)}, u32[]{:S(2)}, u32[]{:S(2)}) collective-permute-start(f32[24,512]{1,0:T(8,128)S(1)} %describe.1), channel_id=1, source_target_pairs={{0,0},{1,8},{2,16},{3,24},{4,4},{5,12},{6,20},{7,28},{8,2},{9,10},... | collective-permute-start | bytes 147464 | tf_op jit(solution)/shard_map/ppermute | solution.py:502
  10.5 3.3 %collective-permute-start = (f32[128,512]{1,0:T(8,128)S(1)}, f32[128,512]{1,0:T(8,128)S(1)}, u32[]{:S(2)}, u32[]{:S(2)}) collective-permute-start(f32[128,512]{1,0:T(8,128)S(1)} %send.1), channel_id=1, source_target_pairs={{0,0},{1,8},{2,16},{3,24},{4,4},{5,12},{6,20},{7,28},{8,2},{9,10},... | collective-permute-start | bytes 786440 | tf_op jit(solution)/shard_map/ppermute | solution.py:502
  15.1 3.3 %collective-permute-start.5 = (f32[24,1024]{1,0:T(8,128)S(1)}, f32[24,1024]{1,0:T(8,128)S(1)}, u32[]{:S(2)}, u32[]{:S(2)}) collective-permute-start(f32[24,1024]{1,0:T(8,128)S(1)} %constant_dynamic-update-slice_fusion.refs_0_), channel_id=1, source_target_pairs={{0,6},{1,7},{2,4},{3,5},{4,2},{5,3},{6,0},{7,1},{8,14},{9,15},{10,... | collective-permute-start | bytes 294920 | tf_op jit(solution)/shard_map/ppermute | solution.py:502
  19.5 2.0 %collective-permute-done.5.refs_1_ = f32[24,1024]{1,0:T(8,128)S(1)} collective-permute-done((f32[24,1024]{1,0:T(8,128)S(1)}, f32[24,1024]{1,0:T(8,128)S(1)}, u32[]{:S(2)}, u32[]{:S(2)}) %collective-permute-start.5) | collective-permute-done | bytes 98336 | tf_op jit(solution)/shard_map/ppermute | solution.py:502
  21.4 5.7 %collective-permute-done.4.refs_0_ = f32[24,1024]{1,0:T(8,128)S(1)} collective-permute-done((f32[24,1024]{1,0:T(8,128)S(1)}, f32[24,1024]{1,0:T(8,128)S(1)}, u32[]{:S(2)}, u32[]{:S(2)}) %collective-permute-start.4) | collective-permute-done | bytes 98336 | tf_op jit(solution)/shard_map/ppermute | solution.py:502
  29.1 2.7 %spread.1 = (f32[128,256]{1,0:T(8,128)S(1)}, f32[128,256]{1,0:T(8,128)S(1)}, f32[128,256]{1,0:T(8,128)S(1)}, f32[128,256]{1,0:T(8,128)S(1)}) custom-call(s32[6]{0:T(128)S(1)} %broadcast_multiply_fusion.first_ref, f32[128,512]{1,0:T(8,128)S(1)} %collective-permute-done.mine_ref, f32[128,512]{1,0:T(8,128)S(1)} %collective-permute-done.6.other_ref, ...), custom_call_target="tpu_custom_call" | custom-call | flops 1 | bytes 1 | tf_op jit(solution)/shard_map/spread/pallas_call | solution.py:689
  33.0 1.9 %collective-permute-start.8 = (f32[128,256]{1,0:T(8,128)S(1)}, f32[128,256]{1,0:T(8,128)S(1)}, u32[]{:S(2)}, u32[]{:S(2)}) collective-permute-start(f32[128,256]{1,0:T(8,128)S(1)} %get-tuple-element.47), channel_id=1, source_target_pairs={{0,2},{1,3},{2,0},{3,1},{4,6},{5,7},{6,4},{7,5},{8,10},{9,11},{10,... | collective-permute-start | bytes 393224 | tf_op jit(solution)/shard_map/ppermute | solution.py:502
  35.1 2.9 %collective-permute-start.13 = (f32[256,128]{1,0:T(8,128)S(1)}, f32[256,128]{1,0:T(8,128)S(1)}, u32[]{:S(2)}, u32[]{:S(2)}) collective-permute-start(f32[256,128]{1,0:T(8,128)S(1)} %copy-done.16), channel_id=1, source_target_pairs={{1,0},{2,8},{3,16},{5,4},{6,12},{7,20},{9,2},{10,10},{11,18},{13,6... | collective-permute-start | bytes 393224 | tf_op jit(solution)/shard_map/ppermute | solution.py:502
  37.9 1.9 %collective-permute-start.12 = (f32[256,128]{1,0:T(8,128)S(1)}, f32[256,128]{1,0:T(8,128)S(1)}, u32[]{:S(2)}, u32[]{:S(2)}) collective-permute-start(f32[256,128]{1,0:T(8,128)S(1)} %copy-done.16), channel_id=1, source_target_pairs={{0,0},{1,8},{2,16},{3,24},{4,4},{5,12},{6,20},{7,28},{8,2},{9,10},... | collective-permute-start | bytes 393224 | tf_op jit(solution)/shard_map/ppermute | solution.py:502
  41.7 4.6 %collective-permute-start.10 = (f32[128,256]{1,0:T(8,128)S(1)}, f32[128,256]{1,0:T(8,128)S(1)}, u32[]{:S(2)}, u32[]{:S(2)}) collective-permute-start(f32[128,256]{1,0:T(8,128)S(1)} %add_add_fusion.here_ref), channel_id=1, source_target_pairs={{0,8},{1,9},{2,10},{3,11},{4,12},{5,13},{6,14},{7,15},{8,0},{9,1},... | collective-permute-start | bytes 393224 | tf_op jit(solution)/shard_map/ppermute | solution.py:502
  46.4 4.6 %plane_couple.2.refs_2_ = f32[1024,512]{1,0:T(8,128)S(1)} custom-call(s32[6]{0:T(128)S(1)} %broadcast_multiply_fusion.first_ref, f32[24,1024]{1,0:T(8,128)S(1)} %constant_dynamic-update-slice_fusion.refs_0_, f32[24,1024]{1,0:T(8,128)S(1)} %collective-permute-done.3.refs_1_), custom_call_target="tpu_custom_call" | custom-call | flops 2147483648 | bytes 2000000 | tf_op jit(solution)/shard_map/plane_couple/pallas_call | solution.py:756
  51.4 3.0 %plane_first.1.a_ref.pulled_ref.refs_4_ = f32[136,256]{1,0:T(8,128)S(1)} custom-call(f32[2]{0:T(128)S(1)} %add_convert_fusion.flag_ref, f32[128,256]{1,0:T(8,128)S(1)} %add_add_fusion.here_ref, f32[128,256]{1,0:T(8,128)S(1)} %collective-permute-done.10.pair_ref, f32[128,256]{1,0:T(8,128)S(1)} %collective-permute-done.11.middle_ref, ...), custom_call_target="tpu_custom_call" | custom-call | flops 1 | bytes 1 | tf_op jit(solution)/shard_map/plane_first/pallas_call | solution.py:862
  57.1 4.9 %plane_couple.3 = (bf16[1024,512]{1,0:T(8,128)(2,1)S(1)}, bf16[1024,512]{1,0:T(8,128)(2,1)S(1)}) custom-call(s32[6]{0:T(128)S(1)} %broadcast_multiply_fusion.first_ref, f32[24,1024]{1,0:T(8,128)S(1)} %collective-permute-done.4.refs_0_, f32[24,1024]{1,0:T(8,128)S(1)} %collective-permute-done.5.refs_1_, f32[1024,512]{1,0:T(8,128)S(1)} %plane_couple.2.refs_2_), custom_call_target="tpu_custom_call" | custom-call | flops 2147483648 | bytes 2000000 | tf_op jit(solution)/shard_map/plane_couple/pallas_call | solution.py:756
  62.1 1.9 %collective-permute-done.15.c_ref = f32[136,256]{1,0:T(8,128)S(1)} collective-permute-done((f32[136,256]{1,0:T(8,128)S(1)}, f32[136,256]{1,0:T(8,128)S(1)}, u32[]{:S(2)}, u32[]{:S(2)}) %collective-permute-start.15) | collective-permute-done | bytes 139296 | tf_op jit(solution)/shard_map/ppermute | solution.py:502
  68.5 2.5 %collective-permute-start.18 = (f32[136,256]{1,0:T(8,128)S(1)}, f32[136,256]{1,0:T(8,128)S(1)}, u32[]{:S(2)}, u32[]{:S(2)}) collective-permute-start(f32[136,256]{1,0:T(8,128)S(1)} %slice_add_fusion.2.here_ref.refs_0_), channel_id=1, source_target_pairs={{0,8},{1,9},{2,10},{3,11},{4,12},{5,13},{6,14},{7,15},{8,0},{9,1},... | collective-permute-start | bytes 417800 | tf_op jit(solution)/shard_map/ppermute | solution.py:502
  71.1 3.7 %collective-permute-done.18.pair_ref.refs_1_ = f32[136,256]{1,0:T(8,128)S(1)} collective-permute-done((f32[136,256]{1,0:T(8,128)S(1)}, f32[136,256]{1,0:T(8,128)S(1)}, u32[]{:S(2)}, u32[]{:S(2)}) %collective-permute-start.18) | collective-permute-done | bytes 139296 | tf_op jit(solution)/shard_map/ppermute | solution.py:502
  74.8 2.1 %plane_open.1 = (f32[136,256]{1,0:T(8,128)S(1)}, f32[128,256]{1,0:T(8,128)S(1)}) custom-call(f32[2]{0:T(128)S(1)} %add_convert_fusion.flag_ref, f32[136,256]{1,0:T(8,128)S(1)} %slice_add_fusion.2.here_ref.refs_0_, f32[136,256]{1,0:T(8,128)S(1)} %collective-permute-done.18.pair_ref.refs_1_, f32[136,256]{1,0:T(8,128)S(1)} %collective-permute-done.19.middle_ref.refs_2_, ...), custom_call_target="tpu_custom_call" | custom-call | flops 1 | bytes 1 | tf_op jit(solution)/shard_map/plane_open/pallas_call | solution.py:899
  79.7 2.5 %collective-permute-done.22.d_ref = f32[136,256]{1,0:T(8,128)S(1)} collective-permute-done((f32[136,256]{1,0:T(8,128)S(1)}, f32[136,256]{1,0:T(8,128)S(1)}, u32[]{:S(2)}, u32[]{:S(2)}) %collective-permute-start.22) | collective-permute-done | bytes 139296 | tf_op jit(solution)/shard_map/ppermute | solution.py:502
  82.2 4.2 %collective-permute-done.21.c_ref = f32[136,256]{1,0:T(8,128)S(1)} collective-permute-done((f32[136,256]{1,0:T(8,128)S(1)}, f32[136,256]{1,0:T(8,128)S(1)}, u32[]{:S(2)}, u32[]{:S(2)}) %collective-permute-start.21) | collective-permute-done | bytes 139296 | tf_op jit(solution)/shard_map/ppermute | solution.py:502
  86.4 1.8 %plane_mix.4 = (f32[136,256]{1,0:T(8,128)S(1)}, f32[392,256]{1,0:T(8,128)S(1)}, f32[128,512]{1,0:T(8,128)S(1)}) custom-call(s32[6]{0:T(128)S(1)} %broadcast_multiply_fusion.first_ref, bf16[1024,512]{1,0:T(8,128)(2,1)S(1)} %get-tuple-element.50.high_ref, bf16[1024,512]{1,0:T(8,128)(2,1)S(1)} %get-tuple-element.51.low_ref, ...), custom_call_target="tpu_custom_call" | custom-call | flops 1 | bytes 1 | tf_op jit(solution)/shard_map/plane_mix/pallas_call | solution.py:802
  90.9 3.6 %collective-permute-start.24 = (f32[136,256]{1,0:T(8,128)S(1)}, f32[136,256]{1,0:T(8,128)S(1)}, u32[]{:S(2)}, u32[]{:S(2)}) collective-permute-start(f32[136,256]{1,0:T(8,128)S(1)} %slice_add_fusion.1.here_ref), channel_id=1, source_target_pairs={{0,8},{1,9},{2,10},{3,11},{4,12},{5,13},{6,14},{7,15},{8,0},{9,1},... | collective-permute-start | bytes 417800 | tf_op jit(solution)/shard_map/ppermute | solution.py:502
  95.7 3.1 %collective-permute-done.27.mirror_ref = f32[8,256]{1,0:T(8,128)S(1)} collective-permute-done((f32[8,256]{1,0:T(8,128)S(1)}, f32[8,256]{1,0:T(8,128)S(1)}, u32[]{:S(2)}, u32[]{:S(2)}) %collective-permute-start.27) | collective-permute-done | bytes 8224 | tf_op jit(solution)/shard_map/ppermute | solution.py:502
  99.1 2.3 %plane_step.1 = (f32[8,256]{1,0:T(8,128)S(1)}, f32[136,256]{1,0:T(8,128)S(1)}, f32[768,256]{1,0:T(8,128)S(1)}) custom-call(f32[2]{0:T(128)S(1)} %add_convert_fusion.flag_ref, f32[136,256]{1,0:T(8,128)S(1)} %slice_add_fusion.1.here_ref, f32[136,256]{1,0:T(8,128)S(1)} %collective-permute-done.24.pair_ref, f32[136,256]{1,0:T(8,128)S(1)} %collective-permute-done.25.middle_ref, ...), custom_call_target="tpu_custom_call" | custom-call | flops 1 | bytes 1 | tf_op jit(solution)/shard_map/plane_step/pallas_call | solution.py:952
  104.2 2.3 %collective-permute-done.30.d_ref = f32[136,256]{1,0:T(8,128)S(1)} collective-permute-done((f32[136,256]{1,0:T(8,128)S(1)}, f32[136,256]{1,0:T(8,128)S(1)}, u32[]{:S(2)}, u32[]{:S(2)}) %collective-permute-start.30) | collective-permute-done | bytes 139296 | tf_op jit(solution)/shard_map/ppermute | solution.py:502
  106.4 1.8 %collective-permute-done.29.c_ref = f32[136,256]{1,0:T(8,128)S(1)} collective-permute-done((f32[136,256]{1,0:T(8,128)S(1)}, f32[136,256]{1,0:T(8,128)S(1)}, u32[]{:S(2)}, u32[]{:S(2)}) %collective-permute-start.29) | collective-permute-done | bytes 139296 | tf_op jit(solution)/shard_map/ppermute | solution.py:502
  110.0 3.3 %collective-permute-start.31 = (f32[392,256]{1,0:T(8,128)S(1)}, f32[392,256]{1,0:T(8,128)S(1)}, u32[]{:S(2)}, u32[]{:S(2)}) collective-permute-start(f32[392,256]{1,0:T(8,128)S(1)} %get-tuple-element.66), channel_id=1, source_target_pairs={{0,1},{1,0},{2,3},{3,2},{4,5},{5,4},{6,7},{7,6},{8,9},{9,8},{10,11... | collective-permute-start | bytes 1204232 | tf_op jit(solution)/shard_map/ppermute | solution.py:502
  115.4 2.5 %collective-permute-start.32 = (f32[136,256]{1,0:T(8,128)S(1)}, f32[136,256]{1,0:T(8,128)S(1)}, u32[]{:S(2)}, u32[]{:S(2)}) collective-permute-start(f32[136,256]{1,0:T(8,128)S(1)} %slice_add_fusion.here_ref), channel_id=1, source_target_pairs={{0,8},{1,9},{2,10},{3,11},{4,12},{5,13},{6,14},{7,15},{8,0},{9,1},... | collective-permute-start | bytes 417800 | tf_op jit(solution)/shard_map/ppermute | solution.py:502
  117.9 3.4 %collective-permute-done.32.pair_ref = f32[136,256]{1,0:T(8,128)S(1)} collective-permute-done((f32[136,256]{1,0:T(8,128)S(1)}, f32[136,256]{1,0:T(8,128)S(1)}, u32[]{:S(2)}, u32[]{:S(2)}) %collective-permute-start.32) | collective-permute-done | bytes 139296 | tf_op jit(solution)/shard_map/ppermute | solution.py:502
  122.5 12.2 %all_to_all.5.close_ref = f32[32,8,128]{2,1,0:T(8,128)S(1)} all-to-all(f32[32,8,128]{2,1,0:T(8,128)S(1)} %plane_close.1), channel_id=1, replica_groups=mesh['basin'=8,'tm'=4] {'basin','tm'}, dimensions={0} | all-to-all | bytes 262144 | tf_op jit(solution)/shard_map/all_to_all | solution.py:1152
  135.3 2.6 %collective-permute-start.34 = (f32[512,128]{1,0:T(8,128)S(1)}, f32[512,128]{1,0:T(8,128)S(1)}, u32[]{:S(2)}, u32[]{:S(2)}) collective-permute-start(f32[512,128]{1,0:T(8,128)S(1)} %plane_combine.1), channel_id=1, source_target_pairs={{0,0},{1,16},{2,8},{3,24},{4,4},{5,20},{6,12},{7,28},{8,1},{9,17},... | collective-permute-start | bytes 786440 | tf_op jit(solution)/shard_map/ppermute | solution.py:502
  137.9 10.7 %collective-permute-done.34.rows_ref = f32[512,128]{1,0:T(8,128)S(1)} collective-permute-done((f32[512,128]{1,0:T(8,128)S(1)}, f32[512,128]{1,0:T(8,128)S(1)}, u32[]{:S(2)}, u32[]{:S(2)}) %collective-permute-start.34) | collective-permute-done | bytes 262176 | tf_op jit(solution)/shard_map/ppermute | solution.py:502
  148.6 2.6 %plane_finish.1 = f32[4096,128]{1,0:T(8,128)} custom-call(f32[512,128]{1,0:T(8,128)S(1)} %collective-permute-done.34.rows_ref, s32[32,16,128]{2,1,0:T(8,128)S(1)} %copy-done.6, f32[4096,128]{1,0:T(8,128)S(1)} %copy-done.1), custom_call_target="tpu_custom_call" | custom-call | tf_op jit(solution)/shard_map/plane_finish/pallas_call | solution.py:1085
  (98 shorter events, 36.0 us)
Async XLA Ops:
  2.6 11.2 %collective-permute-start.1 = (f32[24,512]{1,0:T(8,128)S(1)}, f32[24,512]{1,0:T(8,128)S(1)}, u32[]{:S(2)}, u32[]{:S(2)}) collective-permute-start(f32[24,512]{1,0:T(8,128)S(1)} %describe.1), channel_id=1, source_target_pairs={{0,0},{1,8},{2,16},{3,24},{4,4},{5,12},{6,20},{7,28},{8,2},{9,10},... | collective-permute-start | bytes 147464 | tf_op jit(solution)/shard_map/ppermute | solution.py:502
  10.5 17.1 %collective-permute-start = (f32[128,512]{1,0:T(8,128)S(1)}, f32[128,512]{1,0:T(8,128)S(1)}, u32[]{:S(2)}, u32[]{:S(2)}) collective-permute-start(f32[128,512]{1,0:T(8,128)S(1)} %send.1), channel_id=1, source_target_pairs={{0,0},{1,8},{2,16},{3,24},{4,4},{5,12},{6,20},{7,28},{8,2},{9,10},... | collective-permute-start | bytes 786440 | tf_op jit(solution)/shard_map/ppermute | solution.py:502
  15.1 6.4 %collective-permute-start.5 = (f32[24,1024]{1,0:T(8,128)S(1)}, f32[24,1024]{1,0:T(8,128)S(1)}, u32[]{:S(2)}, u32[]{:S(2)}) collective-permute-start(f32[24,1024]{1,0:T(8,128)S(1)} %constant_dynamic-update-slice_fusion.refs_0_), channel_id=1, source_target_pairs={{0,6},{1,7},{2,4},{3,5},{4,2},{5,3},{6,0},{7,1},{8,14},{9,15},{10,... | collective-permute-start | bytes 294920 | tf_op jit(solution)/shard_map/ppermute | solution.py:502
  18.4 8.7 %collective-permute-start.4 = (f32[24,1024]{1,0:T(8,128)S(1)}, f32[24,1024]{1,0:T(8,128)S(1)}, u32[]{:S(2)}, u32[]{:S(2)}) collective-permute-start(f32[24,1024]{1,0:T(8,128)S(1)} %constant_dynamic-update-slice_fusion.refs_0_), channel_id=1, source_target_pairs={{0,2},{1,3},{2,0},{3,1},{4,6},{5,7},{6,4},{7,5},{8,10},{9,11},{10,... | collective-permute-start | bytes 294920 | tf_op jit(solution)/shard_map/ppermute | solution.py:502
  18.4 8.7 %collective-permute-start.3 = (f32[24,1024]{1,0:T(8,128)S(1)}, f32[24,1024]{1,0:T(8,128)S(1)}, u32[]{:S(2)}, u32[]{:S(2)}) collective-permute-start(f32[24,1024]{1,0:T(8,128)S(1)} %constant_dynamic-update-slice_fusion.refs_0_), channel_id=1, source_target_pairs={{0,4},{1,5},{2,6},{3,7},{4,0},{5,1},{6,2},{7,3},{8,12},{9,13},{10,... | collective-permute-start | bytes 294920 | tf_op jit(solution)/shard_map/ppermute | solution.py:502
  31.8 8.0 %collective-permute-start.7 = (f32[128,256]{1,0:T(8,128)S(1)}, f32[128,256]{1,0:T(8,128)S(1)}, u32[]{:S(2)}, u32[]{:S(2)}) collective-permute-start(f32[128,256]{1,0:T(8,128)S(1)} %get-tuple-element.46), channel_id=1, source_target_pairs={{0,4},{1,5},{2,6},{3,7},{4,0},{5,1},{6,2},{7,3},{8,12},{9,13},{10,... | collective-permute-start | bytes 393224 | tf_op jit(solution)/shard_map/ppermute | solution.py:502
  33.0 6.9 %collective-permute-start.8 = (f32[128,256]{1,0:T(8,128)S(1)}, f32[128,256]{1,0:T(8,128)S(1)}, u32[]{:S(2)}, u32[]{:S(2)}) collective-permute-start(f32[128,256]{1,0:T(8,128)S(1)} %get-tuple-element.47), channel_id=1, source_target_pairs={{0,2},{1,3},{2,0},{3,1},{4,6},{5,7},{6,4},{7,5},{8,10},{9,11},{10,... | collective-permute-start | bytes 393224 | tf_op jit(solution)/shard_map/ppermute | solution.py:502
  35.0 5.8 %collective-permute-start.9 = (f32[128,256]{1,0:T(8,128)S(1)}, f32[128,256]{1,0:T(8,128)S(1)}, u32[]{:S(2)}, u32[]{:S(2)}) collective-permute-start(f32[128,256]{1,0:T(8,128)S(1)} %get-tuple-element.48), channel_id=1, source_target_pairs={{0,6},{1,7},{2,4},{3,5},{4,2},{5,3},{6,0},{7,1},{8,14},{9,15},{10,... | collective-permute-start | bytes 393224 | tf_op jit(solution)/shard_map/ppermute | solution.py:502
  35.1 16.3 %collective-permute-start.13 = (f32[256,128]{1,0:T(8,128)S(1)}, f32[256,128]{1,0:T(8,128)S(1)}, u32[]{:S(2)}, u32[]{:S(2)}) collective-permute-start(f32[256,128]{1,0:T(8,128)S(1)} %copy-done.16), channel_id=1, source_target_pairs={{1,0},{2,8},{3,16},{5,4},{6,12},{7,20},{9,2},{10,10},{11,18},{13,6... | collective-permute-start | bytes 393224 | tf_op jit(solution)/shard_map/ppermute | solution.py:502
  37.9 13.4 %collective-permute-start.12 = (f32[256,128]{1,0:T(8,128)S(1)}, f32[256,128]{1,0:T(8,128)S(1)}, u32[]{:S(2)}, u32[]{:S(2)}) collective-permute-start(f32[256,128]{1,0:T(8,128)S(1)} %copy-done.16), channel_id=1, source_target_pairs={{0,0},{1,8},{2,16},{3,24},{4,4},{5,12},{6,20},{7,28},{8,2},{9,10},... | collective-permute-start | bytes 393224 | tf_op jit(solution)/shard_map/ppermute | solution.py:502
  40.9 10.1 %collective-permute-start.11 = (f32[128,256]{1,0:T(8,128)S(1)}, f32[128,256]{1,0:T(8,128)S(1)}, u32[]{:S(2)}, u32[]{:S(2)}) collective-permute-start(f32[128,256]{1,0:T(8,128)S(1)} %add_add_fusion.here_ref), channel_id=1, source_target_pairs={{8,16},{9,17},{10,18},{11,19},{12,20},{13,21},{14,22},{15,23},{16,... | collective-permute-start | bytes 393224 | tf_op jit(solution)/shard_map/ppermute | solution.py:502
  41.7 9.6 %collective-permute-start.10 = (f32[128,256]{1,0:T(8,128)S(1)}, f32[128,256]{1,0:T(8,128)S(1)}, u32[]{:S(2)}, u32[]{:S(2)}) collective-permute-start(f32[128,256]{1,0:T(8,128)S(1)} %add_add_fusion.here_ref), channel_id=1, source_target_pairs={{0,8},{1,9},{2,10},{3,11},{4,12},{5,13},{6,14},{7,15},{8,0},{9,1},... | collective-permute-start | bytes 393224 | tf_op jit(solution)/shard_map/ppermute | solution.py:502
  54.4 7.6 %collective-permute-start.16 = (f32[136,256]{1,0:T(8,128)S(1)}, f32[136,256]{1,0:T(8,128)S(1)}, u32[]{:S(2)}, u32[]{:S(2)}) collective-permute-start(f32[136,256]{1,0:T(8,128)S(1)} %plane_first.1.a_ref.pulled_ref.refs_4_), channel_id=1, source_target_pairs={{0,6},{1,7},{2,4},{3,5},{4,2},{5,3},{6,0},{7,1},{8,14},{9,15},{10,... | collective-permute-start | bytes 417800 | tf_op jit(solution)/shard_map/ppermute | solution.py:502
  56.1 7.9 %collective-permute-start.15 = (f32[136,256]{1,0:T(8,128)S(1)}, f32[136,256]{1,0:T(8,128)S(1)}, u32[]{:S(2)}, u32[]{:S(2)}) collective-permute-start(f32[136,256]{1,0:T(8,128)S(1)} %plane_first.1.a_ref.pulled_ref.refs_4_), channel_id=1, source_target_pairs={{0,2},{1,3},{2,0},{3,1},{4,6},{5,7},{6,4},{7,5},{8,10},{9,11},{10,... | collective-permute-start | bytes 417800 | tf_op jit(solution)/shard_map/ppermute | solution.py:502
  56.8 7.2 %collective-permute-start.14 = (f32[136,256]{1,0:T(8,128)S(1)}, f32[136,256]{1,0:T(8,128)S(1)}, u32[]{:S(2)}, u32[]{:S(2)}) collective-permute-start(f32[136,256]{1,0:T(8,128)S(1)} %plane_first.1.a_ref.pulled_ref.refs_4_), channel_id=1, source_target_pairs={{0,4},{1,5},{2,6},{3,7},{4,0},{5,1},{6,2},{7,3},{8,12},{9,13},{10,... | collective-permute-start | bytes 417800 | tf_op jit(solution)/shard_map/ppermute | solution.py:502
  67.7 3.4 %collective-permute-start.19 = (f32[136,256]{1,0:T(8,128)S(1)}, f32[136,256]{1,0:T(8,128)S(1)}, u32[]{:S(2)}, u32[]{:S(2)}) collective-permute-start(f32[136,256]{1,0:T(8,128)S(1)} %slice_add_fusion.2.here_ref.refs_0_), channel_id=1, source_target_pairs={{8,16},{9,17},{10,18},{11,19},{12,20},{13,21},{14,22},{15,23},{16,... | collective-permute-start | bytes 417800 | tf_op jit(solution)/shard_map/ppermute | solution.py:502
  68.5 6.3 %collective-permute-start.18 = (f32[136,256]{1,0:T(8,128)S(1)}, f32[136,256]{1,0:T(8,128)S(1)}, u32[]{:S(2)}, u32[]{:S(2)}) collective-permute-start(f32[136,256]{1,0:T(8,128)S(1)} %slice_add_fusion.2.here_ref.refs_0_), channel_id=1, source_target_pairs={{0,8},{1,9},{2,10},{3,11},{4,12},{5,13},{6,14},{7,15},{8,0},{9,1},... | collective-permute-start | bytes 417800 | tf_op jit(solution)/shard_map/ppermute | solution.py:502
  77.0 5.3 %collective-permute-start.22 = (f32[136,256]{1,0:T(8,128)S(1)}, f32[136,256]{1,0:T(8,128)S(1)}, u32[]{:S(2)}, u32[]{:S(2)}) collective-permute-start(f32[136,256]{1,0:T(8,128)S(1)} %get-tuple-element.59.a_ref.refs_3_), channel_id=1, source_target_pairs={{0,6},{1,7},{2,4},{3,5},{4,2},{5,3},{6,0},{7,1},{8,14},{9,15},{10,... | collective-permute-start | bytes 417800 | tf_op jit(solution)/shard_map/ppermute | solution.py:502
  78.2 8.3 %collective-permute-start.21 = (f32[136,256]{1,0:T(8,128)S(1)}, f32[136,256]{1,0:T(8,128)S(1)}, u32[]{:S(2)}, u32[]{:S(2)}) collective-permute-start(f32[136,256]{1,0:T(8,128)S(1)} %get-tuple-element.59.a_ref.refs_3_), channel_id=1, source_target_pairs={{0,2},{1,3},{2,0},{3,1},{4,6},{5,7},{6,4},{7,5},{8,10},{9,11},{10,... | collective-permute-start | bytes 417800 | tf_op jit(solution)/shard_map/ppermute | solution.py:502
  78.6 7.8 %collective-permute-start.20 = (f32[136,256]{1,0:T(8,128)S(1)}, f32[136,256]{1,0:T(8,128)S(1)}, u32[]{:S(2)}, u32[]{:S(2)}) collective-permute-start(f32[136,256]{1,0:T(8,128)S(1)} %get-tuple-element.59.a_ref.refs_3_), channel_id=1, source_target_pairs={{0,4},{1,5},{2,6},{3,7},{4,0},{5,1},{6,2},{7,3},{8,12},{9,13},{10,... | collective-permute-start | bytes 417800 | tf_op jit(solution)/shard_map/ppermute | solution.py:502
  88.2 2.0 %collective-permute-start.23 = (f32[392,256]{1,0:T(8,128)S(1)}, f32[392,256]{1,0:T(8,128)S(1)}, u32[]{:S(2)}, u32[]{:S(2)}) collective-permute-start(f32[392,256]{1,0:T(8,128)S(1)} %get-tuple-element.61), channel_id=1, source_target_pairs={{0,1},{1,0},{2,3},{3,2},{4,5},{5,4},{6,7},{7,6},{8,9},{9,8},{10,11... | collective-permute-start | bytes 1204232 | tf_op jit(solution)/shard_map/ppermute | solution.py:502
  90.2 8.9 %collective-permute-start.25 = (f32[136,256]{1,0:T(8,128)S(1)}, f32[136,256]{1,0:T(8,128)S(1)}, u32[]{:S(2)}, u32[]{:S(2)}) collective-permute-start(f32[136,256]{1,0:T(8,128)S(1)} %slice_add_fusion.1.here_ref), channel_id=1, source_target_pairs={{8,16},{9,17},{10,18},{11,19},{12,20},{13,21},{14,22},{15,23},{16,... | collective-permute-start | bytes 417800 | tf_op jit(solution)/shard_map/ppermute | solution.py:502
  90.9 8.2 %collective-permute-start.24 = (f32[136,256]{1,0:T(8,128)S(1)}, f32[136,256]{1,0:T(8,128)S(1)}, u32[]{:S(2)}, u32[]{:S(2)}) collective-permute-start(f32[136,256]{1,0:T(8,128)S(1)} %slice_add_fusion.1.here_ref), channel_id=1, source_target_pairs={{0,8},{1,9},{2,10},{3,11},{4,12},{5,13},{6,14},{7,15},{8,0},{9,1},... | collective-permute-start | bytes 417800 | tf_op jit(solution)/shard_map/ppermute | solution.py:502
  94.5 4.4 %collective-permute-start.27 = (f32[8,256]{1,0:T(8,128)S(1)}, f32[8,256]{1,0:T(8,128)S(1)}, u32[]{:S(2)}, u32[]{:S(2)}) collective-permute-start(f32[8,256]{1,0:T(8,128)S(1)} %slice.18), channel_id=1, source_target_pairs={{0,24},{1,25},{2,26},{3,27},{4,28},{5,29},{6,30},{7,31},{8,16},{9,... | collective-permute-start | bytes 24584 | tf_op jit(solution)/shard_map/ppermute | solution.py:502
  95.7 3.4 %collective-permute-start.26 = (f32[8,256]{1,0:T(8,128)S(1)}, f32[8,256]{1,0:T(8,128)S(1)}, u32[]{:S(2)}, u32[]{:S(2)}) collective-permute-start(f32[8,256]{1,0:T(8,128)S(1)} %slice.18), channel_id=1, source_target_pairs={{0,16},{1,17},{2,18},{3,19},{4,20},{5,21},{6,22},{7,23},{8,24},{9,... | collective-permute-start | bytes 24584 | tf_op jit(solution)/shard_map/ppermute | solution.py:502
  101.4 5.0 %collective-permute-start.30 = (f32[136,256]{1,0:T(8,128)S(1)}, f32[136,256]{1,0:T(8,128)S(1)}, u32[]{:S(2)}, u32[]{:S(2)}) collective-permute-start(f32[136,256]{1,0:T(8,128)S(1)} %get-tuple-element.64.a_ref.pulled_ref), channel_id=1, source_target_pairs={{0,6},{1,7},{2,4},{3,5},{4,2},{5,3},{6,0},{7,1},{8,14},{9,15},{10,... | collective-permute-start | bytes 417800 | tf_op jit(solution)/shard_map/ppermute | solution.py:502
  102.7 5.5 %collective-permute-start.29 = (f32[136,256]{1,0:T(8,128)S(1)}, f32[136,256]{1,0:T(8,128)S(1)}, u32[]{:S(2)}, u32[]{:S(2)}) collective-permute-start(f32[136,256]{1,0:T(8,128)S(1)} %get-tuple-element.64.a_ref.pulled_ref), channel_id=1, source_target_pairs={{0,2},{1,3},{2,0},{3,1},{4,6},{5,7},{6,4},{7,5},{8,10},{9,11},{10,... | collective-permute-start | bytes 417800 | tf_op jit(solution)/shard_map/ppermute | solution.py:502
  103.1 5.1 %collective-permute-start.28 = (f32[136,256]{1,0:T(8,128)S(1)}, f32[136,256]{1,0:T(8,128)S(1)}, u32[]{:S(2)}, u32[]{:S(2)}) collective-permute-start(f32[136,256]{1,0:T(8,128)S(1)} %get-tuple-element.64.a_ref.pulled_ref), channel_id=1, source_target_pairs={{0,4},{1,5},{2,6},{3,7},{4,0},{5,1},{6,2},{7,3},{8,12},{9,13},{10,... | collective-permute-start | bytes 417800 | tf_op jit(solution)/shard_map/ppermute | solution.py:502
  110.0 4.7 %collective-permute-start.31 = (f32[392,256]{1,0:T(8,128)S(1)}, f32[392,256]{1,0:T(8,128)S(1)}, u32[]{:S(2)}, u32[]{:S(2)}) collective-permute-start(f32[392,256]{1,0:T(8,128)S(1)} %get-tuple-element.66), channel_id=1, source_target_pairs={{0,1},{1,0},{2,3},{3,2},{4,5},{5,4},{6,7},{7,6},{8,9},{9,8},{10,11... | collective-permute-start | bytes 1204232 | tf_op jit(solution)/shard_map/ppermute | solution.py:502
  114.7 3.1 %collective-permute-start.33 = (f32[136,256]{1,0:T(8,128)S(1)}, f32[136,256]{1,0:T(8,128)S(1)}, u32[]{:S(2)}, u32[]{:S(2)}) collective-permute-start(f32[136,256]{1,0:T(8,128)S(1)} %slice_add_fusion.here_ref), channel_id=1, source_target_pairs={{8,16},{9,17},{10,18},{11,19},{12,20},{13,21},{14,22},{15,23},{16,... | collective-permute-start | bytes 417800 | tf_op jit(solution)/shard_map/ppermute | solution.py:502
  115.4 5.9 %collective-permute-start.32 = (f32[136,256]{1,0:T(8,128)S(1)}, f32[136,256]{1,0:T(8,128)S(1)}, u32[]{:S(2)}, u32[]{:S(2)}) collective-permute-start(f32[136,256]{1,0:T(8,128)S(1)} %slice_add_fusion.here_ref), channel_id=1, source_target_pairs={{0,8},{1,9},{2,10},{3,11},{4,12},{5,13},{6,14},{7,15},{8,0},{9,1},... | collective-permute-start | bytes 417800 | tf_op jit(solution)/shard_map/ppermute | solution.py:502
  135.3 13.3 %collective-permute-start.34 = (f32[512,128]{1,0:T(8,128)S(1)}, f32[512,128]{1,0:T(8,128)S(1)}, u32[]{:S(2)}, u32[]{:S(2)}) collective-permute-start(f32[512,128]{1,0:T(8,128)S(1)} %plane_combine.1), channel_id=1, source_target_pairs={{0,0},{1,16},{2,8},{3,24},{4,4},{5,20},{6,12},{7,28},{8,1},{9,17},... | collective-permute-start | bytes 786440 | tf_op jit(solution)/shard_map/ppermute | solution.py:502
  (20 other events, 216.7 us)

commit v9 on v8

--- a/solution.py
+++ b/solution.py
@@ -547,6 +547,10 @@
     return 3 - z, x, y, c
 
 
+def z_next(z, x, y, c):
+    return (z + 1, x, y, c) if z < 3 else None
+
+
 SQUARE = (over_x, over_y, over_xy)
 
 
@@ -554,28 +558,31 @@
     out = []
     for _ in range(3):
         piece = value.astype(jnp.bfloat16)
-        out.append(jnp.asarray(piece))
+        out.append(piece)
         value = value - piece.astype(np.float64)
     return out
 
 
-def turned_transforms():
+ORDERS = {2: ((0, 1), (1, 0), (0, 0)), 3: ((0, 2), (1, 1), (2, 0), (0, 1), (1, 0), (0, 0))}
+
+
+def widened(mat, order):
+    parts = split_constant(mat)
+    return jnp.asarray(np.concatenate([parts[i] for i, _ in ORDERS[order]], axis=1))
+
+
+def product(wide, value, order):
+    parts = pieces(value, order)
+    return dot(wide, jnp.concatenate([parts[j] for _, j in ORDERS[order]], axis=0))
+
+
+def turned_transforms(order):
     half = SPAN // 2
     freq = 2.0 * np.pi * (np.arange(half) + 0.5) / SPAN
     phase = freq[:, None] * np.arange(SPAN)[None, :]
     forward = np.concatenate([np.cos(phase), -np.sin(phase)], axis=0)
     inverse = forward.T * (2.0 / SPAN)
-    return split_constant(forward), split_constant(inverse[:half]), split_constant(inverse[half:])
-
-
-def product(mats, value, order):
-    parts = pieces(value, order)
-    result = None
-    for level in reversed(range(order)):
-        for i in range(level + 1):
-            term = dot(mats[i][...], parts[level - i])
-            result = term if result is None else result + term
-    return result
+    return [widened(mat, order) for mat in (forward, inverse[:half], inverse[half:], forward[:, :half])]
 
 
 def turn(waves, spec, sign):
@@ -586,11 +593,12 @@
 
 
 def plane_delayed(before, here, after, spec, forward, last, order):
-    out = []
-    for pair in ((before, here), (here, after)):
-        waves = product(forward, jnp.concatenate(pair, axis=0), order)
-        out.append(product(last, turn(waves, spec, 1.0), order))
-    return out
+    rows = here.shape[1]
+    pairs = [jnp.concatenate(pair, axis=0) for pair in ((before, here), (here, after))]
+    waves = product(forward, jnp.concatenate(pairs, axis=1), order)
+    turned = [turn(waves[:, i * rows : (i + 1) * rows], spec, 1.0) for i in range(2)]
+    out = product(last, jnp.concatenate(turned, axis=1), order)
+    return out[:, :rows], out[:, rows:]
 
 
 def plane_advanced(here, after, spec, forward, first, order):
@@ -641,7 +649,8 @@
     weights = inc_ref[...].astype(F32).astype(BF16)
     parts = []
     for b in range(blocks):
-        parts.append(pick(weights[b], field_ref[pl.ds(b * width, width), :]))
+        value = jnp.concatenate(pieces(field_ref[pl.ds(b * width, width), :], 3)[::-1], axis=0)
+        parts.append(dot(jnp.concatenate([weights[b]] * 3, axis=1), value))
     out_ref[...] = jnp.transpose(jnp.concatenate(parts, axis=0))
 
 
@@ -670,18 +679,15 @@
 
 
 def spread_kernel(first_ref, mine_ref, other_ref, meta_ref, meta_other_ref, *out_refs):
-    rows = out_refs[0].shape[1]
+    hours, rows = out_refs[0].shape
     where = meta_ref.shape[0] - 8
+    value = jnp.concatenate([mine_ref[...], other_ref[...]], axis=1)
+    gauge = jnp.concatenate([ref[where : where + 1, :] for ref in (meta_ref, meta_other_ref)], axis=1)
+    stacked = jnp.concatenate(pieces(value, 3), axis=0)
     for m, out_ref in enumerate(out_refs):
-        result = None
-        for ref, meta in ((mine_ref, meta_ref), (other_ref, meta_other_ref)):
-            hot = hot_rows(meta[where : where + 1, :], first_ref[m], rows)
-            for piece in reversed(pieces(ref[...], 3)):
-                term = lax.dot_general(
-                    piece, hot, (((1,), (1,)), ((), ())), preferred_element_type=F32
-                )
-                result = term if result is None else result + term
-        out_ref[...] = result
+        hot = hot_rows(gauge, first_ref[m], rows)
+        result = lax.dot_general(stacked, hot, (((1,), (1,)), ((), ())), preferred_element_type=F32)
+        out_ref[...] = (result[2 * hours :] + result[hours : 2 * hours]) + result[:hours]
 
 
 def spread(first, parcels, metas, rows):
@@ -767,55 +773,77 @@
     )(*args)
 
 
-def plane_mix_kernel(
-    first_ref, high_ref, low_ref, meta_ref, meta_other_ref, a_ref, b_ref, c_ref, d_ref, mine_ref, other_ref, rows_ref
-):
+def plane_mix_kernel(high_ref, low_ref, a_ref, b_ref, c_ref, d_ref, *refs):
+    *extra, mine_ref, other_ref = refs
     refs = (a_ref, b_ref, c_ref, d_ref)
     height, rows = a_ref.shape
     hours = height - NOTE
     body, tail = pl.ds(0, hours), pl.ds(hours, NOTE)
-    value = jnp.concatenate([ref[body, :] for ref in refs], axis=1)
-    one, two = pieces(value, 2)
-    high, low = high_ref[...], low_ref[...]
-    result = (dot(two, high) + dot(one, low)) + dot(one, high)
+    one, two = pieces(jnp.concatenate([ref[body, :] for ref in refs], axis=1), 2)
+    both = dot(jnp.concatenate([two, one], axis=0), high_ref[...])
+    result = (both[:hours] + dot(one, low_ref[...])) + both[hours:]
     note = sum(ref[tail, :] for ref in refs)
     mine_ref[body, :] = result[:, :rows]
     other_ref[body, :] = result[:, rows:]
     mine_ref[tail, :] = note
     other_ref[tail, :] = note
+    for ref in extra:
+        other_ref[pl.ds(height, ref.shape[0]), :] = ref[...]
+
+
+def plane_mix(coupling, values, extra):
+    height, rows = values[0].shape
+    return pl.pallas_call(
+        plane_mix_kernel,
+        out_shape=[
+            jax.ShapeDtypeStruct((height, rows), F32),
+            jax.ShapeDtypeStruct((height + sum(value.shape[0] for value in extra), rows), F32),
+        ],
+        compiler_params=params(),
+        name="plane_mix",
+        cost_estimate=SMALL,
+    )(*coupling, *values, *extra)
+
+
+def plane_rows_kernel(first_ref, meta_ref, meta_other_ref, a_ref, b_ref, c_ref, d_ref, mine_ref, other_ref):
+    refs = (a_ref, b_ref, c_ref, d_ref)
+    height, rows = a_ref.shape
+    hours = height - NOTE
+    one, two = pieces(jnp.concatenate([ref[pl.ds(0, hours), :] for ref in refs], axis=1), 2)
+    stacked = jnp.concatenate([two, one], axis=0)
     where = meta_ref.shape[0] - 8
+    picked = []
     for ref in (meta_ref, meta_other_ref):
         gauge = ref[where : where + 1, :]
         hot = jnp.concatenate([hot_rows(gauge, first_ref[m], rows) for m in range(4)], axis=0)
-        picked = dot(two, hot) + dot(one, hot)
-        if ref is meta_ref:
-            rows_ref[...] = picked
-        else:
-            for i in range(gauge.shape[1] // rows):
-                other_ref[pl.ds(height + i * hours, hours), :] = picked[:, i * rows : (i + 1) * rows]
-
-
-def plane_mix(first, coupling, metas, values):
+        both = dot(stacked, hot)
+        picked.append(both[:hours] + both[hours:])
+    mine_ref[...] = picked[0]
+    for i in range(picked[1].shape[1] // rows):
+        other_ref[pl.ds(i * hours, hours), :] = picked[1][:, i * rows : (i + 1) * rows]
+
+
+def plane_rows(first, metas, values):
     height, rows = values[0].shape
     hours = height - NOTE
     slots = metas[0].shape[1]
     return pl.pallas_call(
-        plane_mix_kernel,
-        in_specs=[pl.BlockSpec(memory_space=pltpu.SMEM)] + [pl.BlockSpec(memory_space=pltpu.VMEM)] * 8,
+        plane_rows_kernel,
+        in_specs=[pl.BlockSpec(memory_space=pltpu.SMEM)] + [pl.BlockSpec(memory_space=pltpu.VMEM)] * 6,
         out_shape=[
-            jax.ShapeDtypeStruct((height, rows), F32),
-            jax.ShapeDtypeStruct((height + slots // rows * hours, rows), F32),
             jax.ShapeDtypeStruct((hours, slots), F32),
-        ],
-        compiler_params=params(),
-        name="plane_mix",
-        cost_estimate=SMALL,
-    )(first, *coupling, *metas, *values)
-
-
-def plane_spectrum_kernel(class_ref, kernels_ref, f0_ref, f1_ref, f2_ref, out_ref):
-    classes, taps = kernels_ref.shape
-    kind = class_ref[class_ref.shape[0] - 7 : class_ref.shape[0] - 6, : out_ref.shape[1]]
+            jax.ShapeDtypeStruct((slots // rows * hours, rows), F32),
+        ],
+        compiler_params=params(),
+        name="plane_rows",
+        cost_estimate=pl.CostEstimate(flops=1_000_000_000, bytes_accessed=2_000_000, transcendentals=0),
+    )(first, *metas, *values)
+
+
+def plane_spectrum_kernel(class_ref, kernels_ref, wide_ref, out_ref):
+    classes = kernels_ref.shape[0]
+    where = class_ref.shape[0] - 7
+    kind = class_ref[where : where + 1, : out_ref.shape[1]]
     hot = jnp.where(
         lax.broadcasted_iota(jnp.int32, (classes, kind.shape[1]), 0).astype(F32) == kind, 1.0, 0.0
     ).astype(BF16)
@@ -823,18 +851,17 @@
     for piece in reversed(pieces(jnp.transpose(kernels_ref[...]), 3)):
         term = dot(piece, hot)
         chosen = term if chosen is None else chosen + term
-    mats = [ref[:, :taps] for ref in (f0_ref, f1_ref, f2_ref)]
-    out_ref[...] = product(mats, chosen, 3)
-
-
-def plane_spectrum(meta, kernels, forward, rows):
+    out_ref[...] = product(wide_ref[...], chosen, 3)
+
+
+def plane_spectrum(meta, kernels, wide, rows):
     return pl.pallas_call(
         plane_spectrum_kernel,
         out_shape=jax.ShapeDtypeStruct((SPAN, rows), F32),
         compiler_params=params(),
         name="plane_spectrum",
         cost_estimate=SMALL,
-    )(meta, kernels, *forward)
+    )(meta, kernels, wide)
 
 
 def sides(even, pair, middle):
@@ -842,15 +869,14 @@
 
 
 def plane_first_kernel(flag_ref, here_ref, pair_ref, middle_ref, seen_ref, seen_later_ref, spec_ref, *refs):
-    *mats, out_ref = refs
-    forward, first, last = mats[0:3], mats[3:6], mats[6:9]
+    forward3, last3, forward, first, out_ref = refs
     hours, rows = here_ref.shape
     spec = spec_ref[...]
     before, after = sides(flag_ref[0] > 0.5, pair_ref[...], middle_ref[...])
-    now, later = plane_delayed(before, here_ref[...], after, spec, forward, last, 3)
+    now, later = plane_delayed(before, here_ref[...], after, spec, forward3[...], last3[...], 3)
     start = jnp.transpose(seen_ref[...]) - now
     start_later = (jnp.transpose(seen_later_ref[...]) - later) * flag_ref[1]
-    out_ref[pl.ds(0, hours), :] = plane_advanced(start, start_later, spec, forward, first, 3)
+    out_ref[pl.ds(0, hours), :] = plane_advanced(start, start_later, spec, forward[...], first[...], 2)
     out_ref[pl.ds(hours, NOTE), :] = jnp.concatenate(
         [lanes(start, start), jnp.zeros((NOTE - 1, rows), F32)], axis=0
     )
@@ -871,16 +897,15 @@
 
 
 def plane_open_kernel(flag_ref, here_ref, pair_ref, middle_ref, pulled_ref, spec_ref, *refs):
-    mats, (out_ref, now_ref) = refs[:9], refs[9:]
-    forward, first, last = mats[0:3], mats[3:6], mats[6:9]
+    forward, first, last, out_ref, now_ref = refs
     height, rows = pulled_ref.shape
     hours = height - NOTE
     tail, body = pl.ds(hours, NOTE), pl.ds(0, hours)
     spec = spec_ref[...]
     here = here_ref[body, :]
     before, after = sides(flag_ref[0] > 0.5, pair_ref[body, :], middle_ref[body, :])
-    now, later = plane_delayed(before, here, after, spec, forward, last, 2)
-    out_ref[body, :] = plane_advanced(now, later * flag_ref[1], spec, forward, first, 2)
+    now, later = plane_delayed(before, here, after, spec, forward[...], last[...], 2)
+    out_ref[body, :] = plane_advanced(now, later * flag_ref[1], spec, forward[...], first[...], 2)
     out_ref[tail, :] = jnp.concatenate(
         [
             lanes(pulled_ref[body, :], here),
@@ -918,27 +943,27 @@
     return 1.0 / jnp.sqrt(start), alpha, beta
 
 
-def plane_step_kernel(flag_ref, here_ref, pair_ref, middle_ref, two_ref, mirror_ref, *refs):
+def plane_step_kernel(flag_ref, here_ref, pair_ref, mirror_ref, two_ref, *refs):
     old_refs, (pulled_ref, old_z_ref, old_now_ref, spec_ref), refs = refs[:3], refs[3:7], refs[7:]
-    mats, (total_ref, out_ref, kept_ref) = refs[:9], refs[9:]
-    forward, first, last = mats[0:3], mats[3:6], mats[6:9]
+    forward, first, last, total_ref, out_ref, kept_ref = refs
     height, rows = pulled_ref.shape
     hours = height - NOTE
     tail, body = pl.ds(hours, NOTE), pl.ds(0, hours)
-    total_ref[...] = (here_ref[tail, :] + pair_ref[tail, :]) + (two_ref[...] + mirror_ref[...])
+    total_ref[...] = (here_ref[tail, :] + pair_ref[tail, :]) + (two_ref[...] + mirror_ref[tail, :])
     scale, alpha, beta = opening(total_ref)
     a, b, g = scale / (alpha * beta), scale * alpha / beta, scale * beta / alpha
     spec = spec_ref[...]
     s, su = [], []
-    for ref, old_ref in zip((here_ref, pair_ref, middle_ref), old_refs):
+    for ref, old_ref in zip((here_ref, pair_ref, mirror_ref), old_refs):
         old = old_ref[body, :]
-        su.append(ref[body, :] * a - old * b)
+        new = ref[body, :] * flag_ref[2] if ref is mirror_ref else ref[body, :]
+        su.append(new * a - old * b)
         s.append(su[-1] - old * g)
     zu = pulled_ref[body, :] * a - old_z_ref[body, :] * b
     z = zu - old_z_ref[body, :] * g
     before, after = sides(flag_ref[0] > 0.5, s[1], s[2])
-    now, later = plane_delayed(before, s[0], after, spec, forward, last, 2)
-    out_ref[body, :] = plane_advanced(now, later * flag_ref[1], spec, forward, first, 2)
+    now, later = plane_delayed(before, s[0], after, spec, forward[...], last[...], 2)
+    out_ref[body, :] = plane_advanced(now, later * flag_ref[1], spec, forward[...], first[...], 2)
     out_ref[tail, :] = jnp.concatenate(
         [lanes(z, s[0]), lanes(now, now), lanes(zu, s[0]), jnp.zeros((NOTE - 3, rows), F32)], axis=0
     )
@@ -946,9 +971,9 @@
         kept_ref[pl.ds(i * hours, hours), :] = value
 
 
-def plane_step(flags, sums, two, mirror, old, pulled, old_z, old_now, spec, mats):
+def plane_step(flags, sums, two, old, pulled, old_z, old_now, spec, mats):
     height, rows = pulled.shape
-    args = [flags, *sums, two, mirror, *old, pulled, old_z, old_now, spec, *mats]
+    args = [flags, *sums, two, *old, pulled, old_z, old_now, spec, *mats]
     return pl.pallas_call(
         plane_step_kernel,
         in_specs=[pl.BlockSpec(memory_space=pltpu.SMEM)]
@@ -964,16 +989,13 @@
     )(*args)
 
 
-def plane_close_kernel(flag_ref, here_ref, pair_ref, middle_ref, pulled_ref, kept_ref, spec_ref, *refs):
-    mats, (out_ref,) = refs[:9], refs[9:]
-    forward, last = mats[0:3], mats[6:9]
+def plane_close_kernel(here_ref, before_ref, pulled_ref, kept_ref, spec_ref, forward, last, out_ref):
     height, rows = pulled_ref.shape
     hours = height - NOTE
     body = pl.ds(0, hours)
-    before, after = sides(flag_ref[0] > 0.5, pair_ref[body, :], middle_ref[body, :])
     here = here_ref[body, :]
-    waves = product(forward, jnp.concatenate([before, here], axis=0), 2)
-    now = product(last, turn(waves, spec_ref[...], 1.0), 2)
+    waves = product(forward[...], jnp.concatenate([before_ref[body, :], here], axis=0), 2)
+    now = product(last[...], turn(waves, spec_ref[...], 1.0), 2)
     s, su, z, zu, old_now, old_now_u = (kept_ref[pl.ds(i * hours, hours), :] for i in range(6))
     raw = pulled_ref[body, :]
     note = [pulled_ref[hours + i : hours + i + 1, :] for i in range(3)]
@@ -990,18 +1012,15 @@
     out_ref[...] = jnp.broadcast_to(note[None], out_ref.shape)
 
 
-def plane_close(flags, sums, pulled, kept, spec, mats):
+def plane_close(sums, pulled, kept, spec, mats):
     rows = pulled.shape[1]
-    args = [flags, *sums, pulled, kept, spec, *mats]
     return pl.pallas_call(
         plane_close_kernel,
-        in_specs=[pl.BlockSpec(memory_space=pltpu.SMEM)]
-        + [pl.BlockSpec(memory_space=pltpu.VMEM)] * (len(args) - 1),
         out_shape=jax.ShapeDtypeStruct((Z_ * X_ * Y_ * C_, 8, rows // 2), F32),
         compiler_params=params(),
         name="plane_close",
         cost_estimate=SMALL,
-    )(*args)
+    )(*sums, pulled, kept, spec, *mats)
 
 
 def plane_weights(open_ref, close):
@@ -1048,10 +1067,11 @@
     close = jnp.sum(close_ref[...], axis=0)[0:1, :]
     weights = plane_weights(open_ref, close)
     mine = sum(ref[...] * e for ref, e in zip(parts[:3], weights))
-    skip = parts[3].shape[0] - mine.shape[1] // rows * hours
-    for i in range(mine.shape[1] // rows):
-        here = pl.ds(skip + i * hours, hours)
-        other = sum(ref[here, :] * e for ref, e in zip(parts[3:], weights))
+    count = mine.shape[1] // rows
+    for i in range(count):
+        other = 0.0
+        for ref, e in zip(parts[3:], weights):
+            other = other + ref[pl.ds(ref.shape[0] - (count - i) * hours, hours), :] * e
         out_ref[pl.ds(i * rows, rows), :] = jnp.transpose(mine[:, i * rows : (i + 1) * rows] + other)
 
 
@@ -1071,10 +1091,9 @@
     weights = inc_ref[...].astype(F32).astype(BF16)
     for b in range(blocks):
         here = pl.ds(b * width, width)
-        added = sum(
-            lax.dot_general(weights[b], piece, (((0,), (0,)), ((), ())), preferred_element_type=F32)
-            for piece in pieces(rows_ref[pl.ds(b * slots, slots), :], 2)
-        )
+        rows = jnp.concatenate(pieces(rows_ref[pl.ds(b * slots, slots), :], 2), axis=0)
+        twice = jnp.concatenate([weights[b]] * 2, axis=0)
+        added = lax.dot_general(twice, rows, (((0,), (0,)), ((), ())), preferred_element_type=F32)
         out_ref[here, :] = field_ref[here, :] + added
 
 
@@ -1104,9 +1123,10 @@
     place = 2 * y + x
     first = jnp.stack([4 * c + (place ^ m) for m in range(4)] + [4 * c + place, 4 * (1 - c) + place])
     first = (first * rows).astype(jnp.int32)
-    flags = jnp.stack([1 - z % 2, (z < Z_ - 1).astype(z.dtype)]).astype(F32)
-    forward, inverse_first, inverse_last = turned_transforms()
-    mats = [*forward, *inverse_first, *inverse_last]
+    flags = jnp.stack([1 - z % 2, (z < Z_ - 1).astype(z.dtype), (z > 0).astype(z.dtype)]).astype(F32)
+    forward, inverse_first, inverse_last, _ = turned_transforms(2)
+    forward3, _, inverse_last3, short3 = turned_transforms(3)
+    mats = [forward, inverse_first, inverse_last]
 
     meta = describe(incidence, row_gauge, gauge_kernel)
     meta, field = lax.optimization_barrier((meta, first_guess))
@@ -1115,7 +1135,7 @@
     metas = [meta, moved(meta, over_core)]
     both = jnp.concatenate(metas, axis=1)
     around = [both] + [moved(both, where) for where in SQUARE]
-    spec = plane_spectrum(meta, kernels, forward, rows)
+    spec = plane_spectrum(meta, kernels, short3, rows)
     seen, parcel, around, spec = lax.optimization_barrier((observed, parcel, around, spec))
     seen_later = moved(seen, to_plane_before)
     seen = moved(seen, to_plane)
@@ -1126,31 +1146,39 @@
     coupled = plane_couple(first, around[:2], rows)
     coupled, sums = lax.optimization_barrier((coupled, sums))
     coupling = plane_couple(first, around[2:], rows, coupled)
-    pulled = [plane_first(flags, sums, seen, seen_later, spec, mats)]
-
-    slot_rows, slot_rows_other, mixes = [], [], []
+    pulled = [
+        plane_first(
+            flags, sums, seen, seen_later, spec, [forward3, inverse_last3, forward, inverse_first]
+        )
+    ]
+
+    mine_rows, other_rows, extra, mixes = [], [], [], []
     for k in range(3):
         values = [pulled[k]] + [moved(pulled[k], where) for where in SQUARE]
-        mine, other, picked = plane_mix(first, coupling, metas, values)
+        mine, other = plane_mix(coupling, values, extra)
         beside = moved(other, over_core)
-        slot_rows.append(picked)
-        slot_rows_other.append(beside)
         mixed = mine + beside[: hours + NOTE]
-        sums = [mixed, moved(mixed, z_pair), moved(mixed, z_middle)]
-        mixes.append(sums)
+        if k:
+            other_rows.append(beside)
+        picked, theirs = plane_rows(first, metas, values)
+        mine_rows.append(picked)
+        extra = [theirs]
         if k == 0:
-            following, now = plane_open(flags, sums, pulled[0], spec, mats)
+            mixes = [mixed, moved(mixed, z_pair), moved(mixed, z_middle)]
+            following, now = plane_open(flags, mixes, pulled[0], spec, mats)
         elif k == 1:
-            note = mixed[hours:]
-            two, mirror = moved(note, z_two), moved(note, z_mirror)
+            sums = [mixed, moved(mixed, z_pair), moved(mixed, z_mirror)]
+            two = moved(mixed[hours:], z_two)
             open_note, following, state = plane_step(
-                flags, sums, two, mirror, mixes[0], pulled[1], pulled[0], now, spec, mats
+                flags, sums, two, mixes, pulled[1], pulled[0], now, spec, mats
             )
         else:
-            note = plane_close(flags, sums, pulled[2], state, spec, mats)
+            sums = [mixed, moved(mixed, z_next)]
+            note = plane_close(sums, pulled[2], state, spec, [forward, inverse_last])
+            other_rows.append(moved(theirs, over_core))
         pulled.append(following)
     close_note = lax.all_to_all(note, ("basin", "tm"), 0, 0, tiled=False)
-    answer = moved(plane_combine(open_note, close_note, slot_rows, slot_rows_other), from_plane)
+    answer = moved(plane_combine(open_note, close_note, mine_rows, other_rows), from_plane)
     return plane_finish(answer, incidence, first_guess)
 
 

time: 152 us -> 151 us (level)
  blocking collectives: 12.2 us -> 0 us
  waiting for transfers between devices: 49.9 us -> 58.2 us
  local copies, waits for them, and re-layouts: 4.1 us -> 7.62 us
    all_to_all x1 -> x0, blocking collectives: 12.2 us -> none  [plane_shards(): close_note = lax.all_to_all(note, ('basin', 'tm'), 0, 0, tiled=False)]
    all_to_all x0 -> x1, waiting for transfers between devices: none -> 8.18 us  [plane_shards(): close_note = lax.all_to_all(note, ('basin', 'tm'), 0, 0, tiled=False)]
    all_to_all x0 -> x1, starting transfers between devices: none -> 5.62 us  [plane_shards(): close_note = lax.all_to_all(note, ('basin', 'tm'), 0, 0, tiled=False)]
    ppermute x35 -> x34, starting transfers between devices: 52.4 us -> 47.1 us  [moved(): return lax.ppermute(value, ('basin', 'tm'), pairs)]
    unnamed x35 -> x41, local copies, waits for them, and re-layouts: 4.01 us -> 7.53 us
    pallas_call x4 -> x7, Pallas kernels: 6.53 us -> 7.58 us  [the longest x3 4.49 us: plane_rows(): pl.pallas_call(plane_rows_kernel, in_specs=[pl.BlockSpec(memory_space=plt...]
    ppermute x35 -> x34, waiting for transfers between devices: 49.9 us -> 50 us  [moved(): return lax.ppermute(value, ('basin', 'tm'), pairs)]
  transfers between devices with their start and end apart: 35 -> 35, of which waited for: 21 -> 20; matrix products, arithmetic and copies ran while one was open for 0% -> 0% of each run, Pallas kernels for 7% -> 11%
where the time goes in v9:
time: 151 us; the launch traced here: 150 us
  waiting for transfers between devices  58.2 us (39%)
  starting transfers between devices  52.8 us (35%)
  Pallas kernels  30.9 us (20%)
  local copies, waits for them, and re-layouts  7.62 us (5%)
    ppermute x34, waiting for transfers between devices, moved(): return lax.ppermute(value, ('basin', 'tm'), pairs)  50 us
    ppermute x34, starting transfers between devices, moved(): return lax.ppermute(value, ('basin', 'tm'), pairs)  47.1 us
    pallas_call x2, Pallas kernels, plane_couple(): pl.pallas_call(functools.partial(plane_couple_kernel, last), in_specs=[pl...  9.56 us
    all_to_all x1, waiting for transfers between devices, plane_shards(): close_note = lax.all_to_all(note, ('basin', 'tm'), 0, 0, tiled=False)  8.18 us
    unnamed x41, local copies, waits for them, and re-layouts  7.53 us
    all_to_all x1, starting transfers between devices, plane_shards(): close_note = lax.all_to_all(note, ('basin', 'tm'), 0, 0, tiled=False)  5.62 us
    pallas_call x3, Pallas kernels, plane_rows(): pl.pallas_call(plane_rows_kernel, in_specs=[pl.BlockSpec(memory_space=plt...  4.49 us
  transfers between devices with their start and end apart: 35, of which 20 were waited for; matrix products, arithmetic and copies ran while one was open for 0% of the time, Pallas kernels for 11%

profile of v9, /device:TPU:1, one launch (start us, length us, event | category | flops | bytes accessed | tf_op | source)
XLA Modules:
  0.0 150.0 jit_solution(18298032235175303922)
XLA Ops:
  2.5 4.6 %collective-permute-start.1 = (f32[24,512]{1,0:T(8,128)S(1)}, f32[24,512]{1,0:T(8,128)S(1)}, u32[]{:S(2)}, u32[]{:S(2)}) collective-permute-start(f32[24,512]{1,0:T(8,128)S(1)} %describe.1), channel_id=1, source_target_pairs={{0,0},{1,8},{2,16},{3,24},{4,4},{5,12},{6,20},{7,28},{8,2},{9,10},... | collective-permute-start | bytes 147464 | tf_op jit(solution)/shard_map/ppermute | solution.py:502
  7.1 1.6 %copy-done = f32[4096,128]{1,0:T(8,128)S(1)} copy-done((f32[4096,128]{1,0:T(8,128)S(1)}, f32[4096,128]{1,0:T(8,128)}, u32[]{:S(2)}) %copy-start) | copy-done | bytes 2097176
  10.1 3.3 %collective-permute-start = (f32[128,512]{1,0:T(8,128)S(1)}, f32[128,512]{1,0:T(8,128)S(1)}, u32[]{:S(2)}, u32[]{:S(2)}) collective-permute-start(f32[128,512]{1,0:T(8,128)S(1)} %send.1), channel_id=1, source_target_pairs={{0,0},{1,8},{2,16},{3,24},{4,4},{5,12},{6,20},{7,28},{8,2},{9,10},... | collective-permute-start | bytes 786440 | tf_op jit(solution)/shard_map/ppermute | solution.py:502
  16.0 2.4 %collective-permute-start.4 = (f32[24,1024]{1,0:T(8,128)S(1)}, f32[24,1024]{1,0:T(8,128)S(1)}, u32[]{:S(2)}, u32[]{:S(2)}) collective-permute-start(f32[24,1024]{1,0:T(8,128)S(1)} %constant_dynamic-update-slice_fusion.refs_0_), channel_id=1, source_target_pairs={{0,2},{1,3},{2,0},{3,1},{4,6},{5,7},{6,4},{7,5},{8,10},{9,11},{10,... | collective-permute-start | bytes 294920 | tf_op jit(solution)/shard_map/ppermute | solution.py:502
  19.0 7.8 %collective-permute-done.4.refs_0_ = f32[24,1024]{1,0:T(8,128)S(1)} collective-permute-done((f32[24,1024]{1,0:T(8,128)S(1)}, f32[24,1024]{1,0:T(8,128)S(1)}, u32[]{:S(2)}, u32[]{:S(2)}) %collective-permute-start.4) | collective-permute-done | bytes 98336 | tf_op jit(solution)/shard_map/ppermute | solution.py:502
  28.5 1.6 %spread.1 = (f32[128,256]{1,0:T(8,128)S(1)}, f32[128,256]{1,0:T(8,128)S(1)}, f32[128,256]{1,0:T(8,128)S(1)}, f32[128,256]{1,0:T(8,128)S(1)}) custom-call(s32[6]{0:T(128)S(1)} %broadcast_multiply_fusion.first_ref, f32[128,512]{1,0:T(8,128)S(1)} %collective-permute-done.mine_ref, f32[128,512]{1,0:T(8,128)S(1)} %collective-permute-done.6.other_ref, ...), custom_call_target="tpu_custom_call" | custom-call | flops 1 | bytes 1 | tf_op jit(solution)/shard_map/spread/pallas_call | solution.py:695
  30.1 3.1 %collective-permute-start.9 = (f32[128,256]{1,0:T(8,128)S(1)}, f32[128,256]{1,0:T(8,128)S(1)}, u32[]{:S(2)}, u32[]{:S(2)}) collective-permute-start(f32[128,256]{1,0:T(8,128)S(1)} %get-tuple-element.51), channel_id=1, source_target_pairs={{0,6},{1,7},{2,4},{3,5},{4,2},{5,3},{6,0},{7,1},{8,14},{9,15},{10,... | collective-permute-start | bytes 393224 | tf_op jit(solution)/shard_map/ppermute | solution.py:502
  33.7 1.9 %collective-permute-start.12 = (f32[256,128]{1,0:T(8,128)S(1)}, f32[256,128]{1,0:T(8,128)S(1)}, u32[]{:S(2)}, u32[]{:S(2)}) collective-permute-start(f32[256,128]{1,0:T(8,128)S(1)} %copy-done.19), channel_id=1, source_target_pairs={{0,0},{1,8},{2,16},{3,24},{4,4},{5,12},{6,20},{7,28},{8,2},{9,10},... | collective-permute-start | bytes 393224 | tf_op jit(solution)/shard_map/ppermute | solution.py:502
  35.6 1.9 %collective-permute-start.13 = (f32[256,128]{1,0:T(8,128)S(1)}, f32[256,128]{1,0:T(8,128)S(1)}, u32[]{:S(2)}, u32[]{:S(2)}) collective-permute-start(f32[256,128]{1,0:T(8,128)S(1)} %copy-done.19), channel_id=1, source_target_pairs={{1,0},{2,8},{3,16},{5,4},{6,12},{7,20},{9,2},{10,10},{11,18},{13,6... | collective-permute-start | bytes 393224 | tf_op jit(solution)/shard_map/ppermute | solution.py:502
  37.5 2.0 %collective-permute-done.7 = f32[128,256]{1,0:T(8,128)S(1)} collective-permute-done((f32[128,256]{1,0:T(8,128)S(1)}, f32[128,256]{1,0:T(8,128)S(1)}, u32[]{:S(2)}, u32[]{:S(2)}) %collective-permute-start.7) | collective-permute-done | bytes 131104 | tf_op jit(solution)/shard_map/ppermute | solution.py:502
  39.7 1.6 %collective-permute-start.10 = (f32[128,256]{1,0:T(8,128)S(1)}, f32[128,256]{1,0:T(8,128)S(1)}, u32[]{:S(2)}, u32[]{:S(2)}) collective-permute-start(f32[128,256]{1,0:T(8,128)S(1)} %add_add_fusion.here_ref), channel_id=1, source_target_pairs={{0,8},{1,9},{2,10},{3,11},{4,12},{5,13},{6,14},{7,15},{8,0},{9,1},... | collective-permute-start | bytes 393224 | tf_op jit(solution)/shard_map/ppermute | solution.py:502
  42.0 4.6 %plane_couple.2.refs_2_ = f32[1024,512]{1,0:T(8,128)S(1)} custom-call(s32[6]{0:T(128)S(1)} %broadcast_multiply_fusion.first_ref, f32[24,1024]{1,0:T(8,128)S(1)} %constant_dynamic-update-slice_fusion.refs_0_, f32[24,1024]{1,0:T(8,128)S(1)} %collective-permute-done.3.refs_1_), custom_call_target="tpu_custom_call" | custom-call | flops 2147483648 | bytes 2000000 | tf_op jit(solution)/shard_map/plane_couple/pallas_call | solution.py:762
  46.7 4.3 %collective-permute-done.10.pair_ref = f32[128,256]{1,0:T(8,128)S(1)} collective-permute-done((f32[128,256]{1,0:T(8,128)S(1)}, f32[128,256]{1,0:T(8,128)S(1)}, u32[]{:S(2)}, u32[]{:S(2)}) %collective-permute-start.10) | collective-permute-done | bytes 131104 | tf_op jit(solution)/shard_map/ppermute | solution.py:502
  51.1 2.2 %plane_first.1.a_ref.pulled_ref.refs_4_ = f32[136,256]{1,0:T(8,128)S(1)} custom-call(f32[3]{0:T(128)S(1)} %add_convert_fusion.flag_ref, f32[128,256]{1,0:T(8,128)S(1)} %add_add_fusion.here_ref, f32[128,256]{1,0:T(8,128)S(1)} %collective-permute-done.10.pair_ref, f32[128,256]{1,0:T(8,128)S(1)} %collective-permute-done.11.middle_ref, ...), custom_call_target="tpu_custom_call" | custom-call | flops 1 | bytes 1 | tf_op jit(solution)/shard_map/plane_first/pallas_call | solution.py:888
  56.0 4.9 %plane_couple.3 = (bf16[1024,512]{1,0:T(8,128)(2,1)S(1)}, bf16[1024,512]{1,0:T(8,128)(2,1)S(1)}) custom-call(s32[6]{0:T(128)S(1)} %broadcast_multiply_fusion.first_ref, f32[24,1024]{1,0:T(8,128)S(1)} %collective-permute-done.4.refs_0_, f32[24,1024]{1,0:T(8,128)S(1)} %collective-permute-done.5.refs_1_, f32[1024,512]{1,0:T(8,128)S(1)} %plane_couple.2.refs_2_), custom_call_target="tpu_custom_call" | custom-call | flops 2147483648 | bytes 2000000 | tf_op jit(solution)/shard_map/plane_couple/pallas_call | solution.py:762
  66.3 4.0 %collective-permute-done.18.pair_ref.refs_1_ = f32[136,256]{1,0:T(8,128)S(1)} collective-permute-done((f32[136,256]{1,0:T(8,128)S(1)}, f32[136,256]{1,0:T(8,128)S(1)}, u32[]{:S(2)}, u32[]{:S(2)}) %collective-permute-start.18) | collective-permute-done | bytes 139296 | tf_op jit(solution)/shard_map/ppermute | solution.py:502
  70.3 1.8 %plane_open.1 = (f32[136,256]{1,0:T(8,128)S(1)}, f32[128,256]{1,0:T(8,128)S(1)}) custom-call(f32[3]{0:T(128)S(1)} %add_convert_fusion.flag_ref, f32[136,256]{1,0:T(8,128)S(1)} %add.61.here_ref.refs_0_, f32[136,256]{1,0:T(8,128)S(1)} %collective-permute-done.18.pair_ref.refs_1_, f32[136,256]{1,0:T(8,128)S(1)} %collective-permute-done.19.middle_ref.refs_2_, ...), custom_call_target="tpu_custom_call" | custom-call | flops 1 | bytes 1 | tf_op jit(solution)/shard_map/plane_open/pallas_call | solution.py:924
  76.3 2.7 %collective-permute-done.22.d_ref = f32[136,256]{1,0:T(8,128)S(1)} collective-permute-done((f32[136,256]{1,0:T(8,128)S(1)}, f32[136,256]{1,0:T(8,128)S(1)}, u32[]{:S(2)}, u32[]{:S(2)}) %collective-permute-start.22) | collective-permute-done | bytes 139296 | tf_op jit(solution)/shard_map/ppermute | solution.py:502
  79.6 2.9 %collective-permute-start.23 = (f32[392,256]{1,0:T(8,128)S(1)}, f32[392,256]{1,0:T(8,128)S(1)}, u32[]{:S(2)}, u32[]{:S(2)}) collective-permute-start(f32[392,256]{1,0:T(8,128)S(1)} %get-tuple-element.65), channel_id=1, source_target_pairs={{0,1},{1,0},{2,3},{3,2},{4,5},{5,4},{6,7},{7,6},{8,9},{9,8},{10,11... | collective-permute-start | bytes 1204232 | tf_op jit(solution)/shard_map/ppermute | solution.py:502
  83.9 3.2 %collective-permute-start.24 = (f32[136,256]{1,0:T(8,128)S(1)}, f32[136,256]{1,0:T(8,128)S(1)}, u32[]{:S(2)}, u32[]{:S(2)}) collective-permute-start(f32[136,256]{1,0:T(8,128)S(1)} %slice_add_fusion.1.here_ref), channel_id=1, source_target_pairs={{0,8},{1,9},{2,10},{3,11},{4,12},{5,13},{6,14},{7,15},{8,0},{9,1},... | collective-permute-start | bytes 417800 | tf_op jit(solution)/shard_map/ppermute | solution.py:502
  88.4 4.6 %collective-permute-done.26.two_ref = f32[8,256]{1,0:T(8,128)S(1)} collective-permute-done((f32[8,256]{1,0:T(8,128)S(1)}, f32[8,256]{1,0:T(8,128)S(1)}, u32[]{:S(2)}, u32[]{:S(2)}) %collective-permute-start.26) | collective-permute-done | bytes 8224 | tf_op jit(solution)/shard_map/ppermute | solution.py:502
  93.0 1.7 %collective-permute-done.25.mirror_ref = f32[136,256]{1,0:T(8,128)S(1)} collective-permute-done((f32[136,256]{1,0:T(8,128)S(1)}, f32[136,256]{1,0:T(8,128)S(1)}, u32[]{:S(2)}, u32[]{:S(2)}) %collective-permute-start.25) | collective-permute-done | bytes 139296 | tf_op jit(solution)/shard_map/ppermute | solution.py:502
  94.7 2.0 %plane_step.1 = (f32[8,256]{1,0:T(8,128)S(1)}, f32[136,256]{1,0:T(8,128)S(1)}, f32[768,256]{1,0:T(8,128)S(1)}) custom-call(f32[3]{0:T(128)S(1)} %add_convert_fusion.flag_ref, f32[136,256]{1,0:T(8,128)S(1)} %slice_add_fusion.1.here_ref, f32[136,256]{1,0:T(8,128)S(1)} %collective-permute-done.24.pair_ref, f32[136,256]{1,0:T(8,128)S(1)} %collective-permute-done.25.mirror_ref, ...), custom_call_target="tpu_custom_call" | custom-call | flops 1 | bytes 1 | tf_op jit(solution)/shard_map/plane_step/pallas_call | solution.py:977
  101.9 3.1 %collective-permute-done.29.d_ref = f32[136,256]{1,0:T(8,128)S(1)} collective-permute-done((f32[136,256]{1,0:T(8,128)S(1)}, f32[136,256]{1,0:T(8,128)S(1)}, u32[]{:S(2)}, u32[]{:S(2)}) %collective-permute-start.29) | collective-permute-done | bytes 139296 | tf_op jit(solution)/shard_map/ppermute | solution.py:502
  105.5 2.3 %collective-permute-start.30 = (f32[392,256]{1,0:T(8,128)S(1)}, f32[392,256]{1,0:T(8,128)S(1)}, u32[]{:S(2)}, u32[]{:S(2)}) collective-permute-start(f32[392,256]{1,0:T(8,128)S(1)} %get-tuple-element.71), channel_id=1, source_target_pairs={{0,1},{1,0},{2,3},{3,2},{4,5},{5,4},{6,7},{7,6},{8,9},{9,8},{10,11... | collective-permute-start | bytes 1204232 | tf_op jit(solution)/shard_map/ppermute | solution.py:502
  109.2 2.1 %collective-permute-start.31 = (f32[136,256]{1,0:T(8,128)S(1)}, f32[136,256]{1,0:T(8,128)S(1)}, u32[]{:S(2)}, u32[]{:S(2)}) collective-permute-start(f32[136,256]{1,0:T(8,128)S(1)} %slice_add_fusion.here_ref), channel_id=1, source_target_pairs={{0,8},{1,9},{2,10},{3,11},{4,12},{5,13},{6,14},{7,15},{8,16},{9,17... | collective-permute-start | bytes 417800 | tf_op jit(solution)/shard_map/ppermute | solution.py:502
  111.4 2.0 %plane_rows.5 = (f32[128,512]{1,0:T(8,128)S(1)}, f32[256,256]{1,0:T(8,128)}) custom-call(s32[6]{0:T(128)S(1)} %broadcast_multiply_fusion.first_ref, f32[24,512]{1,0:T(8,128)S(1)} %collective-permute-done.1.class_ref.meta_ref, f32[24,512]{1,0:T(8,128)S(1)} %collective-permute-done.2.meta_other_ref, f32[136,256]{1,0:T(8,128)S(1)} %get-tuple-element.68.a_ref.pulled_ref, ...), custom_call_target="tpu_custom_call" | custom-call | flops 1000000000 | bytes 2000000 | tf_op jit(solution)/shard_map/plane_rows/pallas_call | solution.py:830
  116.1 5.6 %all-to-all-start = ((f32[32,8,128]{2,1,0:T(8,128)}), f32[32,8,128]{2,1,0:T(8,128)S(1)}, u32[]{:S(2)}, u32[]{:S(2)}) async-start(f32[32,8,128]{2,1,0:T(8,128)} %plane_close.1), calls=%async_computation | async-start | bytes 262144 | tf_op jit(solution)/shard_map/all_to_all | solution.py:1180
  121.7 8.2 %all-to-all-done.close_ref = f32[32,8,128]{2,1,0:T(8,128)S(1)} async-done(((f32[32,8,128]{2,1,0:T(8,128)}), f32[32,8,128]{2,1,0:T(8,128)S(1)}, u32[]{:S(2)}, u32[]{:S(2)}) %all-to-all-start) | async-done | bytes 131104 | tf_op jit(solution)/shard_map/all_to_all | solution.py:1180
  134.3 2.6 %collective-permute-start.33 = (f32[512,128]{1,0:T(8,128)S(1)}, f32[512,128]{1,0:T(8,128)S(1)}, u32[]{:S(2)}, u32[]{:S(2)}) collective-permute-start(f32[512,128]{1,0:T(8,128)S(1)} %plane_combine.1), channel_id=1, source_target_pairs={{0,0},{1,16},{2,8},{3,24},{4,4},{5,20},{6,12},{7,28},{8,1},{9,17},... | collective-permute-start | bytes 786440 | tf_op jit(solution)/shard_map/ppermute | solution.py:502
  136.9 10.7 %collective-permute-done.33.rows_ref = f32[512,128]{1,0:T(8,128)S(1)} collective-permute-done((f32[512,128]{1,0:T(8,128)S(1)}, f32[512,128]{1,0:T(8,128)S(1)}, u32[]{:S(2)}, u32[]{:S(2)}) %collective-permute-start.33) | collective-permute-done | bytes 262176 | tf_op jit(solution)/shard_map/ppermute | solution.py:502
  147.6 2.4 %plane_finish.1 = f32[4096,128]{1,0:T(8,128)} custom-call(f32[512,128]{1,0:T(8,128)S(1)} %collective-permute-done.33.rows_ref, s32[32,16,128]{2,1,0:T(8,128)S(1)} %copy-done.4, f32[4096,128]{1,0:T(8,128)S(1)} %copy-done.1), custom_call_target="tpu_custom_call" | custom-call | tf_op jit(solution)/shard_map/plane_finish/pallas_call | solution.py:1104
  (106 shorter events, 39.6 us)
Async XLA Ops:
  2.5 10.9 %collective-permute-start.1 = (f32[24,512]{1,0:T(8,128)S(1)}, f32[24,512]{1,0:T(8,128)S(1)}, u32[]{:S(2)}, u32[]{:S(2)}) collective-permute-start(f32[24,512]{1,0:T(8,128)S(1)} %describe.1), channel_id=1, source_target_pairs={{0,0},{1,8},{2,16},{3,24},{4,4},{5,12},{6,20},{7,28},{8,2},{9,10},... | collective-permute-start | bytes 147464 | tf_op jit(solution)/shard_map/ppermute | solution.py:502
  10.1 16.9 %collective-permute-start = (f32[128,512]{1,0:T(8,128)S(1)}, f32[128,512]{1,0:T(8,128)S(1)}, u32[]{:S(2)}, u32[]{:S(2)}) collective-permute-start(f32[128,512]{1,0:T(8,128)S(1)} %send.1), channel_id=1, source_target_pairs={{0,0},{1,8},{2,16},{3,24},{4,4},{5,12},{6,20},{7,28},{8,2},{9,10},... | collective-permute-start | bytes 786440 | tf_op jit(solution)/shard_map/ppermute | solution.py:502
  14.8 4.2 %collective-permute-start.3 = (f32[24,1024]{1,0:T(8,128)S(1)}, f32[24,1024]{1,0:T(8,128)S(1)}, u32[]{:S(2)}, u32[]{:S(2)}) collective-permute-start(f32[24,1024]{1,0:T(8,128)S(1)} %constant_dynamic-update-slice_fusion.refs_0_), channel_id=1, source_target_pairs={{0,4},{1,5},{2,6},{3,7},{4,0},{5,1},{6,2},{7,3},{8,12},{9,13},{10,... | collective-permute-start | bytes 294920 | tf_op jit(solution)/shard_map/ppermute | solution.py:502
  16.0 10.9 %collective-permute-start.4 = (f32[24,1024]{1,0:T(8,128)S(1)}, f32[24,1024]{1,0:T(8,128)S(1)}, u32[]{:S(2)}, u32[]{:S(2)}) collective-permute-start(f32[24,1024]{1,0:T(8,128)S(1)} %constant_dynamic-update-slice_fusion.refs_0_), channel_id=1, source_target_pairs={{0,2},{1,3},{2,0},{3,1},{4,6},{5,7},{6,4},{7,5},{8,10},{9,11},{10,... | collective-permute-start | bytes 294920 | tf_op jit(solution)/shard_map/ppermute | solution.py:502
  18.4 8.4 %collective-permute-start.5 = (f32[24,1024]{1,0:T(8,128)S(1)}, f32[24,1024]{1,0:T(8,128)S(1)}, u32[]{:S(2)}, u32[]{:S(2)}) collective-permute-start(f32[24,1024]{1,0:T(8,128)S(1)} %constant_dynamic-update-slice_fusion.refs_0_), channel_id=1, source_target_pairs={{0,6},{1,7},{2,4},{3,5},{4,2},{5,3},{6,0},{7,1},{8,14},{9,15},{10,... | collective-permute-start | bytes 294920 | tf_op jit(solution)/shard_map/ppermute | solution.py:502
  30.1 7.4 %collective-permute-start.9 = (f32[128,256]{1,0:T(8,128)S(1)}, f32[128,256]{1,0:T(8,128)S(1)}, u32[]{:S(2)}, u32[]{:S(2)}) collective-permute-start(f32[128,256]{1,0:T(8,128)S(1)} %get-tuple-element.51), channel_id=1, source_target_pairs={{0,6},{1,7},{2,4},{3,5},{4,2},{5,3},{6,0},{7,1},{8,14},{9,15},{10,... | collective-permute-start | bytes 393224 | tf_op jit(solution)/shard_map/ppermute | solution.py:502
  33.2 6.3 %collective-permute-start.7 = (f32[128,256]{1,0:T(8,128)S(1)}, f32[128,256]{1,0:T(8,128)S(1)}, u32[]{:S(2)}, u32[]{:S(2)}) collective-permute-start(f32[128,256]{1,0:T(8,128)S(1)} %get-tuple-element.49), channel_id=1, source_target_pairs={{0,4},{1,5},{2,6},{3,7},{4,0},{5,1},{6,2},{7,3},{8,12},{9,13},{10,... | collective-permute-start | bytes 393224 | tf_op jit(solution)/shard_map/ppermute | solution.py:502
  33.5 6.2 %collective-permute-start.8 = (f32[128,256]{1,0:T(8,128)S(1)}, f32[128,256]{1,0:T(8,128)S(1)}, u32[]{:S(2)}, u32[]{:S(2)}) collective-permute-start(f32[128,256]{1,0:T(8,128)S(1)} %get-tuple-element.50), channel_id=1, source_target_pairs={{0,2},{1,3},{2,0},{3,1},{4,6},{5,7},{6,4},{7,5},{8,10},{9,11},{10,... | collective-permute-start | bytes 393224 | tf_op jit(solution)/shard_map/ppermute | solution.py:502
  33.7 17.3 %collective-permute-start.12 = (f32[256,128]{1,0:T(8,128)S(1)}, f32[256,128]{1,0:T(8,128)S(1)}, u32[]{:S(2)}, u32[]{:S(2)}) collective-permute-start(f32[256,128]{1,0:T(8,128)S(1)} %copy-done.19), channel_id=1, source_target_pairs={{0,0},{1,8},{2,16},{3,24},{4,4},{5,12},{6,20},{7,28},{8,2},{9,10},... | collective-permute-start | bytes 393224 | tf_op jit(solution)/shard_map/ppermute | solution.py:502
  35.6 15.4 %collective-permute-start.13 = (f32[256,128]{1,0:T(8,128)S(1)}, f32[256,128]{1,0:T(8,128)S(1)}, u32[]{:S(2)}, u32[]{:S(2)}) collective-permute-start(f32[256,128]{1,0:T(8,128)S(1)} %copy-done.19), channel_id=1, source_target_pairs={{1,0},{2,8},{3,16},{5,4},{6,12},{7,20},{9,2},{10,10},{11,18},{13,6... | collective-permute-start | bytes 393224 | tf_op jit(solution)/shard_map/ppermute | solution.py:502
  39.7 11.3 %collective-permute-start.10 = (f32[128,256]{1,0:T(8,128)S(1)}, f32[128,256]{1,0:T(8,128)S(1)}, u32[]{:S(2)}, u32[]{:S(2)}) collective-permute-start(f32[128,256]{1,0:T(8,128)S(1)} %add_add_fusion.here_ref), channel_id=1, source_target_pairs={{0,8},{1,9},{2,10},{3,11},{4,12},{5,13},{6,14},{7,15},{8,0},{9,1},... | collective-permute-start | bytes 393224 | tf_op jit(solution)/shard_map/ppermute | solution.py:502
  41.4 9.6 %collective-permute-start.11 = (f32[128,256]{1,0:T(8,128)S(1)}, f32[128,256]{1,0:T(8,128)S(1)}, u32[]{:S(2)}, u32[]{:S(2)}) collective-permute-start(f32[128,256]{1,0:T(8,128)S(1)} %add_add_fusion.here_ref), channel_id=1, source_target_pairs={{8,16},{9,17},{10,18},{11,19},{12,20},{13,21},{14,22},{15,23},{16,... | collective-permute-start | bytes 393224 | tf_op jit(solution)/shard_map/ppermute | solution.py:502
  53.3 7.7 %collective-permute-start.14 = (f32[136,256]{1,0:T(8,128)S(1)}, f32[136,256]{1,0:T(8,128)S(1)}, u32[]{:S(2)}, u32[]{:S(2)}) collective-permute-start(f32[136,256]{1,0:T(8,128)S(1)} %plane_first.1.a_ref.pulled_ref.refs_4_), channel_id=1, source_target_pairs={{0,4},{1,5},{2,6},{3,7},{4,0},{5,1},{6,2},{7,3},{8,12},{9,13},{10,... | collective-permute-start | bytes 417800 | tf_op jit(solution)/shard_map/ppermute | solution.py:502
  54.6 7.7 %collective-permute-start.15 = (f32[136,256]{1,0:T(8,128)S(1)}, f32[136,256]{1,0:T(8,128)S(1)}, u32[]{:S(2)}, u32[]{:S(2)}) collective-permute-start(f32[136,256]{1,0:T(8,128)S(1)} %plane_first.1.a_ref.pulled_ref.refs_4_), channel_id=1, source_target_pairs={{0,2},{1,3},{2,0},{3,1},{4,6},{5,7},{6,4},{7,5},{8,10},{9,11},{10,... | collective-permute-start | bytes 417800 | tf_op jit(solution)/shard_map/ppermute | solution.py:502
  54.6 7.7 %collective-permute-start.16 = (f32[136,256]{1,0:T(8,128)S(1)}, f32[136,256]{1,0:T(8,128)S(1)}, u32[]{:S(2)}, u32[]{:S(2)}) collective-permute-start(f32[136,256]{1,0:T(8,128)S(1)} %plane_first.1.a_ref.pulled_ref.refs_4_), channel_id=1, source_target_pairs={{0,6},{1,7},{2,4},{3,5},{4,2},{5,3},{6,0},{7,1},{8,14},{9,15},{10,... | collective-permute-start | bytes 417800 | tf_op jit(solution)/shard_map/ppermute | solution.py:502
  65.4 5.0 %collective-permute-start.18 = (f32[136,256]{1,0:T(8,128)S(1)}, f32[136,256]{1,0:T(8,128)S(1)}, u32[]{:S(2)}, u32[]{:S(2)}) collective-permute-start(f32[136,256]{1,0:T(8,128)S(1)} %add.61.here_ref.refs_0_), channel_id=1, source_target_pairs={{0,8},{1,9},{2,10},{3,11},{4,12},{5,13},{6,14},{7,15},{8,0},{9,1},... | collective-permute-start | bytes 417800 | tf_op jit(solution)/shard_map/ppermute | solution.py:502
  65.4 4.9 %collective-permute-start.19 = (f32[136,256]{1,0:T(8,128)S(1)}, f32[136,256]{1,0:T(8,128)S(1)}, u32[]{:S(2)}, u32[]{:S(2)}) collective-permute-start(f32[136,256]{1,0:T(8,128)S(1)} %add.61.here_ref.refs_0_), channel_id=1, source_target_pairs={{8,16},{9,17},{10,18},{11,19},{12,20},{13,21},{14,22},{15,23},{16,... | collective-permute-start | bytes 417800 | tf_op jit(solution)/shard_map/ppermute | solution.py:502
  72.2 4.0 %collective-permute-start.20 = (f32[136,256]{1,0:T(8,128)S(1)}, f32[136,256]{1,0:T(8,128)S(1)}, u32[]{:S(2)}, u32[]{:S(2)}) collective-permute-start(f32[136,256]{1,0:T(8,128)S(1)} %get-tuple-element.62.a_ref.refs_3_), channel_id=1, source_target_pairs={{0,4},{1,5},{2,6},{3,7},{4,0},{5,1},{6,2},{7,3},{8,12},{9,13},{10,... | collective-permute-start | bytes 417800 | tf_op jit(solution)/shard_map/ppermute | solution.py:502
  72.4 3.9 %collective-permute-start.21 = (f32[136,256]{1,0:T(8,128)S(1)}, f32[136,256]{1,0:T(8,128)S(1)}, u32[]{:S(2)}, u32[]{:S(2)}) collective-permute-start(f32[136,256]{1,0:T(8,128)S(1)} %get-tuple-element.62.a_ref.refs_3_), channel_id=1, source_target_pairs={{0,2},{1,3},{2,0},{3,1},{4,6},{5,7},{6,4},{7,5},{8,10},{9,11},{10,... | collective-permute-start | bytes 417800 | tf_op jit(solution)/shard_map/ppermute | solution.py:502
  73.4 5.6 %collective-permute-start.22 = (f32[136,256]{1,0:T(8,128)S(1)}, f32[136,256]{1,0:T(8,128)S(1)}, u32[]{:S(2)}, u32[]{:S(2)}) collective-permute-start(f32[136,256]{1,0:T(8,128)S(1)} %get-tuple-element.62.a_ref.refs_3_), channel_id=1, source_target_pairs={{0,6},{1,7},{2,4},{3,5},{4,2},{5,3},{6,0},{7,1},{8,14},{9,15},{10,... | collective-permute-start | bytes 417800 | tf_op jit(solution)/shard_map/ppermute | solution.py:502
  79.6 4.3 %collective-permute-start.23 = (f32[392,256]{1,0:T(8,128)S(1)}, f32[392,256]{1,0:T(8,128)S(1)}, u32[]{:S(2)}, u32[]{:S(2)}) collective-permute-start(f32[392,256]{1,0:T(8,128)S(1)} %get-tuple-element.65), channel_id=1, source_target_pairs={{0,1},{1,0},{2,3},{3,2},{4,5},{5,4},{6,7},{7,6},{8,9},{9,8},{10,11... | collective-permute-start | bytes 1204232 | tf_op jit(solution)/shard_map/ppermute | solution.py:502
  83.9 9.1 %collective-permute-start.24 = (f32[136,256]{1,0:T(8,128)S(1)}, f32[136,256]{1,0:T(8,128)S(1)}, u32[]{:S(2)}, u32[]{:S(2)}) collective-permute-start(f32[136,256]{1,0:T(8,128)S(1)} %slice_add_fusion.1.here_ref), channel_id=1, source_target_pairs={{0,8},{1,9},{2,10},{3,11},{4,12},{5,13},{6,14},{7,15},{8,0},{9,1},... | collective-permute-start | bytes 417800 | tf_op jit(solution)/shard_map/ppermute | solution.py:502
  87.1 7.5 %collective-permute-start.25 = (f32[136,256]{1,0:T(8,128)S(1)}, f32[136,256]{1,0:T(8,128)S(1)}, u32[]{:S(2)}, u32[]{:S(2)}) collective-permute-start(f32[136,256]{1,0:T(8,128)S(1)} %slice_add_fusion.1.here_ref), channel_id=1, source_target_pairs={{0,24},{1,25},{2,26},{3,27},{4,28},{5,29},{6,30},{7,31},{8,16},{9,... | collective-permute-start | bytes 417800 | tf_op jit(solution)/shard_map/ppermute | solution.py:502
  88.2 4.8 %collective-permute-start.26 = (f32[8,256]{1,0:T(8,128)S(1)}, f32[8,256]{1,0:T(8,128)S(1)}, u32[]{:S(2)}, u32[]{:S(2)}) collective-permute-start(f32[8,256]{1,0:T(8,128)S(1)} %slice.13), channel_id=1, source_target_pairs={{0,16},{1,17},{2,18},{3,19},{4,20},{5,21},{6,22},{7,23},{8,24},{9,... | collective-permute-start | bytes 24584 | tf_op jit(solution)/shard_map/ppermute | solution.py:502
  96.7 4.0 %collective-permute-start.27 = (f32[136,256]{1,0:T(8,128)S(1)}, f32[136,256]{1,0:T(8,128)S(1)}, u32[]{:S(2)}, u32[]{:S(2)}) collective-permute-start(f32[136,256]{1,0:T(8,128)S(1)} %get-tuple-element.68.a_ref.pulled_ref), channel_id=1, source_target_pairs={{0,4},{1,5},{2,6},{3,7},{4,0},{5,1},{6,2},{7,3},{8,12},{9,13},{10,... | collective-permute-start | bytes 417800 | tf_op jit(solution)/shard_map/ppermute | solution.py:502
  97.7 4.2 %collective-permute-start.28 = (f32[136,256]{1,0:T(8,128)S(1)}, f32[136,256]{1,0:T(8,128)S(1)}, u32[]{:S(2)}, u32[]{:S(2)}) collective-permute-start(f32[136,256]{1,0:T(8,128)S(1)} %get-tuple-element.68.a_ref.pulled_ref), channel_id=1, source_target_pairs={{0,2},{1,3},{2,0},{3,1},{4,6},{5,7},{6,4},{7,5},{8,10},{9,11},{10,... | collective-permute-start | bytes 417800 | tf_op jit(solution)/shard_map/ppermute | solution.py:502
  98.4 6.6 %collective-permute-start.29 = (f32[136,256]{1,0:T(8,128)S(1)}, f32[136,256]{1,0:T(8,128)S(1)}, u32[]{:S(2)}, u32[]{:S(2)}) collective-permute-start(f32[136,256]{1,0:T(8,128)S(1)} %get-tuple-element.68.a_ref.pulled_ref), channel_id=1, source_target_pairs={{0,6},{1,7},{2,4},{3,5},{4,2},{5,3},{6,0},{7,1},{8,14},{9,15},{10,... | collective-permute-start | bytes 417800 | tf_op jit(solution)/shard_map/ppermute | solution.py:502
  105.5 3.7 %collective-permute-start.30 = (f32[392,256]{1,0:T(8,128)S(1)}, f32[392,256]{1,0:T(8,128)S(1)}, u32[]{:S(2)}, u32[]{:S(2)}) collective-permute-start(f32[392,256]{1,0:T(8,128)S(1)} %get-tuple-element.71), channel_id=1, source_target_pairs={{0,1},{1,0},{2,3},{3,2},{4,5},{5,4},{6,7},{7,6},{8,9},{9,8},{10,11... | collective-permute-start | bytes 1204232 | tf_op jit(solution)/shard_map/ppermute | solution.py:502
  109.2 5.5 %collective-permute-start.31 = (f32[136,256]{1,0:T(8,128)S(1)}, f32[136,256]{1,0:T(8,128)S(1)}, u32[]{:S(2)}, u32[]{:S(2)}) collective-permute-start(f32[136,256]{1,0:T(8,128)S(1)} %slice_add_fusion.here_ref), channel_id=1, source_target_pairs={{0,8},{1,9},{2,10},{3,11},{4,12},{5,13},{6,14},{7,15},{8,16},{9,17... | collective-permute-start | bytes 417800 | tf_op jit(solution)/shard_map/ppermute | solution.py:502
  114.0 7.7 %collective-permute-start.32 = (f32[256,256]{1,0:T(8,128)}, f32[256,256]{1,0:T(8,128)}, u32[]{:S(2)}, u32[]{:S(2)}) collective-permute-start(f32[256,256]{1,0:T(8,128)} %get-tuple-element.76), channel_id=1, source_target_pairs={{0,1},{1,0},{2,3},{3,2},{4,5},{5,4},{6,7},{7,6},{8,9},{9,8},{10,11... | collective-permute-start | bytes 786440 | tf_op jit(solution)/shard_map/ppermute | solution.py:502
  116.1 13.8 %all-to-all-start = ((f32[32,8,128]{2,1,0:T(8,128)}), f32[32,8,128]{2,1,0:T(8,128)S(1)}, u32[]{:S(2)}, u32[]{:S(2)}) async-start(f32[32,8,128]{2,1,0:T(8,128)} %plane_close.1), calls=%async_computation | async-start | bytes 262144 | tf_op jit(solution)/shard_map/all_to_all | solution.py:1180
  134.3 13.3 %collective-permute-start.33 = (f32[512,128]{1,0:T(8,128)S(1)}, f32[512,128]{1,0:T(8,128)S(1)}, u32[]{:S(2)}, u32[]{:S(2)}) collective-permute-start(f32[512,128]{1,0:T(8,128)S(1)} %plane_combine.1), channel_id=1, source_target_pairs={{0,0},{1,16},{2,8},{3,24},{4,4},{5,20},{6,12},{7,28},{8,1},{9,17},... | collective-permute-start | bytes 786440 | tf_op jit(solution)/shard_map/ppermute | solution.py:502
  (23 other events, 213.1 us)

commit v10 on v9

--- a/solution.py
+++ b/solution.py
@@ -487,6 +487,7 @@
 
 Z_, X_, Y_, C_ = 4, 2, 2, 2
 NOTE = 8
+HOURS = SPAN // 2
 
 
 def device(z, x, y, c):
@@ -506,9 +507,9 @@
     return 2 * y + c, x, z & 1, z >> 1
 
 
-def to_plane_before(z, x, y, c):
-    t = 2 * y + c
-    return (t - 1, x, z & 1, z >> 1) if t else None
+def hour_before(z, x, y, c):
+    t = 2 * y + c - 1
+    return (z, x, t >> 1, t & 1) if t >= 0 else None
 
 
 def from_plane(z, x, y, c):
@@ -777,16 +778,17 @@
     *extra, mine_ref, other_ref = refs
     refs = (a_ref, b_ref, c_ref, d_ref)
     height, rows = a_ref.shape
-    hours = height - NOTE
-    body, tail = pl.ds(0, hours), pl.ds(hours, NOTE)
+    body = pl.ds(0, HOURS)
     one, two = pieces(jnp.concatenate([ref[body, :] for ref in refs], axis=1), 2)
     both = dot(jnp.concatenate([two, one], axis=0), high_ref[...])
-    result = (both[:hours] + dot(one, low_ref[...])) + both[hours:]
-    note = sum(ref[tail, :] for ref in refs)
+    result = (both[:HOURS] + dot(one, low_ref[...])) + both[HOURS:]
     mine_ref[body, :] = result[:, :rows]
     other_ref[body, :] = result[:, rows:]
-    mine_ref[tail, :] = note
-    other_ref[tail, :] = note
+    if height > HOURS:
+        tail = pl.ds(HOURS, NOTE)
+        note = sum(ref[tail, :] for ref in refs)
+        mine_ref[tail, :] = note
+        other_ref[tail, :] = note
     for ref in extra:
         other_ref[pl.ds(height, ref.shape[0]), :] = ref[...]
 
@@ -805,11 +807,14 @@
     )(*coupling, *values, *extra)
 
 
-def plane_rows_kernel(first_ref, meta_ref, meta_other_ref, a_ref, b_ref, c_ref, d_ref, mine_ref, other_ref):
-    refs = (a_ref, b_ref, c_ref, d_ref)
-    height, rows = a_ref.shape
-    hours = height - NOTE
-    one, two = pieces(jnp.concatenate([ref[pl.ds(0, hours), :] for ref in refs], axis=1), 2)
+def plane_rows_kernel(first_ref, meta_ref, meta_other_ref, a_ref, b_ref, c_ref, d_ref, *refs):
+    if len(refs) > 2:
+        *stack, last_ref, beside_ref, mine_ref, other_ref, stack_ref = refs
+    else:
+        mine_ref, other_ref = refs
+    rows = a_ref.shape[1]
+    value = jnp.concatenate([ref[pl.ds(0, HOURS), :] for ref in (a_ref, b_ref, c_ref, d_ref)], axis=1)
+    one, two = pieces(value, 2)
     stacked = jnp.concatenate([two, one], axis=0)
     where = meta_ref.shape[0] - 8
     picked = []
@@ -817,41 +822,56 @@
         gauge = ref[where : where + 1, :]
         hot = jnp.concatenate([hot_rows(gauge, first_ref[m], rows) for m in range(4)], axis=0)
         both = dot(stacked, hot)
-        picked.append(both[:hours] + both[hours:])
+        picked.append(both[:HOURS] + both[HOURS:])
     mine_ref[...] = picked[0]
-    for i in range(picked[1].shape[1] // rows):
-        other_ref[pl.ds(i * hours, hours), :] = picked[1][:, i * rows : (i + 1) * rows]
-
-
-def plane_rows(first, metas, values):
-    height, rows = values[0].shape
-    hours = height - NOTE
+    count = picked[1].shape[1] // rows
+    for i in range(count):
+        other_ref[pl.ds(i * HOURS, HOURS), :] = picked[1][:, i * rows : (i + 1) * rows]
+    if len(refs) > 2:
+        top = stack_ref.shape[0] - HOURS
+        for ref in stack:
+            stack_ref[pl.ds(0, top), :] = ref[...]
+        for i in range(count):
+            here = pl.ds(i * rows, rows)
+            beside = beside_ref[pl.ds(beside_ref.shape[0] - (count - i) * HOURS, HOURS), :]
+            stack_ref[pl.ds(top, HOURS), here] = last_ref[:, here] + beside
+
+
+def plane_rows(first, metas, values, before):
+    rows = values[0].shape[1]
     slots = metas[0].shape[1]
+    args = [first, *metas, *values, *before]
+    shapes = [(HOURS, slots), (slots // rows * HOURS, rows)]
+    if before:
+        shapes.append(((len(before) - 1) * HOURS, slots))
     return pl.pallas_call(
         plane_rows_kernel,
-        in_specs=[pl.BlockSpec(memory_space=pltpu.SMEM)] + [pl.BlockSpec(memory_space=pltpu.VMEM)] * 6,
-        out_shape=[
-            jax.ShapeDtypeStruct((hours, slots), F32),
-            jax.ShapeDtypeStruct((slots // rows * hours, rows), F32),
-        ],
+        in_specs=[pl.BlockSpec(memory_space=pltpu.SMEM)]
+        + [pl.BlockSpec(memory_space=pltpu.VMEM)] * (len(args) - 1),
+        out_shape=[jax.ShapeDtypeStruct(shape, F32) for shape in shapes],
         compiler_params=params(),
         name="plane_rows",
         cost_estimate=pl.CostEstimate(flops=1_000_000_000, bytes_accessed=2_000_000, transcendentals=0),
-    )(first, *metas, *values)
+    )(*args)
+
+
+def gain(kernels):
+    return jnp.max(jnp.sum(kernels, axis=1, keepdims=True), axis=0, keepdims=True)
+
+
+def spectra(kind, kernels, wide):
+    classes = kernels.shape[0]
+    row = lax.broadcasted_iota(jnp.int32, (classes, kind.shape[1]), 0).astype(F32)
+    hot = jnp.where(row == kind, 1.0, 0.0).astype(BF16)
+    taps = jnp.transpose(kernels / gain(kernels))
+    chosen = dot(jnp.concatenate(pieces(taps, 3)[::-1], axis=1), jnp.concatenate([hot] * 3, axis=0))
+    return product(wide, chosen, 3)
 
 
 def plane_spectrum_kernel(class_ref, kernels_ref, wide_ref, out_ref):
-    classes = kernels_ref.shape[0]
     where = class_ref.shape[0] - 7
     kind = class_ref[where : where + 1, : out_ref.shape[1]]
-    hot = jnp.where(
-        lax.broadcasted_iota(jnp.int32, (classes, kind.shape[1]), 0).astype(F32) == kind, 1.0, 0.0
-    ).astype(BF16)
-    chosen = None
-    for piece in reversed(pieces(jnp.transpose(kernels_ref[...]), 3)):
-        term = dot(piece, hot)
-        chosen = term if chosen is None else chosen + term
-    out_ref[...] = product(wide_ref[...], chosen, 3)
+    out_ref[...] = spectra(kind, kernels_ref[...], wide_ref[...])
 
 
 def plane_spectrum(meta, kernels, wide, rows):
@@ -864,147 +884,122 @@
     )(meta, kernels, wide)
 
 
+def observe_kernel(seen_ref, later_ref, kind_ref, kernels_ref, wide_ref, forward, first, out_ref):
+    spec = spectra(kind_ref[...].astype(F32), kernels_ref[...], wide_ref[...])
+    here, after = jnp.transpose(seen_ref[...]), jnp.transpose(later_ref[...])
+    out_ref[...] = plane_advanced(here, after, spec, forward[...], first[...], 3)
+
+
+def observe(seen, later, gauge_kernel, kernels, wide, mats):
+    rows, hours = seen.shape
+    return pl.pallas_call(
+        observe_kernel,
+        out_shape=jax.ShapeDtypeStruct((hours, rows), F32),
+        compiler_params=params(),
+        name="observe",
+        cost_estimate=SMALL,
+    )(seen, later, gauge_kernel.reshape(1, rows), kernels, wide, *mats)
+
+
 def sides(even, pair, middle):
     return jnp.where(even, middle, pair), jnp.where(even, pair, middle)
 
 
-def plane_first_kernel(flag_ref, here_ref, pair_ref, middle_ref, seen_ref, seen_later_ref, spec_ref, *refs):
-    forward3, last3, forward, first, out_ref = refs
-    hours, rows = here_ref.shape
+def plane_call(kernel, name, shapes, flags, args):
+    return pl.pallas_call(
+        kernel,
+        in_specs=[pl.BlockSpec(memory_space=pltpu.SMEM)] * len(flags)
+        + [pl.BlockSpec(memory_space=pltpu.VMEM)] * len(args),
+        out_shape=[jax.ShapeDtypeStruct(shape, F32) for shape in shapes],
+        compiler_params=params(),
+        name=name,
+        cost_estimate=SMALL,
+    )(*flags, *args)
+
+
+def plane_first_kernel(
+    flag_ref, here_ref, pair_ref, middle_ref, seen_ref, spec_ref, kernels_ref, forward, first, last, out_ref
+):
     spec = spec_ref[...]
     before, after = sides(flag_ref[0] > 0.5, pair_ref[...], middle_ref[...])
-    now, later = plane_delayed(before, here_ref[...], after, spec, forward3[...], last3[...], 3)
-    start = jnp.transpose(seen_ref[...]) - now
-    start_later = (jnp.transpose(seen_later_ref[...]) - later) * flag_ref[1]
-    out_ref[pl.ds(0, hours), :] = plane_advanced(start, start_later, spec, forward[...], first[...], 2)
-    out_ref[pl.ds(hours, NOTE), :] = jnp.concatenate(
-        [lanes(start, start), jnp.zeros((NOTE - 1, rows), F32)], axis=0
-    )
-
-
-def plane_first(flags, sums, seen, seen_later, spec, mats):
-    hours, rows = sums[0].shape
-    args = [flags, *sums, seen, seen_later, spec, *mats]
-    return pl.pallas_call(
-        plane_first_kernel,
-        in_specs=[pl.BlockSpec(memory_space=pltpu.SMEM)]
-        + [pl.BlockSpec(memory_space=pltpu.VMEM)] * (len(args) - 1),
-        out_shape=jax.ShapeDtypeStruct((hours + NOTE, rows), F32),
-        compiler_params=params(),
-        name="plane_first",
-        cost_estimate=SMALL,
-    )(*args)
-
-
-def plane_open_kernel(flag_ref, here_ref, pair_ref, middle_ref, pulled_ref, spec_ref, *refs):
-    forward, first, last, out_ref, now_ref = refs
-    height, rows = pulled_ref.shape
-    hours = height - NOTE
-    tail, body = pl.ds(hours, NOTE), pl.ds(0, hours)
+    now, later = plane_delayed(before, here_ref[...], after, spec, forward[...], last[...], 3)
+    known = plane_advanced(now, later * flag_ref[1], spec, forward[...], first[...], 3)
+    out_ref[...] = seen_ref[...] - known * gain(kernels_ref[...])
+
+
+def plane_delay_kernel(flag_ref, here_ref, pair_ref, middle_ref, spec_ref, forward, last, out_ref):
+    body = pl.ds(0, HOURS)
+    before, after = sides(flag_ref[0] > 0.5, pair_ref[body, :], middle_ref[body, :])
+    out = plane_delayed(before, here_ref[body, :], after, spec_ref[...], forward[...], last[...], 2)
+    for i in range(2):
+        out_ref[pl.ds(i * HOURS, HOURS), :] = out[i]
+
+
+def write_note(ref, rows):
+    tail = [jnp.zeros((NOTE - len(rows), ref.shape[1]), F32)]
+    ref[pl.ds(HOURS, NOTE), :] = jnp.concatenate(rows + tail, axis=0)
+
+
+def plane_open_kernel(
+    flag_ref, here_ref, pair_ref, middle_ref, pulled_ref, spec_ref, forward, first, last, out_ref, delayed_ref
+):
+    here = here_ref[...]
     spec = spec_ref[...]
-    here = here_ref[body, :]
-    before, after = sides(flag_ref[0] > 0.5, pair_ref[body, :], middle_ref[body, :])
+    before, after = sides(flag_ref[0] > 0.5, pair_ref[...], middle_ref[...])
     now, later = plane_delayed(before, here, after, spec, forward[...], last[...], 2)
-    out_ref[body, :] = plane_advanced(now, later * flag_ref[1], spec, forward[...], first[...], 2)
-    out_ref[tail, :] = jnp.concatenate(
-        [
-            lanes(pulled_ref[body, :], here),
-            lanes(now, now),
-            pulled_ref[hours : hours + 1, :],
-            jnp.zeros((NOTE - 3, rows), F32),
-        ],
-        axis=0,
-    )
-    now_ref[...] = now
-
-
-def plane_open(flags, sums, pulled, spec, mats):
-    height, rows = pulled.shape
-    args = [flags, *sums, pulled, spec, *mats]
-    return pl.pallas_call(
-        plane_open_kernel,
-        in_specs=[pl.BlockSpec(memory_space=pltpu.SMEM)]
-        + [pl.BlockSpec(memory_space=pltpu.VMEM)] * (len(args) - 1),
-        out_shape=[
-            jax.ShapeDtypeStruct((height, rows), F32),
-            jax.ShapeDtypeStruct((height - NOTE, rows), F32),
-        ],
-        compiler_params=params(),
-        name="plane_open",
-        cost_estimate=SMALL,
-    )(*args)
-
-
-def opening(ref):
-    start = total(ref, 2)
-    square = total(ref, 0) / start
-    alpha = jnp.sqrt(square)
-    beta = jnp.sqrt(jnp.maximum(total(ref, 1) / total(ref, 0) - square, 0.0))
-    return 1.0 / jnp.sqrt(start), alpha, beta
-
-
-def plane_step_kernel(flag_ref, here_ref, pair_ref, mirror_ref, two_ref, *refs):
-    old_refs, (pulled_ref, old_z_ref, old_now_ref, spec_ref), refs = refs[:3], refs[3:7], refs[7:]
-    forward, first, last, total_ref, out_ref, kept_ref = refs
-    height, rows = pulled_ref.shape
-    hours = height - NOTE
-    tail, body = pl.ds(hours, NOTE), pl.ds(0, hours)
-    total_ref[...] = (here_ref[tail, :] + pair_ref[tail, :]) + (two_ref[...] + mirror_ref[tail, :])
-    scale, alpha, beta = opening(total_ref)
-    a, b, g = scale / (alpha * beta), scale * alpha / beta, scale * beta / alpha
-    spec = spec_ref[...]
-    s, su = [], []
-    for ref, old_ref in zip((here_ref, pair_ref, mirror_ref), old_refs):
-        old = old_ref[body, :]
-        new = ref[body, :] * flag_ref[2] if ref is mirror_ref else ref[body, :]
-        su.append(new * a - old * b)
-        s.append(su[-1] - old * g)
-    zu = pulled_ref[body, :] * a - old_z_ref[body, :] * b
-    z = zu - old_z_ref[body, :] * g
-    before, after = sides(flag_ref[0] > 0.5, s[1], s[2])
-    now, later = plane_delayed(before, s[0], after, spec, forward[...], last[...], 2)
-    out_ref[body, :] = plane_advanced(now, later * flag_ref[1], spec, forward[...], first[...], 2)
-    out_ref[tail, :] = jnp.concatenate(
-        [lanes(z, s[0]), lanes(now, now), lanes(zu, s[0]), jnp.zeros((NOTE - 3, rows), F32)], axis=0
-    )
-    for i, value in enumerate((s[0], su[0], z, zu, now, now + old_now_ref[...] * g)):
-        kept_ref[pl.ds(i * hours, hours), :] = value
-
-
-def plane_step(flags, sums, two, old, pulled, old_z, old_now, spec, mats):
-    height, rows = pulled.shape
-    args = [flags, *sums, two, *old, pulled, old_z, old_now, spec, *mats]
-    return pl.pallas_call(
-        plane_step_kernel,
-        in_specs=[pl.BlockSpec(memory_space=pltpu.SMEM)]
-        + [pl.BlockSpec(memory_space=pltpu.VMEM)] * (len(args) - 1),
-        out_shape=[
-            jax.ShapeDtypeStruct((NOTE, rows), F32),
-            jax.ShapeDtypeStruct((height, rows), F32),
-            jax.ShapeDtypeStruct((6 * (height - NOTE), rows), F32),
-        ],
-        compiler_params=params(),
-        name="plane_step",
-        cost_estimate=SMALL,
-    )(*args)
-
-
-def plane_close_kernel(here_ref, before_ref, pulled_ref, kept_ref, spec_ref, forward, last, out_ref):
-    height, rows = pulled_ref.shape
-    hours = height - NOTE
-    body = pl.ds(0, hours)
-    here = here_ref[body, :]
+    out_ref[pl.ds(0, HOURS), :] = plane_advanced(now, later * flag_ref[1], spec, forward[...], first[...], 2)
+    write_note(out_ref, [lanes(pulled_ref[...], here), lanes(now, now)])
+    delayed_ref[pl.ds(0, HOURS), :] = now
+    delayed_ref[pl.ds(HOURS, HOURS), :] = later
+
+
+def plane_step_kernel(
+    flag_ref,
+    here_ref,
+    pair_ref,
+    two_ref,
+    mirror_ref,
+    pulled_ref,
+    delayed_ref,
+    old_z_ref,
+    old_s_ref,
+    old_delayed_ref,
+    spec_ref,
+    forward,
+    first,
+    total_ref,
+    out_ref,
+    kept_ref,
+):
+    tail, body = pl.ds(HOURS, NOTE), pl.ds(0, HOURS)
+    total_ref[...] = (here_ref[tail, :] + pair_ref[tail, :]) + (two_ref[...] + mirror_ref[...])
+    inverse = total(total_ref, 0) / total(total_ref, 1)
+    z = pulled_ref[body, :] * inverse - old_z_ref[...]
+    s = here_ref[body, :] * inverse - old_s_ref[...]
+    both = delayed_ref[...] * inverse - old_delayed_ref[...]
+    now, later = both[:HOURS], both[HOURS:]
+    following = plane_advanced(now, later * flag_ref[1], spec_ref[...], forward[...], first[...], 2)
+    out_ref[body, :] = following * inverse
+    write_note(out_ref, [lanes(z, s), lanes(now, now)])
+    for i, value in enumerate((z, s, now)):
+        kept_ref[pl.ds(i * HOURS, HOURS), :] = value
+
+
+def plane_close_kernel(
+    here_ref, before_ref, pulled_ref, kept_ref, old_z_ref, old_s_ref, old_delayed_ref, spec_ref, forward, last, out_ref
+):
+    body = pl.ds(0, HOURS)
+    here, raw = here_ref[body, :], pulled_ref[body, :]
     waves = product(forward[...], jnp.concatenate([before_ref[body, :], here], axis=0), 2)
     now = product(last[...], turn(waves, spec_ref[...], 1.0), 2)
-    s, su, z, zu, old_now, old_now_u = (kept_ref[pl.ds(i * hours, hours), :] for i in range(6))
-    raw = pulled_ref[body, :]
-    note = [pulled_ref[hours + i : hours + i + 1, :] for i in range(3)]
-    for left in (raw, zu, z):
-        note += [lanes(left, right) for right in (here, su, s)]
-    parts = (now, old_now_u, old_now)
+    z, s, delayed = (kept_ref[pl.ds(i * HOURS, HOURS), :] for i in range(3))
+    note = [pulled_ref[HOURS + i : HOURS + i + 1, :] for i in range(2)]
+    for left in (raw, z, old_z_ref[...]):
+        note += [lanes(left, right) for right in (here, s, old_s_ref[...])]
+    parts = (now, delayed, old_delayed_ref[body, :])
     for i in range(3):
         note += [lanes(parts[i], parts[j]) for j in range(i, 3)]
-    note.append(jnp.zeros((24 - len(note), rows), F32))
+    note.append(jnp.zeros((24 - len(note), here.shape[1]), F32))
     note = jnp.sum(jnp.concatenate(note, axis=0), axis=1, keepdims=True)
     shape = (24, out_ref.shape[2])
     row, col = (lax.broadcasted_iota(jnp.int32, shape, i) for i in range(2))
@@ -1012,78 +1007,36 @@
     out_ref[...] = jnp.broadcast_to(note[None], out_ref.shape)
 
 
-def plane_close(sums, pulled, kept, spec, mats):
-    rows = pulled.shape[1]
-    return pl.pallas_call(
-        plane_close_kernel,
-        out_shape=jax.ShapeDtypeStruct((Z_ * X_ * Y_ * C_, 8, rows // 2), F32),
-        compiler_params=params(),
-        name="plane_close",
-        cost_estimate=SMALL,
-    )(*sums, pulled, kept, spec, *mats)
-
-
-def plane_weights(open_ref, close):
-    scale, alpha, beta = opening(open_ref)
-    start = 1.0 / scale
-    phibar, rhobar = start, alpha
-    zero = jnp.zeros_like(start)
-    z = zu = [scale, zero, zero]
-    w = [value / alpha for value in z]
-    result = [zero] * 3
-    for k in range(3):
-        rho = jnp.sqrt(rhobar * rhobar + beta * beta)
-        cosine, sine = rhobar / rho, beta / rho
-        phi, phibar = cosine * phibar, sine * phibar
-        result = [r + phi / rho * value for r, value in zip(result, w)]
-        if k == 2:
-            return result
-        a, b, g = 1.0 / (alpha * beta), alpha / beta, beta / alpha
-        zu = [-b * value for value in zu]
-        zu[k + 1] = zu[k + 1] + (a * scale if k == 0 else a)
-        z = [value - g * old for value, old in zip(zu, z)]
-        if k == 0:
-            square, norm, along = (close[:, i : i + 1] for i in range(3))
-        else:
-            plain = (a, -b, -g)
-            cross = [[close[:, 3 + 3 * i + j : 4 + 3 * i + j] for j in range(3)] for i in range(3)]
-            along = sum(plain[i] * plain[j] * cross[i][j] for i in range(2) for j in range(3))
-            square = along + sum(plain[2] * plain[j] * cross[2][j] for j in range(3))
-            pairs = [(i, j) for i in range(3) for j in range(i, 3)]
-            norm = sum(
-                plain[i] * plain[j] * close[:, 12 + n : 13 + n] * (1.0 if i == j else 2.0)
-                for n, (i, j) in enumerate(pairs)
-            )
-        alpha = jnp.sqrt(square)
-        beta = jnp.sqrt(jnp.maximum(norm / square - 2.0 * along + square, 0.0))
-        theta = sine * alpha
-        rhobar = -cosine * alpha
-        w = [value / alpha - theta / rho * old for value, old in zip(z, w)]
-
-
-def plane_combine_kernel(open_ref, close_ref, *refs):
-    *parts, out_ref = refs
-    hours, rows = out_ref.shape[1], open_ref.shape[1]
+def plane_weights(open_ref, close, scale):
+    entry = lambda i: close[:, i : i + 1]
+    n1, t1 = total(open_ref, 0), total(open_ref, 1)
+    n2, t2 = entry(0), entry(1)
+    a1 = t1 / n1
+    a2, r2 = (t2 / n2) / a1, n2 / n1
+    plain = (1.0, -a2, -r2)
+    n3 = sum(plain[i] * plain[j] * entry(2 + 3 * i + j) for i in range(3) for j in range(3))
+    pairs = [(i, j) for i in range(3) for j in range(i, 3)]
+    t3 = sum(
+        plain[i] * plain[j] * entry(11 + n) * (1.0 if i == j else 2.0) for n, (i, j) in enumerate(pairs)
+    )
+    a3, r3 = (t3 / n3) / a1, n3 / n2
+    unit = 1.0 / (a1 * scale)
+    c3 = unit / (a3 * (a2 - r2) - r3)
+    c2 = -a3 * c3
+    c1 = unit - r2 * c2
+    step = c2 - c3 * a2
+    return c1 - step - c3 * r2, step / a1, c3
+
+
+def plane_combine_kernel(open_ref, close_ref, kernels_ref, stack_ref, mine_ref, beside_ref, out_ref):
+    rows = open_ref.shape[1]
     close = jnp.sum(close_ref[...], axis=0)[0:1, :]
-    weights = plane_weights(open_ref, close)
-    mine = sum(ref[...] * e for ref, e in zip(parts[:3], weights))
-    count = mine.shape[1] // rows
-    for i in range(count):
-        other = 0.0
-        for ref, e in zip(parts[3:], weights):
-            other = other + ref[pl.ds(ref.shape[0] - (count - i) * hours, hours), :] * e
-        out_ref[pl.ds(i * rows, rows), :] = jnp.transpose(mine[:, i * rows : (i + 1) * rows] + other)
-
-
-def plane_combine(open_note, close_note, mine, other):
-    hours, slots = mine[0].shape
-    return pl.pallas_call(
-        plane_combine_kernel,
-        out_shape=jax.ShapeDtypeStruct((slots, hours), F32),
-        compiler_params=params(),
-        name="plane_combine",
-        cost_estimate=SMALL,
-    )(open_note, close_note, *mine, *other)
+    e0, e1, e2 = plane_weights(open_ref, close, gain(kernels_ref[...]))
+    for i in range(out_ref.shape[0] // rows):
+        here = pl.ds(i * rows, rows)
+        last = mine_ref[:, here] + beside_ref[pl.ds(i * HOURS, HOURS), :]
+        value = stack_ref[pl.ds(0, HOURS), here] * e0 + stack_ref[pl.ds(HOURS, HOURS), here] * e1 + last * e2
+        out_ref[here, :] = jnp.transpose(value)
 
 
 def plane_finish_kernel(rows_ref, inc_ref, field_ref, out_ref):
@@ -1125,20 +1078,22 @@
     first = (first * rows).astype(jnp.int32)
     flags = jnp.stack([1 - z % 2, (z < Z_ - 1).astype(z.dtype), (z > 0).astype(z.dtype)]).astype(F32)
     forward, inverse_first, inverse_last, _ = turned_transforms(2)
-    forward3, _, inverse_last3, short3 = turned_transforms(3)
-    mats = [forward, inverse_first, inverse_last]
-
-    meta = describe(incidence, row_gauge, gauge_kernel)
-    meta, field = lax.optimization_barrier((meta, first_guess))
-    meta = moved(meta, to_plane)
-    parcel = moved(send(incidence, field), to_plane)
+    forward3, inverse_first3, inverse_last3, short3 = turned_transforms(3)
+    block, noted = (hours, rows), (hours + NOTE, rows)
+
+    parcel = send(incidence, first_guess)
+    parcel, near, gauges, kinds, seen = lax.optimization_barrier(
+        (parcel, incidence, row_gauge, gauge_kernel, observed)
+    )
+    parcel = moved(parcel, to_plane)
+    meta = moved(describe(near, gauges, kinds), to_plane)
+    seen = observe(seen, moved(seen, hour_before), kinds, kernels, short3, [forward3, inverse_first3])
     metas = [meta, moved(meta, over_core)]
+    spec = plane_spectrum(meta, kernels, short3, rows)
+    parcel, seen, metas, spec = lax.optimization_barrier((parcel, seen, metas, spec))
+    seen = moved(seen, to_plane)
     both = jnp.concatenate(metas, axis=1)
     around = [both] + [moved(both, where) for where in SQUARE]
-    spec = plane_spectrum(meta, kernels, short3, rows)
-    seen, parcel, around, spec = lax.optimization_barrier((observed, parcel, around, spec))
-    seen_later = moved(seen, to_plane_before)
-    seen = moved(seen, to_plane)
 
     dense = spread(first, [parcel, moved(parcel, over_core)], metas, rows)
     sums = dense[0] + sum(moved(value, where) for value, where in zip(dense[1:], SQUARE))
@@ -1146,40 +1101,64 @@
     coupled = plane_couple(first, around[:2], rows)
     coupled, sums = lax.optimization_barrier((coupled, sums))
     coupling = plane_couple(first, around[2:], rows, coupled)
-    pulled = [
-        plane_first(
-            flags, sums, seen, seen_later, spec, [forward3, inverse_last3, forward, inverse_first]
-        )
-    ]
-
-    mine_rows, other_rows, extra, mixes = [], [], [], []
-    for k in range(3):
-        values = [pulled[k]] + [moved(pulled[k], where) for where in SQUARE]
+    (pulled0,) = plane_call(
+        plane_first_kernel,
+        "plane_first",
+        [block],
+        [flags],
+        [*sums, seen, spec, kernels, forward3, inverse_first3, inverse_last3],
+    )
+
+    def mixing(pulled, extra):
+        values = [pulled] + [moved(pulled, where) for where in SQUARE]
         mine, other = plane_mix(coupling, values, extra)
         beside = moved(other, over_core)
-        mixed = mine + beside[: hours + NOTE]
-        if k:
-            other_rows.append(beside)
-        picked, theirs = plane_rows(first, metas, values)
-        mine_rows.append(picked)
-        extra = [theirs]
-        if k == 0:
-            mixes = [mixed, moved(mixed, z_pair), moved(mixed, z_middle)]
-            following, now = plane_open(flags, mixes, pulled[0], spec, mats)
-        elif k == 1:
-            sums = [mixed, moved(mixed, z_pair), moved(mixed, z_mirror)]
-            two = moved(mixed[hours:], z_two)
-            open_note, following, state = plane_step(
-                flags, sums, two, mixes, pulled[1], pulled[0], now, spec, mats
-            )
-        else:
-            sums = [mixed, moved(mixed, z_next)]
-            note = plane_close(sums, pulled[2], state, spec, [forward, inverse_last])
-            other_rows.append(moved(theirs, over_core))
-        pulled.append(following)
+        return values, mine + beside[: pulled.shape[0]], beside
+
+    values, mixed0, _ = mixing(pulled0, [])
+    picked, theirs = plane_rows(first, metas, values, [])
+    sums = [mixed0, moved(mixed0, z_pair), moved(mixed0, z_middle)]
+    pulled1, delayed0 = plane_call(
+        plane_open_kernel,
+        "plane_open",
+        [noted, (2 * hours, rows)],
+        [flags],
+        [*sums, pulled0, spec, forward, inverse_first, inverse_last],
+    )
+
+    values, mixed1, beside = mixing(pulled1, [theirs])
+    picked, theirs, stack = plane_rows(first, metas, values, [picked, beside])
+    sums = [mixed1, moved(mixed1, z_pair), moved(mixed1, z_middle)]
+    two, mirror = moved(mixed1[hours:], z_two), moved(mixed1[hours:], z_mirror)
+    (delayed1,) = plane_call(
+        plane_delay_kernel, "plane_delay", [(2 * hours, rows)], [flags], [*sums, spec, forward, inverse_last]
+    )
+    open_note, pulled2, kept = plane_call(
+        plane_step_kernel,
+        "plane_step",
+        [(NOTE, rows), noted, (3 * hours, rows)],
+        [flags],
+        [*sums[:2], two, mirror, pulled1, delayed1, pulled0, mixed0, delayed0, spec, forward, inverse_first],
+    )
+
+    values, mixed2, beside = mixing(pulled2, [theirs])
+    picked, theirs, stack = plane_rows(first, metas, values, [stack, picked, beside])
+    (note,) = plane_call(
+        plane_close_kernel,
+        "plane_close",
+        [(Z_ * X_ * Y_ * C_, 8, rows // 2)],
+        [],
+        [mixed2, moved(mixed2, z_next), pulled2, kept, pulled0, mixed0, delayed0, spec, forward, inverse_last],
+    )
     close_note = lax.all_to_all(note, ("basin", "tm"), 0, 0, tiled=False)
-    answer = moved(plane_combine(open_note, close_note, mine_rows, other_rows), from_plane)
-    return plane_finish(answer, incidence, first_guess)
+    (answer,) = plane_call(
+        plane_combine_kernel,
+        "plane_combine",
+        [(metas[0].shape[1], hours)],
+        [],
+        [open_note, close_note, kernels, stack, picked, moved(theirs, over_core)],
+    )
+    return plane_finish(moved(answer, from_plane), incidence, first_guess)
 
 
 def solution(mesh):

time: 151 us -> 151 us (level)
  starting transfers between devices: 52.8 us -> 62 us
  waiting for transfers between devices: 58.2 us -> 52.3 us
  local copies, waits for them, and re-layouts: 7.62 us -> 2.7 us
  Pallas kernels: 30.9 us -> 33.1 us
    ppermute x34 -> x35, starting transfers between devices: 47.1 us -> 56.5 us  [moved(): return lax.ppermute(value, ('basin', 'tm'), pairs)]
    ppermute x34 -> x35, waiting for transfers between devices: 50 us -> 44.2 us  [moved(): return lax.ppermute(value, ('basin', 'tm'), pairs)]
    unnamed x41 -> x31, local copies, waits for them, and re-layouts: 7.53 us -> 2.61 us
    pallas_call x5 -> x7, Pallas kernels: 8.98 us -> 11.1 us  [the longest x6 9.8 us: plane_call(): pl.pallas_call(kernel, in_specs=[pl.BlockSpec(memory_space=pltpu.SMEM)] *...]
  transfers between devices with their start and end apart: 35 -> 36, of which waited for: 20 -> 19; matrix products, arithmetic and copies ran while one was open for 0% -> 0% of each run, Pallas kernels for 11% -> 14%
where the time goes in v10:
time: 151 us
  starting transfers between devices  62 us (41%)
  waiting for transfers between devices  52.3 us (35%)
  Pallas kernels  33.1 us (22%)
  local copies, waits for them, and re-layouts  2.7 us (2%)
    ppermute x35, starting transfers between devices, moved(): return lax.ppermute(value, ('basin', 'tm'), pairs)  56.5 us
    ppermute x35, waiting for transfers between devices, moved(): return lax.ppermute(value, ('basin', 'tm'), pairs)  44.2 us
    pallas_call x6, Pallas kernels, plane_call(): pl.pallas_call(kernel, in_specs=[pl.BlockSpec(memory_space=pltpu.SMEM)] *...  9.8 us
    pallas_call x2, Pallas kernels, plane_couple(): pl.pallas_call(functools.partial(plane_couple_kernel, last), in_specs=[pl...  9.56 us
    all_to_all x1, waiting for transfers between devices, plane_shards(): close_note = lax.all_to_all(note, ('basin', 'tm'), 0, 0, tiled=False)  8.18 us
    all_to_all x1, starting transfers between devices, plane_shards(): close_note = lax.all_to_all(note, ('basin', 'tm'), 0, 0, tiled=False)  5.56 us
    pallas_call x3, Pallas kernels, plane_rows(): pl.pallas_call(plane_rows_kernel, in_specs=[pl.BlockSpec(memory_space=plt...  4.51 us
  transfers between devices with their start and end apart: 36, of which 19 were waited for; matrix products, arithmetic and copies ran while one was open for 0% of the time, Pallas kernels for 14%

profile of v10, /device:TPU:1, one launch (start us, length us, event | category | flops | bytes accessed | tf_op | source)
XLA Modules:
  0.0 150.8 jit_solution(7782541638555956788)
XLA Ops:
  0.0 1.6 %copy-done = f32[4096,128]{1,0:T(8,128)S(1)} copy-done((f32[4096,128]{1,0:T(8,128)S(1)}, f32[4096,128]{1,0:T(8,128)}, u32[]{:S(2)}) %copy-start) | copy-done | bytes 2097176
  2.6 1.4 send.1
  4.0 4.6 %collective-permute-start = (f32[128,512]{1,0:T(8,128)S(1)}, f32[128,512]{1,0:T(8,128)S(1)}, u32[]{:S(2)}, u32[]{:S(2)}) collective-permute-start(f32[128,512]{1,0:T(8,128)S(1)} %send.1), channel_id=1, source_target_pairs={{0,0},{1,8},{2,16},{3,24},{4,4},{5,12},{6,20},{7,28},{8,2},{9,10},... | collective-permute-start | bytes 786440 | tf_op jit(solution)/shard_map/ppermute | solution.py:503
  8.6 1.9 %collective-permute-start.1 = (f32[256,128]{1,0:T(8,128)S(1)}, f32[256,128]{1,0:T(8,128)S(1)}, u32[]{:S(2)}, u32[]{:S(2)}) collective-permute-start(f32[256,128]{1,0:T(8,128)S(1)} %copy-done.12), channel_id=1, source_target_pairs={{1,0},{2,1},{3,2},{5,4},{6,5},{7,6},{9,8},{10,9},{11,10},{13,12},{... | collective-permute-start | bytes 393224 | tf_op jit(solution)/shard_map/ppermute | solution.py:503
  10.8 2.7 %collective-permute-start.2 = (f32[24,512]{1,0:T(8,128)S(1)}, f32[24,512]{1,0:T(8,128)S(1)}, u32[]{:S(2)}, u32[]{:S(2)}) collective-permute-start(f32[24,512]{1,0:T(8,128)S(1)} %describe.1), channel_id=1, source_target_pairs={{0,0},{1,8},{2,16},{3,24},{4,4},{5,12},{6,20},{7,28},{8,2},{9,10},... | collective-permute-start | bytes 147464 | tf_op jit(solution)/shard_map/ppermute | solution.py:503
  13.5 10.0 %collective-permute-done.2.class_ref.meta_ref = f32[24,512]{1,0:T(8,128)S(1)} collective-permute-done((f32[24,512]{1,0:T(8,128)S(1)}, f32[24,512]{1,0:T(8,128)S(1)}, u32[]{:S(2)}, u32[]{:S(2)}) %collective-permute-start.2) | collective-permute-done | bytes 49184 | tf_op jit(solution)/shard_map/ppermute | solution.py:503
  27.2 1.6 %spread.1 = (f32[128,256]{1,0:T(8,128)S(1)}, f32[128,256]{1,0:T(8,128)S(1)}, f32[128,256]{1,0:T(8,128)S(1)}, f32[128,256]{1,0:T(8,128)S(1)}) custom-call(s32[6]{0:T(128)S(1)} %broadcast_multiply_fusion.first_ref, f32[128,512]{1,0:T(8,128)S(1)} %collective-permute-done.mine_ref, f32[128,512]{1,0:T(8,128)S(1)} %collective-permute-done.7.other_ref, ...), custom_call_target="tpu_custom_call" | custom-call | flops 1 | bytes 1 | tf_op jit(solution)/shard_map/spread/pallas_call | solution.py:696
  30.1 1.4 collective-permute-start.10
  34.2 2.9 %collective-permute-done.9 = f32[128,256]{1,0:T(8,128)S(1)} collective-permute-done((f32[128,256]{1,0:T(8,128)S(1)}, f32[128,256]{1,0:T(8,128)S(1)}, u32[]{:S(2)}, u32[]{:S(2)}) %collective-permute-start.9) | collective-permute-done | bytes 131104 | tf_op jit(solution)/shard_map/ppermute | solution.py:503
  37.1 6.3 %collective-permute-start.13 = (f32[128,256]{1,0:T(8,128)S(1)}, f32[128,256]{1,0:T(8,128)S(1)}, u32[]{:S(2)}, u32[]{:S(2)}) collective-permute-start(f32[128,256]{1,0:T(8,128)S(1)} %observe.1), channel_id=1, source_target_pairs={{0,0},{1,8},{2,16},{3,24},{4,4},{5,12},{6,20},{7,28},{8,2},{9,10},... | collective-permute-start | bytes 393224 | tf_op jit(solution)/shard_map/ppermute | solution.py:503
  44.3 3.7 %collective-permute-start.11 = (f32[128,256]{1,0:T(8,128)S(1)}, f32[128,256]{1,0:T(8,128)S(1)}, u32[]{:S(2)}, u32[]{:S(2)}) collective-permute-start(f32[128,256]{1,0:T(8,128)S(1)} %add_add_fusion.here_ref), channel_id=1, source_target_pairs={{0,8},{1,9},{2,10},{3,11},{4,12},{5,13},{6,14},{7,15},{8,0},{9,1},... | collective-permute-start | bytes 393224 | tf_op jit(solution)/shard_map/ppermute | solution.py:503
  48.0 4.6 %plane_couple.2.refs_2_ = f32[1024,512]{1,0:T(8,128)S(1)} custom-call(s32[6]{0:T(128)S(1)} %broadcast_multiply_fusion.first_ref, f32[24,1024]{1,0:T(8,128)S(1)} %constant_dynamic-update-slice_fusion.refs_0_, f32[24,1024]{1,0:T(8,128)S(1)} %collective-permute-done.6.refs_1_), custom_call_target="tpu_custom_call" | custom-call | flops 2147483648 | bytes 2000000 | tf_op jit(solution)/shard_map/plane_couple/pallas_call | solution.py:763
  52.6 2.6 %plane_first.1.a_ref.pulled_ref.old_z_ref = f32[128,256]{1,0:T(8,128)S(1)} custom-call(f32[3]{0:T(128)S(1)} %add_convert_fusion.flag_ref, f32[128,256]{1,0:T(8,128)S(1)} %add_add_fusion.here_ref, f32[128,256]{1,0:T(8,128)S(1)} %collective-permute-done.11.pair_ref, f32[128,256]{1,0:T(8,128)S(1)} %collective-permute-done.12.middle_ref, ...), custom_call_target="tpu_custom_call" | custom-call | flops 1 | bytes 1 | tf_op jit(solution)/shard_map/plane_first/pallas_call | solution.py:909
  55.2 3.2 %collective-permute-start.16 = (f32[128,256]{1,0:T(8,128)S(1)}, f32[128,256]{1,0:T(8,128)S(1)}, u32[]{:S(2)}, u32[]{:S(2)}) collective-permute-start(f32[128,256]{1,0:T(8,128)S(1)} %plane_first.1.a_ref.pulled_ref.old_z_ref), channel_id=1, source_target_pairs={{0,6},{1,7},{2,4},{3,5},{4,2},{5,3},{6,0},{7,1},{8,14},{9,15},{10,... | collective-permute-start | bytes 393224 | tf_op jit(solution)/shard_map/ppermute | solution.py:503
  59.7 4.9 %plane_couple.3 = (bf16[1024,512]{1,0:T(8,128)(2,1)S(1)}, bf16[1024,512]{1,0:T(8,128)(2,1)S(1)}) custom-call(s32[6]{0:T(128)S(1)} %broadcast_multiply_fusion.first_ref, f32[24,1024]{1,0:T(8,128)S(1)} %collective-permute-done.4.refs_0_, f32[24,1024]{1,0:T(8,128)S(1)} %collective-permute-done.5.refs_1_, f32[1024,512]{1,0:T(8,128)S(1)} %plane_couple.2.refs_2_), custom_call_target="tpu_custom_call" | custom-call | flops 2147483648 | bytes 2000000 | tf_op jit(solution)/shard_map/plane_couple/pallas_call | solution.py:763
  69.1 4.8 %collective-permute-start.18 = (f32[128,256]{1,0:T(8,128)S(1)}, f32[128,256]{1,0:T(8,128)S(1)}, u32[]{:S(2)}, u32[]{:S(2)}) collective-permute-start(f32[128,256]{1,0:T(8,128)S(1)} %add.61.here_ref.old_s_ref), channel_id=1, source_target_pairs={{0,8},{1,9},{2,10},{3,11},{4,12},{5,13},{6,14},{7,15},{8,0},{9,1},... | collective-permute-start | bytes 393224 | tf_op jit(solution)/shard_map/ppermute | solution.py:503
  73.8 3.3 %collective-permute-done.18.pair_ref = f32[128,256]{1,0:T(8,128)S(1)} collective-permute-done((f32[128,256]{1,0:T(8,128)S(1)}, f32[128,256]{1,0:T(8,128)S(1)}, u32[]{:S(2)}, u32[]{:S(2)}) %collective-permute-start.18) | collective-permute-done | bytes 131104 | tf_op jit(solution)/shard_map/ppermute | solution.py:503
  77.1 1.8 %plane_open.1 = (f32[136,256]{1,0:T(8,128)S(1)}, f32[256,256]{1,0:T(8,128)S(1)}) custom-call(f32[3]{0:T(128)S(1)} %add_convert_fusion.flag_ref, f32[128,256]{1,0:T(8,128)S(1)} %add.61.here_ref.old_s_ref, f32[128,256]{1,0:T(8,128)S(1)} %collective-permute-done.18.pair_ref, f32[128,256]{1,0:T(8,128)S(1)} %collective-permute-done.19.middle_ref, ...), custom_call_target="tpu_custom_call" | custom-call | flops 1 | bytes 1 | tf_op jit(solution)/shard_map/plane_open/pallas_call | solution.py:909
  83.9 4.2 %collective-permute-done.21.c_ref = f32[136,256]{1,0:T(8,128)S(1)} collective-permute-done((f32[136,256]{1,0:T(8,128)S(1)}, f32[136,256]{1,0:T(8,128)S(1)}, u32[]{:S(2)}, u32[]{:S(2)}) %collective-permute-start.21) | collective-permute-done | bytes 139296 | tf_op jit(solution)/shard_map/ppermute | solution.py:503
  91.9 2.8 %collective-permute-start.24 = (f32[136,256]{1,0:T(8,128)S(1)}, f32[136,256]{1,0:T(8,128)S(1)}, u32[]{:S(2)}, u32[]{:S(2)}) collective-permute-start(f32[136,256]{1,0:T(8,128)S(1)} %slice_add_fusion.1.here_ref), channel_id=1, source_target_pairs={{0,8},{1,9},{2,10},{3,11},{4,12},{5,13},{6,14},{7,15},{8,0},{9,1},... | collective-permute-start | bytes 417800 | tf_op jit(solution)/shard_map/ppermute | solution.py:503
  94.7 2.0 %collective-permute-start.26 = (f32[8,256]{1,0:T(8,128)S(1)}, f32[8,256]{1,0:T(8,128)S(1)}, u32[]{:S(2)}, u32[]{:S(2)}) collective-permute-start(f32[8,256]{1,0:T(8,128)S(1)} %slice.14), channel_id=1, source_target_pairs={{0,24},{1,25},{2,26},{3,27},{4,28},{5,29},{6,30},{7,31},{8,16},{9,... | collective-permute-start | bytes 24584 | tf_op jit(solution)/shard_map/ppermute | solution.py:503
  96.7 1.4 collective-permute-done.24.pair_ref
  106.4 1.8 %collective-permute-done.29.c_ref = f32[136,256]{1,0:T(8,128)S(1)} collective-permute-done((f32[136,256]{1,0:T(8,128)S(1)}, f32[136,256]{1,0:T(8,128)S(1)}, u32[]{:S(2)}, u32[]{:S(2)}) %collective-permute-start.29) | collective-permute-done | bytes 139296 | tf_op jit(solution)/shard_map/ppermute | solution.py:503
  108.7 3.4 %collective-permute-start.31 = (f32[392,256]{1,0:T(8,128)S(1)}, f32[392,256]{1,0:T(8,128)S(1)}, u32[]{:S(2)}, u32[]{:S(2)}) collective-permute-start(f32[392,256]{1,0:T(8,128)S(1)} %get-tuple-element.76), channel_id=1, source_target_pairs={{0,1},{1,0},{2,3},{3,2},{4,5},{5,4},{6,7},{7,6},{8,9},{9,8},{10,11... | collective-permute-start | bytes 1204232 | tf_op jit(solution)/shard_map/ppermute | solution.py:503
  113.5 2.3 %collective-permute-start.32 = (f32[136,256]{1,0:T(8,128)S(1)}, f32[136,256]{1,0:T(8,128)S(1)}, u32[]{:S(2)}, u32[]{:S(2)}) collective-permute-start(f32[136,256]{1,0:T(8,128)S(1)} %slice_add_fusion.here_ref), channel_id=1, source_target_pairs={{0,8},{1,9},{2,10},{3,11},{4,12},{5,13},{6,14},{7,15},{8,16},{9,17... | collective-permute-start | bytes 417800 | tf_op jit(solution)/shard_map/ppermute | solution.py:503
  115.8 2.0 %plane_rows.5 = (f32[128,512]{1,0:T(8,128)S(1)}, f32[256,256]{1,0:T(8,128)}, f32[256,512]{1,0:T(8,128)S(1)}) custom-call(s32[6]{0:T(128)S(1)} %broadcast_multiply_fusion.first_ref, f32[24,512]{1,0:T(8,128)S(1)} %collective-permute-done.2.class_ref.meta_ref, f32[24,512]{1,0:T(8,128)S(1)} %collective-permute-done.3.meta_other_ref, ...), custom_call_target="tpu_custom_call" | custom-call | flops 1000000000 | bytes 2000000 | tf_op jit(solution)/shard_map/plane_rows/pallas_call | solution.py:847
  119.8 5.6 %all-to-all-start = ((f32[32,8,128]{2,1,0:T(8,128)}), f32[32,8,128]{2,1,0:T(8,128)S(1)}, u32[]{:S(2)}, u32[]{:S(2)}) async-start(f32[32,8,128]{2,1,0:T(8,128)} %plane_close.1), calls=%async_computation | async-start | bytes 262144 | tf_op jit(solution)/shard_map/all_to_all | solution.py:1153
  125.4 8.2 %all-to-all-done.close_ref = f32[32,8,128]{2,1,0:T(8,128)S(1)} async-done(((f32[32,8,128]{2,1,0:T(8,128)}), f32[32,8,128]{2,1,0:T(8,128)S(1)}, u32[]{:S(2)}, u32[]{:S(2)}) %all-to-all-start) | async-done | bytes 131104 | tf_op jit(solution)/shard_map/all_to_all | solution.py:1153
  133.6 1.5 plane_combine.1
  135.1 2.6 %collective-permute-start.34 = (f32[512,128]{1,0:T(8,128)S(1)}, f32[512,128]{1,0:T(8,128)S(1)}, u32[]{:S(2)}, u32[]{:S(2)}) collective-permute-start(f32[512,128]{1,0:T(8,128)S(1)} %plane_combine.1), channel_id=1, source_target_pairs={{0,0},{1,16},{2,8},{3,24},{4,4},{5,20},{6,12},{7,28},{8,1},{9,17},... | collective-permute-start | bytes 786440 | tf_op jit(solution)/shard_map/ppermute | solution.py:503
  137.7 10.7 %collective-permute-done.34.rows_ref = f32[512,128]{1,0:T(8,128)S(1)} collective-permute-done((f32[512,128]{1,0:T(8,128)S(1)}, f32[512,128]{1,0:T(8,128)S(1)}, u32[]{:S(2)}, u32[]{:S(2)}) %collective-permute-start.34) | collective-permute-done | bytes 262176 | tf_op jit(solution)/shard_map/ppermute | solution.py:503
  148.4 2.4 %plane_finish.1 = f32[4096,128]{1,0:T(8,128)} custom-call(f32[512,128]{1,0:T(8,128)S(1)} %collective-permute-done.34.rows_ref, s32[32,16,128]{2,1,0:T(8,128)S(1)} %copy-done.5, f32[4096,128]{1,0:T(8,128)S(1)} %copy-done.1), custom_call_target="tpu_custom_call" | custom-call | tf_op jit(solution)/shard_map/plane_finish/pallas_call | solution.py:1057
  (100 shorter events, 36.4 us)
Async XLA Ops:
  4.0 21.5 %collective-permute-start = (f32[128,512]{1,0:T(8,128)S(1)}, f32[128,512]{1,0:T(8,128)S(1)}, u32[]{:S(2)}, u32[]{:S(2)}) collective-permute-start(f32[128,512]{1,0:T(8,128)S(1)} %send.1), channel_id=1, source_target_pairs={{0,0},{1,8},{2,16},{3,24},{4,4},{5,12},{6,20},{7,28},{8,2},{9,10},... | collective-permute-start | bytes 786440 | tf_op jit(solution)/shard_map/ppermute | solution.py:503
  8.6 15.5 %collective-permute-start.1 = (f32[256,128]{1,0:T(8,128)S(1)}, f32[256,128]{1,0:T(8,128)S(1)}, u32[]{:S(2)}, u32[]{:S(2)}) collective-permute-start(f32[256,128]{1,0:T(8,128)S(1)} %copy-done.12), channel_id=1, source_target_pairs={{1,0},{2,1},{3,2},{5,4},{6,5},{7,6},{9,8},{10,9},{11,10},{13,12},{... | collective-permute-start | bytes 393224 | tf_op jit(solution)/shard_map/ppermute | solution.py:503
  10.8 12.7 %collective-permute-start.2 = (f32[24,512]{1,0:T(8,128)S(1)}, f32[24,512]{1,0:T(8,128)S(1)}, u32[]{:S(2)}, u32[]{:S(2)}) collective-permute-start(f32[24,512]{1,0:T(8,128)S(1)} %describe.1), channel_id=1, source_target_pairs={{0,0},{1,8},{2,16},{3,24},{4,4},{5,12},{6,20},{7,28},{8,2},{9,10},... | collective-permute-start | bytes 147464 | tf_op jit(solution)/shard_map/ppermute | solution.py:503
  28.8 4.8 %collective-permute-start.8 = (f32[128,256]{1,0:T(8,128)S(1)}, f32[128,256]{1,0:T(8,128)S(1)}, u32[]{:S(2)}, u32[]{:S(2)}) collective-permute-start(f32[128,256]{1,0:T(8,128)S(1)} %get-tuple-element.53), channel_id=1, source_target_pairs={{0,4},{1,5},{2,6},{3,7},{4,0},{5,1},{6,2},{7,3},{8,12},{9,13},{10,... | collective-permute-start | bytes 393224 | tf_op jit(solution)/shard_map/ppermute | solution.py:503
  30.1 7.1 %collective-permute-start.9 = (f32[128,256]{1,0:T(8,128)S(1)}, f32[128,256]{1,0:T(8,128)S(1)}, u32[]{:S(2)}, u32[]{:S(2)}) collective-permute-start(f32[128,256]{1,0:T(8,128)S(1)} %get-tuple-element.54), channel_id=1, source_target_pairs={{0,2},{1,3},{2,0},{3,1},{4,6},{5,7},{6,4},{7,5},{8,10},{9,11},{10,... | collective-permute-start | bytes 393224 | tf_op jit(solution)/shard_map/ppermute | solution.py:503
  30.1 13.3 %collective-permute-start.10 = (f32[128,256]{1,0:T(8,128)S(1)}, f32[128,256]{1,0:T(8,128)S(1)}, u32[]{:S(2)}, u32[]{:S(2)}) collective-permute-start(f32[128,256]{1,0:T(8,128)S(1)} %get-tuple-element.55), channel_id=1, source_target_pairs={{0,6},{1,7},{2,4},{3,5},{4,2},{5,3},{6,0},{7,1},{8,14},{9,15},{10,... | collective-permute-start | bytes 393224 | tf_op jit(solution)/shard_map/ppermute | solution.py:503
  31.5 12.8 %collective-permute-start.6 = (f32[24,1024]{1,0:T(8,128)S(1)}, f32[24,1024]{1,0:T(8,128)S(1)}, u32[]{:S(2)}, u32[]{:S(2)}) collective-permute-start(f32[24,1024]{1,0:T(8,128)S(1)} %constant_dynamic-update-slice_fusion.refs_0_), channel_id=1, source_target_pairs={{0,4},{1,5},{2,6},{3,7},{4,0},{5,1},{6,2},{7,3},{8,12},{9,13},{10,... | collective-permute-start | bytes 294920 | tf_op jit(solution)/shard_map/ppermute | solution.py:503
  32.8 26.9 %collective-permute-start.5 = (f32[24,1024]{1,0:T(8,128)S(1)}, f32[24,1024]{1,0:T(8,128)S(1)}, u32[]{:S(2)}, u32[]{:S(2)}) collective-permute-start(f32[24,1024]{1,0:T(8,128)S(1)} %constant_dynamic-update-slice_fusion.refs_0_), channel_id=1, source_target_pairs={{0,6},{1,7},{2,4},{3,5},{4,2},{5,3},{6,0},{7,1},{8,14},{9,15},{10,... | collective-permute-start | bytes 294920 | tf_op jit(solution)/shard_map/ppermute | solution.py:503
  33.6 26.1 %collective-permute-start.4 = (f32[24,1024]{1,0:T(8,128)S(1)}, f32[24,1024]{1,0:T(8,128)S(1)}, u32[]{:S(2)}, u32[]{:S(2)}) collective-permute-start(f32[24,1024]{1,0:T(8,128)S(1)} %constant_dynamic-update-slice_fusion.refs_0_), channel_id=1, source_target_pairs={{0,2},{1,3},{2,0},{3,1},{4,6},{5,7},{6,4},{7,5},{8,10},{9,11},{10,... | collective-permute-start | bytes 294920 | tf_op jit(solution)/shard_map/ppermute | solution.py:503
  37.1 15.5 %collective-permute-start.13 = (f32[128,256]{1,0:T(8,128)S(1)}, f32[128,256]{1,0:T(8,128)S(1)}, u32[]{:S(2)}, u32[]{:S(2)}) collective-permute-start(f32[128,256]{1,0:T(8,128)S(1)} %observe.1), channel_id=1, source_target_pairs={{0,0},{1,8},{2,16},{3,24},{4,4},{5,12},{6,20},{7,28},{8,2},{9,10},... | collective-permute-start | bytes 393224 | tf_op jit(solution)/shard_map/ppermute | solution.py:503
  43.5 9.1 %collective-permute-start.12 = (f32[128,256]{1,0:T(8,128)S(1)}, f32[128,256]{1,0:T(8,128)S(1)}, u32[]{:S(2)}, u32[]{:S(2)}) collective-permute-start(f32[128,256]{1,0:T(8,128)S(1)} %add_add_fusion.here_ref), channel_id=1, source_target_pairs={{8,16},{9,17},{10,18},{11,19},{12,20},{13,21},{14,22},{15,23},{16,... | collective-permute-start | bytes 393224 | tf_op jit(solution)/shard_map/ppermute | solution.py:503
  44.3 8.3 %collective-permute-start.11 = (f32[128,256]{1,0:T(8,128)S(1)}, f32[128,256]{1,0:T(8,128)S(1)}, u32[]{:S(2)}, u32[]{:S(2)}) collective-permute-start(f32[128,256]{1,0:T(8,128)S(1)} %add_add_fusion.here_ref), channel_id=1, source_target_pairs={{0,8},{1,9},{2,10},{3,11},{4,12},{5,13},{6,14},{7,15},{8,0},{9,1},... | collective-permute-start | bytes 393224 | tf_op jit(solution)/shard_map/ppermute | solution.py:503
  55.2 9.4 %collective-permute-start.16 = (f32[128,256]{1,0:T(8,128)S(1)}, f32[128,256]{1,0:T(8,128)S(1)}, u32[]{:S(2)}, u32[]{:S(2)}) collective-permute-start(f32[128,256]{1,0:T(8,128)S(1)} %plane_first.1.a_ref.pulled_ref.old_z_ref), channel_id=1, source_target_pairs={{0,6},{1,7},{2,4},{3,5},{4,2},{5,3},{6,0},{7,1},{8,14},{9,15},{10,... | collective-permute-start | bytes 393224 | tf_op jit(solution)/shard_map/ppermute | solution.py:503
  58.5 6.9 %collective-permute-start.15 = (f32[128,256]{1,0:T(8,128)S(1)}, f32[128,256]{1,0:T(8,128)S(1)}, u32[]{:S(2)}, u32[]{:S(2)}) collective-permute-start(f32[128,256]{1,0:T(8,128)S(1)} %plane_first.1.a_ref.pulled_ref.old_z_ref), channel_id=1, source_target_pairs={{0,2},{1,3},{2,0},{3,1},{4,6},{5,7},{6,4},{7,5},{8,10},{9,11},{10,... | collective-permute-start | bytes 393224 | tf_op jit(solution)/shard_map/ppermute | solution.py:503
  58.6 7.8 %collective-permute-start.14 = (f32[128,256]{1,0:T(8,128)S(1)}, f32[128,256]{1,0:T(8,128)S(1)}, u32[]{:S(2)}, u32[]{:S(2)}) collective-permute-start(f32[128,256]{1,0:T(8,128)S(1)} %plane_first.1.a_ref.pulled_ref.old_z_ref), channel_id=1, source_target_pairs={{0,4},{1,5},{2,6},{3,7},{4,0},{5,1},{6,2},{7,3},{8,12},{9,13},{10,... | collective-permute-start | bytes 393224 | tf_op jit(solution)/shard_map/ppermute | solution.py:503
  68.4 5.4 %collective-permute-start.19 = (f32[128,256]{1,0:T(8,128)S(1)}, f32[128,256]{1,0:T(8,128)S(1)}, u32[]{:S(2)}, u32[]{:S(2)}) collective-permute-start(f32[128,256]{1,0:T(8,128)S(1)} %add.61.here_ref.old_s_ref), channel_id=1, source_target_pairs={{8,16},{9,17},{10,18},{11,19},{12,20},{13,21},{14,22},{15,23},{16,... | collective-permute-start | bytes 393224 | tf_op jit(solution)/shard_map/ppermute | solution.py:503
  69.1 8.0 %collective-permute-start.18 = (f32[128,256]{1,0:T(8,128)S(1)}, f32[128,256]{1,0:T(8,128)S(1)}, u32[]{:S(2)}, u32[]{:S(2)}) collective-permute-start(f32[128,256]{1,0:T(8,128)S(1)} %add.61.here_ref.old_s_ref), channel_id=1, source_target_pairs={{0,8},{1,9},{2,10},{3,11},{4,12},{5,13},{6,14},{7,15},{8,0},{9,1},... | collective-permute-start | bytes 393224 | tf_op jit(solution)/shard_map/ppermute | solution.py:503
  78.9 5.0 %collective-permute-start.22 = (f32[136,256]{1,0:T(8,128)S(1)}, f32[136,256]{1,0:T(8,128)S(1)}, u32[]{:S(2)}, u32[]{:S(2)}) collective-permute-start(f32[136,256]{1,0:T(8,128)S(1)} %get-tuple-element.66.a_ref.pulled_ref), channel_id=1, source_target_pairs={{0,6},{1,7},{2,4},{3,5},{4,2},{5,3},{6,0},{7,1},{8,14},{9,15},{10,... | collective-permute-start | bytes 417800 | tf_op jit(solution)/shard_map/ppermute | solution.py:503
  80.1 8.0 %collective-permute-start.21 = (f32[136,256]{1,0:T(8,128)S(1)}, f32[136,256]{1,0:T(8,128)S(1)}, u32[]{:S(2)}, u32[]{:S(2)}) collective-permute-start(f32[136,256]{1,0:T(8,128)S(1)} %get-tuple-element.66.a_ref.pulled_ref), channel_id=1, source_target_pairs={{0,2},{1,3},{2,0},{3,1},{4,6},{5,7},{6,4},{7,5},{8,10},{9,11},{10,... | collective-permute-start | bytes 417800 | tf_op jit(solution)/shard_map/ppermute | solution.py:503
  80.4 7.7 %collective-permute-start.20 = (f32[136,256]{1,0:T(8,128)S(1)}, f32[136,256]{1,0:T(8,128)S(1)}, u32[]{:S(2)}, u32[]{:S(2)}) collective-permute-start(f32[136,256]{1,0:T(8,128)S(1)} %get-tuple-element.66.a_ref.pulled_ref), channel_id=1, source_target_pairs={{0,4},{1,5},{2,6},{3,7},{4,0},{5,1},{6,2},{7,3},{8,12},{9,13},{10,... | collective-permute-start | bytes 417800 | tf_op jit(solution)/shard_map/ppermute | solution.py:503
  91.0 5.7 %collective-permute-start.27 = (f32[136,256]{1,0:T(8,128)S(1)}, f32[136,256]{1,0:T(8,128)S(1)}, u32[]{:S(2)}, u32[]{:S(2)}) collective-permute-start(f32[136,256]{1,0:T(8,128)S(1)} %slice_add_fusion.1.here_ref), channel_id=1, source_target_pairs={{8,16},{9,17},{10,18},{11,19},{12,20},{13,21},{14,22},{15,23},{16,... | collective-permute-start | bytes 417800 | tf_op jit(solution)/shard_map/ppermute | solution.py:503
  91.9 6.2 %collective-permute-start.24 = (f32[136,256]{1,0:T(8,128)S(1)}, f32[136,256]{1,0:T(8,128)S(1)}, u32[]{:S(2)}, u32[]{:S(2)}) collective-permute-start(f32[136,256]{1,0:T(8,128)S(1)} %slice_add_fusion.1.here_ref), channel_id=1, source_target_pairs={{0,8},{1,9},{2,10},{3,11},{4,12},{5,13},{6,14},{7,15},{8,0},{9,1},... | collective-permute-start | bytes 417800 | tf_op jit(solution)/shard_map/ppermute | solution.py:503
  94.7 5.0 %collective-permute-start.26 = (f32[8,256]{1,0:T(8,128)S(1)}, f32[8,256]{1,0:T(8,128)S(1)}, u32[]{:S(2)}, u32[]{:S(2)}) collective-permute-start(f32[8,256]{1,0:T(8,128)S(1)} %slice.14), channel_id=1, source_target_pairs={{0,24},{1,25},{2,26},{3,27},{4,28},{5,29},{6,30},{7,31},{8,16},{9,... | collective-permute-start | bytes 24584 | tf_op jit(solution)/shard_map/ppermute | solution.py:503
  96.7 3.4 %collective-permute-start.25 = (f32[8,256]{1,0:T(8,128)S(1)}, f32[8,256]{1,0:T(8,128)S(1)}, u32[]{:S(2)}, u32[]{:S(2)}) collective-permute-start(f32[8,256]{1,0:T(8,128)S(1)} %slice.14), channel_id=1, source_target_pairs={{0,16},{1,17},{2,18},{3,19},{4,20},{5,21},{6,22},{7,23},{8,24},{9,... | collective-permute-start | bytes 24584 | tf_op jit(solution)/shard_map/ppermute | solution.py:503
  101.4 5.0 %collective-permute-start.30 = (f32[136,256]{1,0:T(8,128)S(1)}, f32[136,256]{1,0:T(8,128)S(1)}, u32[]{:S(2)}, u32[]{:S(2)}) collective-permute-start(f32[136,256]{1,0:T(8,128)S(1)} %get-tuple-element.72.a_ref.pulled_ref), channel_id=1, source_target_pairs={{0,6},{1,7},{2,4},{3,5},{4,2},{5,3},{6,0},{7,1},{8,14},{9,15},{10,... | collective-permute-start | bytes 417800 | tf_op jit(solution)/shard_map/ppermute | solution.py:503
  102.6 5.6 %collective-permute-start.29 = (f32[136,256]{1,0:T(8,128)S(1)}, f32[136,256]{1,0:T(8,128)S(1)}, u32[]{:S(2)}, u32[]{:S(2)}) collective-permute-start(f32[136,256]{1,0:T(8,128)S(1)} %get-tuple-element.72.a_ref.pulled_ref), channel_id=1, source_target_pairs={{0,2},{1,3},{2,0},{3,1},{4,6},{5,7},{6,4},{7,5},{8,10},{9,11},{10,... | collective-permute-start | bytes 417800 | tf_op jit(solution)/shard_map/ppermute | solution.py:503
  102.9 5.3 %collective-permute-start.28 = (f32[136,256]{1,0:T(8,128)S(1)}, f32[136,256]{1,0:T(8,128)S(1)}, u32[]{:S(2)}, u32[]{:S(2)}) collective-permute-start(f32[136,256]{1,0:T(8,128)S(1)} %get-tuple-element.72.a_ref.pulled_ref), channel_id=1, source_target_pairs={{0,4},{1,5},{2,6},{3,7},{4,0},{5,1},{6,2},{7,3},{8,12},{9,13},{10,... | collective-permute-start | bytes 417800 | tf_op jit(solution)/shard_map/ppermute | solution.py:503
  108.7 4.7 %collective-permute-start.31 = (f32[392,256]{1,0:T(8,128)S(1)}, f32[392,256]{1,0:T(8,128)S(1)}, u32[]{:S(2)}, u32[]{:S(2)}) collective-permute-start(f32[392,256]{1,0:T(8,128)S(1)} %get-tuple-element.76), channel_id=1, source_target_pairs={{0,1},{1,0},{2,3},{3,2},{4,5},{5,4},{6,7},{7,6},{8,9},{9,8},{10,11... | collective-permute-start | bytes 1204232 | tf_op jit(solution)/shard_map/ppermute | solution.py:503
  113.5 5.0 %collective-permute-start.32 = (f32[136,256]{1,0:T(8,128)S(1)}, f32[136,256]{1,0:T(8,128)S(1)}, u32[]{:S(2)}, u32[]{:S(2)}) collective-permute-start(f32[136,256]{1,0:T(8,128)S(1)} %slice_add_fusion.here_ref), channel_id=1, source_target_pairs={{0,8},{1,9},{2,10},{3,11},{4,12},{5,13},{6,14},{7,15},{8,16},{9,17... | collective-permute-start | bytes 417800 | tf_op jit(solution)/shard_map/ppermute | solution.py:503
  117.8 7.6 %collective-permute-start.33 = (f32[256,256]{1,0:T(8,128)}, f32[256,256]{1,0:T(8,128)}, u32[]{:S(2)}, u32[]{:S(2)}) collective-permute-start(f32[256,256]{1,0:T(8,128)} %get-tuple-element.82), channel_id=1, source_target_pairs={{0,1},{1,0},{2,3},{3,2},{4,5},{5,4},{6,7},{7,6},{8,9},{9,8},{10,11... | collective-permute-start | bytes 786440 | tf_op jit(solution)/shard_map/ppermute | solution.py:503
  119.8 13.8 %all-to-all-start = ((f32[32,8,128]{2,1,0:T(8,128)}), f32[32,8,128]{2,1,0:T(8,128)S(1)}, u32[]{:S(2)}, u32[]{:S(2)}) async-start(f32[32,8,128]{2,1,0:T(8,128)} %plane_close.1), calls=%async_computation | async-start | bytes 262144 | tf_op jit(solution)/shard_map/all_to_all | solution.py:1153
  135.1 13.3 %collective-permute-start.34 = (f32[512,128]{1,0:T(8,128)S(1)}, f32[512,128]{1,0:T(8,128)S(1)}, u32[]{:S(2)}, u32[]{:S(2)}) collective-permute-start(f32[512,128]{1,0:T(8,128)S(1)} %plane_combine.1), channel_id=1, source_target_pairs={{0,0},{1,16},{2,8},{3,24},{4,4},{5,20},{6,12},{7,28},{8,1},{9,17},... | collective-permute-start | bytes 786440 | tf_op jit(solution)/shard_map/ppermute | solution.py:503
  (19 other events, 225.1 us)

commit v11 on v10

--- a/solution.py
+++ b/solution.py
@@ -607,71 +607,82 @@
     return product(first, turn(waves, spec, -1.0), order)
 
 
-def describe_kernel(inc_ref, gauge_ref, kind_ref, out_ref):
+def describe_kernel(inc_ref, seen_ref, later_ref, kind_ref, kernels_ref, wide_ref, forward, first, out_ref):
     blocks, slots, width = inc_ref.shape
+    rows = seen_ref.shape[0]
     tile = 8
-    rows = tile * slots
+    side = tile * slots
     weights = inc_ref[...].astype(F32).astype(BF16)
-    row = lax.broadcasted_iota(jnp.int32, (rows, rows), 0)
-    col = lax.broadcasted_iota(jnp.int32, (rows, rows), 1)
+    row = lax.broadcasted_iota(jnp.int32, (side, side), 0)
+    col = lax.broadcasted_iota(jnp.int32, (side, side), 1)
     same = row // slots == col // slots
     for i in range(blocks // tile):
-        flat = weights[i * tile : (i + 1) * tile].reshape(rows, width)
+        flat = weights[i * tile : (i + 1) * tile].reshape(side, width)
         full = lax.dot_general(flat, flat, (((1,), (1,)), ((), ())), preferred_element_type=F32)
         own = jnp.where(same, full, 0.0)
-        out_ref[pl.ds(0, slots), pl.ds(i * rows, rows)] = jnp.sum(own.reshape(tile, slots, rows), axis=0)
-    kinds = kind_ref.shape[1]
-    out_ref[pl.ds(slots, 8), :] = jnp.concatenate(
-        [
-            gauge_ref[...].astype(F32),
-            jnp.concatenate(
-                [kind_ref[...].astype(F32), jnp.zeros((1, blocks * slots - kinds), F32)], axis=1
-            ),
-            jnp.zeros((6, blocks * slots), F32),
-        ],
-        axis=0,
-    )
-
-
-def describe(incidence, row_gauge, gauge_kernel):
+        out_ref[pl.ds(0, slots), pl.ds(i * side, side)] = jnp.sum(own.reshape(tile, slots, side), axis=0)
+    spec = spectra(kind_ref[...].astype(F32), kernels_ref[...], wide_ref[...])
+    here, after = jnp.transpose(seen_ref[...]), jnp.transpose(later_ref[...])
+    pulled = plane_advanced(here, after, spec, forward[...], first[...], 3)
+    step = out_ref.shape[0] - slots
+    for i in range(HOURS // step):
+        out_ref[pl.ds(slots, step), pl.ds(i * rows, rows)] = pulled[i * step : (i + 1) * step]
+
+
+def describe(incidence, seen, later, gauge_kernel, kernels, wide, mats):
     blocks, slots, _ = incidence.shape
+    rows, hours = seen.shape
     count = blocks * slots
     return pl.pallas_call(
         describe_kernel,
-        out_shape=jax.ShapeDtypeStruct((slots + 8, count), F32),
+        out_shape=jax.ShapeDtypeStruct((slots + hours * rows // count, count), F32),
         compiler_params=params(),
         name="describe",
         cost_estimate=SMALL,
-    )(incidence, row_gauge.reshape(1, count), gauge_kernel.reshape(1, gauge_kernel.shape[0]))
-
-
-def send_kernel(inc_ref, field_ref, out_ref):
+    )(incidence, seen, later, gauge_kernel.reshape(1, rows), kernels, wide, *mats)
+
+
+def send_kernel(inc_ref, field_ref, gauge_ref, kind_ref, out_ref):
     blocks, slots, width = inc_ref.shape
+    count = blocks * slots
     weights = inc_ref[...].astype(F32).astype(BF16)
     parts = []
     for b in range(blocks):
         value = jnp.concatenate(pieces(field_ref[pl.ds(b * width, width), :], 3)[::-1], axis=0)
         parts.append(dot(jnp.concatenate([weights[b]] * 3, axis=1), value))
-    out_ref[...] = jnp.transpose(jnp.concatenate(parts, axis=0))
-
-
-def send(incidence, field):
+    out_ref[pl.ds(0, HOURS), :] = jnp.transpose(jnp.concatenate(parts, axis=0))
+    kinds = kind_ref.shape[1] // count
+    here = jnp.minimum(pl.program_id(0), kinds - 1) * count
+    out_ref[pl.ds(HOURS, 8), :] = jnp.concatenate(
+        [
+            gauge_ref[...].astype(F32),
+            kind_ref[:, pl.ds(pl.multiple_of(here, count), count)].astype(F32),
+            jnp.zeros((6, count), F32),
+        ],
+        axis=0,
+    )
+
+
+def send(incidence, field, row_gauge, gauge_kernel):
     blocks, slots, width = incidence.shape
-    hours = field.shape[1]
+    count = blocks * slots
+    rows = gauge_kernel.shape[0]
     step = 8
     return pl.pallas_call(
         send_kernel,
         grid=(blocks // step,),
         in_specs=[
             pl.BlockSpec((step, slots, width), lambda i: (i, 0, 0)),
-            pl.BlockSpec((step * width, hours), lambda i: (i, 0)),
+            pl.BlockSpec((step * width, HOURS), lambda i: (i, 0)),
+            pl.BlockSpec((1, step * slots), lambda i: (0, i)),
+            pl.BlockSpec((1, rows), lambda i: (0, 0)),
         ],
-        out_specs=pl.BlockSpec((hours, step * slots), lambda i: (0, i)),
-        out_shape=jax.ShapeDtypeStruct((hours, blocks * slots), F32),
+        out_specs=pl.BlockSpec((HOURS + 8, step * slots), lambda i: (0, i)),
+        out_shape=jax.ShapeDtypeStruct((HOURS + 8, count), F32),
         compiler_params=params(),
         name="send",
         cost_estimate=SMALL,
-    )(incidence, field)
+    )(incidence, field, row_gauge.reshape(1, count), gauge_kernel.reshape(1, rows))
 
 
 def hot_rows(gauge, first, rows):
@@ -679,28 +690,25 @@
     return jnp.where(gauge == mine, 1.0, 0.0).astype(BF16)
 
 
-def spread_kernel(first_ref, mine_ref, other_ref, meta_ref, meta_other_ref, *out_refs):
-    hours, rows = out_refs[0].shape
-    where = meta_ref.shape[0] - 8
-    value = jnp.concatenate([mine_ref[...], other_ref[...]], axis=1)
-    gauge = jnp.concatenate([ref[where : where + 1, :] for ref in (meta_ref, meta_other_ref)], axis=1)
-    stacked = jnp.concatenate(pieces(value, 3), axis=0)
+def spread_kernel(first_ref, mine_ref, other_ref, *out_refs):
+    rows = out_refs[0].shape[1]
+    both = jnp.concatenate([mine_ref[...], other_ref[...]], axis=1)
+    stacked = jnp.concatenate(pieces(both[:HOURS], 3), axis=0)
     for m, out_ref in enumerate(out_refs):
-        hot = hot_rows(gauge, first_ref[m], rows)
+        hot = hot_rows(both[HOURS : HOURS + 1], first_ref[m], rows)
         result = lax.dot_general(stacked, hot, (((1,), (1,)), ((), ())), preferred_element_type=F32)
-        out_ref[...] = (result[2 * hours :] + result[hours : 2 * hours]) + result[:hours]
-
-
-def spread(first, parcels, metas, rows):
-    hours = parcels[0].shape[0]
+        out_ref[...] = (result[2 * HOURS :] + result[HOURS : 2 * HOURS]) + result[:HOURS]
+
+
+def spread(first, parcels, rows):
     return pl.pallas_call(
         spread_kernel,
-        in_specs=[pl.BlockSpec(memory_space=pltpu.SMEM)] + [pl.BlockSpec(memory_space=pltpu.VMEM)] * 4,
-        out_shape=[jax.ShapeDtypeStruct((hours, rows), F32)] * 4,
+        in_specs=[pl.BlockSpec(memory_space=pltpu.SMEM)] + [pl.BlockSpec(memory_space=pltpu.VMEM)] * 2,
+        out_shape=[jax.ShapeDtypeStruct((HOURS, rows), F32)] * 4,
         compiler_params=params(),
         name="spread",
         cost_estimate=SMALL,
-    )(first, *parcels, *metas)
+    )(first, *parcels)
 
 
 def plane_couple_kernel(last, first_ref, *refs):
@@ -816,10 +824,9 @@
     value = jnp.concatenate([ref[pl.ds(0, HOURS), :] for ref in (a_ref, b_ref, c_ref, d_ref)], axis=1)
     one, two = pieces(value, 2)
     stacked = jnp.concatenate([two, one], axis=0)
-    where = meta_ref.shape[0] - 8
     picked = []
     for ref in (meta_ref, meta_other_ref):
-        gauge = ref[where : where + 1, :]
+        gauge = ref[0:1, :]
         hot = jnp.concatenate([hot_rows(gauge, first_ref[m], rows) for m in range(4)], axis=0)
         both = dot(stacked, hot)
         picked.append(both[:HOURS] + both[HOURS:])
@@ -869,8 +876,7 @@
 
 
 def plane_spectrum_kernel(class_ref, kernels_ref, wide_ref, out_ref):
-    where = class_ref.shape[0] - 7
-    kind = class_ref[where : where + 1, : out_ref.shape[1]]
+    kind = class_ref[1:2, : out_ref.shape[1]]
     out_ref[...] = spectra(kind, kernels_ref[...], wide_ref[...])
 
 
@@ -882,23 +888,6 @@
         name="plane_spectrum",
         cost_estimate=SMALL,
     )(meta, kernels, wide)
-
-
-def observe_kernel(seen_ref, later_ref, kind_ref, kernels_ref, wide_ref, forward, first, out_ref):
-    spec = spectra(kind_ref[...].astype(F32), kernels_ref[...], wide_ref[...])
-    here, after = jnp.transpose(seen_ref[...]), jnp.transpose(later_ref[...])
-    out_ref[...] = plane_advanced(here, after, spec, forward[...], first[...], 3)
-
-
-def observe(seen, later, gauge_kernel, kernels, wide, mats):
-    rows, hours = seen.shape
-    return pl.pallas_call(
-        observe_kernel,
-        out_shape=jax.ShapeDtypeStruct((hours, rows), F32),
-        compiler_params=params(),
-        name="observe",
-        cost_estimate=SMALL,
-    )(seen, later, gauge_kernel.reshape(1, rows), kernels, wide, *mats)
 
 
 def sides(even, pair, middle):
@@ -1081,23 +1070,26 @@
     forward3, inverse_first3, inverse_last3, short3 = turned_transforms(3)
     block, noted = (hours, rows), (hours + NOTE, rows)
 
-    parcel = send(incidence, first_guess)
-    parcel, near, gauges, kinds, seen = lax.optimization_barrier(
-        (parcel, incidence, row_gauge, gauge_kernel, observed)
-    )
+    parcel = send(incidence, first_guess, row_gauge, gauge_kernel)
+    parcel, near, kinds, seen = lax.optimization_barrier((parcel, incidence, gauge_kernel, observed))
     parcel = moved(parcel, to_plane)
-    meta = moved(describe(near, gauges, kinds), to_plane)
-    seen = observe(seen, moved(seen, hour_before), kinds, kernels, short3, [forward3, inverse_first3])
-    metas = [meta, moved(meta, over_core)]
-    spec = plane_spectrum(meta, kernels, short3, rows)
-    parcel, seen, metas, spec = lax.optimization_barrier((parcel, seen, metas, spec))
-    seen = moved(seen, to_plane)
-    both = jnp.concatenate(metas, axis=1)
-    around = [both] + [moved(both, where) for where in SQUARE]
-
-    dense = spread(first, [parcel, moved(parcel, over_core)], metas, rows)
+    behind = describe(
+        near, seen, moved(seen, hour_before), kinds, kernels, short3, [forward3, inverse_first3]
+    )
+    behind = moved(behind, to_plane)
+    parcels = [parcel, moved(parcel, over_core)]
+    parcels[1], behind = lax.optimization_barrier((parcels[1], behind))
+    dense = spread(first, parcels, rows)
+    slots = incidence.shape[1]
+    gram, seen = behind[:slots], behind[slots:]
+    seen = jnp.concatenate([seen[:, i : i + rows] for i in range(0, seen.shape[1], rows)], axis=0)
+    metas = [value[hours:] for value in parcels]
+    spec = plane_spectrum(metas[0], kernels, short3, rows)
     sums = dense[0] + sum(moved(value, where) for value, where in zip(dense[1:], SQUARE))
     sums = [sums, moved(sums, z_pair), moved(sums, z_middle)]
+    both = jnp.concatenate([gram, moved(gram, over_core)], axis=1)
+    both = jnp.concatenate([both, jnp.concatenate(metas, axis=1)], axis=0)
+    around = [both] + [moved(both, where) for where in SQUARE]
     coupled = plane_couple(first, around[:2], rows)
     coupled, sums = lax.optimization_barrier((coupled, sums))
     coupling = plane_couple(first, around[2:], rows, coupled)
@@ -1154,7 +1146,7 @@
     (answer,) = plane_call(
         plane_combine_kernel,
         "plane_combine",
-        [(metas[0].shape[1], hours)],
+        [(parcel.shape[1], hours)],
         [],
         [open_note, close_note, kernels, stack, picked, moved(theirs, over_core)],
     )

time: 151 us -> 149 us (0.987)
  starting transfers between devices: 62 us -> 56.9 us
  local copies, waits for them, and re-layouts: 2.7 us -> 5.36 us
    ppermute x35 -> x34, starting transfers between devices: 56.5 us -> 51.4 us  [moved(): return lax.ppermute(value, ('basin', 'tm'), pairs)]
    unnamed x31 -> x36, local copies, waits for them, and re-layouts: 2.61 us -> 5.26 us
    ppermute x35 -> x34, waiting for transfers between devices: 44.2 us -> 45.5 us  [moved(): return lax.ppermute(value, ('basin', 'tm'), pairs)]
  transfers between devices with their start and end apart: 36 -> 35, of which waited for: 19 -> 16; matrix products, arithmetic and copies ran while one was open for 0% -> 0% of each run, Pallas kernels for 14% -> 15%
where the time goes in v11:
time: 149 us
  starting transfers between devices  56.9 us (38%)
  waiting for transfers between devices  53.7 us (36%)
  Pallas kernels  31.9 us (21%)
  local copies, waits for them, and re-layouts  5.36 us (4%)
    ppermute x34, starting transfers between devices, moved(): return lax.ppermute(value, ('basin', 'tm'), pairs)  51.4 us
    ppermute x34, waiting for transfers between devices, moved(): return lax.ppermute(value, ('basin', 'tm'), pairs)  45.5 us
    pallas_call x2, Pallas kernels, plane_couple(): pl.pallas_call(functools.partial(plane_couple_kernel, last), in_specs=[pl...  9.55 us
    pallas_call x6, Pallas kernels, plane_call(): pl.pallas_call(kernel, in_specs=[pl.BlockSpec(memory_space=pltpu.SMEM)] *...  8.85 us
    all_to_all x1, waiting for transfers between devices, plane_shards(): close_note = lax.all_to_all(note, ('basin', 'tm'), 0, 0, tiled=False)  8.18 us
    all_to_all x1, starting transfers between devices, plane_shards(): close_note = lax.all_to_all(note, ('basin', 'tm'), 0, 0, tiled=False)  5.49 us
    unnamed x36, local copies, waits for them, and re-layouts  5.26 us
    pallas_call x3, Pallas kernels, plane_rows(): pl.pallas_call(plane_rows_kernel, in_specs=[pl.BlockSpec(memory_space=plt...  4.5 us
  transfers between devices with their start and end apart: 35, of which 16 were waited for; matrix products, arithmetic and copies ran while one was open for 0% of the time, Pallas kernels for 15%

profile of v11, /device:TPU:1, one launch (start us, length us, event | category | flops | bytes accessed | tf_op | source)
XLA Modules:
  0.0 148.6 jit_solution(6001298118750594058)
XLA Ops:
  0.0 1.6 %copy-done = f32[4096,128]{1,0:T(8,128)S(1)} copy-done((f32[4096,128]{1,0:T(8,128)S(1)}, f32[4096,128]{1,0:T(8,128)}, u32[]{:S(2)}) %copy-start) | copy-done | bytes 2097176
  5.4 4.6 %collective-permute-start = (f32[136,512]{1,0:T(8,128)S(1)}, f32[136,512]{1,0:T(8,128)S(1)}, u32[]{:S(2)}, u32[]{:S(2)}) collective-permute-start(f32[136,512]{1,0:T(8,128)S(1)} %send.1), channel_id=1, source_target_pairs={{0,0},{1,8},{2,16},{3,24},{4,4},{5,12},{6,20},{7,28},{8,2},{9,10},... | collective-permute-start | bytes 835592 | tf_op jit(solution)/shard_map/ppermute | solution.py:503
  10.0 1.9 %collective-permute-start.2 = (f32[256,128]{1,0:T(8,128)S(1)}, f32[256,128]{1,0:T(8,128)S(1)}, u32[]{:S(2)}, u32[]{:S(2)}) collective-permute-start(f32[256,128]{1,0:T(8,128)S(1)} %copy-done.12), channel_id=1, source_target_pairs={{1,0},{2,1},{3,2},{5,4},{6,5},{7,6},{9,8},{10,9},{11,10},{13,12},{... | collective-permute-start | bytes 393224 | tf_op jit(solution)/shard_map/ppermute | solution.py:503
  12.0 5.0 %collective-permute-done.2.later_ref = f32[256,128]{1,0:T(8,128)S(1)} collective-permute-done((f32[256,128]{1,0:T(8,128)S(1)}, f32[256,128]{1,0:T(8,128)S(1)}, u32[]{:S(2)}, u32[]{:S(2)}) %collective-permute-start.2) | collective-permute-done | bytes 131104 | tf_op jit(solution)/shard_map/ppermute | solution.py:503
  18.3 1.9 %collective-permute-start.3 = (f32[80,512]{1,0:T(8,128)S(1)}, f32[80,512]{1,0:T(8,128)S(1)}, u32[]{:S(2)}, u32[]{:S(2)}) collective-permute-start(f32[80,512]{1,0:T(8,128)S(1)} %describe.1), channel_id=1, source_target_pairs={{0,0},{1,8},{2,16},{3,24},{4,4},{5,12},{6,20},{7,28},{8,2},{9,10},... | collective-permute-start | bytes 491528 | tf_op jit(solution)/shard_map/ppermute | solution.py:503
  20.3 5.1 %collective-permute-done.mine_ref = f32[136,512]{1,0:T(8,128)S(1)} collective-permute-done((f32[136,512]{1,0:T(8,128)S(1)}, f32[136,512]{1,0:T(8,128)S(1)}, u32[]{:S(2)}, u32[]{:S(2)}) %collective-permute-start) | collective-permute-done | bytes 278560 | tf_op jit(solution)/shard_map/ppermute | solution.py:503
  26.1 4.4 %collective-permute-done.3 = f32[80,512]{1,0:T(8,128)S(1)} collective-permute-done((f32[80,512]{1,0:T(8,128)S(1)}, f32[80,512]{1,0:T(8,128)S(1)}, u32[]{:S(2)}, u32[]{:S(2)}) %collective-permute-start.3) | collective-permute-done | bytes 163872 | tf_op jit(solution)/shard_map/ppermute | solution.py:503
  30.6 1.6 %spread.1 = (f32[128,256]{1,0:T(8,128)S(1)}, f32[128,256]{1,0:T(8,128)S(1)}, f32[128,256]{1,0:T(8,128)S(1)}, f32[128,256]{1,0:T(8,128)S(1)}) custom-call(s32[6]{0:T(128)S(1)} %broadcast_multiply_fusion.first_ref, f32[136,512]{1,0:T(8,128)S(1)} %collective-permute-done.mine_ref, f32[136,512]{1,0:T(8,128)S(1)} %collective-permute-done.1.other_ref), custom_call_target="tpu_custom_call" | custom-call | flops 1 | bytes 1 | tf_op jit(solution)/shard_map/spread/pallas_call | solution.py:704
  33.4 1.4 collective-permute-start.10
  37.6 2.7 %collective-permute-done.9 = f32[128,256]{1,0:T(8,128)S(1)} collective-permute-done((f32[128,256]{1,0:T(8,128)S(1)}, f32[128,256]{1,0:T(8,128)S(1)}, u32[]{:S(2)}, u32[]{:S(2)}) %collective-permute-start.9) | collective-permute-done | bytes 131104 | tf_op jit(solution)/shard_map/ppermute | solution.py:503
  41.2 4.8 %collective-permute-start.11 = (f32[128,256]{1,0:T(8,128)S(1)}, f32[128,256]{1,0:T(8,128)S(1)}, u32[]{:S(2)}, u32[]{:S(2)}) collective-permute-start(f32[128,256]{1,0:T(8,128)S(1)} %add_add_fusion.here_ref), channel_id=1, source_target_pairs={{0,8},{1,9},{2,10},{3,11},{4,12},{5,13},{6,14},{7,15},{8,0},{9,1},... | collective-permute-start | bytes 393224 | tf_op jit(solution)/shard_map/ppermute | solution.py:503
  46.0 4.6 %plane_couple.2.refs_2_ = f32[1024,512]{1,0:T(8,128)S(1)} custom-call(s32[6]{0:T(128)S(1)} %broadcast_multiply_fusion.first_ref, f32[24,1024]{1,0:T(8,128)S(1)} %maximum_maximum_fusion.refs_0_, f32[24,1024]{1,0:T(8,128)S(1)} %collective-permute-done.7.refs_1_), custom_call_target="tpu_custom_call" | custom-call | flops 2147483648 | bytes 2000000 | tf_op jit(solution)/shard_map/plane_couple/pallas_call | solution.py:771
  50.7 2.5 %plane_first.1.a_ref.pulled_ref.old_z_ref = f32[128,256]{1,0:T(8,128)S(1)} custom-call(f32[3]{0:T(128)S(1)} %add_convert_fusion.flag_ref, f32[128,256]{1,0:T(8,128)S(1)} %add_add_fusion.here_ref, f32[128,256]{1,0:T(8,128)S(1)} %collective-permute-done.11.pair_ref, f32[128,256]{1,0:T(8,128)S(1)} %collective-permute-done.12.middle_ref, ...), custom_call_target="tpu_custom_call" | custom-call | flops 1 | bytes 1 | tf_op jit(solution)/shard_map/plane_first/pallas_call | solution.py:898
  53.2 1.5 %collective-permute-start.15 = (f32[128,256]{1,0:T(8,128)S(1)}, f32[128,256]{1,0:T(8,128)S(1)}, u32[]{:S(2)}, u32[]{:S(2)}) collective-permute-start(f32[128,256]{1,0:T(8,128)S(1)} %plane_first.1.a_ref.pulled_ref.old_z_ref), channel_id=1, source_target_pairs={{0,6},{1,7},{2,4},{3,5},{4,2},{5,3},{6,0},{7,1},{8,14},{9,15},{10,... | collective-permute-start | bytes 393224 | tf_op jit(solution)/shard_map/ppermute | solution.py:503
  56.0 4.9 %plane_couple.3 = (bf16[1024,512]{1,0:T(8,128)(2,1)S(1)}, bf16[1024,512]{1,0:T(8,128)(2,1)S(1)}) custom-call(s32[6]{0:T(128)S(1)} %broadcast_multiply_fusion.first_ref, f32[24,1024]{1,0:T(8,128)S(1)} %collective-permute-done.5.refs_0_, f32[24,1024]{1,0:T(8,128)S(1)} %collective-permute-done.6.refs_1_, f32[1024,512]{1,0:T(8,128)S(1)} %plane_couple.2.refs_2_), custom_call_target="tpu_custom_call" | custom-call | flops 2147483648 | bytes 2000000 | tf_op jit(solution)/shard_map/plane_couple/pallas_call | solution.py:771
  61.6 5.1 %collective-permute-start.16 = (f32[128,256]{1,0:T(8,128)S(1)}, f32[128,256]{1,0:T(8,128)S(1)}, u32[]{:S(2)}, u32[]{:S(2)}) collective-permute-start(f32[128,256]{1,0:T(8,128)S(1)} %get-tuple-element.57), channel_id=1, source_target_pairs={{0,1},{1,0},{2,3},{3,2},{4,5},{5,4},{6,7},{7,6},{8,9},{9,8},{10,11... | collective-permute-start | bytes 393224 | tf_op jit(solution)/shard_map/ppermute | solution.py:503
  69.7 3.5 %collective-permute-done.17.pair_ref = f32[128,256]{1,0:T(8,128)S(1)} collective-permute-done((f32[128,256]{1,0:T(8,128)S(1)}, f32[128,256]{1,0:T(8,128)S(1)}, u32[]{:S(2)}, u32[]{:S(2)}) %collective-permute-start.17) | collective-permute-done | bytes 131104 | tf_op jit(solution)/shard_map/ppermute | solution.py:503
  73.2 1.8 %plane_open.1 = (f32[136,256]{1,0:T(8,128)S(1)}, f32[256,256]{1,0:T(8,128)S(1)}) custom-call(f32[3]{0:T(128)S(1)} %add_convert_fusion.flag_ref, f32[128,256]{1,0:T(8,128)S(1)} %add.61.here_ref.old_s_ref, f32[128,256]{1,0:T(8,128)S(1)} %collective-permute-done.17.pair_ref, f32[128,256]{1,0:T(8,128)S(1)} %collective-permute-done.18.middle_ref, ...), custom_call_target="tpu_custom_call" | custom-call | flops 1 | bytes 1 | tf_op jit(solution)/shard_map/plane_open/pallas_call | solution.py:898
  75.0 1.8 %collective-permute-start.21 = (f32[136,256]{1,0:T(8,128)S(1)}, f32[136,256]{1,0:T(8,128)S(1)}, u32[]{:S(2)}, u32[]{:S(2)}) collective-permute-start(f32[136,256]{1,0:T(8,128)S(1)} %get-tuple-element.58.a_ref.pulled_ref), channel_id=1, source_target_pairs={{0,6},{1,7},{2,4},{3,5},{4,2},{5,3},{6,0},{7,1},{8,14},{9,15},{10,... | collective-permute-start | bytes 417800 | tf_op jit(solution)/shard_map/ppermute | solution.py:503
  79.9 4.1 %collective-permute-done.20.c_ref = f32[136,256]{1,0:T(8,128)S(1)} collective-permute-done((f32[136,256]{1,0:T(8,128)S(1)}, f32[136,256]{1,0:T(8,128)S(1)}, u32[]{:S(2)}, u32[]{:S(2)}) %collective-permute-start.20) | collective-permute-done | bytes 139296 | tf_op jit(solution)/shard_map/ppermute | solution.py:503
  84.6 1.7 %collective-permute-start.22 = (f32[392,256]{1,0:T(8,128)S(1)}, f32[392,256]{1,0:T(8,128)S(1)}, u32[]{:S(2)}, u32[]{:S(2)}) collective-permute-start(f32[392,256]{1,0:T(8,128)S(1)} %get-tuple-element.61), channel_id=1, source_target_pairs={{0,1},{1,0},{2,3},{3,2},{4,5},{5,4},{6,7},{7,6},{8,9},{9,8},{10,11... | collective-permute-start | bytes 1204232 | tf_op jit(solution)/shard_map/ppermute | solution.py:503
  88.5 3.7 %collective-permute-start.23 = (f32[136,256]{1,0:T(8,128)S(1)}, f32[136,256]{1,0:T(8,128)S(1)}, u32[]{:S(2)}, u32[]{:S(2)}) collective-permute-start(f32[136,256]{1,0:T(8,128)S(1)} %slice_add_fusion.1.here_ref), channel_id=1, source_target_pairs={{0,8},{1,9},{2,10},{3,11},{4,12},{5,13},{6,14},{7,15},{8,0},{9,1},... | collective-permute-start | bytes 417800 | tf_op jit(solution)/shard_map/ppermute | solution.py:503
  93.5 2.2 %collective-permute-done.23.pair_ref = f32[136,256]{1,0:T(8,128)S(1)} collective-permute-done((f32[136,256]{1,0:T(8,128)S(1)}, f32[136,256]{1,0:T(8,128)S(1)}, u32[]{:S(2)}, u32[]{:S(2)}) %collective-permute-start.23) | collective-permute-done | bytes 139296 | tf_op jit(solution)/shard_map/ppermute | solution.py:503
  103.8 1.9 %collective-permute-done.28.c_ref = f32[136,256]{1,0:T(8,128)S(1)} collective-permute-done((f32[136,256]{1,0:T(8,128)S(1)}, f32[136,256]{1,0:T(8,128)S(1)}, u32[]{:S(2)}, u32[]{:S(2)}) %collective-permute-start.28) | collective-permute-done | bytes 139296 | tf_op jit(solution)/shard_map/ppermute | solution.py:503
  106.3 3.2 %collective-permute-start.30 = (f32[392,256]{1,0:T(8,128)S(1)}, f32[392,256]{1,0:T(8,128)S(1)}, u32[]{:S(2)}, u32[]{:S(2)}) collective-permute-start(f32[392,256]{1,0:T(8,128)S(1)} %get-tuple-element.68), channel_id=1, source_target_pairs={{0,1},{1,0},{2,3},{3,2},{4,5},{5,4},{6,7},{7,6},{8,9},{9,8},{10,11... | collective-permute-start | bytes 1204232 | tf_op jit(solution)/shard_map/ppermute | solution.py:503
  110.8 3.0 %collective-permute-start.31 = (f32[136,256]{1,0:T(8,128)S(1)}, f32[136,256]{1,0:T(8,128)S(1)}, u32[]{:S(2)}, u32[]{:S(2)}) collective-permute-start(f32[136,256]{1,0:T(8,128)S(1)} %slice_add_fusion.here_ref), channel_id=1, source_target_pairs={{0,8},{1,9},{2,10},{3,11},{4,12},{5,13},{6,14},{7,15},{8,16},{9,17... | collective-permute-start | bytes 417800 | tf_op jit(solution)/shard_map/ppermute | solution.py:503
  113.9 2.0 %plane_rows.5 = (f32[128,512]{1,0:T(8,128)S(1)}, f32[256,256]{1,0:T(8,128)}, f32[256,512]{1,0:T(8,128)S(1)}) custom-call(s32[6]{0:T(128)S(1)} %broadcast_multiply_fusion.first_ref, f32[8,512]{1,0:T(8,128)S(1)} %slice.36.class_ref.meta_ref, f32[8,512]{1,0:T(8,128)S(1)} %slice.30.meta_other_ref, f32[136,256]{1,0:T(8,128)S(1)} %get-tuple-element.64.a_ref.pulled_ref, ...), custom_call_target="tpu_custom_call" | custom-call | flops 1000000000 | bytes 2000000 | tf_op jit(solution)/shard_map/plane_rows/pallas_call | solution.py:854
  117.9 5.5 %all-to-all-start = ((f32[32,8,128]{2,1,0:T(8,128)}), f32[32,8,128]{2,1,0:T(8,128)S(1)}, u32[]{:S(2)}, u32[]{:S(2)}) async-start(f32[32,8,128]{2,1,0:T(8,128)} %plane_close.1), calls=%async_computation | async-start | bytes 262144 | tf_op jit(solution)/shard_map/all_to_all | solution.py:1145
  123.4 8.2 %all-to-all-done.close_ref = f32[32,8,128]{2,1,0:T(8,128)S(1)} async-done(((f32[32,8,128]{2,1,0:T(8,128)}), f32[32,8,128]{2,1,0:T(8,128)S(1)}, u32[]{:S(2)}, u32[]{:S(2)}) %all-to-all-start) | async-done | bytes 131104 | tf_op jit(solution)/shard_map/all_to_all | solution.py:1145
  132.9 2.6 %collective-permute-start.33 = (f32[512,128]{1,0:T(8,128)S(1)}, f32[512,128]{1,0:T(8,128)S(1)}, u32[]{:S(2)}, u32[]{:S(2)}) collective-permute-start(f32[512,128]{1,0:T(8,128)S(1)} %plane_combine.1), channel_id=1, source_target_pairs={{0,0},{1,16},{2,8},{3,24},{4,4},{5,20},{6,12},{7,28},{8,1},{9,17},... | collective-permute-start | bytes 786440 | tf_op jit(solution)/shard_map/ppermute | solution.py:503
  135.5 10.7 %collective-permute-done.33.rows_ref = f32[512,128]{1,0:T(8,128)S(1)} collective-permute-done((f32[512,128]{1,0:T(8,128)S(1)}, f32[512,128]{1,0:T(8,128)S(1)}, u32[]{:S(2)}, u32[]{:S(2)}) %collective-permute-start.33) | collective-permute-done | bytes 262176 | tf_op jit(solution)/shard_map/ppermute | solution.py:503
  146.2 2.4 %plane_finish.1 = f32[4096,128]{1,0:T(8,128)} custom-call(f32[512,128]{1,0:T(8,128)S(1)} %collective-permute-done.33.rows_ref, s32[32,16,128]{2,1,0:T(8,128)S(1)} %copy-done.5, f32[4096,128]{1,0:T(8,128)S(1)} %copy-done.1), custom_call_target="tpu_custom_call" | custom-call | tf_op jit(solution)/shard_map/plane_finish/pallas_call | solution.py:1046
  (107 shorter events, 36.2 us)
Async XLA Ops:
  5.4 20.0 %collective-permute-start = (f32[136,512]{1,0:T(8,128)S(1)}, f32[136,512]{1,0:T(8,128)S(1)}, u32[]{:S(2)}, u32[]{:S(2)}) collective-permute-start(f32[136,512]{1,0:T(8,128)S(1)} %send.1), channel_id=1, source_target_pairs={{0,0},{1,8},{2,16},{3,24},{4,4},{5,12},{6,20},{7,28},{8,2},{9,10},... | collective-permute-start | bytes 835592 | tf_op jit(solution)/shard_map/ppermute | solution.py:503
  10.0 7.0 %collective-permute-start.2 = (f32[256,128]{1,0:T(8,128)S(1)}, f32[256,128]{1,0:T(8,128)S(1)}, u32[]{:S(2)}, u32[]{:S(2)}) collective-permute-start(f32[256,128]{1,0:T(8,128)S(1)} %copy-done.12), channel_id=1, source_target_pairs={{1,0},{2,1},{3,2},{5,4},{6,5},{7,6},{9,8},{10,9},{11,10},{13,12},{... | collective-permute-start | bytes 393224 | tf_op jit(solution)/shard_map/ppermute | solution.py:503
  18.3 12.1 %collective-permute-start.3 = (f32[80,512]{1,0:T(8,128)S(1)}, f32[80,512]{1,0:T(8,128)S(1)}, u32[]{:S(2)}, u32[]{:S(2)}) collective-permute-start(f32[80,512]{1,0:T(8,128)S(1)} %describe.1), channel_id=1, source_target_pairs={{0,0},{1,8},{2,16},{3,24},{4,4},{5,12},{6,20},{7,28},{8,2},{9,10},... | collective-permute-start | bytes 491528 | tf_op jit(solution)/shard_map/ppermute | solution.py:503
  25.3 5.2 %collective-permute-start.1 = (f32[136,512]{1,0:T(8,128)S(1)}, f32[136,512]{1,0:T(8,128)S(1)}, u32[]{:S(2)}, u32[]{:S(2)}) collective-permute-start(f32[136,512]{1,0:T(8,128)S(1)} %collective-permute-done.mine_ref), channel_id=1, source_target_pairs={{0,1},{1,0},{2,3},{3,2},{4,5},{5,4},{6,7},{7,6},{8,9},{9,8},{10,11... | collective-permute-start | bytes 835592 | tf_op jit(solution)/shard_map/ppermute | solution.py:503
  30.5 4.4 %collective-permute-start.4 = (f32[16,512]{1,0:T(8,128)S(1)}, f32[16,512]{1,0:T(8,128)S(1)}, u32[]{:S(2)}, u32[]{:S(2)}) collective-permute-start(f32[16,512]{1,0:T(8,128)S(1)} %slice.28), channel_id=1, source_target_pairs={{0,1},{1,0},{2,3},{3,2},{4,5},{5,4},{6,7},{7,6},{8,9},{9,8},{10,11... | collective-permute-start | bytes 98312 | tf_op jit(solution)/shard_map/ppermute | solution.py:503
  32.2 4.6 %collective-permute-start.8 = (f32[128,256]{1,0:T(8,128)S(1)}, f32[128,256]{1,0:T(8,128)S(1)}, u32[]{:S(2)}, u32[]{:S(2)}) collective-permute-start(f32[128,256]{1,0:T(8,128)S(1)} %get-tuple-element.47), channel_id=1, source_target_pairs={{0,4},{1,5},{2,6},{3,7},{4,0},{5,1},{6,2},{7,3},{8,12},{9,13},{10,... | collective-permute-start | bytes 393224 | tf_op jit(solution)/shard_map/ppermute | solution.py:503
  33.4 6.9 %collective-permute-start.9 = (f32[128,256]{1,0:T(8,128)S(1)}, f32[128,256]{1,0:T(8,128)S(1)}, u32[]{:S(2)}, u32[]{:S(2)}) collective-permute-start(f32[128,256]{1,0:T(8,128)S(1)} %get-tuple-element.48), channel_id=1, source_target_pairs={{0,2},{1,3},{2,0},{3,1},{4,6},{5,7},{6,4},{7,5},{8,10},{9,11},{10,... | collective-permute-start | bytes 393224 | tf_op jit(solution)/shard_map/ppermute | solution.py:503
  33.4 6.9 %collective-permute-start.10 = (f32[128,256]{1,0:T(8,128)S(1)}, f32[128,256]{1,0:T(8,128)S(1)}, u32[]{:S(2)}, u32[]{:S(2)}) collective-permute-start(f32[128,256]{1,0:T(8,128)S(1)} %get-tuple-element.49), channel_id=1, source_target_pairs={{0,6},{1,7},{2,4},{3,5},{4,2},{5,3},{6,0},{7,1},{8,14},{9,15},{10,... | collective-permute-start | bytes 393224 | tf_op jit(solution)/shard_map/ppermute | solution.py:503
  34.9 11.1 %collective-permute-start.7 = (f32[24,1024]{1,0:T(8,128)S(1)}, f32[24,1024]{1,0:T(8,128)S(1)}, u32[]{:S(2)}, u32[]{:S(2)}) collective-permute-start(f32[24,1024]{1,0:T(8,128)S(1)} %maximum_maximum_fusion.refs_0_), channel_id=1, source_target_pairs={{0,4},{1,5},{2,6},{3,7},{4,0},{5,1},{6,2},{7,3},{8,12},{9,13},{10,... | collective-permute-start | bytes 294920 | tf_op jit(solution)/shard_map/ppermute | solution.py:503
  36.2 19.8 %collective-permute-start.6 = (f32[24,1024]{1,0:T(8,128)S(1)}, f32[24,1024]{1,0:T(8,128)S(1)}, u32[]{:S(2)}, u32[]{:S(2)}) collective-permute-start(f32[24,1024]{1,0:T(8,128)S(1)} %maximum_maximum_fusion.refs_0_), channel_id=1, source_target_pairs={{0,6},{1,7},{2,4},{3,5},{4,2},{5,3},{6,0},{7,1},{8,14},{9,15},{10,... | collective-permute-start | bytes 294920 | tf_op jit(solution)/shard_map/ppermute | solution.py:503
  36.8 19.2 %collective-permute-start.5 = (f32[24,1024]{1,0:T(8,128)S(1)}, f32[24,1024]{1,0:T(8,128)S(1)}, u32[]{:S(2)}, u32[]{:S(2)}) collective-permute-start(f32[24,1024]{1,0:T(8,128)S(1)} %maximum_maximum_fusion.refs_0_), channel_id=1, source_target_pairs={{0,2},{1,3},{2,0},{3,1},{4,6},{5,7},{6,4},{7,5},{8,10},{9,11},{10,... | collective-permute-start | bytes 294920 | tf_op jit(solution)/shard_map/ppermute | solution.py:503
  40.4 10.3 %collective-permute-start.12 = (f32[128,256]{1,0:T(8,128)S(1)}, f32[128,256]{1,0:T(8,128)S(1)}, u32[]{:S(2)}, u32[]{:S(2)}) collective-permute-start(f32[128,256]{1,0:T(8,128)S(1)} %add_add_fusion.here_ref), channel_id=1, source_target_pairs={{8,16},{9,17},{10,18},{11,19},{12,20},{13,21},{14,22},{15,23},{16,... | collective-permute-start | bytes 393224 | tf_op jit(solution)/shard_map/ppermute | solution.py:503
  41.2 9.5 %collective-permute-start.11 = (f32[128,256]{1,0:T(8,128)S(1)}, f32[128,256]{1,0:T(8,128)S(1)}, u32[]{:S(2)}, u32[]{:S(2)}) collective-permute-start(f32[128,256]{1,0:T(8,128)S(1)} %add_add_fusion.here_ref), channel_id=1, source_target_pairs={{0,8},{1,9},{2,10},{3,11},{4,12},{5,13},{6,14},{7,15},{8,0},{9,1},... | collective-permute-start | bytes 393224 | tf_op jit(solution)/shard_map/ppermute | solution.py:503
  53.2 7.7 %collective-permute-start.15 = (f32[128,256]{1,0:T(8,128)S(1)}, f32[128,256]{1,0:T(8,128)S(1)}, u32[]{:S(2)}, u32[]{:S(2)}) collective-permute-start(f32[128,256]{1,0:T(8,128)S(1)} %plane_first.1.a_ref.pulled_ref.old_z_ref), channel_id=1, source_target_pairs={{0,6},{1,7},{2,4},{3,5},{4,2},{5,3},{6,0},{7,1},{8,14},{9,15},{10,... | collective-permute-start | bytes 393224 | tf_op jit(solution)/shard_map/ppermute | solution.py:503
  54.7 6.2 %collective-permute-start.14 = (f32[128,256]{1,0:T(8,128)S(1)}, f32[128,256]{1,0:T(8,128)S(1)}, u32[]{:S(2)}, u32[]{:S(2)}) collective-permute-start(f32[128,256]{1,0:T(8,128)S(1)} %plane_first.1.a_ref.pulled_ref.old_z_ref), channel_id=1, source_target_pairs={{0,2},{1,3},{2,0},{3,1},{4,6},{5,7},{6,4},{7,5},{8,10},{9,11},{10,... | collective-permute-start | bytes 393224 | tf_op jit(solution)/shard_map/ppermute | solution.py:503
  56.0 5.0 %collective-permute-start.13 = (f32[128,256]{1,0:T(8,128)S(1)}, f32[128,256]{1,0:T(8,128)S(1)}, u32[]{:S(2)}, u32[]{:S(2)}) collective-permute-start(f32[128,256]{1,0:T(8,128)S(1)} %plane_first.1.a_ref.pulled_ref.old_z_ref), channel_id=1, source_target_pairs={{0,4},{1,5},{2,6},{3,7},{4,0},{5,1},{6,2},{7,3},{8,12},{9,13},{10,... | collective-permute-start | bytes 393224 | tf_op jit(solution)/shard_map/ppermute | solution.py:503
  61.6 6.1 %collective-permute-start.16 = (f32[128,256]{1,0:T(8,128)S(1)}, f32[128,256]{1,0:T(8,128)S(1)}, u32[]{:S(2)}, u32[]{:S(2)}) collective-permute-start(f32[128,256]{1,0:T(8,128)S(1)} %get-tuple-element.57), channel_id=1, source_target_pairs={{0,1},{1,0},{2,3},{3,2},{4,5},{5,4},{6,7},{7,6},{8,9},{9,8},{10,11... | collective-permute-start | bytes 393224 | tf_op jit(solution)/shard_map/ppermute | solution.py:503
  68.4 4.8 %collective-permute-start.17 = (f32[128,256]{1,0:T(8,128)S(1)}, f32[128,256]{1,0:T(8,128)S(1)}, u32[]{:S(2)}, u32[]{:S(2)}) collective-permute-start(f32[128,256]{1,0:T(8,128)S(1)} %add.61.here_ref.old_s_ref), channel_id=1, source_target_pairs={{0,8},{1,9},{2,10},{3,11},{4,12},{5,13},{6,14},{7,15},{8,0},{9,1},... | collective-permute-start | bytes 393224 | tf_op jit(solution)/shard_map/ppermute | solution.py:503
  75.0 4.9 %collective-permute-start.21 = (f32[136,256]{1,0:T(8,128)S(1)}, f32[136,256]{1,0:T(8,128)S(1)}, u32[]{:S(2)}, u32[]{:S(2)}) collective-permute-start(f32[136,256]{1,0:T(8,128)S(1)} %get-tuple-element.58.a_ref.pulled_ref), channel_id=1, source_target_pairs={{0,6},{1,7},{2,4},{3,5},{4,2},{5,3},{6,0},{7,1},{8,14},{9,15},{10,... | collective-permute-start | bytes 417800 | tf_op jit(solution)/shard_map/ppermute | solution.py:503
  76.8 7.3 %collective-permute-start.20 = (f32[136,256]{1,0:T(8,128)S(1)}, f32[136,256]{1,0:T(8,128)S(1)}, u32[]{:S(2)}, u32[]{:S(2)}) collective-permute-start(f32[136,256]{1,0:T(8,128)S(1)} %get-tuple-element.58.a_ref.pulled_ref), channel_id=1, source_target_pairs={{0,2},{1,3},{2,0},{3,1},{4,6},{5,7},{6,4},{7,5},{8,10},{9,11},{10,... | collective-permute-start | bytes 417800 | tf_op jit(solution)/shard_map/ppermute | solution.py:503
  76.9 7.2 %collective-permute-start.19 = (f32[136,256]{1,0:T(8,128)S(1)}, f32[136,256]{1,0:T(8,128)S(1)}, u32[]{:S(2)}, u32[]{:S(2)}) collective-permute-start(f32[136,256]{1,0:T(8,128)S(1)} %get-tuple-element.58.a_ref.pulled_ref), channel_id=1, source_target_pairs={{0,4},{1,5},{2,6},{3,7},{4,0},{5,1},{6,2},{7,3},{8,12},{9,13},{10,... | collective-permute-start | bytes 417800 | tf_op jit(solution)/shard_map/ppermute | solution.py:503
  87.7 5.8 %collective-permute-start.26 = (f32[136,256]{1,0:T(8,128)S(1)}, f32[136,256]{1,0:T(8,128)S(1)}, u32[]{:S(2)}, u32[]{:S(2)}) collective-permute-start(f32[136,256]{1,0:T(8,128)S(1)} %slice_add_fusion.1.here_ref), channel_id=1, source_target_pairs={{8,16},{9,17},{10,18},{11,19},{12,20},{13,21},{14,22},{15,23},{16,... | collective-permute-start | bytes 417800 | tf_op jit(solution)/shard_map/ppermute | solution.py:503
  88.5 7.1 %collective-permute-start.23 = (f32[136,256]{1,0:T(8,128)S(1)}, f32[136,256]{1,0:T(8,128)S(1)}, u32[]{:S(2)}, u32[]{:S(2)}) collective-permute-start(f32[136,256]{1,0:T(8,128)S(1)} %slice_add_fusion.1.here_ref), channel_id=1, source_target_pairs={{0,8},{1,9},{2,10},{3,11},{4,12},{5,13},{6,14},{7,15},{8,0},{9,1},... | collective-permute-start | bytes 417800 | tf_op jit(solution)/shard_map/ppermute | solution.py:503
  92.2 4.7 %collective-permute-start.25 = (f32[8,256]{1,0:T(8,128)S(1)}, f32[8,256]{1,0:T(8,128)S(1)}, u32[]{:S(2)}, u32[]{:S(2)}) collective-permute-start(f32[8,256]{1,0:T(8,128)S(1)} %slice.38), channel_id=1, source_target_pairs={{0,24},{1,25},{2,26},{3,27},{4,28},{5,29},{6,30},{7,31},{8,16},{9,... | collective-permute-start | bytes 24584 | tf_op jit(solution)/shard_map/ppermute | solution.py:503
  98.8 4.9 %collective-permute-start.29 = (f32[136,256]{1,0:T(8,128)S(1)}, f32[136,256]{1,0:T(8,128)S(1)}, u32[]{:S(2)}, u32[]{:S(2)}) collective-permute-start(f32[136,256]{1,0:T(8,128)S(1)} %get-tuple-element.64.a_ref.pulled_ref), channel_id=1, source_target_pairs={{0,6},{1,7},{2,4},{3,5},{4,2},{5,3},{6,0},{7,1},{8,14},{9,15},{10,... | collective-permute-start | bytes 417800 | tf_op jit(solution)/shard_map/ppermute | solution.py:503
  99.9 5.7 %collective-permute-start.28 = (f32[136,256]{1,0:T(8,128)S(1)}, f32[136,256]{1,0:T(8,128)S(1)}, u32[]{:S(2)}, u32[]{:S(2)}) collective-permute-start(f32[136,256]{1,0:T(8,128)S(1)} %get-tuple-element.64.a_ref.pulled_ref), channel_id=1, source_target_pairs={{0,2},{1,3},{2,0},{3,1},{4,6},{5,7},{6,4},{7,5},{8,10},{9,11},{10,... | collective-permute-start | bytes 417800 | tf_op jit(solution)/shard_map/ppermute | solution.py:503
  100.2 5.5 %collective-permute-start.27 = (f32[136,256]{1,0:T(8,128)S(1)}, f32[136,256]{1,0:T(8,128)S(1)}, u32[]{:S(2)}, u32[]{:S(2)}) collective-permute-start(f32[136,256]{1,0:T(8,128)S(1)} %get-tuple-element.64.a_ref.pulled_ref), channel_id=1, source_target_pairs={{0,4},{1,5},{2,6},{3,7},{4,0},{5,1},{6,2},{7,3},{8,12},{9,13},{10,... | collective-permute-start | bytes 417800 | tf_op jit(solution)/shard_map/ppermute | solution.py:503
  106.3 4.6 %collective-permute-start.30 = (f32[392,256]{1,0:T(8,128)S(1)}, f32[392,256]{1,0:T(8,128)S(1)}, u32[]{:S(2)}, u32[]{:S(2)}) collective-permute-start(f32[392,256]{1,0:T(8,128)S(1)} %get-tuple-element.68), channel_id=1, source_target_pairs={{0,1},{1,0},{2,3},{3,2},{4,5},{5,4},{6,7},{7,6},{8,9},{9,8},{10,11... | collective-permute-start | bytes 1204232 | tf_op jit(solution)/shard_map/ppermute | solution.py:503
  110.8 5.7 %collective-permute-start.31 = (f32[136,256]{1,0:T(8,128)S(1)}, f32[136,256]{1,0:T(8,128)S(1)}, u32[]{:S(2)}, u32[]{:S(2)}) collective-permute-start(f32[136,256]{1,0:T(8,128)S(1)} %slice_add_fusion.here_ref), channel_id=1, source_target_pairs={{0,8},{1,9},{2,10},{3,11},{4,12},{5,13},{6,14},{7,15},{8,16},{9,17... | collective-permute-start | bytes 417800 | tf_op jit(solution)/shard_map/ppermute | solution.py:503
  115.9 7.5 %collective-permute-start.32 = (f32[256,256]{1,0:T(8,128)}, f32[256,256]{1,0:T(8,128)S(1)}, u32[]{:S(2)}, u32[]{:S(2)}) collective-permute-start(f32[256,256]{1,0:T(8,128)} %get-tuple-element.74), channel_id=1, source_target_pairs={{0,1},{1,0},{2,3},{3,2},{4,5},{5,4},{6,7},{7,6},{8,9},{9,8},{10,11... | collective-permute-start | bytes 786440 | tf_op jit(solution)/shard_map/ppermute | solution.py:503
  117.9 13.7 %all-to-all-start = ((f32[32,8,128]{2,1,0:T(8,128)}), f32[32,8,128]{2,1,0:T(8,128)S(1)}, u32[]{:S(2)}, u32[]{:S(2)}) async-start(f32[32,8,128]{2,1,0:T(8,128)} %plane_close.1), calls=%async_computation | async-start | bytes 262144 | tf_op jit(solution)/shard_map/all_to_all | solution.py:1145
  132.9 13.3 %collective-permute-start.33 = (f32[512,128]{1,0:T(8,128)S(1)}, f32[512,128]{1,0:T(8,128)S(1)}, u32[]{:S(2)}, u32[]{:S(2)}) collective-permute-start(f32[512,128]{1,0:T(8,128)S(1)} %plane_combine.1), channel_id=1, source_target_pairs={{0,0},{1,16},{2,8},{3,24},{4,4},{5,20},{6,12},{7,28},{8,1},{9,17},... | collective-permute-start | bytes 786440 | tf_op jit(solution)/shard_map/ppermute | solution.py:503
  (21 other events, 179.6 us)

commit v12 on v11

--- a/solution.py
+++ b/solution.py
@@ -607,9 +607,8 @@
     return product(first, turn(waves, spec, -1.0), order)
 
 
-def describe_kernel(inc_ref, seen_ref, later_ref, kind_ref, kernels_ref, wide_ref, forward, first, out_ref):
+def describe_kernel(inc_ref, gauge_ref, out_ref):
     blocks, slots, width = inc_ref.shape
-    rows = seen_ref.shape[0]
     tile = 8
     side = tile * slots
     weights = inc_ref[...].astype(F32).astype(BF16)
@@ -621,25 +620,36 @@
         full = lax.dot_general(flat, flat, (((1,), (1,)), ((), ())), preferred_element_type=F32)
         own = jnp.where(same, full, 0.0)
         out_ref[pl.ds(0, slots), pl.ds(i * side, side)] = jnp.sum(own.reshape(tile, slots, side), axis=0)
-    spec = spectra(kind_ref[...].astype(F32), kernels_ref[...], wide_ref[...])
-    here, after = jnp.transpose(seen_ref[...]), jnp.transpose(later_ref[...])
-    pulled = plane_advanced(here, after, spec, forward[...], first[...], 3)
-    step = out_ref.shape[0] - slots
-    for i in range(HOURS // step):
-        out_ref[pl.ds(slots, step), pl.ds(i * rows, rows)] = pulled[i * step : (i + 1) * step]
-
-
-def describe(incidence, seen, later, gauge_kernel, kernels, wide, mats):
+    out_ref[pl.ds(slots, 8), :] = jnp.broadcast_to(gauge_ref[...].astype(F32), (8, blocks * slots))
+
+
+def describe(incidence, row_gauge):
     blocks, slots, _ = incidence.shape
-    rows, hours = seen.shape
     count = blocks * slots
     return pl.pallas_call(
         describe_kernel,
-        out_shape=jax.ShapeDtypeStruct((slots + hours * rows // count, count), F32),
+        out_shape=jax.ShapeDtypeStruct((slots + 8, count), F32),
         compiler_params=params(),
         name="describe",
         cost_estimate=SMALL,
-    )(incidence, seen, later, gauge_kernel.reshape(1, rows), kernels, wide, *mats)
+    )(incidence, row_gauge.reshape(1, count))
+
+
+def observe_kernel(seen_ref, later_ref, kind_ref, kernels_ref, wide_ref, forward, first, out_ref):
+    spec = spectra(kind_ref[...].astype(F32), kernels_ref[...], wide_ref[...])
+    here, after = jnp.transpose(seen_ref[...]), jnp.transpose(later_ref[...])
+    out_ref[...] = plane_advanced(here, after, spec, forward[...], first[...], 3)
+
+
+def observe(seen, later, gauge_kernel, kernels, wide, mats):
+    rows, hours = seen.shape
+    return pl.pallas_call(
+        observe_kernel,
+        out_shape=jax.ShapeDtypeStruct((hours, rows), F32),
+        compiler_params=params(),
+        name="observe",
+        cost_estimate=SMALL,
+    )(seen, later, gauge_kernel.reshape(1, rows), kernels, wide, *mats)
 
 
 def send_kernel(inc_ref, field_ref, gauge_ref, kind_ref, out_ref):
@@ -713,19 +723,17 @@
 
 def plane_couple_kernel(last, first_ref, *refs):
     if last:
-        a_ref, b_ref, before_ref, high_ref, low_ref, total_ref, meta_ref = refs
+        all_ref, before_ref, high_ref, low_ref, total_ref, meta_ref = refs
         total_ref[...] = before_ref[...]
     else:
-        a_ref, b_ref, total_ref, meta_ref = refs
+        all_ref, total_ref, meta_ref = refs
         total_ref[...] = jnp.zeros_like(total_ref)
-    height, double = a_ref.shape
+    parts, height, count = meta_ref.shape
     slots = height - 8
-    count = double // 2
     cols, rows = total_ref.shape
     tile = 256
-    for i, ref in enumerate((a_ref, b_ref)):
-        for j in range(2):
-            meta_ref[2 * i + j] = ref[:, j * count : (j + 1) * count]
+    for i in range(parts):
+        meta_ref[i] = all_ref[:, i * count : (i + 1) * count]
     row = lax.broadcasted_iota(jnp.int32, (tile, tile), 0)
     col = lax.broadcasted_iota(jnp.int32, (tile, tile), 1)
     same = row // slots == col // slots
@@ -755,19 +763,20 @@
 
         return carry
 
-    lax.fori_loop(0, 4, body, 0)
+    lax.fori_loop(0, parts, body, 0)
     if last:
         high, low = pieces(total_ref[...], 2)
         high_ref[...] = high
         low_ref[...] = low
 
 
-def plane_couple(first, metas, rows, before=None):
-    height, double = metas[0].shape
+def plane_couple(first, meta, rows, before=None):
+    height, wide = meta.shape
+    parts = 2 * X_
     shape = (4 * rows, 2 * rows)
     last = before is not None
-    args = [first, *metas] + ([before] if last else [])
-    scratch = [pltpu.VMEM((4, height, double // 2), F32)]
+    args = [first, meta] + ([before] if last else [])
+    scratch = [pltpu.VMEM((parts, height, wide // parts), F32)]
     return pl.pallas_call(
         functools.partial(plane_couple_kernel, last),
         in_specs=[pl.BlockSpec(memory_space=pltpu.SMEM)]
@@ -777,7 +786,7 @@
         compiler_params=params(),
         name="plane_couple",
         cost_estimate=pl.CostEstimate(
-            flops=2 * 2 * double * 8 * rows * rows, bytes_accessed=2_000_000, transcendentals=0
+            flops=2 * 8 * wide * rows * rows, bytes_accessed=2_000_000, transcendentals=0
         ),
     )(*args)
 
@@ -1071,28 +1080,27 @@
     block, noted = (hours, rows), (hours + NOTE, rows)
 
     parcel = send(incidence, first_guess, row_gauge, gauge_kernel)
-    parcel, near, kinds, seen = lax.optimization_barrier((parcel, incidence, gauge_kernel, observed))
+    parcel, near, gauges, kinds, seen = lax.optimization_barrier(
+        (parcel, incidence, row_gauge, gauge_kernel, observed)
+    )
     parcel = moved(parcel, to_plane)
-    behind = describe(
-        near, seen, moved(seen, hour_before), kinds, kernels, short3, [forward3, inverse_first3]
-    )
-    behind = moved(behind, to_plane)
+    meta = describe(near, gauges)
+    meta = jnp.concatenate([meta, moved(meta, over_x)], axis=1)
+    meta = jnp.concatenate([meta, moved(meta, z_pair)], axis=1)
+    seen = observe(seen, moved(seen, hour_before), kinds, kernels, short3, [forward3, inverse_first3])
+    parcel, behind = lax.optimization_barrier((parcel, seen))
+    seen = moved(seen, to_plane)
     parcels = [parcel, moved(parcel, over_core)]
-    parcels[1], behind = lax.optimization_barrier((parcels[1], behind))
+    spec = plane_spectrum(parcel[hours:], kernels, short3, rows)
+    parcels[1], seen, meta, spec = lax.optimization_barrier((parcels[1], seen, meta, spec))
+    around = [meta, moved(meta, z_two)]
     dense = spread(first, parcels, rows)
-    slots = incidence.shape[1]
-    gram, seen = behind[:slots], behind[slots:]
-    seen = jnp.concatenate([seen[:, i : i + rows] for i in range(0, seen.shape[1], rows)], axis=0)
     metas = [value[hours:] for value in parcels]
-    spec = plane_spectrum(metas[0], kernels, short3, rows)
     sums = dense[0] + sum(moved(value, where) for value, where in zip(dense[1:], SQUARE))
     sums = [sums, moved(sums, z_pair), moved(sums, z_middle)]
-    both = jnp.concatenate([gram, moved(gram, over_core)], axis=1)
-    both = jnp.concatenate([both, jnp.concatenate(metas, axis=1)], axis=0)
-    around = [both] + [moved(both, where) for where in SQUARE]
-    coupled = plane_couple(first, around[:2], rows)
+    coupled = plane_couple(first, around[0], rows)
     coupled, sums = lax.optimization_barrier((coupled, sums))
-    coupling = plane_couple(first, around[2:], rows, coupled)
+    coupling = plane_couple(first, around[1], rows, coupled)
     (pulled0,) = plane_call(
         plane_first_kernel,
         "plane_first",

time: 149 us -> 147 us (0.987)
  starting transfers between devices: 56.9 us -> 52.3 us
  waiting for transfers between devices: 53.7 us -> 56.1 us
    ppermute x34 -> x33, starting transfers between devices: 51.4 us -> 46.8 us  [moved(): return lax.ppermute(value, ('basin', 'tm'), pairs)]
    ppermute x34 -> x33, waiting for transfers between devices: 45.5 us -> 47.9 us  [moved(): return lax.ppermute(value, ('basin', 'tm'), pairs)]
    unnamed x36 -> x30, local copies, waits for them, and re-layouts: 5.26 us -> 3.95 us
  transfers between devices with their start and end apart: 35 -> 34, of which waited for: 16 -> 18; matrix products, arithmetic and copies ran while one was open for 0% -> 0% of each run, Pallas kernels for 15% -> 15%
where the time goes in v12:
time: 147 us; the launch traced here: 146 us
  waiting for transfers between devices  56.1 us (38%)
  starting transfers between devices  52.3 us (36%)
  Pallas kernels  33.1 us (23%)
  local copies, waits for them, and re-layouts  4.04 us (3%)
    ppermute x33, waiting for transfers between devices, moved(): return lax.ppermute(value, ('basin', 'tm'), pairs)  47.9 us
    ppermute x33, starting transfers between devices, moved(): return lax.ppermute(value, ('basin', 'tm'), pairs)  46.8 us
    pallas_call x6, Pallas kernels, plane_call(): pl.pallas_call(kernel, in_specs=[pl.BlockSpec(memory_space=pltpu.SMEM)] *...  9.79 us
    pallas_call x2, Pallas kernels, plane_couple(): pl.pallas_call(functools.partial(plane_couple_kernel, last), in_specs=[pl...  9.56 us
    all_to_all x1, waiting for transfers between devices, plane_shards(): close_note = lax.all_to_all(note, ('basin', 'tm'), 0, 0, tiled=False)  8.18 us
    all_to_all x1, starting transfers between devices, plane_shards(): close_note = lax.all_to_all(note, ('basin', 'tm'), 0, 0, tiled=False)  5.49 us
    pallas_call x3, Pallas kernels, plane_rows(): pl.pallas_call(plane_rows_kernel, in_specs=[pl.BlockSpec(memory_space=plt...  4.49 us
    unnamed x30, local copies, waits for them, and re-layouts  3.95 us
  transfers between devices with their start and end apart: 34, of which 18 were waited for; matrix products, arithmetic and copies ran while one was open for 0% of the time, Pallas kernels for 15%

profile of v12, /device:TPU:1, one launch (start us, length us, event | category | flops | bytes accessed | tf_op | source)
XLA Modules:
  0.0 146.1 jit_solution(6610642456718340311)
XLA Ops:
  0.0 1.6 %copy-done = f32[4096,128]{1,0:T(8,128)S(1)} copy-done((f32[4096,128]{1,0:T(8,128)S(1)}, f32[4096,128]{1,0:T(8,128)}, u32[]{:S(2)}) %copy-start) | copy-done | bytes 2097176
  5.4 4.6 %collective-permute-start = (f32[136,512]{1,0:T(8,128)S(1)}, f32[136,512]{1,0:T(8,128)S(1)}, u32[]{:S(2)}, u32[]{:S(2)}) collective-permute-start(f32[136,512]{1,0:T(8,128)S(1)} %send.1), channel_id=1, source_target_pairs={{0,0},{1,8},{2,16},{3,24},{4,4},{5,12},{6,20},{7,28},{8,2},{9,10},... | collective-permute-start | bytes 835592 | tf_op jit(solution)/shard_map/ppermute | solution.py:503
  11.5 1.9 %collective-permute-start.1 = (f32[256,128]{1,0:T(8,128)S(1)}, f32[256,128]{1,0:T(8,128)S(1)}, u32[]{:S(2)}, u32[]{:S(2)}) collective-permute-start(f32[256,128]{1,0:T(8,128)S(1)} %copy-done.12), channel_id=1, source_target_pairs={{1,0},{2,1},{3,2},{5,4},{6,5},{7,6},{9,8},{10,9},{11,10},{13,12},{... | collective-permute-start | bytes 393224 | tf_op jit(solution)/shard_map/ppermute | solution.py:503
  13.5 1.9 %collective-permute-start.5 = (f32[24,1024]{1,0:T(8,128)S(1)}, f32[24,1024]{1,0:T(8,128)S(1)}, u32[]{:S(2)}, u32[]{:S(2)}) collective-permute-start(f32[24,1024]{1,0:T(8,128)S(1)} %pad_maximum_fusion.1), channel_id=1, source_target_pairs={{0,8},{1,9},{2,10},{3,11},{4,12},{5,13},{6,14},{7,15},{8,0},{9,1},... | collective-permute-start | bytes 294920 | tf_op jit(solution)/shard_map/ppermute | solution.py:503
  15.4 3.4 %collective-permute-done.1.later_ref = f32[256,128]{1,0:T(8,128)S(1)} collective-permute-done((f32[256,128]{1,0:T(8,128)S(1)}, f32[256,128]{1,0:T(8,128)S(1)}, u32[]{:S(2)}, u32[]{:S(2)}) %collective-permute-start.1) | collective-permute-done | bytes 131104 | tf_op jit(solution)/shard_map/ppermute | solution.py:503
  20.1 3.4 %collective-permute-done.mine_ref = f32[136,512]{1,0:T(8,128)S(1)} collective-permute-done((f32[136,512]{1,0:T(8,128)S(1)}, f32[136,512]{1,0:T(8,128)S(1)}, u32[]{:S(2)}, u32[]{:S(2)}) %collective-permute-start) | collective-permute-done | bytes 278560 | tf_op jit(solution)/shard_map/ppermute | solution.py:503
  23.4 1.9 %collective-permute-start.3 = (f32[128,256]{1,0:T(8,128)S(1)}, f32[128,256]{1,0:T(8,128)S(1)}, u32[]{:S(2)}, u32[]{:S(2)}) collective-permute-start(f32[128,256]{1,0:T(8,128)S(1)} %observe.1), channel_id=1, source_target_pairs={{0,0},{1,8},{2,16},{3,24},{4,4},{5,12},{6,20},{7,28},{8,2},{9,10},... | collective-permute-start | bytes 393224 | tf_op jit(solution)/shard_map/ppermute | solution.py:503
  26.1 6.7 %collective-permute-done.3.seen_ref = f32[128,256]{1,0:T(8,128)S(1)} collective-permute-done((f32[128,256]{1,0:T(8,128)S(1)}, f32[128,256]{1,0:T(8,128)S(1)}, u32[]{:S(2)}, u32[]{:S(2)}) %collective-permute-start.3) | collective-permute-done | bytes 131104 | tf_op jit(solution)/shard_map/ppermute | solution.py:503
  32.7 1.6 %spread.1 = (f32[128,256]{1,0:T(8,128)S(1)}, f32[128,256]{1,0:T(8,128)S(1)}, f32[128,256]{1,0:T(8,128)S(1)}, f32[128,256]{1,0:T(8,128)S(1)}) custom-call(s32[6]{0:T(128)S(1)} %broadcast_multiply_fusion.first_ref, f32[136,512]{1,0:T(8,128)S(1)} %collective-permute-done.mine_ref, f32[136,512]{1,0:T(8,128)S(1)} %collective-permute-done.2.other_ref), custom_call_target="tpu_custom_call" | custom-call | flops 1 | bytes 1 | tf_op jit(solution)/shard_map/spread/pallas_call | solution.py:714
  34.3 1.7 %collective-permute-start.7 = (f32[128,256]{1,0:T(8,128)S(1)}, f32[128,256]{1,0:T(8,128)S(1)}, u32[]{:S(2)}, u32[]{:S(2)}) collective-permute-start(f32[128,256]{1,0:T(8,128)S(1)} %get-tuple-element.53), channel_id=1, source_target_pairs={{0,4},{1,5},{2,6},{3,7},{4,0},{5,1},{6,2},{7,3},{8,12},{9,13},{10,... | collective-permute-start | bytes 393224 | tf_op jit(solution)/shard_map/ppermute | solution.py:503
  37.4 2.0 %collective-permute-done.7 = f32[128,256]{1,0:T(8,128)S(1)} collective-permute-done((f32[128,256]{1,0:T(8,128)S(1)}, f32[128,256]{1,0:T(8,128)S(1)}, u32[]{:S(2)}, u32[]{:S(2)}) %collective-permute-start.7) | collective-permute-done | bytes 131104 | tf_op jit(solution)/shard_map/ppermute | solution.py:503
  39.4 2.9 %collective-permute-done.8 = f32[128,256]{1,0:T(8,128)S(1)} collective-permute-done((f32[128,256]{1,0:T(8,128)S(1)}, f32[128,256]{1,0:T(8,128)S(1)}, u32[]{:S(2)}, u32[]{:S(2)}) %collective-permute-start.8) | collective-permute-done | bytes 131104 | tf_op jit(solution)/shard_map/ppermute | solution.py:503
  43.1 2.0 %collective-permute-start.10 = (f32[128,256]{1,0:T(8,128)S(1)}, f32[128,256]{1,0:T(8,128)S(1)}, u32[]{:S(2)}, u32[]{:S(2)}) collective-permute-start(f32[128,256]{1,0:T(8,128)S(1)} %add_add_fusion.here_ref), channel_id=1, source_target_pairs={{0,8},{1,9},{2,10},{3,11},{4,12},{5,13},{6,14},{7,15},{8,0},{9,1},... | collective-permute-start | bytes 393224 | tf_op jit(solution)/shard_map/ppermute | solution.py:503
  45.1 4.6 %plane_couple.2.refs_1_ = f32[1024,512]{1,0:T(8,128)S(1)} custom-call(s32[6]{0:T(128)S(1)} %broadcast_multiply_fusion.first_ref, f32[24,2048]{1,0:T(8,128)S(1)} %pad_maximum_fusion.refs_0_), custom_call_target="tpu_custom_call" | custom-call | flops 2147483648 | bytes 2000000 | tf_op jit(solution)/shard_map/plane_couple/pallas_call | solution.py:780
  50.7 2.6 %plane_first.1.a_ref.pulled_ref.old_z_ref = f32[128,256]{1,0:T(8,128)S(1)} custom-call(f32[3]{0:T(128)S(1)} %add_convert_fusion.flag_ref, f32[128,256]{1,0:T(8,128)S(1)} %add_add_fusion.here_ref, f32[128,256]{1,0:T(8,128)S(1)} %collective-permute-done.10.pair_ref, f32[128,256]{1,0:T(8,128)S(1)} %collective-permute-done.11.middle_ref, ...), custom_call_target="tpu_custom_call" | custom-call | flops 1 | bytes 1 | tf_op jit(solution)/shard_map/plane_first/pallas_call | solution.py:907
  53.3 1.9 %collective-permute-start.14 = (f32[128,256]{1,0:T(8,128)S(1)}, f32[128,256]{1,0:T(8,128)S(1)}, u32[]{:S(2)}, u32[]{:S(2)}) collective-permute-start(f32[128,256]{1,0:T(8,128)S(1)} %plane_first.1.a_ref.pulled_ref.old_z_ref), channel_id=1, source_target_pairs={{0,6},{1,7},{2,4},{3,5},{4,2},{5,3},{6,0},{7,1},{8,14},{9,15},{10,... | collective-permute-start | bytes 393224 | tf_op jit(solution)/shard_map/ppermute | solution.py:503
  56.6 4.9 %plane_couple.3 = (bf16[1024,512]{1,0:T(8,128)(2,1)S(1)}, bf16[1024,512]{1,0:T(8,128)(2,1)S(1)}) custom-call(s32[6]{0:T(128)S(1)} %broadcast_multiply_fusion.first_ref, f32[24,2048]{1,0:T(8,128)S(1)} %collective-permute-done.6.refs_0_, f32[1024,512]{1,0:T(8,128)S(1)} %plane_couple.2.refs_1_), custom_call_target="tpu_custom_call" | custom-call | flops 2147483648 | bytes 2000000 | tf_op jit(solution)/shard_map/plane_couple/pallas_call | solution.py:780
  62.7 2.4 %collective-permute-start.15 = (f32[128,256]{1,0:T(8,128)S(1)}, f32[128,256]{1,0:T(8,128)S(1)}, u32[]{:S(2)}, u32[]{:S(2)}) collective-permute-start(f32[128,256]{1,0:T(8,128)S(1)} %get-tuple-element.65), channel_id=1, source_target_pairs={{0,1},{1,0},{2,3},{3,2},{4,5},{5,4},{6,7},{7,6},{8,9},{9,8},{10,11... | collective-permute-start | bytes 393224 | tf_op jit(solution)/shard_map/ppermute | solution.py:503
  68.2 3.5 %collective-permute-done.16.pair_ref = f32[128,256]{1,0:T(8,128)S(1)} collective-permute-done((f32[128,256]{1,0:T(8,128)S(1)}, f32[128,256]{1,0:T(8,128)S(1)}, u32[]{:S(2)}, u32[]{:S(2)}) %collective-permute-start.16) | collective-permute-done | bytes 131104 | tf_op jit(solution)/shard_map/ppermute | solution.py:503
  71.6 1.8 %plane_open.1 = (f32[136,256]{1,0:T(8,128)S(1)}, f32[256,256]{1,0:T(8,128)S(1)}) custom-call(f32[3]{0:T(128)S(1)} %add_convert_fusion.flag_ref, f32[128,256]{1,0:T(8,128)S(1)} %add.61.here_ref.old_s_ref, f32[128,256]{1,0:T(8,128)S(1)} %collective-permute-done.16.pair_ref, f32[128,256]{1,0:T(8,128)S(1)} %collective-permute-done.17.middle_ref, ...), custom_call_target="tpu_custom_call" | custom-call | flops 1 | bytes 1 | tf_op jit(solution)/shard_map/plane_open/pallas_call | solution.py:907
  78.4 4.2 %collective-permute-done.19.c_ref = f32[136,256]{1,0:T(8,128)S(1)} collective-permute-done((f32[136,256]{1,0:T(8,128)S(1)}, f32[136,256]{1,0:T(8,128)S(1)}, u32[]{:S(2)}, u32[]{:S(2)}) %collective-permute-start.19) | collective-permute-done | bytes 139296 | tf_op jit(solution)/shard_map/ppermute | solution.py:503
  86.4 3.7 %collective-permute-start.22 = (f32[136,256]{1,0:T(8,128)S(1)}, f32[136,256]{1,0:T(8,128)S(1)}, u32[]{:S(2)}, u32[]{:S(2)}) collective-permute-start(f32[136,256]{1,0:T(8,128)S(1)} %slice_add_fusion.1.here_ref), channel_id=1, source_target_pairs={{0,8},{1,9},{2,10},{3,11},{4,12},{5,13},{6,14},{7,15},{8,0},{9,1},... | collective-permute-start | bytes 417800 | tf_op jit(solution)/shard_map/ppermute | solution.py:503
  91.4 2.2 %collective-permute-done.22.pair_ref = f32[136,256]{1,0:T(8,128)S(1)} collective-permute-done((f32[136,256]{1,0:T(8,128)S(1)}, f32[136,256]{1,0:T(8,128)S(1)}, u32[]{:S(2)}, u32[]{:S(2)}) %collective-permute-start.22) | collective-permute-done | bytes 139296 | tf_op jit(solution)/shard_map/ppermute | solution.py:503
  101.1 2.0 %collective-permute-done.27.c_ref = f32[136,256]{1,0:T(8,128)S(1)} collective-permute-done((f32[136,256]{1,0:T(8,128)S(1)}, f32[136,256]{1,0:T(8,128)S(1)}, u32[]{:S(2)}, u32[]{:S(2)}) %collective-permute-start.27) | collective-permute-done | bytes 139296 | tf_op jit(solution)/shard_map/ppermute | solution.py:503
  103.6 3.2 %collective-permute-start.29 = (f32[392,256]{1,0:T(8,128)S(1)}, f32[392,256]{1,0:T(8,128)S(1)}, u32[]{:S(2)}, u32[]{:S(2)}) collective-permute-start(f32[392,256]{1,0:T(8,128)S(1)} %get-tuple-element.76), channel_id=1, source_target_pairs={{0,1},{1,0},{2,3},{3,2},{4,5},{5,4},{6,7},{7,6},{8,9},{9,8},{10,11... | collective-permute-start | bytes 1204232 | tf_op jit(solution)/shard_map/ppermute | solution.py:503
  108.2 3.0 %collective-permute-start.30 = (f32[136,256]{1,0:T(8,128)S(1)}, f32[136,256]{1,0:T(8,128)S(1)}, u32[]{:S(2)}, u32[]{:S(2)}) collective-permute-start(f32[136,256]{1,0:T(8,128)S(1)} %slice_add_fusion.here_ref), channel_id=1, source_target_pairs={{0,8},{1,9},{2,10},{3,11},{4,12},{5,13},{6,14},{7,15},{8,16},{9,17... | collective-permute-start | bytes 417800 | tf_op jit(solution)/shard_map/ppermute | solution.py:503
  111.2 2.0 %plane_rows.5 = (f32[128,512]{1,0:T(8,128)S(1)}, f32[256,256]{1,0:T(8,128)}, f32[256,512]{1,0:T(8,128)S(1)}) custom-call(s32[6]{0:T(128)S(1)} %broadcast_multiply_fusion.first_ref, f32[8,512]{1,0:T(8,128)S(1)} %slice.17.class_ref.meta_ref, f32[8,512]{1,0:T(8,128)S(1)} %slice.18.meta_other_ref, f32[136,256]{1,0:T(8,128)S(1)} %get-tuple-element.72.a_ref.pulled_ref, ...), custom_call_target="tpu_custom_call" | custom-call | flops 1000000000 | bytes 2000000 | tf_op jit(solution)/shard_map/plane_rows/pallas_call | solution.py:863
  115.2 5.5 %all-to-all-start = ((f32[32,8,128]{2,1,0:T(8,128)}), f32[32,8,128]{2,1,0:T(8,128)S(1)}, u32[]{:S(2)}, u32[]{:S(2)}) async-start(f32[32,8,128]{2,1,0:T(8,128)} %plane_close.1), calls=%async_computation | async-start | bytes 262144 | tf_op jit(solution)/shard_map/all_to_all | solution.py:1153
  120.7 8.2 %all-to-all-done.close_ref = f32[32,8,128]{2,1,0:T(8,128)S(1)} async-done(((f32[32,8,128]{2,1,0:T(8,128)}), f32[32,8,128]{2,1,0:T(8,128)S(1)}, u32[]{:S(2)}, u32[]{:S(2)}) %all-to-all-start) | async-done | bytes 131104 | tf_op jit(solution)/shard_map/all_to_all | solution.py:1153
  130.4 2.6 %collective-permute-start.32 = (f32[512,128]{1,0:T(8,128)S(1)}, f32[512,128]{1,0:T(8,128)S(1)}, u32[]{:S(2)}, u32[]{:S(2)}) collective-permute-start(f32[512,128]{1,0:T(8,128)S(1)} %plane_combine.1), channel_id=1, source_target_pairs={{0,0},{1,16},{2,8},{3,24},{4,4},{5,20},{6,12},{7,28},{8,1},{9,17},... | collective-permute-start | bytes 786440 | tf_op jit(solution)/shard_map/ppermute | solution.py:503
  133.0 10.7 %collective-permute-done.32.rows_ref = f32[512,128]{1,0:T(8,128)S(1)} collective-permute-done((f32[512,128]{1,0:T(8,128)S(1)}, f32[512,128]{1,0:T(8,128)S(1)}, u32[]{:S(2)}, u32[]{:S(2)}) %collective-permute-start.32) | collective-permute-done | bytes 262176 | tf_op jit(solution)/shard_map/ppermute | solution.py:503
  143.7 2.4 %plane_finish.1 = f32[4096,128]{1,0:T(8,128)} custom-call(f32[512,128]{1,0:T(8,128)S(1)} %collective-permute-done.32.rows_ref, s32[32,16,128]{2,1,0:T(8,128)S(1)} %copy-done.5, f32[4096,128]{1,0:T(8,128)S(1)} %copy-done.1), custom_call_target="tpu_custom_call" | custom-call | tf_op jit(solution)/shard_map/plane_finish/pallas_call | solution.py:1055
  (98 shorter events, 39.0 us)
Async XLA Ops:
  5.4 18.1 %collective-permute-start = (f32[136,512]{1,0:T(8,128)S(1)}, f32[136,512]{1,0:T(8,128)S(1)}, u32[]{:S(2)}, u32[]{:S(2)}) collective-permute-start(f32[136,512]{1,0:T(8,128)S(1)} %send.1), channel_id=1, source_target_pairs={{0,0},{1,8},{2,16},{3,24},{4,4},{5,12},{6,20},{7,28},{8,2},{9,10},... | collective-permute-start | bytes 835592 | tf_op jit(solution)/shard_map/ppermute | solution.py:503
  10.2 3.3 %collective-permute-start.4 = (f32[24,512]{1,0:T(8,128)S(1)}, f32[24,512]{1,0:T(8,128)S(1)}, u32[]{:S(2)}, u32[]{:S(2)}) collective-permute-start(f32[24,512]{1,0:T(8,128)S(1)} %describe.1), channel_id=1, source_target_pairs={{0,4},{1,5},{2,6},{3,7},{4,0},{5,1},{6,2},{7,3},{8,12},{9,13},{10,... | collective-permute-start | bytes 147464 | tf_op jit(solution)/shard_map/ppermute | solution.py:503
  11.5 7.3 %collective-permute-start.1 = (f32[256,128]{1,0:T(8,128)S(1)}, f32[256,128]{1,0:T(8,128)S(1)}, u32[]{:S(2)}, u32[]{:S(2)}) collective-permute-start(f32[256,128]{1,0:T(8,128)S(1)} %copy-done.12), channel_id=1, source_target_pairs={{1,0},{2,1},{3,2},{5,4},{6,5},{7,6},{9,8},{10,9},{11,10},{13,12},{... | collective-permute-start | bytes 393224 | tf_op jit(solution)/shard_map/ppermute | solution.py:503
  13.5 11.9 %collective-permute-start.5 = (f32[24,1024]{1,0:T(8,128)S(1)}, f32[24,1024]{1,0:T(8,128)S(1)}, u32[]{:S(2)}, u32[]{:S(2)}) collective-permute-start(f32[24,1024]{1,0:T(8,128)S(1)} %pad_maximum_fusion.1), channel_id=1, source_target_pairs={{0,8},{1,9},{2,10},{3,11},{4,12},{5,13},{6,14},{7,15},{8,0},{9,1},... | collective-permute-start | bytes 294920 | tf_op jit(solution)/shard_map/ppermute | solution.py:503
  23.4 9.3 %collective-permute-start.2 = (f32[136,512]{1,0:T(8,128)S(1)}, f32[136,512]{1,0:T(8,128)S(1)}, u32[]{:S(2)}, u32[]{:S(2)}) collective-permute-start(f32[136,512]{1,0:T(8,128)S(1)} %collective-permute-done.mine_ref), channel_id=1, source_target_pairs={{0,1},{1,0},{2,3},{3,2},{4,5},{5,4},{6,7},{7,6},{8,9},{9,8},{10,11... | collective-permute-start | bytes 835592 | tf_op jit(solution)/shard_map/ppermute | solution.py:503
  23.4 9.3 %collective-permute-start.3 = (f32[128,256]{1,0:T(8,128)S(1)}, f32[128,256]{1,0:T(8,128)S(1)}, u32[]{:S(2)}, u32[]{:S(2)}) collective-permute-start(f32[128,256]{1,0:T(8,128)S(1)} %observe.1), channel_id=1, source_target_pairs={{0,0},{1,8},{2,16},{3,24},{4,4},{5,12},{6,20},{7,28},{8,2},{9,10},... | collective-permute-start | bytes 393224 | tf_op jit(solution)/shard_map/ppermute | solution.py:503
  34.3 5.1 %collective-permute-start.7 = (f32[128,256]{1,0:T(8,128)S(1)}, f32[128,256]{1,0:T(8,128)S(1)}, u32[]{:S(2)}, u32[]{:S(2)}) collective-permute-start(f32[128,256]{1,0:T(8,128)S(1)} %get-tuple-element.53), channel_id=1, source_target_pairs={{0,4},{1,5},{2,6},{3,7},{4,0},{5,1},{6,2},{7,3},{8,12},{9,13},{10,... | collective-permute-start | bytes 393224 | tf_op jit(solution)/shard_map/ppermute | solution.py:503
  36.0 6.3 %collective-permute-start.8 = (f32[128,256]{1,0:T(8,128)S(1)}, f32[128,256]{1,0:T(8,128)S(1)}, u32[]{:S(2)}, u32[]{:S(2)}) collective-permute-start(f32[128,256]{1,0:T(8,128)S(1)} %get-tuple-element.54), channel_id=1, source_target_pairs={{0,2},{1,3},{2,0},{3,1},{4,6},{5,7},{6,4},{7,5},{8,10},{9,11},{10,... | collective-permute-start | bytes 393224 | tf_op jit(solution)/shard_map/ppermute | solution.py:503
  36.0 6.3 %collective-permute-start.9 = (f32[128,256]{1,0:T(8,128)S(1)}, f32[128,256]{1,0:T(8,128)S(1)}, u32[]{:S(2)}, u32[]{:S(2)}) collective-permute-start(f32[128,256]{1,0:T(8,128)S(1)} %get-tuple-element.55), channel_id=1, source_target_pairs={{0,6},{1,7},{2,4},{3,5},{4,2},{5,3},{6,0},{7,1},{8,14},{9,15},{10,... | collective-permute-start | bytes 393224 | tf_op jit(solution)/shard_map/ppermute | solution.py:503
  37.3 19.3 %collective-permute-start.6 = (f32[24,2048]{1,0:T(8,128)S(1)}, f32[24,2048]{1,0:T(8,128)S(1)}, u32[]{:S(2)}, u32[]{:S(2)}) collective-permute-start(f32[24,2048]{1,0:T(8,128)S(1)} %pad_maximum_fusion.refs_0_), channel_id=1, source_target_pairs={{0,16},{1,17},{2,18},{3,19},{4,20},{5,21},{6,22},{7,23},{8,24},{9,... | collective-permute-start | bytes 589832 | tf_op jit(solution)/shard_map/ppermute | solution.py:503
  42.3 7.5 %collective-permute-start.11 = (f32[128,256]{1,0:T(8,128)S(1)}, f32[128,256]{1,0:T(8,128)S(1)}, u32[]{:S(2)}, u32[]{:S(2)}) collective-permute-start(f32[128,256]{1,0:T(8,128)S(1)} %add_add_fusion.here_ref), channel_id=1, source_target_pairs={{8,16},{9,17},{10,18},{11,19},{12,20},{13,21},{14,22},{15,23},{16,... | collective-permute-start | bytes 393224 | tf_op jit(solution)/shard_map/ppermute | solution.py:503
  43.1 7.6 %collective-permute-start.10 = (f32[128,256]{1,0:T(8,128)S(1)}, f32[128,256]{1,0:T(8,128)S(1)}, u32[]{:S(2)}, u32[]{:S(2)}) collective-permute-start(f32[128,256]{1,0:T(8,128)S(1)} %add_add_fusion.here_ref), channel_id=1, source_target_pairs={{0,8},{1,9},{2,10},{3,11},{4,12},{5,13},{6,14},{7,15},{8,0},{9,1},... | collective-permute-start | bytes 393224 | tf_op jit(solution)/shard_map/ppermute | solution.py:503
  53.3 8.3 %collective-permute-start.14 = (f32[128,256]{1,0:T(8,128)S(1)}, f32[128,256]{1,0:T(8,128)S(1)}, u32[]{:S(2)}, u32[]{:S(2)}) collective-permute-start(f32[128,256]{1,0:T(8,128)S(1)} %plane_first.1.a_ref.pulled_ref.old_z_ref), channel_id=1, source_target_pairs={{0,6},{1,7},{2,4},{3,5},{4,2},{5,3},{6,0},{7,1},{8,14},{9,15},{10,... | collective-permute-start | bytes 393224 | tf_op jit(solution)/shard_map/ppermute | solution.py:503
  55.2 6.4 %collective-permute-start.13 = (f32[128,256]{1,0:T(8,128)S(1)}, f32[128,256]{1,0:T(8,128)S(1)}, u32[]{:S(2)}, u32[]{:S(2)}) collective-permute-start(f32[128,256]{1,0:T(8,128)S(1)} %plane_first.1.a_ref.pulled_ref.old_z_ref), channel_id=1, source_target_pairs={{0,2},{1,3},{2,0},{3,1},{4,6},{5,7},{6,4},{7,5},{8,10},{9,11},{10,... | collective-permute-start | bytes 393224 | tf_op jit(solution)/shard_map/ppermute | solution.py:503
  56.6 5.5 %collective-permute-start.12 = (f32[128,256]{1,0:T(8,128)S(1)}, f32[128,256]{1,0:T(8,128)S(1)}, u32[]{:S(2)}, u32[]{:S(2)}) collective-permute-start(f32[128,256]{1,0:T(8,128)S(1)} %plane_first.1.a_ref.pulled_ref.old_z_ref), channel_id=1, source_target_pairs={{0,4},{1,5},{2,6},{3,7},{4,0},{5,1},{6,2},{7,3},{8,12},{9,13},{10,... | collective-permute-start | bytes 393224 | tf_op jit(solution)/shard_map/ppermute | solution.py:503
  62.7 3.4 %collective-permute-start.15 = (f32[128,256]{1,0:T(8,128)S(1)}, f32[128,256]{1,0:T(8,128)S(1)}, u32[]{:S(2)}, u32[]{:S(2)}) collective-permute-start(f32[128,256]{1,0:T(8,128)S(1)} %get-tuple-element.65), channel_id=1, source_target_pairs={{0,1},{1,0},{2,3},{3,2},{4,5},{5,4},{6,7},{7,6},{8,9},{9,8},{10,11... | collective-permute-start | bytes 393224 | tf_op jit(solution)/shard_map/ppermute | solution.py:503
  66.8 4.8 %collective-permute-start.16 = (f32[128,256]{1,0:T(8,128)S(1)}, f32[128,256]{1,0:T(8,128)S(1)}, u32[]{:S(2)}, u32[]{:S(2)}) collective-permute-start(f32[128,256]{1,0:T(8,128)S(1)} %add.61.here_ref.old_s_ref), channel_id=1, source_target_pairs={{0,8},{1,9},{2,10},{3,11},{4,12},{5,13},{6,14},{7,15},{8,0},{9,1},... | collective-permute-start | bytes 393224 | tf_op jit(solution)/shard_map/ppermute | solution.py:503
  73.5 5.0 %collective-permute-start.20 = (f32[136,256]{1,0:T(8,128)S(1)}, f32[136,256]{1,0:T(8,128)S(1)}, u32[]{:S(2)}, u32[]{:S(2)}) collective-permute-start(f32[136,256]{1,0:T(8,128)S(1)} %get-tuple-element.66.a_ref.pulled_ref), channel_id=1, source_target_pairs={{0,6},{1,7},{2,4},{3,5},{4,2},{5,3},{6,0},{7,1},{8,14},{9,15},{10,... | collective-permute-start | bytes 417800 | tf_op jit(solution)/shard_map/ppermute | solution.py:503
  74.6 8.1 %collective-permute-start.19 = (f32[136,256]{1,0:T(8,128)S(1)}, f32[136,256]{1,0:T(8,128)S(1)}, u32[]{:S(2)}, u32[]{:S(2)}) collective-permute-start(f32[136,256]{1,0:T(8,128)S(1)} %get-tuple-element.66.a_ref.pulled_ref), channel_id=1, source_target_pairs={{0,2},{1,3},{2,0},{3,1},{4,6},{5,7},{6,4},{7,5},{8,10},{9,11},{10,... | collective-permute-start | bytes 417800 | tf_op jit(solution)/shard_map/ppermute | solution.py:503
  75.5 7.1 %collective-permute-start.18 = (f32[136,256]{1,0:T(8,128)S(1)}, f32[136,256]{1,0:T(8,128)S(1)}, u32[]{:S(2)}, u32[]{:S(2)}) collective-permute-start(f32[136,256]{1,0:T(8,128)S(1)} %get-tuple-element.66.a_ref.pulled_ref), channel_id=1, source_target_pairs={{0,4},{1,5},{2,6},{3,7},{4,0},{5,1},{6,2},{7,3},{8,12},{9,13},{10,... | collective-permute-start | bytes 417800 | tf_op jit(solution)/shard_map/ppermute | solution.py:503
  85.5 5.8 %collective-permute-start.25 = (f32[136,256]{1,0:T(8,128)S(1)}, f32[136,256]{1,0:T(8,128)S(1)}, u32[]{:S(2)}, u32[]{:S(2)}) collective-permute-start(f32[136,256]{1,0:T(8,128)S(1)} %slice_add_fusion.1.here_ref), channel_id=1, source_target_pairs={{8,16},{9,17},{10,18},{11,19},{12,20},{13,21},{14,22},{15,23},{16,... | collective-permute-start | bytes 417800 | tf_op jit(solution)/shard_map/ppermute | solution.py:503
  86.4 7.1 %collective-permute-start.22 = (f32[136,256]{1,0:T(8,128)S(1)}, f32[136,256]{1,0:T(8,128)S(1)}, u32[]{:S(2)}, u32[]{:S(2)}) collective-permute-start(f32[136,256]{1,0:T(8,128)S(1)} %slice_add_fusion.1.here_ref), channel_id=1, source_target_pairs={{0,8},{1,9},{2,10},{3,11},{4,12},{5,13},{6,14},{7,15},{8,0},{9,1},... | collective-permute-start | bytes 417800 | tf_op jit(solution)/shard_map/ppermute | solution.py:503
  90.1 4.7 %collective-permute-start.24 = (f32[8,256]{1,0:T(8,128)S(1)}, f32[8,256]{1,0:T(8,128)S(1)}, u32[]{:S(2)}, u32[]{:S(2)}) collective-permute-start(f32[8,256]{1,0:T(8,128)S(1)} %slice.23), channel_id=1, source_target_pairs={{0,24},{1,25},{2,26},{3,27},{4,28},{5,29},{6,30},{7,31},{8,16},{9,... | collective-permute-start | bytes 24584 | tf_op jit(solution)/shard_map/ppermute | solution.py:503
  91.2 3.5 %collective-permute-start.23 = (f32[8,256]{1,0:T(8,128)S(1)}, f32[8,256]{1,0:T(8,128)S(1)}, u32[]{:S(2)}, u32[]{:S(2)}) collective-permute-start(f32[8,256]{1,0:T(8,128)S(1)} %slice.23), channel_id=1, source_target_pairs={{0,16},{1,17},{2,18},{3,19},{4,20},{5,21},{6,22},{7,23},{8,24},{9,... | collective-permute-start | bytes 24584 | tf_op jit(solution)/shard_map/ppermute | solution.py:503
  96.1 5.0 %collective-permute-start.28 = (f32[136,256]{1,0:T(8,128)S(1)}, f32[136,256]{1,0:T(8,128)S(1)}, u32[]{:S(2)}, u32[]{:S(2)}) collective-permute-start(f32[136,256]{1,0:T(8,128)S(1)} %get-tuple-element.72.a_ref.pulled_ref), channel_id=1, source_target_pairs={{0,6},{1,7},{2,4},{3,5},{4,2},{5,3},{6,0},{7,1},{8,14},{9,15},{10,... | collective-permute-start | bytes 417800 | tf_op jit(solution)/shard_map/ppermute | solution.py:503
  97.1 5.9 %collective-permute-start.27 = (f32[136,256]{1,0:T(8,128)S(1)}, f32[136,256]{1,0:T(8,128)S(1)}, u32[]{:S(2)}, u32[]{:S(2)}) collective-permute-start(f32[136,256]{1,0:T(8,128)S(1)} %get-tuple-element.72.a_ref.pulled_ref), channel_id=1, source_target_pairs={{0,2},{1,3},{2,0},{3,1},{4,6},{5,7},{6,4},{7,5},{8,10},{9,11},{10,... | collective-permute-start | bytes 417800 | tf_op jit(solution)/shard_map/ppermute | solution.py:503
  97.9 5.1 %collective-permute-start.26 = (f32[136,256]{1,0:T(8,128)S(1)}, f32[136,256]{1,0:T(8,128)S(1)}, u32[]{:S(2)}, u32[]{:S(2)}) collective-permute-start(f32[136,256]{1,0:T(8,128)S(1)} %get-tuple-element.72.a_ref.pulled_ref), channel_id=1, source_target_pairs={{0,4},{1,5},{2,6},{3,7},{4,0},{5,1},{6,2},{7,3},{8,12},{9,13},{10,... | collective-permute-start | bytes 417800 | tf_op jit(solution)/shard_map/ppermute | solution.py:503
  103.6 4.5 %collective-permute-start.29 = (f32[392,256]{1,0:T(8,128)S(1)}, f32[392,256]{1,0:T(8,128)S(1)}, u32[]{:S(2)}, u32[]{:S(2)}) collective-permute-start(f32[392,256]{1,0:T(8,128)S(1)} %get-tuple-element.76), channel_id=1, source_target_pairs={{0,1},{1,0},{2,3},{3,2},{4,5},{5,4},{6,7},{7,6},{8,9},{9,8},{10,11... | collective-permute-start | bytes 1204232 | tf_op jit(solution)/shard_map/ppermute | solution.py:503
  108.2 5.7 %collective-permute-start.30 = (f32[136,256]{1,0:T(8,128)S(1)}, f32[136,256]{1,0:T(8,128)S(1)}, u32[]{:S(2)}, u32[]{:S(2)}) collective-permute-start(f32[136,256]{1,0:T(8,128)S(1)} %slice_add_fusion.here_ref), channel_id=1, source_target_pairs={{0,8},{1,9},{2,10},{3,11},{4,12},{5,13},{6,14},{7,15},{8,16},{9,17... | collective-permute-start | bytes 417800 | tf_op jit(solution)/shard_map/ppermute | solution.py:503
  113.2 7.5 %collective-permute-start.31 = (f32[256,256]{1,0:T(8,128)}, f32[256,256]{1,0:T(8,128)}, u32[]{:S(2)}, u32[]{:S(2)}) collective-permute-start(f32[256,256]{1,0:T(8,128)} %get-tuple-element.82), channel_id=1, source_target_pairs={{0,1},{1,0},{2,3},{3,2},{4,5},{5,4},{6,7},{7,6},{8,9},{9,8},{10,11... | collective-permute-start | bytes 786440 | tf_op jit(solution)/shard_map/ppermute | solution.py:503
  115.2 13.7 %all-to-all-start = ((f32[32,8,128]{2,1,0:T(8,128)}), f32[32,8,128]{2,1,0:T(8,128)S(1)}, u32[]{:S(2)}, u32[]{:S(2)}) async-start(f32[32,8,128]{2,1,0:T(8,128)} %plane_close.1), calls=%async_computation | async-start | bytes 262144 | tf_op jit(solution)/shard_map/all_to_all | solution.py:1153
  130.4 13.3 %collective-permute-start.32 = (f32[512,128]{1,0:T(8,128)S(1)}, f32[512,128]{1,0:T(8,128)S(1)}, u32[]{:S(2)}, u32[]{:S(2)}) collective-permute-start(f32[512,128]{1,0:T(8,128)S(1)} %plane_combine.1), channel_id=1, source_target_pairs={{0,0},{1,16},{2,8},{3,24},{4,4},{5,20},{6,12},{7,28},{8,1},{9,17},... | collective-permute-start | bytes 786440 | tf_op jit(solution)/shard_map/ppermute | solution.py:503
  (17 other events, 174.9 us)

commit v13 on v12

--- a/solution.py
+++ b/solution.py
@@ -1088,8 +1088,8 @@
     meta = jnp.concatenate([meta, moved(meta, over_x)], axis=1)
     meta = jnp.concatenate([meta, moved(meta, z_pair)], axis=1)
     seen = observe(seen, moved(seen, hour_before), kinds, kernels, short3, [forward3, inverse_first3])
-    parcel, behind = lax.optimization_barrier((parcel, seen))
     seen = moved(seen, to_plane)
+    parcel, seen = lax.optimization_barrier((parcel, seen))
     parcels = [parcel, moved(parcel, over_core)]
     spec = plane_spectrum(parcel[hours:], kernels, short3, rows)
     parcels[1], seen, meta, spec = lax.optimization_barrier((parcels[1], seen, meta, spec))

time: 147 us -> 146 us (level)
  waiting for transfers between devices: 56.1 us -> 51.5 us
  starting transfers between devices: 52.3 us -> 56.3 us
    ppermute x33, waiting for transfers between devices: 47.9 us -> 43.3 us  [moved(): return lax.ppermute(value, ('basin', 'tm'), pairs)]
    ppermute x33, starting transfers between devices: 46.8 us -> 50.5 us  [moved(): return lax.ppermute(value, ('basin', 'tm'), pairs)]
  transfers between devices with their start and end apart: 34 -> 34, of which waited for: 18 -> 20; matrix products, arithmetic and copies ran while one was open for 0% -> 0% of each run, Pallas kernels for 15% -> 15%
where the time goes in v13:
time: 146 us; the launch traced here: 145 us
  starting transfers between devices  56.3 us (39%)
  waiting for transfers between devices  51.5 us (35%)
  Pallas kernels  33.1 us (23%)
  local copies, waits for them, and re-layouts  4.04 us (3%)
    ppermute x33, starting transfers between devices, moved(): return lax.ppermute(value, ('basin', 'tm'), pairs)  50.5 us
    ppermute x33, waiting for transfers between devices, moved(): return lax.ppermute(value, ('basin', 'tm'), pairs)  43.3 us
    pallas_call x6, Pallas kernels, plane_call(): pl.pallas_call(kernel, in_specs=[pl.BlockSpec(memory_space=pltpu.SMEM)] *...  9.78 us
    pallas_call x2, Pallas kernels, plane_couple(): pl.pallas_call(functools.partial(plane_couple_kernel, last), in_specs=[pl...  9.56 us
    all_to_all x1, waiting for transfers between devices, plane_shards(): close_note = lax.all_to_all(note, ('basin', 'tm'), 0, 0, tiled=False)  8.18 us
    all_to_all x1, starting transfers between devices, plane_shards(): close_note = lax.all_to_all(note, ('basin', 'tm'), 0, 0, tiled=False)  5.77 us
    pallas_call x3, Pallas kernels, plane_rows(): pl.pallas_call(plane_rows_kernel, in_specs=[pl.BlockSpec(memory_space=plt...  4.51 us
    unnamed x30, local copies, waits for them, and re-layouts  3.95 us
  transfers between devices with their start and end apart: 34, of which 20 were waited for; matrix products, arithmetic and copies ran while one was open for 0% of the time, Pallas kernels for 15%

profile of v13, /device:TPU:1, one launch (start us, length us, event | category | flops | bytes accessed | tf_op | source)
XLA Modules:
  0.0 145.5 jit_solution(15521532212899562705)
XLA Ops:
  0.0 1.6 %copy-done = f32[4096,128]{1,0:T(8,128)S(1)} copy-done((f32[4096,128]{1,0:T(8,128)S(1)}, f32[4096,128]{1,0:T(8,128)}, u32[]{:S(2)}) %copy-start) | copy-done | bytes 2097176
  5.4 4.6 %collective-permute-start = (f32[136,512]{1,0:T(8,128)S(1)}, f32[136,512]{1,0:T(8,128)S(1)}, u32[]{:S(2)}, u32[]{:S(2)}) collective-permute-start(f32[136,512]{1,0:T(8,128)S(1)} %send.1), channel_id=1, source_target_pairs={{0,0},{1,8},{2,16},{3,24},{4,4},{5,12},{6,20},{7,28},{8,2},{9,10},... | collective-permute-start | bytes 835592 | tf_op jit(solution)/shard_map/ppermute | solution.py:503
  10.0 1.9 %collective-permute-start.1 = (f32[256,128]{1,0:T(8,128)S(1)}, f32[256,128]{1,0:T(8,128)S(1)}, u32[]{:S(2)}, u32[]{:S(2)}) collective-permute-start(f32[256,128]{1,0:T(8,128)S(1)} %copy-done.12), channel_id=1, source_target_pairs={{1,0},{2,1},{3,2},{5,4},{6,5},{7,6},{9,8},{10,9},{11,10},{13,12},{... | collective-permute-start | bytes 393224 | tf_op jit(solution)/shard_map/ppermute | solution.py:503
  13.4 3.6 %collective-permute-done.1.later_ref = f32[256,128]{1,0:T(8,128)S(1)} collective-permute-done((f32[256,128]{1,0:T(8,128)S(1)}, f32[256,128]{1,0:T(8,128)S(1)}, u32[]{:S(2)}, u32[]{:S(2)}) %collective-permute-start.1) | collective-permute-done | bytes 131104 | tf_op jit(solution)/shard_map/ppermute | solution.py:503
  18.3 1.9 %collective-permute-start.2 = (f32[128,256]{1,0:T(8,128)S(1)}, f32[128,256]{1,0:T(8,128)S(1)}, u32[]{:S(2)}, u32[]{:S(2)}) collective-permute-start(f32[128,256]{1,0:T(8,128)S(1)} %observe.1), channel_id=1, source_target_pairs={{0,0},{1,8},{2,16},{3,24},{4,4},{5,12},{6,20},{7,28},{8,2},{9,10},... | collective-permute-start | bytes 393224 | tf_op jit(solution)/shard_map/ppermute | solution.py:503
  20.9 8.3 %collective-permute-done.2.seen_ref = f32[128,256]{1,0:T(8,128)S(1)} collective-permute-done((f32[128,256]{1,0:T(8,128)S(1)}, f32[128,256]{1,0:T(8,128)S(1)}, u32[]{:S(2)}, u32[]{:S(2)}) %collective-permute-start.2) | collective-permute-done | bytes 131104 | tf_op jit(solution)/shard_map/ppermute | solution.py:503
  30.8 1.6 %spread.1 = (f32[128,256]{1,0:T(8,128)S(1)}, f32[128,256]{1,0:T(8,128)S(1)}, f32[128,256]{1,0:T(8,128)S(1)}, f32[128,256]{1,0:T(8,128)S(1)}) custom-call(s32[6]{0:T(128)S(1)} %broadcast_multiply_fusion.first_ref, f32[136,512]{1,0:T(8,128)S(1)} %collective-permute-done.mine_ref, f32[136,512]{1,0:T(8,128)S(1)} %collective-permute-done.3.other_ref), custom_call_target="tpu_custom_call" | custom-call | flops 1 | bytes 1 | tf_op jit(solution)/shard_map/spread/pallas_call | solution.py:714
  35.2 2.0 %collective-permute-start.6 = (f32[24,2048]{1,0:T(8,128)S(1)}, f32[24,2048]{1,0:T(8,128)S(1)}, u32[]{:S(2)}, u32[]{:S(2)}) collective-permute-start(f32[24,2048]{1,0:T(8,128)S(1)} %pad_maximum_fusion.refs_0_), channel_id=1, source_target_pairs={{0,16},{1,17},{2,18},{3,19},{4,20},{5,21},{6,22},{7,23},{8,24},{9,... | collective-permute-start | bytes 589832 | tf_op jit(solution)/shard_map/ppermute | solution.py:503
  38.1 1.8 %collective-permute-done.9 = f32[128,256]{1,0:T(8,128)S(1)} collective-permute-done((f32[128,256]{1,0:T(8,128)S(1)}, f32[128,256]{1,0:T(8,128)S(1)}, u32[]{:S(2)}, u32[]{:S(2)}) %collective-permute-start.9) | collective-permute-done | bytes 131104 | tf_op jit(solution)/shard_map/ppermute | solution.py:503
  40.8 4.6 %collective-permute-start.10 = (f32[128,256]{1,0:T(8,128)S(1)}, f32[128,256]{1,0:T(8,128)S(1)}, u32[]{:S(2)}, u32[]{:S(2)}) collective-permute-start(f32[128,256]{1,0:T(8,128)S(1)} %add_add_fusion.here_ref), channel_id=1, source_target_pairs={{0,8},{1,9},{2,10},{3,11},{4,12},{5,13},{6,14},{7,15},{8,0},{9,1},... | collective-permute-start | bytes 393224 | tf_op jit(solution)/shard_map/ppermute | solution.py:503
  45.3 4.6 %plane_couple.2.refs_1_ = f32[1024,512]{1,0:T(8,128)S(1)} custom-call(s32[6]{0:T(128)S(1)} %broadcast_multiply_fusion.first_ref, f32[24,2048]{1,0:T(8,128)S(1)} %pad_maximum_fusion.refs_0_), custom_call_target="tpu_custom_call" | custom-call | flops 2147483648 | bytes 2000000 | tf_op jit(solution)/shard_map/plane_couple/pallas_call | solution.py:780
  50.0 2.6 %plane_first.1.a_ref.pulled_ref.old_z_ref = f32[128,256]{1,0:T(8,128)S(1)} custom-call(f32[3]{0:T(128)S(1)} %add_convert_fusion.flag_ref, f32[128,256]{1,0:T(8,128)S(1)} %add_add_fusion.here_ref, f32[128,256]{1,0:T(8,128)S(1)} %collective-permute-done.10.pair_ref, f32[128,256]{1,0:T(8,128)S(1)} %collective-permute-done.11.middle_ref, ...), custom_call_target="tpu_custom_call" | custom-call | flops 1 | bytes 1 | tf_op jit(solution)/shard_map/plane_first/pallas_call | solution.py:907
  52.6 1.5 %collective-permute-start.14 = (f32[128,256]{1,0:T(8,128)S(1)}, f32[128,256]{1,0:T(8,128)S(1)}, u32[]{:S(2)}, u32[]{:S(2)}) collective-permute-start(f32[128,256]{1,0:T(8,128)S(1)} %plane_first.1.a_ref.pulled_ref.old_z_ref), channel_id=1, source_target_pairs={{0,6},{1,7},{2,4},{3,5},{4,2},{5,3},{6,0},{7,1},{8,14},{9,15},{10,... | collective-permute-start | bytes 393224 | tf_op jit(solution)/shard_map/ppermute | solution.py:503
  55.4 4.9 %plane_couple.3 = (bf16[1024,512]{1,0:T(8,128)(2,1)S(1)}, bf16[1024,512]{1,0:T(8,128)(2,1)S(1)}) custom-call(s32[6]{0:T(128)S(1)} %broadcast_multiply_fusion.first_ref, f32[24,2048]{1,0:T(8,128)S(1)} %collective-permute-done.6.refs_0_, f32[1024,512]{1,0:T(8,128)S(1)} %plane_couple.2.refs_1_), custom_call_target="tpu_custom_call" | custom-call | flops 2147483648 | bytes 2000000 | tf_op jit(solution)/shard_map/plane_couple/pallas_call | solution.py:780
  61.0 2.9 %collective-permute-start.15 = (f32[128,256]{1,0:T(8,128)S(1)}, f32[128,256]{1,0:T(8,128)S(1)}, u32[]{:S(2)}, u32[]{:S(2)}) collective-permute-start(f32[128,256]{1,0:T(8,128)S(1)} %get-tuple-element.67), channel_id=1, source_target_pairs={{0,1},{1,0},{2,3},{3,2},{4,5},{5,4},{6,7},{7,6},{8,9},{9,8},{10,11... | collective-permute-start | bytes 393224 | tf_op jit(solution)/shard_map/ppermute | solution.py:503
  65.5 2.7 %collective-permute-start.16 = (f32[128,256]{1,0:T(8,128)S(1)}, f32[128,256]{1,0:T(8,128)S(1)}, u32[]{:S(2)}, u32[]{:S(2)}) collective-permute-start(f32[128,256]{1,0:T(8,128)S(1)} %add.61.here_ref.old_s_ref), channel_id=1, source_target_pairs={{0,8},{1,9},{2,10},{3,11},{4,12},{5,13},{6,14},{7,15},{8,0},{9,1},... | collective-permute-start | bytes 393224 | tf_op jit(solution)/shard_map/ppermute | solution.py:503
  68.2 3.3 %collective-permute-done.16.pair_ref = f32[128,256]{1,0:T(8,128)S(1)} collective-permute-done((f32[128,256]{1,0:T(8,128)S(1)}, f32[128,256]{1,0:T(8,128)S(1)}, u32[]{:S(2)}, u32[]{:S(2)}) %collective-permute-start.16) | collective-permute-done | bytes 131104 | tf_op jit(solution)/shard_map/ppermute | solution.py:503
  71.4 1.8 %plane_open.1 = (f32[136,256]{1,0:T(8,128)S(1)}, f32[256,256]{1,0:T(8,128)S(1)}) custom-call(f32[3]{0:T(128)S(1)} %add_convert_fusion.flag_ref, f32[128,256]{1,0:T(8,128)S(1)} %add.61.here_ref.old_s_ref, f32[128,256]{1,0:T(8,128)S(1)} %collective-permute-done.16.pair_ref, f32[128,256]{1,0:T(8,128)S(1)} %collective-permute-done.17.middle_ref, ...), custom_call_target="tpu_custom_call" | custom-call | flops 1 | bytes 1 | tf_op jit(solution)/shard_map/plane_open/pallas_call | solution.py:907
  73.3 1.8 %collective-permute-start.20 = (f32[136,256]{1,0:T(8,128)S(1)}, f32[136,256]{1,0:T(8,128)S(1)}, u32[]{:S(2)}, u32[]{:S(2)}) collective-permute-start(f32[136,256]{1,0:T(8,128)S(1)} %get-tuple-element.68.a_ref.pulled_ref), channel_id=1, source_target_pairs={{0,6},{1,7},{2,4},{3,5},{4,2},{5,3},{6,0},{7,1},{8,14},{9,15},{10,... | collective-permute-start | bytes 417800 | tf_op jit(solution)/shard_map/ppermute | solution.py:503
  78.2 4.1 %collective-permute-done.19.c_ref = f32[136,256]{1,0:T(8,128)S(1)} collective-permute-done((f32[136,256]{1,0:T(8,128)S(1)}, f32[136,256]{1,0:T(8,128)S(1)}, u32[]{:S(2)}, u32[]{:S(2)}) %collective-permute-start.19) | collective-permute-done | bytes 139296 | tf_op jit(solution)/shard_map/ppermute | solution.py:503
  86.2 2.9 %collective-permute-start.22 = (f32[136,256]{1,0:T(8,128)S(1)}, f32[136,256]{1,0:T(8,128)S(1)}, u32[]{:S(2)}, u32[]{:S(2)}) collective-permute-start(f32[136,256]{1,0:T(8,128)S(1)} %slice_add_fusion.1.here_ref), channel_id=1, source_target_pairs={{0,8},{1,9},{2,10},{3,11},{4,12},{5,13},{6,14},{7,15},{8,0},{9,1},... | collective-permute-start | bytes 417800 | tf_op jit(solution)/shard_map/ppermute | solution.py:503
  89.2 2.1 %collective-permute-start.24 = (f32[8,256]{1,0:T(8,128)S(1)}, f32[8,256]{1,0:T(8,128)S(1)}, u32[]{:S(2)}, u32[]{:S(2)}) collective-permute-start(f32[8,256]{1,0:T(8,128)S(1)} %slice.23), channel_id=1, source_target_pairs={{0,24},{1,25},{2,26},{3,27},{4,28},{5,29},{6,30},{7,31},{8,16},{9,... | collective-permute-start | bytes 24584 | tf_op jit(solution)/shard_map/ppermute | solution.py:503
  101.0 1.8 %collective-permute-done.27.c_ref = f32[136,256]{1,0:T(8,128)S(1)} collective-permute-done((f32[136,256]{1,0:T(8,128)S(1)}, f32[136,256]{1,0:T(8,128)S(1)}, u32[]{:S(2)}, u32[]{:S(2)}) %collective-permute-start.27) | collective-permute-done | bytes 139296 | tf_op jit(solution)/shard_map/ppermute | solution.py:503
  103.5 3.4 %collective-permute-start.29 = (f32[392,256]{1,0:T(8,128)S(1)}, f32[392,256]{1,0:T(8,128)S(1)}, u32[]{:S(2)}, u32[]{:S(2)}) collective-permute-start(f32[392,256]{1,0:T(8,128)S(1)} %get-tuple-element.78), channel_id=1, source_target_pairs={{0,1},{1,0},{2,3},{3,2},{4,5},{5,4},{6,7},{7,6},{8,9},{9,8},{10,11... | collective-permute-start | bytes 1204232 | tf_op jit(solution)/shard_map/ppermute | solution.py:503
  108.3 2.0 %collective-permute-start.30 = (f32[136,256]{1,0:T(8,128)S(1)}, f32[136,256]{1,0:T(8,128)S(1)}, u32[]{:S(2)}, u32[]{:S(2)}) collective-permute-start(f32[136,256]{1,0:T(8,128)S(1)} %slice_add_fusion.here_ref), channel_id=1, source_target_pairs={{0,8},{1,9},{2,10},{3,11},{4,12},{5,13},{6,14},{7,15},{8,16},{9,17... | collective-permute-start | bytes 417800 | tf_op jit(solution)/shard_map/ppermute | solution.py:503
  110.3 2.0 %plane_rows.5 = (f32[128,512]{1,0:T(8,128)S(1)}, f32[256,256]{1,0:T(8,128)}, f32[256,512]{1,0:T(8,128)S(1)}) custom-call(s32[6]{0:T(128)S(1)} %broadcast_multiply_fusion.first_ref, f32[8,512]{1,0:T(8,128)S(1)} %slice.17.class_ref.meta_ref, f32[8,512]{1,0:T(8,128)S(1)} %slice.18.meta_other_ref, f32[136,256]{1,0:T(8,128)S(1)} %get-tuple-element.74.a_ref.pulled_ref, ...), custom_call_target="tpu_custom_call" | custom-call | flops 1000000000 | bytes 2000000 | tf_op jit(solution)/shard_map/plane_rows/pallas_call | solution.py:863
  114.3 5.8 %all-to-all-start = ((f32[32,8,128]{2,1,0:T(8,128)}), f32[32,8,128]{2,1,0:T(8,128)S(1)}, u32[]{:S(2)}, u32[]{:S(2)}) async-start(f32[32,8,128]{2,1,0:T(8,128)} %plane_close.1), calls=%async_computation | async-start | bytes 262144 | tf_op jit(solution)/shard_map/all_to_all | solution.py:1153
  120.1 8.2 %all-to-all-done.close_ref = f32[32,8,128]{2,1,0:T(8,128)S(1)} async-done(((f32[32,8,128]{2,1,0:T(8,128)}), f32[32,8,128]{2,1,0:T(8,128)S(1)}, u32[]{:S(2)}, u32[]{:S(2)}) %all-to-all-start) | async-done | bytes 131104 | tf_op jit(solution)/shard_map/all_to_all | solution.py:1153
  128.3 1.5 %plane_combine.1 = f32[512,128]{1,0:T(8,128)S(1)} custom-call(f32[8,256]{1,0:T(8,128)S(1)} %get-tuple-element.73.open_ref, f32[32,8,128]{2,1,0:T(8,128)S(1)} %all-to-all-done.close_ref, f32[32,128]{1,0:T(8,128)S(1)} %copy-done.11, f32[256,512]{1,0:T(8,128)S(1)} %get-tuple-element.82.stack_ref, f32[128,512]{1,0:T(8,128)S(1)} %get-tuple-element.83.mine_ref, ...), custom_call_target="tpu_custom_call" | custom-call | flops 1 | bytes 1 | tf_op jit(solution)/shard_map/plane_combine/pallas_call | solution.py:907
  129.8 2.6 %collective-permute-start.32 = (f32[512,128]{1,0:T(8,128)S(1)}, f32[512,128]{1,0:T(8,128)S(1)}, u32[]{:S(2)}, u32[]{:S(2)}) collective-permute-start(f32[512,128]{1,0:T(8,128)S(1)} %plane_combine.1), channel_id=1, source_target_pairs={{0,0},{1,16},{2,8},{3,24},{4,4},{5,20},{6,12},{7,28},{8,1},{9,17},... | collective-permute-start | bytes 786440 | tf_op jit(solution)/shard_map/ppermute | solution.py:503
  132.4 10.7 %collective-permute-done.32.rows_ref = f32[512,128]{1,0:T(8,128)S(1)} collective-permute-done((f32[512,128]{1,0:T(8,128)S(1)}, f32[512,128]{1,0:T(8,128)S(1)}, u32[]{:S(2)}, u32[]{:S(2)}) %collective-permute-start.32) | collective-permute-done | bytes 262176 | tf_op jit(solution)/shard_map/ppermute | solution.py:503
  143.1 2.4 %plane_finish.1 = f32[4096,128]{1,0:T(8,128)} custom-call(f32[512,128]{1,0:T(8,128)S(1)} %collective-permute-done.32.rows_ref, s32[32,16,128]{2,1,0:T(8,128)S(1)} %copy-done.5, f32[4096,128]{1,0:T(8,128)S(1)} %copy-done.1), custom_call_target="tpu_custom_call" | custom-call | tf_op jit(solution)/shard_map/plane_finish/pallas_call | solution.py:1055
  (98 shorter events, 37.7 us)
Async XLA Ops:
  5.4 23.9 %collective-permute-start = (f32[136,512]{1,0:T(8,128)S(1)}, f32[136,512]{1,0:T(8,128)S(1)}, u32[]{:S(2)}, u32[]{:S(2)}) collective-permute-start(f32[136,512]{1,0:T(8,128)S(1)} %send.1), channel_id=1, source_target_pairs={{0,0},{1,8},{2,16},{3,24},{4,4},{5,12},{6,20},{7,28},{8,2},{9,10},... | collective-permute-start | bytes 835592 | tf_op jit(solution)/shard_map/ppermute | solution.py:503
  10.0 7.0 %collective-permute-start.1 = (f32[256,128]{1,0:T(8,128)S(1)}, f32[256,128]{1,0:T(8,128)S(1)}, u32[]{:S(2)}, u32[]{:S(2)}) collective-permute-start(f32[256,128]{1,0:T(8,128)S(1)} %copy-done.12), channel_id=1, source_target_pairs={{1,0},{2,1},{3,2},{5,4},{6,5},{7,6},{9,8},{10,9},{11,10},{13,12},{... | collective-permute-start | bytes 393224 | tf_op jit(solution)/shard_map/ppermute | solution.py:503
  12.1 8.2 %collective-permute-start.4 = (f32[24,512]{1,0:T(8,128)S(1)}, f32[24,512]{1,0:T(8,128)S(1)}, u32[]{:S(2)}, u32[]{:S(2)}) collective-permute-start(f32[24,512]{1,0:T(8,128)S(1)} %describe.1), channel_id=1, source_target_pairs={{0,4},{1,5},{2,6},{3,7},{4,0},{5,1},{6,2},{7,3},{8,12},{9,13},{10,... | collective-permute-start | bytes 147464 | tf_op jit(solution)/shard_map/ppermute | solution.py:503
  18.3 11.0 %collective-permute-start.2 = (f32[128,256]{1,0:T(8,128)S(1)}, f32[128,256]{1,0:T(8,128)S(1)}, u32[]{:S(2)}, u32[]{:S(2)}) collective-permute-start(f32[128,256]{1,0:T(8,128)S(1)} %observe.1), channel_id=1, source_target_pairs={{0,0},{1,8},{2,16},{3,24},{4,4},{5,12},{6,20},{7,28},{8,2},{9,10},... | collective-permute-start | bytes 393224 | tf_op jit(solution)/shard_map/ppermute | solution.py:503
  20.4 8.9 %collective-permute-start.5 = (f32[24,1024]{1,0:T(8,128)S(1)}, f32[24,1024]{1,0:T(8,128)S(1)}, u32[]{:S(2)}, u32[]{:S(2)}) collective-permute-start(f32[24,1024]{1,0:T(8,128)S(1)} %pad_maximum_fusion.1), channel_id=1, source_target_pairs={{0,8},{1,9},{2,10},{3,11},{4,12},{5,13},{6,14},{7,15},{8,0},{9,1},... | collective-permute-start | bytes 294920 | tf_op jit(solution)/shard_map/ppermute | solution.py:503
  32.4 4.9 %collective-permute-start.7 = (f32[128,256]{1,0:T(8,128)S(1)}, f32[128,256]{1,0:T(8,128)S(1)}, u32[]{:S(2)}, u32[]{:S(2)}) collective-permute-start(f32[128,256]{1,0:T(8,128)S(1)} %get-tuple-element.55), channel_id=1, source_target_pairs={{0,4},{1,5},{2,6},{3,7},{4,0},{5,1},{6,2},{7,3},{8,12},{9,13},{10,... | collective-permute-start | bytes 393224 | tf_op jit(solution)/shard_map/ppermute | solution.py:503
  33.6 4.5 %collective-permute-start.8 = (f32[128,256]{1,0:T(8,128)S(1)}, f32[128,256]{1,0:T(8,128)S(1)}, u32[]{:S(2)}, u32[]{:S(2)}) collective-permute-start(f32[128,256]{1,0:T(8,128)S(1)} %get-tuple-element.56), channel_id=1, source_target_pairs={{0,2},{1,3},{2,0},{3,1},{4,6},{5,7},{6,4},{7,5},{8,10},{9,11},{10,... | collective-permute-start | bytes 393224 | tf_op jit(solution)/shard_map/ppermute | solution.py:503
  34.1 5.8 %collective-permute-start.9 = (f32[128,256]{1,0:T(8,128)S(1)}, f32[128,256]{1,0:T(8,128)S(1)}, u32[]{:S(2)}, u32[]{:S(2)}) collective-permute-start(f32[128,256]{1,0:T(8,128)S(1)} %get-tuple-element.57), channel_id=1, source_target_pairs={{0,6},{1,7},{2,4},{3,5},{4,2},{5,3},{6,0},{7,1},{8,14},{9,15},{10,... | collective-permute-start | bytes 393224 | tf_op jit(solution)/shard_map/ppermute | solution.py:503
  35.2 20.2 %collective-permute-start.6 = (f32[24,2048]{1,0:T(8,128)S(1)}, f32[24,2048]{1,0:T(8,128)S(1)}, u32[]{:S(2)}, u32[]{:S(2)}) collective-permute-start(f32[24,2048]{1,0:T(8,128)S(1)} %pad_maximum_fusion.refs_0_), channel_id=1, source_target_pairs={{0,16},{1,17},{2,18},{3,19},{4,20},{5,21},{6,22},{7,23},{8,24},{9,... | collective-permute-start | bytes 589832 | tf_op jit(solution)/shard_map/ppermute | solution.py:503
  39.9 10.0 %collective-permute-start.11 = (f32[128,256]{1,0:T(8,128)S(1)}, f32[128,256]{1,0:T(8,128)S(1)}, u32[]{:S(2)}, u32[]{:S(2)}) collective-permute-start(f32[128,256]{1,0:T(8,128)S(1)} %add_add_fusion.here_ref), channel_id=1, source_target_pairs={{8,16},{9,17},{10,18},{11,19},{12,20},{13,21},{14,22},{15,23},{16,... | collective-permute-start | bytes 393224 | tf_op jit(solution)/shard_map/ppermute | solution.py:503
  40.8 9.2 %collective-permute-start.10 = (f32[128,256]{1,0:T(8,128)S(1)}, f32[128,256]{1,0:T(8,128)S(1)}, u32[]{:S(2)}, u32[]{:S(2)}) collective-permute-start(f32[128,256]{1,0:T(8,128)S(1)} %add_add_fusion.here_ref), channel_id=1, source_target_pairs={{0,8},{1,9},{2,10},{3,11},{4,12},{5,13},{6,14},{7,15},{8,0},{9,1},... | collective-permute-start | bytes 393224 | tf_op jit(solution)/shard_map/ppermute | solution.py:503
  52.6 7.7 %collective-permute-start.14 = (f32[128,256]{1,0:T(8,128)S(1)}, f32[128,256]{1,0:T(8,128)S(1)}, u32[]{:S(2)}, u32[]{:S(2)}) collective-permute-start(f32[128,256]{1,0:T(8,128)S(1)} %plane_first.1.a_ref.pulled_ref.old_z_ref), channel_id=1, source_target_pairs={{0,6},{1,7},{2,4},{3,5},{4,2},{5,3},{6,0},{7,1},{8,14},{9,15},{10,... | collective-permute-start | bytes 393224 | tf_op jit(solution)/shard_map/ppermute | solution.py:503
  54.1 6.2 %collective-permute-start.13 = (f32[128,256]{1,0:T(8,128)S(1)}, f32[128,256]{1,0:T(8,128)S(1)}, u32[]{:S(2)}, u32[]{:S(2)}) collective-permute-start(f32[128,256]{1,0:T(8,128)S(1)} %plane_first.1.a_ref.pulled_ref.old_z_ref), channel_id=1, source_target_pairs={{0,2},{1,3},{2,0},{3,1},{4,6},{5,7},{6,4},{7,5},{8,10},{9,11},{10,... | collective-permute-start | bytes 393224 | tf_op jit(solution)/shard_map/ppermute | solution.py:503
  55.3 5.1 %collective-permute-start.12 = (f32[128,256]{1,0:T(8,128)S(1)}, f32[128,256]{1,0:T(8,128)S(1)}, u32[]{:S(2)}, u32[]{:S(2)}) collective-permute-start(f32[128,256]{1,0:T(8,128)S(1)} %plane_first.1.a_ref.pulled_ref.old_z_ref), channel_id=1, source_target_pairs={{0,4},{1,5},{2,6},{3,7},{4,0},{5,1},{6,2},{7,3},{8,12},{9,13},{10,... | collective-permute-start | bytes 393224 | tf_op jit(solution)/shard_map/ppermute | solution.py:503
  61.0 3.8 %collective-permute-start.15 = (f32[128,256]{1,0:T(8,128)S(1)}, f32[128,256]{1,0:T(8,128)S(1)}, u32[]{:S(2)}, u32[]{:S(2)}) collective-permute-start(f32[128,256]{1,0:T(8,128)S(1)} %get-tuple-element.67), channel_id=1, source_target_pairs={{0,1},{1,0},{2,3},{3,2},{4,5},{5,4},{6,7},{7,6},{8,9},{9,8},{10,11... | collective-permute-start | bytes 393224 | tf_op jit(solution)/shard_map/ppermute | solution.py:503
  64.8 3.3 %collective-permute-start.17 = (f32[128,256]{1,0:T(8,128)S(1)}, f32[128,256]{1,0:T(8,128)S(1)}, u32[]{:S(2)}, u32[]{:S(2)}) collective-permute-start(f32[128,256]{1,0:T(8,128)S(1)} %add.61.here_ref.old_s_ref), channel_id=1, source_target_pairs={{8,16},{9,17},{10,18},{11,19},{12,20},{13,21},{14,22},{15,23},{16,... | collective-permute-start | bytes 393224 | tf_op jit(solution)/shard_map/ppermute | solution.py:503
  65.5 5.9 %collective-permute-start.16 = (f32[128,256]{1,0:T(8,128)S(1)}, f32[128,256]{1,0:T(8,128)S(1)}, u32[]{:S(2)}, u32[]{:S(2)}) collective-permute-start(f32[128,256]{1,0:T(8,128)S(1)} %add.61.here_ref.old_s_ref), channel_id=1, source_target_pairs={{0,8},{1,9},{2,10},{3,11},{4,12},{5,13},{6,14},{7,15},{8,0},{9,1},... | collective-permute-start | bytes 393224 | tf_op jit(solution)/shard_map/ppermute | solution.py:503
  73.3 4.9 %collective-permute-start.20 = (f32[136,256]{1,0:T(8,128)S(1)}, f32[136,256]{1,0:T(8,128)S(1)}, u32[]{:S(2)}, u32[]{:S(2)}) collective-permute-start(f32[136,256]{1,0:T(8,128)S(1)} %get-tuple-element.68.a_ref.pulled_ref), channel_id=1, source_target_pairs={{0,6},{1,7},{2,4},{3,5},{4,2},{5,3},{6,0},{7,1},{8,14},{9,15},{10,... | collective-permute-start | bytes 417800 | tf_op jit(solution)/shard_map/ppermute | solution.py:503
  75.1 7.2 %collective-permute-start.19 = (f32[136,256]{1,0:T(8,128)S(1)}, f32[136,256]{1,0:T(8,128)S(1)}, u32[]{:S(2)}, u32[]{:S(2)}) collective-permute-start(f32[136,256]{1,0:T(8,128)S(1)} %get-tuple-element.68.a_ref.pulled_ref), channel_id=1, source_target_pairs={{0,2},{1,3},{2,0},{3,1},{4,6},{5,7},{6,4},{7,5},{8,10},{9,11},{10,... | collective-permute-start | bytes 417800 | tf_op jit(solution)/shard_map/ppermute | solution.py:503
  76.0 6.2 %collective-permute-start.18 = (f32[136,256]{1,0:T(8,128)S(1)}, f32[136,256]{1,0:T(8,128)S(1)}, u32[]{:S(2)}, u32[]{:S(2)}) collective-permute-start(f32[136,256]{1,0:T(8,128)S(1)} %get-tuple-element.68.a_ref.pulled_ref), channel_id=1, source_target_pairs={{0,4},{1,5},{2,6},{3,7},{4,0},{5,1},{6,2},{7,3},{8,12},{9,13},{10,... | collective-permute-start | bytes 417800 | tf_op jit(solution)/shard_map/ppermute | solution.py:503
  85.4 5.9 %collective-permute-start.25 = (f32[136,256]{1,0:T(8,128)S(1)}, f32[136,256]{1,0:T(8,128)S(1)}, u32[]{:S(2)}, u32[]{:S(2)}) collective-permute-start(f32[136,256]{1,0:T(8,128)S(1)} %slice_add_fusion.1.here_ref), channel_id=1, source_target_pairs={{8,16},{9,17},{10,18},{11,19},{12,20},{13,21},{14,22},{15,23},{16,... | collective-permute-start | bytes 417800 | tf_op jit(solution)/shard_map/ppermute | solution.py:503
  86.2 6.3 %collective-permute-start.22 = (f32[136,256]{1,0:T(8,128)S(1)}, f32[136,256]{1,0:T(8,128)S(1)}, u32[]{:S(2)}, u32[]{:S(2)}) collective-permute-start(f32[136,256]{1,0:T(8,128)S(1)} %slice_add_fusion.1.here_ref), channel_id=1, source_target_pairs={{0,8},{1,9},{2,10},{3,11},{4,12},{5,13},{6,14},{7,15},{8,0},{9,1},... | collective-permute-start | bytes 417800 | tf_op jit(solution)/shard_map/ppermute | solution.py:503
  89.2 5.1 %collective-permute-start.24 = (f32[8,256]{1,0:T(8,128)S(1)}, f32[8,256]{1,0:T(8,128)S(1)}, u32[]{:S(2)}, u32[]{:S(2)}) collective-permute-start(f32[8,256]{1,0:T(8,128)S(1)} %slice.23), channel_id=1, source_target_pairs={{0,24},{1,25},{2,26},{3,27},{4,28},{5,29},{6,30},{7,31},{8,16},{9,... | collective-permute-start | bytes 24584 | tf_op jit(solution)/shard_map/ppermute | solution.py:503
  91.3 3.4 %collective-permute-start.23 = (f32[8,256]{1,0:T(8,128)S(1)}, f32[8,256]{1,0:T(8,128)S(1)}, u32[]{:S(2)}, u32[]{:S(2)}) collective-permute-start(f32[8,256]{1,0:T(8,128)S(1)} %slice.23), channel_id=1, source_target_pairs={{0,16},{1,17},{2,18},{3,19},{4,20},{5,21},{6,22},{7,23},{8,24},{9,... | collective-permute-start | bytes 24584 | tf_op jit(solution)/shard_map/ppermute | solution.py:503
  96.0 5.0 %collective-permute-start.28 = (f32[136,256]{1,0:T(8,128)S(1)}, f32[136,256]{1,0:T(8,128)S(1)}, u32[]{:S(2)}, u32[]{:S(2)}) collective-permute-start(f32[136,256]{1,0:T(8,128)S(1)} %get-tuple-element.74.a_ref.pulled_ref), channel_id=1, source_target_pairs={{0,6},{1,7},{2,4},{3,5},{4,2},{5,3},{6,0},{7,1},{8,14},{9,15},{10,... | collective-permute-start | bytes 417800 | tf_op jit(solution)/shard_map/ppermute | solution.py:503
  97.3 5.5 %collective-permute-start.27 = (f32[136,256]{1,0:T(8,128)S(1)}, f32[136,256]{1,0:T(8,128)S(1)}, u32[]{:S(2)}, u32[]{:S(2)}) collective-permute-start(f32[136,256]{1,0:T(8,128)S(1)} %get-tuple-element.74.a_ref.pulled_ref), channel_id=1, source_target_pairs={{0,2},{1,3},{2,0},{3,1},{4,6},{5,7},{6,4},{7,5},{8,10},{9,11},{10,... | collective-permute-start | bytes 417800 | tf_op jit(solution)/shard_map/ppermute | solution.py:503
  98.3 4.6 %collective-permute-start.26 = (f32[136,256]{1,0:T(8,128)S(1)}, f32[136,256]{1,0:T(8,128)S(1)}, u32[]{:S(2)}, u32[]{:S(2)}) collective-permute-start(f32[136,256]{1,0:T(8,128)S(1)} %get-tuple-element.74.a_ref.pulled_ref), channel_id=1, source_target_pairs={{0,4},{1,5},{2,6},{3,7},{4,0},{5,1},{6,2},{7,3},{8,12},{9,13},{10,... | collective-permute-start | bytes 417800 | tf_op jit(solution)/shard_map/ppermute | solution.py:503
  103.5 4.8 %collective-permute-start.29 = (f32[392,256]{1,0:T(8,128)S(1)}, f32[392,256]{1,0:T(8,128)S(1)}, u32[]{:S(2)}, u32[]{:S(2)}) collective-permute-start(f32[392,256]{1,0:T(8,128)S(1)} %get-tuple-element.78), channel_id=1, source_target_pairs={{0,1},{1,0},{2,3},{3,2},{4,5},{5,4},{6,7},{7,6},{8,9},{9,8},{10,11... | collective-permute-start | bytes 1204232 | tf_op jit(solution)/shard_map/ppermute | solution.py:503
  108.3 4.6 %collective-permute-start.30 = (f32[136,256]{1,0:T(8,128)S(1)}, f32[136,256]{1,0:T(8,128)S(1)}, u32[]{:S(2)}, u32[]{:S(2)}) collective-permute-start(f32[136,256]{1,0:T(8,128)S(1)} %slice_add_fusion.here_ref), channel_id=1, source_target_pairs={{0,8},{1,9},{2,10},{3,11},{4,12},{5,13},{6,14},{7,15},{8,16},{9,17... | collective-permute-start | bytes 417800 | tf_op jit(solution)/shard_map/ppermute | solution.py:503
  112.3 7.8 %collective-permute-start.31 = (f32[256,256]{1,0:T(8,128)}, f32[256,256]{1,0:T(8,128)}, u32[]{:S(2)}, u32[]{:S(2)}) collective-permute-start(f32[256,256]{1,0:T(8,128)} %get-tuple-element.84), channel_id=1, source_target_pairs={{0,1},{1,0},{2,3},{3,2},{4,5},{5,4},{6,7},{7,6},{8,9},{9,8},{10,11... | collective-permute-start | bytes 786440 | tf_op jit(solution)/shard_map/ppermute | solution.py:503
  114.3 14.0 %all-to-all-start = ((f32[32,8,128]{2,1,0:T(8,128)}), f32[32,8,128]{2,1,0:T(8,128)S(1)}, u32[]{:S(2)}, u32[]{:S(2)}) async-start(f32[32,8,128]{2,1,0:T(8,128)} %plane_close.1), calls=%async_computation | async-start | bytes 262144 | tf_op jit(solution)/shard_map/all_to_all | solution.py:1153
  129.8 13.3 %collective-permute-start.32 = (f32[512,128]{1,0:T(8,128)S(1)}, f32[512,128]{1,0:T(8,128)S(1)}, u32[]{:S(2)}, u32[]{:S(2)}) collective-permute-start(f32[512,128]{1,0:T(8,128)S(1)} %plane_combine.1), channel_id=1, source_target_pairs={{0,0},{1,16},{2,8},{3,24},{4,4},{5,20},{6,12},{7,28},{8,1},{9,17},... | collective-permute-start | bytes 786440 | tf_op jit(solution)/shard_map/ppermute | solution.py:503
  (17 other events, 171.4 us)

commit v14 on v13

--- a/solution.py
+++ b/solution.py
@@ -635,64 +635,75 @@
     )(incidence, row_gauge.reshape(1, count))
 
 
-def observe_kernel(seen_ref, later_ref, kind_ref, kernels_ref, wide_ref, forward, first, out_ref):
-    spec = spectra(kind_ref[...].astype(F32), kernels_ref[...], wide_ref[...])
-    here, after = jnp.transpose(seen_ref[...]), jnp.transpose(later_ref[...])
-    out_ref[...] = plane_advanced(here, after, spec, forward[...], first[...], 3)
-
-
-def observe(seen, later, gauge_kernel, kernels, wide, mats):
+def label_kernel(seen_ref, gauge_ref, kind_ref, out_ref):
+    rows = seen_ref.shape[0]
+    count = gauge_ref.shape[1]
+    turned = jnp.transpose(seen_ref[...])
+    step = out_ref.shape[0] - 8
+    for i in range(count // rows):
+        out_ref[pl.ds(0, step), pl.ds(i * rows, rows)] = turned[i * step : (i + 1) * step]
+    kinds = jnp.concatenate([kind_ref[...].astype(F32), jnp.zeros((1, count - rows), F32)], axis=1)
+    out_ref[pl.ds(step, 8), :] = jnp.concatenate(
+        [gauge_ref[...].astype(F32), kinds, jnp.zeros((6, count), F32)], axis=0
+    )
+
+
+def label(seen, row_gauge, gauge_kernel):
     rows, hours = seen.shape
-    return pl.pallas_call(
-        observe_kernel,
-        out_shape=jax.ShapeDtypeStruct((hours, rows), F32),
+    count = row_gauge.shape[0]
+    return pl.pallas_call(
+        label_kernel,
+        out_shape=jax.ShapeDtypeStruct((hours * rows // count + 8, count), F32),
         compiler_params=params(),
-        name="observe",
+        name="label",
         cost_estimate=SMALL,
-    )(seen, later, gauge_kernel.reshape(1, rows), kernels, wide, *mats)
-
-
-def send_kernel(inc_ref, field_ref, gauge_ref, kind_ref, out_ref):
+    )(seen, row_gauge.reshape(1, count), gauge_kernel.reshape(1, rows))
+
+
+def send_kernel(inc_hbm, field_hbm, out_ref, inc_ref, field_ref, sems):
     blocks, slots, width = inc_ref.shape
-    count = blocks * slots
-    weights = inc_ref[...].astype(F32).astype(BF16)
-    parts = []
-    for b in range(blocks):
-        value = jnp.concatenate(pieces(field_ref[pl.ds(b * width, width), :], 3)[::-1], axis=0)
-        parts.append(dot(jnp.concatenate([weights[b]] * 3, axis=1), value))
-    out_ref[pl.ds(0, HOURS), :] = jnp.transpose(jnp.concatenate(parts, axis=0))
-    kinds = kind_ref.shape[1] // count
-    here = jnp.minimum(pl.program_id(0), kinds - 1) * count
-    out_ref[pl.ds(HOURS, 8), :] = jnp.concatenate(
-        [
-            gauge_ref[...].astype(F32),
-            kind_ref[:, pl.ds(pl.multiple_of(here, count), count)].astype(F32),
-            jnp.zeros((6, count), F32),
+    chunks = sems.shape[0]
+    step = blocks // chunks
+    copies = []
+    for i in range(chunks):
+        near = pl.ds(i * step, step)
+        far = pl.ds(i * step * width, step * width)
+        copies.append(
+            (
+                pltpu.make_async_copy(inc_hbm.at[near], inc_ref.at[near], sems.at[i, 0]),
+                pltpu.make_async_copy(field_hbm.at[far], field_ref.at[far], sems.at[i, 1]),
+            )
+        )
+        for copy in copies[-1]:
+            copy.start()
+    for i in range(chunks):
+        for copy in copies[i]:
+            copy.wait()
+        parts = []
+        for b in range(i * step, (i + 1) * step):
+            weight = inc_ref[b].astype(F32).astype(BF16)
+            value = jnp.concatenate(pieces(field_ref[pl.ds(b * width, width), :], 3)[::-1], axis=0)
+            parts.append(dot(jnp.concatenate([weight] * 3, axis=1), value))
+        out_ref[:, pl.ds(i * step * slots, step * slots)] = jnp.transpose(jnp.concatenate(parts, axis=0))
+
+
+def send(incidence, field):
+    blocks, slots, width = incidence.shape
+    hours = field.shape[1]
+    chunks = 4
+    return pl.pallas_call(
+        send_kernel,
+        in_specs=[pl.BlockSpec(memory_space=pltpu.HBM)] * 2,
+        out_shape=jax.ShapeDtypeStruct((hours, blocks * slots), F32),
+        scratch_shapes=[
+            pltpu.VMEM(incidence.shape, incidence.dtype),
+            pltpu.VMEM(field.shape, F32),
+            pltpu.SemaphoreType.DMA((chunks, 2)),
         ],
-        axis=0,
-    )
-
-
-def send(incidence, field, row_gauge, gauge_kernel):
-    blocks, slots, width = incidence.shape
-    count = blocks * slots
-    rows = gauge_kernel.shape[0]
-    step = 8
-    return pl.pallas_call(
-        send_kernel,
-        grid=(blocks // step,),
-        in_specs=[
-            pl.BlockSpec((step, slots, width), lambda i: (i, 0, 0)),
-            pl.BlockSpec((step * width, HOURS), lambda i: (i, 0)),
-            pl.BlockSpec((1, step * slots), lambda i: (0, i)),
-            pl.BlockSpec((1, rows), lambda i: (0, 0)),
-        ],
-        out_specs=pl.BlockSpec((HOURS + 8, step * slots), lambda i: (0, i)),
-        out_shape=jax.ShapeDtypeStruct((HOURS + 8, count), F32),
         compiler_params=params(),
         name="send",
         cost_estimate=SMALL,
-    )(incidence, field, row_gauge.reshape(1, count), gauge_kernel.reshape(1, rows))
+    )(incidence, field)
 
 
 def hot_rows(gauge, first, rows):
@@ -700,25 +711,26 @@
     return jnp.where(gauge == mine, 1.0, 0.0).astype(BF16)
 
 
-def spread_kernel(first_ref, mine_ref, other_ref, *out_refs):
+def spread_kernel(first_ref, mine_ref, other_ref, meta_ref, meta_other_ref, *out_refs):
     rows = out_refs[0].shape[1]
-    both = jnp.concatenate([mine_ref[...], other_ref[...]], axis=1)
-    stacked = jnp.concatenate(pieces(both[:HOURS], 3), axis=0)
+    value = jnp.concatenate([mine_ref[...], other_ref[...]], axis=1)
+    gauge = jnp.concatenate([meta_ref[0:1, :], meta_other_ref[0:1, :]], axis=1)
+    stacked = jnp.concatenate(pieces(value, 3), axis=0)
     for m, out_ref in enumerate(out_refs):
-        hot = hot_rows(both[HOURS : HOURS + 1], first_ref[m], rows)
+        hot = hot_rows(gauge, first_ref[m], rows)
         result = lax.dot_general(stacked, hot, (((1,), (1,)), ((), ())), preferred_element_type=F32)
         out_ref[...] = (result[2 * HOURS :] + result[HOURS : 2 * HOURS]) + result[:HOURS]
 
 
-def spread(first, parcels, rows):
+def spread(first, parcels, metas, rows):
     return pl.pallas_call(
         spread_kernel,
-        in_specs=[pl.BlockSpec(memory_space=pltpu.SMEM)] + [pl.BlockSpec(memory_space=pltpu.VMEM)] * 2,
+        in_specs=[pl.BlockSpec(memory_space=pltpu.SMEM)] + [pl.BlockSpec(memory_space=pltpu.VMEM)] * 4,
         out_shape=[jax.ShapeDtypeStruct((HOURS, rows), F32)] * 4,
         compiler_params=params(),
         name="spread",
         cost_estimate=SMALL,
-    )(first, *parcels)
+    )(first, *parcels, *metas)
 
 
 def plane_couple_kernel(last, first_ref, *refs):
@@ -916,13 +928,16 @@
 
 
 def plane_first_kernel(
-    flag_ref, here_ref, pair_ref, middle_ref, seen_ref, spec_ref, kernels_ref, forward, first, last, out_ref
+    flag_ref, here_ref, pair_ref, middle_ref, spec_ref, kernels_ref, forward, first, last, out_ref
 ):
     spec = spec_ref[...]
     before, after = sides(flag_ref[0] > 0.5, pair_ref[...], middle_ref[...])
-    now, later = plane_delayed(before, here_ref[...], after, spec, forward[...], last[...], 3)
-    known = plane_advanced(now, later * flag_ref[1], spec, forward[...], first[...], 3)
-    out_ref[...] = seen_ref[...] - known * gain(kernels_ref[...])
+    here = here_ref[...]
+    both = plane_delayed(before[:HOURS], here[:HOURS], after[:HOURS], spec, forward[...], last[...], 3)
+    scale = gain(kernels_ref[...])
+    now = here[HOURS:] - both[0] * scale
+    later = (after[HOURS:] - both[1] * scale) * flag_ref[1]
+    out_ref[...] = plane_advanced(now, later, spec, forward[...], first[...], 3)
 
 
 def plane_delay_kernel(flag_ref, here_ref, pair_ref, middle_ref, spec_ref, forward, last, out_ref):
@@ -1079,24 +1094,26 @@
     forward3, inverse_first3, inverse_last3, short3 = turned_transforms(3)
     block, noted = (hours, rows), (hours + NOTE, rows)
 
-    parcel = send(incidence, first_guess, row_gauge, gauge_kernel)
+    parcel = send(incidence, first_guess)
     parcel, near, gauges, kinds, seen = lax.optimization_barrier(
         (parcel, incidence, row_gauge, gauge_kernel, observed)
     )
     parcel = moved(parcel, to_plane)
+    behind = moved(label(seen, gauges, kinds), to_plane)
     meta = describe(near, gauges)
     meta = jnp.concatenate([meta, moved(meta, over_x)], axis=1)
     meta = jnp.concatenate([meta, moved(meta, z_pair)], axis=1)
-    seen = observe(seen, moved(seen, hour_before), kinds, kernels, short3, [forward3, inverse_first3])
-    seen = moved(seen, to_plane)
-    parcel, seen = lax.optimization_barrier((parcel, seen))
+    parcel, behind = lax.optimization_barrier((parcel, behind))
+    seen, labels = behind[:-8], behind[-8:]
+    seen = jnp.concatenate([seen[:, i : i + rows] for i in range(0, seen.shape[1], rows)], axis=0)
     parcels = [parcel, moved(parcel, over_core)]
-    spec = plane_spectrum(parcel[hours:], kernels, short3, rows)
-    parcels[1], seen, meta, spec = lax.optimization_barrier((parcels[1], seen, meta, spec))
+    metas = [labels, moved(labels, over_core)]
+    spec = plane_spectrum(labels, kernels, short3, rows)
+    parcels[1], meta, spec = lax.optimization_barrier((parcels[1], meta, spec))
     around = [meta, moved(meta, z_two)]
-    dense = spread(first, parcels, rows)
-    metas = [value[hours:] for value in parcels]
+    dense = spread(first, parcels, metas, rows)
     sums = dense[0] + sum(moved(value, where) for value, where in zip(dense[1:], SQUARE))
+    sums = jnp.concatenate([sums, seen], axis=0)
     sums = [sums, moved(sums, z_pair), moved(sums, z_middle)]
     coupled = plane_couple(first, around[0], rows)
     coupled, sums = lax.optimization_barrier((coupled, sums))
@@ -1106,7 +1123,7 @@
         "plane_first",
         [block],
         [flags],
-        [*sums, seen, spec, kernels, forward3, inverse_first3, inverse_last3],
+        [*sums, spec, kernels, forward3, inverse_first3, inverse_last3],
     )
 
     def mixing(pulled, extra):

time: 146 us -> 152 us (1.041)
  waiting for transfers between devices: 51.5 us -> 57.4 us
  starting transfers between devices: 56.3 us -> 58.3 us
  Pallas kernels: 33.1 us -> 31.4 us
    ppermute x33, waiting for transfers between devices: 43.3 us -> 49.2 us  [moved(): return lax.ppermute(value, ('basin', 'tm'), pairs)]
    ppermute x33, starting transfers between devices: 50.5 us -> 52.4 us  [moved(): return lax.ppermute(value, ('basin', 'tm'), pairs)]
    unnamed x30 -> x34, local copies, waits for them, and re-layouts: 3.95 us -> 3.88 us
  transfers between devices with their start and end apart: 34 -> 34, of which waited for: 20 -> 19; matrix products, arithmetic and copies ran while one was open for 0% -> 0% of each run, Pallas kernels for 15% -> 13%
where the time goes in v14:
time: 152 us
  starting transfers between devices  58.3 us (38%)
  waiting for transfers between devices  57.4 us (38%)
  Pallas kernels  31.4 us (21%)
  local copies, waits for them, and re-layouts  3.98 us (3%)
    ppermute x33, starting transfers between devices, moved(): return lax.ppermute(value, ('basin', 'tm'), pairs)  52.4 us
    ppermute x33, waiting for transfers between devices, moved(): return lax.ppermute(value, ('basin', 'tm'), pairs)  49.2 us
    pallas_call x2, Pallas kernels, plane_couple(): pl.pallas_call(functools.partial(plane_couple_kernel, last), in_specs=[pl...  9.56 us
    pallas_call x6, Pallas kernels, plane_call(): pl.pallas_call(kernel, in_specs=[pl.BlockSpec(memory_space=pltpu.SMEM)] *...  8.88 us
    all_to_all x1, waiting for transfers between devices, plane_shards(): close_note = lax.all_to_all(note, ('basin', 'tm'), 0, 0, tiled=False)  8.18 us
    all_to_all x1, starting transfers between devices, plane_shards(): close_note = lax.all_to_all(note, ('basin', 'tm'), 0, 0, tiled=False)  5.89 us
    pallas_call x3, Pallas kernels, plane_rows(): pl.pallas_call(plane_rows_kernel, in_specs=[pl.BlockSpec(memory_space=plt...  4.51 us
    unnamed x34, local copies, waits for them, and re-layouts  3.88 us
  transfers between devices with their start and end apart: 34, of which 19 were waited for; matrix products, arithmetic and copies ran while one was open for 0% of the time, Pallas kernels for 13%

profile of v14, /device:TPU:1, one launch (start us, length us, event | category | flops | bytes accessed | tf_op | source)
XLA Modules:
  0.0 151.8 jit_solution(4794490736340073313)
XLA Ops:
  0.0 1.6 %copy-done = f32[4096,128]{1,0:T(8,128)S(1)} copy-done((f32[4096,128]{1,0:T(8,128)S(1)}, f32[4096,128]{1,0:T(8,128)}, u32[]{:S(2)}) %copy-start) | copy-done | bytes 2097176
  2.6 1.9 %send.1 = f32[128,512]{1,0:T(8,128)S(1)} custom-call(s32[32,16,128]{2,1,0:T(8,128)S(1)} %copy-done.3, f32[4096,128]{1,0:T(8,128)S(1)} %copy-done), custom_call_target="tpu_custom_call" | custom-call | flops 1 | bytes 1 | tf_op jit(solution)/shard_map/send/pallas_call | solution.py:694
  4.5 4.6 %collective-permute-start = (f32[128,512]{1,0:T(8,128)S(1)}, f32[128,512]{1,0:T(8,128)S(1)}, u32[]{:S(2)}, u32[]{:S(2)}) collective-permute-start(f32[128,512]{1,0:T(8,128)S(1)} %send.1), channel_id=1, source_target_pairs={{0,0},{1,8},{2,16},{3,24},{4,4},{5,12},{6,20},{7,28},{8,2},{9,10},... | collective-permute-start | bytes 786440 | tf_op jit(solution)/shard_map/ppermute | solution.py:503
  10.7 3.6 %collective-permute-start.1 = (f32[72,512]{1,0:T(8,128)S(1)}, f32[72,512]{1,0:T(8,128)S(1)}, u32[]{:S(2)}, u32[]{:S(2)}) collective-permute-start(f32[72,512]{1,0:T(8,128)S(1)} %label.1), channel_id=1, source_target_pairs={{0,0},{1,8},{2,16},{3,24},{4,4},{5,12},{6,20},{7,28},{8,2},{9,10},... | collective-permute-start | bytes 442376 | tf_op jit(solution)/shard_map/ppermute | solution.py:503
  14.4 1.5 collective-permute-start.4
  15.9 12.3 %collective-permute-done.1 = f32[72,512]{1,0:T(8,128)S(1)} collective-permute-done((f32[72,512]{1,0:T(8,128)S(1)}, f32[72,512]{1,0:T(8,128)S(1)}, u32[]{:S(2)}, u32[]{:S(2)}) %collective-permute-start.1) | collective-permute-done | bytes 147488 | tf_op jit(solution)/shard_map/ppermute | solution.py:503
  29.7 1.6 %spread.1 = (f32[128,256]{1,0:T(8,128)S(1)}, f32[128,256]{1,0:T(8,128)S(1)}, f32[128,256]{1,0:T(8,128)S(1)}, f32[128,256]{1,0:T(8,128)S(1)}) custom-call(s32[6]{0:T(128)S(1)} %broadcast_multiply_fusion.first_ref, f32[128,512]{1,0:T(8,128)S(1)} %collective-permute-done.mine_ref, f32[128,512]{1,0:T(8,128)S(1)} %collective-permute-done.2.other_ref, ...), custom_call_target="tpu_custom_call" | custom-call | flops 1 | bytes 1 | tf_op jit(solution)/shard_map/spread/pallas_call | solution.py:726
  34.0 2.3 %collective-permute-done.7 = f32[128,256]{1,0:T(8,128)S(1)} collective-permute-done((f32[128,256]{1,0:T(8,128)S(1)}, f32[128,256]{1,0:T(8,128)S(1)}, u32[]{:S(2)}, u32[]{:S(2)}) %collective-permute-start.7) | collective-permute-done | bytes 131104 | tf_op jit(solution)/shard_map/ppermute | solution.py:503
  36.3 3.7 %collective-permute-done.8 = f32[128,256]{1,0:T(8,128)S(1)} collective-permute-done((f32[128,256]{1,0:T(8,128)S(1)}, f32[128,256]{1,0:T(8,128)S(1)}, u32[]{:S(2)}, u32[]{:S(2)}) %collective-permute-start.8) | collective-permute-done | bytes 131104 | tf_op jit(solution)/shard_map/ppermute | solution.py:503
  40.8 3.6 %collective-permute-start.10 = (f32[256,256]{1,0:T(8,128)S(1)}, f32[256,256]{1,0:T(8,128)S(1)}, u32[]{:S(2)}, u32[]{:S(2)}) collective-permute-start(f32[256,256]{1,0:T(8,128)S(1)} %pad_maximum_fusion.here_ref), channel_id=1, source_target_pairs={{0,8},{1,9},{2,10},{3,11},{4,12},{5,13},{6,14},{7,15},{8,0},{9,1},... | collective-permute-start | bytes 786440 | tf_op jit(solution)/shard_map/ppermute | solution.py:503
  44.5 4.6 %plane_couple.2.refs_1_ = f32[1024,512]{1,0:T(8,128)S(1)} custom-call(s32[6]{0:T(128)S(1)} %broadcast_multiply_fusion.first_ref, f32[24,2048]{1,0:T(8,128)S(1)} %pad_maximum_fusion.1.refs_0_), custom_call_target="tpu_custom_call" | custom-call | flops 2147483648 | bytes 2000000 | tf_op jit(solution)/shard_map/plane_couple/pallas_call | solution.py:792
  49.3 2.6 %plane_first.1.a_ref.pulled_ref.old_z_ref = f32[128,256]{1,0:T(8,128)S(1)} custom-call(f32[3]{0:T(128)S(1)} %add_convert_fusion.flag_ref, f32[256,256]{1,0:T(8,128)S(1)} %pad_maximum_fusion.here_ref, f32[256,256]{1,0:T(8,128)S(1)} %collective-permute-done.10.pair_ref, f32[256,256]{1,0:T(8,128)S(1)} %collective-permute-done.11.middle_ref, ...), custom_call_target="tpu_custom_call" | custom-call | flops 1 | bytes 1 | tf_op jit(solution)/shard_map/plane_first/pallas_call | solution.py:919
  51.9 1.5 %collective-permute-start.14 = (f32[128,256]{1,0:T(8,128)S(1)}, f32[128,256]{1,0:T(8,128)S(1)}, u32[]{:S(2)}, u32[]{:S(2)}) collective-permute-start(f32[128,256]{1,0:T(8,128)S(1)} %plane_first.1.a_ref.pulled_ref.old_z_ref), channel_id=1, source_target_pairs={{0,6},{1,7},{2,4},{3,5},{4,2},{5,3},{6,0},{7,1},{8,14},{9,15},{10,... | collective-permute-start | bytes 393224 | tf_op jit(solution)/shard_map/ppermute | solution.py:503
  54.8 2.7 %collective-permute-done.5.refs_0_ = f32[24,2048]{1,0:T(8,128)S(1)} collective-permute-done((f32[24,2048]{1,0:T(8,128)S(1)}, f32[24,2048]{1,0:T(8,128)S(1)}, u32[]{:S(2)}, u32[]{:S(2)}) %collective-permute-start.5) | collective-permute-done | bytes 196640 | tf_op jit(solution)/shard_map/ppermute | solution.py:503
  57.6 4.9 %plane_couple.3 = (bf16[1024,512]{1,0:T(8,128)(2,1)S(1)}, bf16[1024,512]{1,0:T(8,128)(2,1)S(1)}) custom-call(s32[6]{0:T(128)S(1)} %broadcast_multiply_fusion.first_ref, f32[24,2048]{1,0:T(8,128)S(1)} %collective-permute-done.5.refs_0_, f32[1024,512]{1,0:T(8,128)S(1)} %plane_couple.2.refs_1_), custom_call_target="tpu_custom_call" | custom-call | flops 2147483648 | bytes 2000000 | tf_op jit(solution)/shard_map/plane_couple/pallas_call | solution.py:792
  63.1 2.2 %collective-permute-start.15 = (f32[128,256]{1,0:T(8,128)S(1)}, f32[128,256]{1,0:T(8,128)S(1)}, u32[]{:S(2)}, u32[]{:S(2)}) collective-permute-start(f32[128,256]{1,0:T(8,128)S(1)} %get-tuple-element.65), channel_id=1, source_target_pairs={{0,1},{1,0},{2,3},{3,2},{4,5},{5,4},{6,7},{7,6},{8,9},{9,8},{10,11... | collective-permute-start | bytes 393224 | tf_op jit(solution)/shard_map/ppermute | solution.py:503
  67.0 7.0 %collective-permute-start.16 = (f32[128,256]{1,0:T(8,128)S(1)}, f32[128,256]{1,0:T(8,128)S(1)}, u32[]{:S(2)}, u32[]{:S(2)}) collective-permute-start(f32[128,256]{1,0:T(8,128)S(1)} %add.61.here_ref.old_s_ref), channel_id=1, source_target_pairs={{0,8},{1,9},{2,10},{3,11},{4,12},{5,13},{6,14},{7,15},{8,0},{9,1},... | collective-permute-start | bytes 393224 | tf_op jit(solution)/shard_map/ppermute | solution.py:503
  74.0 3.3 %collective-permute-done.16.pair_ref = f32[128,256]{1,0:T(8,128)S(1)} collective-permute-done((f32[128,256]{1,0:T(8,128)S(1)}, f32[128,256]{1,0:T(8,128)S(1)}, u32[]{:S(2)}, u32[]{:S(2)}) %collective-permute-start.16) | collective-permute-done | bytes 131104 | tf_op jit(solution)/shard_map/ppermute | solution.py:503
  77.2 1.8 %plane_open.1 = (f32[136,256]{1,0:T(8,128)S(1)}, f32[256,256]{1,0:T(8,128)S(1)}) custom-call(f32[3]{0:T(128)S(1)} %add_convert_fusion.flag_ref, f32[128,256]{1,0:T(8,128)S(1)} %add.61.here_ref.old_s_ref, f32[128,256]{1,0:T(8,128)S(1)} %collective-permute-done.16.pair_ref, f32[128,256]{1,0:T(8,128)S(1)} %collective-permute-done.17.middle_ref, ...), custom_call_target="tpu_custom_call" | custom-call | flops 1 | bytes 1 | tf_op jit(solution)/shard_map/plane_open/pallas_call | solution.py:919
  79.1 1.5 collective-permute-start.20
  84.1 4.1 %collective-permute-done.19.c_ref = f32[136,256]{1,0:T(8,128)S(1)} collective-permute-done((f32[136,256]{1,0:T(8,128)S(1)}, f32[136,256]{1,0:T(8,128)S(1)}, u32[]{:S(2)}, u32[]{:S(2)}) %collective-permute-start.19) | collective-permute-done | bytes 139296 | tf_op jit(solution)/shard_map/ppermute | solution.py:503
  92.3 2.8 %collective-permute-start.22 = (f32[136,256]{1,0:T(8,128)S(1)}, f32[136,256]{1,0:T(8,128)S(1)}, u32[]{:S(2)}, u32[]{:S(2)}) collective-permute-start(f32[136,256]{1,0:T(8,128)S(1)} %slice_add_fusion.1.here_ref), channel_id=1, source_target_pairs={{0,8},{1,9},{2,10},{3,11},{4,12},{5,13},{6,14},{7,15},{8,0},{9,1},... | collective-permute-start | bytes 417800 | tf_op jit(solution)/shard_map/ppermute | solution.py:503
  95.0 2.0 %collective-permute-start.24 = (f32[8,256]{1,0:T(8,128)S(1)}, f32[8,256]{1,0:T(8,128)S(1)}, u32[]{:S(2)}, u32[]{:S(2)}) collective-permute-start(f32[8,256]{1,0:T(8,128)S(1)} %slice.29), channel_id=1, source_target_pairs={{0,24},{1,25},{2,26},{3,27},{4,28},{5,29},{6,30},{7,31},{8,16},{9,... | collective-permute-start | bytes 24584 | tf_op jit(solution)/shard_map/ppermute | solution.py:503
  107.3 1.8 %collective-permute-done.27.c_ref = f32[136,256]{1,0:T(8,128)S(1)} collective-permute-done((f32[136,256]{1,0:T(8,128)S(1)}, f32[136,256]{1,0:T(8,128)S(1)}, u32[]{:S(2)}, u32[]{:S(2)}) %collective-permute-start.27) | collective-permute-done | bytes 139296 | tf_op jit(solution)/shard_map/ppermute | solution.py:503
  109.7 3.4 %collective-permute-start.29 = (f32[392,256]{1,0:T(8,128)S(1)}, f32[392,256]{1,0:T(8,128)S(1)}, u32[]{:S(2)}, u32[]{:S(2)}) collective-permute-start(f32[392,256]{1,0:T(8,128)S(1)} %get-tuple-element.76), channel_id=1, source_target_pairs={{0,1},{1,0},{2,3},{3,2},{4,5},{5,4},{6,7},{7,6},{8,9},{9,8},{10,11... | collective-permute-start | bytes 1204232 | tf_op jit(solution)/shard_map/ppermute | solution.py:503
  114.5 2.2 %collective-permute-start.30 = (f32[136,256]{1,0:T(8,128)S(1)}, f32[136,256]{1,0:T(8,128)S(1)}, u32[]{:S(2)}, u32[]{:S(2)}) collective-permute-start(f32[136,256]{1,0:T(8,128)S(1)} %slice_add_fusion.here_ref), channel_id=1, source_target_pairs={{0,8},{1,9},{2,10},{3,11},{4,12},{5,13},{6,14},{7,15},{8,16},{9,17... | collective-permute-start | bytes 417800 | tf_op jit(solution)/shard_map/ppermute | solution.py:503
  116.7 2.0 %plane_rows.5 = (f32[128,512]{1,0:T(8,128)S(1)}, f32[256,256]{1,0:T(8,128)}, f32[256,512]{1,0:T(8,128)S(1)}) custom-call(s32[6]{0:T(128)S(1)} %broadcast_multiply_fusion.first_ref, f32[8,512]{1,0:T(8,128)S(1)} %slice.22.class_ref.meta_ref, f32[8,512]{1,0:T(8,128)S(1)} %collective-permute-done.6.meta_other_ref, ...), custom_call_target="tpu_custom_call" | custom-call | flops 1000000000 | bytes 2000000 | tf_op jit(solution)/shard_map/plane_rows/pallas_call | solution.py:875
  120.7 5.9 %all-to-all-start = ((f32[32,8,128]{2,1,0:T(8,128)}), f32[32,8,128]{2,1,0:T(8,128)S(1)}, u32[]{:S(2)}, u32[]{:S(2)}) async-start(f32[32,8,128]{2,1,0:T(8,128)} %plane_close.1), calls=%async_computation | async-start | bytes 262144 | tf_op jit(solution)/shard_map/all_to_all | solution.py:1170
  126.6 8.2 %all-to-all-done.close_ref = f32[32,8,128]{2,1,0:T(8,128)S(1)} async-done(((f32[32,8,128]{2,1,0:T(8,128)}), f32[32,8,128]{2,1,0:T(8,128)S(1)}, u32[]{:S(2)}, u32[]{:S(2)}) %all-to-all-start) | async-done | bytes 131104 | tf_op jit(solution)/shard_map/all_to_all | solution.py:1170
  136.1 2.6 %collective-permute-start.32 = (f32[512,128]{1,0:T(8,128)S(1)}, f32[512,128]{1,0:T(8,128)S(1)}, u32[]{:S(2)}, u32[]{:S(2)}) collective-permute-start(f32[512,128]{1,0:T(8,128)S(1)} %plane_combine.1), channel_id=1, source_target_pairs={{0,0},{1,16},{2,8},{3,24},{4,4},{5,20},{6,12},{7,28},{8,1},{9,17},... | collective-permute-start | bytes 786440 | tf_op jit(solution)/shard_map/ppermute | solution.py:503
  138.7 10.7 %collective-permute-done.32.rows_ref = f32[512,128]{1,0:T(8,128)S(1)} collective-permute-done((f32[512,128]{1,0:T(8,128)S(1)}, f32[512,128]{1,0:T(8,128)S(1)}, u32[]{:S(2)}, u32[]{:S(2)}) %collective-permute-start.32) | collective-permute-done | bytes 262176 | tf_op jit(solution)/shard_map/ppermute | solution.py:503
  149.4 2.4 %plane_finish.1 = f32[4096,128]{1,0:T(8,128)} custom-call(f32[512,128]{1,0:T(8,128)S(1)} %collective-permute-done.32.rows_ref, s32[32,16,128]{2,1,0:T(8,128)S(1)} %copy-done.4, f32[4096,128]{1,0:T(8,128)S(1)} %copy-done.1), custom_call_target="tpu_custom_call" | custom-call | tf_op jit(solution)/shard_map/plane_finish/pallas_call | solution.py:1070
  (103 shorter events, 34.6 us)
Async XLA Ops:
  4.5 23.7 %collective-permute-start = (f32[128,512]{1,0:T(8,128)S(1)}, f32[128,512]{1,0:T(8,128)S(1)}, u32[]{:S(2)}, u32[]{:S(2)}) collective-permute-start(f32[128,512]{1,0:T(8,128)S(1)} %send.1), channel_id=1, source_target_pairs={{0,0},{1,8},{2,16},{3,24},{4,4},{5,12},{6,20},{7,28},{8,2},{9,10},... | collective-permute-start | bytes 786440 | tf_op jit(solution)/shard_map/ppermute | solution.py:503
  9.3 5.1 %collective-permute-start.3 = (f32[24,512]{1,0:T(8,128)S(1)}, f32[24,512]{1,0:T(8,128)S(1)}, u32[]{:S(2)}, u32[]{:S(2)}) collective-permute-start(f32[24,512]{1,0:T(8,128)S(1)} %describe.1), channel_id=1, source_target_pairs={{0,4},{1,5},{2,6},{3,7},{4,0},{5,1},{6,2},{7,3},{8,12},{9,13},{10,... | collective-permute-start | bytes 147464 | tf_op jit(solution)/shard_map/ppermute | solution.py:503
  10.7 17.5 %collective-permute-start.1 = (f32[72,512]{1,0:T(8,128)S(1)}, f32[72,512]{1,0:T(8,128)S(1)}, u32[]{:S(2)}, u32[]{:S(2)}) collective-permute-start(f32[72,512]{1,0:T(8,128)S(1)} %label.1), channel_id=1, source_target_pairs={{0,0},{1,8},{2,16},{3,24},{4,4},{5,12},{6,20},{7,28},{8,2},{9,10},... | collective-permute-start | bytes 442376 | tf_op jit(solution)/shard_map/ppermute | solution.py:503
  14.4 14.3 %collective-permute-start.4 = (f32[24,1024]{1,0:T(8,128)S(1)}, f32[24,1024]{1,0:T(8,128)S(1)}, u32[]{:S(2)}, u32[]{:S(2)}) collective-permute-start(f32[24,1024]{1,0:T(8,128)S(1)} %pad_maximum_fusion.2), channel_id=1, source_target_pairs={{0,8},{1,9},{2,10},{3,11},{4,12},{5,13},{6,14},{7,15},{8,0},{9,1},... | collective-permute-start | bytes 294920 | tf_op jit(solution)/shard_map/ppermute | solution.py:503
  31.3 5.0 %collective-permute-start.7 = (f32[128,256]{1,0:T(8,128)S(1)}, f32[128,256]{1,0:T(8,128)S(1)}, u32[]{:S(2)}, u32[]{:S(2)}) collective-permute-start(f32[128,256]{1,0:T(8,128)S(1)} %get-tuple-element.54), channel_id=1, source_target_pairs={{0,4},{1,5},{2,6},{3,7},{4,0},{5,1},{6,2},{7,3},{8,12},{9,13},{10,... | collective-permute-start | bytes 393224 | tf_op jit(solution)/shard_map/ppermute | solution.py:503
  32.6 7.4 %collective-permute-start.8 = (f32[128,256]{1,0:T(8,128)S(1)}, f32[128,256]{1,0:T(8,128)S(1)}, u32[]{:S(2)}, u32[]{:S(2)}) collective-permute-start(f32[128,256]{1,0:T(8,128)S(1)} %get-tuple-element.55), channel_id=1, source_target_pairs={{0,2},{1,3},{2,0},{3,1},{4,6},{5,7},{6,4},{7,5},{8,10},{9,11},{10,... | collective-permute-start | bytes 393224 | tf_op jit(solution)/shard_map/ppermute | solution.py:503
  32.6 7.4 %collective-permute-start.9 = (f32[128,256]{1,0:T(8,128)S(1)}, f32[128,256]{1,0:T(8,128)S(1)}, u32[]{:S(2)}, u32[]{:S(2)}) collective-permute-start(f32[128,256]{1,0:T(8,128)S(1)} %get-tuple-element.56), channel_id=1, source_target_pairs={{0,6},{1,7},{2,4},{3,5},{4,2},{5,3},{6,0},{7,1},{8,14},{9,15},{10,... | collective-permute-start | bytes 393224 | tf_op jit(solution)/shard_map/ppermute | solution.py:503
  40.1 9.1 %collective-permute-start.11 = (f32[256,256]{1,0:T(8,128)S(1)}, f32[256,256]{1,0:T(8,128)S(1)}, u32[]{:S(2)}, u32[]{:S(2)}) collective-permute-start(f32[256,256]{1,0:T(8,128)S(1)} %pad_maximum_fusion.here_ref), channel_id=1, source_target_pairs={{8,16},{9,17},{10,18},{11,19},{12,20},{13,21},{14,22},{15,23},{16,... | collective-permute-start | bytes 786440 | tf_op jit(solution)/shard_map/ppermute | solution.py:503
  40.8 8.5 %collective-permute-start.10 = (f32[256,256]{1,0:T(8,128)S(1)}, f32[256,256]{1,0:T(8,128)S(1)}, u32[]{:S(2)}, u32[]{:S(2)}) collective-permute-start(f32[256,256]{1,0:T(8,128)S(1)} %pad_maximum_fusion.here_ref), channel_id=1, source_target_pairs={{0,8},{1,9},{2,10},{3,11},{4,12},{5,13},{6,14},{7,15},{8,0},{9,1},... | collective-permute-start | bytes 786440 | tf_op jit(solution)/shard_map/ppermute | solution.py:503
  44.4 13.1 %collective-permute-start.5 = (f32[24,2048]{1,0:T(8,128)S(1)}, f32[24,2048]{1,0:T(8,128)S(1)}, u32[]{:S(2)}, u32[]{:S(2)}) collective-permute-start(f32[24,2048]{1,0:T(8,128)S(1)} %pad_maximum_fusion.1.refs_0_), channel_id=1, source_target_pairs={{0,16},{1,17},{2,18},{3,19},{4,20},{5,21},{6,22},{7,23},{8,24},{9,... | collective-permute-start | bytes 589832 | tf_op jit(solution)/shard_map/ppermute | solution.py:503
  51.9 10.6 %collective-permute-start.14 = (f32[128,256]{1,0:T(8,128)S(1)}, f32[128,256]{1,0:T(8,128)S(1)}, u32[]{:S(2)}, u32[]{:S(2)}) collective-permute-start(f32[128,256]{1,0:T(8,128)S(1)} %plane_first.1.a_ref.pulled_ref.old_z_ref), channel_id=1, source_target_pairs={{0,6},{1,7},{2,4},{3,5},{4,2},{5,3},{6,0},{7,1},{8,14},{9,15},{10,... | collective-permute-start | bytes 393224 | tf_op jit(solution)/shard_map/ppermute | solution.py:503
  53.4 9.1 %collective-permute-start.13 = (f32[128,256]{1,0:T(8,128)S(1)}, f32[128,256]{1,0:T(8,128)S(1)}, u32[]{:S(2)}, u32[]{:S(2)}) collective-permute-start(f32[128,256]{1,0:T(8,128)S(1)} %plane_first.1.a_ref.pulled_ref.old_z_ref), channel_id=1, source_target_pairs={{0,2},{1,3},{2,0},{3,1},{4,6},{5,7},{6,4},{7,5},{8,10},{9,11},{10,... | collective-permute-start | bytes 393224 | tf_op jit(solution)/shard_map/ppermute | solution.py:503
  54.8 7.7 %collective-permute-start.12 = (f32[128,256]{1,0:T(8,128)S(1)}, f32[128,256]{1,0:T(8,128)S(1)}, u32[]{:S(2)}, u32[]{:S(2)}) collective-permute-start(f32[128,256]{1,0:T(8,128)S(1)} %plane_first.1.a_ref.pulled_ref.old_z_ref), channel_id=1, source_target_pairs={{0,4},{1,5},{2,6},{3,7},{4,0},{5,1},{6,2},{7,3},{8,12},{9,13},{10,... | collective-permute-start | bytes 393224 | tf_op jit(solution)/shard_map/ppermute | solution.py:503
  63.1 3.2 %collective-permute-start.15 = (f32[128,256]{1,0:T(8,128)S(1)}, f32[128,256]{1,0:T(8,128)S(1)}, u32[]{:S(2)}, u32[]{:S(2)}) collective-permute-start(f32[128,256]{1,0:T(8,128)S(1)} %get-tuple-element.65), channel_id=1, source_target_pairs={{0,1},{1,0},{2,3},{3,2},{4,5},{5,4},{6,7},{7,6},{8,9},{9,8},{10,11... | collective-permute-start | bytes 393224 | tf_op jit(solution)/shard_map/ppermute | solution.py:503
  66.3 7.6 %collective-permute-start.17 = (f32[128,256]{1,0:T(8,128)S(1)}, f32[128,256]{1,0:T(8,128)S(1)}, u32[]{:S(2)}, u32[]{:S(2)}) collective-permute-start(f32[128,256]{1,0:T(8,128)S(1)} %add.61.here_ref.old_s_ref), channel_id=1, source_target_pairs={{8,16},{9,17},{10,18},{11,19},{12,20},{13,21},{14,22},{15,23},{16,... | collective-permute-start | bytes 393224 | tf_op jit(solution)/shard_map/ppermute | solution.py:503
  67.0 10.2 %collective-permute-start.16 = (f32[128,256]{1,0:T(8,128)S(1)}, f32[128,256]{1,0:T(8,128)S(1)}, u32[]{:S(2)}, u32[]{:S(2)}) collective-permute-start(f32[128,256]{1,0:T(8,128)S(1)} %add.61.here_ref.old_s_ref), channel_id=1, source_target_pairs={{0,8},{1,9},{2,10},{3,11},{4,12},{5,13},{6,14},{7,15},{8,0},{9,1},... | collective-permute-start | bytes 393224 | tf_op jit(solution)/shard_map/ppermute | solution.py:503
  79.1 5.0 %collective-permute-start.20 = (f32[136,256]{1,0:T(8,128)S(1)}, f32[136,256]{1,0:T(8,128)S(1)}, u32[]{:S(2)}, u32[]{:S(2)}) collective-permute-start(f32[136,256]{1,0:T(8,128)S(1)} %get-tuple-element.66.a_ref.pulled_ref), channel_id=1, source_target_pairs={{0,6},{1,7},{2,4},{3,5},{4,2},{5,3},{6,0},{7,1},{8,14},{9,15},{10,... | collective-permute-start | bytes 417800 | tf_op jit(solution)/shard_map/ppermute | solution.py:503
  80.6 7.5 %collective-permute-start.19 = (f32[136,256]{1,0:T(8,128)S(1)}, f32[136,256]{1,0:T(8,128)S(1)}, u32[]{:S(2)}, u32[]{:S(2)}) collective-permute-start(f32[136,256]{1,0:T(8,128)S(1)} %get-tuple-element.66.a_ref.pulled_ref), channel_id=1, source_target_pairs={{0,2},{1,3},{2,0},{3,1},{4,6},{5,7},{6,4},{7,5},{8,10},{9,11},{10,... | collective-permute-start | bytes 417800 | tf_op jit(solution)/shard_map/ppermute | solution.py:503
  81.5 6.6 %collective-permute-start.18 = (f32[136,256]{1,0:T(8,128)S(1)}, f32[136,256]{1,0:T(8,128)S(1)}, u32[]{:S(2)}, u32[]{:S(2)}) collective-permute-start(f32[136,256]{1,0:T(8,128)S(1)} %get-tuple-element.66.a_ref.pulled_ref), channel_id=1, source_target_pairs={{0,4},{1,5},{2,6},{3,7},{4,0},{5,1},{6,2},{7,3},{8,12},{9,13},{10,... | collective-permute-start | bytes 417800 | tf_op jit(solution)/shard_map/ppermute | solution.py:503
  88.7 2.7 %collective-permute-start.21 = (f32[392,256]{1,0:T(8,128)S(1)}, f32[392,256]{1,0:T(8,128)S(1)}, u32[]{:S(2)}, u32[]{:S(2)}) collective-permute-start(f32[392,256]{1,0:T(8,128)S(1)} %get-tuple-element.69), channel_id=1, source_target_pairs={{0,1},{1,0},{2,3},{3,2},{4,5},{5,4},{6,7},{7,6},{8,9},{9,8},{10,11... | collective-permute-start | bytes 1204232 | tf_op jit(solution)/shard_map/ppermute | solution.py:503
  91.4 5.7 %collective-permute-start.25 = (f32[136,256]{1,0:T(8,128)S(1)}, f32[136,256]{1,0:T(8,128)S(1)}, u32[]{:S(2)}, u32[]{:S(2)}) collective-permute-start(f32[136,256]{1,0:T(8,128)S(1)} %slice_add_fusion.1.here_ref), channel_id=1, source_target_pairs={{8,16},{9,17},{10,18},{11,19},{12,20},{13,21},{14,22},{15,23},{16,... | collective-permute-start | bytes 417800 | tf_op jit(solution)/shard_map/ppermute | solution.py:503
  92.3 6.2 %collective-permute-start.22 = (f32[136,256]{1,0:T(8,128)S(1)}, f32[136,256]{1,0:T(8,128)S(1)}, u32[]{:S(2)}, u32[]{:S(2)}) collective-permute-start(f32[136,256]{1,0:T(8,128)S(1)} %slice_add_fusion.1.here_ref), channel_id=1, source_target_pairs={{0,8},{1,9},{2,10},{3,11},{4,12},{5,13},{6,14},{7,15},{8,0},{9,1},... | collective-permute-start | bytes 417800 | tf_op jit(solution)/shard_map/ppermute | solution.py:503
  95.0 5.0 %collective-permute-start.24 = (f32[8,256]{1,0:T(8,128)S(1)}, f32[8,256]{1,0:T(8,128)S(1)}, u32[]{:S(2)}, u32[]{:S(2)}) collective-permute-start(f32[8,256]{1,0:T(8,128)S(1)} %slice.29), channel_id=1, source_target_pairs={{0,24},{1,25},{2,26},{3,27},{4,28},{5,29},{6,30},{7,31},{8,16},{9,... | collective-permute-start | bytes 24584 | tf_op jit(solution)/shard_map/ppermute | solution.py:503
  97.1 3.4 %collective-permute-start.23 = (f32[8,256]{1,0:T(8,128)S(1)}, f32[8,256]{1,0:T(8,128)S(1)}, u32[]{:S(2)}, u32[]{:S(2)}) collective-permute-start(f32[8,256]{1,0:T(8,128)S(1)} %slice.29), channel_id=1, source_target_pairs={{0,16},{1,17},{2,18},{3,19},{4,20},{5,21},{6,22},{7,23},{8,24},{9,... | collective-permute-start | bytes 24584 | tf_op jit(solution)/shard_map/ppermute | solution.py:503
  102.4 4.9 %collective-permute-start.28 = (f32[136,256]{1,0:T(8,128)S(1)}, f32[136,256]{1,0:T(8,128)S(1)}, u32[]{:S(2)}, u32[]{:S(2)}) collective-permute-start(f32[136,256]{1,0:T(8,128)S(1)} %get-tuple-element.72.a_ref.pulled_ref), channel_id=1, source_target_pairs={{0,6},{1,7},{2,4},{3,5},{4,2},{5,3},{6,0},{7,1},{8,14},{9,15},{10,... | collective-permute-start | bytes 417800 | tf_op jit(solution)/shard_map/ppermute | solution.py:503
  103.6 5.5 %collective-permute-start.27 = (f32[136,256]{1,0:T(8,128)S(1)}, f32[136,256]{1,0:T(8,128)S(1)}, u32[]{:S(2)}, u32[]{:S(2)}) collective-permute-start(f32[136,256]{1,0:T(8,128)S(1)} %get-tuple-element.72.a_ref.pulled_ref), channel_id=1, source_target_pairs={{0,2},{1,3},{2,0},{3,1},{4,6},{5,7},{6,4},{7,5},{8,10},{9,11},{10,... | collective-permute-start | bytes 417800 | tf_op jit(solution)/shard_map/ppermute | solution.py:503
  104.5 4.6 %collective-permute-start.26 = (f32[136,256]{1,0:T(8,128)S(1)}, f32[136,256]{1,0:T(8,128)S(1)}, u32[]{:S(2)}, u32[]{:S(2)}) collective-permute-start(f32[136,256]{1,0:T(8,128)S(1)} %get-tuple-element.72.a_ref.pulled_ref), channel_id=1, source_target_pairs={{0,4},{1,5},{2,6},{3,7},{4,0},{5,1},{6,2},{7,3},{8,12},{9,13},{10,... | collective-permute-start | bytes 417800 | tf_op jit(solution)/shard_map/ppermute | solution.py:503
  109.7 4.8 %collective-permute-start.29 = (f32[392,256]{1,0:T(8,128)S(1)}, f32[392,256]{1,0:T(8,128)S(1)}, u32[]{:S(2)}, u32[]{:S(2)}) collective-permute-start(f32[392,256]{1,0:T(8,128)S(1)} %get-tuple-element.76), channel_id=1, source_target_pairs={{0,1},{1,0},{2,3},{3,2},{4,5},{5,4},{6,7},{7,6},{8,9},{9,8},{10,11... | collective-permute-start | bytes 1204232 | tf_op jit(solution)/shard_map/ppermute | solution.py:503
  114.5 4.9 %collective-permute-start.30 = (f32[136,256]{1,0:T(8,128)S(1)}, f32[136,256]{1,0:T(8,128)S(1)}, u32[]{:S(2)}, u32[]{:S(2)}) collective-permute-start(f32[136,256]{1,0:T(8,128)S(1)} %slice_add_fusion.here_ref), channel_id=1, source_target_pairs={{0,8},{1,9},{2,10},{3,11},{4,12},{5,13},{6,14},{7,15},{8,16},{9,17... | collective-permute-start | bytes 417800 | tf_op jit(solution)/shard_map/ppermute | solution.py:503
  118.7 7.9 %collective-permute-start.31 = (f32[256,256]{1,0:T(8,128)}, f32[256,256]{1,0:T(8,128)S(1)}, u32[]{:S(2)}, u32[]{:S(2)}) collective-permute-start(f32[256,256]{1,0:T(8,128)} %get-tuple-element.82), channel_id=1, source_target_pairs={{0,1},{1,0},{2,3},{3,2},{4,5},{5,4},{6,7},{7,6},{8,9},{9,8},{10,11... | collective-permute-start | bytes 786440 | tf_op jit(solution)/shard_map/ppermute | solution.py:503
  120.7 14.1 %all-to-all-start = ((f32[32,8,128]{2,1,0:T(8,128)}), f32[32,8,128]{2,1,0:T(8,128)S(1)}, u32[]{:S(2)}, u32[]{:S(2)}) async-start(f32[32,8,128]{2,1,0:T(8,128)} %plane_close.1), calls=%async_computation | async-start | bytes 262144 | tf_op jit(solution)/shard_map/all_to_all | solution.py:1170
  136.1 13.3 %collective-permute-start.32 = (f32[512,128]{1,0:T(8,128)S(1)}, f32[512,128]{1,0:T(8,128)S(1)}, u32[]{:S(2)}, u32[]{:S(2)}) collective-permute-start(f32[512,128]{1,0:T(8,128)S(1)} %plane_combine.1), channel_id=1, source_target_pairs={{0,0},{1,16},{2,8},{3,24},{4,4},{5,20},{6,12},{7,28},{8,1},{9,17},... | collective-permute-start | bytes 786440 | tf_op jit(solution)/shard_map/ppermute | solution.py:503
  (19 other events, 202.0 us)

commit v15 on v14

--- a/solution.py
+++ b/solution.py
@@ -635,29 +635,32 @@
     )(incidence, row_gauge.reshape(1, count))
 
 
-def label_kernel(seen_ref, gauge_ref, kind_ref, out_ref):
+def observe_kernel(seen_ref, later_ref, gauge_ref, kind_ref, kernels_ref, wide_ref, forward, first, out_ref):
     rows = seen_ref.shape[0]
     count = gauge_ref.shape[1]
-    turned = jnp.transpose(seen_ref[...])
+    kind = kind_ref[...].astype(F32)
+    spec = spectra(kind, kernels_ref[...], wide_ref[...])
+    here, after = jnp.transpose(seen_ref[...]), jnp.transpose(later_ref[...])
+    pulled = plane_advanced(here, after, spec, forward[...], first[...], 3)
     step = out_ref.shape[0] - 8
     for i in range(count // rows):
-        out_ref[pl.ds(0, step), pl.ds(i * rows, rows)] = turned[i * step : (i + 1) * step]
-    kinds = jnp.concatenate([kind_ref[...].astype(F32), jnp.zeros((1, count - rows), F32)], axis=1)
+        out_ref[pl.ds(0, step), pl.ds(i * rows, rows)] = pulled[i * step : (i + 1) * step]
+    kinds = jnp.concatenate([kind, jnp.zeros((1, count - rows), F32)], axis=1)
     out_ref[pl.ds(step, 8), :] = jnp.concatenate(
         [gauge_ref[...].astype(F32), kinds, jnp.zeros((6, count), F32)], axis=0
     )
 
 
-def label(seen, row_gauge, gauge_kernel):
+def observe(seen, later, row_gauge, gauge_kernel, kernels, wide, mats):
     rows, hours = seen.shape
     count = row_gauge.shape[0]
     return pl.pallas_call(
-        label_kernel,
+        observe_kernel,
         out_shape=jax.ShapeDtypeStruct((hours * rows // count + 8, count), F32),
         compiler_params=params(),
-        name="label",
+        name="observe",
         cost_estimate=SMALL,
-    )(seen, row_gauge.reshape(1, count), gauge_kernel.reshape(1, rows))
+    )(seen, later, row_gauge.reshape(1, count), gauge_kernel.reshape(1, rows), kernels, wide, *mats)
 
 
 def send_kernel(inc_hbm, field_hbm, out_ref, inc_ref, field_ref, sems):
@@ -700,7 +703,7 @@
             pltpu.VMEM(field.shape, F32),
             pltpu.SemaphoreType.DMA((chunks, 2)),
         ],
-        compiler_params=params(),
+        compiler_params=params(60),
         name="send",
         cost_estimate=SMALL,
     )(incidence, field)
@@ -928,16 +931,13 @@
 
 
 def plane_first_kernel(
-    flag_ref, here_ref, pair_ref, middle_ref, spec_ref, kernels_ref, forward, first, last, out_ref
+    flag_ref, here_ref, pair_ref, middle_ref, seen_ref, spec_ref, kernels_ref, forward, first, last, out_ref
 ):
     spec = spec_ref[...]
     before, after = sides(flag_ref[0] > 0.5, pair_ref[...], middle_ref[...])
-    here = here_ref[...]
-    both = plane_delayed(before[:HOURS], here[:HOURS], after[:HOURS], spec, forward[...], last[...], 3)
-    scale = gain(kernels_ref[...])
-    now = here[HOURS:] - both[0] * scale
-    later = (after[HOURS:] - both[1] * scale) * flag_ref[1]
-    out_ref[...] = plane_advanced(now, later, spec, forward[...], first[...], 3)
+    now, later = plane_delayed(before, here_ref[...], after, spec, forward[...], last[...], 3)
+    known = plane_advanced(now, later * flag_ref[1], spec, forward[...], first[...], 3)
+    out_ref[...] = seen_ref[...] - known * gain(kernels_ref[...])
 
 
 def plane_delay_kernel(flag_ref, here_ref, pair_ref, middle_ref, spec_ref, forward, last, out_ref):
@@ -1099,10 +1099,13 @@
         (parcel, incidence, row_gauge, gauge_kernel, observed)
     )
     parcel = moved(parcel, to_plane)
-    behind = moved(label(seen, gauges, kinds), to_plane)
     meta = describe(near, gauges)
     meta = jnp.concatenate([meta, moved(meta, over_x)], axis=1)
     meta = jnp.concatenate([meta, moved(meta, z_pair)], axis=1)
+    behind = observe(
+        seen, moved(seen, hour_before), gauges, kinds, kernels, short3, [forward3, inverse_first3]
+    )
+    behind = moved(behind, to_plane)
     parcel, behind = lax.optimization_barrier((parcel, behind))
     seen, labels = behind[:-8], behind[-8:]
     seen = jnp.concatenate([seen[:, i : i + rows] for i in range(0, seen.shape[1], rows)], axis=0)
@@ -1113,7 +1116,6 @@
     around = [meta, moved(meta, z_two)]
     dense = spread(first, parcels, metas, rows)
     sums = dense[0] + sum(moved(value, where) for value, where in zip(dense[1:], SQUARE))
-    sums = jnp.concatenate([sums, seen], axis=0)
     sums = [sums, moved(sums, z_pair), moved(sums, z_middle)]
     coupled = plane_couple(first, around[0], rows)
     coupled, sums = lax.optimization_barrier((coupled, sums))
@@ -1123,7 +1125,7 @@
         "plane_first",
         [block],
         [flags],
-        [*sums, spec, kernels, forward3, inverse_first3, inverse_last3],
+        [*sums, seen, spec, kernels, forward3, inverse_first3, inverse_last3],
     )
 
     def mixing(pulled, extra):

time: 152 us -> 148 us (0.974)
  waiting for transfers between devices: 57.4 us -> 52.9 us
  Pallas kernels: 31.4 us -> 34 us
  local copies, waits for them, and re-layouts: 3.98 us -> 1.44 us
    ppermute x33 -> x34, waiting for transfers between devices: 49.2 us -> 44.8 us  [moved(): return lax.ppermute(value, ('basin', 'tm'), pairs)]
    unnamed x34 -> x30, local copies, waits for them, and re-layouts: 3.88 us -> 1.34 us
    ppermute x33 -> x34, starting transfers between devices: 52.4 us -> 53 us  [moved(): return lax.ppermute(value, ('basin', 'tm'), pairs)]
  transfers between devices with their start and end apart: 34 -> 35, of which waited for: 19 -> 19; matrix products, arithmetic and copies ran while one was open for 0% -> 0% of each run, Pallas kernels for 13% -> 14%
where the time goes in v15:
time: 148 us
  starting transfers between devices  58.5 us (40%)
  waiting for transfers between devices  52.9 us (36%)
  Pallas kernels  34 us (23%)
    ppermute x34, starting transfers between devices, moved(): return lax.ppermute(value, ('basin', 'tm'), pairs)  53 us
    ppermute x34, waiting for transfers between devices, moved(): return lax.ppermute(value, ('basin', 'tm'), pairs)  44.8 us
    pallas_call x2, Pallas kernels, plane_couple(): pl.pallas_call(functools.partial(plane_couple_kernel, last), in_specs=[pl...  9.56 us
    pallas_call x6, Pallas kernels, plane_call(): pl.pallas_call(kernel, in_specs=[pl.BlockSpec(memory_space=pltpu.SMEM)] *...  8.85 us
    all_to_all x1, waiting for transfers between devices, plane_shards(): close_note = lax.all_to_all(note, ('basin', 'tm'), 0, 0, tiled=False)  8.18 us
    all_to_all x1, starting transfers between devices, plane_shards(): close_note = lax.all_to_all(note, ('basin', 'tm'), 0, 0, tiled=False)  5.51 us
    pallas_call x3, Pallas kernels, plane_rows(): pl.pallas_call(plane_rows_kernel, in_specs=[pl.BlockSpec(memory_space=plt...  4.5 us
    pallas_call x1, Pallas kernels, send(): pl.pallas_call(send_kernel, in_specs=[pl.BlockSpec(memory_space=pltpu.HBM...  3.32 us
  transfers between devices with their start and end apart: 35, of which 19 were waited for; matrix products, arithmetic and copies ran while one was open for 0% of the time, Pallas kernels for 14%

profile of v15, /device:TPU:1, one launch (start us, length us, event | category | flops | bytes accessed | tf_op | source)
XLA Modules:
  0.0 147.7 jit_solution(16459305700119995361)
XLA Ops:
  0.1 3.3 %send.1 = f32[128,512]{1,0:T(8,128)} custom-call(s32[32,16,128]{2,1,0:T(8,128)} %inc_ref.2, f32[4096,128]{1,0:T(8,128)} %field_ref.1), custom_call_target="tpu_custom_call" | custom-call | flops 1 | bytes 1 | tf_op jit(solution)/shard_map/send/pallas_call | solution.py:697
  3.4 2.0 %collective-permute-start.1 = (f32[256,128]{1,0:T(8,128)S(1)}, f32[256,128]{1,0:T(8,128)S(1)}, u32[]{:S(2)}, u32[]{:S(2)}) collective-permute-start(f32[256,128]{1,0:T(8,128)S(1)} %copy-done.10), channel_id=1, source_target_pairs={{1,0},{2,1},{3,2},{5,4},{6,5},{7,6},{9,8},{10,9},{11,10},{13,12},{... | collective-permute-start | bytes 393224 | tf_op jit(solution)/shard_map/ppermute | solution.py:503
  5.6 2.7 %collective-permute-start.4 = (f32[24,512]{1,0:T(8,128)S(1)}, f32[24,512]{1,0:T(8,128)S(1)}, u32[]{:S(2)}, u32[]{:S(2)}) collective-permute-start(f32[24,512]{1,0:T(8,128)S(1)} %describe.1), channel_id=1, source_target_pairs={{0,4},{1,5},{2,6},{3,7},{4,0},{5,1},{6,2},{7,3},{8,12},{9,13},{10,... | collective-permute-start | bytes 147464 | tf_op jit(solution)/shard_map/ppermute | solution.py:503
  8.3 2.7 %collective-permute-start = (f32[128,512]{1,0:T(8,128)}, f32[128,512]{1,0:T(8,128)S(1)}, u32[]{:S(2)}, u32[]{:S(2)}) collective-permute-start(f32[128,512]{1,0:T(8,128)} %send.1), channel_id=1, source_target_pairs={{0,0},{1,8},{2,16},{3,24},{4,4},{5,12},{6,20},{7,28},{8,2},{9,10},... | collective-permute-start | bytes 786440 | tf_op jit(solution)/shard_map/ppermute | solution.py:503
  12.5 3.9 %collective-permute-start.2 = (f32[72,512]{1,0:T(8,128)S(1)}, f32[72,512]{1,0:T(8,128)S(1)}, u32[]{:S(2)}, u32[]{:S(2)}) collective-permute-start(f32[72,512]{1,0:T(8,128)S(1)} %observe.1), channel_id=1, source_target_pairs={{0,0},{1,8},{2,16},{3,24},{4,4},{5,12},{6,20},{7,28},{8,2},{9,10},... | collective-permute-start | bytes 442376 | tf_op jit(solution)/shard_map/ppermute | solution.py:503
  18.0 10.6 %collective-permute-done.mine_ref = f32[128,512]{1,0:T(8,128)S(1)} collective-permute-done((f32[128,512]{1,0:T(8,128)}, f32[128,512]{1,0:T(8,128)S(1)}, u32[]{:S(2)}, u32[]{:S(2)}) %collective-permute-start) | collective-permute-done | bytes 262176 | tf_op jit(solution)/shard_map/ppermute | solution.py:503
  28.6 2.8 %collective-permute-done.2 = f32[72,512]{1,0:T(8,128)S(1)} collective-permute-done((f32[72,512]{1,0:T(8,128)S(1)}, f32[72,512]{1,0:T(8,128)S(1)}, u32[]{:S(2)}, u32[]{:S(2)}) %collective-permute-start.2) | collective-permute-done | bytes 147488 | tf_op jit(solution)/shard_map/ppermute | solution.py:503
  33.0 1.6 %spread.1 = (f32[128,256]{1,0:T(8,128)S(1)}, f32[128,256]{1,0:T(8,128)S(1)}, f32[128,256]{1,0:T(8,128)S(1)}, f32[128,256]{1,0:T(8,128)S(1)}) custom-call(s32[6]{0:T(128)S(1)} %broadcast_multiply_fusion.first_ref, f32[128,512]{1,0:T(8,128)S(1)} %collective-permute-done.mine_ref, f32[128,512]{1,0:T(8,128)S(1)} %collective-permute-done.3.other_ref, ...), custom_call_target="tpu_custom_call" | custom-call | flops 1 | bytes 1 | tf_op jit(solution)/shard_map/spread/pallas_call | solution.py:729
  34.9 2.4 %collective-permute-start.10 = (f32[128,256]{1,0:T(8,128)S(1)}, f32[128,256]{1,0:T(8,128)S(1)}, u32[]{:S(2)}, u32[]{:S(2)}) collective-permute-start(f32[128,256]{1,0:T(8,128)S(1)} %get-tuple-element.56), channel_id=1, source_target_pairs={{0,6},{1,7},{2,4},{3,5},{4,2},{5,3},{6,0},{7,1},{8,14},{9,15},{10,... | collective-permute-start | bytes 393224 | tf_op jit(solution)/shard_map/ppermute | solution.py:503
  37.3 2.0 %collective-permute-start.6 = (f32[24,2048]{1,0:T(8,128)S(1)}, f32[24,2048]{1,0:T(8,128)S(1)}, u32[]{:S(2)}, u32[]{:S(2)}) collective-permute-start(f32[24,2048]{1,0:T(8,128)S(1)} %pad_maximum_fusion.refs_0_), channel_id=1, source_target_pairs={{0,16},{1,17},{2,18},{3,19},{4,20},{5,21},{6,22},{7,23},{8,24},{9,... | collective-permute-start | bytes 589832 | tf_op jit(solution)/shard_map/ppermute | solution.py:503
  39.5 2.8 %collective-permute-done.9 = f32[128,256]{1,0:T(8,128)S(1)} collective-permute-done((f32[128,256]{1,0:T(8,128)S(1)}, f32[128,256]{1,0:T(8,128)S(1)}, u32[]{:S(2)}, u32[]{:S(2)}) %collective-permute-start.9) | collective-permute-done | bytes 131104 | tf_op jit(solution)/shard_map/ppermute | solution.py:503
  43.1 4.7 %collective-permute-start.11 = (f32[128,256]{1,0:T(8,128)S(1)}, f32[128,256]{1,0:T(8,128)S(1)}, u32[]{:S(2)}, u32[]{:S(2)}) collective-permute-start(f32[128,256]{1,0:T(8,128)S(1)} %add_add_fusion.here_ref), channel_id=1, source_target_pairs={{0,8},{1,9},{2,10},{3,11},{4,12},{5,13},{6,14},{7,15},{8,0},{9,1},... | collective-permute-start | bytes 393224 | tf_op jit(solution)/shard_map/ppermute | solution.py:503
  47.8 4.6 %plane_couple.2.refs_1_ = f32[1024,512]{1,0:T(8,128)S(1)} custom-call(s32[6]{0:T(128)S(1)} %broadcast_multiply_fusion.first_ref, f32[24,2048]{1,0:T(8,128)S(1)} %pad_maximum_fusion.refs_0_), custom_call_target="tpu_custom_call" | custom-call | flops 2147483648 | bytes 2000000 | tf_op jit(solution)/shard_map/plane_couple/pallas_call | solution.py:795
  52.4 2.5 %plane_first.1.a_ref.pulled_ref.old_z_ref = f32[128,256]{1,0:T(8,128)S(1)} custom-call(f32[3]{0:T(128)S(1)} %add_convert_fusion.flag_ref, f32[128,256]{1,0:T(8,128)S(1)} %add_add_fusion.here_ref, f32[128,256]{1,0:T(8,128)S(1)} %collective-permute-done.11.pair_ref, f32[128,256]{1,0:T(8,128)S(1)} %collective-permute-done.12.middle_ref, ...), custom_call_target="tpu_custom_call" | custom-call | flops 1 | bytes 1 | tf_op jit(solution)/shard_map/plane_first/pallas_call | solution.py:922
  57.7 4.9 %plane_couple.3 = (bf16[1024,512]{1,0:T(8,128)(2,1)S(1)}, bf16[1024,512]{1,0:T(8,128)(2,1)S(1)}) custom-call(s32[6]{0:T(128)S(1)} %broadcast_multiply_fusion.first_ref, f32[24,2048]{1,0:T(8,128)S(1)} %collective-permute-done.6.refs_0_, f32[1024,512]{1,0:T(8,128)S(1)} %plane_couple.2.refs_1_), custom_call_target="tpu_custom_call" | custom-call | flops 2147483648 | bytes 2000000 | tf_op jit(solution)/shard_map/plane_couple/pallas_call | solution.py:795
  63.7 2.2 %collective-permute-start.16 = (f32[128,256]{1,0:T(8,128)S(1)}, f32[128,256]{1,0:T(8,128)S(1)}, u32[]{:S(2)}, u32[]{:S(2)}) collective-permute-start(f32[128,256]{1,0:T(8,128)S(1)} %get-tuple-element.65), channel_id=1, source_target_pairs={{0,1},{1,0},{2,3},{3,2},{4,5},{5,4},{6,7},{7,6},{8,9},{9,8},{10,11... | collective-permute-start | bytes 393224 | tf_op jit(solution)/shard_map/ppermute | solution.py:503
  67.6 3.0 %collective-permute-start.17 = (f32[128,256]{1,0:T(8,128)S(1)}, f32[128,256]{1,0:T(8,128)S(1)}, u32[]{:S(2)}, u32[]{:S(2)}) collective-permute-start(f32[128,256]{1,0:T(8,128)S(1)} %add.61.here_ref.old_s_ref), channel_id=1, source_target_pairs={{0,8},{1,9},{2,10},{3,11},{4,12},{5,13},{6,14},{7,15},{8,0},{9,1},... | collective-permute-start | bytes 393224 | tf_op jit(solution)/shard_map/ppermute | solution.py:503
  70.6 3.3 %collective-permute-done.17.pair_ref = f32[128,256]{1,0:T(8,128)S(1)} collective-permute-done((f32[128,256]{1,0:T(8,128)S(1)}, f32[128,256]{1,0:T(8,128)S(1)}, u32[]{:S(2)}, u32[]{:S(2)}) %collective-permute-start.17) | collective-permute-done | bytes 131104 | tf_op jit(solution)/shard_map/ppermute | solution.py:503
  73.8 1.8 %plane_open.1 = (f32[136,256]{1,0:T(8,128)S(1)}, f32[256,256]{1,0:T(8,128)S(1)}) custom-call(f32[3]{0:T(128)S(1)} %add_convert_fusion.flag_ref, f32[128,256]{1,0:T(8,128)S(1)} %add.61.here_ref.old_s_ref, f32[128,256]{1,0:T(8,128)S(1)} %collective-permute-done.17.pair_ref, f32[128,256]{1,0:T(8,128)S(1)} %collective-permute-done.18.middle_ref, ...), custom_call_target="tpu_custom_call" | custom-call | flops 1 | bytes 1 | tf_op jit(solution)/shard_map/plane_open/pallas_call | solution.py:922
  76.9 1.5 %collective-permute-start.19 = (f32[136,256]{1,0:T(8,128)S(1)}, f32[136,256]{1,0:T(8,128)S(1)}, u32[]{:S(2)}, u32[]{:S(2)}) collective-permute-start(f32[136,256]{1,0:T(8,128)S(1)} %get-tuple-element.66.a_ref.pulled_ref), channel_id=1, source_target_pairs={{0,4},{1,5},{2,6},{3,7},{4,0},{5,1},{6,2},{7,3},{8,12},{9,13},{10,... | collective-permute-start | bytes 417800 | tf_op jit(solution)/shard_map/ppermute | solution.py:503
  80.6 4.1 %collective-permute-done.20.c_ref = f32[136,256]{1,0:T(8,128)S(1)} collective-permute-done((f32[136,256]{1,0:T(8,128)S(1)}, f32[136,256]{1,0:T(8,128)S(1)}, u32[]{:S(2)}, u32[]{:S(2)}) %collective-permute-start.20) | collective-permute-done | bytes 139296 | tf_op jit(solution)/shard_map/ppermute | solution.py:503
  88.5 2.8 %collective-permute-start.23 = (f32[136,256]{1,0:T(8,128)S(1)}, f32[136,256]{1,0:T(8,128)S(1)}, u32[]{:S(2)}, u32[]{:S(2)}) collective-permute-start(f32[136,256]{1,0:T(8,128)S(1)} %slice_add_fusion.1.here_ref), channel_id=1, source_target_pairs={{0,8},{1,9},{2,10},{3,11},{4,12},{5,13},{6,14},{7,15},{8,0},{9,1},... | collective-permute-start | bytes 417800 | tf_op jit(solution)/shard_map/ppermute | solution.py:503
  91.3 2.0 %collective-permute-start.25 = (f32[8,256]{1,0:T(8,128)S(1)}, f32[8,256]{1,0:T(8,128)S(1)}, u32[]{:S(2)}, u32[]{:S(2)}) collective-permute-start(f32[8,256]{1,0:T(8,128)S(1)} %slice.29), channel_id=1, source_target_pairs={{0,24},{1,25},{2,26},{3,27},{4,28},{5,29},{6,30},{7,31},{8,16},{9,... | collective-permute-start | bytes 24584 | tf_op jit(solution)/shard_map/ppermute | solution.py:503
  103.5 1.8 %collective-permute-done.28.c_ref = f32[136,256]{1,0:T(8,128)S(1)} collective-permute-done((f32[136,256]{1,0:T(8,128)S(1)}, f32[136,256]{1,0:T(8,128)S(1)}, u32[]{:S(2)}, u32[]{:S(2)}) %collective-permute-start.28) | collective-permute-done | bytes 139296 | tf_op jit(solution)/shard_map/ppermute | solution.py:503
  105.9 3.4 %collective-permute-start.30 = (f32[392,256]{1,0:T(8,128)S(1)}, f32[392,256]{1,0:T(8,128)S(1)}, u32[]{:S(2)}, u32[]{:S(2)}) collective-permute-start(f32[392,256]{1,0:T(8,128)S(1)} %get-tuple-element.76), channel_id=1, source_target_pairs={{0,1},{1,0},{2,3},{3,2},{4,5},{5,4},{6,7},{7,6},{8,9},{9,8},{10,11... | collective-permute-start | bytes 1204232 | tf_op jit(solution)/shard_map/ppermute | solution.py:503
  110.6 2.4 %collective-permute-start.31 = (f32[136,256]{1,0:T(8,128)S(1)}, f32[136,256]{1,0:T(8,128)S(1)}, u32[]{:S(2)}, u32[]{:S(2)}) collective-permute-start(f32[136,256]{1,0:T(8,128)S(1)} %slice_add_fusion.here_ref), channel_id=1, source_target_pairs={{0,8},{1,9},{2,10},{3,11},{4,12},{5,13},{6,14},{7,15},{8,16},{9,17... | collective-permute-start | bytes 417800 | tf_op jit(solution)/shard_map/ppermute | solution.py:503
  113.0 2.0 %plane_rows.5 = (f32[128,512]{1,0:T(8,128)S(1)}, f32[256,256]{1,0:T(8,128)}, f32[256,512]{1,0:T(8,128)S(1)}) custom-call(s32[6]{0:T(128)S(1)} %broadcast_multiply_fusion.first_ref, f32[8,512]{1,0:T(8,128)S(1)} %slice.22.class_ref.meta_ref, f32[8,512]{1,0:T(8,128)S(1)} %collective-permute-done.7.meta_other_ref, ...), custom_call_target="tpu_custom_call" | custom-call | flops 1000000000 | bytes 2000000 | tf_op jit(solution)/shard_map/plane_rows/pallas_call | solution.py:878
  117.0 5.5 %all-to-all-start = ((f32[32,8,128]{2,1,0:T(8,128)}), f32[32,8,128]{2,1,0:T(8,128)S(1)}, u32[]{:S(2)}, u32[]{:S(2)}) async-start(f32[32,8,128]{2,1,0:T(8,128)} %plane_close.1), calls=%async_computation | async-start | bytes 262144 | tf_op jit(solution)/shard_map/all_to_all | solution.py:1172
  122.5 8.2 %all-to-all-done.close_ref = f32[32,8,128]{2,1,0:T(8,128)S(1)} async-done(((f32[32,8,128]{2,1,0:T(8,128)}), f32[32,8,128]{2,1,0:T(8,128)S(1)}, u32[]{:S(2)}, u32[]{:S(2)}) %all-to-all-start) | async-done | bytes 131104 | tf_op jit(solution)/shard_map/all_to_all | solution.py:1172
  132.0 2.6 %collective-permute-start.33 = (f32[512,128]{1,0:T(8,128)S(1)}, f32[512,128]{1,0:T(8,128)S(1)}, u32[]{:S(2)}, u32[]{:S(2)}) collective-permute-start(f32[512,128]{1,0:T(8,128)S(1)} %plane_combine.1), channel_id=1, source_target_pairs={{0,0},{1,16},{2,8},{3,24},{4,4},{5,20},{6,12},{7,28},{8,1},{9,17},... | collective-permute-start | bytes 786440 | tf_op jit(solution)/shard_map/ppermute | solution.py:503
  134.6 10.7 %collective-permute-done.33.rows_ref = f32[512,128]{1,0:T(8,128)S(1)} collective-permute-done((f32[512,128]{1,0:T(8,128)S(1)}, f32[512,128]{1,0:T(8,128)S(1)}, u32[]{:S(2)}, u32[]{:S(2)}) %collective-permute-start.33) | collective-permute-done | bytes 262176 | tf_op jit(solution)/shard_map/ppermute | solution.py:503
  145.3 2.4 %plane_finish.1 = f32[4096,128]{1,0:T(8,128)} custom-call(f32[512,128]{1,0:T(8,128)S(1)} %collective-permute-done.33.rows_ref, s32[32,16,128]{2,1,0:T(8,128)S(1)} %copy-done.3, f32[4096,128]{1,0:T(8,128)S(1)} %copy-done), custom_call_target="tpu_custom_call" | custom-call | tf_op jit(solution)/shard_map/plane_finish/pallas_call | solution.py:1070
  (101 shorter events, 34.1 us)
Async XLA Ops:
  3.4 7.8 %collective-permute-start.1 = (f32[256,128]{1,0:T(8,128)S(1)}, f32[256,128]{1,0:T(8,128)S(1)}, u32[]{:S(2)}, u32[]{:S(2)}) collective-permute-start(f32[256,128]{1,0:T(8,128)S(1)} %copy-done.10), channel_id=1, source_target_pairs={{1,0},{2,1},{3,2},{5,4},{6,5},{7,6},{9,8},{10,9},{11,10},{13,12},{... | collective-permute-start | bytes 393224 | tf_op jit(solution)/shard_map/ppermute | solution.py:503
  5.6 10.9 %collective-permute-start.4 = (f32[24,512]{1,0:T(8,128)S(1)}, f32[24,512]{1,0:T(8,128)S(1)}, u32[]{:S(2)}, u32[]{:S(2)}) collective-permute-start(f32[24,512]{1,0:T(8,128)S(1)} %describe.1), channel_id=1, source_target_pairs={{0,4},{1,5},{2,6},{3,7},{4,0},{5,1},{6,2},{7,3},{8,12},{9,13},{10,... | collective-permute-start | bytes 147464 | tf_op jit(solution)/shard_map/ppermute | solution.py:503
  8.3 20.3 %collective-permute-start = (f32[128,512]{1,0:T(8,128)}, f32[128,512]{1,0:T(8,128)S(1)}, u32[]{:S(2)}, u32[]{:S(2)}) collective-permute-start(f32[128,512]{1,0:T(8,128)} %send.1), channel_id=1, source_target_pairs={{0,0},{1,8},{2,16},{3,24},{4,4},{5,12},{6,20},{7,28},{8,2},{9,10},... | collective-permute-start | bytes 786440 | tf_op jit(solution)/shard_map/ppermute | solution.py:503
  12.5 18.9 %collective-permute-start.2 = (f32[72,512]{1,0:T(8,128)S(1)}, f32[72,512]{1,0:T(8,128)S(1)}, u32[]{:S(2)}, u32[]{:S(2)}) collective-permute-start(f32[72,512]{1,0:T(8,128)S(1)} %observe.1), channel_id=1, source_target_pairs={{0,0},{1,8},{2,16},{3,24},{4,4},{5,12},{6,20},{7,28},{8,2},{9,10},... | collective-permute-start | bytes 442376 | tf_op jit(solution)/shard_map/ppermute | solution.py:503
  16.6 15.5 %collective-permute-start.5 = (f32[24,1024]{1,0:T(8,128)S(1)}, f32[24,1024]{1,0:T(8,128)S(1)}, u32[]{:S(2)}, u32[]{:S(2)}) collective-permute-start(f32[24,1024]{1,0:T(8,128)S(1)} %pad_maximum_fusion.2), channel_id=1, source_target_pairs={{0,8},{1,9},{2,10},{3,11},{4,12},{5,13},{6,14},{7,15},{8,0},{9,1},... | collective-permute-start | bytes 294920 | tf_op jit(solution)/shard_map/ppermute | solution.py:503
  34.5 4.9 %collective-permute-start.8 = (f32[128,256]{1,0:T(8,128)S(1)}, f32[128,256]{1,0:T(8,128)S(1)}, u32[]{:S(2)}, u32[]{:S(2)}) collective-permute-start(f32[128,256]{1,0:T(8,128)S(1)} %get-tuple-element.54), channel_id=1, source_target_pairs={{0,4},{1,5},{2,6},{3,7},{4,0},{5,1},{6,2},{7,3},{8,12},{9,13},{10,... | collective-permute-start | bytes 393224 | tf_op jit(solution)/shard_map/ppermute | solution.py:503
  34.9 7.4 %collective-permute-start.9 = (f32[128,256]{1,0:T(8,128)S(1)}, f32[128,256]{1,0:T(8,128)S(1)}, u32[]{:S(2)}, u32[]{:S(2)}) collective-permute-start(f32[128,256]{1,0:T(8,128)S(1)} %get-tuple-element.55), channel_id=1, source_target_pairs={{0,2},{1,3},{2,0},{3,1},{4,6},{5,7},{6,4},{7,5},{8,10},{9,11},{10,... | collective-permute-start | bytes 393224 | tf_op jit(solution)/shard_map/ppermute | solution.py:503
  34.9 7.4 %collective-permute-start.10 = (f32[128,256]{1,0:T(8,128)S(1)}, f32[128,256]{1,0:T(8,128)S(1)}, u32[]{:S(2)}, u32[]{:S(2)}) collective-permute-start(f32[128,256]{1,0:T(8,128)S(1)} %get-tuple-element.56), channel_id=1, source_target_pairs={{0,6},{1,7},{2,4},{3,5},{4,2},{5,3},{6,0},{7,1},{8,14},{9,15},{10,... | collective-permute-start | bytes 393224 | tf_op jit(solution)/shard_map/ppermute | solution.py:503
  37.3 20.4 %collective-permute-start.6 = (f32[24,2048]{1,0:T(8,128)S(1)}, f32[24,2048]{1,0:T(8,128)S(1)}, u32[]{:S(2)}, u32[]{:S(2)}) collective-permute-start(f32[24,2048]{1,0:T(8,128)S(1)} %pad_maximum_fusion.refs_0_), channel_id=1, source_target_pairs={{0,16},{1,17},{2,18},{3,19},{4,20},{5,21},{6,22},{7,23},{8,24},{9,... | collective-permute-start | bytes 589832 | tf_op jit(solution)/shard_map/ppermute | solution.py:503
  42.3 10.1 %collective-permute-start.12 = (f32[128,256]{1,0:T(8,128)S(1)}, f32[128,256]{1,0:T(8,128)S(1)}, u32[]{:S(2)}, u32[]{:S(2)}) collective-permute-start(f32[128,256]{1,0:T(8,128)S(1)} %add_add_fusion.here_ref), channel_id=1, source_target_pairs={{8,16},{9,17},{10,18},{11,19},{12,20},{13,21},{14,22},{15,23},{16,... | collective-permute-start | bytes 393224 | tf_op jit(solution)/shard_map/ppermute | solution.py:503
  43.1 9.3 %collective-permute-start.11 = (f32[128,256]{1,0:T(8,128)S(1)}, f32[128,256]{1,0:T(8,128)S(1)}, u32[]{:S(2)}, u32[]{:S(2)}) collective-permute-start(f32[128,256]{1,0:T(8,128)S(1)} %add_add_fusion.here_ref), channel_id=1, source_target_pairs={{0,8},{1,9},{2,10},{3,11},{4,12},{5,13},{6,14},{7,15},{8,0},{9,1},... | collective-permute-start | bytes 393224 | tf_op jit(solution)/shard_map/ppermute | solution.py:503
  55.0 7.7 %collective-permute-start.15 = (f32[128,256]{1,0:T(8,128)S(1)}, f32[128,256]{1,0:T(8,128)S(1)}, u32[]{:S(2)}, u32[]{:S(2)}) collective-permute-start(f32[128,256]{1,0:T(8,128)S(1)} %plane_first.1.a_ref.pulled_ref.old_z_ref), channel_id=1, source_target_pairs={{0,6},{1,7},{2,4},{3,5},{4,2},{5,3},{6,0},{7,1},{8,14},{9,15},{10,... | collective-permute-start | bytes 393224 | tf_op jit(solution)/shard_map/ppermute | solution.py:503
  56.2 6.9 %collective-permute-start.14 = (f32[128,256]{1,0:T(8,128)S(1)}, f32[128,256]{1,0:T(8,128)S(1)}, u32[]{:S(2)}, u32[]{:S(2)}) collective-permute-start(f32[128,256]{1,0:T(8,128)S(1)} %plane_first.1.a_ref.pulled_ref.old_z_ref), channel_id=1, source_target_pairs={{0,2},{1,3},{2,0},{3,1},{4,6},{5,7},{6,4},{7,5},{8,10},{9,11},{10,... | collective-permute-start | bytes 393224 | tf_op jit(solution)/shard_map/ppermute | solution.py:503
  56.3 6.8 %collective-permute-start.13 = (f32[128,256]{1,0:T(8,128)S(1)}, f32[128,256]{1,0:T(8,128)S(1)}, u32[]{:S(2)}, u32[]{:S(2)}) collective-permute-start(f32[128,256]{1,0:T(8,128)S(1)} %plane_first.1.a_ref.pulled_ref.old_z_ref), channel_id=1, source_target_pairs={{0,4},{1,5},{2,6},{3,7},{4,0},{5,1},{6,2},{7,3},{8,12},{9,13},{10,... | collective-permute-start | bytes 393224 | tf_op jit(solution)/shard_map/ppermute | solution.py:503
  63.7 3.2 %collective-permute-start.16 = (f32[128,256]{1,0:T(8,128)S(1)}, f32[128,256]{1,0:T(8,128)S(1)}, u32[]{:S(2)}, u32[]{:S(2)}) collective-permute-start(f32[128,256]{1,0:T(8,128)S(1)} %get-tuple-element.65), channel_id=1, source_target_pairs={{0,1},{1,0},{2,3},{3,2},{4,5},{5,4},{6,7},{7,6},{8,9},{9,8},{10,11... | collective-permute-start | bytes 393224 | tf_op jit(solution)/shard_map/ppermute | solution.py:503
  66.9 3.7 %collective-permute-start.18 = (f32[128,256]{1,0:T(8,128)S(1)}, f32[128,256]{1,0:T(8,128)S(1)}, u32[]{:S(2)}, u32[]{:S(2)}) collective-permute-start(f32[128,256]{1,0:T(8,128)S(1)} %add.61.here_ref.old_s_ref), channel_id=1, source_target_pairs={{8,16},{9,17},{10,18},{11,19},{12,20},{13,21},{14,22},{15,23},{16,... | collective-permute-start | bytes 393224 | tf_op jit(solution)/shard_map/ppermute | solution.py:503
  67.6 6.3 %collective-permute-start.17 = (f32[128,256]{1,0:T(8,128)S(1)}, f32[128,256]{1,0:T(8,128)S(1)}, u32[]{:S(2)}, u32[]{:S(2)}) collective-permute-start(f32[128,256]{1,0:T(8,128)S(1)} %add.61.here_ref.old_s_ref), channel_id=1, source_target_pairs={{0,8},{1,9},{2,10},{3,11},{4,12},{5,13},{6,14},{7,15},{8,0},{9,1},... | collective-permute-start | bytes 393224 | tf_op jit(solution)/shard_map/ppermute | solution.py:503
  75.7 5.0 %collective-permute-start.21 = (f32[136,256]{1,0:T(8,128)S(1)}, f32[136,256]{1,0:T(8,128)S(1)}, u32[]{:S(2)}, u32[]{:S(2)}) collective-permute-start(f32[136,256]{1,0:T(8,128)S(1)} %get-tuple-element.66.a_ref.pulled_ref), channel_id=1, source_target_pairs={{0,6},{1,7},{2,4},{3,5},{4,2},{5,3},{6,0},{7,1},{8,14},{9,15},{10,... | collective-permute-start | bytes 417800 | tf_op jit(solution)/shard_map/ppermute | solution.py:503
  76.5 8.2 %collective-permute-start.20 = (f32[136,256]{1,0:T(8,128)S(1)}, f32[136,256]{1,0:T(8,128)S(1)}, u32[]{:S(2)}, u32[]{:S(2)}) collective-permute-start(f32[136,256]{1,0:T(8,128)S(1)} %get-tuple-element.66.a_ref.pulled_ref), channel_id=1, source_target_pairs={{0,2},{1,3},{2,0},{3,1},{4,6},{5,7},{6,4},{7,5},{8,10},{9,11},{10,... | collective-permute-start | bytes 417800 | tf_op jit(solution)/shard_map/ppermute | solution.py:503
  76.9 7.9 %collective-permute-start.19 = (f32[136,256]{1,0:T(8,128)S(1)}, f32[136,256]{1,0:T(8,128)S(1)}, u32[]{:S(2)}, u32[]{:S(2)}) collective-permute-start(f32[136,256]{1,0:T(8,128)S(1)} %get-tuple-element.66.a_ref.pulled_ref), channel_id=1, source_target_pairs={{0,4},{1,5},{2,6},{3,7},{4,0},{5,1},{6,2},{7,3},{8,12},{9,13},{10,... | collective-permute-start | bytes 417800 | tf_op jit(solution)/shard_map/ppermute | solution.py:503
  87.6 5.7 %collective-permute-start.26 = (f32[136,256]{1,0:T(8,128)S(1)}, f32[136,256]{1,0:T(8,128)S(1)}, u32[]{:S(2)}, u32[]{:S(2)}) collective-permute-start(f32[136,256]{1,0:T(8,128)S(1)} %slice_add_fusion.1.here_ref), channel_id=1, source_target_pairs={{8,16},{9,17},{10,18},{11,19},{12,20},{13,21},{14,22},{15,23},{16,... | collective-permute-start | bytes 417800 | tf_op jit(solution)/shard_map/ppermute | solution.py:503
  88.5 6.2 %collective-permute-start.23 = (f32[136,256]{1,0:T(8,128)S(1)}, f32[136,256]{1,0:T(8,128)S(1)}, u32[]{:S(2)}, u32[]{:S(2)}) collective-permute-start(f32[136,256]{1,0:T(8,128)S(1)} %slice_add_fusion.1.here_ref), channel_id=1, source_target_pairs={{0,8},{1,9},{2,10},{3,11},{4,12},{5,13},{6,14},{7,15},{8,0},{9,1},... | collective-permute-start | bytes 417800 | tf_op jit(solution)/shard_map/ppermute | solution.py:503
  91.3 5.0 %collective-permute-start.25 = (f32[8,256]{1,0:T(8,128)S(1)}, f32[8,256]{1,0:T(8,128)S(1)}, u32[]{:S(2)}, u32[]{:S(2)}) collective-permute-start(f32[8,256]{1,0:T(8,128)S(1)} %slice.29), channel_id=1, source_target_pairs={{0,24},{1,25},{2,26},{3,27},{4,28},{5,29},{6,30},{7,31},{8,16},{9,... | collective-permute-start | bytes 24584 | tf_op jit(solution)/shard_map/ppermute | solution.py:503
  93.3 3.4 %collective-permute-start.24 = (f32[8,256]{1,0:T(8,128)S(1)}, f32[8,256]{1,0:T(8,128)S(1)}, u32[]{:S(2)}, u32[]{:S(2)}) collective-permute-start(f32[8,256]{1,0:T(8,128)S(1)} %slice.29), channel_id=1, source_target_pairs={{0,16},{1,17},{2,18},{3,19},{4,20},{5,21},{6,22},{7,23},{8,24},{9,... | collective-permute-start | bytes 24584 | tf_op jit(solution)/shard_map/ppermute | solution.py:503
  98.6 4.9 %collective-permute-start.29 = (f32[136,256]{1,0:T(8,128)S(1)}, f32[136,256]{1,0:T(8,128)S(1)}, u32[]{:S(2)}, u32[]{:S(2)}) collective-permute-start(f32[136,256]{1,0:T(8,128)S(1)} %get-tuple-element.72.a_ref.pulled_ref), channel_id=1, source_target_pairs={{0,6},{1,7},{2,4},{3,5},{4,2},{5,3},{6,0},{7,1},{8,14},{9,15},{10,... | collective-permute-start | bytes 417800 | tf_op jit(solution)/shard_map/ppermute | solution.py:503
  99.5 5.8 %collective-permute-start.28 = (f32[136,256]{1,0:T(8,128)S(1)}, f32[136,256]{1,0:T(8,128)S(1)}, u32[]{:S(2)}, u32[]{:S(2)}) collective-permute-start(f32[136,256]{1,0:T(8,128)S(1)} %get-tuple-element.72.a_ref.pulled_ref), channel_id=1, source_target_pairs={{0,2},{1,3},{2,0},{3,1},{4,6},{5,7},{6,4},{7,5},{8,10},{9,11},{10,... | collective-permute-start | bytes 417800 | tf_op jit(solution)/shard_map/ppermute | solution.py:503
  100.1 5.1 %collective-permute-start.27 = (f32[136,256]{1,0:T(8,128)S(1)}, f32[136,256]{1,0:T(8,128)S(1)}, u32[]{:S(2)}, u32[]{:S(2)}) collective-permute-start(f32[136,256]{1,0:T(8,128)S(1)} %get-tuple-element.72.a_ref.pulled_ref), channel_id=1, source_target_pairs={{0,4},{1,5},{2,6},{3,7},{4,0},{5,1},{6,2},{7,3},{8,12},{9,13},{10,... | collective-permute-start | bytes 417800 | tf_op jit(solution)/shard_map/ppermute | solution.py:503
  105.9 4.7 %collective-permute-start.30 = (f32[392,256]{1,0:T(8,128)S(1)}, f32[392,256]{1,0:T(8,128)S(1)}, u32[]{:S(2)}, u32[]{:S(2)}) collective-permute-start(f32[392,256]{1,0:T(8,128)S(1)} %get-tuple-element.76), channel_id=1, source_target_pairs={{0,1},{1,0},{2,3},{3,2},{4,5},{5,4},{6,7},{7,6},{8,9},{9,8},{10,11... | collective-permute-start | bytes 1204232 | tf_op jit(solution)/shard_map/ppermute | solution.py:503
  110.6 5.0 %collective-permute-start.31 = (f32[136,256]{1,0:T(8,128)S(1)}, f32[136,256]{1,0:T(8,128)S(1)}, u32[]{:S(2)}, u32[]{:S(2)}) collective-permute-start(f32[136,256]{1,0:T(8,128)S(1)} %slice_add_fusion.here_ref), channel_id=1, source_target_pairs={{0,8},{1,9},{2,10},{3,11},{4,12},{5,13},{6,14},{7,15},{8,16},{9,17... | collective-permute-start | bytes 417800 | tf_op jit(solution)/shard_map/ppermute | solution.py:503
  114.9 7.6 %collective-permute-start.32 = (f32[256,256]{1,0:T(8,128)}, f32[256,256]{1,0:T(8,128)S(1)}, u32[]{:S(2)}, u32[]{:S(2)}) collective-permute-start(f32[256,256]{1,0:T(8,128)} %get-tuple-element.82), channel_id=1, source_target_pairs={{0,1},{1,0},{2,3},{3,2},{4,5},{5,4},{6,7},{7,6},{8,9},{9,8},{10,11... | collective-permute-start | bytes 786440 | tf_op jit(solution)/shard_map/ppermute | solution.py:503
  117.0 13.7 %all-to-all-start = ((f32[32,8,128]{2,1,0:T(8,128)}), f32[32,8,128]{2,1,0:T(8,128)S(1)}, u32[]{:S(2)}, u32[]{:S(2)}) async-start(f32[32,8,128]{2,1,0:T(8,128)} %plane_close.1), calls=%async_computation | async-start | bytes 262144 | tf_op jit(solution)/shard_map/all_to_all | solution.py:1172
  132.0 13.3 %collective-permute-start.33 = (f32[512,128]{1,0:T(8,128)S(1)}, f32[512,128]{1,0:T(8,128)S(1)}, u32[]{:S(2)}, u32[]{:S(2)}) collective-permute-start(f32[512,128]{1,0:T(8,128)S(1)} %plane_combine.1), channel_id=1, source_target_pairs={{0,0},{1,16},{2,8},{3,24},{4,4},{5,20},{6,12},{7,28},{8,1},{9,17},... | collective-permute-start | bytes 786440 | tf_op jit(solution)/shard_map/ppermute | solution.py:503
  (18 other events, 150.7 us)

commit v16 on v13

--- a/solution.py
+++ b/solution.py
@@ -652,44 +652,66 @@
     )(seen, later, gauge_kernel.reshape(1, rows), kernels, wide, *mats)
 
 
-def send_kernel(inc_ref, field_ref, gauge_ref, kind_ref, out_ref):
+def send_kernel(
+    inc_hbm, field_hbm, gauge_hbm, kind_hbm, out_ref, inc_ref, field_ref, gauge_ref, kind_ref, sems, label_sems
+):
     blocks, slots, width = inc_ref.shape
-    count = blocks * slots
-    weights = inc_ref[...].astype(F32).astype(BF16)
-    parts = []
-    for b in range(blocks):
-        value = jnp.concatenate(pieces(field_ref[pl.ds(b * width, width), :], 3)[::-1], axis=0)
-        parts.append(dot(jnp.concatenate([weights[b]] * 3, axis=1), value))
-    out_ref[pl.ds(0, HOURS), :] = jnp.transpose(jnp.concatenate(parts, axis=0))
-    kinds = kind_ref.shape[1] // count
-    here = jnp.minimum(pl.program_id(0), kinds - 1) * count
+    chunks = sems.shape[0]
+    step = blocks // chunks
+    copies = []
+    for i in range(chunks):
+        near = pl.ds(i * step, step)
+        far = pl.ds(i * step * width, step * width)
+        copies.append(
+            (
+                pltpu.make_async_copy(inc_hbm.at[near], inc_ref.at[near], sems.at[i, 0]),
+                pltpu.make_async_copy(field_hbm.at[far], field_ref.at[far], sems.at[i, 1]),
+            )
+        )
+        for copy in copies[-1]:
+            copy.start()
+    labels = (
+        pltpu.make_async_copy(gauge_hbm, gauge_ref, label_sems.at[0]),
+        pltpu.make_async_copy(kind_hbm, kind_ref, label_sems.at[1]),
+    )
+    for copy in labels:
+        copy.start()
+    for i in range(chunks):
+        for copy in copies[i]:
+            copy.wait()
+        parts = []
+        for b in range(i * step, (i + 1) * step):
+            weight = inc_ref[b].astype(F32).astype(BF16)
+            value = jnp.concatenate(pieces(field_ref[pl.ds(b * width, width), :], 3)[::-1], axis=0)
+            parts.append(dot(jnp.concatenate([weight] * 3, axis=1), value))
+        out_ref[pl.ds(0, HOURS), pl.ds(i * step * slots, step * slots)] = jnp.transpose(
+            jnp.concatenate(parts, axis=0)
+        )
+    for copy in labels:
+        copy.wait()
+    count, kinds = gauge_ref.shape[1], kind_ref.shape[1]
+    kind = jnp.concatenate([kind_ref[...].astype(F32), jnp.zeros((1, count - kinds), F32)], axis=1)
     out_ref[pl.ds(HOURS, 8), :] = jnp.concatenate(
-        [
-            gauge_ref[...].astype(F32),
-            kind_ref[:, pl.ds(pl.multiple_of(here, count), count)].astype(F32),
-            jnp.zeros((6, count), F32),
+        [gauge_ref[...].astype(F32), kind, jnp.zeros((6, count), F32)], axis=0
+    )
+
+
+def send(incidence, field, row_gauge, gauge_kernel):
+    count, rows = row_gauge.shape[0], gauge_kernel.shape[0]
+    chunks = 4
+    return pl.pallas_call(
+        send_kernel,
+        in_specs=[pl.BlockSpec(memory_space=pltpu.HBM)] * 4,
+        out_shape=jax.ShapeDtypeStruct((HOURS + 8, count), F32),
+        scratch_shapes=[
+            pltpu.VMEM(incidence.shape, incidence.dtype),
+            pltpu.VMEM(field.shape, F32),
+            pltpu.VMEM((1, count), row_gauge.dtype),
+            pltpu.VMEM((1, rows), gauge_kernel.dtype),
+            pltpu.SemaphoreType.DMA((chunks, 2)),
+            pltpu.SemaphoreType.DMA((2,)),
         ],
-        axis=0,
-    )
-
-
-def send(incidence, field, row_gauge, gauge_kernel):
-    blocks, slots, width = incidence.shape
-    count = blocks * slots
-    rows = gauge_kernel.shape[0]
-    step = 8
-    return pl.pallas_call(
-        send_kernel,
-        grid=(blocks // step,),
-        in_specs=[
-            pl.BlockSpec((step, slots, width), lambda i: (i, 0, 0)),
-            pl.BlockSpec((step * width, HOURS), lambda i: (i, 0)),
-            pl.BlockSpec((1, step * slots), lambda i: (0, i)),
-            pl.BlockSpec((1, rows), lambda i: (0, 0)),
-        ],
-        out_specs=pl.BlockSpec((HOURS + 8, step * slots), lambda i: (0, i)),
-        out_shape=jax.ShapeDtypeStruct((HOURS + 8, count), F32),
-        compiler_params=params(),
+        compiler_params=params(60),
         name="send",
         cost_estimate=SMALL,
     )(incidence, field, row_gauge.reshape(1, count), gauge_kernel.reshape(1, rows))
@@ -1084,11 +1106,12 @@
         (parcel, incidence, row_gauge, gauge_kernel, observed)
     )
     parcel = moved(parcel, to_plane)
+    seen = observe(seen, moved(seen, hour_before), kinds, kernels, short3, [forward3, inverse_first3])
+    seen, near = lax.optimization_barrier((seen, near))
+    seen = moved(seen, to_plane)
     meta = describe(near, gauges)
     meta = jnp.concatenate([meta, moved(meta, over_x)], axis=1)
     meta = jnp.concatenate([meta, moved(meta, z_pair)], axis=1)
-    seen = observe(seen, moved(seen, hour_before), kinds, kernels, short3, [forward3, inverse_first3])
-    seen = moved(seen, to_plane)
     parcel, seen = lax.optimization_barrier((parcel, seen))
     parcels = [parcel, moved(parcel, over_core)]
     spec = plane_spectrum(parcel[hours:], kernels, short3, rows)

time: 146 us -> 146 us (level)
  local copies, waits for them, and re-layouts: 4.04 us -> 0.15 us
  Pallas kernels: 33.1 us -> 35.3 us
  waiting for transfers between devices: 51.5 us -> 53.6 us
    unnamed x30 -> x26, local copies, waits for them, and re-layouts: 3.95 us -> 0.06 us
    ppermute x33, waiting for transfers between devices: 43.3 us -> 45.4 us  [moved(): return lax.ppermute(value, ('basin', 'tm'), pairs)]
    pallas_call x1, Pallas kernels: 1.42 us -> 3.34 us  [send(): pl.pallas_call(send_kernel, in_specs=[pl.BlockSpec(memory_space=pltpu.HBM...]
where the time goes in v16:
time: 146 us
  starting transfers between devices  56.2 us (38%)
  waiting for transfers between devices  53.6 us (37%)
  Pallas kernels  35.3 us (24%)
    ppermute x33, starting transfers between devices, moved(): return lax.ppermute(value, ('basin', 'tm'), pairs)  50.5 us
    ppermute x33, waiting for transfers between devices, moved(): return lax.ppermute(value, ('basin', 'tm'), pairs)  45.4 us
    pallas_call x6, Pallas kernels, plane_call(): pl.pallas_call(kernel, in_specs=[pl.BlockSpec(memory_space=pltpu.SMEM)] *...  9.78 us
    pallas_call x2, Pallas kernels, plane_couple(): pl.pallas_call(functools.partial(plane_couple_kernel, last), in_specs=[pl...  9.57 us
    all_to_all x1, waiting for transfers between devices, plane_shards(): close_note = lax.all_to_all(note, ('basin', 'tm'), 0, 0, tiled=False)  8.18 us
    all_to_all x1, starting transfers between devices, plane_shards(): close_note = lax.all_to_all(note, ('basin', 'tm'), 0, 0, tiled=False)  5.75 us
    pallas_call x3, Pallas kernels, plane_rows(): pl.pallas_call(plane_rows_kernel, in_specs=[pl.BlockSpec(memory_space=plt...  4.51 us
    pallas_call x1, Pallas kernels, send(): pl.pallas_call(send_kernel, in_specs=[pl.BlockSpec(memory_space=pltpu.HBM...  3.34 us
  transfers between devices with their start and end apart: 34, of which 20 were waited for; matrix products, arithmetic and copies ran while one was open for 0% of the time, Pallas kernels for 15%

profile of v16, /device:TPU:1, one launch (start us, length us, event | category | flops | bytes accessed | tf_op | source)
XLA Modules:
  0.0 146.0 jit_solution(16303253091699942465)
XLA Ops:
  0.1 3.3 %send.1 = f32[136,512]{1,0:T(8,128)} custom-call(s32[32,16,128]{2,1,0:T(8,128)} %inc_ref.2, f32[4096,128]{1,0:T(8,128)} %field_ref.1, s32[1,512]{1,0:T(1,128)} %bitcast.12, s32[1,256]{1,0:T(1,128)} %bitcast.14), custom_call_target="tpu_custom_call" | custom-call | flops 1 | bytes 1 | tf_op jit(solution)/shard_map/send/pallas_call | solution.py:702
  3.4 2.0 %collective-permute-start.1 = (f32[256,128]{1,0:T(8,128)S(1)}, f32[256,128]{1,0:T(8,128)S(1)}, u32[]{:S(2)}, u32[]{:S(2)}) collective-permute-start(f32[256,128]{1,0:T(8,128)S(1)} %copy-done.10), channel_id=1, source_target_pairs={{1,0},{2,1},{3,2},{5,4},{6,5},{7,6},{9,8},{10,9},{11,10},{13,12},{... | collective-permute-start | bytes 393224 | tf_op jit(solution)/shard_map/ppermute | solution.py:503
  5.4 3.9 %collective-permute-start = (f32[136,512]{1,0:T(8,128)}, f32[136,512]{1,0:T(8,128)S(1)}, u32[]{:S(2)}, u32[]{:S(2)}) collective-permute-start(f32[136,512]{1,0:T(8,128)} %send.1), channel_id=1, source_target_pairs={{0,0},{1,8},{2,16},{3,24},{4,4},{5,12},{6,20},{7,28},{8,2},{9,10},... | collective-permute-start | bytes 835592 | tf_op jit(solution)/shard_map/ppermute | solution.py:503
  13.4 3.0 %collective-permute-start.2 = (f32[128,256]{1,0:T(8,128)S(1)}, f32[128,256]{1,0:T(8,128)S(1)}, u32[]{:S(2)}, u32[]{:S(2)}) collective-permute-start(f32[128,256]{1,0:T(8,128)S(1)} %observe.1), channel_id=1, source_target_pairs={{0,0},{1,8},{2,16},{3,24},{4,4},{5,12},{6,20},{7,28},{8,2},{9,10},... | collective-permute-start | bytes 393224 | tf_op jit(solution)/shard_map/ppermute | solution.py:503
  16.5 1.5 %collective-permute-start.5 = (f32[24,1024]{1,0:T(8,128)S(1)}, f32[24,1024]{1,0:T(8,128)S(1)}, u32[]{:S(2)}, u32[]{:S(2)}) collective-permute-start(f32[24,1024]{1,0:T(8,128)S(1)} %pad_maximum_fusion.1), channel_id=1, source_target_pairs={{0,8},{1,9},{2,10},{3,11},{4,12},{5,13},{6,14},{7,15},{8,0},{9,1},... | collective-permute-start | bytes 294920 | tf_op jit(solution)/shard_map/ppermute | solution.py:503
  18.0 10.8 %collective-permute-done.2.seen_ref = f32[128,256]{1,0:T(8,128)S(1)} collective-permute-done((f32[128,256]{1,0:T(8,128)S(1)}, f32[128,256]{1,0:T(8,128)S(1)}, u32[]{:S(2)}, u32[]{:S(2)}) %collective-permute-start.2) | collective-permute-done | bytes 131104 | tf_op jit(solution)/shard_map/ppermute | solution.py:503
  30.4 1.9 %spread.1 = (f32[128,256]{1,0:T(8,128)S(1)}, f32[128,256]{1,0:T(8,128)}, f32[128,256]{1,0:T(8,128)S(1)}, f32[128,256]{1,0:T(8,128)S(1)}) custom-call(s32[6]{0:T(128)S(1)} %broadcast_multiply_fusion.first_ref, f32[136,512]{1,0:T(8,128)S(1)} %collective-permute-done.mine_ref, f32[136,512]{1,0:T(8,128)S(1)} %collective-permute-done.3.other_ref), custom_call_target="tpu_custom_call" | custom-call | flops 1 | bytes 1 | tf_op jit(solution)/shard_map/spread/pallas_call | solution.py:736
  32.3 2.3 %collective-permute-start.7 = (f32[128,256]{1,0:T(8,128)}, f32[128,256]{1,0:T(8,128)S(1)}, u32[]{:S(2)}, u32[]{:S(2)}) collective-permute-start(f32[128,256]{1,0:T(8,128)} %get-tuple-element.59), channel_id=1, source_target_pairs={{0,4},{1,5},{2,6},{3,7},{4,0},{5,1},{6,2},{7,3},{8,12},{9,13},{10,... | collective-permute-start | bytes 393224 | tf_op jit(solution)/shard_map/ppermute | solution.py:503
  35.9 1.8 %collective-permute-start.6 = (f32[24,2048]{1,0:T(8,128)S(1)}, f32[24,2048]{1,0:T(8,128)S(1)}, u32[]{:S(2)}, u32[]{:S(2)}) collective-permute-start(f32[24,2048]{1,0:T(8,128)S(1)} %pad_maximum_fusion.refs_0_), channel_id=1, source_target_pairs={{0,16},{1,17},{2,18},{3,19},{4,20},{5,21},{6,22},{7,23},{8,24},{9,... | collective-permute-start | bytes 589832 | tf_op jit(solution)/shard_map/ppermute | solution.py:503
  38.5 3.5 %collective-permute-done.8 = f32[128,256]{1,0:T(8,128)S(1)} collective-permute-done((f32[128,256]{1,0:T(8,128)S(1)}, f32[128,256]{1,0:T(8,128)S(1)}, u32[]{:S(2)}, u32[]{:S(2)}) %collective-permute-start.8) | collective-permute-done | bytes 131104 | tf_op jit(solution)/shard_map/ppermute | solution.py:503
  42.9 3.4 %collective-permute-start.10 = (f32[128,256]{1,0:T(8,128)S(1)}, f32[128,256]{1,0:T(8,128)S(1)}, u32[]{:S(2)}, u32[]{:S(2)}) collective-permute-start(f32[128,256]{1,0:T(8,128)S(1)} %add_add_fusion.here_ref), channel_id=1, source_target_pairs={{0,8},{1,9},{2,10},{3,11},{4,12},{5,13},{6,14},{7,15},{8,0},{9,1},... | collective-permute-start | bytes 393224 | tf_op jit(solution)/shard_map/ppermute | solution.py:503
  46.3 4.6 %plane_couple.2.refs_1_ = f32[1024,512]{1,0:T(8,128)S(1)} custom-call(s32[6]{0:T(128)S(1)} %broadcast_multiply_fusion.first_ref, f32[24,2048]{1,0:T(8,128)S(1)} %pad_maximum_fusion.refs_0_), custom_call_target="tpu_custom_call" | custom-call | flops 2147483648 | bytes 2000000 | tf_op jit(solution)/shard_map/plane_couple/pallas_call | solution.py:802
  51.0 2.5 %plane_first.1.a_ref.pulled_ref.old_z_ref = f32[128,256]{1,0:T(8,128)S(1)} custom-call(f32[3]{0:T(128)S(1)} %add_convert_fusion.flag_ref, f32[128,256]{1,0:T(8,128)S(1)} %add_add_fusion.here_ref, f32[128,256]{1,0:T(8,128)S(1)} %collective-permute-done.10.pair_ref, f32[128,256]{1,0:T(8,128)S(1)} %collective-permute-done.11.middle_ref, ...), custom_call_target="tpu_custom_call" | custom-call | flops 1 | bytes 1 | tf_op jit(solution)/shard_map/plane_first/pallas_call | solution.py:929
  56.2 4.9 %plane_couple.3 = (bf16[1024,512]{1,0:T(8,128)(2,1)S(1)}, bf16[1024,512]{1,0:T(8,128)(2,1)S(1)}) custom-call(s32[6]{0:T(128)S(1)} %broadcast_multiply_fusion.first_ref, f32[24,2048]{1,0:T(8,128)S(1)} %collective-permute-done.6.refs_0_, f32[1024,512]{1,0:T(8,128)S(1)} %plane_couple.2.refs_1_), custom_call_target="tpu_custom_call" | custom-call | flops 2147483648 | bytes 2000000 | tf_op jit(solution)/shard_map/plane_couple/pallas_call | solution.py:802
  62.1 2.4 %collective-permute-start.15 = (f32[128,256]{1,0:T(8,128)S(1)}, f32[128,256]{1,0:T(8,128)S(1)}, u32[]{:S(2)}, u32[]{:S(2)}) collective-permute-start(f32[128,256]{1,0:T(8,128)S(1)} %get-tuple-element.71), channel_id=1, source_target_pairs={{0,1},{1,0},{2,3},{3,2},{4,5},{5,4},{6,7},{7,6},{8,9},{9,8},{10,11... | collective-permute-start | bytes 393224 | tf_op jit(solution)/shard_map/ppermute | solution.py:503
  66.2 2.5 %collective-permute-start.16 = (f32[128,256]{1,0:T(8,128)S(1)}, f32[128,256]{1,0:T(8,128)S(1)}, u32[]{:S(2)}, u32[]{:S(2)}) collective-permute-start(f32[128,256]{1,0:T(8,128)S(1)} %add.61.here_ref.old_s_ref), channel_id=1, source_target_pairs={{0,8},{1,9},{2,10},{3,11},{4,12},{5,13},{6,14},{7,15},{8,0},{9,1},... | collective-permute-start | bytes 393224 | tf_op jit(solution)/shard_map/ppermute | solution.py:503
  68.7 3.3 %collective-permute-done.16.pair_ref = f32[128,256]{1,0:T(8,128)S(1)} collective-permute-done((f32[128,256]{1,0:T(8,128)S(1)}, f32[128,256]{1,0:T(8,128)S(1)}, u32[]{:S(2)}, u32[]{:S(2)}) %collective-permute-start.16) | collective-permute-done | bytes 131104 | tf_op jit(solution)/shard_map/ppermute | solution.py:503
  71.9 1.8 %plane_open.1 = (f32[136,256]{1,0:T(8,128)S(1)}, f32[256,256]{1,0:T(8,128)S(1)}) custom-call(f32[3]{0:T(128)S(1)} %add_convert_fusion.flag_ref, f32[128,256]{1,0:T(8,128)S(1)} %add.61.here_ref.old_s_ref, f32[128,256]{1,0:T(8,128)S(1)} %collective-permute-done.16.pair_ref, f32[128,256]{1,0:T(8,128)S(1)} %collective-permute-done.17.middle_ref, ...), custom_call_target="tpu_custom_call" | custom-call | flops 1 | bytes 1 | tf_op jit(solution)/shard_map/plane_open/pallas_call | solution.py:929
  73.8 1.8 %collective-permute-start.20 = (f32[136,256]{1,0:T(8,128)S(1)}, f32[136,256]{1,0:T(8,128)S(1)}, u32[]{:S(2)}, u32[]{:S(2)}) collective-permute-start(f32[136,256]{1,0:T(8,128)S(1)} %get-tuple-element.72.a_ref.pulled_ref), channel_id=1, source_target_pairs={{0,6},{1,7},{2,4},{3,5},{4,2},{5,3},{6,0},{7,1},{8,14},{9,15},{10,... | collective-permute-start | bytes 417800 | tf_op jit(solution)/shard_map/ppermute | solution.py:503
  78.7 4.1 %collective-permute-done.19.c_ref = f32[136,256]{1,0:T(8,128)S(1)} collective-permute-done((f32[136,256]{1,0:T(8,128)S(1)}, f32[136,256]{1,0:T(8,128)S(1)}, u32[]{:S(2)}, u32[]{:S(2)}) %collective-permute-start.19) | collective-permute-done | bytes 139296 | tf_op jit(solution)/shard_map/ppermute | solution.py:503
  86.7 2.9 %collective-permute-start.22 = (f32[136,256]{1,0:T(8,128)S(1)}, f32[136,256]{1,0:T(8,128)S(1)}, u32[]{:S(2)}, u32[]{:S(2)}) collective-permute-start(f32[136,256]{1,0:T(8,128)S(1)} %slice_add_fusion.1.here_ref), channel_id=1, source_target_pairs={{0,8},{1,9},{2,10},{3,11},{4,12},{5,13},{6,14},{7,15},{8,0},{9,1},... | collective-permute-start | bytes 417800 | tf_op jit(solution)/shard_map/ppermute | solution.py:503
  89.7 2.1 %collective-permute-start.24 = (f32[8,256]{1,0:T(8,128)S(1)}, f32[8,256]{1,0:T(8,128)S(1)}, u32[]{:S(2)}, u32[]{:S(2)}) collective-permute-start(f32[8,256]{1,0:T(8,128)S(1)} %slice.23), channel_id=1, source_target_pairs={{0,24},{1,25},{2,26},{3,27},{4,28},{5,29},{6,30},{7,31},{8,16},{9,... | collective-permute-start | bytes 24584 | tf_op jit(solution)/shard_map/ppermute | solution.py:503
  101.5 1.8 %collective-permute-done.27.c_ref = f32[136,256]{1,0:T(8,128)S(1)} collective-permute-done((f32[136,256]{1,0:T(8,128)S(1)}, f32[136,256]{1,0:T(8,128)S(1)}, u32[]{:S(2)}, u32[]{:S(2)}) %collective-permute-start.27) | collective-permute-done | bytes 139296 | tf_op jit(solution)/shard_map/ppermute | solution.py:503
  104.0 3.4 %collective-permute-start.29 = (f32[392,256]{1,0:T(8,128)S(1)}, f32[392,256]{1,0:T(8,128)S(1)}, u32[]{:S(2)}, u32[]{:S(2)}) collective-permute-start(f32[392,256]{1,0:T(8,128)S(1)} %get-tuple-element.82), channel_id=1, source_target_pairs={{0,1},{1,0},{2,3},{3,2},{4,5},{5,4},{6,7},{7,6},{8,9},{9,8},{10,11... | collective-permute-start | bytes 1204232 | tf_op jit(solution)/shard_map/ppermute | solution.py:503
  108.8 2.0 %collective-permute-start.30 = (f32[136,256]{1,0:T(8,128)S(1)}, f32[136,256]{1,0:T(8,128)S(1)}, u32[]{:S(2)}, u32[]{:S(2)}) collective-permute-start(f32[136,256]{1,0:T(8,128)S(1)} %slice_add_fusion.here_ref), channel_id=1, source_target_pairs={{0,8},{1,9},{2,10},{3,11},{4,12},{5,13},{6,14},{7,15},{8,16},{9,17... | collective-permute-start | bytes 417800 | tf_op jit(solution)/shard_map/ppermute | solution.py:503
  110.8 2.0 %plane_rows.5 = (f32[128,512]{1,0:T(8,128)S(1)}, f32[256,256]{1,0:T(8,128)}, f32[256,512]{1,0:T(8,128)S(1)}) custom-call(s32[6]{0:T(128)S(1)} %broadcast_multiply_fusion.first_ref, f32[8,512]{1,0:T(8,128)S(1)} %slice.17.class_ref.meta_ref, f32[8,512]{1,0:T(8,128)S(1)} %slice.18.meta_other_ref, f32[136,256]{1,0:T(8,128)S(1)} %get-tuple-element.78.a_ref.pulled_ref, ...), custom_call_target="tpu_custom_call" | custom-call | flops 1000000000 | bytes 2000000 | tf_op jit(solution)/shard_map/plane_rows/pallas_call | solution.py:885
  114.8 5.8 %all-to-all-start = ((f32[32,8,128]{2,1,0:T(8,128)}), f32[32,8,128]{2,1,0:T(8,128)S(1)}, u32[]{:S(2)}, u32[]{:S(2)}) async-start(f32[32,8,128]{2,1,0:T(8,128)} %plane_close.1), calls=%async_computation | async-start | bytes 262144 | tf_op jit(solution)/shard_map/all_to_all | solution.py:1176
  120.6 8.2 %all-to-all-done.close_ref = f32[32,8,128]{2,1,0:T(8,128)S(1)} async-done(((f32[32,8,128]{2,1,0:T(8,128)}), f32[32,8,128]{2,1,0:T(8,128)S(1)}, u32[]{:S(2)}, u32[]{:S(2)}) %all-to-all-start) | async-done | bytes 131104 | tf_op jit(solution)/shard_map/all_to_all | solution.py:1176
  128.8 1.5 %plane_combine.1 = f32[512,128]{1,0:T(8,128)S(1)} custom-call(f32[8,256]{1,0:T(8,128)S(1)} %get-tuple-element.77.open_ref, f32[32,8,128]{2,1,0:T(8,128)S(1)} %all-to-all-done.close_ref, f32[32,128]{1,0:T(8,128)S(1)} %copy-done.9, f32[256,512]{1,0:T(8,128)S(1)} %get-tuple-element.86.stack_ref, f32[128,512]{1,0:T(8,128)S(1)} %get-tuple-element.87.mine_ref, ...), custom_call_target="tpu_custom_call" | custom-call | flops 1 | bytes 1 | tf_op jit(solution)/shard_map/plane_combine/pallas_call | solution.py:929
  130.3 2.6 %collective-permute-start.32 = (f32[512,128]{1,0:T(8,128)S(1)}, f32[512,128]{1,0:T(8,128)S(1)}, u32[]{:S(2)}, u32[]{:S(2)}) collective-permute-start(f32[512,128]{1,0:T(8,128)S(1)} %plane_combine.1), channel_id=1, source_target_pairs={{0,0},{1,16},{2,8},{3,24},{4,4},{5,20},{6,12},{7,28},{8,1},{9,17},... | collective-permute-start | bytes 786440 | tf_op jit(solution)/shard_map/ppermute | solution.py:503
  132.9 10.7 %collective-permute-done.32.rows_ref = f32[512,128]{1,0:T(8,128)S(1)} collective-permute-done((f32[512,128]{1,0:T(8,128)S(1)}, f32[512,128]{1,0:T(8,128)S(1)}, u32[]{:S(2)}, u32[]{:S(2)}) %collective-permute-start.32) | collective-permute-done | bytes 262176 | tf_op jit(solution)/shard_map/ppermute | solution.py:503
  143.6 2.4 %plane_finish.1 = f32[4096,128]{1,0:T(8,128)} custom-call(f32[512,128]{1,0:T(8,128)S(1)} %collective-permute-done.32.rows_ref, s32[32,16,128]{2,1,0:T(8,128)S(1)} %copy-done.3, f32[4096,128]{1,0:T(8,128)S(1)} %copy-done), custom_call_target="tpu_custom_call" | custom-call | tf_op jit(solution)/shard_map/plane_finish/pallas_call | solution.py:1077
  (94 shorter events, 34.9 us)
Async XLA Ops:
  3.4 7.2 %collective-permute-start.1 = (f32[256,128]{1,0:T(8,128)S(1)}, f32[256,128]{1,0:T(8,128)S(1)}, u32[]{:S(2)}, u32[]{:S(2)}) collective-permute-start(f32[256,128]{1,0:T(8,128)S(1)} %copy-done.10), channel_id=1, source_target_pairs={{1,0},{2,1},{3,2},{5,4},{6,5},{7,6},{9,8},{10,9},{11,10},{13,12},{... | collective-permute-start | bytes 393224 | tf_op jit(solution)/shard_map/ppermute | solution.py:503
  5.4 23.4 %collective-permute-start = (f32[136,512]{1,0:T(8,128)}, f32[136,512]{1,0:T(8,128)S(1)}, u32[]{:S(2)}, u32[]{:S(2)}) collective-permute-start(f32[136,512]{1,0:T(8,128)} %send.1), channel_id=1, source_target_pairs={{0,0},{1,8},{2,16},{3,24},{4,4},{5,12},{6,20},{7,28},{8,2},{9,10},... | collective-permute-start | bytes 835592 | tf_op jit(solution)/shard_map/ppermute | solution.py:503
  12.2 4.4 %collective-permute-start.4 = (f32[24,512]{1,0:T(8,128)S(1)}, f32[24,512]{1,0:T(8,128)S(1)}, u32[]{:S(2)}, u32[]{:S(2)}) collective-permute-start(f32[24,512]{1,0:T(8,128)S(1)} %describe.1), channel_id=1, source_target_pairs={{0,4},{1,5},{2,6},{3,7},{4,0},{5,1},{6,2},{7,3},{8,12},{9,13},{10,... | collective-permute-start | bytes 147464 | tf_op jit(solution)/shard_map/ppermute | solution.py:503
  13.4 15.4 %collective-permute-start.2 = (f32[128,256]{1,0:T(8,128)S(1)}, f32[128,256]{1,0:T(8,128)S(1)}, u32[]{:S(2)}, u32[]{:S(2)}) collective-permute-start(f32[128,256]{1,0:T(8,128)S(1)} %observe.1), channel_id=1, source_target_pairs={{0,0},{1,8},{2,16},{3,24},{4,4},{5,12},{6,20},{7,28},{8,2},{9,10},... | collective-permute-start | bytes 393224 | tf_op jit(solution)/shard_map/ppermute | solution.py:503
  16.5 12.9 %collective-permute-start.5 = (f32[24,1024]{1,0:T(8,128)S(1)}, f32[24,1024]{1,0:T(8,128)S(1)}, u32[]{:S(2)}, u32[]{:S(2)}) collective-permute-start(f32[24,1024]{1,0:T(8,128)S(1)} %pad_maximum_fusion.1), channel_id=1, source_target_pairs={{0,8},{1,9},{2,10},{3,11},{4,12},{5,13},{6,14},{7,15},{8,0},{9,1},... | collective-permute-start | bytes 294920 | tf_op jit(solution)/shard_map/ppermute | solution.py:503
  32.3 6.3 %collective-permute-start.7 = (f32[128,256]{1,0:T(8,128)}, f32[128,256]{1,0:T(8,128)S(1)}, u32[]{:S(2)}, u32[]{:S(2)}) collective-permute-start(f32[128,256]{1,0:T(8,128)} %get-tuple-element.59), channel_id=1, source_target_pairs={{0,4},{1,5},{2,6},{3,7},{4,0},{5,1},{6,2},{7,3},{8,12},{9,13},{10,... | collective-permute-start | bytes 393224 | tf_op jit(solution)/shard_map/ppermute | solution.py:503
  34.6 7.5 %collective-permute-start.8 = (f32[128,256]{1,0:T(8,128)S(1)}, f32[128,256]{1,0:T(8,128)S(1)}, u32[]{:S(2)}, u32[]{:S(2)}) collective-permute-start(f32[128,256]{1,0:T(8,128)S(1)} %get-tuple-element.60), channel_id=1, source_target_pairs={{0,2},{1,3},{2,0},{3,1},{4,6},{5,7},{6,4},{7,5},{8,10},{9,11},{10,... | collective-permute-start | bytes 393224 | tf_op jit(solution)/shard_map/ppermute | solution.py:503
  34.6 7.5 %collective-permute-start.9 = (f32[128,256]{1,0:T(8,128)S(1)}, f32[128,256]{1,0:T(8,128)S(1)}, u32[]{:S(2)}, u32[]{:S(2)}) collective-permute-start(f32[128,256]{1,0:T(8,128)S(1)} %get-tuple-element.61), channel_id=1, source_target_pairs={{0,6},{1,7},{2,4},{3,5},{4,2},{5,3},{6,0},{7,1},{8,14},{9,15},{10,... | collective-permute-start | bytes 393224 | tf_op jit(solution)/shard_map/ppermute | solution.py:503
  35.9 20.4 %collective-permute-start.6 = (f32[24,2048]{1,0:T(8,128)S(1)}, f32[24,2048]{1,0:T(8,128)S(1)}, u32[]{:S(2)}, u32[]{:S(2)}) collective-permute-start(f32[24,2048]{1,0:T(8,128)S(1)} %pad_maximum_fusion.refs_0_), channel_id=1, source_target_pairs={{0,16},{1,17},{2,18},{3,19},{4,20},{5,21},{6,22},{7,23},{8,24},{9,... | collective-permute-start | bytes 589832 | tf_op jit(solution)/shard_map/ppermute | solution.py:503
  42.1 8.8 %collective-permute-start.11 = (f32[128,256]{1,0:T(8,128)S(1)}, f32[128,256]{1,0:T(8,128)S(1)}, u32[]{:S(2)}, u32[]{:S(2)}) collective-permute-start(f32[128,256]{1,0:T(8,128)S(1)} %add_add_fusion.here_ref), channel_id=1, source_target_pairs={{8,16},{9,17},{10,18},{11,19},{12,20},{13,21},{14,22},{15,23},{16,... | collective-permute-start | bytes 393224 | tf_op jit(solution)/shard_map/ppermute | solution.py:503
  42.9 8.0 %collective-permute-start.10 = (f32[128,256]{1,0:T(8,128)S(1)}, f32[128,256]{1,0:T(8,128)S(1)}, u32[]{:S(2)}, u32[]{:S(2)}) collective-permute-start(f32[128,256]{1,0:T(8,128)S(1)} %add_add_fusion.here_ref), channel_id=1, source_target_pairs={{0,8},{1,9},{2,10},{3,11},{4,12},{5,13},{6,14},{7,15},{8,0},{9,1},... | collective-permute-start | bytes 393224 | tf_op jit(solution)/shard_map/ppermute | solution.py:503
  53.5 7.7 %collective-permute-start.14 = (f32[128,256]{1,0:T(8,128)S(1)}, f32[128,256]{1,0:T(8,128)S(1)}, u32[]{:S(2)}, u32[]{:S(2)}) collective-permute-start(f32[128,256]{1,0:T(8,128)S(1)} %plane_first.1.a_ref.pulled_ref.old_z_ref), channel_id=1, source_target_pairs={{0,6},{1,7},{2,4},{3,5},{4,2},{5,3},{6,0},{7,1},{8,14},{9,15},{10,... | collective-permute-start | bytes 393224 | tf_op jit(solution)/shard_map/ppermute | solution.py:503
  54.6 6.9 %collective-permute-start.13 = (f32[128,256]{1,0:T(8,128)S(1)}, f32[128,256]{1,0:T(8,128)S(1)}, u32[]{:S(2)}, u32[]{:S(2)}) collective-permute-start(f32[128,256]{1,0:T(8,128)S(1)} %plane_first.1.a_ref.pulled_ref.old_z_ref), channel_id=1, source_target_pairs={{0,2},{1,3},{2,0},{3,1},{4,6},{5,7},{6,4},{7,5},{8,10},{9,11},{10,... | collective-permute-start | bytes 393224 | tf_op jit(solution)/shard_map/ppermute | solution.py:503
  56.0 5.6 %collective-permute-start.12 = (f32[128,256]{1,0:T(8,128)S(1)}, f32[128,256]{1,0:T(8,128)S(1)}, u32[]{:S(2)}, u32[]{:S(2)}) collective-permute-start(f32[128,256]{1,0:T(8,128)S(1)} %plane_first.1.a_ref.pulled_ref.old_z_ref), channel_id=1, source_target_pairs={{0,4},{1,5},{2,6},{3,7},{4,0},{5,1},{6,2},{7,3},{8,12},{9,13},{10,... | collective-permute-start | bytes 393224 | tf_op jit(solution)/shard_map/ppermute | solution.py:503
  62.1 3.3 %collective-permute-start.15 = (f32[128,256]{1,0:T(8,128)S(1)}, f32[128,256]{1,0:T(8,128)S(1)}, u32[]{:S(2)}, u32[]{:S(2)}) collective-permute-start(f32[128,256]{1,0:T(8,128)S(1)} %get-tuple-element.71), channel_id=1, source_target_pairs={{0,1},{1,0},{2,3},{3,2},{4,5},{5,4},{6,7},{7,6},{8,9},{9,8},{10,11... | collective-permute-start | bytes 393224 | tf_op jit(solution)/shard_map/ppermute | solution.py:503
  65.5 3.2 %collective-permute-start.17 = (f32[128,256]{1,0:T(8,128)S(1)}, f32[128,256]{1,0:T(8,128)S(1)}, u32[]{:S(2)}, u32[]{:S(2)}) collective-permute-start(f32[128,256]{1,0:T(8,128)S(1)} %add.61.here_ref.old_s_ref), channel_id=1, source_target_pairs={{8,16},{9,17},{10,18},{11,19},{12,20},{13,21},{14,22},{15,23},{16,... | collective-permute-start | bytes 393224 | tf_op jit(solution)/shard_map/ppermute | solution.py:503
  66.2 5.7 %collective-permute-start.16 = (f32[128,256]{1,0:T(8,128)S(1)}, f32[128,256]{1,0:T(8,128)S(1)}, u32[]{:S(2)}, u32[]{:S(2)}) collective-permute-start(f32[128,256]{1,0:T(8,128)S(1)} %add.61.here_ref.old_s_ref), channel_id=1, source_target_pairs={{0,8},{1,9},{2,10},{3,11},{4,12},{5,13},{6,14},{7,15},{8,0},{9,1},... | collective-permute-start | bytes 393224 | tf_op jit(solution)/shard_map/ppermute | solution.py:503
  73.8 4.9 %collective-permute-start.20 = (f32[136,256]{1,0:T(8,128)S(1)}, f32[136,256]{1,0:T(8,128)S(1)}, u32[]{:S(2)}, u32[]{:S(2)}) collective-permute-start(f32[136,256]{1,0:T(8,128)S(1)} %get-tuple-element.72.a_ref.pulled_ref), channel_id=1, source_target_pairs={{0,6},{1,7},{2,4},{3,5},{4,2},{5,3},{6,0},{7,1},{8,14},{9,15},{10,... | collective-permute-start | bytes 417800 | tf_op jit(solution)/shard_map/ppermute | solution.py:503
  75.5 7.2 %collective-permute-start.19 = (f32[136,256]{1,0:T(8,128)S(1)}, f32[136,256]{1,0:T(8,128)S(1)}, u32[]{:S(2)}, u32[]{:S(2)}) collective-permute-start(f32[136,256]{1,0:T(8,128)S(1)} %get-tuple-element.72.a_ref.pulled_ref), channel_id=1, source_target_pairs={{0,2},{1,3},{2,0},{3,1},{4,6},{5,7},{6,4},{7,5},{8,10},{9,11},{10,... | collective-permute-start | bytes 417800 | tf_op jit(solution)/shard_map/ppermute | solution.py:503
  76.5 6.3 %collective-permute-start.18 = (f32[136,256]{1,0:T(8,128)S(1)}, f32[136,256]{1,0:T(8,128)S(1)}, u32[]{:S(2)}, u32[]{:S(2)}) collective-permute-start(f32[136,256]{1,0:T(8,128)S(1)} %get-tuple-element.72.a_ref.pulled_ref), channel_id=1, source_target_pairs={{0,4},{1,5},{2,6},{3,7},{4,0},{5,1},{6,2},{7,3},{8,12},{9,13},{10,... | collective-permute-start | bytes 417800 | tf_op jit(solution)/shard_map/ppermute | solution.py:503
  85.9 5.9 %collective-permute-start.25 = (f32[136,256]{1,0:T(8,128)S(1)}, f32[136,256]{1,0:T(8,128)S(1)}, u32[]{:S(2)}, u32[]{:S(2)}) collective-permute-start(f32[136,256]{1,0:T(8,128)S(1)} %slice_add_fusion.1.here_ref), channel_id=1, source_target_pairs={{8,16},{9,17},{10,18},{11,19},{12,20},{13,21},{14,22},{15,23},{16,... | collective-permute-start | bytes 417800 | tf_op jit(solution)/shard_map/ppermute | solution.py:503
  86.7 6.4 %collective-permute-start.22 = (f32[136,256]{1,0:T(8,128)S(1)}, f32[136,256]{1,0:T(8,128)S(1)}, u32[]{:S(2)}, u32[]{:S(2)}) collective-permute-start(f32[136,256]{1,0:T(8,128)S(1)} %slice_add_fusion.1.here_ref), channel_id=1, source_target_pairs={{0,8},{1,9},{2,10},{3,11},{4,12},{5,13},{6,14},{7,15},{8,0},{9,1},... | collective-permute-start | bytes 417800 | tf_op jit(solution)/shard_map/ppermute | solution.py:503
  89.7 5.1 %collective-permute-start.24 = (f32[8,256]{1,0:T(8,128)S(1)}, f32[8,256]{1,0:T(8,128)S(1)}, u32[]{:S(2)}, u32[]{:S(2)}) collective-permute-start(f32[8,256]{1,0:T(8,128)S(1)} %slice.23), channel_id=1, source_target_pairs={{0,24},{1,25},{2,26},{3,27},{4,28},{5,29},{6,30},{7,31},{8,16},{9,... | collective-permute-start | bytes 24584 | tf_op jit(solution)/shard_map/ppermute | solution.py:503
  91.8 3.4 %collective-permute-start.23 = (f32[8,256]{1,0:T(8,128)S(1)}, f32[8,256]{1,0:T(8,128)S(1)}, u32[]{:S(2)}, u32[]{:S(2)}) collective-permute-start(f32[8,256]{1,0:T(8,128)S(1)} %slice.23), channel_id=1, source_target_pairs={{0,16},{1,17},{2,18},{3,19},{4,20},{5,21},{6,22},{7,23},{8,24},{9,... | collective-permute-start | bytes 24584 | tf_op jit(solution)/shard_map/ppermute | solution.py:503
  96.5 5.0 %collective-permute-start.28 = (f32[136,256]{1,0:T(8,128)S(1)}, f32[136,256]{1,0:T(8,128)S(1)}, u32[]{:S(2)}, u32[]{:S(2)}) collective-permute-start(f32[136,256]{1,0:T(8,128)S(1)} %get-tuple-element.78.a_ref.pulled_ref), channel_id=1, source_target_pairs={{0,6},{1,7},{2,4},{3,5},{4,2},{5,3},{6,0},{7,1},{8,14},{9,15},{10,... | collective-permute-start | bytes 417800 | tf_op jit(solution)/shard_map/ppermute | solution.py:503
  97.8 5.5 %collective-permute-start.27 = (f32[136,256]{1,0:T(8,128)S(1)}, f32[136,256]{1,0:T(8,128)S(1)}, u32[]{:S(2)}, u32[]{:S(2)}) collective-permute-start(f32[136,256]{1,0:T(8,128)S(1)} %get-tuple-element.78.a_ref.pulled_ref), channel_id=1, source_target_pairs={{0,2},{1,3},{2,0},{3,1},{4,6},{5,7},{6,4},{7,5},{8,10},{9,11},{10,... | collective-permute-start | bytes 417800 | tf_op jit(solution)/shard_map/ppermute | solution.py:503
  98.8 4.6 %collective-permute-start.26 = (f32[136,256]{1,0:T(8,128)S(1)}, f32[136,256]{1,0:T(8,128)S(1)}, u32[]{:S(2)}, u32[]{:S(2)}) collective-permute-start(f32[136,256]{1,0:T(8,128)S(1)} %get-tuple-element.78.a_ref.pulled_ref), channel_id=1, source_target_pairs={{0,4},{1,5},{2,6},{3,7},{4,0},{5,1},{6,2},{7,3},{8,12},{9,13},{10,... | collective-permute-start | bytes 417800 | tf_op jit(solution)/shard_map/ppermute | solution.py:503
  104.0 4.8 %collective-permute-start.29 = (f32[392,256]{1,0:T(8,128)S(1)}, f32[392,256]{1,0:T(8,128)S(1)}, u32[]{:S(2)}, u32[]{:S(2)}) collective-permute-start(f32[392,256]{1,0:T(8,128)S(1)} %get-tuple-element.82), channel_id=1, source_target_pairs={{0,1},{1,0},{2,3},{3,2},{4,5},{5,4},{6,7},{7,6},{8,9},{9,8},{10,11... | collective-permute-start | bytes 1204232 | tf_op jit(solution)/shard_map/ppermute | solution.py:503
  108.8 4.6 %collective-permute-start.30 = (f32[136,256]{1,0:T(8,128)S(1)}, f32[136,256]{1,0:T(8,128)S(1)}, u32[]{:S(2)}, u32[]{:S(2)}) collective-permute-start(f32[136,256]{1,0:T(8,128)S(1)} %slice_add_fusion.here_ref), channel_id=1, source_target_pairs={{0,8},{1,9},{2,10},{3,11},{4,12},{5,13},{6,14},{7,15},{8,16},{9,17... | collective-permute-start | bytes 417800 | tf_op jit(solution)/shard_map/ppermute | solution.py:503
  112.8 7.8 %collective-permute-start.31 = (f32[256,256]{1,0:T(8,128)}, f32[256,256]{1,0:T(8,128)}, u32[]{:S(2)}, u32[]{:S(2)}) collective-permute-start(f32[256,256]{1,0:T(8,128)} %get-tuple-element.88), channel_id=1, source_target_pairs={{0,1},{1,0},{2,3},{3,2},{4,5},{5,4},{6,7},{7,6},{8,9},{9,8},{10,11... | collective-permute-start | bytes 786440 | tf_op jit(solution)/shard_map/ppermute | solution.py:503
  114.8 14.0 %all-to-all-start = ((f32[32,8,128]{2,1,0:T(8,128)}), f32[32,8,128]{2,1,0:T(8,128)S(1)}, u32[]{:S(2)}, u32[]{:S(2)}) async-start(f32[32,8,128]{2,1,0:T(8,128)} %plane_close.1), calls=%async_computation | async-start | bytes 262144 | tf_op jit(solution)/shard_map/all_to_all | solution.py:1176
  130.3 13.3 %collective-permute-start.32 = (f32[512,128]{1,0:T(8,128)S(1)}, f32[512,128]{1,0:T(8,128)S(1)}, u32[]{:S(2)}, u32[]{:S(2)}) collective-permute-start(f32[512,128]{1,0:T(8,128)S(1)} %plane_combine.1), channel_id=1, source_target_pairs={{0,0},{1,16},{2,8},{3,24},{4,4},{5,20},{6,12},{7,28},{8,1},{9,17},... | collective-permute-start | bytes 786440 | tf_op jit(solution)/shard_map/ppermute | solution.py:503
  (15 other events, 156.1 us)

commit v17 on v13

--- a/solution.py
+++ b/solution.py
@@ -1079,16 +1079,18 @@
     forward3, inverse_first3, inverse_last3, short3 = turned_transforms(3)
     block, noted = (hours, rows), (hours + NOTE, rows)
 
-    parcel = send(incidence, first_guess, row_gauge, gauge_kernel)
-    parcel, near, gauges, kinds, seen = lax.optimization_barrier(
-        (parcel, incidence, row_gauge, gauge_kernel, observed)
-    )
+    seen = observe(
+        observed, moved(observed, hour_before), gauge_kernel, kernels, short3, [forward3, inverse_first3]
+    )
+    seen, field = lax.optimization_barrier((seen, first_guess))
+    seen = moved(seen, to_plane)
+    parcel = send(incidence, field, row_gauge, gauge_kernel)
+    parcel, near = lax.optimization_barrier((parcel, incidence))
     parcel = moved(parcel, to_plane)
-    meta = describe(near, gauges)
+    near, seen = lax.optimization_barrier((near, seen))
+    meta = describe(near, row_gauge)
     meta = jnp.concatenate([meta, moved(meta, over_x)], axis=1)
     meta = jnp.concatenate([meta, moved(meta, z_pair)], axis=1)
-    seen = observe(seen, moved(seen, hour_before), kinds, kernels, short3, [forward3, inverse_first3])
-    seen = moved(seen, to_plane)
     parcel, seen = lax.optimization_barrier((parcel, seen))
     parcels = [parcel, moved(parcel, over_core)]
     spec = plane_spectrum(parcel[hours:], kernels, short3, rows)

time: 146 us -> 153 us (1.048)
  waiting for transfers between devices: 51.5 us -> 58.5 us
  starting transfers between devices: 56.3 us -> 52.4 us
  local copies, waits for them, and re-layouts: 4.04 us -> 7.84 us
    ppermute x33, waiting for transfers between devices: 43.3 us -> 50.3 us  [moved(): return lax.ppermute(value, ('basin', 'tm'), pairs)]
    ppermute x33, starting transfers between devices: 50.5 us -> 46.6 us  [moved(): return lax.ppermute(value, ('basin', 'tm'), pairs)]
    unnamed x30 -> x38, local copies, waits for them, and re-layouts: 3.95 us -> 7.75 us
  transfers between devices with their start and end apart: 34 -> 34, of which waited for: 20 -> 18; matrix products, arithmetic and copies ran while one was open for 0% -> 0% of each run, Pallas kernels for 15% -> 13%
where the time goes in v17:
time: 153 us; the launch traced here: 152 us
  waiting for transfers between devices  58.5 us (38%)
  starting transfers between devices  52.4 us (34%)
  Pallas kernels  33.1 us (22%)
  local copies, waits for them, and re-layouts  7.84 us (5%)
    ppermute x33, waiting for transfers between devices, moved(): return lax.ppermute(value, ('basin', 'tm'), pairs)  50.3 us
    ppermute x33, starting transfers between devices, moved(): return lax.ppermute(value, ('basin', 'tm'), pairs)  46.6 us
    pallas_call x6, Pallas kernels, plane_call(): pl.pallas_call(kernel, in_specs=[pl.BlockSpec(memory_space=pltpu.SMEM)] *...  9.8 us
    pallas_call x2, Pallas kernels, plane_couple(): pl.pallas_call(functools.partial(plane_couple_kernel, last), in_specs=[pl...  9.56 us
    all_to_all x1, waiting for transfers between devices, plane_shards(): close_note = lax.all_to_all(note, ('basin', 'tm'), 0, 0, tiled=False)  8.18 us
    unnamed x38, local copies, waits for them, and re-layouts  7.75 us
    all_to_all x1, starting transfers between devices, plane_shards(): close_note = lax.all_to_all(note, ('basin', 'tm'), 0, 0, tiled=False)  5.84 us
    pallas_call x3, Pallas kernels, plane_rows(): pl.pallas_call(plane_rows_kernel, in_specs=[pl.BlockSpec(memory_space=plt...  4.5 us
  transfers between devices with their start and end apart: 34, of which 18 were waited for; matrix products, arithmetic and copies ran while one was open for 0% of the time, Pallas kernels for 13%

profile of v17, /device:TPU:1, one launch (start us, length us, event | category | flops | bytes accessed | tf_op | source)
XLA Modules:
  0.0 152.5 jit_solution(11541180947863033916)
XLA Ops:
  0.0 2.0 %collective-permute-start = (f32[256,128]{1,0:T(8,128)}, f32[256,128]{1,0:T(8,128)S(1)}, u32[]{:S(2)}, u32[]{:S(2)}) collective-permute-start(f32[256,128]{1,0:T(8,128)} %seen_ref.1), channel_id=1, source_target_pairs={{1,0},{2,1},{3,2},{5,4},{6,5},{7,6},{9,8},{10,9},{11,10},{13,12},{... | collective-permute-start | bytes 393224 | tf_op jit(solution)/shard_map/ppermute | solution.py:503
  2.0 5.4 %collective-permute-done.later_ref = f32[256,128]{1,0:T(8,128)S(1)} collective-permute-done((f32[256,128]{1,0:T(8,128)}, f32[256,128]{1,0:T(8,128)S(1)}, u32[]{:S(2)}, u32[]{:S(2)}) %collective-permute-start) | collective-permute-done | bytes 131104 | tf_op jit(solution)/shard_map/ppermute | solution.py:503
  14.1 1.9 %collective-permute-start.2 = (f32[128,256]{1,0:T(8,128)S(1)}, f32[128,256]{1,0:T(8,128)S(1)}, u32[]{:S(2)}, u32[]{:S(2)}) collective-permute-start(f32[128,256]{1,0:T(8,128)S(1)} %observe.1), channel_id=1, source_target_pairs={{0,0},{1,8},{2,16},{3,24},{4,4},{5,12},{6,20},{7,28},{8,2},{9,10},... | collective-permute-start | bytes 393224 | tf_op jit(solution)/shard_map/ppermute | solution.py:503
  16.1 1.6 %copy-done = f32[4096,128]{1,0:T(8,128)S(1)} copy-done((f32[4096,128]{1,0:T(8,128)S(1)}, f32[4096,128]{1,0:T(8,128)}, u32[]{:S(2)}) %copy-start) | copy-done | bytes 2097176
  19.7 3.3 %collective-permute-start.1 = (f32[136,512]{1,0:T(8,128)S(1)}, f32[136,512]{1,0:T(8,128)S(1)}, u32[]{:S(2)}, u32[]{:S(2)}) collective-permute-start(f32[136,512]{1,0:T(8,128)S(1)} %send.1), channel_id=1, source_target_pairs={{0,0},{1,8},{2,16},{3,24},{4,4},{5,12},{6,20},{7,28},{8,2},{9,10},... | collective-permute-start | bytes 835592 | tf_op jit(solution)/shard_map/ppermute | solution.py:503
  23.1 1.5 collective-permute-done.2.seen_ref
  26.2 1.6 %collective-permute-done.4 = f32[24,512]{1,0:T(8,128)S(1)} collective-permute-done((f32[24,512]{1,0:T(8,128)S(1)}, f32[24,512]{1,0:T(8,128)S(1)}, u32[]{:S(2)}, u32[]{:S(2)}) %collective-permute-start.4) | collective-permute-done | bytes 49184 | tf_op jit(solution)/shard_map/ppermute | solution.py:503
  28.8 8.2 %collective-permute-done.1.mine_ref = f32[136,512]{1,0:T(8,128)S(1)} collective-permute-done((f32[136,512]{1,0:T(8,128)S(1)}, f32[136,512]{1,0:T(8,128)S(1)}, u32[]{:S(2)}, u32[]{:S(2)}) %collective-permute-start.1) | collective-permute-done | bytes 278560 | tf_op jit(solution)/shard_map/ppermute | solution.py:503
  38.6 1.6 %spread.1 = (f32[128,256]{1,0:T(8,128)S(1)}, f32[128,256]{1,0:T(8,128)S(1)}, f32[128,256]{1,0:T(8,128)S(1)}, f32[128,256]{1,0:T(8,128)S(1)}) custom-call(s32[6]{0:T(128)S(1)} %broadcast_multiply_fusion.first_ref, f32[136,512]{1,0:T(8,128)S(1)} %collective-permute-done.1.mine_ref, f32[136,512]{1,0:T(8,128)S(1)} %collective-permute-done.3.other_ref), custom_call_target="tpu_custom_call" | custom-call | flops 1 | bytes 1 | tf_op jit(solution)/shard_map/spread/pallas_call | solution.py:714
  45.1 3.7 %collective-permute-done.8 = f32[128,256]{1,0:T(8,128)S(1)} collective-permute-done((f32[128,256]{1,0:T(8,128)S(1)}, f32[128,256]{1,0:T(8,128)S(1)}, u32[]{:S(2)}, u32[]{:S(2)}) %collective-permute-start.8) | collective-permute-done | bytes 131104 | tf_op jit(solution)/shard_map/ppermute | solution.py:503
  49.7 2.6 %collective-permute-start.10 = (f32[128,256]{1,0:T(8,128)S(1)}, f32[128,256]{1,0:T(8,128)S(1)}, u32[]{:S(2)}, u32[]{:S(2)}) collective-permute-start(f32[128,256]{1,0:T(8,128)S(1)} %add_add_fusion.here_ref), channel_id=1, source_target_pairs={{0,8},{1,9},{2,10},{3,11},{4,12},{5,13},{6,14},{7,15},{8,0},{9,1},... | collective-permute-start | bytes 393224 | tf_op jit(solution)/shard_map/ppermute | solution.py:503
  52.3 4.6 %plane_couple.2.refs_1_ = f32[1024,512]{1,0:T(8,128)S(1)} custom-call(s32[6]{0:T(128)S(1)} %broadcast_multiply_fusion.first_ref, f32[24,2048]{1,0:T(8,128)S(1)} %pad_maximum_fusion.refs_0_), custom_call_target="tpu_custom_call" | custom-call | flops 2147483648 | bytes 2000000 | tf_op jit(solution)/shard_map/plane_couple/pallas_call | solution.py:780
  57.0 2.6 %plane_first.1.a_ref.pulled_ref.old_z_ref = f32[128,256]{1,0:T(8,128)S(1)} custom-call(f32[3]{0:T(128)S(1)} %add_convert_fusion.flag_ref, f32[128,256]{1,0:T(8,128)S(1)} %add_add_fusion.here_ref, f32[128,256]{1,0:T(8,128)S(1)} %collective-permute-done.10.pair_ref, f32[128,256]{1,0:T(8,128)S(1)} %collective-permute-done.11.middle_ref, ...), custom_call_target="tpu_custom_call" | custom-call | flops 1 | bytes 1 | tf_op jit(solution)/shard_map/plane_first/pallas_call | solution.py:907
  59.6 1.5 collective-permute-start.14
  62.3 4.9 %plane_couple.3 = (bf16[1024,512]{1,0:T(8,128)(2,1)S(1)}, bf16[1024,512]{1,0:T(8,128)(2,1)S(1)}) custom-call(s32[6]{0:T(128)S(1)} %broadcast_multiply_fusion.first_ref, f32[24,2048]{1,0:T(8,128)S(1)} %collective-permute-done.6.refs_0_, f32[1024,512]{1,0:T(8,128)S(1)} %plane_couple.2.refs_1_), custom_call_target="tpu_custom_call" | custom-call | flops 2147483648 | bytes 2000000 | tf_op jit(solution)/shard_map/plane_couple/pallas_call | solution.py:780
  67.9 2.9 %collective-permute-start.15 = (f32[128,256]{1,0:T(8,128)S(1)}, f32[128,256]{1,0:T(8,128)S(1)}, u32[]{:S(2)}, u32[]{:S(2)}) collective-permute-start(f32[128,256]{1,0:T(8,128)S(1)} %get-tuple-element.69), channel_id=1, source_target_pairs={{0,1},{1,0},{2,3},{3,2},{4,5},{5,4},{6,7},{7,6},{8,9},{9,8},{10,11... | collective-permute-start | bytes 393224 | tf_op jit(solution)/shard_map/ppermute | solution.py:503
  73.9 3.4 %collective-permute-done.16.pair_ref = f32[128,256]{1,0:T(8,128)S(1)} collective-permute-done((f32[128,256]{1,0:T(8,128)S(1)}, f32[128,256]{1,0:T(8,128)S(1)}, u32[]{:S(2)}, u32[]{:S(2)}) %collective-permute-start.16) | collective-permute-done | bytes 131104 | tf_op jit(solution)/shard_map/ppermute | solution.py:503
  77.3 1.8 %plane_open.1 = (f32[136,256]{1,0:T(8,128)S(1)}, f32[256,256]{1,0:T(8,128)S(1)}) custom-call(f32[3]{0:T(128)S(1)} %add_convert_fusion.flag_ref, f32[128,256]{1,0:T(8,128)S(1)} %add.61.here_ref.old_s_ref, f32[128,256]{1,0:T(8,128)S(1)} %collective-permute-done.16.pair_ref, f32[128,256]{1,0:T(8,128)S(1)} %collective-permute-done.17.middle_ref, ...), custom_call_target="tpu_custom_call" | custom-call | flops 1 | bytes 1 | tf_op jit(solution)/shard_map/plane_open/pallas_call | solution.py:907
  79.1 2.3 %collective-permute-start.20 = (f32[136,256]{1,0:T(8,128)S(1)}, f32[136,256]{1,0:T(8,128)S(1)}, u32[]{:S(2)}, u32[]{:S(2)}) collective-permute-start(f32[136,256]{1,0:T(8,128)S(1)} %get-tuple-element.70.a_ref.pulled_ref), channel_id=1, source_target_pairs={{0,6},{1,7},{2,4},{3,5},{4,2},{5,3},{6,0},{7,1},{8,14},{9,15},{10,... | collective-permute-start | bytes 417800 | tf_op jit(solution)/shard_map/ppermute | solution.py:503
  84.0 4.1 %collective-permute-done.19.c_ref = f32[136,256]{1,0:T(8,128)S(1)} collective-permute-done((f32[136,256]{1,0:T(8,128)S(1)}, f32[136,256]{1,0:T(8,128)S(1)}, u32[]{:S(2)}, u32[]{:S(2)}) %collective-permute-start.19) | collective-permute-done | bytes 139296 | tf_op jit(solution)/shard_map/ppermute | solution.py:503
  92.3 3.7 %collective-permute-start.22 = (f32[136,256]{1,0:T(8,128)S(1)}, f32[136,256]{1,0:T(8,128)S(1)}, u32[]{:S(2)}, u32[]{:S(2)}) collective-permute-start(f32[136,256]{1,0:T(8,128)S(1)} %slice_add_fusion.1.here_ref), channel_id=1, source_target_pairs={{0,8},{1,9},{2,10},{3,11},{4,12},{5,13},{6,14},{7,15},{8,0},{9,1},... | collective-permute-start | bytes 417800 | tf_op jit(solution)/shard_map/ppermute | solution.py:503
  97.3 2.2 %collective-permute-done.22.pair_ref = f32[136,256]{1,0:T(8,128)S(1)} collective-permute-done((f32[136,256]{1,0:T(8,128)S(1)}, f32[136,256]{1,0:T(8,128)S(1)}, u32[]{:S(2)}, u32[]{:S(2)}) %collective-permute-start.22) | collective-permute-done | bytes 139296 | tf_op jit(solution)/shard_map/ppermute | solution.py:503
  107.1 2.0 %collective-permute-done.27.c_ref = f32[136,256]{1,0:T(8,128)S(1)} collective-permute-done((f32[136,256]{1,0:T(8,128)S(1)}, f32[136,256]{1,0:T(8,128)S(1)}, u32[]{:S(2)}, u32[]{:S(2)}) %collective-permute-start.27) | collective-permute-done | bytes 139296 | tf_op jit(solution)/shard_map/ppermute | solution.py:503
  109.6 3.2 %collective-permute-start.29 = (f32[392,256]{1,0:T(8,128)S(1)}, f32[392,256]{1,0:T(8,128)S(1)}, u32[]{:S(2)}, u32[]{:S(2)}) collective-permute-start(f32[392,256]{1,0:T(8,128)S(1)} %get-tuple-element.80), channel_id=1, source_target_pairs={{0,1},{1,0},{2,3},{3,2},{4,5},{5,4},{6,7},{7,6},{8,9},{9,8},{10,11... | collective-permute-start | bytes 1204232 | tf_op jit(solution)/shard_map/ppermute | solution.py:503
  114.2 3.0 %collective-permute-start.30 = (f32[136,256]{1,0:T(8,128)S(1)}, f32[136,256]{1,0:T(8,128)S(1)}, u32[]{:S(2)}, u32[]{:S(2)}) collective-permute-start(f32[136,256]{1,0:T(8,128)S(1)} %slice_add_fusion.here_ref), channel_id=1, source_target_pairs={{0,8},{1,9},{2,10},{3,11},{4,12},{5,13},{6,14},{7,15},{8,16},{9,17... | collective-permute-start | bytes 417800 | tf_op jit(solution)/shard_map/ppermute | solution.py:503
  117.2 2.0 %plane_rows.5 = (f32[128,512]{1,0:T(8,128)S(1)}, f32[256,256]{1,0:T(8,128)}, f32[256,512]{1,0:T(8,128)S(1)}) custom-call(s32[6]{0:T(128)S(1)} %broadcast_multiply_fusion.first_ref, f32[8,512]{1,0:T(8,128)S(1)} %slice.17.class_ref.meta_ref, f32[8,512]{1,0:T(8,128)S(1)} %slice.18.meta_other_ref, f32[136,256]{1,0:T(8,128)S(1)} %get-tuple-element.76.a_ref.pulled_ref, ...), custom_call_target="tpu_custom_call" | custom-call | flops 1000000000 | bytes 2000000 | tf_op jit(solution)/shard_map/plane_rows/pallas_call | solution.py:863
  121.2 5.8 %all-to-all-start = ((f32[32,8,128]{2,1,0:T(8,128)}), f32[32,8,128]{2,1,0:T(8,128)S(1)}, u32[]{:S(2)}, u32[]{:S(2)}) async-start(f32[32,8,128]{2,1,0:T(8,128)} %plane_close.1), calls=%async_computation | async-start | bytes 262144 | tf_op jit(solution)/shard_map/all_to_all | solution.py:1155
  127.1 8.2 %all-to-all-done.close_ref = f32[32,8,128]{2,1,0:T(8,128)S(1)} async-done(((f32[32,8,128]{2,1,0:T(8,128)}), f32[32,8,128]{2,1,0:T(8,128)S(1)}, u32[]{:S(2)}, u32[]{:S(2)}) %all-to-all-start) | async-done | bytes 131104 | tf_op jit(solution)/shard_map/all_to_all | solution.py:1155
  135.3 1.5 plane_combine.1
  136.8 2.6 %collective-permute-start.32 = (f32[512,128]{1,0:T(8,128)S(1)}, f32[512,128]{1,0:T(8,128)S(1)}, u32[]{:S(2)}, u32[]{:S(2)}) collective-permute-start(f32[512,128]{1,0:T(8,128)S(1)} %plane_combine.1), channel_id=1, source_target_pairs={{0,0},{1,16},{2,8},{3,24},{4,4},{5,20},{6,12},{7,28},{8,1},{9,17},... | collective-permute-start | bytes 786440 | tf_op jit(solution)/shard_map/ppermute | solution.py:503
  139.4 10.7 %collective-permute-done.32.rows_ref = f32[512,128]{1,0:T(8,128)S(1)} collective-permute-done((f32[512,128]{1,0:T(8,128)S(1)}, f32[512,128]{1,0:T(8,128)S(1)}, u32[]{:S(2)}, u32[]{:S(2)}) %collective-permute-start.32) | collective-permute-done | bytes 262176 | tf_op jit(solution)/shard_map/ppermute | solution.py:503
  150.1 2.4 %plane_finish.1 = f32[4096,128]{1,0:T(8,128)} custom-call(f32[512,128]{1,0:T(8,128)S(1)} %collective-permute-done.32.rows_ref, s32[32,16,128]{2,1,0:T(8,128)S(1)} %copy-done.5, f32[4096,128]{1,0:T(8,128)S(1)} %copy-done.1), custom_call_target="tpu_custom_call" | custom-call | tf_op jit(solution)/shard_map/plane_finish/pallas_call | solution.py:1055
  (106 shorter events, 43.3 us)
Async XLA Ops:
  0.0 7.4 %collective-permute-start = (f32[256,128]{1,0:T(8,128)}, f32[256,128]{1,0:T(8,128)S(1)}, u32[]{:S(2)}, u32[]{:S(2)}) collective-permute-start(f32[256,128]{1,0:T(8,128)} %seen_ref.1), channel_id=1, source_target_pairs={{1,0},{2,1},{3,2},{5,4},{6,5},{7,6},{9,8},{10,9},{11,10},{13,12},{... | collective-permute-start | bytes 393224 | tf_op jit(solution)/shard_map/ppermute | solution.py:503
  14.1 10.5 %collective-permute-start.2 = (f32[128,256]{1,0:T(8,128)S(1)}, f32[128,256]{1,0:T(8,128)S(1)}, u32[]{:S(2)}, u32[]{:S(2)}) collective-permute-start(f32[128,256]{1,0:T(8,128)S(1)} %observe.1), channel_id=1, source_target_pairs={{0,0},{1,8},{2,16},{3,24},{4,4},{5,12},{6,20},{7,28},{8,2},{9,10},... | collective-permute-start | bytes 393224 | tf_op jit(solution)/shard_map/ppermute | solution.py:503
  19.7 17.3 %collective-permute-start.1 = (f32[136,512]{1,0:T(8,128)S(1)}, f32[136,512]{1,0:T(8,128)S(1)}, u32[]{:S(2)}, u32[]{:S(2)}) collective-permute-start(f32[136,512]{1,0:T(8,128)S(1)} %send.1), channel_id=1, source_target_pairs={{0,0},{1,8},{2,16},{3,24},{4,4},{5,12},{6,20},{7,28},{8,2},{9,10},... | collective-permute-start | bytes 835592 | tf_op jit(solution)/shard_map/ppermute | solution.py:503
  24.8 3.0 %collective-permute-start.4 = (f32[24,512]{1,0:T(8,128)S(1)}, f32[24,512]{1,0:T(8,128)S(1)}, u32[]{:S(2)}, u32[]{:S(2)}) collective-permute-start(f32[24,512]{1,0:T(8,128)S(1)} %describe.1), channel_id=1, source_target_pairs={{0,4},{1,5},{2,6},{3,7},{4,0},{5,1},{6,2},{7,3},{8,12},{9,13},{10,... | collective-permute-start | bytes 147464 | tf_op jit(solution)/shard_map/ppermute | solution.py:503
  27.8 9.9 %collective-permute-start.5 = (f32[24,1024]{1,0:T(8,128)S(1)}, f32[24,1024]{1,0:T(8,128)S(1)}, u32[]{:S(2)}, u32[]{:S(2)}) collective-permute-start(f32[24,1024]{1,0:T(8,128)S(1)} %pad_maximum_fusion.1), channel_id=1, source_target_pairs={{0,8},{1,9},{2,10},{3,11},{4,12},{5,13},{6,14},{7,15},{8,0},{9,1},... | collective-permute-start | bytes 294920 | tf_op jit(solution)/shard_map/ppermute | solution.py:503
  40.1 5.0 %collective-permute-start.7 = (f32[128,256]{1,0:T(8,128)S(1)}, f32[128,256]{1,0:T(8,128)S(1)}, u32[]{:S(2)}, u32[]{:S(2)}) collective-permute-start(f32[128,256]{1,0:T(8,128)S(1)} %get-tuple-element.57), channel_id=1, source_target_pairs={{0,4},{1,5},{2,6},{3,7},{4,0},{5,1},{6,2},{7,3},{8,12},{9,13},{10,... | collective-permute-start | bytes 393224 | tf_op jit(solution)/shard_map/ppermute | solution.py:503
  41.4 7.4 %collective-permute-start.8 = (f32[128,256]{1,0:T(8,128)S(1)}, f32[128,256]{1,0:T(8,128)S(1)}, u32[]{:S(2)}, u32[]{:S(2)}) collective-permute-start(f32[128,256]{1,0:T(8,128)S(1)} %get-tuple-element.58), channel_id=1, source_target_pairs={{0,2},{1,3},{2,0},{3,1},{4,6},{5,7},{6,4},{7,5},{8,10},{9,11},{10,... | collective-permute-start | bytes 393224 | tf_op jit(solution)/shard_map/ppermute | solution.py:503
  41.4 7.4 %collective-permute-start.9 = (f32[128,256]{1,0:T(8,128)S(1)}, f32[128,256]{1,0:T(8,128)S(1)}, u32[]{:S(2)}, u32[]{:S(2)}) collective-permute-start(f32[128,256]{1,0:T(8,128)S(1)} %get-tuple-element.59), channel_id=1, source_target_pairs={{0,6},{1,7},{2,4},{3,5},{4,2},{5,3},{6,0},{7,1},{8,14},{9,15},{10,... | collective-permute-start | bytes 393224 | tf_op jit(solution)/shard_map/ppermute | solution.py:503
  42.9 19.4 %collective-permute-start.6 = (f32[24,2048]{1,0:T(8,128)S(1)}, f32[24,2048]{1,0:T(8,128)S(1)}, u32[]{:S(2)}, u32[]{:S(2)}) collective-permute-start(f32[24,2048]{1,0:T(8,128)S(1)} %pad_maximum_fusion.refs_0_), channel_id=1, source_target_pairs={{0,16},{1,17},{2,18},{3,19},{4,20},{5,21},{6,22},{7,23},{8,24},{9,... | collective-permute-start | bytes 589832 | tf_op jit(solution)/shard_map/ppermute | solution.py:503
  48.9 8.0 %collective-permute-start.11 = (f32[128,256]{1,0:T(8,128)S(1)}, f32[128,256]{1,0:T(8,128)S(1)}, u32[]{:S(2)}, u32[]{:S(2)}) collective-permute-start(f32[128,256]{1,0:T(8,128)S(1)} %add_add_fusion.here_ref), channel_id=1, source_target_pairs={{8,16},{9,17},{10,18},{11,19},{12,20},{13,21},{14,22},{15,23},{16,... | collective-permute-start | bytes 393224 | tf_op jit(solution)/shard_map/ppermute | solution.py:503
  49.7 7.2 %collective-permute-start.10 = (f32[128,256]{1,0:T(8,128)S(1)}, f32[128,256]{1,0:T(8,128)S(1)}, u32[]{:S(2)}, u32[]{:S(2)}) collective-permute-start(f32[128,256]{1,0:T(8,128)S(1)} %add_add_fusion.here_ref), channel_id=1, source_target_pairs={{0,8},{1,9},{2,10},{3,11},{4,12},{5,13},{6,14},{7,15},{8,0},{9,1},... | collective-permute-start | bytes 393224 | tf_op jit(solution)/shard_map/ppermute | solution.py:503
  59.6 7.7 %collective-permute-start.14 = (f32[128,256]{1,0:T(8,128)S(1)}, f32[128,256]{1,0:T(8,128)S(1)}, u32[]{:S(2)}, u32[]{:S(2)}) collective-permute-start(f32[128,256]{1,0:T(8,128)S(1)} %plane_first.1.a_ref.pulled_ref.old_z_ref), channel_id=1, source_target_pairs={{0,6},{1,7},{2,4},{3,5},{4,2},{5,3},{6,0},{7,1},{8,14},{9,15},{10,... | collective-permute-start | bytes 393224 | tf_op jit(solution)/shard_map/ppermute | solution.py:503
  61.1 6.2 %collective-permute-start.13 = (f32[128,256]{1,0:T(8,128)S(1)}, f32[128,256]{1,0:T(8,128)S(1)}, u32[]{:S(2)}, u32[]{:S(2)}) collective-permute-start(f32[128,256]{1,0:T(8,128)S(1)} %plane_first.1.a_ref.pulled_ref.old_z_ref), channel_id=1, source_target_pairs={{0,2},{1,3},{2,0},{3,1},{4,6},{5,7},{6,4},{7,5},{8,10},{9,11},{10,... | collective-permute-start | bytes 393224 | tf_op jit(solution)/shard_map/ppermute | solution.py:503
  62.3 5.1 %collective-permute-start.12 = (f32[128,256]{1,0:T(8,128)S(1)}, f32[128,256]{1,0:T(8,128)S(1)}, u32[]{:S(2)}, u32[]{:S(2)}) collective-permute-start(f32[128,256]{1,0:T(8,128)S(1)} %plane_first.1.a_ref.pulled_ref.old_z_ref), channel_id=1, source_target_pairs={{0,4},{1,5},{2,6},{3,7},{4,0},{5,1},{6,2},{7,3},{8,12},{9,13},{10,... | collective-permute-start | bytes 393224 | tf_op jit(solution)/shard_map/ppermute | solution.py:503
  67.9 3.9 %collective-permute-start.15 = (f32[128,256]{1,0:T(8,128)S(1)}, f32[128,256]{1,0:T(8,128)S(1)}, u32[]{:S(2)}, u32[]{:S(2)}) collective-permute-start(f32[128,256]{1,0:T(8,128)S(1)} %get-tuple-element.69), channel_id=1, source_target_pairs={{0,1},{1,0},{2,3},{3,2},{4,5},{5,4},{6,7},{7,6},{8,9},{9,8},{10,11... | collective-permute-start | bytes 393224 | tf_op jit(solution)/shard_map/ppermute | solution.py:503
  72.5 4.8 %collective-permute-start.16 = (f32[128,256]{1,0:T(8,128)S(1)}, f32[128,256]{1,0:T(8,128)S(1)}, u32[]{:S(2)}, u32[]{:S(2)}) collective-permute-start(f32[128,256]{1,0:T(8,128)S(1)} %add.61.here_ref.old_s_ref), channel_id=1, source_target_pairs={{0,8},{1,9},{2,10},{3,11},{4,12},{5,13},{6,14},{7,15},{8,0},{9,1},... | collective-permute-start | bytes 393224 | tf_op jit(solution)/shard_map/ppermute | solution.py:503
  79.1 4.9 %collective-permute-start.20 = (f32[136,256]{1,0:T(8,128)S(1)}, f32[136,256]{1,0:T(8,128)S(1)}, u32[]{:S(2)}, u32[]{:S(2)}) collective-permute-start(f32[136,256]{1,0:T(8,128)S(1)} %get-tuple-element.70.a_ref.pulled_ref), channel_id=1, source_target_pairs={{0,6},{1,7},{2,4},{3,5},{4,2},{5,3},{6,0},{7,1},{8,14},{9,15},{10,... | collective-permute-start | bytes 417800 | tf_op jit(solution)/shard_map/ppermute | solution.py:503
  81.4 6.8 %collective-permute-start.19 = (f32[136,256]{1,0:T(8,128)S(1)}, f32[136,256]{1,0:T(8,128)S(1)}, u32[]{:S(2)}, u32[]{:S(2)}) collective-permute-start(f32[136,256]{1,0:T(8,128)S(1)} %get-tuple-element.70.a_ref.pulled_ref), channel_id=1, source_target_pairs={{0,2},{1,3},{2,0},{3,1},{4,6},{5,7},{6,4},{7,5},{8,10},{9,11},{10,... | collective-permute-start | bytes 417800 | tf_op jit(solution)/shard_map/ppermute | solution.py:503
  81.7 6.5 %collective-permute-start.18 = (f32[136,256]{1,0:T(8,128)S(1)}, f32[136,256]{1,0:T(8,128)S(1)}, u32[]{:S(2)}, u32[]{:S(2)}) collective-permute-start(f32[136,256]{1,0:T(8,128)S(1)} %get-tuple-element.70.a_ref.pulled_ref), channel_id=1, source_target_pairs={{0,4},{1,5},{2,6},{3,7},{4,0},{5,1},{6,2},{7,3},{8,12},{9,13},{10,... | collective-permute-start | bytes 417800 | tf_op jit(solution)/shard_map/ppermute | solution.py:503
  88.7 2.7 %collective-permute-start.21 = (f32[392,256]{1,0:T(8,128)S(1)}, f32[392,256]{1,0:T(8,128)S(1)}, u32[]{:S(2)}, u32[]{:S(2)}) collective-permute-start(f32[392,256]{1,0:T(8,128)S(1)} %get-tuple-element.73), channel_id=1, source_target_pairs={{0,1},{1,0},{2,3},{3,2},{4,5},{5,4},{6,7},{7,6},{8,9},{9,8},{10,11... | collective-permute-start | bytes 1204232 | tf_op jit(solution)/shard_map/ppermute | solution.py:503
  91.5 5.9 %collective-permute-start.25 = (f32[136,256]{1,0:T(8,128)S(1)}, f32[136,256]{1,0:T(8,128)S(1)}, u32[]{:S(2)}, u32[]{:S(2)}) collective-permute-start(f32[136,256]{1,0:T(8,128)S(1)} %slice_add_fusion.1.here_ref), channel_id=1, source_target_pairs={{8,16},{9,17},{10,18},{11,19},{12,20},{13,21},{14,22},{15,23},{16,... | collective-permute-start | bytes 417800 | tf_op jit(solution)/shard_map/ppermute | solution.py:503
  92.3 7.2 %collective-permute-start.22 = (f32[136,256]{1,0:T(8,128)S(1)}, f32[136,256]{1,0:T(8,128)S(1)}, u32[]{:S(2)}, u32[]{:S(2)}) collective-permute-start(f32[136,256]{1,0:T(8,128)S(1)} %slice_add_fusion.1.here_ref), channel_id=1, source_target_pairs={{0,8},{1,9},{2,10},{3,11},{4,12},{5,13},{6,14},{7,15},{8,0},{9,1},... | collective-permute-start | bytes 417800 | tf_op jit(solution)/shard_map/ppermute | solution.py:503
  96.1 4.7 %collective-permute-start.24 = (f32[8,256]{1,0:T(8,128)S(1)}, f32[8,256]{1,0:T(8,128)S(1)}, u32[]{:S(2)}, u32[]{:S(2)}) collective-permute-start(f32[8,256]{1,0:T(8,128)S(1)} %slice.23), channel_id=1, source_target_pairs={{0,24},{1,25},{2,26},{3,27},{4,28},{5,29},{6,30},{7,31},{8,16},{9,... | collective-permute-start | bytes 24584 | tf_op jit(solution)/shard_map/ppermute | solution.py:503
  97.2 3.6 %collective-permute-start.23 = (f32[8,256]{1,0:T(8,128)S(1)}, f32[8,256]{1,0:T(8,128)S(1)}, u32[]{:S(2)}, u32[]{:S(2)}) collective-permute-start(f32[8,256]{1,0:T(8,128)S(1)} %slice.23), channel_id=1, source_target_pairs={{0,16},{1,17},{2,18},{3,19},{4,20},{5,21},{6,22},{7,23},{8,24},{9,... | collective-permute-start | bytes 24584 | tf_op jit(solution)/shard_map/ppermute | solution.py:503
  102.1 5.0 %collective-permute-start.28 = (f32[136,256]{1,0:T(8,128)S(1)}, f32[136,256]{1,0:T(8,128)S(1)}, u32[]{:S(2)}, u32[]{:S(2)}) collective-permute-start(f32[136,256]{1,0:T(8,128)S(1)} %get-tuple-element.76.a_ref.pulled_ref), channel_id=1, source_target_pairs={{0,6},{1,7},{2,4},{3,5},{4,2},{5,3},{6,0},{7,1},{8,14},{9,15},{10,... | collective-permute-start | bytes 417800 | tf_op jit(solution)/shard_map/ppermute | solution.py:503
  103.3 5.8 %collective-permute-start.27 = (f32[136,256]{1,0:T(8,128)S(1)}, f32[136,256]{1,0:T(8,128)S(1)}, u32[]{:S(2)}, u32[]{:S(2)}) collective-permute-start(f32[136,256]{1,0:T(8,128)S(1)} %get-tuple-element.76.a_ref.pulled_ref), channel_id=1, source_target_pairs={{0,2},{1,3},{2,0},{3,1},{4,6},{5,7},{6,4},{7,5},{8,10},{9,11},{10,... | collective-permute-start | bytes 417800 | tf_op jit(solution)/shard_map/ppermute | solution.py:503
  104.2 4.9 %collective-permute-start.26 = (f32[136,256]{1,0:T(8,128)S(1)}, f32[136,256]{1,0:T(8,128)S(1)}, u32[]{:S(2)}, u32[]{:S(2)}) collective-permute-start(f32[136,256]{1,0:T(8,128)S(1)} %get-tuple-element.76.a_ref.pulled_ref), channel_id=1, source_target_pairs={{0,4},{1,5},{2,6},{3,7},{4,0},{5,1},{6,2},{7,3},{8,12},{9,13},{10,... | collective-permute-start | bytes 417800 | tf_op jit(solution)/shard_map/ppermute | solution.py:503
  109.6 4.5 %collective-permute-start.29 = (f32[392,256]{1,0:T(8,128)S(1)}, f32[392,256]{1,0:T(8,128)S(1)}, u32[]{:S(2)}, u32[]{:S(2)}) collective-permute-start(f32[392,256]{1,0:T(8,128)S(1)} %get-tuple-element.80), channel_id=1, source_target_pairs={{0,1},{1,0},{2,3},{3,2},{4,5},{5,4},{6,7},{7,6},{8,9},{9,8},{10,11... | collective-permute-start | bytes 1204232 | tf_op jit(solution)/shard_map/ppermute | solution.py:503
  114.2 5.7 %collective-permute-start.30 = (f32[136,256]{1,0:T(8,128)S(1)}, f32[136,256]{1,0:T(8,128)S(1)}, u32[]{:S(2)}, u32[]{:S(2)}) collective-permute-start(f32[136,256]{1,0:T(8,128)S(1)} %slice_add_fusion.here_ref), channel_id=1, source_target_pairs={{0,8},{1,9},{2,10},{3,11},{4,12},{5,13},{6,14},{7,15},{8,16},{9,17... | collective-permute-start | bytes 417800 | tf_op jit(solution)/shard_map/ppermute | solution.py:503
  119.2 7.9 %collective-permute-start.31 = (f32[256,256]{1,0:T(8,128)}, f32[256,256]{1,0:T(8,128)}, u32[]{:S(2)}, u32[]{:S(2)}) collective-permute-start(f32[256,256]{1,0:T(8,128)} %get-tuple-element.86), channel_id=1, source_target_pairs={{0,1},{1,0},{2,3},{3,2},{4,5},{5,4},{6,7},{7,6},{8,9},{9,8},{10,11... | collective-permute-start | bytes 786440 | tf_op jit(solution)/shard_map/ppermute | solution.py:503
  121.2 14.0 %all-to-all-start = ((f32[32,8,128]{2,1,0:T(8,128)}), f32[32,8,128]{2,1,0:T(8,128)S(1)}, u32[]{:S(2)}, u32[]{:S(2)}) async-start(f32[32,8,128]{2,1,0:T(8,128)} %plane_close.1), calls=%async_computation | async-start | bytes 262144 | tf_op jit(solution)/shard_map/all_to_all | solution.py:1155
  136.8 13.3 %collective-permute-start.32 = (f32[512,128]{1,0:T(8,128)S(1)}, f32[512,128]{1,0:T(8,128)S(1)}, u32[]{:S(2)}, u32[]{:S(2)}) collective-permute-start(f32[512,128]{1,0:T(8,128)S(1)} %plane_combine.1), channel_id=1, source_target_pairs={{0,0},{1,16},{2,8},{3,24},{4,4},{5,20},{6,12},{7,28},{8,1},{9,17},... | collective-permute-start | bytes 786440 | tf_op jit(solution)/shard_map/ppermute | solution.py:503
  (21 other events, 159.8 us)

commit v18 on v16

--- a/solution.py
+++ b/solution.py
@@ -635,23 +635,6 @@
     )(incidence, row_gauge.reshape(1, count))
 
 
-def observe_kernel(seen_ref, later_ref, kind_ref, kernels_ref, wide_ref, forward, first, out_ref):
-    spec = spectra(kind_ref[...].astype(F32), kernels_ref[...], wide_ref[...])
-    here, after = jnp.transpose(seen_ref[...]), jnp.transpose(later_ref[...])
-    out_ref[...] = plane_advanced(here, after, spec, forward[...], first[...], 3)
-
-
-def observe(seen, later, gauge_kernel, kernels, wide, mats):
-    rows, hours = seen.shape
-    return pl.pallas_call(
-        observe_kernel,
-        out_shape=jax.ShapeDtypeStruct((hours, rows), F32),
-        compiler_params=params(),
-        name="observe",
-        cost_estimate=SMALL,
-    )(seen, later, gauge_kernel.reshape(1, rows), kernels, wide, *mats)
-
-
 def send_kernel(
     inc_hbm, field_hbm, gauge_hbm, kind_hbm, out_ref, inc_ref, field_ref, gauge_ref, kind_ref, sems, label_sems
 ):
@@ -938,13 +921,16 @@
 
 
 def plane_first_kernel(
-    flag_ref, here_ref, pair_ref, middle_ref, seen_ref, spec_ref, kernels_ref, forward, first, last, out_ref
+    flag_ref, here_ref, pair_ref, middle_ref, spec_ref, kernels_ref, forward, first, last, out_ref
 ):
     spec = spec_ref[...]
     before, after = sides(flag_ref[0] > 0.5, pair_ref[...], middle_ref[...])
-    now, later = plane_delayed(before, here_ref[...], after, spec, forward[...], last[...], 3)
-    known = plane_advanced(now, later * flag_ref[1], spec, forward[...], first[...], 3)
-    out_ref[...] = seen_ref[...] - known * gain(kernels_ref[...])
+    here = here_ref[...]
+    both = plane_delayed(before[:HOURS], here[:HOURS], after[:HOURS], spec, forward[...], last[...], 3)
+    scale = gain(kernels_ref[...])
+    now = here[HOURS:] - both[0] * scale
+    later = (after[HOURS:] - both[1] * scale) * flag_ref[1]
+    out_ref[...] = plane_advanced(now, later, spec, forward[...], first[...], 3)
 
 
 def plane_delay_kernel(flag_ref, here_ref, pair_ref, middle_ref, spec_ref, forward, last, out_ref):
@@ -1101,15 +1087,12 @@
     forward3, inverse_first3, inverse_last3, short3 = turned_transforms(3)
     block, noted = (hours, rows), (hours + NOTE, rows)
 
+    seen = moved(observed, to_plane)
     parcel = send(incidence, first_guess, row_gauge, gauge_kernel)
-    parcel, near, gauges, kinds, seen = lax.optimization_barrier(
-        (parcel, incidence, row_gauge, gauge_kernel, observed)
-    )
+    parcel, near = lax.optimization_barrier((parcel, incidence))
     parcel = moved(parcel, to_plane)
-    seen = observe(seen, moved(seen, hour_before), kinds, kernels, short3, [forward3, inverse_first3])
-    seen, near = lax.optimization_barrier((seen, near))
-    seen = moved(seen, to_plane)
-    meta = describe(near, gauges)
+    near, seen = lax.optimization_barrier((near, seen))
+    meta = describe(near, row_gauge)
     meta = jnp.concatenate([meta, moved(meta, over_x)], axis=1)
     meta = jnp.concatenate([meta, moved(meta, z_pair)], axis=1)
     parcel, seen = lax.optimization_barrier((parcel, seen))
@@ -1120,6 +1103,8 @@
     dense = spread(first, parcels, rows)
     metas = [value[hours:] for value in parcels]
     sums = dense[0] + sum(moved(value, where) for value, where in zip(dense[1:], SQUARE))
+    sums, around = lax.optimization_barrier((sums, around))
+    sums = jnp.concatenate([sums, jnp.transpose(seen)], axis=0)
     sums = [sums, moved(sums, z_pair), moved(sums, z_middle)]
     coupled = plane_couple(first, around[0], rows)
     coupled, sums = lax.optimization_barrier((coupled, sums))
@@ -1129,7 +1114,7 @@
         "plane_first",
         [block],
         [flags],
-        [*sums, seen, spec, kernels, forward3, inverse_first3, inverse_last3],
+        [*sums, spec, kernels, forward3, inverse_first3, inverse_last3],
     )
 
     def mixing(pulled, extra):

time: 146 us -> 148 us (1.014)
  waiting for transfers between devices: 53.6 us -> 61.3 us
  starting transfers between devices: 56.2 us -> 50.7 us
  Pallas kernels: 35.3 us -> 33.7 us
    ppermute x33 -> x32, waiting for transfers between devices: 45.4 us -> 53.2 us  [moved(): return lax.ppermute(value, ('basin', 'tm'), pairs)]
    ppermute x33 -> x32, starting transfers between devices: 50.5 us -> 44.9 us  [moved(): return lax.ppermute(value, ('basin', 'tm'), pairs)]
  transfers between devices with their start and end apart: 34 -> 33, of which waited for: 20 -> 23; matrix products, arithmetic and copies ran while one was open for 0% -> 0% of each run, Pallas kernels for 15% -> 12%
where the time goes in v18:
time: 148 us; the launch traced here: 147 us
  waiting for transfers between devices  61.3 us (41%)
  starting transfers between devices  50.7 us (34%)
  Pallas kernels  33.7 us (23%)
    ppermute x32, waiting for transfers between devices, moved(): return lax.ppermute(value, ('basin', 'tm'), pairs)  53.2 us
    ppermute x32, starting transfers between devices, moved(): return lax.ppermute(value, ('basin', 'tm'), pairs)  44.9 us
    pallas_call x6, Pallas kernels, plane_call(): pl.pallas_call(kernel, in_specs=[pl.BlockSpec(memory_space=pltpu.SMEM)] *...  9.84 us
    pallas_call x2, Pallas kernels, plane_couple(): pl.pallas_call(functools.partial(plane_couple_kernel, last), in_specs=[pl...  9.57 us
    all_to_all x1, waiting for transfers between devices, plane_shards(): close_note = lax.all_to_all(note, ('basin', 'tm'), 0, 0, tiled=False)  8.18 us
    all_to_all x1, starting transfers between devices, plane_shards(): close_note = lax.all_to_all(note, ('basin', 'tm'), 0, 0, tiled=False)  5.84 us
    pallas_call x3, Pallas kernels, plane_rows(): pl.pallas_call(plane_rows_kernel, in_specs=[pl.BlockSpec(memory_space=plt...  4.51 us
    pallas_call x1, Pallas kernels, send(): pl.pallas_call(send_kernel, in_specs=[pl.BlockSpec(memory_space=pltpu.HBM...  3.21 us
  transfers between devices with their start and end apart: 33, of which 23 were waited for; matrix products, arithmetic and copies ran while one was open for 0% of the time, Pallas kernels for 12%

profile of v18, /device:TPU:1, one launch (start us, length us, event | category | flops | bytes accessed | tf_op | source)
XLA Modules:
  0.0 147.5 jit_solution(6568583830050430428)
XLA Ops:
  1.1 4.6 %collective-permute-start.1 = (f32[256,128]{0,1:T(8,128)S(1)}, f32[256,128]{0,1:T(8,128)S(1)}, u32[]{:S(2)}, u32[]{:S(2)}) collective-permute-start(f32[256,128]{0,1:T(8,128)S(1)} %copy.14), channel_id=1, source_target_pairs={{0,0},{1,8},{2,16},{3,24},{4,4},{5,12},{6,20},{7,28},{8,2},{9,10},... | collective-permute-start | bytes 393224 | tf_op jit(solution)/shard_map/ppermute | solution.py:503
  5.7 3.2 %send.1 = f32[136,512]{1,0:T(8,128)} custom-call(s32[32,16,128]{2,1,0:T(8,128)} %inc_ref.2, f32[4096,128]{1,0:T(8,128)} %field_ref.1, s32[1,512]{1,0:T(1,128)} %bitcast.11, s32[1,256]{1,0:T(1,128)} %bitcast.14), custom_call_target="tpu_custom_call" | custom-call | flops 1 | bytes 1 | tf_op jit(solution)/shard_map/send/pallas_call | solution.py:685
  8.9 3.3 %collective-permute-start = (f32[136,512]{1,0:T(8,128)}, f32[136,512]{1,0:T(8,128)S(1)}, u32[]{:S(2)}, u32[]{:S(2)}) collective-permute-start(f32[136,512]{1,0:T(8,128)} %send.1), channel_id=1, source_target_pairs={{0,0},{1,8},{2,16},{3,24},{4,4},{5,12},{6,20},{7,28},{8,2},{9,10},... | collective-permute-start | bytes 835592 | tf_op jit(solution)/shard_map/ppermute | solution.py:503
  14.4 1.6 %collective-permute-done.3 = f32[24,512]{1,0:T(8,128)S(1)} collective-permute-done((f32[24,512]{1,0:T(8,128)S(1)}, f32[24,512]{1,0:T(8,128)S(1)}, u32[]{:S(2)}, u32[]{:S(2)}) %collective-permute-start.3) | collective-permute-done | bytes 49184 | tf_op jit(solution)/shard_map/ppermute | solution.py:503
  17.3 9.1 %collective-permute-done.mine_ref = f32[136,512]{1,0:T(8,128)S(1)} collective-permute-done((f32[136,512]{1,0:T(8,128)}, f32[136,512]{1,0:T(8,128)S(1)}, u32[]{:S(2)}, u32[]{:S(2)}) %collective-permute-start) | collective-permute-done | bytes 278560 | tf_op jit(solution)/shard_map/ppermute | solution.py:503
  27.9 1.6 %spread.1 = (f32[128,256]{1,0:T(8,128)S(1)}, f32[128,256]{1,0:T(8,128)S(1)}, f32[128,256]{1,0:T(8,128)S(1)}, f32[128,256]{1,0:T(8,128)S(1)}) custom-call(s32[6]{0:T(128)S(1)} %broadcast_multiply_fusion.first_ref, f32[136,512]{1,0:T(8,128)S(1)} %collective-permute-done.mine_ref, f32[136,512]{1,0:T(8,128)S(1)} %collective-permute-done.2.other_ref), custom_call_target="tpu_custom_call" | custom-call | flops 1 | bytes 1 | tf_op jit(solution)/shard_map/spread/pallas_call | solution.py:719
  33.0 1.5 %collective-permute-done.5 = f32[128,256]{1,0:T(8,128)S(1)} collective-permute-done((f32[128,256]{1,0:T(8,128)S(1)}, f32[128,256]{1,0:T(8,128)S(1)}, u32[]{:S(2)}, u32[]{:S(2)}) %collective-permute-start.5) | collective-permute-done | bytes 131104 | tf_op jit(solution)/shard_map/ppermute | solution.py:503
  34.5 3.7 %collective-permute-done.6 = f32[128,256]{1,0:T(8,128)S(1)} collective-permute-done((f32[128,256]{1,0:T(8,128)S(1)}, f32[128,256]{1,0:T(8,128)S(1)}, u32[]{:S(2)}, u32[]{:S(2)}) %collective-permute-start.6) | collective-permute-done | bytes 131104 | tf_op jit(solution)/shard_map/ppermute | solution.py:503
  38.3 5.4 %collective-permute-done.8.refs_0_ = f32[24,2048]{1,0:T(8,128)S(1)} collective-permute-done((f32[24,2048]{1,0:T(8,128)S(1)}, f32[24,2048]{1,0:T(8,128)S(1)}, u32[]{:S(2)}, u32[]{:S(2)}) %collective-permute-start.8) | collective-permute-done | bytes 196640 | tf_op jit(solution)/shard_map/ppermute | solution.py:503
  45.3 4.7 %plane_couple.2.refs_1_ = f32[1024,512]{1,0:T(8,128)S(1)} custom-call(s32[6]{0:T(128)S(1)} %broadcast_multiply_fusion.first_ref, f32[24,2048]{1,0:T(8,128)S(1)} %pad_maximum_fusion.1.refs_0_), custom_call_target="tpu_custom_call" | custom-call | flops 2147483648 | bytes 2000000 | tf_op jit(solution)/shard_map/plane_couple/pallas_call | solution.py:785
  50.0 1.8 %collective-permute-done.9.pair_ref = f32[256,256]{1,0:T(8,128)S(1)} collective-permute-done((f32[256,256]{1,0:T(8,128)S(1)}, f32[256,256]{1,0:T(8,128)S(1)}, u32[]{:S(2)}, u32[]{:S(2)}) %collective-permute-start.9) | collective-permute-done | bytes 262176 | tf_op jit(solution)/shard_map/ppermute | solution.py:503
  51.9 2.6 %plane_first.1.a_ref.pulled_ref.old_z_ref = f32[128,256]{1,0:T(8,128)S(1)} custom-call(f32[3]{0:T(128)S(1)} %add_convert_fusion.flag_ref, f32[256,256]{1,0:T(8,128)S(1)} %pad_maximum_fusion.here_ref, f32[256,256]{1,0:T(8,128)S(1)} %collective-permute-done.9.pair_ref, f32[256,256]{1,0:T(8,128)S(1)} %collective-permute-done.10.middle_ref, ...), custom_call_target="tpu_custom_call" | custom-call | flops 1 | bytes 1 | tf_op jit(solution)/shard_map/plane_first/pallas_call | solution.py:912
  54.4 1.7 %collective-permute-start.13 = (f32[128,256]{1,0:T(8,128)S(1)}, f32[128,256]{1,0:T(8,128)S(1)}, u32[]{:S(2)}, u32[]{:S(2)}) collective-permute-start(f32[128,256]{1,0:T(8,128)S(1)} %plane_first.1.a_ref.pulled_ref.old_z_ref), channel_id=1, source_target_pairs={{0,6},{1,7},{2,4},{3,5},{4,2},{5,3},{6,0},{7,1},{8,14},{9,15},{10,... | collective-permute-start | bytes 393224 | tf_op jit(solution)/shard_map/ppermute | solution.py:503
  57.2 4.9 %plane_couple.3 = (bf16[1024,512]{1,0:T(8,128)(2,1)S(1)}, bf16[1024,512]{1,0:T(8,128)(2,1)S(1)}) custom-call(s32[6]{0:T(128)S(1)} %broadcast_multiply_fusion.first_ref, f32[24,2048]{1,0:T(8,128)S(1)} %collective-permute-done.8.refs_0_, f32[1024,512]{1,0:T(8,128)S(1)} %plane_couple.2.refs_1_), custom_call_target="tpu_custom_call" | custom-call | flops 2147483648 | bytes 2000000 | tf_op jit(solution)/shard_map/plane_couple/pallas_call | solution.py:785
  63.5 1.5 %collective-permute-start.14 = (f32[128,256]{1,0:T(8,128)S(1)}, f32[128,256]{1,0:T(8,128)S(1)}, u32[]{:S(2)}, u32[]{:S(2)}) collective-permute-start(f32[128,256]{1,0:T(8,128)S(1)} %get-tuple-element.71), channel_id=1, source_target_pairs={{0,1},{1,0},{2,3},{3,2},{4,5},{5,4},{6,7},{7,6},{8,9},{9,8},{10,11... | collective-permute-start | bytes 393224 | tf_op jit(solution)/shard_map/ppermute | solution.py:503
  66.7 3.4 %collective-permute-start.15 = (f32[128,256]{1,0:T(8,128)S(1)}, f32[128,256]{1,0:T(8,128)S(1)}, u32[]{:S(2)}, u32[]{:S(2)}) collective-permute-start(f32[128,256]{1,0:T(8,128)S(1)} %add.61.here_ref.old_s_ref), channel_id=1, source_target_pairs={{0,8},{1,9},{2,10},{3,11},{4,12},{5,13},{6,14},{7,15},{8,0},{9,1},... | collective-permute-start | bytes 393224 | tf_op jit(solution)/shard_map/ppermute | solution.py:503
  70.0 3.3 %collective-permute-done.15.pair_ref = f32[128,256]{1,0:T(8,128)S(1)} collective-permute-done((f32[128,256]{1,0:T(8,128)S(1)}, f32[128,256]{1,0:T(8,128)S(1)}, u32[]{:S(2)}, u32[]{:S(2)}) %collective-permute-start.15) | collective-permute-done | bytes 131104 | tf_op jit(solution)/shard_map/ppermute | solution.py:503
  73.3 1.8 %plane_open.1 = (f32[136,256]{1,0:T(8,128)S(1)}, f32[256,256]{1,0:T(8,128)S(1)}) custom-call(f32[3]{0:T(128)S(1)} %add_convert_fusion.flag_ref, f32[128,256]{1,0:T(8,128)S(1)} %add.61.here_ref.old_s_ref, f32[128,256]{1,0:T(8,128)S(1)} %collective-permute-done.15.pair_ref, f32[128,256]{1,0:T(8,128)S(1)} %collective-permute-done.16.middle_ref, ...), custom_call_target="tpu_custom_call" | custom-call | flops 1 | bytes 1 | tf_op jit(solution)/shard_map/plane_open/pallas_call | solution.py:912
  75.2 2.4 %collective-permute-start.19 = (f32[136,256]{1,0:T(8,128)S(1)}, f32[136,256]{1,0:T(8,128)S(1)}, u32[]{:S(2)}, u32[]{:S(2)}) collective-permute-start(f32[136,256]{1,0:T(8,128)S(1)} %get-tuple-element.72.a_ref.pulled_ref), channel_id=1, source_target_pairs={{0,6},{1,7},{2,4},{3,5},{4,2},{5,3},{6,0},{7,1},{8,14},{9,15},{10,... | collective-permute-start | bytes 417800 | tf_op jit(solution)/shard_map/ppermute | solution.py:503
  80.0 4.2 %collective-permute-done.18.c_ref = f32[136,256]{1,0:T(8,128)S(1)} collective-permute-done((f32[136,256]{1,0:T(8,128)S(1)}, f32[136,256]{1,0:T(8,128)S(1)}, u32[]{:S(2)}, u32[]{:S(2)}) %collective-permute-start.18) | collective-permute-done | bytes 139296 | tf_op jit(solution)/shard_map/ppermute | solution.py:503
  88.3 2.7 %collective-permute-start.21 = (f32[136,256]{1,0:T(8,128)S(1)}, f32[136,256]{1,0:T(8,128)S(1)}, u32[]{:S(2)}, u32[]{:S(2)}) collective-permute-start(f32[136,256]{1,0:T(8,128)S(1)} %slice_add_fusion.1.here_ref), channel_id=1, source_target_pairs={{0,8},{1,9},{2,10},{3,11},{4,12},{5,13},{6,14},{7,15},{8,0},{9,1},... | collective-permute-start | bytes 417800 | tf_op jit(solution)/shard_map/ppermute | solution.py:503
  91.0 2.1 %collective-permute-start.23 = (f32[8,256]{1,0:T(8,128)S(1)}, f32[8,256]{1,0:T(8,128)S(1)}, u32[]{:S(2)}, u32[]{:S(2)}) collective-permute-start(f32[8,256]{1,0:T(8,128)S(1)} %slice.23), channel_id=1, source_target_pairs={{0,24},{1,25},{2,26},{3,27},{4,28},{5,29},{6,30},{7,31},{8,16},{9,... | collective-permute-start | bytes 24584 | tf_op jit(solution)/shard_map/ppermute | solution.py:503
  102.8 1.8 %collective-permute-done.26.c_ref = f32[136,256]{1,0:T(8,128)S(1)} collective-permute-done((f32[136,256]{1,0:T(8,128)S(1)}, f32[136,256]{1,0:T(8,128)S(1)}, u32[]{:S(2)}, u32[]{:S(2)}) %collective-permute-start.26) | collective-permute-done | bytes 139296 | tf_op jit(solution)/shard_map/ppermute | solution.py:503
  105.3 3.7 %collective-permute-start.28 = (f32[392,256]{1,0:T(8,128)S(1)}, f32[392,256]{1,0:T(8,128)S(1)}, u32[]{:S(2)}, u32[]{:S(2)}) collective-permute-start(f32[392,256]{1,0:T(8,128)S(1)} %get-tuple-element.82), channel_id=1, source_target_pairs={{0,1},{1,0},{2,3},{3,2},{4,5},{5,4},{6,7},{7,6},{8,9},{9,8},{10,11... | collective-permute-start | bytes 1204232 | tf_op jit(solution)/shard_map/ppermute | solution.py:503
  110.4 1.8 %collective-permute-start.29 = (f32[136,256]{1,0:T(8,128)S(1)}, f32[136,256]{1,0:T(8,128)S(1)}, u32[]{:S(2)}, u32[]{:S(2)}) collective-permute-start(f32[136,256]{1,0:T(8,128)S(1)} %slice_add_fusion.here_ref), channel_id=1, source_target_pairs={{0,8},{1,9},{2,10},{3,11},{4,12},{5,13},{6,14},{7,15},{8,16},{9,17... | collective-permute-start | bytes 417800 | tf_op jit(solution)/shard_map/ppermute | solution.py:503
  112.2 2.0 %plane_rows.5 = (f32[128,512]{1,0:T(8,128)S(1)}, f32[256,256]{1,0:T(8,128)}, f32[256,512]{1,0:T(8,128)S(1)}) custom-call(s32[6]{0:T(128)S(1)} %broadcast_multiply_fusion.first_ref, f32[8,512]{1,0:T(8,128)S(1)} %slice.17.class_ref.meta_ref, f32[8,512]{1,0:T(8,128)S(1)} %slice.18.meta_other_ref, f32[136,256]{1,0:T(8,128)S(1)} %get-tuple-element.78.a_ref.pulled_ref, ...), custom_call_target="tpu_custom_call" | custom-call | flops 1000000000 | bytes 2000000 | tf_op jit(solution)/shard_map/plane_rows/pallas_call | solution.py:868
  116.2 5.8 %all-to-all-start = ((f32[32,8,128]{2,1,0:T(8,128)}), f32[32,8,128]{2,1,0:T(8,128)S(1)}, u32[]{:S(2)}, u32[]{:S(2)}) async-start(f32[32,8,128]{2,1,0:T(8,128)} %plane_close.1), calls=%async_computation | async-start | bytes 262144 | tf_op jit(solution)/shard_map/all_to_all | solution.py:1161
  122.1 8.2 %all-to-all-done.close_ref = f32[32,8,128]{2,1,0:T(8,128)S(1)} async-done(((f32[32,8,128]{2,1,0:T(8,128)}), f32[32,8,128]{2,1,0:T(8,128)S(1)}, u32[]{:S(2)}, u32[]{:S(2)}) %all-to-all-start) | async-done | bytes 131104 | tf_op jit(solution)/shard_map/all_to_all | solution.py:1161
  130.3 1.5 %plane_combine.1 = f32[512,128]{1,0:T(8,128)S(1)} custom-call(f32[8,256]{1,0:T(8,128)S(1)} %get-tuple-element.77.open_ref, f32[32,8,128]{2,1,0:T(8,128)S(1)} %all-to-all-done.close_ref, f32[32,128]{1,0:T(8,128)S(1)} %copy-done.9, f32[256,512]{1,0:T(8,128)S(1)} %get-tuple-element.86.stack_ref, f32[128,512]{1,0:T(8,128)S(1)} %get-tuple-element.87.mine_ref, ...), custom_call_target="tpu_custom_call" | custom-call | flops 1 | bytes 1 | tf_op jit(solution)/shard_map/plane_combine/pallas_call | solution.py:912
  131.8 2.6 %collective-permute-start.31 = (f32[512,128]{1,0:T(8,128)S(1)}, f32[512,128]{1,0:T(8,128)S(1)}, u32[]{:S(2)}, u32[]{:S(2)}) collective-permute-start(f32[512,128]{1,0:T(8,128)S(1)} %plane_combine.1), channel_id=1, source_target_pairs={{0,0},{1,16},{2,8},{3,24},{4,4},{5,20},{6,12},{7,28},{8,1},{9,17},... | collective-permute-start | bytes 786440 | tf_op jit(solution)/shard_map/ppermute | solution.py:503
  134.4 10.7 %collective-permute-done.31.rows_ref = f32[512,128]{1,0:T(8,128)S(1)} collective-permute-done((f32[512,128]{1,0:T(8,128)S(1)}, f32[512,128]{1,0:T(8,128)S(1)}, u32[]{:S(2)}, u32[]{:S(2)}) %collective-permute-start.31) | collective-permute-done | bytes 262176 | tf_op jit(solution)/shard_map/ppermute | solution.py:503
  145.1 2.4 %plane_finish.1 = f32[4096,128]{1,0:T(8,128)} custom-call(f32[512,128]{1,0:T(8,128)S(1)} %collective-permute-done.31.rows_ref, s32[32,16,128]{2,1,0:T(8,128)S(1)} %copy-done.2, f32[4096,128]{1,0:T(8,128)S(1)} %copy-done), custom_call_target="tpu_custom_call" | custom-call | tf_op jit(solution)/shard_map/plane_finish/pallas_call | solution.py:1063
  (89 shorter events, 35.5 us)
Async XLA Ops:
  1.1 11.8 %collective-permute-start.1 = (f32[256,128]{0,1:T(8,128)S(1)}, f32[256,128]{0,1:T(8,128)S(1)}, u32[]{:S(2)}, u32[]{:S(2)}) collective-permute-start(f32[256,128]{0,1:T(8,128)S(1)} %copy.14), channel_id=1, source_target_pairs={{0,0},{1,8},{2,16},{3,24},{4,4},{5,12},{6,20},{7,28},{8,2},{9,10},... | collective-permute-start | bytes 393224 | tf_op jit(solution)/shard_map/ppermute | solution.py:503
  8.9 17.5 %collective-permute-start = (f32[136,512]{1,0:T(8,128)}, f32[136,512]{1,0:T(8,128)S(1)}, u32[]{:S(2)}, u32[]{:S(2)}) collective-permute-start(f32[136,512]{1,0:T(8,128)} %send.1), channel_id=1, source_target_pairs={{0,0},{1,8},{2,16},{3,24},{4,4},{5,12},{6,20},{7,28},{8,2},{9,10},... | collective-permute-start | bytes 835592 | tf_op jit(solution)/shard_map/ppermute | solution.py:503
  13.1 3.0 %collective-permute-start.3 = (f32[24,512]{1,0:T(8,128)S(1)}, f32[24,512]{1,0:T(8,128)S(1)}, u32[]{:S(2)}, u32[]{:S(2)}) collective-permute-start(f32[24,512]{1,0:T(8,128)S(1)} %describe.1), channel_id=1, source_target_pairs={{0,4},{1,5},{2,6},{3,7},{4,0},{5,1},{6,2},{7,3},{8,12},{9,13},{10,... | collective-permute-start | bytes 147464 | tf_op jit(solution)/shard_map/ppermute | solution.py:503
  16.1 11.0 %collective-permute-start.4 = (f32[24,1024]{1,0:T(8,128)S(1)}, f32[24,1024]{1,0:T(8,128)S(1)}, u32[]{:S(2)}, u32[]{:S(2)}) collective-permute-start(f32[24,1024]{1,0:T(8,128)S(1)} %pad_maximum_fusion.2), channel_id=1, source_target_pairs={{0,8},{1,9},{2,10},{3,11},{4,12},{5,13},{6,14},{7,15},{8,0},{9,1},... | collective-permute-start | bytes 294920 | tf_op jit(solution)/shard_map/ppermute | solution.py:503
  29.5 5.0 %collective-permute-start.5 = (f32[128,256]{1,0:T(8,128)S(1)}, f32[128,256]{1,0:T(8,128)S(1)}, u32[]{:S(2)}, u32[]{:S(2)}) collective-permute-start(f32[128,256]{1,0:T(8,128)S(1)} %get-tuple-element.55), channel_id=1, source_target_pairs={{0,4},{1,5},{2,6},{3,7},{4,0},{5,1},{6,2},{7,3},{8,12},{9,13},{10,... | collective-permute-start | bytes 393224 | tf_op jit(solution)/shard_map/ppermute | solution.py:503
  30.8 7.4 %collective-permute-start.6 = (f32[128,256]{1,0:T(8,128)S(1)}, f32[128,256]{1,0:T(8,128)S(1)}, u32[]{:S(2)}, u32[]{:S(2)}) collective-permute-start(f32[128,256]{1,0:T(8,128)S(1)} %get-tuple-element.56), channel_id=1, source_target_pairs={{0,2},{1,3},{2,0},{3,1},{4,6},{5,7},{6,4},{7,5},{8,10},{9,11},{10,... | collective-permute-start | bytes 393224 | tf_op jit(solution)/shard_map/ppermute | solution.py:503
  30.8 7.4 %collective-permute-start.7 = (f32[128,256]{1,0:T(8,128)S(1)}, f32[128,256]{1,0:T(8,128)S(1)}, u32[]{:S(2)}, u32[]{:S(2)}) collective-permute-start(f32[128,256]{1,0:T(8,128)S(1)} %get-tuple-element.57), channel_id=1, source_target_pairs={{0,6},{1,7},{2,4},{3,5},{4,2},{5,3},{6,0},{7,1},{8,14},{9,15},{10,... | collective-permute-start | bytes 393224 | tf_op jit(solution)/shard_map/ppermute | solution.py:503
  32.2 11.5 %collective-permute-start.8 = (f32[24,2048]{1,0:T(8,128)S(1)}, f32[24,2048]{1,0:T(8,128)S(1)}, u32[]{:S(2)}, u32[]{:S(2)}) collective-permute-start(f32[24,2048]{1,0:T(8,128)S(1)} %pad_maximum_fusion.1.refs_0_), channel_id=1, source_target_pairs={{0,16},{1,17},{2,18},{3,19},{4,20},{5,21},{6,22},{7,23},{8,24},{9,... | collective-permute-start | bytes 589832 | tf_op jit(solution)/shard_map/ppermute | solution.py:503
  43.7 6.3 %collective-permute-start.10 = (f32[256,256]{1,0:T(8,128)S(1)}, f32[256,256]{1,0:T(8,128)S(1)}, u32[]{:S(2)}, u32[]{:S(2)}) collective-permute-start(f32[256,256]{1,0:T(8,128)S(1)} %pad_maximum_fusion.here_ref), channel_id=1, source_target_pairs={{8,16},{9,17},{10,18},{11,19},{12,20},{13,21},{14,22},{15,23},{16,... | collective-permute-start | bytes 786440 | tf_op jit(solution)/shard_map/ppermute | solution.py:503
  44.4 7.4 %collective-permute-start.9 = (f32[256,256]{1,0:T(8,128)S(1)}, f32[256,256]{1,0:T(8,128)S(1)}, u32[]{:S(2)}, u32[]{:S(2)}) collective-permute-start(f32[256,256]{1,0:T(8,128)S(1)} %pad_maximum_fusion.here_ref), channel_id=1, source_target_pairs={{0,8},{1,9},{2,10},{3,11},{4,12},{5,13},{6,14},{7,15},{8,0},{9,1},... | collective-permute-start | bytes 786440 | tf_op jit(solution)/shard_map/ppermute | solution.py:503
  54.4 7.7 %collective-permute-start.13 = (f32[128,256]{1,0:T(8,128)S(1)}, f32[128,256]{1,0:T(8,128)S(1)}, u32[]{:S(2)}, u32[]{:S(2)}) collective-permute-start(f32[128,256]{1,0:T(8,128)S(1)} %plane_first.1.a_ref.pulled_ref.old_z_ref), channel_id=1, source_target_pairs={{0,6},{1,7},{2,4},{3,5},{4,2},{5,3},{6,0},{7,1},{8,14},{9,15},{10,... | collective-permute-start | bytes 393224 | tf_op jit(solution)/shard_map/ppermute | solution.py:503
  56.2 6.7 %collective-permute-start.12 = (f32[128,256]{1,0:T(8,128)S(1)}, f32[128,256]{1,0:T(8,128)S(1)}, u32[]{:S(2)}, u32[]{:S(2)}) collective-permute-start(f32[128,256]{1,0:T(8,128)S(1)} %plane_first.1.a_ref.pulled_ref.old_z_ref), channel_id=1, source_target_pairs={{0,2},{1,3},{2,0},{3,1},{4,6},{5,7},{6,4},{7,5},{8,10},{9,11},{10,... | collective-permute-start | bytes 393224 | tf_op jit(solution)/shard_map/ppermute | solution.py:503
  56.9 6.0 %collective-permute-start.11 = (f32[128,256]{1,0:T(8,128)S(1)}, f32[128,256]{1,0:T(8,128)S(1)}, u32[]{:S(2)}, u32[]{:S(2)}) collective-permute-start(f32[128,256]{1,0:T(8,128)S(1)} %plane_first.1.a_ref.pulled_ref.old_z_ref), channel_id=1, source_target_pairs={{0,4},{1,5},{2,6},{3,7},{4,0},{5,1},{6,2},{7,3},{8,12},{9,13},{10,... | collective-permute-start | bytes 393224 | tf_op jit(solution)/shard_map/ppermute | solution.py:503
  63.5 2.5 %collective-permute-start.14 = (f32[128,256]{1,0:T(8,128)S(1)}, f32[128,256]{1,0:T(8,128)S(1)}, u32[]{:S(2)}, u32[]{:S(2)}) collective-permute-start(f32[128,256]{1,0:T(8,128)S(1)} %get-tuple-element.71), channel_id=1, source_target_pairs={{0,1},{1,0},{2,3},{3,2},{4,5},{5,4},{6,7},{7,6},{8,9},{9,8},{10,11... | collective-permute-start | bytes 393224 | tf_op jit(solution)/shard_map/ppermute | solution.py:503
  66.0 4.0 %collective-permute-start.16 = (f32[128,256]{1,0:T(8,128)S(1)}, f32[128,256]{1,0:T(8,128)S(1)}, u32[]{:S(2)}, u32[]{:S(2)}) collective-permute-start(f32[128,256]{1,0:T(8,128)S(1)} %add.61.here_ref.old_s_ref), channel_id=1, source_target_pairs={{8,16},{9,17},{10,18},{11,19},{12,20},{13,21},{14,22},{15,23},{16,... | collective-permute-start | bytes 393224 | tf_op jit(solution)/shard_map/ppermute | solution.py:503
  66.7 6.6 %collective-permute-start.15 = (f32[128,256]{1,0:T(8,128)S(1)}, f32[128,256]{1,0:T(8,128)S(1)}, u32[]{:S(2)}, u32[]{:S(2)}) collective-permute-start(f32[128,256]{1,0:T(8,128)S(1)} %add.61.here_ref.old_s_ref), channel_id=1, source_target_pairs={{0,8},{1,9},{2,10},{3,11},{4,12},{5,13},{6,14},{7,15},{8,0},{9,1},... | collective-permute-start | bytes 393224 | tf_op jit(solution)/shard_map/ppermute | solution.py:503
  75.2 4.9 %collective-permute-start.19 = (f32[136,256]{1,0:T(8,128)S(1)}, f32[136,256]{1,0:T(8,128)S(1)}, u32[]{:S(2)}, u32[]{:S(2)}) collective-permute-start(f32[136,256]{1,0:T(8,128)S(1)} %get-tuple-element.72.a_ref.pulled_ref), channel_id=1, source_target_pairs={{0,6},{1,7},{2,4},{3,5},{4,2},{5,3},{6,0},{7,1},{8,14},{9,15},{10,... | collective-permute-start | bytes 417800 | tf_op jit(solution)/shard_map/ppermute | solution.py:503
  77.6 6.6 %collective-permute-start.18 = (f32[136,256]{1,0:T(8,128)S(1)}, f32[136,256]{1,0:T(8,128)S(1)}, u32[]{:S(2)}, u32[]{:S(2)}) collective-permute-start(f32[136,256]{1,0:T(8,128)S(1)} %get-tuple-element.72.a_ref.pulled_ref), channel_id=1, source_target_pairs={{0,2},{1,3},{2,0},{3,1},{4,6},{5,7},{6,4},{7,5},{8,10},{9,11},{10,... | collective-permute-start | bytes 417800 | tf_op jit(solution)/shard_map/ppermute | solution.py:503
  77.6 6.6 %collective-permute-start.17 = (f32[136,256]{1,0:T(8,128)S(1)}, f32[136,256]{1,0:T(8,128)S(1)}, u32[]{:S(2)}, u32[]{:S(2)}) collective-permute-start(f32[136,256]{1,0:T(8,128)S(1)} %get-tuple-element.72.a_ref.pulled_ref), channel_id=1, source_target_pairs={{0,4},{1,5},{2,6},{3,7},{4,0},{5,1},{6,2},{7,3},{8,12},{9,13},{10,... | collective-permute-start | bytes 417800 | tf_op jit(solution)/shard_map/ppermute | solution.py:503
  84.8 2.7 %collective-permute-start.20 = (f32[392,256]{1,0:T(8,128)S(1)}, f32[392,256]{1,0:T(8,128)S(1)}, u32[]{:S(2)}, u32[]{:S(2)}) collective-permute-start(f32[392,256]{1,0:T(8,128)S(1)} %get-tuple-element.75), channel_id=1, source_target_pairs={{0,1},{1,0},{2,3},{3,2},{4,5},{5,4},{6,7},{7,6},{8,9},{9,8},{10,11... | collective-permute-start | bytes 1204232 | tf_op jit(solution)/shard_map/ppermute | solution.py:503
  87.5 5.7 %collective-permute-start.24 = (f32[136,256]{1,0:T(8,128)S(1)}, f32[136,256]{1,0:T(8,128)S(1)}, u32[]{:S(2)}, u32[]{:S(2)}) collective-permute-start(f32[136,256]{1,0:T(8,128)S(1)} %slice_add_fusion.1.here_ref), channel_id=1, source_target_pairs={{8,16},{9,17},{10,18},{11,19},{12,20},{13,21},{14,22},{15,23},{16,... | collective-permute-start | bytes 417800 | tf_op jit(solution)/shard_map/ppermute | solution.py:503
  88.3 6.1 %collective-permute-start.21 = (f32[136,256]{1,0:T(8,128)S(1)}, f32[136,256]{1,0:T(8,128)S(1)}, u32[]{:S(2)}, u32[]{:S(2)}) collective-permute-start(f32[136,256]{1,0:T(8,128)S(1)} %slice_add_fusion.1.here_ref), channel_id=1, source_target_pairs={{0,8},{1,9},{2,10},{3,11},{4,12},{5,13},{6,14},{7,15},{8,0},{9,1},... | collective-permute-start | bytes 417800 | tf_op jit(solution)/shard_map/ppermute | solution.py:503
  91.0 5.1 %collective-permute-start.23 = (f32[8,256]{1,0:T(8,128)S(1)}, f32[8,256]{1,0:T(8,128)S(1)}, u32[]{:S(2)}, u32[]{:S(2)}) collective-permute-start(f32[8,256]{1,0:T(8,128)S(1)} %slice.23), channel_id=1, source_target_pairs={{0,24},{1,25},{2,26},{3,27},{4,28},{5,29},{6,30},{7,31},{8,16},{9,... | collective-permute-start | bytes 24584 | tf_op jit(solution)/shard_map/ppermute | solution.py:503
  93.1 3.4 %collective-permute-start.22 = (f32[8,256]{1,0:T(8,128)S(1)}, f32[8,256]{1,0:T(8,128)S(1)}, u32[]{:S(2)}, u32[]{:S(2)}) collective-permute-start(f32[8,256]{1,0:T(8,128)S(1)} %slice.23), channel_id=1, source_target_pairs={{0,16},{1,17},{2,18},{3,19},{4,20},{5,21},{6,22},{7,23},{8,24},{9,... | collective-permute-start | bytes 24584 | tf_op jit(solution)/shard_map/ppermute | solution.py:503
  97.9 5.0 %collective-permute-start.27 = (f32[136,256]{1,0:T(8,128)S(1)}, f32[136,256]{1,0:T(8,128)S(1)}, u32[]{:S(2)}, u32[]{:S(2)}) collective-permute-start(f32[136,256]{1,0:T(8,128)S(1)} %get-tuple-element.78.a_ref.pulled_ref), channel_id=1, source_target_pairs={{0,6},{1,7},{2,4},{3,5},{4,2},{5,3},{6,0},{7,1},{8,14},{9,15},{10,... | collective-permute-start | bytes 417800 | tf_op jit(solution)/shard_map/ppermute | solution.py:503
  99.2 5.4 %collective-permute-start.26 = (f32[136,256]{1,0:T(8,128)S(1)}, f32[136,256]{1,0:T(8,128)S(1)}, u32[]{:S(2)}, u32[]{:S(2)}) collective-permute-start(f32[136,256]{1,0:T(8,128)S(1)} %get-tuple-element.78.a_ref.pulled_ref), channel_id=1, source_target_pairs={{0,2},{1,3},{2,0},{3,1},{4,6},{5,7},{6,4},{7,5},{8,10},{9,11},{10,... | collective-permute-start | bytes 417800 | tf_op jit(solution)/shard_map/ppermute | solution.py:503
  100.4 4.4 %collective-permute-start.25 = (f32[136,256]{1,0:T(8,128)S(1)}, f32[136,256]{1,0:T(8,128)S(1)}, u32[]{:S(2)}, u32[]{:S(2)}) collective-permute-start(f32[136,256]{1,0:T(8,128)S(1)} %get-tuple-element.78.a_ref.pulled_ref), channel_id=1, source_target_pairs={{0,4},{1,5},{2,6},{3,7},{4,0},{5,1},{6,2},{7,3},{8,12},{9,13},{10,... | collective-permute-start | bytes 417800 | tf_op jit(solution)/shard_map/ppermute | solution.py:503
  105.3 5.0 %collective-permute-start.28 = (f32[392,256]{1,0:T(8,128)S(1)}, f32[392,256]{1,0:T(8,128)S(1)}, u32[]{:S(2)}, u32[]{:S(2)}) collective-permute-start(f32[392,256]{1,0:T(8,128)S(1)} %get-tuple-element.82), channel_id=1, source_target_pairs={{0,1},{1,0},{2,3},{3,2},{4,5},{5,4},{6,7},{7,6},{8,9},{9,8},{10,11... | collective-permute-start | bytes 1204232 | tf_op jit(solution)/shard_map/ppermute | solution.py:503
  110.4 4.5 %collective-permute-start.29 = (f32[136,256]{1,0:T(8,128)S(1)}, f32[136,256]{1,0:T(8,128)S(1)}, u32[]{:S(2)}, u32[]{:S(2)}) collective-permute-start(f32[136,256]{1,0:T(8,128)S(1)} %slice_add_fusion.here_ref), channel_id=1, source_target_pairs={{0,8},{1,9},{2,10},{3,11},{4,12},{5,13},{6,14},{7,15},{8,16},{9,17... | collective-permute-start | bytes 417800 | tf_op jit(solution)/shard_map/ppermute | solution.py:503
  114.2 7.9 %collective-permute-start.30 = (f32[256,256]{1,0:T(8,128)}, f32[256,256]{1,0:T(8,128)}, u32[]{:S(2)}, u32[]{:S(2)}) collective-permute-start(f32[256,256]{1,0:T(8,128)} %get-tuple-element.88), channel_id=1, source_target_pairs={{0,1},{1,0},{2,3},{3,2},{4,5},{5,4},{6,7},{7,6},{8,9},{9,8},{10,11... | collective-permute-start | bytes 786440 | tf_op jit(solution)/shard_map/ppermute | solution.py:503
  116.2 14.0 %all-to-all-start = ((f32[32,8,128]{2,1,0:T(8,128)}), f32[32,8,128]{2,1,0:T(8,128)S(1)}, u32[]{:S(2)}, u32[]{:S(2)}) async-start(f32[32,8,128]{2,1,0:T(8,128)} %plane_close.1), calls=%async_computation | async-start | bytes 262144 | tf_op jit(solution)/shard_map/all_to_all | solution.py:1161
  131.8 13.3 %collective-permute-start.31 = (f32[512,128]{1,0:T(8,128)S(1)}, f32[512,128]{1,0:T(8,128)S(1)}, u32[]{:S(2)}, u32[]{:S(2)}) collective-permute-start(f32[512,128]{1,0:T(8,128)S(1)} %plane_combine.1), channel_id=1, source_target_pairs={{0,0},{1,16},{2,8},{3,24},{4,4},{5,20},{6,12},{7,28},{8,1},{9,17},... | collective-permute-start | bytes 786440 | tf_op jit(solution)/shard_map/ppermute | solution.py:503
  (12 other events, 164.2 us)

commit v19 on v18

--- a/solution.py
+++ b/solution.py
@@ -1099,11 +1099,13 @@
     parcels = [parcel, moved(parcel, over_core)]
     spec = plane_spectrum(parcel[hours:], kernels, short3, rows)
     parcels[1], seen, meta, spec = lax.optimization_barrier((parcels[1], seen, meta, spec))
-    around = [meta, moved(meta, z_two)]
+    half = meta.shape[1] // 2
+    far = moved(jnp.where(c == 0, meta[:, :half], meta[:, half:]), z_two)
     dense = spread(first, parcels, rows)
     metas = [value[hours:] for value in parcels]
     sums = dense[0] + sum(moved(value, where) for value, where in zip(dense[1:], SQUARE))
-    sums, around = lax.optimization_barrier((sums, around))
+    sums, far = lax.optimization_barrier((sums, far))
+    around = [meta, jnp.concatenate([far, moved(far, over_core)], axis=1)]
     sums = jnp.concatenate([sums, jnp.transpose(seen)], axis=0)
     sums = [sums, moved(sums, z_pair), moved(sums, z_middle)]
     coupled = plane_couple(first, around[0], rows)

time: 148 us -> 144 us (0.973)
  waiting for transfers between devices: 61.3 us -> 55.8 us
  starting transfers between devices: 50.7 us -> 52.3 us
    ppermute x32 -> x33, waiting for transfers between devices: 53.2 us -> 47.6 us  [moved(): return lax.ppermute(value, ('basin', 'tm'), pairs)]
    ppermute x32 -> x33, starting transfers between devices: 44.9 us -> 46.4 us  [moved(): return lax.ppermute(value, ('basin', 'tm'), pairs)]
  transfers between devices with their start and end apart: 33 -> 34, of which waited for: 23 -> 21; matrix products, arithmetic and copies ran while one was open for 0% -> 0% of each run, Pallas kernels for 12% -> 12%
where the time goes in v19:
time: 144 us
  waiting for transfers between devices  55.8 us (39%)
  starting transfers between devices  52.3 us (36%)
  Pallas kernels  32.7 us (23%)
  local copies, waits for them, and re-layouts  2.49 us (2%)
    ppermute x33, waiting for transfers between devices, moved(): return lax.ppermute(value, ('basin', 'tm'), pairs)  47.6 us
    ppermute x33, starting transfers between devices, moved(): return lax.ppermute(value, ('basin', 'tm'), pairs)  46.4 us
    pallas_call x2, Pallas kernels, plane_couple(): pl.pallas_call(functools.partial(plane_couple_kernel, last), in_specs=[pl...  9.56 us
    pallas_call x6, Pallas kernels, plane_call(): pl.pallas_call(kernel, in_specs=[pl.BlockSpec(memory_space=pltpu.SMEM)] *...  8.89 us
    all_to_all x1, waiting for transfers between devices, plane_shards(): close_note = lax.all_to_all(note, ('basin', 'tm'), 0, 0, tiled=False)  8.18 us
    all_to_all x1, starting transfers between devices, plane_shards(): close_note = lax.all_to_all(note, ('basin', 'tm'), 0, 0, tiled=False)  5.89 us
    pallas_call x3, Pallas kernels, plane_rows(): pl.pallas_call(plane_rows_kernel, in_specs=[pl.BlockSpec(memory_space=plt...  4.5 us
    pallas_call x1, Pallas kernels, send(): pl.pallas_call(send_kernel, in_specs=[pl.BlockSpec(memory_space=pltpu.HBM...  3.21 us
  transfers between devices with their start and end apart: 34, of which 21 were waited for; matrix products, arithmetic and copies ran while one was open for 0% of the time, Pallas kernels for 12%

profile of v19, /device:TPU:1, one launch (start us, length us, event | category | flops | bytes accessed | tf_op | source)
XLA Modules:
  0.0 143.9 jit_solution(6755847678847932118)
XLA Ops:
  1.1 4.6 %collective-permute-start.1 = (f32[256,128]{0,1:T(8,128)S(1)}, f32[256,128]{0,1:T(8,128)S(1)}, u32[]{:S(2)}, u32[]{:S(2)}) collective-permute-start(f32[256,128]{0,1:T(8,128)S(1)} %copy.14), channel_id=1, source_target_pairs={{0,0},{1,8},{2,16},{3,24},{4,4},{5,12},{6,20},{7,28},{8,2},{9,10},... | collective-permute-start | bytes 393224 | tf_op jit(solution)/shard_map/ppermute | solution.py:503
  5.7 3.2 %send.1 = f32[136,512]{1,0:T(8,128)} custom-call(s32[32,16,128]{2,1,0:T(8,128)} %inc_ref.2, f32[4096,128]{1,0:T(8,128)} %field_ref.1, s32[1,512]{1,0:T(1,128)} %bitcast.11, s32[1,256]{1,0:T(1,128)} %bitcast.14), custom_call_target="tpu_custom_call" | custom-call | flops 1 | bytes 1 | tf_op jit(solution)/shard_map/send/pallas_call | solution.py:685
  8.9 3.3 %collective-permute-start = (f32[136,512]{1,0:T(8,128)}, f32[136,512]{1,0:T(8,128)S(1)}, u32[]{:S(2)}, u32[]{:S(2)}) collective-permute-start(f32[136,512]{1,0:T(8,128)} %send.1), channel_id=1, source_target_pairs={{0,0},{1,8},{2,16},{3,24},{4,4},{5,12},{6,20},{7,28},{8,2},{9,10},... | collective-permute-start | bytes 835592 | tf_op jit(solution)/shard_map/ppermute | solution.py:503
  14.4 1.7 %collective-permute-done.3 = f32[24,512]{1,0:T(8,128)S(1)} collective-permute-done((f32[24,512]{1,0:T(8,128)S(1)}, f32[24,512]{1,0:T(8,128)S(1)}, u32[]{:S(2)}, u32[]{:S(2)}) %collective-permute-start.3) | collective-permute-done | bytes 49184 | tf_op jit(solution)/shard_map/ppermute | solution.py:503
  17.4 9.0 %collective-permute-done.mine_ref = f32[136,512]{1,0:T(8,128)S(1)} collective-permute-done((f32[136,512]{1,0:T(8,128)}, f32[136,512]{1,0:T(8,128)S(1)}, u32[]{:S(2)}, u32[]{:S(2)}) %collective-permute-start) | collective-permute-done | bytes 278560 | tf_op jit(solution)/shard_map/ppermute | solution.py:503
  27.9 1.6 %spread.1 = (f32[128,256]{1,0:T(8,128)S(1)}, f32[128,256]{1,0:T(8,128)S(1)}, f32[128,256]{1,0:T(8,128)S(1)}, f32[128,256]{1,0:T(8,128)S(1)}) custom-call(s32[6]{0:T(128)S(1)} %broadcast_multiply_fusion.first_ref, f32[136,512]{1,0:T(8,128)S(1)} %collective-permute-done.mine_ref, f32[136,512]{1,0:T(8,128)S(1)} %collective-permute-done.2.other_ref), custom_call_target="tpu_custom_call" | custom-call | flops 1 | bytes 1 | tf_op jit(solution)/shard_map/spread/pallas_call | solution.py:719
  30.8 1.4 collective-permute-start.7
  34.5 3.7 %collective-permute-done.6 = f32[128,256]{1,0:T(8,128)S(1)} collective-permute-done((f32[128,256]{1,0:T(8,128)S(1)}, f32[128,256]{1,0:T(8,128)S(1)}, u32[]{:S(2)}, u32[]{:S(2)}) %collective-permute-start.6) | collective-permute-done | bytes 131104 | tf_op jit(solution)/shard_map/ppermute | solution.py:503
  41.3 2.0 %collective-permute-start.9 = (f32[24,1024]{1,0:T(8,128)S(1)}, f32[24,1024]{1,0:T(8,128)S(1)}, u32[]{:S(2)}, u32[]{:S(2)}) collective-permute-start(f32[24,1024]{1,0:T(8,128)S(1)} %collective-permute-done.8), channel_id=1, source_target_pairs={{0,1},{1,0},{2,3},{3,2},{4,5},{5,4},{6,7},{7,6},{8,9},{9,8},{10,11... | collective-permute-start | bytes 294920 | tf_op jit(solution)/shard_map/ppermute | solution.py:503
  43.4 4.6 %plane_couple.2.refs_1_ = f32[1024,512]{1,0:T(8,128)S(1)} custom-call(s32[6]{0:T(128)S(1)} %broadcast_multiply_fusion.first_ref, f32[24,2048]{1,0:T(8,128)S(1)} %pad_maximum_fusion.1.refs_0_), custom_call_target="tpu_custom_call" | custom-call | flops 2147483648 | bytes 2000000 | tf_op jit(solution)/shard_map/plane_couple/pallas_call | solution.py:785
  48.1 2.6 %plane_first.1.a_ref.pulled_ref.old_z_ref = f32[128,256]{1,0:T(8,128)S(1)} custom-call(f32[3]{0:T(128)S(1)} %add_convert_fusion.flag_ref, f32[256,256]{1,0:T(8,128)S(1)} %pad_maximum_fusion.here_ref, f32[256,256]{1,0:T(8,128)S(1)} %collective-permute-done.10.pair_ref, f32[256,256]{1,0:T(8,128)S(1)} %collective-permute-done.11.middle_ref, ...), custom_call_target="tpu_custom_call" | custom-call | flops 1 | bytes 1 | tf_op jit(solution)/shard_map/plane_first/pallas_call | solution.py:912
  50.7 2.0 %collective-permute-start.14 = (f32[128,256]{1,0:T(8,128)S(1)}, f32[128,256]{1,0:T(8,128)S(1)}, u32[]{:S(2)}, u32[]{:S(2)}) collective-permute-start(f32[128,256]{1,0:T(8,128)S(1)} %plane_first.1.a_ref.pulled_ref.old_z_ref), channel_id=1, source_target_pairs={{0,6},{1,7},{2,4},{3,5},{4,2},{5,3},{6,0},{7,1},{8,14},{9,15},{10,... | collective-permute-start | bytes 393224 | tf_op jit(solution)/shard_map/ppermute | solution.py:503
  53.4 4.9 %plane_couple.3 = (bf16[1024,512]{1,0:T(8,128)(2,1)S(1)}, bf16[1024,512]{1,0:T(8,128)(2,1)S(1)}) custom-call(s32[6]{0:T(128)S(1)} %broadcast_multiply_fusion.first_ref, f32[24,2048]{1,0:T(8,128)S(1)} %pad_maximum_fusion.2.refs_0_, f32[1024,512]{1,0:T(8,128)S(1)} %plane_couple.2.refs_1_), custom_call_target="tpu_custom_call" | custom-call | flops 2147483648 | bytes 2000000 | tf_op jit(solution)/shard_map/plane_couple/pallas_call | solution.py:785
  58.4 1.5 %collective-permute-done.13.c_ref = f32[128,256]{1,0:T(8,128)S(1)} collective-permute-done((f32[128,256]{1,0:T(8,128)S(1)}, f32[128,256]{1,0:T(8,128)S(1)}, u32[]{:S(2)}, u32[]{:S(2)}) %collective-permute-start.13) | collective-permute-done | bytes 131104 | tf_op jit(solution)/shard_map/ppermute | solution.py:503
  63.0 2.8 %collective-permute-start.16 = (f32[128,256]{1,0:T(8,128)S(1)}, f32[128,256]{1,0:T(8,128)S(1)}, u32[]{:S(2)}, u32[]{:S(2)}) collective-permute-start(f32[128,256]{1,0:T(8,128)S(1)} %add.61.here_ref.old_s_ref), channel_id=1, source_target_pairs={{0,8},{1,9},{2,10},{3,11},{4,12},{5,13},{6,14},{7,15},{8,0},{9,1},... | collective-permute-start | bytes 393224 | tf_op jit(solution)/shard_map/ppermute | solution.py:503
  65.8 3.3 %collective-permute-done.16.pair_ref = f32[128,256]{1,0:T(8,128)S(1)} collective-permute-done((f32[128,256]{1,0:T(8,128)S(1)}, f32[128,256]{1,0:T(8,128)S(1)}, u32[]{:S(2)}, u32[]{:S(2)}) %collective-permute-start.16) | collective-permute-done | bytes 131104 | tf_op jit(solution)/shard_map/ppermute | solution.py:503
  69.1 1.8 %plane_open.1 = (f32[136,256]{1,0:T(8,128)S(1)}, f32[256,256]{1,0:T(8,128)S(1)}) custom-call(f32[3]{0:T(128)S(1)} %add_convert_fusion.flag_ref, f32[128,256]{1,0:T(8,128)S(1)} %add.61.here_ref.old_s_ref, f32[128,256]{1,0:T(8,128)S(1)} %collective-permute-done.16.pair_ref, f32[128,256]{1,0:T(8,128)S(1)} %collective-permute-done.17.middle_ref, ...), custom_call_target="tpu_custom_call" | custom-call | flops 1 | bytes 1 | tf_op jit(solution)/shard_map/plane_open/pallas_call | solution.py:912
  70.9 1.8 %collective-permute-start.20 = (f32[136,256]{1,0:T(8,128)S(1)}, f32[136,256]{1,0:T(8,128)S(1)}, u32[]{:S(2)}, u32[]{:S(2)}) collective-permute-start(f32[136,256]{1,0:T(8,128)S(1)} %get-tuple-element.70.a_ref.pulled_ref), channel_id=1, source_target_pairs={{0,6},{1,7},{2,4},{3,5},{4,2},{5,3},{6,0},{7,1},{8,14},{9,15},{10,... | collective-permute-start | bytes 417800 | tf_op jit(solution)/shard_map/ppermute | solution.py:503
  75.9 4.1 %collective-permute-done.19.c_ref = f32[136,256]{1,0:T(8,128)S(1)} collective-permute-done((f32[136,256]{1,0:T(8,128)S(1)}, f32[136,256]{1,0:T(8,128)S(1)}, u32[]{:S(2)}, u32[]{:S(2)}) %collective-permute-start.19) | collective-permute-done | bytes 139296 | tf_op jit(solution)/shard_map/ppermute | solution.py:503
  83.9 3.3 %collective-permute-start.22 = (f32[136,256]{1,0:T(8,128)S(1)}, f32[136,256]{1,0:T(8,128)S(1)}, u32[]{:S(2)}, u32[]{:S(2)}) collective-permute-start(f32[136,256]{1,0:T(8,128)S(1)} %slice_add_fusion.1.here_ref), channel_id=1, source_target_pairs={{0,8},{1,9},{2,10},{3,11},{4,12},{5,13},{6,14},{7,15},{8,0},{9,1},... | collective-permute-start | bytes 417800 | tf_op jit(solution)/shard_map/ppermute | solution.py:503
  87.1 1.5 %collective-permute-start.24 = (f32[8,256]{1,0:T(8,128)S(1)}, f32[8,256]{1,0:T(8,128)S(1)}, u32[]{:S(2)}, u32[]{:S(2)}) collective-permute-start(f32[8,256]{1,0:T(8,128)S(1)} %slice.31), channel_id=1, source_target_pairs={{0,24},{1,25},{2,26},{3,27},{4,28},{5,29},{6,30},{7,31},{8,16},{9,... | collective-permute-start | bytes 24584 | tf_op jit(solution)/shard_map/ppermute | solution.py:503
  88.7 1.9 %collective-permute-done.22.pair_ref = f32[136,256]{1,0:T(8,128)S(1)} collective-permute-done((f32[136,256]{1,0:T(8,128)S(1)}, f32[136,256]{1,0:T(8,128)S(1)}, u32[]{:S(2)}, u32[]{:S(2)}) %collective-permute-start.22) | collective-permute-done | bytes 139296 | tf_op jit(solution)/shard_map/ppermute | solution.py:503
  94.0 1.5 %collective-permute-start.28 = (f32[136,256]{1,0:T(8,128)S(1)}, f32[136,256]{1,0:T(8,128)S(1)}, u32[]{:S(2)}, u32[]{:S(2)}) collective-permute-start(f32[136,256]{1,0:T(8,128)S(1)} %get-tuple-element.76.a_ref.pulled_ref), channel_id=1, source_target_pairs={{0,6},{1,7},{2,4},{3,5},{4,2},{5,3},{6,0},{7,1},{8,14},{9,15},{10,... | collective-permute-start | bytes 417800 | tf_op jit(solution)/shard_map/ppermute | solution.py:503
  98.9 1.8 %collective-permute-done.27.c_ref = f32[136,256]{1,0:T(8,128)S(1)} collective-permute-done((f32[136,256]{1,0:T(8,128)S(1)}, f32[136,256]{1,0:T(8,128)S(1)}, u32[]{:S(2)}, u32[]{:S(2)}) %collective-permute-start.27) | collective-permute-done | bytes 139296 | tf_op jit(solution)/shard_map/ppermute | solution.py:503
  101.5 3.4 %collective-permute-start.29 = (f32[392,256]{1,0:T(8,128)S(1)}, f32[392,256]{1,0:T(8,128)S(1)}, u32[]{:S(2)}, u32[]{:S(2)}) collective-permute-start(f32[392,256]{1,0:T(8,128)S(1)} %get-tuple-element.80), channel_id=1, source_target_pairs={{0,1},{1,0},{2,3},{3,2},{4,5},{5,4},{6,7},{7,6},{8,9},{9,8},{10,11... | collective-permute-start | bytes 1204232 | tf_op jit(solution)/shard_map/ppermute | solution.py:503
  106.3 2.5 %collective-permute-start.30 = (f32[136,256]{1,0:T(8,128)S(1)}, f32[136,256]{1,0:T(8,128)S(1)}, u32[]{:S(2)}, u32[]{:S(2)}) collective-permute-start(f32[136,256]{1,0:T(8,128)S(1)} %slice_add_fusion.here_ref), channel_id=1, source_target_pairs={{0,8},{1,9},{2,10},{3,11},{4,12},{5,13},{6,14},{7,15},{8,16},{9,17... | collective-permute-start | bytes 417800 | tf_op jit(solution)/shard_map/ppermute | solution.py:503
  108.8 2.0 %plane_rows.5 = (f32[128,512]{1,0:T(8,128)S(1)}, f32[256,256]{1,0:T(8,128)}, f32[256,512]{1,0:T(8,128)S(1)}) custom-call(s32[6]{0:T(128)S(1)} %broadcast_multiply_fusion.first_ref, f32[8,512]{1,0:T(8,128)S(1)} %slice.23.class_ref.meta_ref, f32[8,512]{1,0:T(8,128)S(1)} %slice.26.meta_other_ref, f32[136,256]{1,0:T(8,128)S(1)} %get-tuple-element.76.a_ref.pulled_ref, ...), custom_call_target="tpu_custom_call" | custom-call | flops 1000000000 | bytes 2000000 | tf_op jit(solution)/shard_map/plane_rows/pallas_call | solution.py:868
  112.8 5.9 %all-to-all-start = ((f32[32,8,128]{2,1,0:T(8,128)}), f32[32,8,128]{2,1,0:T(8,128)S(1)}, u32[]{:S(2)}, u32[]{:S(2)}) async-start(f32[32,8,128]{2,1,0:T(8,128)} %plane_close.1), calls=%async_computation | async-start | bytes 262144 | tf_op jit(solution)/shard_map/all_to_all | solution.py:1163
  118.7 8.2 %all-to-all-done.close_ref = f32[32,8,128]{2,1,0:T(8,128)S(1)} async-done(((f32[32,8,128]{2,1,0:T(8,128)}), f32[32,8,128]{2,1,0:T(8,128)S(1)}, u32[]{:S(2)}, u32[]{:S(2)}) %all-to-all-start) | async-done | bytes 131104 | tf_op jit(solution)/shard_map/all_to_all | solution.py:1163
  128.2 2.6 %collective-permute-start.32 = (f32[512,128]{1,0:T(8,128)S(1)}, f32[512,128]{1,0:T(8,128)S(1)}, u32[]{:S(2)}, u32[]{:S(2)}) collective-permute-start(f32[512,128]{1,0:T(8,128)S(1)} %plane_combine.1), channel_id=1, source_target_pairs={{0,0},{1,16},{2,8},{3,24},{4,4},{5,20},{6,12},{7,28},{8,1},{9,17},... | collective-permute-start | bytes 786440 | tf_op jit(solution)/shard_map/ppermute | solution.py:503
  130.8 10.7 %collective-permute-done.32.rows_ref = f32[512,128]{1,0:T(8,128)S(1)} collective-permute-done((f32[512,128]{1,0:T(8,128)S(1)}, f32[512,128]{1,0:T(8,128)S(1)}, u32[]{:S(2)}, u32[]{:S(2)}) %collective-permute-start.32) | collective-permute-done | bytes 262176 | tf_op jit(solution)/shard_map/ppermute | solution.py:503
  141.5 2.4 %plane_finish.1 = f32[4096,128]{1,0:T(8,128)} custom-call(f32[512,128]{1,0:T(8,128)S(1)} %collective-permute-done.32.rows_ref, s32[32,16,128]{2,1,0:T(8,128)S(1)} %copy-done.2, f32[4096,128]{1,0:T(8,128)S(1)} %copy-done), custom_call_target="tpu_custom_call" | custom-call | tf_op jit(solution)/shard_map/plane_finish/pallas_call | solution.py:1063
  (97 shorter events, 35.8 us)
Async XLA Ops:
  1.1 11.8 %collective-permute-start.1 = (f32[256,128]{0,1:T(8,128)S(1)}, f32[256,128]{0,1:T(8,128)S(1)}, u32[]{:S(2)}, u32[]{:S(2)}) collective-permute-start(f32[256,128]{0,1:T(8,128)S(1)} %copy.14), channel_id=1, source_target_pairs={{0,0},{1,8},{2,16},{3,24},{4,4},{5,12},{6,20},{7,28},{8,2},{9,10},... | collective-permute-start | bytes 393224 | tf_op jit(solution)/shard_map/ppermute | solution.py:503
  8.9 17.5 %collective-permute-start = (f32[136,512]{1,0:T(8,128)}, f32[136,512]{1,0:T(8,128)S(1)}, u32[]{:S(2)}, u32[]{:S(2)}) collective-permute-start(f32[136,512]{1,0:T(8,128)} %send.1), channel_id=1, source_target_pairs={{0,0},{1,8},{2,16},{3,24},{4,4},{5,12},{6,20},{7,28},{8,2},{9,10},... | collective-permute-start | bytes 835592 | tf_op jit(solution)/shard_map/ppermute | solution.py:503
  13.1 3.0 %collective-permute-start.3 = (f32[24,512]{1,0:T(8,128)S(1)}, f32[24,512]{1,0:T(8,128)S(1)}, u32[]{:S(2)}, u32[]{:S(2)}) collective-permute-start(f32[24,512]{1,0:T(8,128)S(1)} %describe.1), channel_id=1, source_target_pairs={{0,4},{1,5},{2,6},{3,7},{4,0},{5,1},{6,2},{7,3},{8,12},{9,13},{10,... | collective-permute-start | bytes 147464 | tf_op jit(solution)/shard_map/ppermute | solution.py:503
  16.1 11.0 %collective-permute-start.4 = (f32[24,1024]{1,0:T(8,128)S(1)}, f32[24,1024]{1,0:T(8,128)S(1)}, u32[]{:S(2)}, u32[]{:S(2)}) collective-permute-start(f32[24,1024]{1,0:T(8,128)S(1)} %pad_maximum_fusion.3), channel_id=1, source_target_pairs={{0,8},{1,9},{2,10},{3,11},{4,12},{5,13},{6,14},{7,15},{8,0},{9,1},... | collective-permute-start | bytes 294920 | tf_op jit(solution)/shard_map/ppermute | solution.py:503
  29.5 5.0 %collective-permute-start.5 = (f32[128,256]{1,0:T(8,128)S(1)}, f32[128,256]{1,0:T(8,128)S(1)}, u32[]{:S(2)}, u32[]{:S(2)}) collective-permute-start(f32[128,256]{1,0:T(8,128)S(1)} %get-tuple-element.54), channel_id=1, source_target_pairs={{0,4},{1,5},{2,6},{3,7},{4,0},{5,1},{6,2},{7,3},{8,12},{9,13},{10,... | collective-permute-start | bytes 393224 | tf_op jit(solution)/shard_map/ppermute | solution.py:503
  30.8 7.4 %collective-permute-start.6 = (f32[128,256]{1,0:T(8,128)S(1)}, f32[128,256]{1,0:T(8,128)S(1)}, u32[]{:S(2)}, u32[]{:S(2)}) collective-permute-start(f32[128,256]{1,0:T(8,128)S(1)} %get-tuple-element.55), channel_id=1, source_target_pairs={{0,2},{1,3},{2,0},{3,1},{4,6},{5,7},{6,4},{7,5},{8,10},{9,11},{10,... | collective-permute-start | bytes 393224 | tf_op jit(solution)/shard_map/ppermute | solution.py:503
  30.8 7.4 %collective-permute-start.7 = (f32[128,256]{1,0:T(8,128)S(1)}, f32[128,256]{1,0:T(8,128)S(1)}, u32[]{:S(2)}, u32[]{:S(2)}) collective-permute-start(f32[128,256]{1,0:T(8,128)S(1)} %get-tuple-element.56), channel_id=1, source_target_pairs={{0,6},{1,7},{2,4},{3,5},{4,2},{5,3},{6,0},{7,1},{8,14},{9,15},{10,... | collective-permute-start | bytes 393224 | tf_op jit(solution)/shard_map/ppermute | solution.py:503
  32.2 7.1 %collective-permute-start.8 = (f32[24,1024]{1,0:T(8,128)S(1)}, f32[24,1024]{1,0:T(8,128)S(1)}, u32[]{:S(2)}, u32[]{:S(2)}) collective-permute-start(f32[24,1024]{1,0:T(8,128)S(1)} %slice_select_fusion), channel_id=1, source_target_pairs={{0,16},{1,17},{2,18},{3,19},{4,20},{5,21},{6,22},{7,23},{8,24},{9,... | collective-permute-start | bytes 294920 | tf_op jit(solution)/shard_map/ppermute | solution.py:503
  39.4 8.7 %collective-permute-start.11 = (f32[256,256]{1,0:T(8,128)S(1)}, f32[256,256]{1,0:T(8,128)S(1)}, u32[]{:S(2)}, u32[]{:S(2)}) collective-permute-start(f32[256,256]{1,0:T(8,128)S(1)} %pad_maximum_fusion.here_ref), channel_id=1, source_target_pairs={{8,16},{9,17},{10,18},{11,19},{12,20},{13,21},{14,22},{15,23},{16,... | collective-permute-start | bytes 786440 | tf_op jit(solution)/shard_map/ppermute | solution.py:503
  40.2 7.9 %collective-permute-start.10 = (f32[256,256]{1,0:T(8,128)S(1)}, f32[256,256]{1,0:T(8,128)S(1)}, u32[]{:S(2)}, u32[]{:S(2)}) collective-permute-start(f32[256,256]{1,0:T(8,128)S(1)} %pad_maximum_fusion.here_ref), channel_id=1, source_target_pairs={{0,8},{1,9},{2,10},{3,11},{4,12},{5,13},{6,14},{7,15},{8,0},{9,1},... | collective-permute-start | bytes 786440 | tf_op jit(solution)/shard_map/ppermute | solution.py:503
  41.3 6.7 %collective-permute-start.9 = (f32[24,1024]{1,0:T(8,128)S(1)}, f32[24,1024]{1,0:T(8,128)S(1)}, u32[]{:S(2)}, u32[]{:S(2)}) collective-permute-start(f32[24,1024]{1,0:T(8,128)S(1)} %collective-permute-done.8), channel_id=1, source_target_pairs={{0,1},{1,0},{2,3},{3,2},{4,5},{5,4},{6,7},{7,6},{8,9},{9,8},{10,11... | collective-permute-start | bytes 294920 | tf_op jit(solution)/shard_map/ppermute | solution.py:503
  50.7 7.7 %collective-permute-start.14 = (f32[128,256]{1,0:T(8,128)S(1)}, f32[128,256]{1,0:T(8,128)S(1)}, u32[]{:S(2)}, u32[]{:S(2)}) collective-permute-start(f32[128,256]{1,0:T(8,128)S(1)} %plane_first.1.a_ref.pulled_ref.old_z_ref), channel_id=1, source_target_pairs={{0,6},{1,7},{2,4},{3,5},{4,2},{5,3},{6,0},{7,1},{8,14},{9,15},{10,... | collective-permute-start | bytes 393224 | tf_op jit(solution)/shard_map/ppermute | solution.py:503
  52.7 7.2 %collective-permute-start.13 = (f32[128,256]{1,0:T(8,128)S(1)}, f32[128,256]{1,0:T(8,128)S(1)}, u32[]{:S(2)}, u32[]{:S(2)}) collective-permute-start(f32[128,256]{1,0:T(8,128)S(1)} %plane_first.1.a_ref.pulled_ref.old_z_ref), channel_id=1, source_target_pairs={{0,2},{1,3},{2,0},{3,1},{4,6},{5,7},{6,4},{7,5},{8,10},{9,11},{10,... | collective-permute-start | bytes 393224 | tf_op jit(solution)/shard_map/ppermute | solution.py:503
  53.1 6.8 %collective-permute-start.12 = (f32[128,256]{1,0:T(8,128)S(1)}, f32[128,256]{1,0:T(8,128)S(1)}, u32[]{:S(2)}, u32[]{:S(2)}) collective-permute-start(f32[128,256]{1,0:T(8,128)S(1)} %plane_first.1.a_ref.pulled_ref.old_z_ref), channel_id=1, source_target_pairs={{0,4},{1,5},{2,6},{3,7},{4,0},{5,1},{6,2},{7,3},{8,12},{9,13},{10,... | collective-permute-start | bytes 393224 | tf_op jit(solution)/shard_map/ppermute | solution.py:503
  62.4 3.5 %collective-permute-start.17 = (f32[128,256]{1,0:T(8,128)S(1)}, f32[128,256]{1,0:T(8,128)S(1)}, u32[]{:S(2)}, u32[]{:S(2)}) collective-permute-start(f32[128,256]{1,0:T(8,128)S(1)} %add.61.here_ref.old_s_ref), channel_id=1, source_target_pairs={{8,16},{9,17},{10,18},{11,19},{12,20},{13,21},{14,22},{15,23},{16,... | collective-permute-start | bytes 393224 | tf_op jit(solution)/shard_map/ppermute | solution.py:503
  63.0 6.1 %collective-permute-start.16 = (f32[128,256]{1,0:T(8,128)S(1)}, f32[128,256]{1,0:T(8,128)S(1)}, u32[]{:S(2)}, u32[]{:S(2)}) collective-permute-start(f32[128,256]{1,0:T(8,128)S(1)} %add.61.here_ref.old_s_ref), channel_id=1, source_target_pairs={{0,8},{1,9},{2,10},{3,11},{4,12},{5,13},{6,14},{7,15},{8,0},{9,1},... | collective-permute-start | bytes 393224 | tf_op jit(solution)/shard_map/ppermute | solution.py:503
  70.9 4.9 %collective-permute-start.20 = (f32[136,256]{1,0:T(8,128)S(1)}, f32[136,256]{1,0:T(8,128)S(1)}, u32[]{:S(2)}, u32[]{:S(2)}) collective-permute-start(f32[136,256]{1,0:T(8,128)S(1)} %get-tuple-element.70.a_ref.pulled_ref), channel_id=1, source_target_pairs={{0,6},{1,7},{2,4},{3,5},{4,2},{5,3},{6,0},{7,1},{8,14},{9,15},{10,... | collective-permute-start | bytes 417800 | tf_op jit(solution)/shard_map/ppermute | solution.py:503
  72.8 7.2 %collective-permute-start.19 = (f32[136,256]{1,0:T(8,128)S(1)}, f32[136,256]{1,0:T(8,128)S(1)}, u32[]{:S(2)}, u32[]{:S(2)}) collective-permute-start(f32[136,256]{1,0:T(8,128)S(1)} %get-tuple-element.70.a_ref.pulled_ref), channel_id=1, source_target_pairs={{0,2},{1,3},{2,0},{3,1},{4,6},{5,7},{6,4},{7,5},{8,10},{9,11},{10,... | collective-permute-start | bytes 417800 | tf_op jit(solution)/shard_map/ppermute | solution.py:503
  73.4 6.6 %collective-permute-start.18 = (f32[136,256]{1,0:T(8,128)S(1)}, f32[136,256]{1,0:T(8,128)S(1)}, u32[]{:S(2)}, u32[]{:S(2)}) collective-permute-start(f32[136,256]{1,0:T(8,128)S(1)} %get-tuple-element.70.a_ref.pulled_ref), channel_id=1, source_target_pairs={{0,4},{1,5},{2,6},{3,7},{4,0},{5,1},{6,2},{7,3},{8,12},{9,13},{10,... | collective-permute-start | bytes 417800 | tf_op jit(solution)/shard_map/ppermute | solution.py:503
  80.5 2.5 %collective-permute-start.21 = (f32[392,256]{1,0:T(8,128)S(1)}, f32[392,256]{1,0:T(8,128)S(1)}, u32[]{:S(2)}, u32[]{:S(2)}) collective-permute-start(f32[392,256]{1,0:T(8,128)S(1)} %get-tuple-element.73), channel_id=1, source_target_pairs={{0,1},{1,0},{2,3},{3,2},{4,5},{5,4},{6,7},{7,6},{8,9},{9,8},{10,11... | collective-permute-start | bytes 1204232 | tf_op jit(solution)/shard_map/ppermute | solution.py:503
  83.0 5.7 %collective-permute-start.25 = (f32[136,256]{1,0:T(8,128)S(1)}, f32[136,256]{1,0:T(8,128)S(1)}, u32[]{:S(2)}, u32[]{:S(2)}) collective-permute-start(f32[136,256]{1,0:T(8,128)S(1)} %slice_add_fusion.1.here_ref), channel_id=1, source_target_pairs={{8,16},{9,17},{10,18},{11,19},{12,20},{13,21},{14,22},{15,23},{16,... | collective-permute-start | bytes 417800 | tf_op jit(solution)/shard_map/ppermute | solution.py:503
  83.9 6.7 %collective-permute-start.22 = (f32[136,256]{1,0:T(8,128)S(1)}, f32[136,256]{1,0:T(8,128)S(1)}, u32[]{:S(2)}, u32[]{:S(2)}) collective-permute-start(f32[136,256]{1,0:T(8,128)S(1)} %slice_add_fusion.1.here_ref), channel_id=1, source_target_pairs={{0,8},{1,9},{2,10},{3,11},{4,12},{5,13},{6,14},{7,15},{8,0},{9,1},... | collective-permute-start | bytes 417800 | tf_op jit(solution)/shard_map/ppermute | solution.py:503
  87.1 4.7 %collective-permute-start.24 = (f32[8,256]{1,0:T(8,128)S(1)}, f32[8,256]{1,0:T(8,128)S(1)}, u32[]{:S(2)}, u32[]{:S(2)}) collective-permute-start(f32[8,256]{1,0:T(8,128)S(1)} %slice.31), channel_id=1, source_target_pairs={{0,24},{1,25},{2,26},{3,27},{4,28},{5,29},{6,30},{7,31},{8,16},{9,... | collective-permute-start | bytes 24584 | tf_op jit(solution)/shard_map/ppermute | solution.py:503
  88.7 3.4 %collective-permute-start.23 = (f32[8,256]{1,0:T(8,128)S(1)}, f32[8,256]{1,0:T(8,128)S(1)}, u32[]{:S(2)}, u32[]{:S(2)}) collective-permute-start(f32[8,256]{1,0:T(8,128)S(1)} %slice.31), channel_id=1, source_target_pairs={{0,16},{1,17},{2,18},{3,19},{4,20},{5,21},{6,22},{7,23},{8,24},{9,... | collective-permute-start | bytes 24584 | tf_op jit(solution)/shard_map/ppermute | solution.py:503
  94.0 4.9 %collective-permute-start.28 = (f32[136,256]{1,0:T(8,128)S(1)}, f32[136,256]{1,0:T(8,128)S(1)}, u32[]{:S(2)}, u32[]{:S(2)}) collective-permute-start(f32[136,256]{1,0:T(8,128)S(1)} %get-tuple-element.76.a_ref.pulled_ref), channel_id=1, source_target_pairs={{0,6},{1,7},{2,4},{3,5},{4,2},{5,3},{6,0},{7,1},{8,14},{9,15},{10,... | collective-permute-start | bytes 417800 | tf_op jit(solution)/shard_map/ppermute | solution.py:503
  95.5 5.3 %collective-permute-start.27 = (f32[136,256]{1,0:T(8,128)S(1)}, f32[136,256]{1,0:T(8,128)S(1)}, u32[]{:S(2)}, u32[]{:S(2)}) collective-permute-start(f32[136,256]{1,0:T(8,128)S(1)} %get-tuple-element.76.a_ref.pulled_ref), channel_id=1, source_target_pairs={{0,2},{1,3},{2,0},{3,1},{4,6},{5,7},{6,4},{7,5},{8,10},{9,11},{10,... | collective-permute-start | bytes 417800 | tf_op jit(solution)/shard_map/ppermute | solution.py:503
  96.3 4.6 %collective-permute-start.26 = (f32[136,256]{1,0:T(8,128)S(1)}, f32[136,256]{1,0:T(8,128)S(1)}, u32[]{:S(2)}, u32[]{:S(2)}) collective-permute-start(f32[136,256]{1,0:T(8,128)S(1)} %get-tuple-element.76.a_ref.pulled_ref), channel_id=1, source_target_pairs={{0,4},{1,5},{2,6},{3,7},{4,0},{5,1},{6,2},{7,3},{8,12},{9,13},{10,... | collective-permute-start | bytes 417800 | tf_op jit(solution)/shard_map/ppermute | solution.py:503
  101.5 4.8 %collective-permute-start.29 = (f32[392,256]{1,0:T(8,128)S(1)}, f32[392,256]{1,0:T(8,128)S(1)}, u32[]{:S(2)}, u32[]{:S(2)}) collective-permute-start(f32[392,256]{1,0:T(8,128)S(1)} %get-tuple-element.80), channel_id=1, source_target_pairs={{0,1},{1,0},{2,3},{3,2},{4,5},{5,4},{6,7},{7,6},{8,9},{9,8},{10,11... | collective-permute-start | bytes 1204232 | tf_op jit(solution)/shard_map/ppermute | solution.py:503
  106.3 5.1 %collective-permute-start.30 = (f32[136,256]{1,0:T(8,128)S(1)}, f32[136,256]{1,0:T(8,128)S(1)}, u32[]{:S(2)}, u32[]{:S(2)}) collective-permute-start(f32[136,256]{1,0:T(8,128)S(1)} %slice_add_fusion.here_ref), channel_id=1, source_target_pairs={{0,8},{1,9},{2,10},{3,11},{4,12},{5,13},{6,14},{7,15},{8,16},{9,17... | collective-permute-start | bytes 417800 | tf_op jit(solution)/shard_map/ppermute | solution.py:503
  110.8 8.0 %collective-permute-start.31 = (f32[256,256]{1,0:T(8,128)}, f32[256,256]{1,0:T(8,128)S(1)}, u32[]{:S(2)}, u32[]{:S(2)}) collective-permute-start(f32[256,256]{1,0:T(8,128)} %get-tuple-element.86), channel_id=1, source_target_pairs={{0,1},{1,0},{2,3},{3,2},{4,5},{5,4},{6,7},{7,6},{8,9},{9,8},{10,11... | collective-permute-start | bytes 786440 | tf_op jit(solution)/shard_map/ppermute | solution.py:503
  112.8 14.1 %all-to-all-start = ((f32[32,8,128]{2,1,0:T(8,128)}), f32[32,8,128]{2,1,0:T(8,128)S(1)}, u32[]{:S(2)}, u32[]{:S(2)}) async-start(f32[32,8,128]{2,1,0:T(8,128)} %plane_close.1), calls=%async_computation | async-start | bytes 262144 | tf_op jit(solution)/shard_map/all_to_all | solution.py:1163
  128.2 13.3 %collective-permute-start.32 = (f32[512,128]{1,0:T(8,128)S(1)}, f32[512,128]{1,0:T(8,128)S(1)}, u32[]{:S(2)}, u32[]{:S(2)}) collective-permute-start(f32[512,128]{1,0:T(8,128)S(1)} %plane_combine.1), channel_id=1, source_target_pairs={{0,0},{1,16},{2,8},{3,24},{4,4},{5,20},{6,12},{7,28},{8,1},{9,17},... | collective-permute-start | bytes 786440 | tf_op jit(solution)/shard_map/ppermute | solution.py:503
  (15 other events, 172.4 us)

commit v20 on v19

--- a/solution.py
+++ b/solution.py
@@ -681,7 +681,7 @@
 
 def send(incidence, field, row_gauge, gauge_kernel):
     count, rows = row_gauge.shape[0], gauge_kernel.shape[0]
-    chunks = 4
+    chunks = 8
     return pl.pallas_call(
         send_kernel,
         in_specs=[pl.BlockSpec(memory_space=pltpu.HBM)] * 4,
@@ -1087,10 +1087,10 @@
     forward3, inverse_first3, inverse_last3, short3 = turned_transforms(3)
     block, noted = (hours, rows), (hours + NOTE, rows)
 
-    seen = moved(observed, to_plane)
     parcel = send(incidence, first_guess, row_gauge, gauge_kernel)
-    parcel, near = lax.optimization_barrier((parcel, incidence))
+    parcel, near, seen = lax.optimization_barrier((parcel, incidence, observed))
     parcel = moved(parcel, to_plane)
+    seen = moved(seen, to_plane)
     near, seen = lax.optimization_barrier((near, seen))
     meta = describe(near, row_gauge)
     meta = jnp.concatenate([meta, moved(meta, over_x)], axis=1)

time: 144 us -> 148 us (1.028)
  starting transfers between devices: 52.3 us -> 56.1 us
    ppermute x33, starting transfers between devices: 46.4 us -> 50.3 us  [moved(): return lax.ppermute(value, ('basin', 'tm'), pairs)]
  transfers between devices with their start and end apart: 34 -> 34, of which waited for: 21 -> 19; matrix products, arithmetic and copies ran while one was open for 0% -> 0% of each run, Pallas kernels for 12% -> 12%
where the time goes in v20:
time: 148 us
  starting transfers between devices  56.1 us (38%)
  waiting for transfers between devices  55.5 us (38%)
  Pallas kernels  33.9 us (23%)
  local copies, waits for them, and re-layouts  1.54 us (1%)
    ppermute x33, starting transfers between devices, moved(): return lax.ppermute(value, ('basin', 'tm'), pairs)  50.3 us
    ppermute x33, waiting for transfers between devices, moved(): return lax.ppermute(value, ('basin', 'tm'), pairs)  47.3 us
    pallas_call x2, Pallas kernels, plane_couple(): pl.pallas_call(functools.partial(plane_couple_kernel, last), in_specs=[pl...  9.56 us
    pallas_call x6, Pallas kernels, plane_call(): pl.pallas_call(kernel, in_specs=[pl.BlockSpec(memory_space=pltpu.SMEM)] *...  8.9 us
    all_to_all x1, waiting for transfers between devices, plane_shards(): close_note = lax.all_to_all(note, ('basin', 'tm'), 0, 0, tiled=False)  8.18 us
    all_to_all x1, starting transfers between devices, plane_shards(): close_note = lax.all_to_all(note, ('basin', 'tm'), 0, 0, tiled=False)  5.83 us
    pallas_call x3, Pallas kernels, plane_rows(): pl.pallas_call(plane_rows_kernel, in_specs=[pl.BlockSpec(memory_space=plt...  4.5 us
    pallas_call x1, Pallas kernels, send(): pl.pallas_call(send_kernel, in_specs=[pl.BlockSpec(memory_space=pltpu.HBM...  4.45 us
  transfers between devices with their start and end apart: 34, of which 19 were waited for; matrix products, arithmetic and copies ran while one was open for 0% of the time, Pallas kernels for 12%

profile of v20, /device:TPU:1, one launch (start us, length us, event | category | flops | bytes accessed | tf_op | source)
XLA Modules:
  0.0 147.8 jit_solution(16884318467052233820)
XLA Ops:
  0.0 4.5 %send.1 = f32[136,512]{1,0:T(8,128)} custom-call(s32[32,16,128]{2,1,0:T(8,128)} %inc_ref.2, f32[4096,128]{1,0:T(8,128)} %field_ref.1, s32[1,512]{1,0:T(1,128)} %bitcast.11, s32[1,256]{1,0:T(1,128)} %bitcast.14), custom_call_target="tpu_custom_call" | custom-call | flops 1 | bytes 1 | tf_op jit(solution)/shard_map/send/pallas_call | solution.py:685
  4.6 4.6 %collective-permute-start.1 = (f32[256,128]{0,1:T(8,128)S(1)}, f32[256,128]{0,1:T(8,128)S(1)}, u32[]{:S(2)}, u32[]{:S(2)}) collective-permute-start(f32[256,128]{0,1:T(8,128)S(1)} %copy.14), channel_id=1, source_target_pairs={{0,0},{1,8},{2,16},{3,24},{4,4},{5,12},{6,20},{7,28},{8,2},{9,10},... | collective-permute-start | bytes 393224 | tf_op jit(solution)/shard_map/ppermute | solution.py:503
  9.2 3.3 %collective-permute-start = (f32[136,512]{1,0:T(8,128)}, f32[136,512]{1,0:T(8,128)S(1)}, u32[]{:S(2)}, u32[]{:S(2)}) collective-permute-start(f32[136,512]{1,0:T(8,128)} %send.1), channel_id=1, source_target_pairs={{0,0},{1,8},{2,16},{3,24},{4,4},{5,12},{6,20},{7,28},{8,2},{9,10},... | collective-permute-start | bytes 835592 | tf_op jit(solution)/shard_map/ppermute | solution.py:503
  12.7 4.4 %collective-permute-done.1 = f32[256,128]{0,1:T(8,128)S(1)} collective-permute-done((f32[256,128]{0,1:T(8,128)S(1)}, f32[256,128]{0,1:T(8,128)S(1)}, u32[]{:S(2)}, u32[]{:S(2)}) %collective-permute-start.1) | collective-permute-done | bytes 131104 | tf_op jit(solution)/shard_map/ppermute | solution.py:503
  18.5 1.7 %collective-permute-done.3 = f32[24,512]{1,0:T(8,128)S(1)} collective-permute-done((f32[24,512]{1,0:T(8,128)S(1)}, f32[24,512]{1,0:T(8,128)S(1)}, u32[]{:S(2)}, u32[]{:S(2)}) %collective-permute-start.3) | collective-permute-done | bytes 49184 | tf_op jit(solution)/shard_map/ppermute | solution.py:503
  20.3 8.0 %collective-permute-done.mine_ref = f32[136,512]{1,0:T(8,128)S(1)} collective-permute-done((f32[136,512]{1,0:T(8,128)}, f32[136,512]{1,0:T(8,128)S(1)}, u32[]{:S(2)}, u32[]{:S(2)}) %collective-permute-start) | collective-permute-done | bytes 278560 | tf_op jit(solution)/shard_map/ppermute | solution.py:503
  29.9 1.6 %spread.1 = (f32[128,256]{1,0:T(8,128)S(1)}, f32[128,256]{1,0:T(8,128)S(1)}, f32[128,256]{1,0:T(8,128)S(1)}, f32[128,256]{1,0:T(8,128)S(1)}) custom-call(s32[6]{0:T(128)S(1)} %broadcast_multiply_fusion.first_ref, f32[136,512]{1,0:T(8,128)S(1)} %collective-permute-done.mine_ref, f32[136,512]{1,0:T(8,128)S(1)} %collective-permute-done.2.other_ref), custom_call_target="tpu_custom_call" | custom-call | flops 1 | bytes 1 | tf_op jit(solution)/shard_map/spread/pallas_call | solution.py:719
  32.7 1.6 %collective-permute-start.6 = (f32[128,256]{1,0:T(8,128)S(1)}, f32[128,256]{1,0:T(8,128)S(1)}, u32[]{:S(2)}, u32[]{:S(2)}) collective-permute-start(f32[128,256]{1,0:T(8,128)S(1)} %get-tuple-element.57), channel_id=1, source_target_pairs={{0,2},{1,3},{2,0},{3,1},{4,6},{5,7},{6,4},{7,5},{8,10},{9,11},{10,... | collective-permute-start | bytes 393224 | tf_op jit(solution)/shard_map/ppermute | solution.py:503
  34.3 2.8 %collective-permute-start.8 = (f32[24,1024]{1,0:T(8,128)S(1)}, f32[24,1024]{1,0:T(8,128)S(1)}, u32[]{:S(2)}, u32[]{:S(2)}) collective-permute-start(f32[24,1024]{1,0:T(8,128)S(1)} %slice_select_fusion), channel_id=1, source_target_pairs={{0,16},{1,17},{2,18},{3,19},{4,20},{5,21},{6,22},{7,23},{8,24},{9,... | collective-permute-start | bytes 294920 | tf_op jit(solution)/shard_map/ppermute | solution.py:503
  37.1 2.5 %collective-permute-done.7 = f32[128,256]{1,0:T(8,128)S(1)} collective-permute-done((f32[128,256]{1,0:T(8,128)S(1)}, f32[128,256]{1,0:T(8,128)S(1)}, u32[]{:S(2)}, u32[]{:S(2)}) %collective-permute-start.7) | collective-permute-done | bytes 131104 | tf_op jit(solution)/shard_map/ppermute | solution.py:503
  41.3 3.9 %collective-permute-start.10 = (f32[256,256]{1,0:T(8,128)S(1)}, f32[256,256]{1,0:T(8,128)S(1)}, u32[]{:S(2)}, u32[]{:S(2)}) collective-permute-start(f32[256,256]{1,0:T(8,128)S(1)} %pad_maximum_fusion.here_ref), channel_id=1, source_target_pairs={{0,8},{1,9},{2,10},{3,11},{4,12},{5,13},{6,14},{7,15},{8,0},{9,1},... | collective-permute-start | bytes 786440 | tf_op jit(solution)/shard_map/ppermute | solution.py:503
  45.2 2.8 %collective-permute-start.9 = (f32[24,1024]{1,0:T(8,128)S(1)}, f32[24,1024]{1,0:T(8,128)S(1)}, u32[]{:S(2)}, u32[]{:S(2)}) collective-permute-start(f32[24,1024]{1,0:T(8,128)S(1)} %collective-permute-done.8), channel_id=1, source_target_pairs={{0,1},{1,0},{2,3},{3,2},{4,5},{5,4},{6,7},{7,6},{8,9},{9,8},{10,11... | collective-permute-start | bytes 294920 | tf_op jit(solution)/shard_map/ppermute | solution.py:503
  47.9 4.6 %plane_couple.2.refs_1_ = f32[1024,512]{1,0:T(8,128)S(1)} custom-call(s32[6]{0:T(128)S(1)} %broadcast_multiply_fusion.first_ref, f32[24,2048]{1,0:T(8,128)S(1)} %pad_maximum_fusion.1.refs_0_), custom_call_target="tpu_custom_call" | custom-call | flops 2147483648 | bytes 2000000 | tf_op jit(solution)/shard_map/plane_couple/pallas_call | solution.py:785
  52.7 2.6 %plane_first.1.a_ref.pulled_ref.old_z_ref = f32[128,256]{1,0:T(8,128)S(1)} custom-call(f32[3]{0:T(128)S(1)} %add_convert_fusion.flag_ref, f32[256,256]{1,0:T(8,128)S(1)} %pad_maximum_fusion.here_ref, f32[256,256]{1,0:T(8,128)S(1)} %collective-permute-done.10.pair_ref, f32[256,256]{1,0:T(8,128)S(1)} %collective-permute-done.11.middle_ref, ...), custom_call_target="tpu_custom_call" | custom-call | flops 1 | bytes 1 | tf_op jit(solution)/shard_map/plane_first/pallas_call | solution.py:912
  55.3 2.4 %collective-permute-start.14 = (f32[128,256]{1,0:T(8,128)S(1)}, f32[128,256]{1,0:T(8,128)S(1)}, u32[]{:S(2)}, u32[]{:S(2)}) collective-permute-start(f32[128,256]{1,0:T(8,128)S(1)} %plane_first.1.a_ref.pulled_ref.old_z_ref), channel_id=1, source_target_pairs={{0,6},{1,7},{2,4},{3,5},{4,2},{5,3},{6,0},{7,1},{8,14},{9,15},{10,... | collective-permute-start | bytes 393224 | tf_op jit(solution)/shard_map/ppermute | solution.py:503
  58.1 4.9 %plane_couple.3 = (bf16[1024,512]{1,0:T(8,128)(2,1)S(1)}, bf16[1024,512]{1,0:T(8,128)(2,1)S(1)}) custom-call(s32[6]{0:T(128)S(1)} %broadcast_multiply_fusion.first_ref, f32[24,2048]{1,0:T(8,128)S(1)} %pad_maximum_fusion.2.refs_0_, f32[1024,512]{1,0:T(8,128)S(1)} %plane_couple.2.refs_1_), custom_call_target="tpu_custom_call" | custom-call | flops 2147483648 | bytes 2000000 | tf_op jit(solution)/shard_map/plane_couple/pallas_call | solution.py:785
  67.6 1.9 %collective-permute-start.16 = (f32[128,256]{1,0:T(8,128)S(1)}, f32[128,256]{1,0:T(8,128)S(1)}, u32[]{:S(2)}, u32[]{:S(2)}) collective-permute-start(f32[128,256]{1,0:T(8,128)S(1)} %add.61.here_ref.old_s_ref), channel_id=1, source_target_pairs={{0,8},{1,9},{2,10},{3,11},{4,12},{5,13},{6,14},{7,15},{8,0},{9,1},... | collective-permute-start | bytes 393224 | tf_op jit(solution)/shard_map/ppermute | solution.py:503
  69.5 3.3 %collective-permute-done.16.pair_ref = f32[128,256]{1,0:T(8,128)S(1)} collective-permute-done((f32[128,256]{1,0:T(8,128)S(1)}, f32[128,256]{1,0:T(8,128)S(1)}, u32[]{:S(2)}, u32[]{:S(2)}) %collective-permute-start.16) | collective-permute-done | bytes 131104 | tf_op jit(solution)/shard_map/ppermute | solution.py:503
  72.8 1.8 %plane_open.1 = (f32[136,256]{1,0:T(8,128)S(1)}, f32[256,256]{1,0:T(8,128)S(1)}) custom-call(f32[3]{0:T(128)S(1)} %add_convert_fusion.flag_ref, f32[128,256]{1,0:T(8,128)S(1)} %add.61.here_ref.old_s_ref, f32[128,256]{1,0:T(8,128)S(1)} %collective-permute-done.16.pair_ref, f32[128,256]{1,0:T(8,128)S(1)} %collective-permute-done.17.middle_ref, ...), custom_call_target="tpu_custom_call" | custom-call | flops 1 | bytes 1 | tf_op jit(solution)/shard_map/plane_open/pallas_call | solution.py:912
  74.6 2.0 %collective-permute-start.20 = (f32[136,256]{1,0:T(8,128)S(1)}, f32[136,256]{1,0:T(8,128)S(1)}, u32[]{:S(2)}, u32[]{:S(2)}) collective-permute-start(f32[136,256]{1,0:T(8,128)S(1)} %get-tuple-element.72.a_ref.pulled_ref), channel_id=1, source_target_pairs={{0,6},{1,7},{2,4},{3,5},{4,2},{5,3},{6,0},{7,1},{8,14},{9,15},{10,... | collective-permute-start | bytes 417800 | tf_op jit(solution)/shard_map/ppermute | solution.py:503
  79.5 4.1 %collective-permute-done.19.c_ref = f32[136,256]{1,0:T(8,128)S(1)} collective-permute-done((f32[136,256]{1,0:T(8,128)S(1)}, f32[136,256]{1,0:T(8,128)S(1)}, u32[]{:S(2)}, u32[]{:S(2)}) %collective-permute-start.19) | collective-permute-done | bytes 139296 | tf_op jit(solution)/shard_map/ppermute | solution.py:503
  87.6 3.4 %collective-permute-start.22 = (f32[136,256]{1,0:T(8,128)S(1)}, f32[136,256]{1,0:T(8,128)S(1)}, u32[]{:S(2)}, u32[]{:S(2)}) collective-permute-start(f32[136,256]{1,0:T(8,128)S(1)} %slice_add_fusion.1.here_ref), channel_id=1, source_target_pairs={{0,8},{1,9},{2,10},{3,11},{4,12},{5,13},{6,14},{7,15},{8,0},{9,1},... | collective-permute-start | bytes 417800 | tf_op jit(solution)/shard_map/ppermute | solution.py:503
  92.4 2.0 %collective-permute-done.22.pair_ref = f32[136,256]{1,0:T(8,128)S(1)} collective-permute-done((f32[136,256]{1,0:T(8,128)S(1)}, f32[136,256]{1,0:T(8,128)S(1)}, u32[]{:S(2)}, u32[]{:S(2)}) %collective-permute-start.22) | collective-permute-done | bytes 139296 | tf_op jit(solution)/shard_map/ppermute | solution.py:503
  102.6 1.8 %collective-permute-done.27.c_ref = f32[136,256]{1,0:T(8,128)S(1)} collective-permute-done((f32[136,256]{1,0:T(8,128)S(1)}, f32[136,256]{1,0:T(8,128)S(1)}, u32[]{:S(2)}, u32[]{:S(2)}) %collective-permute-start.27) | collective-permute-done | bytes 139296 | tf_op jit(solution)/shard_map/ppermute | solution.py:503
  105.1 3.7 %collective-permute-start.29 = (f32[392,256]{1,0:T(8,128)S(1)}, f32[392,256]{1,0:T(8,128)S(1)}, u32[]{:S(2)}, u32[]{:S(2)}) collective-permute-start(f32[392,256]{1,0:T(8,128)S(1)} %get-tuple-element.82), channel_id=1, source_target_pairs={{0,1},{1,0},{2,3},{3,2},{4,5},{5,4},{6,7},{7,6},{8,9},{9,8},{10,11... | collective-permute-start | bytes 1204232 | tf_op jit(solution)/shard_map/ppermute | solution.py:503
  110.1 2.6 %collective-permute-start.30 = (f32[136,256]{1,0:T(8,128)S(1)}, f32[136,256]{1,0:T(8,128)S(1)}, u32[]{:S(2)}, u32[]{:S(2)}) collective-permute-start(f32[136,256]{1,0:T(8,128)S(1)} %slice_add_fusion.here_ref), channel_id=1, source_target_pairs={{0,8},{1,9},{2,10},{3,11},{4,12},{5,13},{6,14},{7,15},{8,16},{9,17... | collective-permute-start | bytes 417800 | tf_op jit(solution)/shard_map/ppermute | solution.py:503
  112.8 2.0 %plane_rows.5 = (f32[128,512]{1,0:T(8,128)S(1)}, f32[256,256]{1,0:T(8,128)}, f32[256,512]{1,0:T(8,128)S(1)}) custom-call(s32[6]{0:T(128)S(1)} %broadcast_multiply_fusion.first_ref, f32[8,512]{1,0:T(8,128)S(1)} %slice.23.class_ref.meta_ref, f32[8,512]{1,0:T(8,128)S(1)} %slice.26.meta_other_ref, f32[136,256]{1,0:T(8,128)S(1)} %get-tuple-element.78.a_ref.pulled_ref, ...), custom_call_target="tpu_custom_call" | custom-call | flops 1000000000 | bytes 2000000 | tf_op jit(solution)/shard_map/plane_rows/pallas_call | solution.py:868
  116.8 5.8 %all-to-all-start = ((f32[32,8,128]{2,1,0:T(8,128)}), f32[32,8,128]{2,1,0:T(8,128)S(1)}, u32[]{:S(2)}, u32[]{:S(2)}) async-start(f32[32,8,128]{2,1,0:T(8,128)} %plane_close.1), calls=%async_computation | async-start | bytes 262144 | tf_op jit(solution)/shard_map/all_to_all | solution.py:1163
  122.7 8.2 %all-to-all-done.close_ref = f32[32,8,128]{2,1,0:T(8,128)S(1)} async-done(((f32[32,8,128]{2,1,0:T(8,128)}), f32[32,8,128]{2,1,0:T(8,128)S(1)}, u32[]{:S(2)}, u32[]{:S(2)}) %all-to-all-start) | async-done | bytes 131104 | tf_op jit(solution)/shard_map/all_to_all | solution.py:1163
  132.1 2.6 %collective-permute-start.32 = (f32[512,128]{1,0:T(8,128)S(1)}, f32[512,128]{1,0:T(8,128)S(1)}, u32[]{:S(2)}, u32[]{:S(2)}) collective-permute-start(f32[512,128]{1,0:T(8,128)S(1)} %plane_combine.1), channel_id=1, source_target_pairs={{0,0},{1,16},{2,8},{3,24},{4,4},{5,20},{6,12},{7,28},{8,1},{9,17},... | collective-permute-start | bytes 786440 | tf_op jit(solution)/shard_map/ppermute | solution.py:503
  134.7 10.7 %collective-permute-done.32.rows_ref = f32[512,128]{1,0:T(8,128)S(1)} collective-permute-done((f32[512,128]{1,0:T(8,128)S(1)}, f32[512,128]{1,0:T(8,128)S(1)}, u32[]{:S(2)}, u32[]{:S(2)}) %collective-permute-start.32) | collective-permute-done | bytes 262176 | tf_op jit(solution)/shard_map/ppermute | solution.py:503
  145.4 2.4 %plane_finish.1 = f32[4096,128]{1,0:T(8,128)} custom-call(f32[512,128]{1,0:T(8,128)S(1)} %collective-permute-done.32.rows_ref, s32[32,16,128]{2,1,0:T(8,128)S(1)} %copy-done.2, f32[4096,128]{1,0:T(8,128)S(1)} %copy-done), custom_call_target="tpu_custom_call" | custom-call | tf_op jit(solution)/shard_map/plane_finish/pallas_call | solution.py:1063
  (99 shorter events, 32.9 us)
Async XLA Ops:
  4.6 12.4 %collective-permute-start.1 = (f32[256,128]{0,1:T(8,128)S(1)}, f32[256,128]{0,1:T(8,128)S(1)}, u32[]{:S(2)}, u32[]{:S(2)}) collective-permute-start(f32[256,128]{0,1:T(8,128)S(1)} %copy.14), channel_id=1, source_target_pairs={{0,0},{1,8},{2,16},{3,24},{4,4},{5,12},{6,20},{7,28},{8,2},{9,10},... | collective-permute-start | bytes 393224 | tf_op jit(solution)/shard_map/ppermute | solution.py:503
  9.2 19.1 %collective-permute-start = (f32[136,512]{1,0:T(8,128)}, f32[136,512]{1,0:T(8,128)S(1)}, u32[]{:S(2)}, u32[]{:S(2)}) collective-permute-start(f32[136,512]{1,0:T(8,128)} %send.1), channel_id=1, source_target_pairs={{0,0},{1,8},{2,16},{3,24},{4,4},{5,12},{6,20},{7,28},{8,2},{9,10},... | collective-permute-start | bytes 835592 | tf_op jit(solution)/shard_map/ppermute | solution.py:503
  17.3 3.0 %collective-permute-start.3 = (f32[24,512]{1,0:T(8,128)S(1)}, f32[24,512]{1,0:T(8,128)S(1)}, u32[]{:S(2)}, u32[]{:S(2)}) collective-permute-start(f32[24,512]{1,0:T(8,128)S(1)} %describe.1), channel_id=1, source_target_pairs={{0,4},{1,5},{2,6},{3,7},{4,0},{5,1},{6,2},{7,3},{8,12},{9,13},{10,... | collective-permute-start | bytes 147464 | tf_op jit(solution)/shard_map/ppermute | solution.py:503
  20.3 8.8 %collective-permute-start.4 = (f32[24,1024]{1,0:T(8,128)S(1)}, f32[24,1024]{1,0:T(8,128)S(1)}, u32[]{:S(2)}, u32[]{:S(2)}) collective-permute-start(f32[24,1024]{1,0:T(8,128)S(1)} %pad_maximum_fusion.3), channel_id=1, source_target_pairs={{0,8},{1,9},{2,10},{3,11},{4,12},{5,13},{6,14},{7,15},{8,0},{9,1},... | collective-permute-start | bytes 294920 | tf_op jit(solution)/shard_map/ppermute | solution.py:503
  31.4 5.7 %collective-permute-start.5 = (f32[128,256]{1,0:T(8,128)S(1)}, f32[128,256]{1,0:T(8,128)S(1)}, u32[]{:S(2)}, u32[]{:S(2)}) collective-permute-start(f32[128,256]{1,0:T(8,128)S(1)} %get-tuple-element.56), channel_id=1, source_target_pairs={{0,4},{1,5},{2,6},{3,7},{4,0},{5,1},{6,2},{7,3},{8,12},{9,13},{10,... | collective-permute-start | bytes 393224 | tf_op jit(solution)/shard_map/ppermute | solution.py:503
  32.7 4.4 %collective-permute-start.6 = (f32[128,256]{1,0:T(8,128)S(1)}, f32[128,256]{1,0:T(8,128)S(1)}, u32[]{:S(2)}, u32[]{:S(2)}) collective-permute-start(f32[128,256]{1,0:T(8,128)S(1)} %get-tuple-element.57), channel_id=1, source_target_pairs={{0,2},{1,3},{2,0},{3,1},{4,6},{5,7},{6,4},{7,5},{8,10},{9,11},{10,... | collective-permute-start | bytes 393224 | tf_op jit(solution)/shard_map/ppermute | solution.py:503
  34.3 5.3 %collective-permute-start.7 = (f32[128,256]{1,0:T(8,128)S(1)}, f32[128,256]{1,0:T(8,128)S(1)}, u32[]{:S(2)}, u32[]{:S(2)}) collective-permute-start(f32[128,256]{1,0:T(8,128)S(1)} %get-tuple-element.58), channel_id=1, source_target_pairs={{0,6},{1,7},{2,4},{3,5},{4,2},{5,3},{6,0},{7,1},{8,14},{9,15},{10,... | collective-permute-start | bytes 393224 | tf_op jit(solution)/shard_map/ppermute | solution.py:503
  34.3 6.2 %collective-permute-start.8 = (f32[24,1024]{1,0:T(8,128)S(1)}, f32[24,1024]{1,0:T(8,128)S(1)}, u32[]{:S(2)}, u32[]{:S(2)}) collective-permute-start(f32[24,1024]{1,0:T(8,128)S(1)} %slice_select_fusion), channel_id=1, source_target_pairs={{0,16},{1,17},{2,18},{3,19},{4,20},{5,21},{6,22},{7,23},{8,24},{9,... | collective-permute-start | bytes 294920 | tf_op jit(solution)/shard_map/ppermute | solution.py:503
  40.5 12.1 %collective-permute-start.11 = (f32[256,256]{1,0:T(8,128)S(1)}, f32[256,256]{1,0:T(8,128)S(1)}, u32[]{:S(2)}, u32[]{:S(2)}) collective-permute-start(f32[256,256]{1,0:T(8,128)S(1)} %pad_maximum_fusion.here_ref), channel_id=1, source_target_pairs={{8,16},{9,17},{10,18},{11,19},{12,20},{13,21},{14,22},{15,23},{16,... | collective-permute-start | bytes 786440 | tf_op jit(solution)/shard_map/ppermute | solution.py:503
  41.3 11.3 %collective-permute-start.10 = (f32[256,256]{1,0:T(8,128)S(1)}, f32[256,256]{1,0:T(8,128)S(1)}, u32[]{:S(2)}, u32[]{:S(2)}) collective-permute-start(f32[256,256]{1,0:T(8,128)S(1)} %pad_maximum_fusion.here_ref), channel_id=1, source_target_pairs={{0,8},{1,9},{2,10},{3,11},{4,12},{5,13},{6,14},{7,15},{8,0},{9,1},... | collective-permute-start | bytes 786440 | tf_op jit(solution)/shard_map/ppermute | solution.py:503
  45.2 7.4 %collective-permute-start.9 = (f32[24,1024]{1,0:T(8,128)S(1)}, f32[24,1024]{1,0:T(8,128)S(1)}, u32[]{:S(2)}, u32[]{:S(2)}) collective-permute-start(f32[24,1024]{1,0:T(8,128)S(1)} %collective-permute-done.8), channel_id=1, source_target_pairs={{0,1},{1,0},{2,3},{3,2},{4,5},{5,4},{6,7},{7,6},{8,9},{9,8},{10,11... | collective-permute-start | bytes 294920 | tf_op jit(solution)/shard_map/ppermute | solution.py:503
  55.3 7.8 %collective-permute-start.14 = (f32[128,256]{1,0:T(8,128)S(1)}, f32[128,256]{1,0:T(8,128)S(1)}, u32[]{:S(2)}, u32[]{:S(2)}) collective-permute-start(f32[128,256]{1,0:T(8,128)S(1)} %plane_first.1.a_ref.pulled_ref.old_z_ref), channel_id=1, source_target_pairs={{0,6},{1,7},{2,4},{3,5},{4,2},{5,3},{6,0},{7,1},{8,14},{9,15},{10,... | collective-permute-start | bytes 393224 | tf_op jit(solution)/shard_map/ppermute | solution.py:503
  57.7 6.8 %collective-permute-start.13 = (f32[128,256]{1,0:T(8,128)S(1)}, f32[128,256]{1,0:T(8,128)S(1)}, u32[]{:S(2)}, u32[]{:S(2)}) collective-permute-start(f32[128,256]{1,0:T(8,128)S(1)} %plane_first.1.a_ref.pulled_ref.old_z_ref), channel_id=1, source_target_pairs={{0,2},{1,3},{2,0},{3,1},{4,6},{5,7},{6,4},{7,5},{8,10},{9,11},{10,... | collective-permute-start | bytes 393224 | tf_op jit(solution)/shard_map/ppermute | solution.py:503
  57.7 6.8 %collective-permute-start.12 = (f32[128,256]{1,0:T(8,128)S(1)}, f32[128,256]{1,0:T(8,128)S(1)}, u32[]{:S(2)}, u32[]{:S(2)}) collective-permute-start(f32[128,256]{1,0:T(8,128)S(1)} %plane_first.1.a_ref.pulled_ref.old_z_ref), channel_id=1, source_target_pairs={{0,4},{1,5},{2,6},{3,7},{4,0},{5,1},{6,2},{7,3},{8,12},{9,13},{10,... | collective-permute-start | bytes 393224 | tf_op jit(solution)/shard_map/ppermute | solution.py:503
  66.9 2.6 %collective-permute-start.17 = (f32[128,256]{1,0:T(8,128)S(1)}, f32[128,256]{1,0:T(8,128)S(1)}, u32[]{:S(2)}, u32[]{:S(2)}) collective-permute-start(f32[128,256]{1,0:T(8,128)S(1)} %add.61.here_ref.old_s_ref), channel_id=1, source_target_pairs={{8,16},{9,17},{10,18},{11,19},{12,20},{13,21},{14,22},{15,23},{16,... | collective-permute-start | bytes 393224 | tf_op jit(solution)/shard_map/ppermute | solution.py:503
  67.6 5.2 %collective-permute-start.16 = (f32[128,256]{1,0:T(8,128)S(1)}, f32[128,256]{1,0:T(8,128)S(1)}, u32[]{:S(2)}, u32[]{:S(2)}) collective-permute-start(f32[128,256]{1,0:T(8,128)S(1)} %add.61.here_ref.old_s_ref), channel_id=1, source_target_pairs={{0,8},{1,9},{2,10},{3,11},{4,12},{5,13},{6,14},{7,15},{8,0},{9,1},... | collective-permute-start | bytes 393224 | tf_op jit(solution)/shard_map/ppermute | solution.py:503
  74.6 4.9 %collective-permute-start.20 = (f32[136,256]{1,0:T(8,128)S(1)}, f32[136,256]{1,0:T(8,128)S(1)}, u32[]{:S(2)}, u32[]{:S(2)}) collective-permute-start(f32[136,256]{1,0:T(8,128)S(1)} %get-tuple-element.72.a_ref.pulled_ref), channel_id=1, source_target_pairs={{0,6},{1,7},{2,4},{3,5},{4,2},{5,3},{6,0},{7,1},{8,14},{9,15},{10,... | collective-permute-start | bytes 417800 | tf_op jit(solution)/shard_map/ppermute | solution.py:503
  76.6 7.0 %collective-permute-start.19 = (f32[136,256]{1,0:T(8,128)S(1)}, f32[136,256]{1,0:T(8,128)S(1)}, u32[]{:S(2)}, u32[]{:S(2)}) collective-permute-start(f32[136,256]{1,0:T(8,128)S(1)} %get-tuple-element.72.a_ref.pulled_ref), channel_id=1, source_target_pairs={{0,2},{1,3},{2,0},{3,1},{4,6},{5,7},{6,4},{7,5},{8,10},{9,11},{10,... | collective-permute-start | bytes 417800 | tf_op jit(solution)/shard_map/ppermute | solution.py:503
  77.1 6.5 %collective-permute-start.18 = (f32[136,256]{1,0:T(8,128)S(1)}, f32[136,256]{1,0:T(8,128)S(1)}, u32[]{:S(2)}, u32[]{:S(2)}) collective-permute-start(f32[136,256]{1,0:T(8,128)S(1)} %get-tuple-element.72.a_ref.pulled_ref), channel_id=1, source_target_pairs={{0,4},{1,5},{2,6},{3,7},{4,0},{5,1},{6,2},{7,3},{8,12},{9,13},{10,... | collective-permute-start | bytes 417800 | tf_op jit(solution)/shard_map/ppermute | solution.py:503
  84.2 2.5 %collective-permute-start.21 = (f32[392,256]{1,0:T(8,128)S(1)}, f32[392,256]{1,0:T(8,128)S(1)}, u32[]{:S(2)}, u32[]{:S(2)}) collective-permute-start(f32[392,256]{1,0:T(8,128)S(1)} %get-tuple-element.75), channel_id=1, source_target_pairs={{0,1},{1,0},{2,3},{3,2},{4,5},{5,4},{6,7},{7,6},{8,9},{9,8},{10,11... | collective-permute-start | bytes 1204232 | tf_op jit(solution)/shard_map/ppermute | solution.py:503
  86.7 5.7 %collective-permute-start.25 = (f32[136,256]{1,0:T(8,128)S(1)}, f32[136,256]{1,0:T(8,128)S(1)}, u32[]{:S(2)}, u32[]{:S(2)}) collective-permute-start(f32[136,256]{1,0:T(8,128)S(1)} %slice_add_fusion.1.here_ref), channel_id=1, source_target_pairs={{8,16},{9,17},{10,18},{11,19},{12,20},{13,21},{14,22},{15,23},{16,... | collective-permute-start | bytes 417800 | tf_op jit(solution)/shard_map/ppermute | solution.py:503
  87.6 6.9 %collective-permute-start.22 = (f32[136,256]{1,0:T(8,128)S(1)}, f32[136,256]{1,0:T(8,128)S(1)}, u32[]{:S(2)}, u32[]{:S(2)}) collective-permute-start(f32[136,256]{1,0:T(8,128)S(1)} %slice_add_fusion.1.here_ref), channel_id=1, source_target_pairs={{0,8},{1,9},{2,10},{3,11},{4,12},{5,13},{6,14},{7,15},{8,0},{9,1},... | collective-permute-start | bytes 417800 | tf_op jit(solution)/shard_map/ppermute | solution.py:503
  91.0 4.7 %collective-permute-start.24 = (f32[8,256]{1,0:T(8,128)S(1)}, f32[8,256]{1,0:T(8,128)S(1)}, u32[]{:S(2)}, u32[]{:S(2)}) collective-permute-start(f32[8,256]{1,0:T(8,128)S(1)} %slice.31), channel_id=1, source_target_pairs={{0,24},{1,25},{2,26},{3,27},{4,28},{5,29},{6,30},{7,31},{8,16},{9,... | collective-permute-start | bytes 24584 | tf_op jit(solution)/shard_map/ppermute | solution.py:503
  92.4 3.4 %collective-permute-start.23 = (f32[8,256]{1,0:T(8,128)S(1)}, f32[8,256]{1,0:T(8,128)S(1)}, u32[]{:S(2)}, u32[]{:S(2)}) collective-permute-start(f32[8,256]{1,0:T(8,128)S(1)} %slice.31), channel_id=1, source_target_pairs={{0,16},{1,17},{2,18},{3,19},{4,20},{5,21},{6,22},{7,23},{8,24},{9,... | collective-permute-start | bytes 24584 | tf_op jit(solution)/shard_map/ppermute | solution.py:503
  97.7 4.9 %collective-permute-start.28 = (f32[136,256]{1,0:T(8,128)S(1)}, f32[136,256]{1,0:T(8,128)S(1)}, u32[]{:S(2)}, u32[]{:S(2)}) collective-permute-start(f32[136,256]{1,0:T(8,128)S(1)} %get-tuple-element.78.a_ref.pulled_ref), channel_id=1, source_target_pairs={{0,6},{1,7},{2,4},{3,5},{4,2},{5,3},{6,0},{7,1},{8,14},{9,15},{10,... | collective-permute-start | bytes 417800 | tf_op jit(solution)/shard_map/ppermute | solution.py:503
  99.2 5.3 %collective-permute-start.27 = (f32[136,256]{1,0:T(8,128)S(1)}, f32[136,256]{1,0:T(8,128)S(1)}, u32[]{:S(2)}, u32[]{:S(2)}) collective-permute-start(f32[136,256]{1,0:T(8,128)S(1)} %get-tuple-element.78.a_ref.pulled_ref), channel_id=1, source_target_pairs={{0,2},{1,3},{2,0},{3,1},{4,6},{5,7},{6,4},{7,5},{8,10},{9,11},{10,... | collective-permute-start | bytes 417800 | tf_op jit(solution)/shard_map/ppermute | solution.py:503
  100.1 4.4 %collective-permute-start.26 = (f32[136,256]{1,0:T(8,128)S(1)}, f32[136,256]{1,0:T(8,128)S(1)}, u32[]{:S(2)}, u32[]{:S(2)}) collective-permute-start(f32[136,256]{1,0:T(8,128)S(1)} %get-tuple-element.78.a_ref.pulled_ref), channel_id=1, source_target_pairs={{0,4},{1,5},{2,6},{3,7},{4,0},{5,1},{6,2},{7,3},{8,12},{9,13},{10,... | collective-permute-start | bytes 417800 | tf_op jit(solution)/shard_map/ppermute | solution.py:503
  105.1 5.1 %collective-permute-start.29 = (f32[392,256]{1,0:T(8,128)S(1)}, f32[392,256]{1,0:T(8,128)S(1)}, u32[]{:S(2)}, u32[]{:S(2)}) collective-permute-start(f32[392,256]{1,0:T(8,128)S(1)} %get-tuple-element.82), channel_id=1, source_target_pairs={{0,1},{1,0},{2,3},{3,2},{4,5},{5,4},{6,7},{7,6},{8,9},{9,8},{10,11... | collective-permute-start | bytes 1204232 | tf_op jit(solution)/shard_map/ppermute | solution.py:503
  110.1 5.3 %collective-permute-start.30 = (f32[136,256]{1,0:T(8,128)S(1)}, f32[136,256]{1,0:T(8,128)S(1)}, u32[]{:S(2)}, u32[]{:S(2)}) collective-permute-start(f32[136,256]{1,0:T(8,128)S(1)} %slice_add_fusion.here_ref), channel_id=1, source_target_pairs={{0,8},{1,9},{2,10},{3,11},{4,12},{5,13},{6,14},{7,15},{8,16},{9,17... | collective-permute-start | bytes 417800 | tf_op jit(solution)/shard_map/ppermute | solution.py:503
  114.7 7.9 %collective-permute-start.31 = (f32[256,256]{1,0:T(8,128)}, f32[256,256]{1,0:T(8,128)S(1)}, u32[]{:S(2)}, u32[]{:S(2)}) collective-permute-start(f32[256,256]{1,0:T(8,128)} %get-tuple-element.88), channel_id=1, source_target_pairs={{0,1},{1,0},{2,3},{3,2},{4,5},{5,4},{6,7},{7,6},{8,9},{9,8},{10,11... | collective-permute-start | bytes 786440 | tf_op jit(solution)/shard_map/ppermute | solution.py:503
  116.8 14.0 %all-to-all-start = ((f32[32,8,128]{2,1,0:T(8,128)}), f32[32,8,128]{2,1,0:T(8,128)S(1)}, u32[]{:S(2)}, u32[]{:S(2)}) async-start(f32[32,8,128]{2,1,0:T(8,128)} %plane_close.1), calls=%async_computation | async-start | bytes 262144 | tf_op jit(solution)/shard_map/all_to_all | solution.py:1163
  132.1 13.3 %collective-permute-start.32 = (f32[512,128]{1,0:T(8,128)S(1)}, f32[512,128]{1,0:T(8,128)S(1)}, u32[]{:S(2)}, u32[]{:S(2)}) collective-permute-start(f32[512,128]{1,0:T(8,128)S(1)} %plane_combine.1), channel_id=1, source_target_pairs={{0,0},{1,16},{2,8},{3,24},{4,4},{5,20},{6,12},{7,28},{8,1},{9,17},... | collective-permute-start | bytes 786440 | tf_op jit(solution)/shard_map/ppermute | solution.py:503
  (16 other events, 196.6 us)

commit v21 on v19

--- a/solution.py
+++ b/solution.py
@@ -507,11 +507,6 @@
     return 2 * y + c, x, z & 1, z >> 1
 
 
-def hour_before(z, x, y, c):
-    t = 2 * y + c - 1
-    return (z, x, t >> 1, t & 1) if t >= 0 else None
-
-
 def from_plane(z, x, y, c):
     return 2 * c + y, x, z >> 1, z & 1
 
@@ -921,16 +916,16 @@
 
 
 def plane_first_kernel(
-    flag_ref, here_ref, pair_ref, middle_ref, spec_ref, kernels_ref, forward, first, last, out_ref
+    flag_ref, here_ref, pair_ref, middle_ref, spec_ref, kernels_ref, forward3, last3, forward, first, out_ref
 ):
     spec = spec_ref[...]
     before, after = sides(flag_ref[0] > 0.5, pair_ref[...], middle_ref[...])
     here = here_ref[...]
-    both = plane_delayed(before[:HOURS], here[:HOURS], after[:HOURS], spec, forward[...], last[...], 3)
+    both = plane_delayed(before[:HOURS], here[:HOURS], after[:HOURS], spec, forward3[...], last3[...], 3)
     scale = gain(kernels_ref[...])
     now = here[HOURS:] - both[0] * scale
     later = (after[HOURS:] - both[1] * scale) * flag_ref[1]
-    out_ref[...] = plane_advanced(now, later, spec, forward[...], first[...], 3)
+    out_ref[...] = plane_advanced(now, later, spec, forward[...], first[...], 2)
 
 
 def plane_delay_kernel(flag_ref, here_ref, pair_ref, middle_ref, spec_ref, forward, last, out_ref):
@@ -992,7 +987,19 @@
 
 
 def plane_close_kernel(
-    here_ref, before_ref, pulled_ref, kept_ref, old_z_ref, old_s_ref, old_delayed_ref, spec_ref, forward, last, out_ref
+    here_ref,
+    before_ref,
+    pulled_ref,
+    kept_ref,
+    old_z_ref,
+    old_s_ref,
+    old_delayed_ref,
+    open_ref,
+    spec_ref,
+    kernels_ref,
+    forward,
+    last,
+    out_ref,
 ):
     body = pl.ds(0, HOURS)
     here, raw = here_ref[body, :], pulled_ref[body, :]
@@ -1005,17 +1012,20 @@
     parts = (now, delayed, old_delayed_ref[body, :])
     for i in range(3):
         note += [lanes(parts[i], parts[j]) for j in range(i, 3)]
-    note.append(jnp.zeros((24 - len(note), here.shape[1]), F32))
-    note = jnp.sum(jnp.concatenate(note, axis=0), axis=1, keepdims=True)
+    known = [total(open_ref, 0), total(open_ref, 1), gain(kernels_ref[...])]
+    note = [jnp.sum(jnp.concatenate(note, axis=0), axis=1, keepdims=True)]
+    note += [value / out_ref.shape[0] for value in known]
+    count = sum(value.shape[0] for value in note)
+    note = jnp.concatenate(note + [jnp.zeros((24 - count, 1), F32)], axis=0)
     shape = (24, out_ref.shape[2])
     row, col = (lax.broadcasted_iota(jnp.int32, shape, i) for i in range(2))
     note = jnp.sum(jnp.where(row == col, jnp.broadcast_to(note, shape), 0.0), axis=0, keepdims=True)
     out_ref[...] = jnp.broadcast_to(note[None], out_ref.shape)
 
 
-def plane_weights(open_ref, close, scale):
+def plane_weights(close):
     entry = lambda i: close[:, i : i + 1]
-    n1, t1 = total(open_ref, 0), total(open_ref, 1)
+    n1, t1, scale = (entry(17 + i) for i in range(3))
     n2, t2 = entry(0), entry(1)
     a1 = t1 / n1
     a2, r2 = (t2 / n2) / a1, n2 / n1
@@ -1034,10 +1044,10 @@
     return c1 - step - c3 * r2, step / a1, c3
 
 
-def plane_combine_kernel(open_ref, close_ref, kernels_ref, stack_ref, mine_ref, beside_ref, out_ref):
-    rows = open_ref.shape[1]
+def plane_combine_kernel(close_ref, stack_ref, mine_ref, beside_ref, out_ref):
+    rows = beside_ref.shape[1]
     close = jnp.sum(close_ref[...], axis=0)[0:1, :]
-    e0, e1, e2 = plane_weights(open_ref, close, gain(kernels_ref[...]))
+    e0, e1, e2 = plane_weights(close)
     for i in range(out_ref.shape[0] // rows):
         here = pl.ds(i * rows, rows)
         last = mine_ref[:, here] + beside_ref[pl.ds(i * HOURS, HOURS), :]
@@ -1059,7 +1069,7 @@
 def plane_finish(rows, incidence, field):
     blocks, slots, width = incidence.shape
     hours = field.shape[1]
-    step = 8
+    step = 16
     return pl.pallas_call(
         plane_finish_kernel,
         grid=(blocks // step,),
@@ -1084,7 +1094,7 @@
     first = (first * rows).astype(jnp.int32)
     flags = jnp.stack([1 - z % 2, (z < Z_ - 1).astype(z.dtype), (z > 0).astype(z.dtype)]).astype(F32)
     forward, inverse_first, inverse_last, _ = turned_transforms(2)
-    forward3, inverse_first3, inverse_last3, short3 = turned_transforms(3)
+    forward3, _, inverse_last3, short3 = turned_transforms(3)
     block, noted = (hours, rows), (hours + NOTE, rows)
 
     seen = moved(observed, to_plane)
@@ -1116,7 +1126,7 @@
         "plane_first",
         [block],
         [flags],
-        [*sums, spec, kernels, forward3, inverse_first3, inverse_last3],
+        [*sums, spec, kernels, forward3, inverse_last3, forward, inverse_first],
     )
 
     def mixing(pulled, extra):
@@ -1158,7 +1168,10 @@
         "plane_close",
         [(Z_ * X_ * Y_ * C_, 8, rows // 2)],
         [],
-        [mixed2, moved(mixed2, z_next), pulled2, kept, pulled0, mixed0, delayed0, spec, forward, inverse_last],
+        [
+            *(mixed2, moved(mixed2, z_next), pulled2, kept, pulled0, mixed0, delayed0),
+            *(open_note, spec, kernels, forward, inverse_last),
+        ],
     )
     close_note = lax.all_to_all(note, ("basin", "tm"), 0, 0, tiled=False)
     (answer,) = plane_call(
@@ -1166,7 +1179,7 @@
         "plane_combine",
         [(parcel.shape[1], hours)],
         [],
-        [open_note, close_note, kernels, stack, picked, moved(theirs, over_core)],
+        [close_note, stack, picked, moved(theirs, over_core)],
     )
     return plane_finish(moved(answer, from_plane), incidence, first_guess)
 

time: 144 us -> 142 us (0.986)
  no operation moved by 1% of the time
where the time goes in v21:
time: 142 us
  waiting for transfers between devices  55.8 us (39%)
  starting transfers between devices  52.3 us (37%)
  Pallas kernels  31.9 us (22%)
    ppermute x33, waiting for transfers between devices, moved(): return lax.ppermute(value, ('basin', 'tm'), pairs)  47.6 us
    ppermute x33, starting transfers between devices, moved(): return lax.ppermute(value, ('basin', 'tm'), pairs)  46.4 us
    pallas_call x2, Pallas kernels, plane_couple(): pl.pallas_call(functools.partial(plane_couple_kernel, last), in_specs=[pl...  9.55 us
    pallas_call x6, Pallas kernels, plane_call(): pl.pallas_call(kernel, in_specs=[pl.BlockSpec(memory_space=pltpu.SMEM)] *...  8.89 us
    all_to_all x1, waiting for transfers between devices, plane_shards(): close_note = lax.all_to_all(note, ('basin', 'tm'), 0, 0, tiled=False)  8.18 us
    all_to_all x1, starting transfers between devices, plane_shards(): close_note = lax.all_to_all(note, ('basin', 'tm'), 0, 0, tiled=False)  5.88 us
    pallas_call x3, Pallas kernels, plane_rows(): pl.pallas_call(plane_rows_kernel, in_specs=[pl.BlockSpec(memory_space=plt...  4.49 us
    pallas_call x1, Pallas kernels, send(): pl.pallas_call(send_kernel, in_specs=[pl.BlockSpec(memory_space=pltpu.HBM...  3.21 us
  transfers between devices with their start and end apart: 34, of which 21 were waited for; matrix products, arithmetic and copies ran while one was open for 0% of the time, Pallas kernels for 12%

profile of v21, /device:TPU:1, one launch (start us, length us, event | category | flops | bytes accessed | tf_op | source)
XLA Modules:
  0.0 141.9 jit_solution(17172387962946019638)
XLA Ops:
  1.1 4.6 %collective-permute-start.1 = (f32[256,128]{0,1:T(8,128)S(1)}, f32[256,128]{0,1:T(8,128)S(1)}, u32[]{:S(2)}, u32[]{:S(2)}) collective-permute-start(f32[256,128]{0,1:T(8,128)S(1)} %copy.13), channel_id=1, source_target_pairs={{0,0},{1,8},{2,16},{3,24},{4,4},{5,12},{6,20},{7,28},{8,2},{9,10},... | collective-permute-start | bytes 393224 | tf_op jit(solution)/shard_map/ppermute | solution.py:503
  5.7 3.2 %send.1 = f32[136,512]{1,0:T(8,128)} custom-call(s32[32,16,128]{2,1,0:T(8,128)} %inc_ref.2, f32[4096,128]{1,0:T(8,128)} %field_ref.1, s32[1,512]{1,0:T(1,128)} %bitcast.11, s32[1,256]{1,0:T(1,128)} %bitcast.14), custom_call_target="tpu_custom_call" | custom-call | flops 1 | bytes 1 | tf_op jit(solution)/shard_map/send/pallas_call | solution.py:680
  8.9 3.3 %collective-permute-start = (f32[136,512]{1,0:T(8,128)}, f32[136,512]{1,0:T(8,128)S(1)}, u32[]{:S(2)}, u32[]{:S(2)}) collective-permute-start(f32[136,512]{1,0:T(8,128)} %send.1), channel_id=1, source_target_pairs={{0,0},{1,8},{2,16},{3,24},{4,4},{5,12},{6,20},{7,28},{8,2},{9,10},... | collective-permute-start | bytes 835592 | tf_op jit(solution)/shard_map/ppermute | solution.py:503
  14.4 1.7 %collective-permute-done.3 = f32[24,512]{1,0:T(8,128)S(1)} collective-permute-done((f32[24,512]{1,0:T(8,128)S(1)}, f32[24,512]{1,0:T(8,128)S(1)}, u32[]{:S(2)}, u32[]{:S(2)}) %collective-permute-start.3) | collective-permute-done | bytes 49184 | tf_op jit(solution)/shard_map/ppermute | solution.py:503
  17.4 9.0 %collective-permute-done.mine_ref = f32[136,512]{1,0:T(8,128)S(1)} collective-permute-done((f32[136,512]{1,0:T(8,128)}, f32[136,512]{1,0:T(8,128)S(1)}, u32[]{:S(2)}, u32[]{:S(2)}) %collective-permute-start) | collective-permute-done | bytes 278560 | tf_op jit(solution)/shard_map/ppermute | solution.py:503
  27.9 1.6 %spread.1 = (f32[128,256]{1,0:T(8,128)S(1)}, f32[128,256]{1,0:T(8,128)S(1)}, f32[128,256]{1,0:T(8,128)S(1)}, f32[128,256]{1,0:T(8,128)S(1)}) custom-call(s32[6]{0:T(128)S(1)} %broadcast_multiply_fusion.first_ref, f32[136,512]{1,0:T(8,128)S(1)} %collective-permute-done.mine_ref, f32[136,512]{1,0:T(8,128)S(1)} %collective-permute-done.2.other_ref), custom_call_target="tpu_custom_call" | custom-call | flops 1 | bytes 1 | tf_op jit(solution)/shard_map/spread/pallas_call | solution.py:714
  34.5 3.7 %collective-permute-done.6 = f32[128,256]{1,0:T(8,128)S(1)} collective-permute-done((f32[128,256]{1,0:T(8,128)S(1)}, f32[128,256]{1,0:T(8,128)S(1)}, u32[]{:S(2)}, u32[]{:S(2)}) %collective-permute-start.6) | collective-permute-done | bytes 131104 | tf_op jit(solution)/shard_map/ppermute | solution.py:503
  41.4 2.0 %collective-permute-start.9 = (f32[24,1024]{1,0:T(8,128)S(1)}, f32[24,1024]{1,0:T(8,128)S(1)}, u32[]{:S(2)}, u32[]{:S(2)}) collective-permute-start(f32[24,1024]{1,0:T(8,128)S(1)} %collective-permute-done.8), channel_id=1, source_target_pairs={{0,1},{1,0},{2,3},{3,2},{4,5},{5,4},{6,7},{7,6},{8,9},{9,8},{10,11... | collective-permute-start | bytes 294920 | tf_op jit(solution)/shard_map/ppermute | solution.py:503
  43.4 4.6 %plane_couple.2.refs_1_ = f32[1024,512]{1,0:T(8,128)S(1)} custom-call(s32[6]{0:T(128)S(1)} %broadcast_multiply_fusion.first_ref, f32[24,2048]{1,0:T(8,128)S(1)} %pad_maximum_fusion.1.refs_0_), custom_call_target="tpu_custom_call" | custom-call | flops 2147483648 | bytes 2000000 | tf_op jit(solution)/shard_map/plane_couple/pallas_call | solution.py:780
  48.1 2.2 %plane_first.1.a_ref.pulled_ref.old_z_ref = f32[128,256]{1,0:T(8,128)S(1)} custom-call(f32[3]{0:T(128)S(1)} %add_convert_fusion.flag_ref, f32[256,256]{1,0:T(8,128)S(1)} %pad_maximum_fusion.here_ref, f32[256,256]{1,0:T(8,128)S(1)} %collective-permute-done.10.pair_ref, f32[256,256]{1,0:T(8,128)S(1)} %collective-permute-done.11.middle_ref, ...), custom_call_target="tpu_custom_call" | custom-call | flops 1 | bytes 1 | tf_op jit(solution)/shard_map/plane_first/pallas_call | solution.py:907
  50.3 2.0 %collective-permute-start.14 = (f32[128,256]{1,0:T(8,128)S(1)}, f32[128,256]{1,0:T(8,128)S(1)}, u32[]{:S(2)}, u32[]{:S(2)}) collective-permute-start(f32[128,256]{1,0:T(8,128)S(1)} %plane_first.1.a_ref.pulled_ref.old_z_ref), channel_id=1, source_target_pairs={{0,6},{1,7},{2,4},{3,5},{4,2},{5,3},{6,0},{7,1},{8,14},{9,15},{10,... | collective-permute-start | bytes 393224 | tf_op jit(solution)/shard_map/ppermute | solution.py:503
  53.0 4.9 %plane_couple.3 = (bf16[1024,512]{1,0:T(8,128)(2,1)S(1)}, bf16[1024,512]{1,0:T(8,128)(2,1)S(1)}) custom-call(s32[6]{0:T(128)S(1)} %broadcast_multiply_fusion.first_ref, f32[24,2048]{1,0:T(8,128)S(1)} %pad_maximum_fusion.2.refs_0_, f32[1024,512]{1,0:T(8,128)S(1)} %plane_couple.2.refs_1_), custom_call_target="tpu_custom_call" | custom-call | flops 2147483648 | bytes 2000000 | tf_op jit(solution)/shard_map/plane_couple/pallas_call | solution.py:780
  58.0 1.5 %collective-permute-done.13.c_ref = f32[128,256]{1,0:T(8,128)S(1)} collective-permute-done((f32[128,256]{1,0:T(8,128)S(1)}, f32[128,256]{1,0:T(8,128)S(1)}, u32[]{:S(2)}, u32[]{:S(2)}) %collective-permute-start.13) | collective-permute-done | bytes 131104 | tf_op jit(solution)/shard_map/ppermute | solution.py:503
  62.7 2.8 %collective-permute-start.16 = (f32[128,256]{1,0:T(8,128)S(1)}, f32[128,256]{1,0:T(8,128)S(1)}, u32[]{:S(2)}, u32[]{:S(2)}) collective-permute-start(f32[128,256]{1,0:T(8,128)S(1)} %add.61.here_ref.old_s_ref), channel_id=1, source_target_pairs={{0,8},{1,9},{2,10},{3,11},{4,12},{5,13},{6,14},{7,15},{8,0},{9,1},... | collective-permute-start | bytes 393224 | tf_op jit(solution)/shard_map/ppermute | solution.py:503
  65.5 3.3 %collective-permute-done.16.pair_ref = f32[128,256]{1,0:T(8,128)S(1)} collective-permute-done((f32[128,256]{1,0:T(8,128)S(1)}, f32[128,256]{1,0:T(8,128)S(1)}, u32[]{:S(2)}, u32[]{:S(2)}) %collective-permute-start.16) | collective-permute-done | bytes 131104 | tf_op jit(solution)/shard_map/ppermute | solution.py:503
  68.7 1.8 %plane_open.1 = (f32[136,256]{1,0:T(8,128)S(1)}, f32[256,256]{1,0:T(8,128)S(1)}) custom-call(f32[3]{0:T(128)S(1)} %add_convert_fusion.flag_ref, f32[128,256]{1,0:T(8,128)S(1)} %add.61.here_ref.old_s_ref, f32[128,256]{1,0:T(8,128)S(1)} %collective-permute-done.16.pair_ref, f32[128,256]{1,0:T(8,128)S(1)} %collective-permute-done.17.middle_ref, ...), custom_call_target="tpu_custom_call" | custom-call | flops 1 | bytes 1 | tf_op jit(solution)/shard_map/plane_open/pallas_call | solution.py:907
  70.6 1.8 %collective-permute-start.20 = (f32[136,256]{1,0:T(8,128)S(1)}, f32[136,256]{1,0:T(8,128)S(1)}, u32[]{:S(2)}, u32[]{:S(2)}) collective-permute-start(f32[136,256]{1,0:T(8,128)S(1)} %get-tuple-element.70.a_ref.pulled_ref), channel_id=1, source_target_pairs={{0,6},{1,7},{2,4},{3,5},{4,2},{5,3},{6,0},{7,1},{8,14},{9,15},{10,... | collective-permute-start | bytes 417800 | tf_op jit(solution)/shard_map/ppermute | solution.py:503
  75.5 4.1 %collective-permute-done.19.c_ref = f32[136,256]{1,0:T(8,128)S(1)} collective-permute-done((f32[136,256]{1,0:T(8,128)S(1)}, f32[136,256]{1,0:T(8,128)S(1)}, u32[]{:S(2)}, u32[]{:S(2)}) %collective-permute-start.19) | collective-permute-done | bytes 139296 | tf_op jit(solution)/shard_map/ppermute | solution.py:503
  83.5 3.3 %collective-permute-start.22 = (f32[136,256]{1,0:T(8,128)S(1)}, f32[136,256]{1,0:T(8,128)S(1)}, u32[]{:S(2)}, u32[]{:S(2)}) collective-permute-start(f32[136,256]{1,0:T(8,128)S(1)} %slice_add_fusion.1.here_ref), channel_id=1, source_target_pairs={{0,8},{1,9},{2,10},{3,11},{4,12},{5,13},{6,14},{7,15},{8,0},{9,1},... | collective-permute-start | bytes 417800 | tf_op jit(solution)/shard_map/ppermute | solution.py:503
  86.8 1.5 %collective-permute-start.24 = (f32[8,256]{1,0:T(8,128)S(1)}, f32[8,256]{1,0:T(8,128)S(1)}, u32[]{:S(2)}, u32[]{:S(2)}) collective-permute-start(f32[8,256]{1,0:T(8,128)S(1)} %slice.31), channel_id=1, source_target_pairs={{0,24},{1,25},{2,26},{3,27},{4,28},{5,29},{6,30},{7,31},{8,16},{9,... | collective-permute-start | bytes 24584 | tf_op jit(solution)/shard_map/ppermute | solution.py:503
  88.3 1.9 %collective-permute-done.22.pair_ref = f32[136,256]{1,0:T(8,128)S(1)} collective-permute-done((f32[136,256]{1,0:T(8,128)S(1)}, f32[136,256]{1,0:T(8,128)S(1)}, u32[]{:S(2)}, u32[]{:S(2)}) %collective-permute-start.22) | collective-permute-done | bytes 139296 | tf_op jit(solution)/shard_map/ppermute | solution.py:503
  93.0 1.5 %collective-permute-start.28 = (f32[136,256]{1,0:T(8,128)S(1)}, f32[136,256]{1,0:T(8,128)S(1)}, u32[]{:S(2)}, u32[]{:S(2)}) collective-permute-start(f32[136,256]{1,0:T(8,128)S(1)} %get-tuple-element.75.a_ref.pulled_ref), channel_id=1, source_target_pairs={{0,6},{1,7},{2,4},{3,5},{4,2},{5,3},{6,0},{7,1},{8,14},{9,15},{10,... | collective-permute-start | bytes 417800 | tf_op jit(solution)/shard_map/ppermute | solution.py:503
  98.0 1.8 %collective-permute-done.27.c_ref = f32[136,256]{1,0:T(8,128)S(1)} collective-permute-done((f32[136,256]{1,0:T(8,128)S(1)}, f32[136,256]{1,0:T(8,128)S(1)}, u32[]{:S(2)}, u32[]{:S(2)}) %collective-permute-start.27) | collective-permute-done | bytes 139296 | tf_op jit(solution)/shard_map/ppermute | solution.py:503
  100.6 3.4 %collective-permute-start.29 = (f32[392,256]{1,0:T(8,128)S(1)}, f32[392,256]{1,0:T(8,128)S(1)}, u32[]{:S(2)}, u32[]{:S(2)}) collective-permute-start(f32[392,256]{1,0:T(8,128)S(1)} %get-tuple-element.79), channel_id=1, source_target_pairs={{0,1},{1,0},{2,3},{3,2},{4,5},{5,4},{6,7},{7,6},{8,9},{9,8},{10,11... | collective-permute-start | bytes 1204232 | tf_op jit(solution)/shard_map/ppermute | solution.py:503
  105.4 2.5 %collective-permute-start.30 = (f32[136,256]{1,0:T(8,128)S(1)}, f32[136,256]{1,0:T(8,128)S(1)}, u32[]{:S(2)}, u32[]{:S(2)}) collective-permute-start(f32[136,256]{1,0:T(8,128)S(1)} %slice_add_fusion.here_ref), channel_id=1, source_target_pairs={{0,8},{1,9},{2,10},{3,11},{4,12},{5,13},{6,14},{7,15},{8,16},{9,17... | collective-permute-start | bytes 417800 | tf_op jit(solution)/shard_map/ppermute | solution.py:503
  107.9 2.0 %plane_rows.5 = (f32[128,512]{1,0:T(8,128)S(1)}, f32[256,256]{1,0:T(8,128)}, f32[256,512]{1,0:T(8,128)S(1)}) custom-call(s32[6]{0:T(128)S(1)} %broadcast_multiply_fusion.first_ref, f32[8,512]{1,0:T(8,128)S(1)} %slice.23.class_ref.meta_ref, f32[8,512]{1,0:T(8,128)S(1)} %slice.26.meta_other_ref, f32[136,256]{1,0:T(8,128)S(1)} %get-tuple-element.75.a_ref.pulled_ref, ...), custom_call_target="tpu_custom_call" | custom-call | flops 1000000000 | bytes 2000000 | tf_op jit(solution)/shard_map/plane_rows/pallas_call | solution.py:863
  110.6 1.4 %plane_close.1 = f32[32,8,128]{2,1,0:T(8,128)} custom-call(f32[136,256]{1,0:T(8,128)S(1)} %slice_add_fusion.here_ref, f32[136,256]{1,0:T(8,128)S(1)} %collective-permute-done.30.before_ref, f32[136,256]{1,0:T(8,128)S(1)} %get-tuple-element.75.a_ref.pulled_ref, f32[384,256]{1,0:T(8,128)S(1)} %get-tuple-element.80.kept_ref, ...), custom_call_target="tpu_custom_call" | custom-call | flops 1 | bytes 1 | tf_op jit(solution)/shard_map/plane_close/pallas_call | solution.py:907
  112.0 5.9 %all-to-all-start = ((f32[32,8,128]{2,1,0:T(8,128)}), f32[32,8,128]{2,1,0:T(8,128)S(1)}, u32[]{:S(2)}, u32[]{:S(2)}) async-start(f32[32,8,128]{2,1,0:T(8,128)} %plane_close.1), calls=%async_computation | async-start | bytes 262144 | tf_op jit(solution)/shard_map/all_to_all | solution.py:1176
  117.9 8.2 %all-to-all-done.close_ref = f32[32,8,128]{2,1,0:T(8,128)S(1)} async-done(((f32[32,8,128]{2,1,0:T(8,128)}), f32[32,8,128]{2,1,0:T(8,128)S(1)}, u32[]{:S(2)}, u32[]{:S(2)}) %all-to-all-start) | async-done | bytes 131104 | tf_op jit(solution)/shard_map/all_to_all | solution.py:1176
  126.9 2.6 %collective-permute-start.32 = (f32[512,128]{1,0:T(8,128)S(1)}, f32[512,128]{1,0:T(8,128)S(1)}, u32[]{:S(2)}, u32[]{:S(2)}) collective-permute-start(f32[512,128]{1,0:T(8,128)S(1)} %plane_combine.1), channel_id=1, source_target_pairs={{0,0},{1,16},{2,8},{3,24},{4,4},{5,20},{6,12},{7,28},{8,1},{9,17},... | collective-permute-start | bytes 786440 | tf_op jit(solution)/shard_map/ppermute | solution.py:503
  129.5 10.7 %collective-permute-done.32.rows_ref = f32[512,128]{1,0:T(8,128)S(1)} collective-permute-done((f32[512,128]{1,0:T(8,128)S(1)}, f32[512,128]{1,0:T(8,128)S(1)}, u32[]{:S(2)}, u32[]{:S(2)}) %collective-permute-start.32) | collective-permute-done | bytes 262176 | tf_op jit(solution)/shard_map/ppermute | solution.py:503
  140.3 1.6 %plane_finish.1 = f32[4096,128]{1,0:T(8,128)} custom-call(f32[512,128]{1,0:T(8,128)S(1)} %collective-permute-done.32.rows_ref, s32[32,16,128]{2,1,0:T(8,128)S(1)} %copy-done.2, f32[4096,128]{1,0:T(8,128)S(1)} %copy-done.1), custom_call_target="tpu_custom_call" | custom-call | tf_op jit(solution)/shard_map/plane_finish/pallas_call | solution.py:1073
  (91 shorter events, 34.8 us)
Async XLA Ops:
  1.1 11.8 %collective-permute-start.1 = (f32[256,128]{0,1:T(8,128)S(1)}, f32[256,128]{0,1:T(8,128)S(1)}, u32[]{:S(2)}, u32[]{:S(2)}) collective-permute-start(f32[256,128]{0,1:T(8,128)S(1)} %copy.13), channel_id=1, source_target_pairs={{0,0},{1,8},{2,16},{3,24},{4,4},{5,12},{6,20},{7,28},{8,2},{9,10},... | collective-permute-start | bytes 393224 | tf_op jit(solution)/shard_map/ppermute | solution.py:503
  8.9 17.5 %collective-permute-start = (f32[136,512]{1,0:T(8,128)}, f32[136,512]{1,0:T(8,128)S(1)}, u32[]{:S(2)}, u32[]{:S(2)}) collective-permute-start(f32[136,512]{1,0:T(8,128)} %send.1), channel_id=1, source_target_pairs={{0,0},{1,8},{2,16},{3,24},{4,4},{5,12},{6,20},{7,28},{8,2},{9,10},... | collective-permute-start | bytes 835592 | tf_op jit(solution)/shard_map/ppermute | solution.py:503
  13.1 3.0 %collective-permute-start.3 = (f32[24,512]{1,0:T(8,128)S(1)}, f32[24,512]{1,0:T(8,128)S(1)}, u32[]{:S(2)}, u32[]{:S(2)}) collective-permute-start(f32[24,512]{1,0:T(8,128)S(1)} %describe.1), channel_id=1, source_target_pairs={{0,4},{1,5},{2,6},{3,7},{4,0},{5,1},{6,2},{7,3},{8,12},{9,13},{10,... | collective-permute-start | bytes 147464 | tf_op jit(solution)/shard_map/ppermute | solution.py:503
  16.1 11.0 %collective-permute-start.4 = (f32[24,1024]{1,0:T(8,128)S(1)}, f32[24,1024]{1,0:T(8,128)S(1)}, u32[]{:S(2)}, u32[]{:S(2)}) collective-permute-start(f32[24,1024]{1,0:T(8,128)S(1)} %pad_maximum_fusion.3), channel_id=1, source_target_pairs={{0,8},{1,9},{2,10},{3,11},{4,12},{5,13},{6,14},{7,15},{8,0},{9,1},... | collective-permute-start | bytes 294920 | tf_op jit(solution)/shard_map/ppermute | solution.py:503
  29.5 5.0 %collective-permute-start.5 = (f32[128,256]{1,0:T(8,128)S(1)}, f32[128,256]{1,0:T(8,128)S(1)}, u32[]{:S(2)}, u32[]{:S(2)}) collective-permute-start(f32[128,256]{1,0:T(8,128)S(1)} %get-tuple-element.54), channel_id=1, source_target_pairs={{0,4},{1,5},{2,6},{3,7},{4,0},{5,1},{6,2},{7,3},{8,12},{9,13},{10,... | collective-permute-start | bytes 393224 | tf_op jit(solution)/shard_map/ppermute | solution.py:503
  30.8 7.4 %collective-permute-start.6 = (f32[128,256]{1,0:T(8,128)S(1)}, f32[128,256]{1,0:T(8,128)S(1)}, u32[]{:S(2)}, u32[]{:S(2)}) collective-permute-start(f32[128,256]{1,0:T(8,128)S(1)} %get-tuple-element.55), channel_id=1, source_target_pairs={{0,2},{1,3},{2,0},{3,1},{4,6},{5,7},{6,4},{7,5},{8,10},{9,11},{10,... | collective-permute-start | bytes 393224 | tf_op jit(solution)/shard_map/ppermute | solution.py:503
  30.8 7.4 %collective-permute-start.7 = (f32[128,256]{1,0:T(8,128)S(1)}, f32[128,256]{1,0:T(8,128)S(1)}, u32[]{:S(2)}, u32[]{:S(2)}) collective-permute-start(f32[128,256]{1,0:T(8,128)S(1)} %get-tuple-element.56), channel_id=1, source_target_pairs={{0,6},{1,7},{2,4},{3,5},{4,2},{5,3},{6,0},{7,1},{8,14},{9,15},{10,... | collective-permute-start | bytes 393224 | tf_op jit(solution)/shard_map/ppermute | solution.py:503
  32.2 7.1 %collective-permute-start.8 = (f32[24,1024]{1,0:T(8,128)S(1)}, f32[24,1024]{1,0:T(8,128)S(1)}, u32[]{:S(2)}, u32[]{:S(2)}) collective-permute-start(f32[24,1024]{1,0:T(8,128)S(1)} %slice_select_fusion), channel_id=1, source_target_pairs={{0,16},{1,17},{2,18},{3,19},{4,20},{5,21},{6,22},{7,23},{8,24},{9,... | collective-permute-start | bytes 294920 | tf_op jit(solution)/shard_map/ppermute | solution.py:503
  39.4 8.6 %collective-permute-start.11 = (f32[256,256]{1,0:T(8,128)S(1)}, f32[256,256]{1,0:T(8,128)S(1)}, u32[]{:S(2)}, u32[]{:S(2)}) collective-permute-start(f32[256,256]{1,0:T(8,128)S(1)} %pad_maximum_fusion.here_ref), channel_id=1, source_target_pairs={{8,16},{9,17},{10,18},{11,19},{12,20},{13,21},{14,22},{15,23},{16,... | collective-permute-start | bytes 786440 | tf_op jit(solution)/shard_map/ppermute | solution.py:503
  40.2 7.8 %collective-permute-start.10 = (f32[256,256]{1,0:T(8,128)S(1)}, f32[256,256]{1,0:T(8,128)S(1)}, u32[]{:S(2)}, u32[]{:S(2)}) collective-permute-start(f32[256,256]{1,0:T(8,128)S(1)} %pad_maximum_fusion.here_ref), channel_id=1, source_target_pairs={{0,8},{1,9},{2,10},{3,11},{4,12},{5,13},{6,14},{7,15},{8,0},{9,1},... | collective-permute-start | bytes 786440 | tf_op jit(solution)/shard_map/ppermute | solution.py:503
  41.4 6.7 %collective-permute-start.9 = (f32[24,1024]{1,0:T(8,128)S(1)}, f32[24,1024]{1,0:T(8,128)S(1)}, u32[]{:S(2)}, u32[]{:S(2)}) collective-permute-start(f32[24,1024]{1,0:T(8,128)S(1)} %collective-permute-done.8), channel_id=1, source_target_pairs={{0,1},{1,0},{2,3},{3,2},{4,5},{5,4},{6,7},{7,6},{8,9},{9,8},{10,11... | collective-permute-start | bytes 294920 | tf_op jit(solution)/shard_map/ppermute | solution.py:503
  50.3 7.7 %collective-permute-start.14 = (f32[128,256]{1,0:T(8,128)S(1)}, f32[128,256]{1,0:T(8,128)S(1)}, u32[]{:S(2)}, u32[]{:S(2)}) collective-permute-start(f32[128,256]{1,0:T(8,128)S(1)} %plane_first.1.a_ref.pulled_ref.old_z_ref), channel_id=1, source_target_pairs={{0,6},{1,7},{2,4},{3,5},{4,2},{5,3},{6,0},{7,1},{8,14},{9,15},{10,... | collective-permute-start | bytes 393224 | tf_op jit(solution)/shard_map/ppermute | solution.py:503
  52.4 7.2 %collective-permute-start.13 = (f32[128,256]{1,0:T(8,128)S(1)}, f32[128,256]{1,0:T(8,128)S(1)}, u32[]{:S(2)}, u32[]{:S(2)}) collective-permute-start(f32[128,256]{1,0:T(8,128)S(1)} %plane_first.1.a_ref.pulled_ref.old_z_ref), channel_id=1, source_target_pairs={{0,2},{1,3},{2,0},{3,1},{4,6},{5,7},{6,4},{7,5},{8,10},{9,11},{10,... | collective-permute-start | bytes 393224 | tf_op jit(solution)/shard_map/ppermute | solution.py:503
  52.8 6.8 %collective-permute-start.12 = (f32[128,256]{1,0:T(8,128)S(1)}, f32[128,256]{1,0:T(8,128)S(1)}, u32[]{:S(2)}, u32[]{:S(2)}) collective-permute-start(f32[128,256]{1,0:T(8,128)S(1)} %plane_first.1.a_ref.pulled_ref.old_z_ref), channel_id=1, source_target_pairs={{0,4},{1,5},{2,6},{3,7},{4,0},{5,1},{6,2},{7,3},{8,12},{9,13},{10,... | collective-permute-start | bytes 393224 | tf_op jit(solution)/shard_map/ppermute | solution.py:503
  62.0 3.5 %collective-permute-start.17 = (f32[128,256]{1,0:T(8,128)S(1)}, f32[128,256]{1,0:T(8,128)S(1)}, u32[]{:S(2)}, u32[]{:S(2)}) collective-permute-start(f32[128,256]{1,0:T(8,128)S(1)} %add.61.here_ref.old_s_ref), channel_id=1, source_target_pairs={{8,16},{9,17},{10,18},{11,19},{12,20},{13,21},{14,22},{15,23},{16,... | collective-permute-start | bytes 393224 | tf_op jit(solution)/shard_map/ppermute | solution.py:503
  62.7 6.1 %collective-permute-start.16 = (f32[128,256]{1,0:T(8,128)S(1)}, f32[128,256]{1,0:T(8,128)S(1)}, u32[]{:S(2)}, u32[]{:S(2)}) collective-permute-start(f32[128,256]{1,0:T(8,128)S(1)} %add.61.here_ref.old_s_ref), channel_id=1, source_target_pairs={{0,8},{1,9},{2,10},{3,11},{4,12},{5,13},{6,14},{7,15},{8,0},{9,1},... | collective-permute-start | bytes 393224 | tf_op jit(solution)/shard_map/ppermute | solution.py:503
  70.6 4.9 %collective-permute-start.20 = (f32[136,256]{1,0:T(8,128)S(1)}, f32[136,256]{1,0:T(8,128)S(1)}, u32[]{:S(2)}, u32[]{:S(2)}) collective-permute-start(f32[136,256]{1,0:T(8,128)S(1)} %get-tuple-element.70.a_ref.pulled_ref), channel_id=1, source_target_pairs={{0,6},{1,7},{2,4},{3,5},{4,2},{5,3},{6,0},{7,1},{8,14},{9,15},{10,... | collective-permute-start | bytes 417800 | tf_op jit(solution)/shard_map/ppermute | solution.py:503
  72.4 7.2 %collective-permute-start.19 = (f32[136,256]{1,0:T(8,128)S(1)}, f32[136,256]{1,0:T(8,128)S(1)}, u32[]{:S(2)}, u32[]{:S(2)}) collective-permute-start(f32[136,256]{1,0:T(8,128)S(1)} %get-tuple-element.70.a_ref.pulled_ref), channel_id=1, source_target_pairs={{0,2},{1,3},{2,0},{3,1},{4,6},{5,7},{6,4},{7,5},{8,10},{9,11},{10,... | collective-permute-start | bytes 417800 | tf_op jit(solution)/shard_map/ppermute | solution.py:503
  73.0 6.6 %collective-permute-start.18 = (f32[136,256]{1,0:T(8,128)S(1)}, f32[136,256]{1,0:T(8,128)S(1)}, u32[]{:S(2)}, u32[]{:S(2)}) collective-permute-start(f32[136,256]{1,0:T(8,128)S(1)} %get-tuple-element.70.a_ref.pulled_ref), channel_id=1, source_target_pairs={{0,4},{1,5},{2,6},{3,7},{4,0},{5,1},{6,2},{7,3},{8,12},{9,13},{10,... | collective-permute-start | bytes 417800 | tf_op jit(solution)/shard_map/ppermute | solution.py:503
  80.1 2.5 %collective-permute-start.21 = (f32[392,256]{1,0:T(8,128)S(1)}, f32[392,256]{1,0:T(8,128)S(1)}, u32[]{:S(2)}, u32[]{:S(2)}) collective-permute-start(f32[392,256]{1,0:T(8,128)S(1)} %get-tuple-element.73), channel_id=1, source_target_pairs={{0,1},{1,0},{2,3},{3,2},{4,5},{5,4},{6,7},{7,6},{8,9},{9,8},{10,11... | collective-permute-start | bytes 1204232 | tf_op jit(solution)/shard_map/ppermute | solution.py:503
  82.6 5.7 %collective-permute-start.25 = (f32[136,256]{1,0:T(8,128)S(1)}, f32[136,256]{1,0:T(8,128)S(1)}, u32[]{:S(2)}, u32[]{:S(2)}) collective-permute-start(f32[136,256]{1,0:T(8,128)S(1)} %slice_add_fusion.1.here_ref), channel_id=1, source_target_pairs={{8,16},{9,17},{10,18},{11,19},{12,20},{13,21},{14,22},{15,23},{16,... | collective-permute-start | bytes 417800 | tf_op jit(solution)/shard_map/ppermute | solution.py:503
  83.5 6.7 %collective-permute-start.22 = (f32[136,256]{1,0:T(8,128)S(1)}, f32[136,256]{1,0:T(8,128)S(1)}, u32[]{:S(2)}, u32[]{:S(2)}) collective-permute-start(f32[136,256]{1,0:T(8,128)S(1)} %slice_add_fusion.1.here_ref), channel_id=1, source_target_pairs={{0,8},{1,9},{2,10},{3,11},{4,12},{5,13},{6,14},{7,15},{8,0},{9,1},... | collective-permute-start | bytes 417800 | tf_op jit(solution)/shard_map/ppermute | solution.py:503
  86.8 4.7 %collective-permute-start.24 = (f32[8,256]{1,0:T(8,128)S(1)}, f32[8,256]{1,0:T(8,128)S(1)}, u32[]{:S(2)}, u32[]{:S(2)}) collective-permute-start(f32[8,256]{1,0:T(8,128)S(1)} %slice.31), channel_id=1, source_target_pairs={{0,24},{1,25},{2,26},{3,27},{4,28},{5,29},{6,30},{7,31},{8,16},{9,... | collective-permute-start | bytes 24584 | tf_op jit(solution)/shard_map/ppermute | solution.py:503
  88.3 3.4 %collective-permute-start.23 = (f32[8,256]{1,0:T(8,128)S(1)}, f32[8,256]{1,0:T(8,128)S(1)}, u32[]{:S(2)}, u32[]{:S(2)}) collective-permute-start(f32[8,256]{1,0:T(8,128)S(1)} %slice.31), channel_id=1, source_target_pairs={{0,16},{1,17},{2,18},{3,19},{4,20},{5,21},{6,22},{7,23},{8,24},{9,... | collective-permute-start | bytes 24584 | tf_op jit(solution)/shard_map/ppermute | solution.py:503
  93.0 5.0 %collective-permute-start.28 = (f32[136,256]{1,0:T(8,128)S(1)}, f32[136,256]{1,0:T(8,128)S(1)}, u32[]{:S(2)}, u32[]{:S(2)}) collective-permute-start(f32[136,256]{1,0:T(8,128)S(1)} %get-tuple-element.75.a_ref.pulled_ref), channel_id=1, source_target_pairs={{0,6},{1,7},{2,4},{3,5},{4,2},{5,3},{6,0},{7,1},{8,14},{9,15},{10,... | collective-permute-start | bytes 417800 | tf_op jit(solution)/shard_map/ppermute | solution.py:503
  94.5 5.3 %collective-permute-start.27 = (f32[136,256]{1,0:T(8,128)S(1)}, f32[136,256]{1,0:T(8,128)S(1)}, u32[]{:S(2)}, u32[]{:S(2)}) collective-permute-start(f32[136,256]{1,0:T(8,128)S(1)} %get-tuple-element.75.a_ref.pulled_ref), channel_id=1, source_target_pairs={{0,2},{1,3},{2,0},{3,1},{4,6},{5,7},{6,4},{7,5},{8,10},{9,11},{10,... | collective-permute-start | bytes 417800 | tf_op jit(solution)/shard_map/ppermute | solution.py:503
  95.4 4.6 %collective-permute-start.26 = (f32[136,256]{1,0:T(8,128)S(1)}, f32[136,256]{1,0:T(8,128)S(1)}, u32[]{:S(2)}, u32[]{:S(2)}) collective-permute-start(f32[136,256]{1,0:T(8,128)S(1)} %get-tuple-element.75.a_ref.pulled_ref), channel_id=1, source_target_pairs={{0,4},{1,5},{2,6},{3,7},{4,0},{5,1},{6,2},{7,3},{8,12},{9,13},{10,... | collective-permute-start | bytes 417800 | tf_op jit(solution)/shard_map/ppermute | solution.py:503
  100.6 4.8 %collective-permute-start.29 = (f32[392,256]{1,0:T(8,128)S(1)}, f32[392,256]{1,0:T(8,128)S(1)}, u32[]{:S(2)}, u32[]{:S(2)}) collective-permute-start(f32[392,256]{1,0:T(8,128)S(1)} %get-tuple-element.79), channel_id=1, source_target_pairs={{0,1},{1,0},{2,3},{3,2},{4,5},{5,4},{6,7},{7,6},{8,9},{9,8},{10,11... | collective-permute-start | bytes 1204232 | tf_op jit(solution)/shard_map/ppermute | solution.py:503
  105.4 5.2 %collective-permute-start.30 = (f32[136,256]{1,0:T(8,128)S(1)}, f32[136,256]{1,0:T(8,128)S(1)}, u32[]{:S(2)}, u32[]{:S(2)}) collective-permute-start(f32[136,256]{1,0:T(8,128)S(1)} %slice_add_fusion.here_ref), channel_id=1, source_target_pairs={{0,8},{1,9},{2,10},{3,11},{4,12},{5,13},{6,14},{7,15},{8,16},{9,17... | collective-permute-start | bytes 417800 | tf_op jit(solution)/shard_map/ppermute | solution.py:503
  109.9 8.0 %collective-permute-start.31 = (f32[256,256]{1,0:T(8,128)}, f32[256,256]{1,0:T(8,128)S(1)}, u32[]{:S(2)}, u32[]{:S(2)}) collective-permute-start(f32[256,256]{1,0:T(8,128)} %get-tuple-element.86), channel_id=1, source_target_pairs={{0,1},{1,0},{2,3},{3,2},{4,5},{5,4},{6,7},{7,6},{8,9},{9,8},{10,11... | collective-permute-start | bytes 786440 | tf_op jit(solution)/shard_map/ppermute | solution.py:503
  112.0 14.1 %all-to-all-start = ((f32[32,8,128]{2,1,0:T(8,128)}), f32[32,8,128]{2,1,0:T(8,128)S(1)}, u32[]{:S(2)}, u32[]{:S(2)}) async-start(f32[32,8,128]{2,1,0:T(8,128)} %plane_close.1), calls=%async_computation | async-start | bytes 262144 | tf_op jit(solution)/shard_map/all_to_all | solution.py:1176
  126.9 13.3 %collective-permute-start.32 = (f32[512,128]{1,0:T(8,128)S(1)}, f32[512,128]{1,0:T(8,128)S(1)}, u32[]{:S(2)}, u32[]{:S(2)}) collective-permute-start(f32[512,128]{1,0:T(8,128)S(1)} %plane_combine.1), channel_id=1, source_target_pairs={{0,0},{1,16},{2,8},{3,24},{4,4},{5,20},{6,12},{7,28},{8,1},{9,17},... | collective-permute-start | bytes 786440 | tf_op jit(solution)/shard_map/ppermute | solution.py:503
  (12 other events, 158.0 us)

commit v22 on v21

--- a/solution.py
+++ b/solution.py
@@ -1097,13 +1097,13 @@
     forward3, _, inverse_last3, short3 = turned_transforms(3)
     block, noted = (hours, rows), (hours + NOTE, rows)
 
-    seen = moved(observed, to_plane)
     parcel = send(incidence, first_guess, row_gauge, gauge_kernel)
     parcel, near = lax.optimization_barrier((parcel, incidence))
     parcel = moved(parcel, to_plane)
-    near, seen = lax.optimization_barrier((near, seen))
     meta = describe(near, row_gauge)
     meta = jnp.concatenate([meta, moved(meta, over_x)], axis=1)
+    meta, seen = lax.optimization_barrier((meta, observed))
+    seen = moved(seen, to_plane)
     meta = jnp.concatenate([meta, moved(meta, z_pair)], axis=1)
     parcel, seen = lax.optimization_barrier((parcel, seen))
     parcels = [parcel, moved(parcel, over_core)]

time: 142 us -> 146 us (1.028)
  starting transfers between devices: 52.3 us -> 57.7 us
    ppermute x33, starting transfers between devices: 46.4 us -> 52.1 us  [moved(): return lax.ppermute(value, ('basin', 'tm'), pairs)]
  transfers between devices with their start and end apart: 34 -> 34, of which waited for: 21 -> 16; matrix products, arithmetic and copies ran while one was open for 0% -> 0% of each run, Pallas kernels for 12% -> 12%
where the time goes in v22:
time: 146 us
  starting transfers between devices  57.7 us (40%)
  waiting for transfers between devices  54.8 us (38%)
  Pallas kernels  32 us (22%)
    ppermute x33, starting transfers between devices, moved(): return lax.ppermute(value, ('basin', 'tm'), pairs)  52.1 us
    ppermute x33, waiting for transfers between devices, moved(): return lax.ppermute(value, ('basin', 'tm'), pairs)  46.6 us
    pallas_call x2, Pallas kernels, plane_couple(): pl.pallas_call(functools.partial(plane_couple_kernel, last), in_specs=[pl...  9.56 us
    pallas_call x6, Pallas kernels, plane_call(): pl.pallas_call(kernel, in_specs=[pl.BlockSpec(memory_space=pltpu.SMEM)] *...  8.9 us
    all_to_all x1, waiting for transfers between devices, plane_shards(): close_note = lax.all_to_all(note, ('basin', 'tm'), 0, 0, tiled=False)  8.18 us
    all_to_all x1, starting transfers between devices, plane_shards(): close_note = lax.all_to_all(note, ('basin', 'tm'), 0, 0, tiled=False)  5.6 us
    pallas_call x3, Pallas kernels, plane_rows(): pl.pallas_call(plane_rows_kernel, in_specs=[pl.BlockSpec(memory_space=plt...  4.49 us
    pallas_call x1, Pallas kernels, send(): pl.pallas_call(send_kernel, in_specs=[pl.BlockSpec(memory_space=pltpu.HBM...  3.27 us
  transfers between devices with their start and end apart: 34, of which 16 were waited for; matrix products, arithmetic and copies ran while one was open for 0% of the time, Pallas kernels for 12%

profile of v22, /device:TPU:1, one launch (start us, length us, event | category | flops | bytes accessed | tf_op | source)
XLA Modules:
  0.0 145.5 jit_solution(16871778625250444566)
XLA Ops:
  0.0 3.3 %send.1 = f32[136,512]{1,0:T(8,128)} custom-call(s32[32,16,128]{2,1,0:T(8,128)} %inc_ref.2, f32[4096,128]{1,0:T(8,128)} %field_ref.1, s32[1,512]{1,0:T(1,128)} %bitcast.11, s32[1,256]{1,0:T(1,128)} %bitcast.14), custom_call_target="tpu_custom_call" | custom-call | flops 1 | bytes 1 | tf_op jit(solution)/shard_map/send/pallas_call | solution.py:680
  3.5 2.1 %collective-permute-start.1 = (f32[24,512]{1,0:T(8,128)S(1)}, f32[24,512]{1,0:T(8,128)S(1)}, u32[]{:S(2)}, u32[]{:S(2)}) collective-permute-start(f32[24,512]{1,0:T(8,128)S(1)} %describe.1), channel_id=1, source_target_pairs={{0,4},{1,5},{2,6},{3,7},{4,0},{5,1},{6,2},{7,3},{8,12},{9,13},{10,... | collective-permute-start | bytes 147464 | tf_op jit(solution)/shard_map/ppermute | solution.py:503
  5.7 4.0 %collective-permute-start = (f32[136,512]{1,0:T(8,128)}, f32[136,512]{1,0:T(8,128)S(1)}, u32[]{:S(2)}, u32[]{:S(2)}) collective-permute-start(f32[136,512]{1,0:T(8,128)} %send.1), channel_id=1, source_target_pairs={{0,0},{1,8},{2,16},{3,24},{4,4},{5,12},{6,20},{7,28},{8,2},{9,10},... | collective-permute-start | bytes 835592 | tf_op jit(solution)/shard_map/ppermute | solution.py:503
  10.0 3.3 %collective-permute-start.2 = (f32[256,128]{0,1:T(8,128)S(1)}, f32[256,128]{0,1:T(8,128)S(1)}, u32[]{:S(2)}, u32[]{:S(2)}) collective-permute-start(f32[256,128]{0,1:T(8,128)S(1)} %copy.13), channel_id=1, source_target_pairs={{0,0},{1,8},{2,16},{3,24},{4,4},{5,12},{6,20},{7,28},{8,2},{9,10},... | collective-permute-start | bytes 393224 | tf_op jit(solution)/shard_map/ppermute | solution.py:503
  14.8 13.9 %collective-permute-done.2 = f32[256,128]{0,1:T(8,128)S(1)} collective-permute-done((f32[256,128]{0,1:T(8,128)S(1)}, f32[256,128]{0,1:T(8,128)S(1)}, u32[]{:S(2)}, u32[]{:S(2)}) %collective-permute-start.2) | collective-permute-done | bytes 131104 | tf_op jit(solution)/shard_map/ppermute | solution.py:503
  30.3 1.6 %spread.1 = (f32[128,256]{1,0:T(8,128)S(1)}, f32[128,256]{1,0:T(8,128)S(1)}, f32[128,256]{1,0:T(8,128)S(1)}, f32[128,256]{1,0:T(8,128)S(1)}) custom-call(s32[6]{0:T(128)S(1)} %broadcast_multiply_fusion.first_ref, f32[136,512]{1,0:T(8,128)S(1)} %collective-permute-done.mine_ref, f32[136,512]{1,0:T(8,128)S(1)} %collective-permute-done.3.other_ref), custom_call_target="tpu_custom_call" | custom-call | flops 1 | bytes 1 | tf_op jit(solution)/shard_map/spread/pallas_call | solution.py:714
  32.2 2.4 %collective-permute-start.7 = (f32[128,256]{1,0:T(8,128)S(1)}, f32[128,256]{1,0:T(8,128)S(1)}, u32[]{:S(2)}, u32[]{:S(2)}) collective-permute-start(f32[128,256]{1,0:T(8,128)S(1)} %get-tuple-element.56), channel_id=1, source_target_pairs={{0,6},{1,7},{2,4},{3,5},{4,2},{5,3},{6,0},{7,1},{8,14},{9,15},{10,... | collective-permute-start | bytes 393224 | tf_op jit(solution)/shard_map/ppermute | solution.py:503
  34.6 2.5 %collective-permute-start.8 = (f32[24,1024]{1,0:T(8,128)S(1)}, f32[24,1024]{1,0:T(8,128)S(1)}, u32[]{:S(2)}, u32[]{:S(2)}) collective-permute-start(f32[24,1024]{1,0:T(8,128)S(1)} %slice_select_fusion), channel_id=1, source_target_pairs={{0,16},{1,17},{2,18},{3,19},{4,20},{5,21},{6,22},{7,23},{8,24},{9,... | collective-permute-start | bytes 294920 | tf_op jit(solution)/shard_map/ppermute | solution.py:503
  37.1 2.5 %collective-permute-done.6 = f32[128,256]{1,0:T(8,128)S(1)} collective-permute-done((f32[128,256]{1,0:T(8,128)S(1)}, f32[128,256]{1,0:T(8,128)S(1)}, u32[]{:S(2)}, u32[]{:S(2)}) %collective-permute-start.6) | collective-permute-done | bytes 131104 | tf_op jit(solution)/shard_map/ppermute | solution.py:503
  40.6 5.0 %collective-permute-start.10 = (f32[256,256]{1,0:T(8,128)S(1)}, f32[256,256]{1,0:T(8,128)S(1)}, u32[]{:S(2)}, u32[]{:S(2)}) collective-permute-start(f32[256,256]{1,0:T(8,128)S(1)} %pad_maximum_fusion.here_ref), channel_id=1, source_target_pairs={{0,8},{1,9},{2,10},{3,11},{4,12},{5,13},{6,14},{7,15},{8,0},{9,1},... | collective-permute-start | bytes 786440 | tf_op jit(solution)/shard_map/ppermute | solution.py:503
  45.6 1.8 %collective-permute-start.9 = (f32[24,1024]{1,0:T(8,128)S(1)}, f32[24,1024]{1,0:T(8,128)S(1)}, u32[]{:S(2)}, u32[]{:S(2)}) collective-permute-start(f32[24,1024]{1,0:T(8,128)S(1)} %collective-permute-done.8), channel_id=1, source_target_pairs={{0,1},{1,0},{2,3},{3,2},{4,5},{5,4},{6,7},{7,6},{8,9},{9,8},{10,11... | collective-permute-start | bytes 294920 | tf_op jit(solution)/shard_map/ppermute | solution.py:503
  47.4 4.6 %plane_couple.2.refs_1_ = f32[1024,512]{1,0:T(8,128)S(1)} custom-call(s32[6]{0:T(128)S(1)} %broadcast_multiply_fusion.first_ref, f32[24,2048]{1,0:T(8,128)S(1)} %pad_maximum_fusion.1.refs_0_), custom_call_target="tpu_custom_call" | custom-call | flops 2147483648 | bytes 2000000 | tf_op jit(solution)/shard_map/plane_couple/pallas_call | solution.py:780
  52.1 2.2 %plane_first.1.a_ref.pulled_ref.old_z_ref = f32[128,256]{1,0:T(8,128)S(1)} custom-call(f32[3]{0:T(128)S(1)} %add_convert_fusion.flag_ref, f32[256,256]{1,0:T(8,128)S(1)} %pad_maximum_fusion.here_ref, f32[256,256]{1,0:T(8,128)S(1)} %collective-permute-done.10.pair_ref, f32[256,256]{1,0:T(8,128)S(1)} %collective-permute-done.11.middle_ref, ...), custom_call_target="tpu_custom_call" | custom-call | flops 1 | bytes 1 | tf_op jit(solution)/shard_map/plane_first/pallas_call | solution.py:907
  54.3 1.5 %collective-permute-start.14 = (f32[128,256]{1,0:T(8,128)S(1)}, f32[128,256]{1,0:T(8,128)S(1)}, u32[]{:S(2)}, u32[]{:S(2)}) collective-permute-start(f32[128,256]{1,0:T(8,128)S(1)} %plane_first.1.a_ref.pulled_ref.old_z_ref), channel_id=1, source_target_pairs={{0,6},{1,7},{2,4},{3,5},{4,2},{5,3},{6,0},{7,1},{8,14},{9,15},{10,... | collective-permute-start | bytes 393224 | tf_op jit(solution)/shard_map/ppermute | solution.py:503
  57.0 4.9 %plane_couple.3 = (bf16[1024,512]{1,0:T(8,128)(2,1)S(1)}, bf16[1024,512]{1,0:T(8,128)(2,1)S(1)}) custom-call(s32[6]{0:T(128)S(1)} %broadcast_multiply_fusion.first_ref, f32[24,2048]{1,0:T(8,128)S(1)} %pad_maximum_fusion.2.refs_0_, f32[1024,512]{1,0:T(8,128)S(1)} %plane_couple.2.refs_1_), custom_call_target="tpu_custom_call" | custom-call | flops 2147483648 | bytes 2000000 | tf_op jit(solution)/shard_map/plane_couple/pallas_call | solution.py:780
  62.0 1.5 %collective-permute-done.13.c_ref = f32[128,256]{1,0:T(8,128)S(1)} collective-permute-done((f32[128,256]{1,0:T(8,128)S(1)}, f32[128,256]{1,0:T(8,128)S(1)}, u32[]{:S(2)}, u32[]{:S(2)}) %collective-permute-start.13) | collective-permute-done | bytes 131104 | tf_op jit(solution)/shard_map/ppermute | solution.py:503
  66.3 3.1 %collective-permute-start.16 = (f32[128,256]{1,0:T(8,128)S(1)}, f32[128,256]{1,0:T(8,128)S(1)}, u32[]{:S(2)}, u32[]{:S(2)}) collective-permute-start(f32[128,256]{1,0:T(8,128)S(1)} %add.61.here_ref.old_s_ref), channel_id=1, source_target_pairs={{0,8},{1,9},{2,10},{3,11},{4,12},{5,13},{6,14},{7,15},{8,0},{9,1},... | collective-permute-start | bytes 393224 | tf_op jit(solution)/shard_map/ppermute | solution.py:503
  69.4 3.3 %collective-permute-done.16.pair_ref = f32[128,256]{1,0:T(8,128)S(1)} collective-permute-done((f32[128,256]{1,0:T(8,128)S(1)}, f32[128,256]{1,0:T(8,128)S(1)}, u32[]{:S(2)}, u32[]{:S(2)}) %collective-permute-start.16) | collective-permute-done | bytes 131104 | tf_op jit(solution)/shard_map/ppermute | solution.py:503
  72.7 1.8 %plane_open.1 = (f32[136,256]{1,0:T(8,128)S(1)}, f32[256,256]{1,0:T(8,128)S(1)}) custom-call(f32[3]{0:T(128)S(1)} %add_convert_fusion.flag_ref, f32[128,256]{1,0:T(8,128)S(1)} %add.61.here_ref.old_s_ref, f32[128,256]{1,0:T(8,128)S(1)} %collective-permute-done.16.pair_ref, f32[128,256]{1,0:T(8,128)S(1)} %collective-permute-done.17.middle_ref, ...), custom_call_target="tpu_custom_call" | custom-call | flops 1 | bytes 1 | tf_op jit(solution)/shard_map/plane_open/pallas_call | solution.py:907
  79.5 4.2 %collective-permute-done.19.c_ref = f32[136,256]{1,0:T(8,128)S(1)} collective-permute-done((f32[136,256]{1,0:T(8,128)S(1)}, f32[136,256]{1,0:T(8,128)S(1)}, u32[]{:S(2)}, u32[]{:S(2)}) %collective-permute-start.19) | collective-permute-done | bytes 139296 | tf_op jit(solution)/shard_map/ppermute | solution.py:503
  87.4 3.2 %collective-permute-start.22 = (f32[136,256]{1,0:T(8,128)S(1)}, f32[136,256]{1,0:T(8,128)S(1)}, u32[]{:S(2)}, u32[]{:S(2)}) collective-permute-start(f32[136,256]{1,0:T(8,128)S(1)} %slice_add_fusion.1.here_ref), channel_id=1, source_target_pairs={{0,8},{1,9},{2,10},{3,11},{4,12},{5,13},{6,14},{7,15},{8,0},{9,1},... | collective-permute-start | bytes 417800 | tf_op jit(solution)/shard_map/ppermute | solution.py:503
  90.7 1.6 %collective-permute-start.24 = (f32[8,256]{1,0:T(8,128)S(1)}, f32[8,256]{1,0:T(8,128)S(1)}, u32[]{:S(2)}, u32[]{:S(2)}) collective-permute-start(f32[8,256]{1,0:T(8,128)S(1)} %slice.31), channel_id=1, source_target_pairs={{0,24},{1,25},{2,26},{3,27},{4,28},{5,29},{6,30},{7,31},{8,16},{9,... | collective-permute-start | bytes 24584 | tf_op jit(solution)/shard_map/ppermute | solution.py:503
  92.2 1.8 %collective-permute-done.22.pair_ref = f32[136,256]{1,0:T(8,128)S(1)} collective-permute-done((f32[136,256]{1,0:T(8,128)S(1)}, f32[136,256]{1,0:T(8,128)S(1)}, u32[]{:S(2)}, u32[]{:S(2)}) %collective-permute-start.22) | collective-permute-done | bytes 139296 | tf_op jit(solution)/shard_map/ppermute | solution.py:503
  101.9 1.8 %collective-permute-done.27.c_ref = f32[136,256]{1,0:T(8,128)S(1)} collective-permute-done((f32[136,256]{1,0:T(8,128)S(1)}, f32[136,256]{1,0:T(8,128)S(1)}, u32[]{:S(2)}, u32[]{:S(2)}) %collective-permute-start.27) | collective-permute-done | bytes 139296 | tf_op jit(solution)/shard_map/ppermute | solution.py:503
  104.3 3.4 %collective-permute-start.29 = (f32[392,256]{1,0:T(8,128)S(1)}, f32[392,256]{1,0:T(8,128)S(1)}, u32[]{:S(2)}, u32[]{:S(2)}) collective-permute-start(f32[392,256]{1,0:T(8,128)S(1)} %get-tuple-element.79), channel_id=1, source_target_pairs={{0,1},{1,0},{2,3},{3,2},{4,5},{5,4},{6,7},{7,6},{8,9},{9,8},{10,11... | collective-permute-start | bytes 1204232 | tf_op jit(solution)/shard_map/ppermute | solution.py:503
  109.0 2.8 %collective-permute-start.30 = (f32[136,256]{1,0:T(8,128)S(1)}, f32[136,256]{1,0:T(8,128)S(1)}, u32[]{:S(2)}, u32[]{:S(2)}) collective-permute-start(f32[136,256]{1,0:T(8,128)S(1)} %slice_add_fusion.here_ref), channel_id=1, source_target_pairs={{0,8},{1,9},{2,10},{3,11},{4,12},{5,13},{6,14},{7,15},{8,16},{9,17... | collective-permute-start | bytes 417800 | tf_op jit(solution)/shard_map/ppermute | solution.py:503
  111.8 2.0 %plane_rows.5 = (f32[128,512]{1,0:T(8,128)S(1)}, f32[256,256]{1,0:T(8,128)}, f32[256,512]{1,0:T(8,128)S(1)}) custom-call(s32[6]{0:T(128)S(1)} %broadcast_multiply_fusion.first_ref, f32[8,512]{1,0:T(8,128)S(1)} %slice.23.class_ref.meta_ref, f32[8,512]{1,0:T(8,128)S(1)} %slice.26.meta_other_ref, f32[136,256]{1,0:T(8,128)S(1)} %get-tuple-element.75.a_ref.pulled_ref, ...), custom_call_target="tpu_custom_call" | custom-call | flops 1000000000 | bytes 2000000 | tf_op jit(solution)/shard_map/plane_rows/pallas_call | solution.py:863
  115.9 5.6 %all-to-all-start = ((f32[32,8,128]{2,1,0:T(8,128)}), f32[32,8,128]{2,1,0:T(8,128)S(1)}, u32[]{:S(2)}, u32[]{:S(2)}) async-start(f32[32,8,128]{2,1,0:T(8,128)} %plane_close.1), calls=%async_computation | async-start | bytes 262144 | tf_op jit(solution)/shard_map/all_to_all | solution.py:1176
  121.5 8.2 %all-to-all-done.close_ref = f32[32,8,128]{2,1,0:T(8,128)S(1)} async-done(((f32[32,8,128]{2,1,0:T(8,128)}), f32[32,8,128]{2,1,0:T(8,128)S(1)}, u32[]{:S(2)}, u32[]{:S(2)}) %all-to-all-start) | async-done | bytes 131104 | tf_op jit(solution)/shard_map/all_to_all | solution.py:1176
  130.6 2.6 %collective-permute-start.32 = (f32[512,128]{1,0:T(8,128)S(1)}, f32[512,128]{1,0:T(8,128)S(1)}, u32[]{:S(2)}, u32[]{:S(2)}) collective-permute-start(f32[512,128]{1,0:T(8,128)S(1)} %plane_combine.1), channel_id=1, source_target_pairs={{0,0},{1,16},{2,8},{3,24},{4,4},{5,20},{6,12},{7,28},{8,1},{9,17},... | collective-permute-start | bytes 786440 | tf_op jit(solution)/shard_map/ppermute | solution.py:503
  133.2 10.7 %collective-permute-done.32.rows_ref = f32[512,128]{1,0:T(8,128)S(1)} collective-permute-done((f32[512,128]{1,0:T(8,128)S(1)}, f32[512,128]{1,0:T(8,128)S(1)}, u32[]{:S(2)}, u32[]{:S(2)}) %collective-permute-start.32) | collective-permute-done | bytes 262176 | tf_op jit(solution)/shard_map/ppermute | solution.py:503
  143.9 1.6 %plane_finish.1 = f32[4096,128]{1,0:T(8,128)} custom-call(f32[512,128]{1,0:T(8,128)S(1)} %collective-permute-done.32.rows_ref, s32[32,16,128]{2,1,0:T(8,128)S(1)} %copy-done.2, f32[4096,128]{1,0:T(8,128)S(1)} %copy-done.1), custom_call_target="tpu_custom_call" | custom-call | tf_op jit(solution)/shard_map/plane_finish/pallas_call | solution.py:1073
  (93 shorter events, 30.1 us)
Async XLA Ops:
  3.5 6.3 %collective-permute-start.1 = (f32[24,512]{1,0:T(8,128)S(1)}, f32[24,512]{1,0:T(8,128)S(1)}, u32[]{:S(2)}, u32[]{:S(2)}) collective-permute-start(f32[24,512]{1,0:T(8,128)S(1)} %describe.1), channel_id=1, source_target_pairs={{0,4},{1,5},{2,6},{3,7},{4,0},{5,1},{6,2},{7,3},{8,12},{9,13},{10,... | collective-permute-start | bytes 147464 | tf_op jit(solution)/shard_map/ppermute | solution.py:503
  5.7 23.1 %collective-permute-start = (f32[136,512]{1,0:T(8,128)}, f32[136,512]{1,0:T(8,128)S(1)}, u32[]{:S(2)}, u32[]{:S(2)}) collective-permute-start(f32[136,512]{1,0:T(8,128)} %send.1), channel_id=1, source_target_pairs={{0,0},{1,8},{2,16},{3,24},{4,4},{5,12},{6,20},{7,28},{8,2},{9,10},... | collective-permute-start | bytes 835592 | tf_op jit(solution)/shard_map/ppermute | solution.py:503
  10.0 18.8 %collective-permute-start.2 = (f32[256,128]{0,1:T(8,128)S(1)}, f32[256,128]{0,1:T(8,128)S(1)}, u32[]{:S(2)}, u32[]{:S(2)}) collective-permute-start(f32[256,128]{0,1:T(8,128)S(1)} %copy.13), channel_id=1, source_target_pairs={{0,0},{1,8},{2,16},{3,24},{4,4},{5,12},{6,20},{7,28},{8,2},{9,10},... | collective-permute-start | bytes 393224 | tf_op jit(solution)/shard_map/ppermute | solution.py:503
  13.3 15.5 %collective-permute-start.4 = (f32[24,1024]{1,0:T(8,128)S(1)}, f32[24,1024]{1,0:T(8,128)S(1)}, u32[]{:S(2)}, u32[]{:S(2)}) collective-permute-start(f32[24,1024]{1,0:T(8,128)S(1)} %pad_maximum_fusion.3), channel_id=1, source_target_pairs={{0,8},{1,9},{2,10},{3,11},{4,12},{5,13},{6,14},{7,15},{8,0},{9,1},... | collective-permute-start | bytes 294920 | tf_op jit(solution)/shard_map/ppermute | solution.py:503
  31.9 5.2 %collective-permute-start.5 = (f32[128,256]{1,0:T(8,128)S(1)}, f32[128,256]{1,0:T(8,128)S(1)}, u32[]{:S(2)}, u32[]{:S(2)}) collective-permute-start(f32[128,256]{1,0:T(8,128)S(1)} %get-tuple-element.54), channel_id=1, source_target_pairs={{0,4},{1,5},{2,6},{3,7},{4,0},{5,1},{6,2},{7,3},{8,12},{9,13},{10,... | collective-permute-start | bytes 393224 | tf_op jit(solution)/shard_map/ppermute | solution.py:503
  32.2 7.4 %collective-permute-start.6 = (f32[128,256]{1,0:T(8,128)S(1)}, f32[128,256]{1,0:T(8,128)S(1)}, u32[]{:S(2)}, u32[]{:S(2)}) collective-permute-start(f32[128,256]{1,0:T(8,128)S(1)} %get-tuple-element.55), channel_id=1, source_target_pairs={{0,2},{1,3},{2,0},{3,1},{4,6},{5,7},{6,4},{7,5},{8,10},{9,11},{10,... | collective-permute-start | bytes 393224 | tf_op jit(solution)/shard_map/ppermute | solution.py:503
  32.2 7.4 %collective-permute-start.7 = (f32[128,256]{1,0:T(8,128)S(1)}, f32[128,256]{1,0:T(8,128)S(1)}, u32[]{:S(2)}, u32[]{:S(2)}) collective-permute-start(f32[128,256]{1,0:T(8,128)S(1)} %get-tuple-element.56), channel_id=1, source_target_pairs={{0,6},{1,7},{2,4},{3,5},{4,2},{5,3},{6,0},{7,1},{8,14},{9,15},{10,... | collective-permute-start | bytes 393224 | tf_op jit(solution)/shard_map/ppermute | solution.py:503
  34.6 5.1 %collective-permute-start.8 = (f32[24,1024]{1,0:T(8,128)S(1)}, f32[24,1024]{1,0:T(8,128)S(1)}, u32[]{:S(2)}, u32[]{:S(2)}) collective-permute-start(f32[24,1024]{1,0:T(8,128)S(1)} %slice_select_fusion), channel_id=1, source_target_pairs={{0,16},{1,17},{2,18},{3,19},{4,20},{5,21},{6,22},{7,23},{8,24},{9,... | collective-permute-start | bytes 294920 | tf_op jit(solution)/shard_map/ppermute | solution.py:503
  39.8 12.3 %collective-permute-start.11 = (f32[256,256]{1,0:T(8,128)S(1)}, f32[256,256]{1,0:T(8,128)S(1)}, u32[]{:S(2)}, u32[]{:S(2)}) collective-permute-start(f32[256,256]{1,0:T(8,128)S(1)} %pad_maximum_fusion.here_ref), channel_id=1, source_target_pairs={{8,16},{9,17},{10,18},{11,19},{12,20},{13,21},{14,22},{15,23},{16,... | collective-permute-start | bytes 786440 | tf_op jit(solution)/shard_map/ppermute | solution.py:503
  40.6 11.5 %collective-permute-start.10 = (f32[256,256]{1,0:T(8,128)S(1)}, f32[256,256]{1,0:T(8,128)S(1)}, u32[]{:S(2)}, u32[]{:S(2)}) collective-permute-start(f32[256,256]{1,0:T(8,128)S(1)} %pad_maximum_fusion.here_ref), channel_id=1, source_target_pairs={{0,8},{1,9},{2,10},{3,11},{4,12},{5,13},{6,14},{7,15},{8,0},{9,1},... | collective-permute-start | bytes 786440 | tf_op jit(solution)/shard_map/ppermute | solution.py:503
  45.6 6.4 %collective-permute-start.9 = (f32[24,1024]{1,0:T(8,128)S(1)}, f32[24,1024]{1,0:T(8,128)S(1)}, u32[]{:S(2)}, u32[]{:S(2)}) collective-permute-start(f32[24,1024]{1,0:T(8,128)S(1)} %collective-permute-done.8), channel_id=1, source_target_pairs={{0,1},{1,0},{2,3},{3,2},{4,5},{5,4},{6,7},{7,6},{8,9},{9,8},{10,11... | collective-permute-start | bytes 294920 | tf_op jit(solution)/shard_map/ppermute | solution.py:503
  54.3 7.7 %collective-permute-start.14 = (f32[128,256]{1,0:T(8,128)S(1)}, f32[128,256]{1,0:T(8,128)S(1)}, u32[]{:S(2)}, u32[]{:S(2)}) collective-permute-start(f32[128,256]{1,0:T(8,128)S(1)} %plane_first.1.a_ref.pulled_ref.old_z_ref), channel_id=1, source_target_pairs={{0,6},{1,7},{2,4},{3,5},{4,2},{5,3},{6,0},{7,1},{8,14},{9,15},{10,... | collective-permute-start | bytes 393224 | tf_op jit(solution)/shard_map/ppermute | solution.py:503
  55.8 7.7 %collective-permute-start.13 = (f32[128,256]{1,0:T(8,128)S(1)}, f32[128,256]{1,0:T(8,128)S(1)}, u32[]{:S(2)}, u32[]{:S(2)}) collective-permute-start(f32[128,256]{1,0:T(8,128)S(1)} %plane_first.1.a_ref.pulled_ref.old_z_ref), channel_id=1, source_target_pairs={{0,2},{1,3},{2,0},{3,1},{4,6},{5,7},{6,4},{7,5},{8,10},{9,11},{10,... | collective-permute-start | bytes 393224 | tf_op jit(solution)/shard_map/ppermute | solution.py:503
  55.8 7.7 %collective-permute-start.12 = (f32[128,256]{1,0:T(8,128)S(1)}, f32[128,256]{1,0:T(8,128)S(1)}, u32[]{:S(2)}, u32[]{:S(2)}) collective-permute-start(f32[128,256]{1,0:T(8,128)S(1)} %plane_first.1.a_ref.pulled_ref.old_z_ref), channel_id=1, source_target_pairs={{0,4},{1,5},{2,6},{3,7},{4,0},{5,1},{6,2},{7,3},{8,12},{9,13},{10,... | collective-permute-start | bytes 393224 | tf_op jit(solution)/shard_map/ppermute | solution.py:503
  65.7 3.8 %collective-permute-start.17 = (f32[128,256]{1,0:T(8,128)S(1)}, f32[128,256]{1,0:T(8,128)S(1)}, u32[]{:S(2)}, u32[]{:S(2)}) collective-permute-start(f32[128,256]{1,0:T(8,128)S(1)} %add.61.here_ref.old_s_ref), channel_id=1, source_target_pairs={{8,16},{9,17},{10,18},{11,19},{12,20},{13,21},{14,22},{15,23},{16,... | collective-permute-start | bytes 393224 | tf_op jit(solution)/shard_map/ppermute | solution.py:503
  66.3 6.4 %collective-permute-start.16 = (f32[128,256]{1,0:T(8,128)S(1)}, f32[128,256]{1,0:T(8,128)S(1)}, u32[]{:S(2)}, u32[]{:S(2)}) collective-permute-start(f32[128,256]{1,0:T(8,128)S(1)} %add.61.here_ref.old_s_ref), channel_id=1, source_target_pairs={{0,8},{1,9},{2,10},{3,11},{4,12},{5,13},{6,14},{7,15},{8,0},{9,1},... | collective-permute-start | bytes 393224 | tf_op jit(solution)/shard_map/ppermute | solution.py:503
  74.5 5.0 %collective-permute-start.20 = (f32[136,256]{1,0:T(8,128)S(1)}, f32[136,256]{1,0:T(8,128)S(1)}, u32[]{:S(2)}, u32[]{:S(2)}) collective-permute-start(f32[136,256]{1,0:T(8,128)S(1)} %get-tuple-element.70.a_ref.pulled_ref), channel_id=1, source_target_pairs={{0,6},{1,7},{2,4},{3,5},{4,2},{5,3},{6,0},{7,1},{8,14},{9,15},{10,... | collective-permute-start | bytes 417800 | tf_op jit(solution)/shard_map/ppermute | solution.py:503
  75.5 8.3 %collective-permute-start.19 = (f32[136,256]{1,0:T(8,128)S(1)}, f32[136,256]{1,0:T(8,128)S(1)}, u32[]{:S(2)}, u32[]{:S(2)}) collective-permute-start(f32[136,256]{1,0:T(8,128)S(1)} %get-tuple-element.70.a_ref.pulled_ref), channel_id=1, source_target_pairs={{0,2},{1,3},{2,0},{3,1},{4,6},{5,7},{6,4},{7,5},{8,10},{9,11},{10,... | collective-permute-start | bytes 417800 | tf_op jit(solution)/shard_map/ppermute | solution.py:503
  76.1 7.7 %collective-permute-start.18 = (f32[136,256]{1,0:T(8,128)S(1)}, f32[136,256]{1,0:T(8,128)S(1)}, u32[]{:S(2)}, u32[]{:S(2)}) collective-permute-start(f32[136,256]{1,0:T(8,128)S(1)} %get-tuple-element.70.a_ref.pulled_ref), channel_id=1, source_target_pairs={{0,4},{1,5},{2,6},{3,7},{4,0},{5,1},{6,2},{7,3},{8,12},{9,13},{10,... | collective-permute-start | bytes 417800 | tf_op jit(solution)/shard_map/ppermute | solution.py:503
  84.3 2.2 %collective-permute-start.21 = (f32[392,256]{1,0:T(8,128)S(1)}, f32[392,256]{1,0:T(8,128)S(1)}, u32[]{:S(2)}, u32[]{:S(2)}) collective-permute-start(f32[392,256]{1,0:T(8,128)S(1)} %get-tuple-element.73), channel_id=1, source_target_pairs={{0,1},{1,0},{2,3},{3,2},{4,5},{5,4},{6,7},{7,6},{8,9},{9,8},{10,11... | collective-permute-start | bytes 1204232 | tf_op jit(solution)/shard_map/ppermute | solution.py:503
  86.6 5.7 %collective-permute-start.25 = (f32[136,256]{1,0:T(8,128)S(1)}, f32[136,256]{1,0:T(8,128)S(1)}, u32[]{:S(2)}, u32[]{:S(2)}) collective-permute-start(f32[136,256]{1,0:T(8,128)S(1)} %slice_add_fusion.1.here_ref), channel_id=1, source_target_pairs={{8,16},{9,17},{10,18},{11,19},{12,20},{13,21},{14,22},{15,23},{16,... | collective-permute-start | bytes 417800 | tf_op jit(solution)/shard_map/ppermute | solution.py:503
  87.4 6.7 %collective-permute-start.22 = (f32[136,256]{1,0:T(8,128)S(1)}, f32[136,256]{1,0:T(8,128)S(1)}, u32[]{:S(2)}, u32[]{:S(2)}) collective-permute-start(f32[136,256]{1,0:T(8,128)S(1)} %slice_add_fusion.1.here_ref), channel_id=1, source_target_pairs={{0,8},{1,9},{2,10},{3,11},{4,12},{5,13},{6,14},{7,15},{8,0},{9,1},... | collective-permute-start | bytes 417800 | tf_op jit(solution)/shard_map/ppermute | solution.py:503
  90.7 4.7 %collective-permute-start.24 = (f32[8,256]{1,0:T(8,128)S(1)}, f32[8,256]{1,0:T(8,128)S(1)}, u32[]{:S(2)}, u32[]{:S(2)}) collective-permute-start(f32[8,256]{1,0:T(8,128)S(1)} %slice.31), channel_id=1, source_target_pairs={{0,24},{1,25},{2,26},{3,27},{4,28},{5,29},{6,30},{7,31},{8,16},{9,... | collective-permute-start | bytes 24584 | tf_op jit(solution)/shard_map/ppermute | solution.py:503
  92.2 3.4 %collective-permute-start.23 = (f32[8,256]{1,0:T(8,128)S(1)}, f32[8,256]{1,0:T(8,128)S(1)}, u32[]{:S(2)}, u32[]{:S(2)}) collective-permute-start(f32[8,256]{1,0:T(8,128)S(1)} %slice.31), channel_id=1, source_target_pairs={{0,16},{1,17},{2,18},{3,19},{4,20},{5,21},{6,22},{7,23},{8,24},{9,... | collective-permute-start | bytes 24584 | tf_op jit(solution)/shard_map/ppermute | solution.py:503
  97.0 5.0 %collective-permute-start.28 = (f32[136,256]{1,0:T(8,128)S(1)}, f32[136,256]{1,0:T(8,128)S(1)}, u32[]{:S(2)}, u32[]{:S(2)}) collective-permute-start(f32[136,256]{1,0:T(8,128)S(1)} %get-tuple-element.75.a_ref.pulled_ref), channel_id=1, source_target_pairs={{0,6},{1,7},{2,4},{3,5},{4,2},{5,3},{6,0},{7,1},{8,14},{9,15},{10,... | collective-permute-start | bytes 417800 | tf_op jit(solution)/shard_map/ppermute | solution.py:503
  98.0 5.7 %collective-permute-start.27 = (f32[136,256]{1,0:T(8,128)S(1)}, f32[136,256]{1,0:T(8,128)S(1)}, u32[]{:S(2)}, u32[]{:S(2)}) collective-permute-start(f32[136,256]{1,0:T(8,128)S(1)} %get-tuple-element.75.a_ref.pulled_ref), channel_id=1, source_target_pairs={{0,2},{1,3},{2,0},{3,1},{4,6},{5,7},{6,4},{7,5},{8,10},{9,11},{10,... | collective-permute-start | bytes 417800 | tf_op jit(solution)/shard_map/ppermute | solution.py:503
  98.5 5.2 %collective-permute-start.26 = (f32[136,256]{1,0:T(8,128)S(1)}, f32[136,256]{1,0:T(8,128)S(1)}, u32[]{:S(2)}, u32[]{:S(2)}) collective-permute-start(f32[136,256]{1,0:T(8,128)S(1)} %get-tuple-element.75.a_ref.pulled_ref), channel_id=1, source_target_pairs={{0,4},{1,5},{2,6},{3,7},{4,0},{5,1},{6,2},{7,3},{8,12},{9,13},{10,... | collective-permute-start | bytes 417800 | tf_op jit(solution)/shard_map/ppermute | solution.py:503
  104.3 4.7 %collective-permute-start.29 = (f32[392,256]{1,0:T(8,128)S(1)}, f32[392,256]{1,0:T(8,128)S(1)}, u32[]{:S(2)}, u32[]{:S(2)}) collective-permute-start(f32[392,256]{1,0:T(8,128)S(1)} %get-tuple-element.79), channel_id=1, source_target_pairs={{0,1},{1,0},{2,3},{3,2},{4,5},{5,4},{6,7},{7,6},{8,9},{9,8},{10,11... | collective-permute-start | bytes 1204232 | tf_op jit(solution)/shard_map/ppermute | solution.py:503
  109.0 5.4 %collective-permute-start.30 = (f32[136,256]{1,0:T(8,128)S(1)}, f32[136,256]{1,0:T(8,128)S(1)}, u32[]{:S(2)}, u32[]{:S(2)}) collective-permute-start(f32[136,256]{1,0:T(8,128)S(1)} %slice_add_fusion.here_ref), channel_id=1, source_target_pairs={{0,8},{1,9},{2,10},{3,11},{4,12},{5,13},{6,14},{7,15},{8,16},{9,17... | collective-permute-start | bytes 417800 | tf_op jit(solution)/shard_map/ppermute | solution.py:503
  113.8 7.7 %collective-permute-start.31 = (f32[256,256]{1,0:T(8,128)}, f32[256,256]{1,0:T(8,128)S(1)}, u32[]{:S(2)}, u32[]{:S(2)}) collective-permute-start(f32[256,256]{1,0:T(8,128)} %get-tuple-element.86), channel_id=1, source_target_pairs={{0,1},{1,0},{2,3},{3,2},{4,5},{5,4},{6,7},{7,6},{8,9},{9,8},{10,11... | collective-permute-start | bytes 786440 | tf_op jit(solution)/shard_map/ppermute | solution.py:503
  115.9 13.8 %all-to-all-start = ((f32[32,8,128]{2,1,0:T(8,128)}), f32[32,8,128]{2,1,0:T(8,128)S(1)}, u32[]{:S(2)}, u32[]{:S(2)}) async-start(f32[32,8,128]{2,1,0:T(8,128)} %plane_close.1), calls=%async_computation | async-start | bytes 262144 | tf_op jit(solution)/shard_map/all_to_all | solution.py:1176
  130.6 13.3 %collective-permute-start.32 = (f32[512,128]{1,0:T(8,128)S(1)}, f32[512,128]{1,0:T(8,128)S(1)}, u32[]{:S(2)}, u32[]{:S(2)}) collective-permute-start(f32[512,128]{1,0:T(8,128)S(1)} %plane_combine.1), channel_id=1, source_target_pairs={{0,0},{1,16},{2,8},{3,24},{4,4},{5,20},{6,12},{7,28},{8,1},{9,17},... | collective-permute-start | bytes 786440 | tf_op jit(solution)/shard_map/ppermute | solution.py:503
  (13 other events, 167.5 us)

commit v23 on v21

--- a/solution.py
+++ b/solution.py
@@ -1017,10 +1017,10 @@
     note += [value / out_ref.shape[0] for value in known]
     count = sum(value.shape[0] for value in note)
     note = jnp.concatenate(note + [jnp.zeros((24 - count, 1), F32)], axis=0)
-    shape = (24, out_ref.shape[2])
+    shape = (24, out_ref.shape[1])
     row, col = (lax.broadcasted_iota(jnp.int32, shape, i) for i in range(2))
     note = jnp.sum(jnp.where(row == col, jnp.broadcast_to(note, shape), 0.0), axis=0, keepdims=True)
-    out_ref[...] = jnp.broadcast_to(note[None], out_ref.shape)
+    out_ref[...] = jnp.broadcast_to(note, out_ref.shape)
 
 
 def plane_weights(close):
@@ -1046,7 +1046,7 @@
 
 def plane_combine_kernel(close_ref, stack_ref, mine_ref, beside_ref, out_ref):
     rows = beside_ref.shape[1]
-    close = jnp.sum(close_ref[...], axis=0)[0:1, :]
+    close = jnp.sum(close_ref[...], axis=0, keepdims=True)
     e0, e1, e2 = plane_weights(close)
     for i in range(out_ref.shape[0] // rows):
         here = pl.ds(i * rows, rows)
@@ -1166,14 +1166,14 @@
     (note,) = plane_call(
         plane_close_kernel,
         "plane_close",
-        [(Z_ * X_ * Y_ * C_, 8, rows // 2)],
+        [(Z_ * X_ * Y_ * C_, rows // 2)],
         [],
         [
             *(mixed2, moved(mixed2, z_next), pulled2, kept, pulled0, mixed0, delayed0),
             *(open_note, spec, kernels, forward, inverse_last),
         ],
     )
-    close_note = lax.all_to_all(note, ("basin", "tm"), 0, 0, tiled=False)
+    close_note = lax.all_to_all(note, ("basin", "tm"), 0, 0, tiled=True)
     (answer,) = plane_call(
         plane_combine_kernel,
         "plane_combine",

time: 142 us -> 142 us (level)
  blocking collectives: 0 us -> 12.2 us
  starting transfers between devices: 52.3 us -> 46.5 us
  waiting for transfers between devices: 55.8 us -> 50.3 us
    all_to_all x0 -> x1, blocking collectives: none -> 12.2 us  [plane_shards(): close_note = lax.all_to_all(note, ('basin', 'tm'), 0, 0, tiled=True)]
    all_to_all x1 -> x0, waiting for transfers between devices: 8.18 us -> none  [plane_shards(): close_note = lax.all_to_all(note, ('basin', 'tm'), 0, 0, tiled=False)]
    all_to_all x1 -> x0, starting transfers between devices: 5.88 us -> none  [plane_shards(): close_note = lax.all_to_all(note, ('basin', 'tm'), 0, 0, tiled=False)]
    ppermute x33, waiting for transfers between devices: 47.6 us -> 50.3 us  [moved(): return lax.ppermute(value, ('basin', 'tm'), pairs)]
  transfers between devices with their start and end apart: 34 -> 33, of which waited for: 21 -> 21; matrix products, arithmetic and copies ran while one was open for 0% -> 0% of each run, Pallas kernels for 12% -> 11%
where the time goes in v23:
time: 142 us; the launch traced here: 141 us
  waiting for transfers between devices  50.3 us (35%)
  starting transfers between devices  46.5 us (33%)
  Pallas kernels  30.5 us (21%)
  blocking collectives  12.2 us (9%)
    ppermute x33, waiting for transfers between devices, moved(): return lax.ppermute(value, ('basin', 'tm'), pairs)  50.3 us
    ppermute x33, starting transfers between devices, moved(): return lax.ppermute(value, ('basin', 'tm'), pairs)  46.5 us
    all_to_all x1, blocking collectives, plane_shards(): close_note = lax.all_to_all(note, ('basin', 'tm'), 0, 0, tiled=True)  12.2 us
    pallas_call x2, Pallas kernels, plane_couple(): pl.pallas_call(functools.partial(plane_couple_kernel, last), in_specs=[pl...  9.56 us
    pallas_call x6, Pallas kernels, plane_call(): pl.pallas_call(kernel, in_specs=[pl.BlockSpec(memory_space=pltpu.SMEM)] *...  8.16 us
    pallas_call x3, Pallas kernels, plane_rows(): pl.pallas_call(plane_rows_kernel, in_specs=[pl.BlockSpec(memory_space=plt...  3.8 us
    pallas_call x1, Pallas kernels, send(): pl.pallas_call(send_kernel, in_specs=[pl.BlockSpec(memory_space=pltpu.HBM...  3.21 us
  transfers between devices with their start and end apart: 33, of which 21 were waited for; matrix products, arithmetic and copies ran while one was open for 0% of the time, Pallas kernels for 11%

profile of v23, /device:TPU:1, one launch (start us, length us, event | category | flops | bytes accessed | tf_op | source)
XLA Modules:
  0.0 141.4 jit_solution(4364708019040780395)
XLA Ops:
  1.1 4.6 %collective-permute-start.1 = (f32[256,128]{0,1:T(8,128)S(1)}, f32[256,128]{0,1:T(8,128)S(1)}, u32[]{:S(2)}, u32[]{:S(2)}) collective-permute-start(f32[256,128]{0,1:T(8,128)S(1)} %copy.14), channel_id=1, source_target_pairs={{0,0},{1,8},{2,16},{3,24},{4,4},{5,12},{6,20},{7,28},{8,2},{9,10},... | collective-permute-start | bytes 393224 | tf_op jit(solution)/shard_map/ppermute | solution.py:503
  5.7 3.2 %send.1 = f32[136,512]{1,0:T(8,128)} custom-call(s32[32,16,128]{2,1,0:T(8,128)} %inc_ref.2, f32[4096,128]{1,0:T(8,128)} %field_ref.1, s32[1,512]{1,0:T(1,128)} %bitcast.17, s32[1,256]{1,0:T(1,128)} %bitcast.20), custom_call_target="tpu_custom_call" | custom-call | flops 1 | bytes 1 | tf_op jit(solution)/shard_map/send/pallas_call | solution.py:680
  8.9 3.3 %collective-permute-start = (f32[136,512]{1,0:T(8,128)}, f32[136,512]{1,0:T(8,128)S(1)}, u32[]{:S(2)}, u32[]{:S(2)}) collective-permute-start(f32[136,512]{1,0:T(8,128)} %send.1), channel_id=1, source_target_pairs={{0,0},{1,8},{2,16},{3,24},{4,4},{5,12},{6,20},{7,28},{8,2},{9,10},... | collective-permute-start | bytes 835592 | tf_op jit(solution)/shard_map/ppermute | solution.py:503
  14.4 1.7 %collective-permute-done.3 = f32[24,512]{1,0:T(8,128)S(1)} collective-permute-done((f32[24,512]{1,0:T(8,128)S(1)}, f32[24,512]{1,0:T(8,128)S(1)}, u32[]{:S(2)}, u32[]{:S(2)}) %collective-permute-start.3) | collective-permute-done | bytes 49184 | tf_op jit(solution)/shard_map/ppermute | solution.py:503
  17.4 9.0 %collective-permute-done.mine_ref = f32[136,512]{1,0:T(8,128)S(1)} collective-permute-done((f32[136,512]{1,0:T(8,128)}, f32[136,512]{1,0:T(8,128)S(1)}, u32[]{:S(2)}, u32[]{:S(2)}) %collective-permute-start) | collective-permute-done | bytes 278560 | tf_op jit(solution)/shard_map/ppermute | solution.py:503
  27.9 1.6 %spread.1 = (f32[128,256]{1,0:T(8,128)S(1)}, f32[128,256]{1,0:T(8,128)S(1)}, f32[128,256]{1,0:T(8,128)S(1)}, f32[128,256]{1,0:T(8,128)S(1)}) custom-call(s32[6]{0:T(128)S(1)} %broadcast_multiply_fusion.first_ref, f32[136,512]{1,0:T(8,128)S(1)} %collective-permute-done.mine_ref, f32[136,512]{1,0:T(8,128)S(1)} %collective-permute-done.2.other_ref), custom_call_target="tpu_custom_call" | custom-call | flops 1 | bytes 1 | tf_op jit(solution)/shard_map/spread/pallas_call | solution.py:714
  30.8 1.4 %collective-permute-start.7 = (f32[128,256]{1,0:T(8,128)S(1)}, f32[128,256]{1,0:T(8,128)S(1)}, u32[]{:S(2)}, u32[]{:S(2)}) collective-permute-start(f32[128,256]{1,0:T(8,128)S(1)} %get-tuple-element.56), channel_id=1, source_target_pairs={{0,6},{1,7},{2,4},{3,5},{4,2},{5,3},{6,0},{7,1},{8,14},{9,15},{10,... | collective-permute-start | bytes 393224 | tf_op jit(solution)/shard_map/ppermute | solution.py:503
  33.1 1.4 collective-permute-done.5
  34.5 3.7 %collective-permute-done.6 = f32[128,256]{1,0:T(8,128)S(1)} collective-permute-done((f32[128,256]{1,0:T(8,128)S(1)}, f32[128,256]{1,0:T(8,128)S(1)}, u32[]{:S(2)}, u32[]{:S(2)}) %collective-permute-start.6) | collective-permute-done | bytes 131104 | tf_op jit(solution)/shard_map/ppermute | solution.py:503
  41.4 2.0 %collective-permute-start.9 = (f32[24,1024]{1,0:T(8,128)S(1)}, f32[24,1024]{1,0:T(8,128)S(1)}, u32[]{:S(2)}, u32[]{:S(2)}) collective-permute-start(f32[24,1024]{1,0:T(8,128)S(1)} %collective-permute-done.8), channel_id=1, source_target_pairs={{0,1},{1,0},{2,3},{3,2},{4,5},{5,4},{6,7},{7,6},{8,9},{9,8},{10,11... | collective-permute-start | bytes 294920 | tf_op jit(solution)/shard_map/ppermute | solution.py:503
  43.4 4.6 %plane_couple.2.refs_1_ = f32[1024,512]{1,0:T(8,128)S(1)} custom-call(s32[6]{0:T(128)S(1)} %broadcast_multiply_fusion.first_ref, f32[24,2048]{1,0:T(8,128)S(1)} %pad_maximum_fusion.1.refs_0_), custom_call_target="tpu_custom_call" | custom-call | flops 2147483648 | bytes 2000000 | tf_op jit(solution)/shard_map/plane_couple/pallas_call | solution.py:780
  48.1 2.2 %plane_first.1.a_ref.pulled_ref.old_z_ref = f32[128,256]{1,0:T(8,128)S(1)} custom-call(f32[3]{0:T(128)S(1)} %add_convert_fusion.flag_ref, f32[256,256]{1,0:T(8,128)S(1)} %pad_maximum_fusion.here_ref, f32[256,256]{1,0:T(8,128)S(1)} %collective-permute-done.10.pair_ref, f32[256,256]{1,0:T(8,128)S(1)} %collective-permute-done.11.middle_ref, ...), custom_call_target="tpu_custom_call" | custom-call | flops 1 | bytes 1 | tf_op jit(solution)/shard_map/plane_first/pallas_call | solution.py:907
  50.3 2.0 %collective-permute-start.14 = (f32[128,256]{1,0:T(8,128)S(1)}, f32[128,256]{1,0:T(8,128)S(1)}, u32[]{:S(2)}, u32[]{:S(2)}) collective-permute-start(f32[128,256]{1,0:T(8,128)S(1)} %plane_first.1.a_ref.pulled_ref.old_z_ref), channel_id=1, source_target_pairs={{0,6},{1,7},{2,4},{3,5},{4,2},{5,3},{6,0},{7,1},{8,14},{9,15},{10,... | collective-permute-start | bytes 393224 | tf_op jit(solution)/shard_map/ppermute | solution.py:503
  53.0 4.9 %plane_couple.3 = (bf16[1024,512]{1,0:T(8,128)(2,1)S(1)}, bf16[1024,512]{1,0:T(8,128)(2,1)S(1)}) custom-call(s32[6]{0:T(128)S(1)} %broadcast_multiply_fusion.first_ref, f32[24,2048]{1,0:T(8,128)S(1)} %pad_maximum_fusion.2.refs_0_, f32[1024,512]{1,0:T(8,128)S(1)} %plane_couple.2.refs_1_), custom_call_target="tpu_custom_call" | custom-call | flops 2147483648 | bytes 2000000 | tf_op jit(solution)/shard_map/plane_couple/pallas_call | solution.py:780
  58.0 1.5 %collective-permute-done.13.c_ref = f32[128,256]{1,0:T(8,128)S(1)} collective-permute-done((f32[128,256]{1,0:T(8,128)S(1)}, f32[128,256]{1,0:T(8,128)S(1)}, u32[]{:S(2)}, u32[]{:S(2)}) %collective-permute-start.13) | collective-permute-done | bytes 131104 | tf_op jit(solution)/shard_map/ppermute | solution.py:503
  62.6 2.8 %collective-permute-start.16 = (f32[128,256]{1,0:T(8,128)S(1)}, f32[128,256]{1,0:T(8,128)S(1)}, u32[]{:S(2)}, u32[]{:S(2)}) collective-permute-start(f32[128,256]{1,0:T(8,128)S(1)} %add.61.here_ref.old_s_ref), channel_id=1, source_target_pairs={{0,8},{1,9},{2,10},{3,11},{4,12},{5,13},{6,14},{7,15},{8,0},{9,1},... | collective-permute-start | bytes 393224 | tf_op jit(solution)/shard_map/ppermute | solution.py:503
  65.4 3.3 %collective-permute-done.16.pair_ref = f32[128,256]{1,0:T(8,128)S(1)} collective-permute-done((f32[128,256]{1,0:T(8,128)S(1)}, f32[128,256]{1,0:T(8,128)S(1)}, u32[]{:S(2)}, u32[]{:S(2)}) %collective-permute-start.16) | collective-permute-done | bytes 131104 | tf_op jit(solution)/shard_map/ppermute | solution.py:503
  68.7 1.8 %plane_open.1 = (f32[136,256]{1,0:T(8,128)S(1)}, f32[256,256]{1,0:T(8,128)S(1)}) custom-call(f32[3]{0:T(128)S(1)} %add_convert_fusion.flag_ref, f32[128,256]{1,0:T(8,128)S(1)} %add.61.here_ref.old_s_ref, f32[128,256]{1,0:T(8,128)S(1)} %collective-permute-done.16.pair_ref, f32[128,256]{1,0:T(8,128)S(1)} %collective-permute-done.17.middle_ref, ...), custom_call_target="tpu_custom_call" | custom-call | flops 1 | bytes 1 | tf_op jit(solution)/shard_map/plane_open/pallas_call | solution.py:907
  70.5 1.9 %collective-permute-start.20 = (f32[136,256]{1,0:T(8,128)S(1)}, f32[136,256]{1,0:T(8,128)S(1)}, u32[]{:S(2)}, u32[]{:S(2)}) collective-permute-start(f32[136,256]{1,0:T(8,128)S(1)} %get-tuple-element.70.a_ref.pulled_ref), channel_id=1, source_target_pairs={{0,6},{1,7},{2,4},{3,5},{4,2},{5,3},{6,0},{7,1},{8,14},{9,15},{10,... | collective-permute-start | bytes 417800 | tf_op jit(solution)/shard_map/ppermute | solution.py:503
  75.5 4.1 %collective-permute-done.19.c_ref = f32[136,256]{1,0:T(8,128)S(1)} collective-permute-done((f32[136,256]{1,0:T(8,128)S(1)}, f32[136,256]{1,0:T(8,128)S(1)}, u32[]{:S(2)}, u32[]{:S(2)}) %collective-permute-start.19) | collective-permute-done | bytes 139296 | tf_op jit(solution)/shard_map/ppermute | solution.py:503
  83.4 3.3 %collective-permute-start.22 = (f32[136,256]{1,0:T(8,128)S(1)}, f32[136,256]{1,0:T(8,128)S(1)}, u32[]{:S(2)}, u32[]{:S(2)}) collective-permute-start(f32[136,256]{1,0:T(8,128)S(1)} %slice_add_fusion.1.here_ref), channel_id=1, source_target_pairs={{0,8},{1,9},{2,10},{3,11},{4,12},{5,13},{6,14},{7,15},{8,0},{9,1},... | collective-permute-start | bytes 417800 | tf_op jit(solution)/shard_map/ppermute | solution.py:503
  86.7 1.5 %collective-permute-start.24 = (f32[8,256]{1,0:T(8,128)S(1)}, f32[8,256]{1,0:T(8,128)S(1)}, u32[]{:S(2)}, u32[]{:S(2)}) collective-permute-start(f32[8,256]{1,0:T(8,128)S(1)} %slice.31), channel_id=1, source_target_pairs={{0,24},{1,25},{2,26},{3,27},{4,28},{5,29},{6,30},{7,31},{8,16},{9,... | collective-permute-start | bytes 24584 | tf_op jit(solution)/shard_map/ppermute | solution.py:503
  88.3 1.9 %collective-permute-done.22.pair_ref = f32[136,256]{1,0:T(8,128)S(1)} collective-permute-done((f32[136,256]{1,0:T(8,128)S(1)}, f32[136,256]{1,0:T(8,128)S(1)}, u32[]{:S(2)}, u32[]{:S(2)}) %collective-permute-start.22) | collective-permute-done | bytes 139296 | tf_op jit(solution)/shard_map/ppermute | solution.py:503
  93.0 1.5 %collective-permute-start.28 = (f32[136,256]{1,0:T(8,128)S(1)}, f32[136,256]{1,0:T(8,128)S(1)}, u32[]{:S(2)}, u32[]{:S(2)}) collective-permute-start(f32[136,256]{1,0:T(8,128)S(1)} %get-tuple-element.75.a_ref.pulled_ref), channel_id=1, source_target_pairs={{0,6},{1,7},{2,4},{3,5},{4,2},{5,3},{6,0},{7,1},{8,14},{9,15},{10,... | collective-permute-start | bytes 417800 | tf_op jit(solution)/shard_map/ppermute | solution.py:503
  97.9 1.8 %collective-permute-done.27.c_ref = f32[136,256]{1,0:T(8,128)S(1)} collective-permute-done((f32[136,256]{1,0:T(8,128)S(1)}, f32[136,256]{1,0:T(8,128)S(1)}, u32[]{:S(2)}, u32[]{:S(2)}) %collective-permute-start.27) | collective-permute-done | bytes 139296 | tf_op jit(solution)/shard_map/ppermute | solution.py:503
  100.5 3.4 %collective-permute-start.29 = (f32[392,256]{1,0:T(8,128)S(1)}, f32[392,256]{1,0:T(8,128)S(1)}, u32[]{:S(2)}, u32[]{:S(2)}) collective-permute-start(f32[392,256]{1,0:T(8,128)S(1)} %get-tuple-element.79), channel_id=1, source_target_pairs={{0,1},{1,0},{2,3},{3,2},{4,5},{5,4},{6,7},{7,6},{8,9},{9,8},{10,11... | collective-permute-start | bytes 1204232 | tf_op jit(solution)/shard_map/ppermute | solution.py:503
  107.1 2.6 %collective-permute-start.30 = (f32[136,256]{1,0:T(8,128)S(1)}, f32[136,256]{1,0:T(8,128)S(1)}, u32[]{:S(2)}, u32[]{:S(2)}) collective-permute-start(f32[136,256]{1,0:T(8,128)S(1)} %slice_add_fusion.here_ref), channel_id=1, source_target_pairs={{0,8},{1,9},{2,10},{3,11},{4,12},{5,13},{6,14},{7,15},{8,16},{9,17... | collective-permute-start | bytes 417800 | tf_op jit(solution)/shard_map/ppermute | solution.py:503
  109.7 2.9 %collective-permute-done.30.before_ref = f32[136,256]{1,0:T(8,128)S(1)} collective-permute-done((f32[136,256]{1,0:T(8,128)S(1)}, f32[136,256]{1,0:T(8,128)S(1)}, u32[]{:S(2)}, u32[]{:S(2)}) %collective-permute-start.30) | collective-permute-done | bytes 139296 | tf_op jit(solution)/shard_map/ppermute | solution.py:503
  113.4 12.2 %all_to_all.11 = f32[32,1,128]{2,1,0:T(1,128)S(1)} all-to-all(f32[32,1,128]{2,1,0:T(1,128)S(1)} %bitcast.15), channel_id=1, replica_groups=mesh['basin'=8,'tm'=4] {'basin','tm'}, dimensions={0} | all-to-all | bytes 32768 | tf_op jit(solution)/shard_map/all_to_all | solution.py:1176
  126.4 2.7 %collective-permute-start.32 = (f32[512,128]{1,0:T(8,128)S(1)}, f32[512,128]{1,0:T(8,128)S(1)}, u32[]{:S(2)}, u32[]{:S(2)}) collective-permute-start(f32[512,128]{1,0:T(8,128)S(1)} %plane_combine.1), channel_id=1, source_target_pairs={{0,0},{1,16},{2,8},{3,24},{4,4},{5,20},{6,12},{7,28},{8,1},{9,17},... | collective-permute-start | bytes 786440 | tf_op jit(solution)/shard_map/ppermute | solution.py:503
  129.2 10.6 %collective-permute-done.32.rows_ref = f32[512,128]{1,0:T(8,128)S(1)} collective-permute-done((f32[512,128]{1,0:T(8,128)S(1)}, f32[512,128]{1,0:T(8,128)S(1)}, u32[]{:S(2)}, u32[]{:S(2)}) %collective-permute-start.32) | collective-permute-done | bytes 262176 | tf_op jit(solution)/shard_map/ppermute | solution.py:503
  139.8 1.6 %plane_finish.1 = f32[4096,128]{1,0:T(8,128)} custom-call(f32[512,128]{1,0:T(8,128)S(1)} %collective-permute-done.32.rows_ref, s32[32,16,128]{2,1,0:T(8,128)S(1)} %copy-done.2, f32[4096,128]{1,0:T(8,128)S(1)} %copy-done.1), custom_call_target="tpu_custom_call" | custom-call | tf_op jit(solution)/shard_map/plane_finish/pallas_call | solution.py:1073
  (90 shorter events, 33.7 us)
Async XLA Ops:
  1.1 11.8 %collective-permute-start.1 = (f32[256,128]{0,1:T(8,128)S(1)}, f32[256,128]{0,1:T(8,128)S(1)}, u32[]{:S(2)}, u32[]{:S(2)}) collective-permute-start(f32[256,128]{0,1:T(8,128)S(1)} %copy.14), channel_id=1, source_target_pairs={{0,0},{1,8},{2,16},{3,24},{4,4},{5,12},{6,20},{7,28},{8,2},{9,10},... | collective-permute-start | bytes 393224 | tf_op jit(solution)/shard_map/ppermute | solution.py:503
  8.9 17.5 %collective-permute-start = (f32[136,512]{1,0:T(8,128)}, f32[136,512]{1,0:T(8,128)S(1)}, u32[]{:S(2)}, u32[]{:S(2)}) collective-permute-start(f32[136,512]{1,0:T(8,128)} %send.1), channel_id=1, source_target_pairs={{0,0},{1,8},{2,16},{3,24},{4,4},{5,12},{6,20},{7,28},{8,2},{9,10},... | collective-permute-start | bytes 835592 | tf_op jit(solution)/shard_map/ppermute | solution.py:503
  13.1 3.0 %collective-permute-start.3 = (f32[24,512]{1,0:T(8,128)S(1)}, f32[24,512]{1,0:T(8,128)S(1)}, u32[]{:S(2)}, u32[]{:S(2)}) collective-permute-start(f32[24,512]{1,0:T(8,128)S(1)} %describe.1), channel_id=1, source_target_pairs={{0,4},{1,5},{2,6},{3,7},{4,0},{5,1},{6,2},{7,3},{8,12},{9,13},{10,... | collective-permute-start | bytes 147464 | tf_op jit(solution)/shard_map/ppermute | solution.py:503
  16.1 11.0 %collective-permute-start.4 = (f32[24,1024]{1,0:T(8,128)S(1)}, f32[24,1024]{1,0:T(8,128)S(1)}, u32[]{:S(2)}, u32[]{:S(2)}) collective-permute-start(f32[24,1024]{1,0:T(8,128)S(1)} %pad_maximum_fusion.3), channel_id=1, source_target_pairs={{0,8},{1,9},{2,10},{3,11},{4,12},{5,13},{6,14},{7,15},{8,0},{9,1},... | collective-permute-start | bytes 294920 | tf_op jit(solution)/shard_map/ppermute | solution.py:503
  29.5 5.0 %collective-permute-start.5 = (f32[128,256]{1,0:T(8,128)S(1)}, f32[128,256]{1,0:T(8,128)S(1)}, u32[]{:S(2)}, u32[]{:S(2)}) collective-permute-start(f32[128,256]{1,0:T(8,128)S(1)} %get-tuple-element.54), channel_id=1, source_target_pairs={{0,4},{1,5},{2,6},{3,7},{4,0},{5,1},{6,2},{7,3},{8,12},{9,13},{10,... | collective-permute-start | bytes 393224 | tf_op jit(solution)/shard_map/ppermute | solution.py:503
  30.8 7.4 %collective-permute-start.6 = (f32[128,256]{1,0:T(8,128)S(1)}, f32[128,256]{1,0:T(8,128)S(1)}, u32[]{:S(2)}, u32[]{:S(2)}) collective-permute-start(f32[128,256]{1,0:T(8,128)S(1)} %get-tuple-element.55), channel_id=1, source_target_pairs={{0,2},{1,3},{2,0},{3,1},{4,6},{5,7},{6,4},{7,5},{8,10},{9,11},{10,... | collective-permute-start | bytes 393224 | tf_op jit(solution)/shard_map/ppermute | solution.py:503
  30.8 7.4 %collective-permute-start.7 = (f32[128,256]{1,0:T(8,128)S(1)}, f32[128,256]{1,0:T(8,128)S(1)}, u32[]{:S(2)}, u32[]{:S(2)}) collective-permute-start(f32[128,256]{1,0:T(8,128)S(1)} %get-tuple-element.56), channel_id=1, source_target_pairs={{0,6},{1,7},{2,4},{3,5},{4,2},{5,3},{6,0},{7,1},{8,14},{9,15},{10,... | collective-permute-start | bytes 393224 | tf_op jit(solution)/shard_map/ppermute | solution.py:503
  32.2 7.1 %collective-permute-start.8 = (f32[24,1024]{1,0:T(8,128)S(1)}, f32[24,1024]{1,0:T(8,128)S(1)}, u32[]{:S(2)}, u32[]{:S(2)}) collective-permute-start(f32[24,1024]{1,0:T(8,128)S(1)} %slice_select_fusion), channel_id=1, source_target_pairs={{0,16},{1,17},{2,18},{3,19},{4,20},{5,21},{6,22},{7,23},{8,24},{9,... | collective-permute-start | bytes 294920 | tf_op jit(solution)/shard_map/ppermute | solution.py:503
  39.4 8.7 %collective-permute-start.11 = (f32[256,256]{1,0:T(8,128)S(1)}, f32[256,256]{1,0:T(8,128)S(1)}, u32[]{:S(2)}, u32[]{:S(2)}) collective-permute-start(f32[256,256]{1,0:T(8,128)S(1)} %pad_maximum_fusion.here_ref), channel_id=1, source_target_pairs={{8,16},{9,17},{10,18},{11,19},{12,20},{13,21},{14,22},{15,23},{16,... | collective-permute-start | bytes 786440 | tf_op jit(solution)/shard_map/ppermute | solution.py:503
  40.2 7.9 %collective-permute-start.10 = (f32[256,256]{1,0:T(8,128)S(1)}, f32[256,256]{1,0:T(8,128)S(1)}, u32[]{:S(2)}, u32[]{:S(2)}) collective-permute-start(f32[256,256]{1,0:T(8,128)S(1)} %pad_maximum_fusion.here_ref), channel_id=1, source_target_pairs={{0,8},{1,9},{2,10},{3,11},{4,12},{5,13},{6,14},{7,15},{8,0},{9,1},... | collective-permute-start | bytes 786440 | tf_op jit(solution)/shard_map/ppermute | solution.py:503
  41.4 6.7 %collective-permute-start.9 = (f32[24,1024]{1,0:T(8,128)S(1)}, f32[24,1024]{1,0:T(8,128)S(1)}, u32[]{:S(2)}, u32[]{:S(2)}) collective-permute-start(f32[24,1024]{1,0:T(8,128)S(1)} %collective-permute-done.8), channel_id=1, source_target_pairs={{0,1},{1,0},{2,3},{3,2},{4,5},{5,4},{6,7},{7,6},{8,9},{9,8},{10,11... | collective-permute-start | bytes 294920 | tf_op jit(solution)/shard_map/ppermute | solution.py:503
  50.3 7.7 %collective-permute-start.14 = (f32[128,256]{1,0:T(8,128)S(1)}, f32[128,256]{1,0:T(8,128)S(1)}, u32[]{:S(2)}, u32[]{:S(2)}) collective-permute-start(f32[128,256]{1,0:T(8,128)S(1)} %plane_first.1.a_ref.pulled_ref.old_z_ref), channel_id=1, source_target_pairs={{0,6},{1,7},{2,4},{3,5},{4,2},{5,3},{6,0},{7,1},{8,14},{9,15},{10,... | collective-permute-start | bytes 393224 | tf_op jit(solution)/shard_map/ppermute | solution.py:503
  52.3 7.2 %collective-permute-start.13 = (f32[128,256]{1,0:T(8,128)S(1)}, f32[128,256]{1,0:T(8,128)S(1)}, u32[]{:S(2)}, u32[]{:S(2)}) collective-permute-start(f32[128,256]{1,0:T(8,128)S(1)} %plane_first.1.a_ref.pulled_ref.old_z_ref), channel_id=1, source_target_pairs={{0,2},{1,3},{2,0},{3,1},{4,6},{5,7},{6,4},{7,5},{8,10},{9,11},{10,... | collective-permute-start | bytes 393224 | tf_op jit(solution)/shard_map/ppermute | solution.py:503
  52.7 6.8 %collective-permute-start.12 = (f32[128,256]{1,0:T(8,128)S(1)}, f32[128,256]{1,0:T(8,128)S(1)}, u32[]{:S(2)}, u32[]{:S(2)}) collective-permute-start(f32[128,256]{1,0:T(8,128)S(1)} %plane_first.1.a_ref.pulled_ref.old_z_ref), channel_id=1, source_target_pairs={{0,4},{1,5},{2,6},{3,7},{4,0},{5,1},{6,2},{7,3},{8,12},{9,13},{10,... | collective-permute-start | bytes 393224 | tf_op jit(solution)/shard_map/ppermute | solution.py:503
  60.1 1.8 %collective-permute-start.15 = (f32[128,256]{1,0:T(8,128)S(1)}, f32[128,256]{1,0:T(8,128)S(1)}, u32[]{:S(2)}, u32[]{:S(2)}) collective-permute-start(f32[128,256]{1,0:T(8,128)S(1)} %get-tuple-element.69), channel_id=1, source_target_pairs={{0,1},{1,0},{2,3},{3,2},{4,5},{5,4},{6,7},{7,6},{8,9},{9,8},{10,11... | collective-permute-start | bytes 393224 | tf_op jit(solution)/shard_map/ppermute | solution.py:503
  62.0 3.5 %collective-permute-start.17 = (f32[128,256]{1,0:T(8,128)S(1)}, f32[128,256]{1,0:T(8,128)S(1)}, u32[]{:S(2)}, u32[]{:S(2)}) collective-permute-start(f32[128,256]{1,0:T(8,128)S(1)} %add.61.here_ref.old_s_ref), channel_id=1, source_target_pairs={{8,16},{9,17},{10,18},{11,19},{12,20},{13,21},{14,22},{15,23},{16,... | collective-permute-start | bytes 393224 | tf_op jit(solution)/shard_map/ppermute | solution.py:503
  62.6 6.1 %collective-permute-start.16 = (f32[128,256]{1,0:T(8,128)S(1)}, f32[128,256]{1,0:T(8,128)S(1)}, u32[]{:S(2)}, u32[]{:S(2)}) collective-permute-start(f32[128,256]{1,0:T(8,128)S(1)} %add.61.here_ref.old_s_ref), channel_id=1, source_target_pairs={{0,8},{1,9},{2,10},{3,11},{4,12},{5,13},{6,14},{7,15},{8,0},{9,1},... | collective-permute-start | bytes 393224 | tf_op jit(solution)/shard_map/ppermute | solution.py:503
  70.5 4.9 %collective-permute-start.20 = (f32[136,256]{1,0:T(8,128)S(1)}, f32[136,256]{1,0:T(8,128)S(1)}, u32[]{:S(2)}, u32[]{:S(2)}) collective-permute-start(f32[136,256]{1,0:T(8,128)S(1)} %get-tuple-element.70.a_ref.pulled_ref), channel_id=1, source_target_pairs={{0,6},{1,7},{2,4},{3,5},{4,2},{5,3},{6,0},{7,1},{8,14},{9,15},{10,... | collective-permute-start | bytes 417800 | tf_op jit(solution)/shard_map/ppermute | solution.py:503
  72.4 7.1 %collective-permute-start.19 = (f32[136,256]{1,0:T(8,128)S(1)}, f32[136,256]{1,0:T(8,128)S(1)}, u32[]{:S(2)}, u32[]{:S(2)}) collective-permute-start(f32[136,256]{1,0:T(8,128)S(1)} %get-tuple-element.70.a_ref.pulled_ref), channel_id=1, source_target_pairs={{0,2},{1,3},{2,0},{3,1},{4,6},{5,7},{6,4},{7,5},{8,10},{9,11},{10,... | collective-permute-start | bytes 417800 | tf_op jit(solution)/shard_map/ppermute | solution.py:503
  73.0 6.6 %collective-permute-start.18 = (f32[136,256]{1,0:T(8,128)S(1)}, f32[136,256]{1,0:T(8,128)S(1)}, u32[]{:S(2)}, u32[]{:S(2)}) collective-permute-start(f32[136,256]{1,0:T(8,128)S(1)} %get-tuple-element.70.a_ref.pulled_ref), channel_id=1, source_target_pairs={{0,4},{1,5},{2,6},{3,7},{4,0},{5,1},{6,2},{7,3},{8,12},{9,13},{10,... | collective-permute-start | bytes 417800 | tf_op jit(solution)/shard_map/ppermute | solution.py:503
  80.1 2.5 %collective-permute-start.21 = (f32[392,256]{1,0:T(8,128)S(1)}, f32[392,256]{1,0:T(8,128)S(1)}, u32[]{:S(2)}, u32[]{:S(2)}) collective-permute-start(f32[392,256]{1,0:T(8,128)S(1)} %get-tuple-element.73), channel_id=1, source_target_pairs={{0,1},{1,0},{2,3},{3,2},{4,5},{5,4},{6,7},{7,6},{8,9},{9,8},{10,11... | collective-permute-start | bytes 1204232 | tf_op jit(solution)/shard_map/ppermute | solution.py:503
  82.6 5.7 %collective-permute-start.25 = (f32[136,256]{1,0:T(8,128)S(1)}, f32[136,256]{1,0:T(8,128)S(1)}, u32[]{:S(2)}, u32[]{:S(2)}) collective-permute-start(f32[136,256]{1,0:T(8,128)S(1)} %slice_add_fusion.1.here_ref), channel_id=1, source_target_pairs={{8,16},{9,17},{10,18},{11,19},{12,20},{13,21},{14,22},{15,23},{16,... | collective-permute-start | bytes 417800 | tf_op jit(solution)/shard_map/ppermute | solution.py:503
  83.4 6.7 %collective-permute-start.22 = (f32[136,256]{1,0:T(8,128)S(1)}, f32[136,256]{1,0:T(8,128)S(1)}, u32[]{:S(2)}, u32[]{:S(2)}) collective-permute-start(f32[136,256]{1,0:T(8,128)S(1)} %slice_add_fusion.1.here_ref), channel_id=1, source_target_pairs={{0,8},{1,9},{2,10},{3,11},{4,12},{5,13},{6,14},{7,15},{8,0},{9,1},... | collective-permute-start | bytes 417800 | tf_op jit(solution)/shard_map/ppermute | solution.py:503
  86.7 4.7 %collective-permute-start.24 = (f32[8,256]{1,0:T(8,128)S(1)}, f32[8,256]{1,0:T(8,128)S(1)}, u32[]{:S(2)}, u32[]{:S(2)}) collective-permute-start(f32[8,256]{1,0:T(8,128)S(1)} %slice.31), channel_id=1, source_target_pairs={{0,24},{1,25},{2,26},{3,27},{4,28},{5,29},{6,30},{7,31},{8,16},{9,... | collective-permute-start | bytes 24584 | tf_op jit(solution)/shard_map/ppermute | solution.py:503
  88.3 3.4 %collective-permute-start.23 = (f32[8,256]{1,0:T(8,128)S(1)}, f32[8,256]{1,0:T(8,128)S(1)}, u32[]{:S(2)}, u32[]{:S(2)}) collective-permute-start(f32[8,256]{1,0:T(8,128)S(1)} %slice.31), channel_id=1, source_target_pairs={{0,16},{1,17},{2,18},{3,19},{4,20},{5,21},{6,22},{7,23},{8,24},{9,... | collective-permute-start | bytes 24584 | tf_op jit(solution)/shard_map/ppermute | solution.py:503
  93.0 5.0 %collective-permute-start.28 = (f32[136,256]{1,0:T(8,128)S(1)}, f32[136,256]{1,0:T(8,128)S(1)}, u32[]{:S(2)}, u32[]{:S(2)}) collective-permute-start(f32[136,256]{1,0:T(8,128)S(1)} %get-tuple-element.75.a_ref.pulled_ref), channel_id=1, source_target_pairs={{0,6},{1,7},{2,4},{3,5},{4,2},{5,3},{6,0},{7,1},{8,14},{9,15},{10,... | collective-permute-start | bytes 417800 | tf_op jit(solution)/shard_map/ppermute | solution.py:503
  94.5 5.3 %collective-permute-start.27 = (f32[136,256]{1,0:T(8,128)S(1)}, f32[136,256]{1,0:T(8,128)S(1)}, u32[]{:S(2)}, u32[]{:S(2)}) collective-permute-start(f32[136,256]{1,0:T(8,128)S(1)} %get-tuple-element.75.a_ref.pulled_ref), channel_id=1, source_target_pairs={{0,2},{1,3},{2,0},{3,1},{4,6},{5,7},{6,4},{7,5},{8,10},{9,11},{10,... | collective-permute-start | bytes 417800 | tf_op jit(solution)/shard_map/ppermute | solution.py:503
  95.4 4.6 %collective-permute-start.26 = (f32[136,256]{1,0:T(8,128)S(1)}, f32[136,256]{1,0:T(8,128)S(1)}, u32[]{:S(2)}, u32[]{:S(2)}) collective-permute-start(f32[136,256]{1,0:T(8,128)S(1)} %get-tuple-element.75.a_ref.pulled_ref), channel_id=1, source_target_pairs={{0,4},{1,5},{2,6},{3,7},{4,0},{5,1},{6,2},{7,3},{8,12},{9,13},{10,... | collective-permute-start | bytes 417800 | tf_op jit(solution)/shard_map/ppermute | solution.py:503
  100.5 4.8 %collective-permute-start.29 = (f32[392,256]{1,0:T(8,128)S(1)}, f32[392,256]{1,0:T(8,128)S(1)}, u32[]{:S(2)}, u32[]{:S(2)}) collective-permute-start(f32[392,256]{1,0:T(8,128)S(1)} %get-tuple-element.79), channel_id=1, source_target_pairs={{0,1},{1,0},{2,3},{3,2},{4,5},{5,4},{6,7},{7,6},{8,9},{9,8},{10,11... | collective-permute-start | bytes 1204232 | tf_op jit(solution)/shard_map/ppermute | solution.py:503
  106.6 19.0 %collective-permute-start.31 = (f32[256,256]{1,0:T(8,128)S(1)}, f32[256,256]{1,0:T(8,128)S(1)}, u32[]{:S(2)}, u32[]{:S(2)}) collective-permute-start(f32[256,256]{1,0:T(8,128)S(1)} %get-tuple-element.86), channel_id=1, source_target_pairs={{0,1},{1,0},{2,3},{3,2},{4,5},{5,4},{6,7},{7,6},{8,9},{9,8},{10,11... | collective-permute-start | bytes 786440 | tf_op jit(solution)/shard_map/ppermute | solution.py:503
  107.1 5.5 %collective-permute-start.30 = (f32[136,256]{1,0:T(8,128)S(1)}, f32[136,256]{1,0:T(8,128)S(1)}, u32[]{:S(2)}, u32[]{:S(2)}) collective-permute-start(f32[136,256]{1,0:T(8,128)S(1)} %slice_add_fusion.here_ref), channel_id=1, source_target_pairs={{0,8},{1,9},{2,10},{3,11},{4,12},{5,13},{6,14},{7,15},{8,16},{9,17... | collective-permute-start | bytes 417800 | tf_op jit(solution)/shard_map/ppermute | solution.py:503
  126.4 13.3 %collective-permute-start.32 = (f32[512,128]{1,0:T(8,128)S(1)}, f32[512,128]{1,0:T(8,128)S(1)}, u32[]{:S(2)}, u32[]{:S(2)}) collective-permute-start(f32[512,128]{1,0:T(8,128)S(1)} %plane_combine.1), channel_id=1, source_target_pairs={{0,0},{1,16},{2,8},{3,24},{4,4},{5,20},{6,12},{7,28},{8,1},{9,17},... | collective-permute-start | bytes 786440 | tf_op jit(solution)/shard_map/ppermute | solution.py:503
  (11 other events, 159.0 us)

commit v24 on v23

--- a/solution.py
+++ b/solution.py
@@ -1104,18 +1104,23 @@
     near, seen = lax.optimization_barrier((near, seen))
     meta = describe(near, row_gauge)
     meta = jnp.concatenate([meta, moved(meta, over_x)], axis=1)
-    meta = jnp.concatenate([meta, moved(meta, z_pair)], axis=1)
+    half = meta.shape[1] // 2
+    share = jnp.where(c == 0, meta[:, :half], meta[:, half:])
+    close = moved(share, z_pair)
     parcel, seen = lax.optimization_barrier((parcel, seen))
     parcels = [parcel, moved(parcel, over_core)]
     spec = plane_spectrum(parcel[hours:], kernels, short3, rows)
-    parcels[1], seen, meta, spec = lax.optimization_barrier((parcels[1], seen, meta, spec))
-    half = meta.shape[1] // 2
-    far = moved(jnp.where(c == 0, meta[:, :half], meta[:, half:]), z_two)
+    parcels[1], seen, close, spec = lax.optimization_barrier((parcels[1], seen, close, spec))
+    far = moved(jnp.concatenate([share, close], axis=1), z_two)
     dense = spread(first, parcels, rows)
     metas = [value[hours:] for value in parcels]
     sums = dense[0] + sum(moved(value, where) for value, where in zip(dense[1:], SQUARE))
     sums, far = lax.optimization_barrier((sums, far))
-    around = [meta, jnp.concatenate([far, moved(far, over_core)], axis=1)]
+    held = jnp.concatenate([close, far], axis=1)
+    around = [
+        jnp.concatenate([meta, held[:, : 2 * half]], axis=1),
+        jnp.concatenate([held[:, 2 * half :], moved(held, over_core)], axis=1),
+    ]
     sums = jnp.concatenate([sums, jnp.transpose(seen)], axis=0)
     sums = [sums, moved(sums, z_pair), moved(sums, z_middle)]
     coupled = plane_couple(first, around[0], rows)

time: 142 us -> 145 us (1.021)
  waiting for transfers between devices: 50.3 us -> 52.4 us
  starting transfers between devices: 46.5 us -> 48 us
    ppermute x33, waiting for transfers between devices: 50.3 us -> 52.4 us  [moved(): return lax.ppermute(value, ('basin', 'tm'), pairs)]
    ppermute x33, starting transfers between devices: 46.5 us -> 48 us  [moved(): return lax.ppermute(value, ('basin', 'tm'), pairs)]
  transfers between devices with their start and end apart: 33 -> 33, of which waited for: 21 -> 18; matrix products, arithmetic and copies ran while one was open for 0% -> 0% of each run, Pallas kernels for 11% -> 10%
where the time goes in v24:
time: 145 us
  waiting for transfers between devices  52.4 us (36%)
  starting transfers between devices  48 us (33%)
  Pallas kernels  30.6 us (21%)
  blocking collectives  12.2 us (8%)
    ppermute x33, waiting for transfers between devices, moved(): return lax.ppermute(value, ('basin', 'tm'), pairs)  52.4 us
    ppermute x33, starting transfers between devices, moved(): return lax.ppermute(value, ('basin', 'tm'), pairs)  48 us
    all_to_all x1, blocking collectives, plane_shards(): close_note = lax.all_to_all(note, ('basin', 'tm'), 0, 0, tiled=True)  12.2 us
    pallas_call x2, Pallas kernels, plane_couple(): pl.pallas_call(functools.partial(plane_couple_kernel, last), in_specs=[pl...  9.59 us
    pallas_call x6, Pallas kernels, plane_call(): pl.pallas_call(kernel, in_specs=[pl.BlockSpec(memory_space=pltpu.SMEM)] *...  8.22 us
    pallas_call x3, Pallas kernels, plane_rows(): pl.pallas_call(plane_rows_kernel, in_specs=[pl.BlockSpec(memory_space=plt...  3.8 us
    pallas_call x1, Pallas kernels, send(): pl.pallas_call(send_kernel, in_specs=[pl.BlockSpec(memory_space=pltpu.HBM...  3.21 us
  transfers between devices with their start and end apart: 33, of which 18 were waited for; matrix products, arithmetic and copies ran while one was open for 0% of the time, Pallas kernels for 10%

profile of v24, /device:TPU:1, one launch (start us, length us, event | category | flops | bytes accessed | tf_op | source)
XLA Modules:
  0.0 145.0 jit_solution(4930475678513196751)
XLA Ops:
  1.1 4.6 %collective-permute-start.1 = (f32[256,128]{0,1:T(8,128)S(1)}, f32[256,128]{0,1:T(8,128)S(1)}, u32[]{:S(2)}, u32[]{:S(2)}) collective-permute-start(f32[256,128]{0,1:T(8,128)S(1)} %copy.14), channel_id=1, source_target_pairs={{0,0},{1,8},{2,16},{3,24},{4,4},{5,12},{6,20},{7,28},{8,2},{9,10},... | collective-permute-start | bytes 393224 | tf_op jit(solution)/shard_map/ppermute | solution.py:503
  5.7 3.2 %send.1 = f32[136,512]{1,0:T(8,128)} custom-call(s32[32,16,128]{2,1,0:T(8,128)} %inc_ref.2, f32[4096,128]{1,0:T(8,128)} %field_ref.1, s32[1,512]{1,0:T(1,128)} %bitcast.17, s32[1,256]{1,0:T(1,128)} %bitcast.20), custom_call_target="tpu_custom_call" | custom-call | flops 1 | bytes 1 | tf_op jit(solution)/shard_map/send/pallas_call | solution.py:680
  8.9 3.3 %collective-permute-start = (f32[136,512]{1,0:T(8,128)}, f32[136,512]{1,0:T(8,128)S(1)}, u32[]{:S(2)}, u32[]{:S(2)}) collective-permute-start(f32[136,512]{1,0:T(8,128)} %send.1), channel_id=1, source_target_pairs={{0,0},{1,8},{2,16},{3,24},{4,4},{5,12},{6,20},{7,28},{8,2},{9,10},... | collective-permute-start | bytes 835592 | tf_op jit(solution)/shard_map/ppermute | solution.py:503
  14.4 12.0 %collective-permute-done.mine_ref = f32[136,512]{1,0:T(8,128)S(1)} collective-permute-done((f32[136,512]{1,0:T(8,128)}, f32[136,512]{1,0:T(8,128)S(1)}, u32[]{:S(2)}, u32[]{:S(2)}) %collective-permute-start) | collective-permute-done | bytes 278560 | tf_op jit(solution)/shard_map/ppermute | solution.py:503
  27.2 2.2 %collective-permute-done.4 = f32[24,512]{1,0:T(8,128)S(1)} collective-permute-done((f32[24,512]{1,0:T(8,128)S(1)}, f32[24,512]{1,0:T(8,128)S(1)}, u32[]{:S(2)}, u32[]{:S(2)}) %collective-permute-start.4) | collective-permute-done | bytes 49184 | tf_op jit(solution)/shard_map/ppermute | solution.py:503
  29.4 1.6 %spread.1 = (f32[128,256]{1,0:T(8,128)S(1)}, f32[128,256]{1,0:T(8,128)S(1)}, f32[128,256]{1,0:T(8,128)S(1)}, f32[128,256]{1,0:T(8,128)S(1)}) custom-call(s32[6]{0:T(128)S(1)} %broadcast_multiply_fusion.first_ref, f32[136,512]{1,0:T(8,128)S(1)} %collective-permute-done.mine_ref, f32[136,512]{1,0:T(8,128)S(1)} %collective-permute-done.2.other_ref), custom_call_target="tpu_custom_call" | custom-call | flops 1 | bytes 1 | tf_op jit(solution)/shard_map/spread/pallas_call | solution.py:714
  33.6 1.7 %collective-permute-start.8 = (f32[24,1024]{1,0:T(8,128)S(1)}, f32[24,1024]{1,0:T(8,128)S(1)}, u32[]{:S(2)}, u32[]{:S(2)}) collective-permute-start(f32[24,1024]{1,0:T(8,128)S(1)} %pad_maximum_fusion.3), channel_id=1, source_target_pairs={{0,16},{1,17},{2,18},{3,19},{4,20},{5,21},{6,22},{7,23},{8,24},{9,... | collective-permute-start | bytes 294920 | tf_op jit(solution)/shard_map/ppermute | solution.py:503
  35.4 2.5 %collective-permute-done.6 = f32[128,256]{1,0:T(8,128)S(1)} collective-permute-done((f32[128,256]{1,0:T(8,128)S(1)}, f32[128,256]{1,0:T(8,128)S(1)}, u32[]{:S(2)}, u32[]{:S(2)}) %collective-permute-start.6) | collective-permute-done | bytes 131104 | tf_op jit(solution)/shard_map/ppermute | solution.py:503
  37.9 1.5 %collective-permute-done.8 = f32[24,1024]{1,0:T(8,128)S(1)} collective-permute-done((f32[24,1024]{1,0:T(8,128)S(1)}, f32[24,1024]{1,0:T(8,128)S(1)}, u32[]{:S(2)}, u32[]{:S(2)}) %collective-permute-start.8) | collective-permute-done | bytes 98336 | tf_op jit(solution)/shard_map/ppermute | solution.py:503
  39.5 3.0 %collective-permute-start.9 = (f32[24,1536]{1,0:T(8,128)S(1)}, f32[24,1536]{1,0:T(8,128)S(1)}, u32[]{:S(2)}, u32[]{:S(2)}) collective-permute-start(f32[24,1536]{1,0:T(8,128)S(1)} %constant_dynamic-update-slice_fusion), channel_id=1, source_target_pairs={{0,1},{1,0},{2,3},{3,2},{4,5},{5,4},{6,7},{7,6},{8,9},{9,8},{10,11... | collective-permute-start | bytes 442376 | tf_op jit(solution)/shard_map/ppermute | solution.py:503
  43.1 1.8 %collective-permute-start.10 = (f32[256,256]{1,0:T(8,128)S(1)}, f32[256,256]{1,0:T(8,128)S(1)}, u32[]{:S(2)}, u32[]{:S(2)}) collective-permute-start(f32[256,256]{1,0:T(8,128)S(1)} %pad_maximum_fusion.here_ref), channel_id=1, source_target_pairs={{0,8},{1,9},{2,10},{3,11},{4,12},{5,13},{6,14},{7,15},{8,0},{9,1},... | collective-permute-start | bytes 786440 | tf_op jit(solution)/shard_map/ppermute | solution.py:503
  45.0 4.7 %plane_couple.2.refs_1_ = f32[1024,512]{1,0:T(8,128)S(1)} custom-call(s32[6]{0:T(128)S(1)} %broadcast_multiply_fusion.first_ref, f32[24,2048]{1,0:T(8,128)S(1)} %pad_maximum_fusion.2.refs_0_), custom_call_target="tpu_custom_call" | custom-call | flops 2147483648 | bytes 2000000 | tf_op jit(solution)/shard_map/plane_couple/pallas_call | solution.py:780
  49.8 1.7 %collective-permute-done.10.pair_ref = f32[256,256]{1,0:T(8,128)S(1)} collective-permute-done((f32[256,256]{1,0:T(8,128)S(1)}, f32[256,256]{1,0:T(8,128)S(1)}, u32[]{:S(2)}, u32[]{:S(2)}) %collective-permute-start.10) | collective-permute-done | bytes 262176 | tf_op jit(solution)/shard_map/ppermute | solution.py:503
  51.4 2.2 %plane_first.1.a_ref.pulled_ref.old_z_ref = f32[128,256]{1,0:T(8,128)S(1)} custom-call(f32[3]{0:T(128)S(1)} %add_convert_fusion.flag_ref, f32[256,256]{1,0:T(8,128)S(1)} %pad_maximum_fusion.here_ref, f32[256,256]{1,0:T(8,128)S(1)} %collective-permute-done.10.pair_ref, f32[256,256]{1,0:T(8,128)S(1)} %collective-permute-done.11.middle_ref, ...), custom_call_target="tpu_custom_call" | custom-call | flops 1 | bytes 1 | tf_op jit(solution)/shard_map/plane_first/pallas_call | solution.py:907
  53.7 2.4 %collective-permute-start.14 = (f32[128,256]{1,0:T(8,128)S(1)}, f32[128,256]{1,0:T(8,128)S(1)}, u32[]{:S(2)}, u32[]{:S(2)}) collective-permute-start(f32[128,256]{1,0:T(8,128)S(1)} %plane_first.1.a_ref.pulled_ref.old_z_ref), channel_id=1, source_target_pairs={{0,6},{1,7},{2,4},{3,5},{4,2},{5,3},{6,0},{7,1},{8,14},{9,15},{10,... | collective-permute-start | bytes 393224 | tf_op jit(solution)/shard_map/ppermute | solution.py:503
  56.4 4.9 %plane_couple.3 = (bf16[1024,512]{1,0:T(8,128)(2,1)S(1)}, bf16[1024,512]{1,0:T(8,128)(2,1)S(1)}) custom-call(s32[6]{0:T(128)S(1)} %broadcast_multiply_fusion.first_ref, f32[24,2048]{1,0:T(8,128)S(1)} %pad_maximum_fusion.1.refs_0_, f32[1024,512]{1,0:T(8,128)S(1)} %plane_couple.2.refs_1_), custom_call_target="tpu_custom_call" | custom-call | flops 2147483648 | bytes 2000000 | tf_op jit(solution)/shard_map/plane_couple/pallas_call | solution.py:780
  66.0 2.6 %collective-permute-start.16 = (f32[128,256]{1,0:T(8,128)S(1)}, f32[128,256]{1,0:T(8,128)S(1)}, u32[]{:S(2)}, u32[]{:S(2)}) collective-permute-start(f32[128,256]{1,0:T(8,128)S(1)} %add.61.here_ref.old_s_ref), channel_id=1, source_target_pairs={{0,8},{1,9},{2,10},{3,11},{4,12},{5,13},{6,14},{7,15},{8,0},{9,1},... | collective-permute-start | bytes 393224 | tf_op jit(solution)/shard_map/ppermute | solution.py:503
  68.6 3.3 %collective-permute-done.16.pair_ref = f32[128,256]{1,0:T(8,128)S(1)} collective-permute-done((f32[128,256]{1,0:T(8,128)S(1)}, f32[128,256]{1,0:T(8,128)S(1)}, u32[]{:S(2)}, u32[]{:S(2)}) %collective-permute-start.16) | collective-permute-done | bytes 131104 | tf_op jit(solution)/shard_map/ppermute | solution.py:503
  71.9 1.8 %plane_open.1 = (f32[136,256]{1,0:T(8,128)S(1)}, f32[256,256]{1,0:T(8,128)S(1)}) custom-call(f32[3]{0:T(128)S(1)} %add_convert_fusion.flag_ref, f32[128,256]{1,0:T(8,128)S(1)} %add.61.here_ref.old_s_ref, f32[128,256]{1,0:T(8,128)S(1)} %collective-permute-done.16.pair_ref, f32[128,256]{1,0:T(8,128)S(1)} %collective-permute-done.17.middle_ref, ...), custom_call_target="tpu_custom_call" | custom-call | flops 1 | bytes 1 | tf_op jit(solution)/shard_map/plane_open/pallas_call | solution.py:907
  73.8 2.1 %collective-permute-start.20 = (f32[136,256]{1,0:T(8,128)S(1)}, f32[136,256]{1,0:T(8,128)S(1)}, u32[]{:S(2)}, u32[]{:S(2)}) collective-permute-start(f32[136,256]{1,0:T(8,128)S(1)} %get-tuple-element.70.a_ref.pulled_ref), channel_id=1, source_target_pairs={{0,6},{1,7},{2,4},{3,5},{4,2},{5,3},{6,0},{7,1},{8,14},{9,15},{10,... | collective-permute-start | bytes 417800 | tf_op jit(solution)/shard_map/ppermute | solution.py:503
  78.7 4.1 %collective-permute-done.19.c_ref = f32[136,256]{1,0:T(8,128)S(1)} collective-permute-done((f32[136,256]{1,0:T(8,128)S(1)}, f32[136,256]{1,0:T(8,128)S(1)}, u32[]{:S(2)}, u32[]{:S(2)}) %collective-permute-start.19) | collective-permute-done | bytes 139296 | tf_op jit(solution)/shard_map/ppermute | solution.py:503
  86.7 3.7 %collective-permute-start.22 = (f32[136,256]{1,0:T(8,128)S(1)}, f32[136,256]{1,0:T(8,128)S(1)}, u32[]{:S(2)}, u32[]{:S(2)}) collective-permute-start(f32[136,256]{1,0:T(8,128)S(1)} %slice_add_fusion.1.here_ref), channel_id=1, source_target_pairs={{0,8},{1,9},{2,10},{3,11},{4,12},{5,13},{6,14},{7,15},{8,0},{9,1},... | collective-permute-start | bytes 417800 | tf_op jit(solution)/shard_map/ppermute | solution.py:503
  91.6 2.2 %collective-permute-done.22.pair_ref = f32[136,256]{1,0:T(8,128)S(1)} collective-permute-done((f32[136,256]{1,0:T(8,128)S(1)}, f32[136,256]{1,0:T(8,128)S(1)}, u32[]{:S(2)}, u32[]{:S(2)}) %collective-permute-start.22) | collective-permute-done | bytes 139296 | tf_op jit(solution)/shard_map/ppermute | solution.py:503
  96.4 1.5 %collective-permute-start.28 = (f32[136,256]{1,0:T(8,128)S(1)}, f32[136,256]{1,0:T(8,128)S(1)}, u32[]{:S(2)}, u32[]{:S(2)}) collective-permute-start(f32[136,256]{1,0:T(8,128)S(1)} %get-tuple-element.75.a_ref.pulled_ref), channel_id=1, source_target_pairs={{0,6},{1,7},{2,4},{3,5},{4,2},{5,3},{6,0},{7,1},{8,14},{9,15},{10,... | collective-permute-start | bytes 417800 | tf_op jit(solution)/shard_map/ppermute | solution.py:503
  101.4 2.0 %collective-permute-done.27.c_ref = f32[136,256]{1,0:T(8,128)S(1)} collective-permute-done((f32[136,256]{1,0:T(8,128)S(1)}, f32[136,256]{1,0:T(8,128)S(1)}, u32[]{:S(2)}, u32[]{:S(2)}) %collective-permute-start.27) | collective-permute-done | bytes 139296 | tf_op jit(solution)/shard_map/ppermute | solution.py:503
  104.0 3.3 %collective-permute-start.29 = (f32[392,256]{1,0:T(8,128)S(1)}, f32[392,256]{1,0:T(8,128)S(1)}, u32[]{:S(2)}, u32[]{:S(2)}) collective-permute-start(f32[392,256]{1,0:T(8,128)S(1)} %get-tuple-element.79), channel_id=1, source_target_pairs={{0,1},{1,0},{2,3},{3,2},{4,5},{5,4},{6,7},{7,6},{8,9},{9,8},{10,11... | collective-permute-start | bytes 1204232 | tf_op jit(solution)/shard_map/ppermute | solution.py:503
  110.4 3.0 %collective-permute-start.30 = (f32[136,256]{1,0:T(8,128)S(1)}, f32[136,256]{1,0:T(8,128)S(1)}, u32[]{:S(2)}, u32[]{:S(2)}) collective-permute-start(f32[136,256]{1,0:T(8,128)S(1)} %slice_add_fusion.here_ref), channel_id=1, source_target_pairs={{0,8},{1,9},{2,10},{3,11},{4,12},{5,13},{6,14},{7,15},{8,16},{9,17... | collective-permute-start | bytes 417800 | tf_op jit(solution)/shard_map/ppermute | solution.py:503
  113.3 2.9 %collective-permute-done.30.before_ref = f32[136,256]{1,0:T(8,128)S(1)} collective-permute-done((f32[136,256]{1,0:T(8,128)S(1)}, f32[136,256]{1,0:T(8,128)S(1)}, u32[]{:S(2)}, u32[]{:S(2)}) %collective-permute-start.30) | collective-permute-done | bytes 139296 | tf_op jit(solution)/shard_map/ppermute | solution.py:503
  117.0 12.2 %all_to_all.11 = f32[32,1,128]{2,1,0:T(1,128)S(1)} all-to-all(f32[32,1,128]{2,1,0:T(1,128)S(1)} %bitcast.15), channel_id=1, replica_groups=mesh['basin'=8,'tm'=4] {'basin','tm'}, dimensions={0} | all-to-all | bytes 32768 | tf_op jit(solution)/shard_map/all_to_all | solution.py:1181
  130.1 2.7 %collective-permute-start.32 = (f32[512,128]{1,0:T(8,128)S(1)}, f32[512,128]{1,0:T(8,128)S(1)}, u32[]{:S(2)}, u32[]{:S(2)}) collective-permute-start(f32[512,128]{1,0:T(8,128)S(1)} %plane_combine.1), channel_id=1, source_target_pairs={{0,0},{1,16},{2,8},{3,24},{4,4},{5,20},{6,12},{7,28},{8,1},{9,17},... | collective-permute-start | bytes 786440 | tf_op jit(solution)/shard_map/ppermute | solution.py:503
  132.8 10.6 %collective-permute-done.32.rows_ref = f32[512,128]{1,0:T(8,128)S(1)} collective-permute-done((f32[512,128]{1,0:T(8,128)S(1)}, f32[512,128]{1,0:T(8,128)S(1)}, u32[]{:S(2)}, u32[]{:S(2)}) %collective-permute-start.32) | collective-permute-done | bytes 262176 | tf_op jit(solution)/shard_map/ppermute | solution.py:503
  143.4 1.6 %plane_finish.1 = f32[4096,128]{1,0:T(8,128)} custom-call(f32[512,128]{1,0:T(8,128)S(1)} %collective-permute-done.32.rows_ref, s32[32,16,128]{2,1,0:T(8,128)S(1)} %copy-done.2, f32[4096,128]{1,0:T(8,128)S(1)} %copy-done.1), custom_call_target="tpu_custom_call" | custom-call | tf_op jit(solution)/shard_map/plane_finish/pallas_call | solution.py:1073
  (94 shorter events, 31.7 us)
Async XLA Ops:
  1.1 11.8 %collective-permute-start.1 = (f32[256,128]{0,1:T(8,128)S(1)}, f32[256,128]{0,1:T(8,128)S(1)}, u32[]{:S(2)}, u32[]{:S(2)}) collective-permute-start(f32[256,128]{0,1:T(8,128)S(1)} %copy.14), channel_id=1, source_target_pairs={{0,0},{1,8},{2,16},{3,24},{4,4},{5,12},{6,20},{7,28},{8,2},{9,10},... | collective-permute-start | bytes 393224 | tf_op jit(solution)/shard_map/ppermute | solution.py:503
  8.9 17.4 %collective-permute-start = (f32[136,512]{1,0:T(8,128)}, f32[136,512]{1,0:T(8,128)S(1)}, u32[]{:S(2)}, u32[]{:S(2)}) collective-permute-start(f32[136,512]{1,0:T(8,128)} %send.1), channel_id=1, source_target_pairs={{0,0},{1,8},{2,16},{3,24},{4,4},{5,12},{6,20},{7,28},{8,2},{9,10},... | collective-permute-start | bytes 835592 | tf_op jit(solution)/shard_map/ppermute | solution.py:503
  13.1 13.3 %collective-permute-start.3 = (f32[24,512]{1,0:T(8,128)S(1)}, f32[24,512]{1,0:T(8,128)S(1)}, u32[]{:S(2)}, u32[]{:S(2)}) collective-permute-start(f32[24,512]{1,0:T(8,128)S(1)} %describe.1), channel_id=1, source_target_pairs={{0,4},{1,5},{2,6},{3,7},{4,0},{5,1},{6,2},{7,3},{8,12},{9,13},{10,... | collective-permute-start | bytes 147464 | tf_op jit(solution)/shard_map/ppermute | solution.py:503
  26.3 3.0 %collective-permute-start.2 = (f32[136,512]{1,0:T(8,128)S(1)}, f32[136,512]{1,0:T(8,128)S(1)}, u32[]{:S(2)}, u32[]{:S(2)}) collective-permute-start(f32[136,512]{1,0:T(8,128)S(1)} %collective-permute-done.mine_ref), channel_id=1, source_target_pairs={{0,1},{1,0},{2,3},{3,2},{4,5},{5,4},{6,7},{7,6},{8,9},{9,8},{10,11... | collective-permute-start | bytes 835592 | tf_op jit(solution)/shard_map/ppermute | solution.py:503
  26.3 3.0 %collective-permute-start.4 = (f32[24,512]{1,0:T(8,128)S(1)}, f32[24,512]{1,0:T(8,128)S(1)}, u32[]{:S(2)}, u32[]{:S(2)}) collective-permute-start(f32[24,512]{1,0:T(8,128)S(1)} %broadcast_select_fusion), channel_id=1, source_target_pairs={{0,8},{1,9},{2,10},{3,11},{4,12},{5,13},{6,14},{7,15},{8,0},{9,1},... | collective-permute-start | bytes 147464 | tf_op jit(solution)/shard_map/ppermute | solution.py:503
  30.9 4.4 %collective-permute-start.5 = (f32[128,256]{1,0:T(8,128)S(1)}, f32[128,256]{1,0:T(8,128)S(1)}, u32[]{:S(2)}, u32[]{:S(2)}) collective-permute-start(f32[128,256]{1,0:T(8,128)S(1)} %get-tuple-element.54), channel_id=1, source_target_pairs={{0,4},{1,5},{2,6},{3,7},{4,0},{5,1},{6,2},{7,3},{8,12},{9,13},{10,... | collective-permute-start | bytes 393224 | tf_op jit(solution)/shard_map/ppermute | solution.py:503
  32.2 5.7 %collective-permute-start.6 = (f32[128,256]{1,0:T(8,128)S(1)}, f32[128,256]{1,0:T(8,128)S(1)}, u32[]{:S(2)}, u32[]{:S(2)}) collective-permute-start(f32[128,256]{1,0:T(8,128)S(1)} %get-tuple-element.55), channel_id=1, source_target_pairs={{0,2},{1,3},{2,0},{3,1},{4,6},{5,7},{6,4},{7,5},{8,10},{9,11},{10,... | collective-permute-start | bytes 393224 | tf_op jit(solution)/shard_map/ppermute | solution.py:503
  32.2 5.7 %collective-permute-start.7 = (f32[128,256]{1,0:T(8,128)S(1)}, f32[128,256]{1,0:T(8,128)S(1)}, u32[]{:S(2)}, u32[]{:S(2)}) collective-permute-start(f32[128,256]{1,0:T(8,128)S(1)} %get-tuple-element.56), channel_id=1, source_target_pairs={{0,6},{1,7},{2,4},{3,5},{4,2},{5,3},{6,0},{7,1},{8,14},{9,15},{10,... | collective-permute-start | bytes 393224 | tf_op jit(solution)/shard_map/ppermute | solution.py:503
  33.6 5.8 %collective-permute-start.8 = (f32[24,1024]{1,0:T(8,128)S(1)}, f32[24,1024]{1,0:T(8,128)S(1)}, u32[]{:S(2)}, u32[]{:S(2)}) collective-permute-start(f32[24,1024]{1,0:T(8,128)S(1)} %pad_maximum_fusion.3), channel_id=1, source_target_pairs={{0,16},{1,17},{2,18},{3,19},{4,20},{5,21},{6,22},{7,23},{8,24},{9,... | collective-permute-start | bytes 294920 | tf_op jit(solution)/shard_map/ppermute | solution.py:503
  39.5 10.3 %collective-permute-start.9 = (f32[24,1536]{1,0:T(8,128)S(1)}, f32[24,1536]{1,0:T(8,128)S(1)}, u32[]{:S(2)}, u32[]{:S(2)}) collective-permute-start(f32[24,1536]{1,0:T(8,128)S(1)} %constant_dynamic-update-slice_fusion), channel_id=1, source_target_pairs={{0,1},{1,0},{2,3},{3,2},{4,5},{5,4},{6,7},{7,6},{8,9},{9,8},{10,11... | collective-permute-start | bytes 442376 | tf_op jit(solution)/shard_map/ppermute | solution.py:503
  42.4 7.3 %collective-permute-start.11 = (f32[256,256]{1,0:T(8,128)S(1)}, f32[256,256]{1,0:T(8,128)S(1)}, u32[]{:S(2)}, u32[]{:S(2)}) collective-permute-start(f32[256,256]{1,0:T(8,128)S(1)} %pad_maximum_fusion.here_ref), channel_id=1, source_target_pairs={{8,16},{9,17},{10,18},{11,19},{12,20},{13,21},{14,22},{15,23},{16,... | collective-permute-start | bytes 786440 | tf_op jit(solution)/shard_map/ppermute | solution.py:503
  43.1 8.3 %collective-permute-start.10 = (f32[256,256]{1,0:T(8,128)S(1)}, f32[256,256]{1,0:T(8,128)S(1)}, u32[]{:S(2)}, u32[]{:S(2)}) collective-permute-start(f32[256,256]{1,0:T(8,128)S(1)} %pad_maximum_fusion.here_ref), channel_id=1, source_target_pairs={{0,8},{1,9},{2,10},{3,11},{4,12},{5,13},{6,14},{7,15},{8,0},{9,1},... | collective-permute-start | bytes 786440 | tf_op jit(solution)/shard_map/ppermute | solution.py:503
  53.7 7.7 %collective-permute-start.14 = (f32[128,256]{1,0:T(8,128)S(1)}, f32[128,256]{1,0:T(8,128)S(1)}, u32[]{:S(2)}, u32[]{:S(2)}) collective-permute-start(f32[128,256]{1,0:T(8,128)S(1)} %plane_first.1.a_ref.pulled_ref.old_z_ref), channel_id=1, source_target_pairs={{0,6},{1,7},{2,4},{3,5},{4,2},{5,3},{6,0},{7,1},{8,14},{9,15},{10,... | collective-permute-start | bytes 393224 | tf_op jit(solution)/shard_map/ppermute | solution.py:503
  56.1 6.7 %collective-permute-start.13 = (f32[128,256]{1,0:T(8,128)S(1)}, f32[128,256]{1,0:T(8,128)S(1)}, u32[]{:S(2)}, u32[]{:S(2)}) collective-permute-start(f32[128,256]{1,0:T(8,128)S(1)} %plane_first.1.a_ref.pulled_ref.old_z_ref), channel_id=1, source_target_pairs={{0,2},{1,3},{2,0},{3,1},{4,6},{5,7},{6,4},{7,5},{8,10},{9,11},{10,... | collective-permute-start | bytes 393224 | tf_op jit(solution)/shard_map/ppermute | solution.py:503
  56.1 6.7 %collective-permute-start.12 = (f32[128,256]{1,0:T(8,128)S(1)}, f32[128,256]{1,0:T(8,128)S(1)}, u32[]{:S(2)}, u32[]{:S(2)}) collective-permute-start(f32[128,256]{1,0:T(8,128)S(1)} %plane_first.1.a_ref.pulled_ref.old_z_ref), channel_id=1, source_target_pairs={{0,4},{1,5},{2,6},{3,7},{4,0},{5,1},{6,2},{7,3},{8,12},{9,13},{10,... | collective-permute-start | bytes 393224 | tf_op jit(solution)/shard_map/ppermute | solution.py:503
  65.3 3.3 %collective-permute-start.17 = (f32[128,256]{1,0:T(8,128)S(1)}, f32[128,256]{1,0:T(8,128)S(1)}, u32[]{:S(2)}, u32[]{:S(2)}) collective-permute-start(f32[128,256]{1,0:T(8,128)S(1)} %add.61.here_ref.old_s_ref), channel_id=1, source_target_pairs={{8,16},{9,17},{10,18},{11,19},{12,20},{13,21},{14,22},{15,23},{16,... | collective-permute-start | bytes 393224 | tf_op jit(solution)/shard_map/ppermute | solution.py:503
  66.0 5.9 %collective-permute-start.16 = (f32[128,256]{1,0:T(8,128)S(1)}, f32[128,256]{1,0:T(8,128)S(1)}, u32[]{:S(2)}, u32[]{:S(2)}) collective-permute-start(f32[128,256]{1,0:T(8,128)S(1)} %add.61.here_ref.old_s_ref), channel_id=1, source_target_pairs={{0,8},{1,9},{2,10},{3,11},{4,12},{5,13},{6,14},{7,15},{8,0},{9,1},... | collective-permute-start | bytes 393224 | tf_op jit(solution)/shard_map/ppermute | solution.py:503
  73.8 4.9 %collective-permute-start.20 = (f32[136,256]{1,0:T(8,128)S(1)}, f32[136,256]{1,0:T(8,128)S(1)}, u32[]{:S(2)}, u32[]{:S(2)}) collective-permute-start(f32[136,256]{1,0:T(8,128)S(1)} %get-tuple-element.70.a_ref.pulled_ref), channel_id=1, source_target_pairs={{0,6},{1,7},{2,4},{3,5},{4,2},{5,3},{6,0},{7,1},{8,14},{9,15},{10,... | collective-permute-start | bytes 417800 | tf_op jit(solution)/shard_map/ppermute | solution.py:503
  75.8 6.9 %collective-permute-start.19 = (f32[136,256]{1,0:T(8,128)S(1)}, f32[136,256]{1,0:T(8,128)S(1)}, u32[]{:S(2)}, u32[]{:S(2)}) collective-permute-start(f32[136,256]{1,0:T(8,128)S(1)} %get-tuple-element.70.a_ref.pulled_ref), channel_id=1, source_target_pairs={{0,2},{1,3},{2,0},{3,1},{4,6},{5,7},{6,4},{7,5},{8,10},{9,11},{10,... | collective-permute-start | bytes 417800 | tf_op jit(solution)/shard_map/ppermute | solution.py:503
  76.2 6.6 %collective-permute-start.18 = (f32[136,256]{1,0:T(8,128)S(1)}, f32[136,256]{1,0:T(8,128)S(1)}, u32[]{:S(2)}, u32[]{:S(2)}) collective-permute-start(f32[136,256]{1,0:T(8,128)S(1)} %get-tuple-element.70.a_ref.pulled_ref), channel_id=1, source_target_pairs={{0,4},{1,5},{2,6},{3,7},{4,0},{5,1},{6,2},{7,3},{8,12},{9,13},{10,... | collective-permute-start | bytes 417800 | tf_op jit(solution)/shard_map/ppermute | solution.py:503
  83.4 2.4 %collective-permute-start.21 = (f32[392,256]{1,0:T(8,128)S(1)}, f32[392,256]{1,0:T(8,128)S(1)}, u32[]{:S(2)}, u32[]{:S(2)}) collective-permute-start(f32[392,256]{1,0:T(8,128)S(1)} %get-tuple-element.73), channel_id=1, source_target_pairs={{0,1},{1,0},{2,3},{3,2},{4,5},{5,4},{6,7},{7,6},{8,9},{9,8},{10,11... | collective-permute-start | bytes 1204232 | tf_op jit(solution)/shard_map/ppermute | solution.py:503
  85.8 5.8 %collective-permute-start.25 = (f32[136,256]{1,0:T(8,128)S(1)}, f32[136,256]{1,0:T(8,128)S(1)}, u32[]{:S(2)}, u32[]{:S(2)}) collective-permute-start(f32[136,256]{1,0:T(8,128)S(1)} %slice_add_fusion.1.here_ref), channel_id=1, source_target_pairs={{8,16},{9,17},{10,18},{11,19},{12,20},{13,21},{14,22},{15,23},{16,... | collective-permute-start | bytes 417800 | tf_op jit(solution)/shard_map/ppermute | solution.py:503
  86.7 7.1 %collective-permute-start.22 = (f32[136,256]{1,0:T(8,128)S(1)}, f32[136,256]{1,0:T(8,128)S(1)}, u32[]{:S(2)}, u32[]{:S(2)}) collective-permute-start(f32[136,256]{1,0:T(8,128)S(1)} %slice_add_fusion.1.here_ref), channel_id=1, source_target_pairs={{0,8},{1,9},{2,10},{3,11},{4,12},{5,13},{6,14},{7,15},{8,0},{9,1},... | collective-permute-start | bytes 417800 | tf_op jit(solution)/shard_map/ppermute | solution.py:503
  90.4 4.7 %collective-permute-start.24 = (f32[8,256]{1,0:T(8,128)S(1)}, f32[8,256]{1,0:T(8,128)S(1)}, u32[]{:S(2)}, u32[]{:S(2)}) collective-permute-start(f32[8,256]{1,0:T(8,128)S(1)} %slice.32), channel_id=1, source_target_pairs={{0,24},{1,25},{2,26},{3,27},{4,28},{5,29},{6,30},{7,31},{8,16},{9,... | collective-permute-start | bytes 24584 | tf_op jit(solution)/shard_map/ppermute | solution.py:503
  91.5 3.6 %collective-permute-start.23 = (f32[8,256]{1,0:T(8,128)S(1)}, f32[8,256]{1,0:T(8,128)S(1)}, u32[]{:S(2)}, u32[]{:S(2)}) collective-permute-start(f32[8,256]{1,0:T(8,128)S(1)} %slice.32), channel_id=1, source_target_pairs={{0,16},{1,17},{2,18},{3,19},{4,20},{5,21},{6,22},{7,23},{8,24},{9,... | collective-permute-start | bytes 24584 | tf_op jit(solution)/shard_map/ppermute | solution.py:503
  96.4 5.0 %collective-permute-start.28 = (f32[136,256]{1,0:T(8,128)S(1)}, f32[136,256]{1,0:T(8,128)S(1)}, u32[]{:S(2)}, u32[]{:S(2)}) collective-permute-start(f32[136,256]{1,0:T(8,128)S(1)} %get-tuple-element.75.a_ref.pulled_ref), channel_id=1, source_target_pairs={{0,6},{1,7},{2,4},{3,5},{4,2},{5,3},{6,0},{7,1},{8,14},{9,15},{10,... | collective-permute-start | bytes 417800 | tf_op jit(solution)/shard_map/ppermute | solution.py:503
  97.9 5.5 %collective-permute-start.27 = (f32[136,256]{1,0:T(8,128)S(1)}, f32[136,256]{1,0:T(8,128)S(1)}, u32[]{:S(2)}, u32[]{:S(2)}) collective-permute-start(f32[136,256]{1,0:T(8,128)S(1)} %get-tuple-element.75.a_ref.pulled_ref), channel_id=1, source_target_pairs={{0,2},{1,3},{2,0},{3,1},{4,6},{5,7},{6,4},{7,5},{8,10},{9,11},{10,... | collective-permute-start | bytes 417800 | tf_op jit(solution)/shard_map/ppermute | solution.py:503
  98.8 4.6 %collective-permute-start.26 = (f32[136,256]{1,0:T(8,128)S(1)}, f32[136,256]{1,0:T(8,128)S(1)}, u32[]{:S(2)}, u32[]{:S(2)}) collective-permute-start(f32[136,256]{1,0:T(8,128)S(1)} %get-tuple-element.75.a_ref.pulled_ref), channel_id=1, source_target_pairs={{0,4},{1,5},{2,6},{3,7},{4,0},{5,1},{6,2},{7,3},{8,12},{9,13},{10,... | collective-permute-start | bytes 417800 | tf_op jit(solution)/shard_map/ppermute | solution.py:503
  104.0 4.7 %collective-permute-start.29 = (f32[392,256]{1,0:T(8,128)S(1)}, f32[392,256]{1,0:T(8,128)S(1)}, u32[]{:S(2)}, u32[]{:S(2)}) collective-permute-start(f32[392,256]{1,0:T(8,128)S(1)} %get-tuple-element.79), channel_id=1, source_target_pairs={{0,1},{1,0},{2,3},{3,2},{4,5},{5,4},{6,7},{7,6},{8,9},{9,8},{10,11... | collective-permute-start | bytes 1204232 | tf_op jit(solution)/shard_map/ppermute | solution.py:503
  109.9 19.3 %collective-permute-start.31 = (f32[256,256]{1,0:T(8,128)S(1)}, f32[256,256]{1,0:T(8,128)S(1)}, u32[]{:S(2)}, u32[]{:S(2)}) collective-permute-start(f32[256,256]{1,0:T(8,128)S(1)} %get-tuple-element.86), channel_id=1, source_target_pairs={{0,1},{1,0},{2,3},{3,2},{4,5},{5,4},{6,7},{7,6},{8,9},{9,8},{10,11... | collective-permute-start | bytes 786440 | tf_op jit(solution)/shard_map/ppermute | solution.py:503
  110.4 5.9 %collective-permute-start.30 = (f32[136,256]{1,0:T(8,128)S(1)}, f32[136,256]{1,0:T(8,128)S(1)}, u32[]{:S(2)}, u32[]{:S(2)}) collective-permute-start(f32[136,256]{1,0:T(8,128)S(1)} %slice_add_fusion.here_ref), channel_id=1, source_target_pairs={{0,8},{1,9},{2,10},{3,11},{4,12},{5,13},{6,14},{7,15},{8,16},{9,17... | collective-permute-start | bytes 417800 | tf_op jit(solution)/shard_map/ppermute | solution.py:503
  130.1 13.3 %collective-permute-start.32 = (f32[512,128]{1,0:T(8,128)S(1)}, f32[512,128]{1,0:T(8,128)S(1)}, u32[]{:S(2)}, u32[]{:S(2)}) collective-permute-start(f32[512,128]{1,0:T(8,128)S(1)} %plane_combine.1), channel_id=1, source_target_pairs={{0,0},{1,16},{2,8},{3,24},{4,4},{5,20},{6,12},{7,28},{8,1},{9,17},... | collective-permute-start | bytes 786440 | tf_op jit(solution)/shard_map/ppermute | solution.py:503
  (11 other events, 150.4 us)

commit v25 on v24

--- a/solution.py
+++ b/solution.py
@@ -1107,10 +1107,10 @@
     half = meta.shape[1] // 2
     share = jnp.where(c == 0, meta[:, :half], meta[:, half:])
     close = moved(share, z_pair)
-    parcel, seen = lax.optimization_barrier((parcel, seen))
+    parcel, seen, close = lax.optimization_barrier((parcel, seen, close))
     parcels = [parcel, moved(parcel, over_core)]
     spec = plane_spectrum(parcel[hours:], kernels, short3, rows)
-    parcels[1], seen, close, spec = lax.optimization_barrier((parcels[1], seen, close, spec))
+    parcels[1], seen, spec = lax.optimization_barrier((parcels[1], seen, spec))
     far = moved(jnp.concatenate([share, close], axis=1), z_two)
     dense = spread(first, parcels, rows)
     metas = [value[hours:] for value in parcels]

time: 145 us -> 150 us (1.034)
  starting transfers between devices: 48 us -> 53.2 us
    ppermute x33, starting transfers between devices: 48 us -> 53.2 us  [moved(): return lax.ppermute(value, ('basin', 'tm'), pairs)]
  transfers between devices with their start and end apart: 33 -> 33, of which waited for: 18 -> 20; matrix products, arithmetic and copies ran while one was open for 0% -> 0% of each run, Pallas kernels for 10% -> 10%
where the time goes in v25:
time: 150 us; the launch traced here: 149 us
  starting transfers between devices  53.2 us (35%)
  waiting for transfers between devices  51.8 us (35%)
  Pallas kernels  30.5 us (20%)
  blocking collectives  12.1 us (8%)
    ppermute x33, starting transfers between devices, moved(): return lax.ppermute(value, ('basin', 'tm'), pairs)  53.2 us
    ppermute x33, waiting for transfers between devices, moved(): return lax.ppermute(value, ('basin', 'tm'), pairs)  51.8 us
    all_to_all x1, blocking collectives, plane_shards(): close_note = lax.all_to_all(note, ('basin', 'tm'), 0, 0, tiled=True)  12.1 us
    pallas_call x2, Pallas kernels, plane_couple(): pl.pallas_call(functools.partial(plane_couple_kernel, last), in_specs=[pl...  9.56 us
    pallas_call x6, Pallas kernels, plane_call(): pl.pallas_call(kernel, in_specs=[pl.BlockSpec(memory_space=pltpu.SMEM)] *...  8.2 us
    pallas_call x3, Pallas kernels, plane_rows(): pl.pallas_call(plane_rows_kernel, in_specs=[pl.BlockSpec(memory_space=plt...  3.79 us
    pallas_call x1, Pallas kernels, send(): pl.pallas_call(send_kernel, in_specs=[pl.BlockSpec(memory_space=pltpu.HBM...  3.21 us
  transfers between devices with their start and end apart: 33, of which 20 were waited for; matrix products, arithmetic and copies ran while one was open for 0% of the time, Pallas kernels for 10%

profile of v25, /device:TPU:1, one launch (start us, length us, event | category | flops | bytes accessed | tf_op | source)
XLA Modules:
  0.0 149.5 jit_solution(12636689706097028634)
XLA Ops:
  1.1 4.6 %collective-permute-start.1 = (f32[256,128]{0,1:T(8,128)S(1)}, f32[256,128]{0,1:T(8,128)S(1)}, u32[]{:S(2)}, u32[]{:S(2)}) collective-permute-start(f32[256,128]{0,1:T(8,128)S(1)} %copy.14), channel_id=1, source_target_pairs={{0,0},{1,8},{2,16},{3,24},{4,4},{5,12},{6,20},{7,28},{8,2},{9,10},... | collective-permute-start | bytes 393224 | tf_op jit(solution)/shard_map/ppermute | solution.py:503
  5.7 3.2 %send.1 = f32[136,512]{1,0:T(8,128)} custom-call(s32[32,16,128]{2,1,0:T(8,128)} %inc_ref.2, f32[4096,128]{1,0:T(8,128)} %field_ref.1, s32[1,512]{1,0:T(1,128)} %bitcast.17, s32[1,256]{1,0:T(1,128)} %bitcast.20), custom_call_target="tpu_custom_call" | custom-call | flops 1 | bytes 1 | tf_op jit(solution)/shard_map/send/pallas_call | solution.py:680
  8.9 3.9 %collective-permute-done.1 = f32[256,128]{0,1:T(8,128)S(1)} collective-permute-done((f32[256,128]{0,1:T(8,128)S(1)}, f32[256,128]{0,1:T(8,128)S(1)}, u32[]{:S(2)}, u32[]{:S(2)}) %collective-permute-start.1) | collective-permute-done | bytes 131104 | tf_op jit(solution)/shard_map/ppermute | solution.py:503
  14.4 1.9 %collective-permute-start = (f32[136,512]{1,0:T(8,128)}, f32[136,512]{1,0:T(8,128)S(1)}, u32[]{:S(2)}, u32[]{:S(2)}) collective-permute-start(f32[136,512]{1,0:T(8,128)} %send.1), channel_id=1, source_target_pairs={{0,0},{1,8},{2,16},{3,24},{4,4},{5,12},{6,20},{7,28},{8,2},{9,10},... | collective-permute-start | bytes 835592 | tf_op jit(solution)/shard_map/ppermute | solution.py:503
  16.3 2.3 %collective-permute-start.3 = (f32[24,512]{1,0:T(8,128)S(1)}, f32[24,512]{1,0:T(8,128)S(1)}, u32[]{:S(2)}, u32[]{:S(2)}) collective-permute-start(f32[24,512]{1,0:T(8,128)S(1)} %broadcast_select_fusion), channel_id=1, source_target_pairs={{0,8},{1,9},{2,10},{3,11},{4,12},{5,13},{6,14},{7,15},{8,0},{9,1},... | collective-permute-start | bytes 147464 | tf_op jit(solution)/shard_map/ppermute | solution.py:503
  18.6 2.4 %collective-permute-done.3 = f32[24,512]{1,0:T(8,128)S(1)} collective-permute-done((f32[24,512]{1,0:T(8,128)S(1)}, f32[24,512]{1,0:T(8,128)S(1)}, u32[]{:S(2)}, u32[]{:S(2)}) %collective-permute-start.3) | collective-permute-done | bytes 49184 | tf_op jit(solution)/shard_map/ppermute | solution.py:503
  21.0 9.1 %collective-permute-done.mine_ref = f32[136,512]{1,0:T(8,128)S(1)} collective-permute-done((f32[136,512]{1,0:T(8,128)}, f32[136,512]{1,0:T(8,128)S(1)}, u32[]{:S(2)}, u32[]{:S(2)}) %collective-permute-start) | collective-permute-done | bytes 278560 | tf_op jit(solution)/shard_map/ppermute | solution.py:503
  31.7 1.6 %spread.1 = (f32[128,256]{1,0:T(8,128)S(1)}, f32[128,256]{1,0:T(8,128)S(1)}, f32[128,256]{1,0:T(8,128)S(1)}, f32[128,256]{1,0:T(8,128)S(1)}) custom-call(s32[6]{0:T(128)S(1)} %broadcast_multiply_fusion.first_ref, f32[136,512]{1,0:T(8,128)S(1)} %collective-permute-done.mine_ref, f32[136,512]{1,0:T(8,128)S(1)} %collective-permute-done.4.other_ref), custom_call_target="tpu_custom_call" | custom-call | flops 1 | bytes 1 | tf_op jit(solution)/shard_map/spread/pallas_call | solution.py:714
  33.6 2.4 %collective-permute-start.7 = (f32[128,256]{1,0:T(8,128)S(1)}, f32[128,256]{1,0:T(8,128)S(1)}, u32[]{:S(2)}, u32[]{:S(2)}) collective-permute-start(f32[128,256]{1,0:T(8,128)S(1)} %get-tuple-element.56), channel_id=1, source_target_pairs={{0,6},{1,7},{2,4},{3,5},{4,2},{5,3},{6,0},{7,1},{8,14},{9,15},{10,... | collective-permute-start | bytes 393224 | tf_op jit(solution)/shard_map/ppermute | solution.py:503
  36.0 4.2 %collective-permute-start.8 = (f32[24,1024]{1,0:T(8,128)S(1)}, f32[24,1024]{1,0:T(8,128)S(1)}, u32[]{:S(2)}, u32[]{:S(2)}) collective-permute-start(f32[24,1024]{1,0:T(8,128)S(1)} %pad_maximum_fusion.3), channel_id=1, source_target_pairs={{0,16},{1,17},{2,18},{3,19},{4,20},{5,21},{6,22},{7,23},{8,24},{9,... | collective-permute-start | bytes 294920 | tf_op jit(solution)/shard_map/ppermute | solution.py:503
  42.2 3.9 %collective-permute-start.9 = (f32[24,1536]{1,0:T(8,128)S(1)}, f32[24,1536]{1,0:T(8,128)S(1)}, u32[]{:S(2)}, u32[]{:S(2)}) collective-permute-start(f32[24,1536]{1,0:T(8,128)S(1)} %constant_dynamic-update-slice_fusion), channel_id=1, source_target_pairs={{0,1},{1,0},{2,3},{3,2},{4,5},{5,4},{6,7},{7,6},{8,9},{9,8},{10,11... | collective-permute-start | bytes 442376 | tf_op jit(solution)/shard_map/ppermute | solution.py:503
  46.8 3.0 %collective-permute-start.10 = (f32[256,256]{1,0:T(8,128)S(1)}, f32[256,256]{1,0:T(8,128)S(1)}, u32[]{:S(2)}, u32[]{:S(2)}) collective-permute-start(f32[256,256]{1,0:T(8,128)S(1)} %pad_maximum_fusion.here_ref), channel_id=1, source_target_pairs={{0,8},{1,9},{2,10},{3,11},{4,12},{5,13},{6,14},{7,15},{8,0},{9,1},... | collective-permute-start | bytes 786440 | tf_op jit(solution)/shard_map/ppermute | solution.py:503
  49.9 4.6 %plane_couple.2.refs_1_ = f32[1024,512]{1,0:T(8,128)S(1)} custom-call(s32[6]{0:T(128)S(1)} %broadcast_multiply_fusion.first_ref, f32[24,2048]{1,0:T(8,128)S(1)} %pad_maximum_fusion.2.refs_0_), custom_call_target="tpu_custom_call" | custom-call | flops 2147483648 | bytes 2000000 | tf_op jit(solution)/shard_map/plane_couple/pallas_call | solution.py:780
  54.6 1.7 %collective-permute-done.10.pair_ref = f32[256,256]{1,0:T(8,128)S(1)} collective-permute-done((f32[256,256]{1,0:T(8,128)S(1)}, f32[256,256]{1,0:T(8,128)S(1)}, u32[]{:S(2)}, u32[]{:S(2)}) %collective-permute-start.10) | collective-permute-done | bytes 262176 | tf_op jit(solution)/shard_map/ppermute | solution.py:503
  56.3 2.2 %plane_first.1.a_ref.pulled_ref.old_z_ref = f32[128,256]{1,0:T(8,128)S(1)} custom-call(f32[3]{0:T(128)S(1)} %add_convert_fusion.flag_ref, f32[256,256]{1,0:T(8,128)S(1)} %pad_maximum_fusion.here_ref, f32[256,256]{1,0:T(8,128)S(1)} %collective-permute-done.10.pair_ref, f32[256,256]{1,0:T(8,128)S(1)} %collective-permute-done.11.middle_ref, ...), custom_call_target="tpu_custom_call" | custom-call | flops 1 | bytes 1 | tf_op jit(solution)/shard_map/plane_first/pallas_call | solution.py:907
  58.5 1.5 %collective-permute-start.14 = (f32[128,256]{1,0:T(8,128)S(1)}, f32[128,256]{1,0:T(8,128)S(1)}, u32[]{:S(2)}, u32[]{:S(2)}) collective-permute-start(f32[128,256]{1,0:T(8,128)S(1)} %plane_first.1.a_ref.pulled_ref.old_z_ref), channel_id=1, source_target_pairs={{0,6},{1,7},{2,4},{3,5},{4,2},{5,3},{6,0},{7,1},{8,14},{9,15},{10,... | collective-permute-start | bytes 393224 | tf_op jit(solution)/shard_map/ppermute | solution.py:503
  61.2 4.9 %plane_couple.3 = (bf16[1024,512]{1,0:T(8,128)(2,1)S(1)}, bf16[1024,512]{1,0:T(8,128)(2,1)S(1)}) custom-call(s32[6]{0:T(128)S(1)} %broadcast_multiply_fusion.first_ref, f32[24,2048]{1,0:T(8,128)S(1)} %pad_maximum_fusion.1.refs_0_, f32[1024,512]{1,0:T(8,128)S(1)} %plane_couple.2.refs_1_), custom_call_target="tpu_custom_call" | custom-call | flops 2147483648 | bytes 2000000 | tf_op jit(solution)/shard_map/plane_couple/pallas_call | solution.py:780
  70.5 3.0 %collective-permute-start.16 = (f32[128,256]{1,0:T(8,128)S(1)}, f32[128,256]{1,0:T(8,128)S(1)}, u32[]{:S(2)}, u32[]{:S(2)}) collective-permute-start(f32[128,256]{1,0:T(8,128)S(1)} %add.61.here_ref.old_s_ref), channel_id=1, source_target_pairs={{0,8},{1,9},{2,10},{3,11},{4,12},{5,13},{6,14},{7,15},{8,0},{9,1},... | collective-permute-start | bytes 393224 | tf_op jit(solution)/shard_map/ppermute | solution.py:503
  73.5 3.3 %collective-permute-done.16.pair_ref = f32[128,256]{1,0:T(8,128)S(1)} collective-permute-done((f32[128,256]{1,0:T(8,128)S(1)}, f32[128,256]{1,0:T(8,128)S(1)}, u32[]{:S(2)}, u32[]{:S(2)}) %collective-permute-start.16) | collective-permute-done | bytes 131104 | tf_op jit(solution)/shard_map/ppermute | solution.py:503
  76.8 1.8 %plane_open.1 = (f32[136,256]{1,0:T(8,128)S(1)}, f32[256,256]{1,0:T(8,128)S(1)}) custom-call(f32[3]{0:T(128)S(1)} %add_convert_fusion.flag_ref, f32[128,256]{1,0:T(8,128)S(1)} %add.61.here_ref.old_s_ref, f32[128,256]{1,0:T(8,128)S(1)} %collective-permute-done.16.pair_ref, f32[128,256]{1,0:T(8,128)S(1)} %collective-permute-done.17.middle_ref, ...), custom_call_target="tpu_custom_call" | custom-call | flops 1 | bytes 1 | tf_op jit(solution)/shard_map/plane_open/pallas_call | solution.py:907
  83.6 4.1 %collective-permute-done.19.c_ref = f32[136,256]{1,0:T(8,128)S(1)} collective-permute-done((f32[136,256]{1,0:T(8,128)S(1)}, f32[136,256]{1,0:T(8,128)S(1)}, u32[]{:S(2)}, u32[]{:S(2)}) %collective-permute-start.19) | collective-permute-done | bytes 139296 | tf_op jit(solution)/shard_map/ppermute | solution.py:503
  91.5 3.4 %collective-permute-start.22 = (f32[136,256]{1,0:T(8,128)S(1)}, f32[136,256]{1,0:T(8,128)S(1)}, u32[]{:S(2)}, u32[]{:S(2)}) collective-permute-start(f32[136,256]{1,0:T(8,128)S(1)} %slice_add_fusion.1.here_ref), channel_id=1, source_target_pairs={{0,8},{1,9},{2,10},{3,11},{4,12},{5,13},{6,14},{7,15},{8,0},{9,1},... | collective-permute-start | bytes 417800 | tf_op jit(solution)/shard_map/ppermute | solution.py:503
  94.9 1.5 collective-permute-start.24
  96.4 2.0 %collective-permute-done.22.pair_ref = f32[136,256]{1,0:T(8,128)S(1)} collective-permute-done((f32[136,256]{1,0:T(8,128)S(1)}, f32[136,256]{1,0:T(8,128)S(1)}, u32[]{:S(2)}, u32[]{:S(2)}) %collective-permute-start.22) | collective-permute-done | bytes 139296 | tf_op jit(solution)/shard_map/ppermute | solution.py:503
  106.0 1.8 %collective-permute-done.27.c_ref = f32[136,256]{1,0:T(8,128)S(1)} collective-permute-done((f32[136,256]{1,0:T(8,128)S(1)}, f32[136,256]{1,0:T(8,128)S(1)}, u32[]{:S(2)}, u32[]{:S(2)}) %collective-permute-start.27) | collective-permute-done | bytes 139296 | tf_op jit(solution)/shard_map/ppermute | solution.py:503
  108.4 3.4 %collective-permute-start.29 = (f32[392,256]{1,0:T(8,128)S(1)}, f32[392,256]{1,0:T(8,128)S(1)}, u32[]{:S(2)}, u32[]{:S(2)}) collective-permute-start(f32[392,256]{1,0:T(8,128)S(1)} %get-tuple-element.79), channel_id=1, source_target_pairs={{0,1},{1,0},{2,3},{3,2},{4,5},{5,4},{6,7},{7,6},{8,9},{9,8},{10,11... | collective-permute-start | bytes 1204232 | tf_op jit(solution)/shard_map/ppermute | solution.py:503
  115.0 2.9 %collective-permute-start.30 = (f32[136,256]{1,0:T(8,128)S(1)}, f32[136,256]{1,0:T(8,128)S(1)}, u32[]{:S(2)}, u32[]{:S(2)}) collective-permute-start(f32[136,256]{1,0:T(8,128)S(1)} %slice_add_fusion.here_ref), channel_id=1, source_target_pairs={{0,8},{1,9},{2,10},{3,11},{4,12},{5,13},{6,14},{7,15},{8,16},{9,17... | collective-permute-start | bytes 417800 | tf_op jit(solution)/shard_map/ppermute | solution.py:503
  117.9 2.9 %collective-permute-done.30.before_ref = f32[136,256]{1,0:T(8,128)S(1)} collective-permute-done((f32[136,256]{1,0:T(8,128)S(1)}, f32[136,256]{1,0:T(8,128)S(1)}, u32[]{:S(2)}, u32[]{:S(2)}) %collective-permute-start.30) | collective-permute-done | bytes 139296 | tf_op jit(solution)/shard_map/ppermute | solution.py:503
  121.6 12.1 %all_to_all.11 = f32[32,1,128]{2,1,0:T(1,128)S(1)} all-to-all(f32[32,1,128]{2,1,0:T(1,128)S(1)} %bitcast.15), channel_id=1, replica_groups=mesh['basin'=8,'tm'=4] {'basin','tm'}, dimensions={0} | all-to-all | bytes 32768 | tf_op jit(solution)/shard_map/all_to_all | solution.py:1181
  134.5 2.7 %collective-permute-start.32 = (f32[512,128]{1,0:T(8,128)S(1)}, f32[512,128]{1,0:T(8,128)S(1)}, u32[]{:S(2)}, u32[]{:S(2)}) collective-permute-start(f32[512,128]{1,0:T(8,128)S(1)} %plane_combine.1), channel_id=1, source_target_pairs={{0,0},{1,16},{2,8},{3,24},{4,4},{5,20},{6,12},{7,28},{8,1},{9,17},... | collective-permute-start | bytes 786440 | tf_op jit(solution)/shard_map/ppermute | solution.py:503
  137.3 10.6 %collective-permute-done.32.rows_ref = f32[512,128]{1,0:T(8,128)S(1)} collective-permute-done((f32[512,128]{1,0:T(8,128)S(1)}, f32[512,128]{1,0:T(8,128)S(1)}, u32[]{:S(2)}, u32[]{:S(2)}) %collective-permute-start.32) | collective-permute-done | bytes 262176 | tf_op jit(solution)/shard_map/ppermute | solution.py:503
  147.8 1.6 %plane_finish.1 = f32[4096,128]{1,0:T(8,128)} custom-call(f32[512,128]{1,0:T(8,128)S(1)} %collective-permute-done.32.rows_ref, s32[32,16,128]{2,1,0:T(8,128)S(1)} %copy-done.2, f32[4096,128]{1,0:T(8,128)S(1)} %copy-done.1), custom_call_target="tpu_custom_call" | custom-call | tf_op jit(solution)/shard_map/plane_finish/pallas_call | solution.py:1073
  (94 shorter events, 34.5 us)
Async XLA Ops:
  1.1 11.8 %collective-permute-start.1 = (f32[256,128]{0,1:T(8,128)S(1)}, f32[256,128]{0,1:T(8,128)S(1)}, u32[]{:S(2)}, u32[]{:S(2)}) collective-permute-start(f32[256,128]{0,1:T(8,128)S(1)} %copy.14), channel_id=1, source_target_pairs={{0,0},{1,8},{2,16},{3,24},{4,4},{5,12},{6,20},{7,28},{8,2},{9,10},... | collective-permute-start | bytes 393224 | tf_op jit(solution)/shard_map/ppermute | solution.py:503
  13.1 3.2 %collective-permute-start.2 = (f32[24,512]{1,0:T(8,128)S(1)}, f32[24,512]{1,0:T(8,128)S(1)}, u32[]{:S(2)}, u32[]{:S(2)}) collective-permute-start(f32[24,512]{1,0:T(8,128)S(1)} %describe.1), channel_id=1, source_target_pairs={{0,4},{1,5},{2,6},{3,7},{4,0},{5,1},{6,2},{7,3},{8,12},{9,13},{10,... | collective-permute-start | bytes 147464 | tf_op jit(solution)/shard_map/ppermute | solution.py:503
  14.4 15.8 %collective-permute-start = (f32[136,512]{1,0:T(8,128)}, f32[136,512]{1,0:T(8,128)S(1)}, u32[]{:S(2)}, u32[]{:S(2)}) collective-permute-start(f32[136,512]{1,0:T(8,128)} %send.1), channel_id=1, source_target_pairs={{0,0},{1,8},{2,16},{3,24},{4,4},{5,12},{6,20},{7,28},{8,2},{9,10},... | collective-permute-start | bytes 835592 | tf_op jit(solution)/shard_map/ppermute | solution.py:503
  16.3 4.7 %collective-permute-start.3 = (f32[24,512]{1,0:T(8,128)S(1)}, f32[24,512]{1,0:T(8,128)S(1)}, u32[]{:S(2)}, u32[]{:S(2)}) collective-permute-start(f32[24,512]{1,0:T(8,128)S(1)} %broadcast_select_fusion), channel_id=1, source_target_pairs={{0,8},{1,9},{2,10},{3,11},{4,12},{5,13},{6,14},{7,15},{8,0},{9,1},... | collective-permute-start | bytes 147464 | tf_op jit(solution)/shard_map/ppermute | solution.py:503
  33.3 6.9 %collective-permute-start.5 = (f32[128,256]{1,0:T(8,128)S(1)}, f32[128,256]{1,0:T(8,128)S(1)}, u32[]{:S(2)}, u32[]{:S(2)}) collective-permute-start(f32[128,256]{1,0:T(8,128)S(1)} %get-tuple-element.54), channel_id=1, source_target_pairs={{0,4},{1,5},{2,6},{3,7},{4,0},{5,1},{6,2},{7,3},{8,12},{9,13},{10,... | collective-permute-start | bytes 393224 | tf_op jit(solution)/shard_map/ppermute | solution.py:503
  33.6 7.4 %collective-permute-start.6 = (f32[128,256]{1,0:T(8,128)S(1)}, f32[128,256]{1,0:T(8,128)S(1)}, u32[]{:S(2)}, u32[]{:S(2)}) collective-permute-start(f32[128,256]{1,0:T(8,128)S(1)} %get-tuple-element.55), channel_id=1, source_target_pairs={{0,2},{1,3},{2,0},{3,1},{4,6},{5,7},{6,4},{7,5},{8,10},{9,11},{10,... | collective-permute-start | bytes 393224 | tf_op jit(solution)/shard_map/ppermute | solution.py:503
  33.6 7.4 %collective-permute-start.7 = (f32[128,256]{1,0:T(8,128)S(1)}, f32[128,256]{1,0:T(8,128)S(1)}, u32[]{:S(2)}, u32[]{:S(2)}) collective-permute-start(f32[128,256]{1,0:T(8,128)S(1)} %get-tuple-element.56), channel_id=1, source_target_pairs={{0,6},{1,7},{2,4},{3,5},{4,2},{5,3},{6,0},{7,1},{8,14},{9,15},{10,... | collective-permute-start | bytes 393224 | tf_op jit(solution)/shard_map/ppermute | solution.py:503
  36.0 6.2 %collective-permute-start.8 = (f32[24,1024]{1,0:T(8,128)S(1)}, f32[24,1024]{1,0:T(8,128)S(1)}, u32[]{:S(2)}, u32[]{:S(2)}) collective-permute-start(f32[24,1024]{1,0:T(8,128)S(1)} %pad_maximum_fusion.3), channel_id=1, source_target_pairs={{0,16},{1,17},{2,18},{3,19},{4,20},{5,21},{6,22},{7,23},{8,24},{9,... | collective-permute-start | bytes 294920 | tf_op jit(solution)/shard_map/ppermute | solution.py:503
  42.2 12.3 %collective-permute-start.9 = (f32[24,1536]{1,0:T(8,128)S(1)}, f32[24,1536]{1,0:T(8,128)S(1)}, u32[]{:S(2)}, u32[]{:S(2)}) collective-permute-start(f32[24,1536]{1,0:T(8,128)S(1)} %constant_dynamic-update-slice_fusion), channel_id=1, source_target_pairs={{0,1},{1,0},{2,3},{3,2},{4,5},{5,4},{6,7},{7,6},{8,9},{9,8},{10,11... | collective-permute-start | bytes 442376 | tf_op jit(solution)/shard_map/ppermute | solution.py:503
  46.1 8.4 %collective-permute-start.11 = (f32[256,256]{1,0:T(8,128)S(1)}, f32[256,256]{1,0:T(8,128)S(1)}, u32[]{:S(2)}, u32[]{:S(2)}) collective-permute-start(f32[256,256]{1,0:T(8,128)S(1)} %pad_maximum_fusion.here_ref), channel_id=1, source_target_pairs={{8,16},{9,17},{10,18},{11,19},{12,20},{13,21},{14,22},{15,23},{16,... | collective-permute-start | bytes 786440 | tf_op jit(solution)/shard_map/ppermute | solution.py:503
  46.8 9.4 %collective-permute-start.10 = (f32[256,256]{1,0:T(8,128)S(1)}, f32[256,256]{1,0:T(8,128)S(1)}, u32[]{:S(2)}, u32[]{:S(2)}) collective-permute-start(f32[256,256]{1,0:T(8,128)S(1)} %pad_maximum_fusion.here_ref), channel_id=1, source_target_pairs={{0,8},{1,9},{2,10},{3,11},{4,12},{5,13},{6,14},{7,15},{8,0},{9,1},... | collective-permute-start | bytes 786440 | tf_op jit(solution)/shard_map/ppermute | solution.py:503
  58.5 7.7 %collective-permute-start.14 = (f32[128,256]{1,0:T(8,128)S(1)}, f32[128,256]{1,0:T(8,128)S(1)}, u32[]{:S(2)}, u32[]{:S(2)}) collective-permute-start(f32[128,256]{1,0:T(8,128)S(1)} %plane_first.1.a_ref.pulled_ref.old_z_ref), channel_id=1, source_target_pairs={{0,6},{1,7},{2,4},{3,5},{4,2},{5,3},{6,0},{7,1},{8,14},{9,15},{10,... | collective-permute-start | bytes 393224 | tf_op jit(solution)/shard_map/ppermute | solution.py:503
  60.0 7.5 %collective-permute-start.13 = (f32[128,256]{1,0:T(8,128)S(1)}, f32[128,256]{1,0:T(8,128)S(1)}, u32[]{:S(2)}, u32[]{:S(2)}) collective-permute-start(f32[128,256]{1,0:T(8,128)S(1)} %plane_first.1.a_ref.pulled_ref.old_z_ref), channel_id=1, source_target_pairs={{0,2},{1,3},{2,0},{3,1},{4,6},{5,7},{6,4},{7,5},{8,10},{9,11},{10,... | collective-permute-start | bytes 393224 | tf_op jit(solution)/shard_map/ppermute | solution.py:503
  60.0 7.5 %collective-permute-start.12 = (f32[128,256]{1,0:T(8,128)S(1)}, f32[128,256]{1,0:T(8,128)S(1)}, u32[]{:S(2)}, u32[]{:S(2)}) collective-permute-start(f32[128,256]{1,0:T(8,128)S(1)} %plane_first.1.a_ref.pulled_ref.old_z_ref), channel_id=1, source_target_pairs={{0,4},{1,5},{2,6},{3,7},{4,0},{5,1},{6,2},{7,3},{8,12},{9,13},{10,... | collective-permute-start | bytes 393224 | tf_op jit(solution)/shard_map/ppermute | solution.py:503
  68.2 1.7 %collective-permute-start.15 = (f32[128,256]{1,0:T(8,128)S(1)}, f32[128,256]{1,0:T(8,128)S(1)}, u32[]{:S(2)}, u32[]{:S(2)}) collective-permute-start(f32[128,256]{1,0:T(8,128)S(1)} %get-tuple-element.69), channel_id=1, source_target_pairs={{0,1},{1,0},{2,3},{3,2},{4,5},{5,4},{6,7},{7,6},{8,9},{9,8},{10,11... | collective-permute-start | bytes 393224 | tf_op jit(solution)/shard_map/ppermute | solution.py:503
  69.8 3.7 %collective-permute-start.17 = (f32[128,256]{1,0:T(8,128)S(1)}, f32[128,256]{1,0:T(8,128)S(1)}, u32[]{:S(2)}, u32[]{:S(2)}) collective-permute-start(f32[128,256]{1,0:T(8,128)S(1)} %add.61.here_ref.old_s_ref), channel_id=1, source_target_pairs={{8,16},{9,17},{10,18},{11,19},{12,20},{13,21},{14,22},{15,23},{16,... | collective-permute-start | bytes 393224 | tf_op jit(solution)/shard_map/ppermute | solution.py:503
  70.5 6.3 %collective-permute-start.16 = (f32[128,256]{1,0:T(8,128)S(1)}, f32[128,256]{1,0:T(8,128)S(1)}, u32[]{:S(2)}, u32[]{:S(2)}) collective-permute-start(f32[128,256]{1,0:T(8,128)S(1)} %add.61.here_ref.old_s_ref), channel_id=1, source_target_pairs={{0,8},{1,9},{2,10},{3,11},{4,12},{5,13},{6,14},{7,15},{8,0},{9,1},... | collective-permute-start | bytes 393224 | tf_op jit(solution)/shard_map/ppermute | solution.py:503
  78.6 5.0 %collective-permute-start.20 = (f32[136,256]{1,0:T(8,128)S(1)}, f32[136,256]{1,0:T(8,128)S(1)}, u32[]{:S(2)}, u32[]{:S(2)}) collective-permute-start(f32[136,256]{1,0:T(8,128)S(1)} %get-tuple-element.70.a_ref.pulled_ref), channel_id=1, source_target_pairs={{0,6},{1,7},{2,4},{3,5},{4,2},{5,3},{6,0},{7,1},{8,14},{9,15},{10,... | collective-permute-start | bytes 417800 | tf_op jit(solution)/shard_map/ppermute | solution.py:503
  79.8 7.9 %collective-permute-start.19 = (f32[136,256]{1,0:T(8,128)S(1)}, f32[136,256]{1,0:T(8,128)S(1)}, u32[]{:S(2)}, u32[]{:S(2)}) collective-permute-start(f32[136,256]{1,0:T(8,128)S(1)} %get-tuple-element.70.a_ref.pulled_ref), channel_id=1, source_target_pairs={{0,2},{1,3},{2,0},{3,1},{4,6},{5,7},{6,4},{7,5},{8,10},{9,11},{10,... | collective-permute-start | bytes 417800 | tf_op jit(solution)/shard_map/ppermute | solution.py:503
  80.2 7.6 %collective-permute-start.18 = (f32[136,256]{1,0:T(8,128)S(1)}, f32[136,256]{1,0:T(8,128)S(1)}, u32[]{:S(2)}, u32[]{:S(2)}) collective-permute-start(f32[136,256]{1,0:T(8,128)S(1)} %get-tuple-element.70.a_ref.pulled_ref), channel_id=1, source_target_pairs={{0,4},{1,5},{2,6},{3,7},{4,0},{5,1},{6,2},{7,3},{8,12},{9,13},{10,... | collective-permute-start | bytes 417800 | tf_op jit(solution)/shard_map/ppermute | solution.py:503
  88.3 2.3 %collective-permute-start.21 = (f32[392,256]{1,0:T(8,128)S(1)}, f32[392,256]{1,0:T(8,128)S(1)}, u32[]{:S(2)}, u32[]{:S(2)}) collective-permute-start(f32[392,256]{1,0:T(8,128)S(1)} %get-tuple-element.73), channel_id=1, source_target_pairs={{0,1},{1,0},{2,3},{3,2},{4,5},{5,4},{6,7},{7,6},{8,9},{9,8},{10,11... | collective-permute-start | bytes 1204232 | tf_op jit(solution)/shard_map/ppermute | solution.py:503
  90.7 5.7 %collective-permute-start.25 = (f32[136,256]{1,0:T(8,128)S(1)}, f32[136,256]{1,0:T(8,128)S(1)}, u32[]{:S(2)}, u32[]{:S(2)}) collective-permute-start(f32[136,256]{1,0:T(8,128)S(1)} %slice_add_fusion.1.here_ref), channel_id=1, source_target_pairs={{8,16},{9,17},{10,18},{11,19},{12,20},{13,21},{14,22},{15,23},{16,... | collective-permute-start | bytes 417800 | tf_op jit(solution)/shard_map/ppermute | solution.py:503
  91.5 6.8 %collective-permute-start.22 = (f32[136,256]{1,0:T(8,128)S(1)}, f32[136,256]{1,0:T(8,128)S(1)}, u32[]{:S(2)}, u32[]{:S(2)}) collective-permute-start(f32[136,256]{1,0:T(8,128)S(1)} %slice_add_fusion.1.here_ref), channel_id=1, source_target_pairs={{0,8},{1,9},{2,10},{3,11},{4,12},{5,13},{6,14},{7,15},{8,0},{9,1},... | collective-permute-start | bytes 417800 | tf_op jit(solution)/shard_map/ppermute | solution.py:503
  94.9 4.7 %collective-permute-start.24 = (f32[8,256]{1,0:T(8,128)S(1)}, f32[8,256]{1,0:T(8,128)S(1)}, u32[]{:S(2)}, u32[]{:S(2)}) collective-permute-start(f32[8,256]{1,0:T(8,128)S(1)} %slice.32), channel_id=1, source_target_pairs={{0,24},{1,25},{2,26},{3,27},{4,28},{5,29},{6,30},{7,31},{8,16},{9,... | collective-permute-start | bytes 24584 | tf_op jit(solution)/shard_map/ppermute | solution.py:503
  96.4 3.4 %collective-permute-start.23 = (f32[8,256]{1,0:T(8,128)S(1)}, f32[8,256]{1,0:T(8,128)S(1)}, u32[]{:S(2)}, u32[]{:S(2)}) collective-permute-start(f32[8,256]{1,0:T(8,128)S(1)} %slice.32), channel_id=1, source_target_pairs={{0,16},{1,17},{2,18},{3,19},{4,20},{5,21},{6,22},{7,23},{8,24},{9,... | collective-permute-start | bytes 24584 | tf_op jit(solution)/shard_map/ppermute | solution.py:503
  101.1 5.0 %collective-permute-start.28 = (f32[136,256]{1,0:T(8,128)S(1)}, f32[136,256]{1,0:T(8,128)S(1)}, u32[]{:S(2)}, u32[]{:S(2)}) collective-permute-start(f32[136,256]{1,0:T(8,128)S(1)} %get-tuple-element.75.a_ref.pulled_ref), channel_id=1, source_target_pairs={{0,6},{1,7},{2,4},{3,5},{4,2},{5,3},{6,0},{7,1},{8,14},{9,15},{10,... | collective-permute-start | bytes 417800 | tf_op jit(solution)/shard_map/ppermute | solution.py:503
  102.4 5.4 %collective-permute-start.27 = (f32[136,256]{1,0:T(8,128)S(1)}, f32[136,256]{1,0:T(8,128)S(1)}, u32[]{:S(2)}, u32[]{:S(2)}) collective-permute-start(f32[136,256]{1,0:T(8,128)S(1)} %get-tuple-element.75.a_ref.pulled_ref), channel_id=1, source_target_pairs={{0,2},{1,3},{2,0},{3,1},{4,6},{5,7},{6,4},{7,5},{8,10},{9,11},{10,... | collective-permute-start | bytes 417800 | tf_op jit(solution)/shard_map/ppermute | solution.py:503
  102.8 5.1 %collective-permute-start.26 = (f32[136,256]{1,0:T(8,128)S(1)}, f32[136,256]{1,0:T(8,128)S(1)}, u32[]{:S(2)}, u32[]{:S(2)}) collective-permute-start(f32[136,256]{1,0:T(8,128)S(1)} %get-tuple-element.75.a_ref.pulled_ref), channel_id=1, source_target_pairs={{0,4},{1,5},{2,6},{3,7},{4,0},{5,1},{6,2},{7,3},{8,12},{9,13},{10,... | collective-permute-start | bytes 417800 | tf_op jit(solution)/shard_map/ppermute | solution.py:503
  108.4 4.8 %collective-permute-start.29 = (f32[392,256]{1,0:T(8,128)S(1)}, f32[392,256]{1,0:T(8,128)S(1)}, u32[]{:S(2)}, u32[]{:S(2)}) collective-permute-start(f32[392,256]{1,0:T(8,128)S(1)} %get-tuple-element.79), channel_id=1, source_target_pairs={{0,1},{1,0},{2,3},{3,2},{4,5},{5,4},{6,7},{7,6},{8,9},{9,8},{10,11... | collective-permute-start | bytes 1204232 | tf_op jit(solution)/shard_map/ppermute | solution.py:503
  114.5 19.2 %collective-permute-start.31 = (f32[256,256]{1,0:T(8,128)S(1)}, f32[256,256]{1,0:T(8,128)S(1)}, u32[]{:S(2)}, u32[]{:S(2)}) collective-permute-start(f32[256,256]{1,0:T(8,128)S(1)} %get-tuple-element.86), channel_id=1, source_target_pairs={{0,1},{1,0},{2,3},{3,2},{4,5},{5,4},{6,7},{7,6},{8,9},{9,8},{10,11... | collective-permute-start | bytes 786440 | tf_op jit(solution)/shard_map/ppermute | solution.py:503
  115.0 5.8 %collective-permute-start.30 = (f32[136,256]{1,0:T(8,128)S(1)}, f32[136,256]{1,0:T(8,128)S(1)}, u32[]{:S(2)}, u32[]{:S(2)}) collective-permute-start(f32[136,256]{1,0:T(8,128)S(1)} %slice_add_fusion.here_ref), channel_id=1, source_target_pairs={{0,8},{1,9},{2,10},{3,11},{4,12},{5,13},{6,14},{7,15},{8,16},{9,17... | collective-permute-start | bytes 417800 | tf_op jit(solution)/shard_map/ppermute | solution.py:503
  134.5 13.3 %collective-permute-start.32 = (f32[512,128]{1,0:T(8,128)S(1)}, f32[512,128]{1,0:T(8,128)S(1)}, u32[]{:S(2)}, u32[]{:S(2)}) collective-permute-start(f32[512,128]{1,0:T(8,128)S(1)} %plane_combine.1), channel_id=1, source_target_pairs={{0,0},{1,16},{2,8},{3,24},{4,4},{5,20},{6,12},{7,28},{8,1},{9,17},... | collective-permute-start | bytes 786440 | tf_op jit(solution)/shard_map/ppermute | solution.py:503
  (11 other events, 157.6 us)
